TPU v7x, 32 devices: a whole 2x2x4 slice. The times are simulated.
32 devices in a mesh: dom: 8 (over z, y), feat: 4 (over x, core).
Axes of the slice: x: 2, y: 2, z: 4, core: 2. Of those that a mesh axis runs over, the one named last changes fastest.
Arguments:
- features: bfloat16 [8192, 512], P('dom', 'feat'), may hold values from -6 to 6
- w_self: bfloat16 [512, 512], P('feat'), may hold values from -0.25 to 0.25
- w_neigh: bfloat16 [512, 512], P('feat'), may hold values from -0.25 to 0.25
- degree: int32 [8192], P('dom'), may hold values from 1 to 32
- local_vals: bfloat16 [8, 16, 128, 128], P('dom'), may hold values from 0 to 0.19921875
- local_dst: int32 [8, 16], P('dom'), may hold values from 0 to 7
- local_src: int32 [8, 16], P('dom'), may hold values from 0 to 7
- remote_vals: bfloat16 [8, 6, 8, 128, 128], P('dom'), may hold values from 0 to 0.19921875
- remote_dst: int32 [8, 6, 8], P('dom'), may hold values from 0 to 7
- remote_src: int32 [8, 6, 8], P('dom'), may hold values from 0 to 7
- cotangent: bfloat16 [8192, 512], P('dom', 'feat'), may hold values from -6 to 6
Outputs:
- out: bfloat16 [8192, 512], P('dom', 'feat')
- grad_x: float32 [8192, 512], P('dom', 'feat')
- grad_self: float32 [512, 512], P('feat')
- grad_neigh: float32 [512, 512], P('feat')
All inputs are finite; a program needn't handle non-finite values.
Results may differ from a plain program's by a relative error of at most 0.0068.
Values may be sent and summed in bfloat16 or wider, within the bound.
No kernel may reach another device: no remote copies, remote signals or barrier semaphores. Data moves between devices by JAX's collectives and lax.ppermute only.
A program may use at most 64 MiB of HBM per device.

v0:
```python
import jax
import jax.numpy as jnp
from jax import lax
from jax.sharding import PartitionSpec as P


def shifted(x, axis, by):
    devices = lax.axis_size(axis)
    return lax.ppermute(x, axis, [(i, (i + by) % devices) for i in range(devices)])


def spread(parts, block_ids, count):
    table = (block_ids[:, None] == jnp.arange(count, dtype=jnp.int32)[None, :]).astype(jnp.float32)
    return jnp.einsum("kc,kif->cif", table, parts, precision=lax.Precision.HIGHEST)


def tile_apply(tiles, blocks):
    return jnp.einsum("kij,kjf->kif", tiles, blocks, preferred_element_type=jnp.float32)


def tile_apply_back(tiles, blocks):
    return jnp.einsum("kji,kjf->kif", tiles, blocks, preferred_element_type=jnp.float32)


def make_back_piece(weights, stacked):

    def back_piece(carry, piece, start):
        dz_acc = lax.dot_general(
            piece, weights, (((1,), (1,)), ((), ())), preferred_element_type=jnp.float32
        )
        product = lax.dot_general(
            stacked, piece, (((0,), (0,)), ((), ())), preferred_element_type=jnp.float32
        )
        return (dz_acc, product)

    return back_piece


def body(
    features,
    w_self,
    w_neigh,
    degree,
    local_vals,
    local_dst,
    local_src,
    remote_vals,
    remote_dst,
    remote_src,
    cotangent,
):
    rows = features.shape[0]
    width = features.shape[1]
    block = local_vals.shape[-1]
    nblocks = rows // block
    rounds = remote_vals.shape[1]
    parts_total = lax.axis_size("dom")
    offsets = [(step + 1) * parts_total // (rounds + 1) for step in range(rounds)]
    blocks = features.reshape(nblocks, block, width)
    totals = spread(
        tile_apply(local_vals[0], jnp.take(blocks, local_src[0], axis=0)), local_dst[0], nblocks
    )
    arrived_ids = []
    for step in range(rounds):
        partial_blocks = tile_apply(
            remote_vals[0, step], jnp.take(blocks, remote_src[0, step], axis=0)
        ).astype(jnp.bfloat16)
        arrived, block_ids = shifted((partial_blocks, remote_dst[0, step]), "dom", offsets[step])
        arrived_ids.append(block_ids)
        totals = totals + spread(arrived.astype(jnp.float32), block_ids, nblocks)
    inverse = 1.0 / degree.astype(jnp.float32)
    agg = (totals.reshape(rows, width) * inverse[:, None]).astype(jnp.bfloat16)
    stacked = jnp.concatenate([features, agg], axis=1)
    weights = jnp.concatenate([w_self, w_neigh], axis=0)
    start_carry = (
        jnp.zeros((rows, 2 * width), jnp.float32),
        jnp.zeros((2 * width, weights.shape[1]), jnp.float32),
    )
    back_piece = make_back_piece(weights, stacked)
    pre = lax.psum_scatter(
        lax.dot_general(
            weights, stacked, (((0,), (1,)), ((), ())), preferred_element_type=jnp.float32
        ),
        "feat",
        scatter_dimension=0,
        tiled=True,
    ).T
    sigma = jax.nn.sigmoid(pre)
    out = (pre * sigma).astype(jnp.bfloat16)
    dpre = (cotangent.astype(jnp.float32) * sigma * (1.0 + pre * (1.0 - sigma))).astype(
        jnp.bfloat16
    )
    dz_total, grad_local = back_piece(
        start_carry, lax.all_gather(dpre, "feat", axis=1, tiled=True), jnp.int32(0)
    )
    dx_self = dz_total[:, :width]
    dsum = (
        (dz_total[:, width:] * inverse[:, None]).astype(jnp.bfloat16).reshape(nblocks, block, width)
    )
    grad_all = lax.psum(grad_local, "dom")
    back = spread(
        tile_apply_back(local_vals[0], jnp.take(dsum, local_dst[0], axis=0)), local_src[0], nblocks
    )
    for step in range(rounds):
        picked = jnp.take(dsum, arrived_ids[step], axis=0)
        returned = shifted(picked, "dom", parts_total - offsets[step])
        back = back + spread(
            tile_apply_back(remote_vals[0, step], returned), remote_src[0, step], nblocks
        )
    grad_x = dx_self + back.reshape(rows, width)
    return (out, grad_x, grad_all[:width], grad_all[width:])


def solution(mesh):
    placed = (
        P("dom", "feat"),
        P("feat", None),
        P("feat", None),
        P("dom"),
        P("dom", None, None, None),
        P("dom", None),
        P("dom", None),
        P("dom", None, None, None, None),
        P("dom", None, None),
        P("dom", None, None),
        P("dom", "feat"),
    )
    return jax.shard_map(
        body,
        mesh=mesh,
        in_specs=placed,
        out_specs=(P("dom", "feat"), P("dom", "feat"), P("feat", None), P("feat", None)),
        check_vma=False,
    )
```

profile of v0, /device:TPU:0, one launch (start us, length us, event | category | flops | bytes accessed | tf_op | source)
XLA Modules:
  0.0 245.0 jit_solution(15145179043249609235)
XLA Ops:
  7.2 0.8 compare_and_fusion.11
  8.1 1.5 gather_fusion.6
  9.6 1.4 fusion.35
  11.0 0.9 copy.28
  11.9 5.0 %collective-permute-start.11 = (bf16[8,128,128]{2,0,1:T(8,128)(2,1)}, bf16[8,128,128]{2,0,1:T(8,128)(2,1)}, u32[]{:S(2)}, u32[]{:S(2)}) collective-permute-start(bf16[8,128,128]{2,0,1:T(8,128)(2,1)} %bitcast.187), channel_id=1, source_target_pairs={{0,24},{4,28},{8,0},{12,4},{16,8},{20,12},{24,16},{28,20},{1,25},{... | collective-permute-start | bytes 786440 | tf_op jit(solution)/shard_map/ppermute | solution.py:9
  18.0 1.4 fusion.39
  19.4 0.9 copy.27
  20.7 3.5 %collective-permute-start.8 = (s32[8]{0:T(128)S(1)}, s32[8]{0:T(128)S(1)}, u32[]{:S(2)}, u32[]{:S(2)}) collective-permute-start(s32[8]{0:T(128)S(1)} %get-tuple-element.41), channel_id=1, source_target_pairs={{0,20},{4,24},{8,28},{12,0},{16,4},{20,8},{24,12},{28,16},{1,21},{... | collective-permute-start | bytes 104 | tf_op jit(solution)/shard_map/ppermute | solution.py:9
  24.8 1.4 fusion.43
  26.2 0.9 copy.26
  27.5 1.3 gather_fusion.3
  28.8 0.6 gather_fusion
  29.4 0.7 fusion.25
  30.6 0.6 gather_fusion.1
  31.9 1.4 fusion.47
  33.7 1.4 fusion.55
  35.1 1.4 fusion.51
  37.1 2.7 %collective-permute-start.6 = (s32[8]{0:T(128)S(1)}, s32[8]{0:T(128)S(1)}, u32[]{:S(2)}, u32[]{:S(2)}) collective-permute-start(s32[8]{0:T(128)S(1)} %get-tuple-element.37), channel_id=1, source_target_pairs={{0,16},{4,20},{8,24},{12,28},{16,0},{20,4},{24,8},{28,12},{1,17},{... | collective-permute-start | bytes 104 | tf_op jit(solution)/shard_map/ppermute | solution.py:9
  39.8 1.2 fusion.105
  41.0 2.9 %collective-permute-start.4 = (s32[8]{0:T(128)S(1)}, s32[8]{0:T(128)S(1)}, u32[]{:S(2)}, u32[]{:S(2)}) collective-permute-start(s32[8]{0:T(128)S(1)} %get-tuple-element.38), channel_id=1, source_target_pairs={{0,12},{4,16},{8,20},{12,24},{16,28},{20,0},{24,4},{28,8},{1,13},{... | collective-permute-start | bytes 104 | tf_op jit(solution)/shard_map/ppermute | solution.py:9
  43.8 1.5 collective-permute-start.1
  45.4 1.2 fusion.102
  46.5 6.0 %collective-permute-done.6 = s32[8]{0:T(128)S(1)} collective-permute-done((s32[8]{0:T(128)S(1)}, s32[8]{0:T(128)S(1)}, u32[]{:S(2)}, u32[]{:S(2)}) %collective-permute-start.6) | collective-permute-done | bytes 64 | tf_op jit(solution)/shard_map/ppermute | solution.py:9
  52.5 1.2 fusion.99
  53.6 10.4 %collective-permute-done.4 = s32[8]{0:T(128)S(1)} collective-permute-done((s32[8]{0:T(128)S(1)}, s32[8]{0:T(128)S(1)}, u32[]{:S(2)}, u32[]{:S(2)}) %collective-permute-start.4) | collective-permute-done | bytes 64 | tf_op jit(solution)/shard_map/ppermute | solution.py:9
  64.5 4.9 %collective-permute-done.2 = s32[8]{0:T(128)S(1)} collective-permute-done((s32[8]{0:T(128)S(1)}, s32[8]{0:T(128)S(1)}, u32[]{:S(2)}, u32[]{:S(2)}) %collective-permute-start.2) | collective-permute-done | bytes 64 | tf_op jit(solution)/shard_map/ppermute | solution.py:9
  70.0 0.7 copy-done.7
  70.7 1.8 fusion.32
  72.6 0.9 copy-done.9
  73.7 27.7 %reduce-scatter.2.cloned.1.call-done = f32[128,1024]{1,0:T(8,128)} async-done(((f32[512,1024]{1,0:T(8,128)}), f32[128,1024]{1,0:T(8,128)}) %reduce-scatter.2.cloned.1.call-update) | async-done | bytes 524304 | tf_op jit(solution)/shard_map/reduce_scatter | solution.py:80
  101.4 2.0 fusion.21
  103.5 0.8 copy.21
  104.4 16.0 %all-gather.2.cloned.1.call-done = bf16[1024,512]{0,1:T(8,128)(2,1)} async-done(((bf16[1024,128]{0,1:T(8,128)(2,1)}), bf16[1024,512]{0,1:T(8,128)(2,1)}) %all-gather.2.cloned.1.call-update) | async-done | bytes 1048592 | tf_op jit(solution)/shard_map/all_gather | solution.py:94
  120.3 1.7 fusion.146
  122.3 1.4 gather_fusion.7
  123.7 1.5 fusion.23
  125.1 1.4 copy.29
  127.1 0.8 broadcast_select_fusion.5
  127.9 4.2 %collective-permute-start.12 = (bf16[8,128,128]{2,1,0:T(8,128)(2,1)}, bf16[8,128,128]{2,1,0:T(8,128)(2,1)}, u32[]{:S(2)}, u32[]{:S(2)}) collective-permute-start(bf16[8,128,128]{2,1,0:T(8,128)(2,1)} %broadcast_select_fusion.5), channel_id=1, source_target_pairs={{0,28},{4,0},{8,4},{12,8},{16,12},{20,16},{24,20},{28,24},{1,29},{... | collective-permute-start | bytes 786440 | tf_op jit(solution)/shard_map/ppermute | solution.py:9
  132.8 0.8 broadcast_select_fusion.4
  134.7 0.8 broadcast_select_fusion.3
  136.1 0.8 broadcast_select_fusion.2
  136.9 2.9 %collective-permute-start.15 = (bf16[8,128,128]{2,1,0:T(8,128)(2,1)}, bf16[8,128,128]{2,1,0:T(8,128)(2,1)}, u32[]{:S(2)}, u32[]{:S(2)}) collective-permute-start(bf16[8,128,128]{2,1,0:T(8,128)(2,1)} %broadcast_select_fusion.2), channel_id=1, source_target_pairs={{0,16},{4,20},{8,24},{12,28},{16,0},{20,4},{24,8},{28,12},{1,17},{... | collective-permute-start | bytes 786440 | tf_op jit(solution)/shard_map/ppermute | solution.py:9
  140.5 0.8 broadcast_select_fusion.1
  141.3 2.6 %fusion.31 = f32[256,512]{1,0:T(8,128)} fusion(bf16[1024,512]{0,1:T(8,128)(2,1)} %all-gather.2.cloned.1.call-done, bf16[1024,128]{1,0:T(8,128)(2,1)} %copy-done.7, bf16[1024,128]{1,0:T(8,128)(2,1)S(1)} %copy-done.1), kind=kOutput, calls=%fused_computation.60 | convolution fusion | flops 269484032 | bytes 2097152 | tf_op jit(solution)/shard_map/dot_general | solution.py:31
  143.9 1.3 fusion.4
  145.8 0.8 broadcast_select_fusion
  146.6 2.0 collective-permute-start.17
  148.5 1.3 fusion.53
  149.9 1.3 fusion.49
  151.2 1.3 fusion.45
  152.5 31.2 %collective-permute-done.15 = bf16[8,128,128]{2,1,0:T(8,128)(2,1)} collective-permute-done((bf16[8,128,128]{2,1,0:T(8,128)(2,1)}, bf16[8,128,128]{2,1,0:T(8,128)(2,1)}, u32[]{:S(2)}, u32[]{:S(2)}) %collective-permute-start.15) | collective-permute-done | bytes 262176 | tf_op jit(solution)/shard_map/ppermute | solution.py:9
  183.7 2.1 fusion.41
  185.8 1.0 copy.30
  186.8 1.0 copy.31
  188.1 1.3 copy.33
  189.4 2.1 fusion.37
  191.5 2.1 copy.34
  193.6 2.0 fusion.33
  195.6 2.0 copy.35
  197.7 1.5 convolution_add_fusion.5
  201.5 0.9 slice_add_fusion
  202.3 34.3 %all-reduce.2.cloned.1.call-done = f32[256,512]{1,0:T(8,128)} async-done(((f32[256,512]{1,0:T(8,128)}), f32[256,512]{1,0:T(8,128)}) %all-reduce.2.cloned.1.call-update) | async-done | bytes 524304 | tf_op jit(solution)/shard_map/psum | solution.py:100
  236.6 1.9 fusion.145
  (118 shorter events, 12.9 us)
Async XLA Ops:
  7.2 22.2 %copy-start = (bf16[1,16,128,128]{3,2,1,0:T(8,128)(2,1)S(1)}, bf16[1,16,128,128]{3,2,1,0:T(8,128)(2,1)}, u32[]{:S(2)}) copy-start(bf16[1,16,128,128]{3,2,1,0:T(8,128)(2,1)} %param.19) | copy-start | bytes 1572868
  7.2 10.2 %copy-start.1 = (bf16[1024,128]{1,0:T(8,128)(2,1)S(1)}, bf16[1024,128]{1,0:T(8,128)(2,1)}, u32[]{:S(2)}) copy-start(bf16[1024,128]{1,0:T(8,128)(2,1)} %param.15) | copy-start | bytes 786436
  7.2 9.8 %copy-start.14 = (s32[1,6,8]{2,0,1:T(1,128)S(1)}, s32[1,6,8]{2,0,1:T(1,128)}, u32[]{:S(2)}) copy-start(s32[1,6,8]{2,0,1:T(1,128)} %param.23) | copy-start | bytes 580
  7.2 94.2 %reduce-scatter.2.cloned.1.call-start = ((), (), s32[]{:S(2)}) async-start(), calls=%async_computation.1 | async-start | bytes 2621440 | tf_op jit(solution)/shard_map/reduce_scatter | solution.py:80
  11.9 27.9 %collective-permute-start.11 = (bf16[8,128,128]{2,0,1:T(8,128)(2,1)}, bf16[8,128,128]{2,0,1:T(8,128)(2,1)}, u32[]{:S(2)}, u32[]{:S(2)}) collective-permute-start(bf16[8,128,128]{2,0,1:T(8,128)(2,1)} %bitcast.187), channel_id=1, source_target_pairs={{0,24},{4,28},{8,0},{12,4},{16,8},{20,12},{24,16},{28,20},{1,25},{... | collective-permute-start | bytes 786440 | tf_op jit(solution)/shard_map/ppermute | solution.py:9
  17.0 20.2 %collective-permute-start.10 = (s32[8]{0:T(128)S(1)}, s32[8]{0:T(128)S(1)}, u32[]{:S(2)}, u32[]{:S(2)}) collective-permute-start(s32[8]{0:T(128)S(1)} %get-tuple-element.40), channel_id=1, source_target_pairs={{0,24},{4,28},{8,0},{12,4},{16,8},{20,12},{24,16},{28,20},{1,25},{... | collective-permute-start | bytes 104 | tf_op jit(solution)/shard_map/ppermute | solution.py:9
  18.0 9.4 %copy-start.16 = (s32[1,16]{1,0:T(1,128)S(1)}, s32[1,16]{1,0:T(1,128)}, u32[]{:S(2)}) copy-start(s32[1,16]{1,0:T(1,128)} %param.21) | copy-start | bytes 196
  19.4 9.3 %copy-start.15 = (s32[1,16]{1,0:T(1,128)S(1)}, s32[1,16]{1,0:T(1,128)}, u32[]{:S(2)}) copy-start(s32[1,16]{1,0:T(1,128)} %param.20) | copy-start | bytes 196
  20.3 23.5 %collective-permute-start.9 = (bf16[8,128,128]{2,0,1:T(8,128)(2,1)}, bf16[8,128,128]{2,0,1:T(8,128)(2,1)}, u32[]{:S(2)}, u32[]{:S(2)}) collective-permute-start(bf16[8,128,128]{2,0,1:T(8,128)(2,1)} %bitcast.188), channel_id=1, source_target_pairs={{0,20},{4,24},{8,28},{12,0},{16,4},{20,8},{24,12},{28,16},{1,21},{... | collective-permute-start | bytes 786440 | tf_op jit(solution)/shard_map/ppermute | solution.py:9
  20.7 20.3 %collective-permute-start.8 = (s32[8]{0:T(128)S(1)}, s32[8]{0:T(128)S(1)}, u32[]{:S(2)}, u32[]{:S(2)}) collective-permute-start(s32[8]{0:T(128)S(1)} %get-tuple-element.41), channel_id=1, source_target_pairs={{0,20},{4,24},{8,28},{12,0},{16,4},{20,8},{24,12},{28,16},{1,21},{... | collective-permute-start | bytes 104 | tf_op jit(solution)/shard_map/ppermute | solution.py:9
  27.1 25.4 %collective-permute-start.7 = (bf16[8,128,128]{2,0,1:T(8,128)(2,1)}, bf16[8,128,128]{2,0,1:T(8,128)(2,1)}, u32[]{:S(2)}, u32[]{:S(2)}) collective-permute-start(bf16[8,128,128]{2,0,1:T(8,128)(2,1)} %bitcast.189), channel_id=1, source_target_pairs={{0,16},{4,20},{8,24},{12,28},{16,0},{20,4},{24,8},{28,12},{1,17},{... | collective-permute-start | bytes 786440 | tf_op jit(solution)/shard_map/ppermute | solution.py:9
  30.1 1.7 copy-start.8
  33.2 3.3 %copy-start.13 = (s32[1024]{0:T(1024)S(1)}, s32[1024]{0:T(1024)}, u32[]{:S(2)}) copy-start(s32[1024]{0:T(1024)} %param.18) | copy-start | bytes 12292
  33.2 3.3 %copy-start.10 = (bf16[128,512]{1,0:T(8,128)(2,1)S(1)}, bf16[128,512]{1,0:T(8,128)(2,1)}, u32[]{:S(2)}) copy-start(bf16[128,512]{1,0:T(8,128)(2,1)} %param.16) | copy-start | bytes 393220
  33.2 3.3 %copy-start.11 = (bf16[128,512]{1,0:T(8,128)(2,1)S(1)}, bf16[128,512]{1,0:T(8,128)(2,1)}, u32[]{:S(2)}) copy-start(bf16[128,512]{1,0:T(8,128)(2,1)} %param.17) | copy-start | bytes 393220
  37.1 15.3 %collective-permute-start.6 = (s32[8]{0:T(128)S(1)}, s32[8]{0:T(128)S(1)}, u32[]{:S(2)}, u32[]{:S(2)}) collective-permute-start(s32[8]{0:T(128)S(1)} %get-tuple-element.37), channel_id=1, source_target_pairs={{0,16},{4,20},{8,24},{12,28},{16,0},{20,4},{24,8},{28,12},{1,17},{... | collective-permute-start | bytes 104 | tf_op jit(solution)/shard_map/ppermute | solution.py:9
  39.8 24.2 %collective-permute-start.5 = (bf16[8,128,128]{2,0,1:T(8,128)(2,1)S(1)}, bf16[8,128,128]{2,0,1:T(8,128)(2,1)S(1)}, u32[]{:S(2)}, u32[]{:S(2)}) collective-permute-start(bf16[8,128,128]{2,0,1:T(8,128)(2,1)S(1)} %bitcast.231), channel_id=1, source_target_pairs={{0,12},{4,16},{8,20},{12,24},{16,28},{20,0},{24,4},{28,8},{1,13},{... | collective-permute-start | bytes 786440 | tf_op jit(solution)/shard_map/ppermute | solution.py:9
  41.0 23.1 %collective-permute-start.4 = (s32[8]{0:T(128)S(1)}, s32[8]{0:T(128)S(1)}, u32[]{:S(2)}, u32[]{:S(2)}) collective-permute-start(s32[8]{0:T(128)S(1)} %get-tuple-element.38), channel_id=1, source_target_pairs={{0,12},{4,16},{8,20},{12,24},{16,28},{20,0},{24,4},{28,8},{1,13},{... | collective-permute-start | bytes 104 | tf_op jit(solution)/shard_map/ppermute | solution.py:9
  43.8 20.4 %collective-permute-start.1 = (bf16[8,128,128]{2,0,1:T(8,128)(2,1)S(1)}, bf16[8,128,128]{2,0,1:T(8,128)(2,1)S(1)}, u32[]{:S(2)}, u32[]{:S(2)}) collective-permute-start(bf16[8,128,128]{2,0,1:T(8,128)(2,1)S(1)} %bitcast.230), channel_id=1, source_target_pairs={{0,4},{4,8},{8,12},{12,16},{16,20},{20,24},{24,28},{28,0},{1,5},{5... | collective-permute-start | bytes 786440 | tf_op jit(solution)/shard_map/ppermute | solution.py:9
  52.5 11.8 %collective-permute-start = (s32[8]{0:T(128)S(1)}, s32[8]{0:T(128)S(1)}, u32[]{:S(2)}, u32[]{:S(2)}) collective-permute-start(s32[8]{0:T(128)S(1)} %get-tuple-element.39), channel_id=1, source_target_pairs={{0,4},{4,8},{8,12},{12,16},{16,20},{20,24},{24,28},{28,0},{1,5},{5... | collective-permute-start | bytes 104 | tf_op jit(solution)/shard_map/ppermute | solution.py:9
  52.5 16.9 %collective-permute-start.3 = (bf16[8,128,128]{2,0,1:T(8,128)(2,1)S(1)}, bf16[8,128,128]{2,0,1:T(8,128)(2,1)S(1)}, u32[]{:S(2)}, u32[]{:S(2)}) collective-permute-start(bf16[8,128,128]{2,0,1:T(8,128)(2,1)S(1)} %bitcast.229), channel_id=1, source_target_pairs={{0,8},{4,12},{8,16},{12,20},{16,24},{20,28},{24,0},{28,4},{1,9},{5... | collective-permute-start | bytes 786440 | tf_op jit(solution)/shard_map/ppermute | solution.py:9
  64.1 5.3 %collective-permute-start.2 = (s32[8]{0:T(128)S(1)}, s32[8]{0:T(128)S(1)}, u32[]{:S(2)}, u32[]{:S(2)}) collective-permute-start(s32[8]{0:T(128)S(1)} %get-tuple-element.36), channel_id=1, source_target_pairs={{0,8},{4,12},{8,16},{12,20},{16,24},{20,28},{24,0},{28,4},{1,9},{5... | collective-permute-start | bytes 104 | tf_op jit(solution)/shard_map/ppermute | solution.py:9
  70.0 0.7 copy-start.7
  72.5 0.9 copy-start.9
  72.5 1.1 copy-start.12
  72.5 47.8 %all-gather.2.cloned.1.call-start = ((), (), s32[]{:S(2)}) async-start(), calls=%async_computation.2 | async-start | bytes 1310720 | tf_op jit(solution)/shard_map/all_gather | solution.py:94
  103.4 133.3 %all-reduce.2.cloned.1.call-start = ((), (), s32[]{:S(2)}) async-start(), calls=%async_computation.3 | async-start | bytes 1048576 | tf_op jit(solution)/shard_map/psum | solution.py:100
  127.9 18.6 %collective-permute-start.12 = (bf16[8,128,128]{2,1,0:T(8,128)(2,1)}, bf16[8,128,128]{2,1,0:T(8,128)(2,1)}, u32[]{:S(2)}, u32[]{:S(2)}) collective-permute-start(bf16[8,128,128]{2,1,0:T(8,128)(2,1)} %broadcast_select_fusion.5), channel_id=1, source_target_pairs={{0,28},{4,0},{8,4},{12,8},{16,12},{20,16},{24,20},{28,24},{1,29},{... | collective-permute-start | bytes 786440 | tf_op jit(solution)/shard_map/ppermute | solution.py:9
  133.6 16.3 %collective-permute-start.13 = (bf16[8,128,128]{2,1,0:T(8,128)(2,1)}, bf16[8,128,128]{2,1,0:T(8,128)(2,1)}, u32[]{:S(2)}, u32[]{:S(2)}) collective-permute-start(bf16[8,128,128]{2,1,0:T(8,128)(2,1)} %broadcast_select_fusion.4), channel_id=1, source_target_pairs={{0,24},{4,28},{8,0},{12,4},{16,8},{20,12},{24,16},{28,20},{1,25},{... | collective-permute-start | bytes 786440 | tf_op jit(solution)/shard_map/ppermute | solution.py:9
  135.5 15.7 %collective-permute-start.14 = (bf16[8,128,128]{2,1,0:T(8,128)(2,1)}, bf16[8,128,128]{2,1,0:T(8,128)(2,1)}, u32[]{:S(2)}, u32[]{:S(2)}) collective-permute-start(bf16[8,128,128]{2,1,0:T(8,128)(2,1)} %broadcast_select_fusion.3), channel_id=1, source_target_pairs={{0,20},{4,24},{8,28},{12,0},{16,4},{20,8},{24,12},{28,16},{1,21},{... | collective-permute-start | bytes 786440 | tf_op jit(solution)/shard_map/ppermute | solution.py:9
  136.9 46.8 %collective-permute-start.15 = (bf16[8,128,128]{2,1,0:T(8,128)(2,1)}, bf16[8,128,128]{2,1,0:T(8,128)(2,1)}, u32[]{:S(2)}, u32[]{:S(2)}) collective-permute-start(bf16[8,128,128]{2,1,0:T(8,128)(2,1)} %broadcast_select_fusion.2), channel_id=1, source_target_pairs={{0,16},{4,20},{8,24},{12,28},{16,0},{20,4},{24,8},{28,12},{1,17},{... | collective-permute-start | bytes 786440 | tf_op jit(solution)/shard_map/ppermute | solution.py:9
  140.5 3.4 %copy-start.2 = (f32[16,128,128]{1,0,2:T(8,128)S(1)}, f32[16,128,128]{1,0,2:T(8,128)}, u32[]{:S(2)}) copy-start(f32[16,128,128]{1,0,2:T(8,128)} %copy.29) | copy-start | bytes 3145732
  141.3 48.1 %collective-permute-start.16 = (bf16[8,128,128]{2,1,0:T(8,128)(2,1)}, bf16[8,128,128]{2,1,0:T(8,128)(2,1)}, u32[]{:S(2)}, u32[]{:S(2)}) collective-permute-start(bf16[8,128,128]{2,1,0:T(8,128)(2,1)} %broadcast_select_fusion.1), channel_id=1, source_target_pairs={{0,12},{4,16},{8,20},{12,24},{16,28},{20,0},{24,4},{28,8},{1,13},{... | collective-permute-start | bytes 786440 | tf_op jit(solution)/shard_map/ppermute | solution.py:9
  146.6 47.0 %collective-permute-start.17 = (bf16[8,128,128]{2,1,0:T(8,128)(2,1)}, bf16[8,128,128]{2,1,0:T(8,128)(2,1)S(1)}, u32[]{:S(2)}, u32[]{:S(2)}) collective-permute-start(bf16[8,128,128]{2,1,0:T(8,128)(2,1)} %broadcast_select_fusion), channel_id=1, source_target_pairs={{0,8},{4,12},{8,16},{12,20},{16,24},{20,28},{24,0},{28,4},{1,9},{5... | collective-permute-start | bytes 786440 | tf_op jit(solution)/shard_map/ppermute | solution.py:9
  191.5 6.2 %copy-start.3 = (f32[8,128,128]{2,0,1:T(8,128)S(1)}, f32[8,128,128]{2,0,1:T(8,128)}, u32[]{:S(2)}) copy-start(f32[8,128,128]{2,0,1:T(8,128)} %fusion.4) | copy-start | bytes 1572868
  197.7 1.5 copy-start.4
  199.5 1.0 copy-start.5
  199.9 1.1 copy-start.6
Sparse Core Ops, SparseCore 0:
  72.6 28.6 reduce-scatter.1
  103.6 16.7 all-gather.1
  144.0 92.5 all-reduce.1
where the time goes:
time: 246 us; the launch traced here: 245 us
  waiting for transfers between devices  130 us (53%)
  matrix products  35.8 us (15%)
  local copies, waits for them, and re-layouts  28.7 us (12%)
  starting transfers between devices  26.6 us (11%)
  between operations  14.4 us (6%)
  other arithmetic  8.98 us (4%)
    ppermute x18, waiting for transfers between devices, shifted(): lax.ppermute(x, axis, [(i, (i + by) % devices) for i in range(devices)])  52.5 us
    psum x1, waiting for transfers between devices, body(): grad_all = lax.psum(grad_local, 'dom')  34.3 us
    reduce_scatter x1, waiting for transfers between devices, body(): lax.psum_scatter(lax.dot_general(weights, stacked, (((0,), (1,)), ((), ()...  27.7 us
    ppermute x18, starting transfers between devices, shifted(): lax.ppermute(x, axis, [(i, (i + by) % devices) for i in range(devices)])  26.5 us
    all_gather x1, waiting for transfers between devices, body(): lax.all_gather(dpre, 'feat', axis=1, tiled=True)  16 us
    dot_general x7, matrix products, tile_apply_back(): jnp.einsum('kji,kjf->kif', tiles, blocks, preferred_element_type=jnp.floa...  11.6 us
    dot_general x14, matrix products, spread(): jnp.einsum('kc,kif->cif', table, parts, precision=lax.Precision.HIGHEST)  9.15 us
    dot_general x7, local copies, waits for them, and re-layouts, tile_apply_back(): jnp.einsum('kji,kjf->kif', tiles, blocks, preferred_element_type=jnp.floa...  9.07 us
  transfers between devices with their start and end apart: 21, of which 7 were waited for; matrix products, arithmetic and copies ran while one was open for 22% of the time, Pallas kernels for 0%

commit v1 on v0

v1 whole, which is shorter than its diff:
```python
import functools

import jax
import jax.numpy as jnp
from jax import lax
from jax.experimental import pallas as pl
from jax.experimental.pallas import tpu as pltpu
from jax.sharding import PartitionSpec as P

F32 = jnp.float32
BF16 = jnp.bfloat16
VMEM = pl.BlockSpec(memory_space=pltpu.VMEM)
SMEM = pl.BlockSpec(memory_space=pltpu.SMEM)


def shifted(x, axis, by):
    devices = lax.axis_size(axis)
    return lax.ppermute(x, axis, [(i, (i + by) % devices) for i in range(devices)])


def spread(parts, block_ids, count):
    table = (block_ids[:, None] == jnp.arange(count, dtype=jnp.int32)[None, :]).astype(F32)
    return jnp.einsum("kc,kif->cif", table, parts, precision=lax.Precision.HIGHEST)


def tile_apply(tiles, blocks):
    return jnp.einsum("kij,kjf->kif", tiles, blocks, preferred_element_type=F32)


def tile_apply_back(tiles, blocks):
    return jnp.einsum("kji,kjf->kif", tiles, blocks, preferred_element_type=F32)


def round_offsets(parts_total, rounds):
    return [(step + 1) * parts_total // (rounds + 1) for step in range(rounds)]


def sparse_body(
    features,
    w_self,
    w_neigh,
    degree,
    local_vals,
    local_dst,
    local_src,
    remote_vals,
    remote_dst,
    remote_src,
    cotangent,
):
    rows, width = features.shape
    block = local_vals.shape[-1]
    nblocks = rows // block
    rounds = remote_vals.shape[1]
    parts_total = lax.axis_size("dom")
    offsets = round_offsets(parts_total, rounds)
    blocks = features.reshape(nblocks, block, width)
    totals = spread(
        tile_apply(local_vals[0], jnp.take(blocks, local_src[0], axis=0)), local_dst[0], nblocks
    )
    arrived_ids = []
    for step in range(rounds):
        partial_blocks = tile_apply(
            remote_vals[0, step], jnp.take(blocks, remote_src[0, step], axis=0)
        ).astype(BF16)
        arrived, block_ids = shifted((partial_blocks, remote_dst[0, step]), "dom", offsets[step])
        arrived_ids.append(block_ids)
        totals = totals + spread(arrived.astype(F32), block_ids, nblocks)
    inverse = 1.0 / degree.astype(F32)
    agg = (totals.reshape(rows, width) * inverse[:, None]).astype(BF16)
    stacked = jnp.concatenate([features, agg], axis=1)
    weights = jnp.concatenate([w_self, w_neigh], axis=0)
    pre = lax.psum_scatter(
        lax.dot_general(weights, stacked, (((0,), (1,)), ((), ())), preferred_element_type=F32),
        "feat",
        scatter_dimension=0,
        tiled=True,
    ).T
    sigma = jax.nn.sigmoid(pre)
    out = (pre * sigma).astype(BF16)
    dpre = (cotangent.astype(F32) * sigma * (1.0 + pre * (1.0 - sigma))).astype(BF16)
    dpre_all = lax.all_gather(dpre, "feat", axis=1, tiled=True)
    dz_total = lax.dot_general(
        dpre_all, weights, (((1,), (1,)), ((), ())), preferred_element_type=F32
    )
    grad_local = lax.dot_general(
        stacked, dpre_all, (((0,), (0,)), ((), ())), preferred_element_type=F32
    )
    dx_self = dz_total[:, :width]
    dsum = (dz_total[:, width:] * inverse[:, None]).astype(BF16).reshape(nblocks, block, width)
    grad_all = lax.psum(grad_local, "dom")
    back = spread(
        tile_apply_back(local_vals[0], jnp.take(dsum, local_dst[0], axis=0)), local_src[0], nblocks
    )
    for step in range(rounds):
        picked = jnp.take(dsum, arrived_ids[step], axis=0)
        returned = shifted(picked, "dom", parts_total - offsets[step])
        back = back + spread(
            tile_apply_back(remote_vals[0, step], returned), remote_src[0, step], nblocks
        )
    grad_x = dx_self + back.reshape(rows, width)
    return (out, grad_x, grad_all[:width], grad_all[width:])


def forward_tiles_kernel(
    offsets, me_ref, ldst, lsrc, rdst, rsrc, x_ref, lvals, rvals, send_ref, local_ref, prod, acc
):
    parts_total = send_ref.shape[0]
    nblocks = x_ref.shape[0]
    me = me_ref[0]
    groups = rvals.shape[1]

    def product(tile, src):
        return jnp.dot(tile, x_ref[src], preferred_element_type=F32)

    filled = set(offsets) | {0}
    for offset in range(parts_total):
        if offset not in filled:
            send_ref[lax.rem(me + offset, parts_total)] = jnp.zeros(send_ref.shape[1:], BF16)
    for step, offset in enumerate(offsets):
        slot = step % 2
        for k in range(groups):
            prod[slot, k] = product(rvals[step, k], rsrc[0, step, k])
        acc[slot] = jnp.zeros(acc.shape[1:], F32)
        for k in range(groups):
            dst = rdst[0, step, k]
            acc[slot, dst] = acc[slot, dst] + prod[slot, k]
        send_ref[lax.rem(me + offset, parts_total)] = acc[slot].astype(BF16)
    local_ref[...] = jnp.zeros_like(local_ref)
    tiles = lvals.shape[0]
    for start in range(0, tiles, groups):
        slot = (start // groups + len(offsets)) % 2
        ks = range(start, min(start + groups, tiles))
        for k in ks:
            prod[slot, k - start] = product(lvals[k], lsrc[0, k])
        for k in ks:
            dst = ldst[0, k]
            local_ref[dst] = local_ref[dst] + prod[slot, k - start]
    send_ref[me] = jnp.zeros(send_ref.shape[1:], BF16)


def forward_tiles(offsets, parts_total, me, ldst, lsrc, rdst, rsrc, blocks, lvals, rvals):
    nblocks, block, width = blocks.shape
    groups = rvals.shape[1]
    return pl.pallas_call(
        functools.partial(forward_tiles_kernel, offsets),
        out_shape=(
            jax.ShapeDtypeStruct((parts_total, nblocks, block, width), BF16),
            jax.ShapeDtypeStruct((nblocks, block, width), F32),
        ),
        in_specs=[SMEM] * 5 + [VMEM] * 3,
        out_specs=(VMEM, VMEM),
        scratch_shapes=[
            pltpu.VMEM((2, groups, block, width), F32),
            pltpu.VMEM((2, nblocks, block, width), F32),
        ],
        compiler_params=pltpu.CompilerParams(vmem_limit_bytes=24 * 2**20),
    )(me, ldst, lsrc, rdst, rsrc, blocks, lvals, rvals)


def backward_tiles_kernel(
    offsets, me_ref, ldst, lsrc, rdst, rsrc, d_ref, own_ref, lvals, rvals, grad_ref, prod
):
    parts_total = d_ref.shape[0]
    me = me_ref[0]
    groups = rvals.shape[1]

    def product(tile, blk):
        return lax.dot_general(
            tile, blk, (((0,), (0,)), ((), ())), preferred_element_type=F32
        )

    grad_ref[...] = own_ref[...]
    for step, offset in enumerate(offsets):
        slot = step % 2
        other = lax.rem(me + offset, parts_total)
        for k in range(groups):
            prod[slot, k] = product(rvals[step, k], d_ref[other, rdst[0, step, k]])
        for k in range(groups):
            src = rsrc[0, step, k]
            grad_ref[src] = grad_ref[src] + prod[slot, k]
    tiles = lvals.shape[0]
    for start in range(0, tiles, groups):
        slot = (start // groups + len(offsets)) % 2
        ks = range(start, min(start + groups, tiles))
        for k in ks:
            prod[slot, k - start] = product(lvals[k], d_ref[me, ldst[0, k]])
        for k in ks:
            src = lsrc[0, k]
            grad_ref[src] = grad_ref[src] + prod[slot, k - start]


def backward_tiles(offsets, me, ldst, lsrc, rdst, rsrc, dsum_all, own, lvals, rvals):
    nblocks, block, width = own.shape
    groups = rvals.shape[1]
    return pl.pallas_call(
        functools.partial(backward_tiles_kernel, offsets),
        out_shape=jax.ShapeDtypeStruct((nblocks, block, width), F32),
        in_specs=[SMEM] * 5 + [VMEM] * 4,
        out_specs=VMEM,
        scratch_shapes=[pltpu.VMEM((2, groups, block, width), F32)],
        compiler_params=pltpu.CompilerParams(vmem_limit_bytes=24 * 2**20),
    )(me, ldst, lsrc, rdst, rsrc, dsum_all, own, lvals, rvals)


def joined(ref):
    return jnp.concatenate([ref[j] for j in range(ref.shape[0])], axis=1)


def dense_kernel(f_ref, a_ref, c_ref, ws_ref, wn_ref, inv_ref, out_ref, dpre_ref, dsum_ref):
    feats, _, width = f_ref.shape
    pre = jnp.dot(joined(f_ref), ws_ref[...], preferred_element_type=F32)
    pre = pre + jnp.dot(joined(a_ref), wn_ref[...], preferred_element_type=F32)
    sigma = 1.0 / (1.0 + jnp.exp(-pre))
    out = (pre * sigma).astype(BF16)
    dpre = (joined(c_ref).astype(F32) * sigma * (1.0 + pre * (1.0 - sigma))).astype(BF16)
    dagg = lax.dot_general(
        dpre, wn_ref[...], (((1,), (1,)), ((), ())), preferred_element_type=F32
    )
    dsum = (dagg * inv_ref[...]).astype(BF16)
    dpre_ref[...] = dpre
    for j in range(feats):
        out_ref[j] = out[:, j * width : (j + 1) * width]
        dsum_ref[j] = dsum[:, j * width : (j + 1) * width]


def dense(f_rows, a_rows, c_rows, ws_all, wn_all, inv_rows):
    feats, some, width = f_rows.shape
    return pl.pallas_call(
        dense_kernel,
        out_shape=(
            jax.ShapeDtypeStruct((feats, some, width), BF16),
            jax.ShapeDtypeStruct((some, feats * width), BF16),
            jax.ShapeDtypeStruct((feats, some, width), BF16),
        ),
        in_specs=[VMEM] * 6,
        out_specs=(VMEM, VMEM, VMEM),
        compiler_params=pltpu.CompilerParams(vmem_limit_bytes=24 * 2**20),
    )(f_rows, a_rows, c_rows, ws_all, wn_all, inv_rows)


def swap_feat(x):
    return lax.all_to_all(x, "feat", split_axis=0, concat_axis=0, tiled=True)


def dense_body(
    features,
    w_self,
    w_neigh,
    degree,
    local_vals,
    local_dst,
    local_src,
    remote_vals,
    remote_dst,
    remote_src,
    cotangent,
):
    rows, width = features.shape
    block = local_vals.shape[-1]
    nblocks = rows // block
    rounds = remote_vals.shape[1]
    parts_total = lax.axis_size("dom")
    feats = lax.axis_size("feat")
    some = rows // feats
    offsets = round_offsets(parts_total, rounds)
    me = lax.axis_index("dom").astype(jnp.int32).reshape(1)
    mine = lax.axis_index("feat").astype(jnp.int32)
    inverse = 1.0 / degree.astype(F32)
    inv_rows = lax.dynamic_slice(inverse, (mine * some,), (some,))[:, None]

    weights = lax.all_gather(jnp.stack([w_self, w_neigh]), "feat", axis=1, tiled=True)
    early = swap_feat(
        jnp.stack(
            [features.reshape(feats, some, width), cotangent.reshape(feats, some, width)], axis=1
        )
    )
    ids = (local_dst, local_src, remote_dst, remote_src)
    send, local_sum = forward_tiles(
        offsets,
        parts_total,
        me,
        *ids,
        features.reshape(nblocks, block, width),
        local_vals[0],
        remote_vals[0],
    )
    arrived = lax.psum_scatter(send, "dom", scatter_dimension=0, tiled=True)
    sums = local_sum + arrived[0].astype(F32)
    agg = (sums.reshape(rows, width) * inverse[:, None]).astype(BF16)
    agg_rows = swap_feat(agg.reshape(feats, some, width))
    out_rows, dpre_rows, dsum_rows = dense(
        early[:, 0], agg_rows, early[:, 1], weights[0], weights[1], inv_rows
    )
    dsum = swap_feat(dsum_rows)
    dsum_all = lax.all_gather(dsum.reshape(nblocks, block, width), "dom", axis=0, tiled=False)
    dpre = lax.all_gather(dpre_rows, "feat", axis=0, tiled=True)
    out = swap_feat(out_rows).reshape(rows, width)
    dx_self = lax.dot_general(dpre, w_self, (((1,), (1,)), ((), ())), preferred_element_type=F32)
    grad_local = lax.dot_general(
        jnp.concatenate([features, agg], axis=1),
        dpre,
        (((0,), (0,)), ((), ())),
        preferred_element_type=F32,
    )
    grad_all = lax.psum(grad_local, "dom")
    grad_x = backward_tiles(
        offsets,
        me,
        *ids,
        dsum_all,
        dx_self.reshape(nblocks, block, width),
        local_vals[0],
        remote_vals[0],
    )
    return (out, grad_x.reshape(rows, width), grad_all[:width], grad_all[width:])


def solution(mesh):
    def body(*args):
        rounds = args[7].shape[1]
        nearly_all = mesh.shape["dom"] <= rounds + 2
        return (dense_body if nearly_all else sparse_body)(*args)

    placed = (
        P("dom", "feat"),
        P("feat", None),
        P("feat", None),
        P("dom"),
        P("dom", None, None, None),
        P("dom", None),
        P("dom", None),
        P("dom", None, None, None, None),
        P("dom", None, None),
        P("dom", None, None),
        P("dom", "feat"),
    )
    return jax.shard_map(
        body,
        mesh=mesh,
        in_specs=placed,
        out_specs=(P("dom", "feat"), P("dom", "feat"), P("feat", None), P("feat", None)),
        check_vma=False,
    )
```

time: 246 us -> 254 us (1.033)
  waiting for transfers between devices: 130 us -> 186 us
  matrix products: 35.8 us -> 4.13 us
  starting transfers between devices: 26.6 us -> 7.82 us
  blocking collectives: 0 us -> 17.7 us
  local copies, waits for them, and re-layouts: 28.7 us -> 11.8 us
  Pallas kernels: 0 us -> 7.21 us
  other arithmetic: 8.98 us -> 3.69 us
    ppermute x18 -> x0, waiting for transfers between devices: 52.5 us -> none  [shifted(): lax.ppermute(x, axis, [(i, (i + by) % devices) for i in range(devices)])]
    all_gather x1 -> x3, waiting for transfers between devices: 16 us -> 63.6 us  [the longest x1 49.1 us: dense_body(): lax.all_gather(dsum.reshape(nblocks, block, width), 'dom', axis=0, tiled=...]
    dot_general x31 -> x2, matrix products: 35.8 us -> 4.13 us  [the longest x1 2.47 us: dense_body(): lax.dot_general(jnp.concatenate([features, agg], axis=1), dpre, (((0,), (...]
    reduce_scatter x1, waiting for transfers between devices: 27.7 us -> 55.7 us  [dense_body(): arrived = lax.psum_scatter(send, 'dom', scatter_dimension=0, tiled=True)]
    ppermute x18 -> x0, starting transfers between devices: 26.5 us -> none  [shifted(): lax.ppermute(x, axis, [(i, (i + by) % devices) for i in range(devices)])]
    psum x1, waiting for transfers between devices: 34.3 us -> 53.1 us  [dense_body(): grad_all = lax.psum(grad_local, 'dom')]
    all_to_all x0 -> x2, blocking collectives: none -> 17.7 us  [swap_feat(): return lax.all_to_all(x, 'feat', split_axis=0, concat_axis=0, tiled=True)]
    all_to_all x0 -> x2, waiting for transfers between devices: none -> 13.3 us  [swap_feat(): return lax.all_to_all(x, 'feat', split_axis=0, concat_axis=0, tiled=True)]
  transfers between devices with their start and end apart: 21 -> 7, of which waited for: 7 -> 6; matrix products, arithmetic and copies ran while one was open for 22% -> 3% of each run, Pallas kernels for 0% -> 0%
where the time goes in v1:
time: 254 us; the launch traced here: 253 us
  waiting for transfers between devices  186 us (73%)
  blocking collectives  17.7 us (7%)
  between operations  15.3 us (6%)
  local copies, waits for them, and re-layouts  11.8 us (5%)
  starting transfers between devices  7.82 us (3%)
  Pallas kernels  7.21 us (3%)
  matrix products  4.13 us (2%)
  other arithmetic  3.69 us (1%)
    reduce_scatter x1, waiting for transfers between devices, dense_body(): arrived = lax.psum_scatter(send, 'dom', scatter_dimension=0, tiled=True)  55.7 us
    psum x1, waiting for transfers between devices, dense_body(): grad_all = lax.psum(grad_local, 'dom')  53.1 us
    all_gather x1, waiting for transfers between devices, dense_body(): lax.all_gather(dsum.reshape(nblocks, block, width), 'dom', axis=0, tiled=...  49.1 us
    all_to_all x2, blocking collectives, swap_feat(): return lax.all_to_all(x, 'feat', split_axis=0, concat_axis=0, tiled=True)  17.7 us
    all_gather x1, waiting for transfers between devices, dense_body(): dpre = lax.all_gather(dpre_rows, 'feat', axis=0, tiled=True)  14.5 us
    all_to_all x2, waiting for transfers between devices, swap_feat(): return lax.all_to_all(x, 'feat', split_axis=0, concat_axis=0, tiled=True)  13.3 us
    unnamed x33, local copies, waits for them, and re-layouts  8.41 us
    all_to_all x2, starting transfers between devices, swap_feat(): return lax.all_to_all(x, 'feat', split_axis=0, concat_axis=0, tiled=True)  7.61 us
  transfers between devices with their start and end apart: 7, of which 6 were waited for; matrix products, arithmetic and copies ran while one was open for 3% of the time, Pallas kernels for 0%

profile of v1, /device:TPU:0, one launch (start us, length us, event | category | flops | bytes accessed | tf_op | source)
XLA Modules:
  0.0 253.5 jit_solution(9622498964251959785)
XLA Ops:
  8.0 0.0 reduce-scatter.2.cloned.1.call-start
  8.0 0.7 copy.25.rdst
  8.7 0.7 copy.26.rsrc
  9.4 0.0 copy-start
  9.4 1.4 copy-done
  10.8 0.0 copy-start.2
  10.8 1.0 copy-done.2
  11.9 0.0 copy-start.5
  11.9 0.9 copy-done.5
  12.8 0.0 copy-start.7
  12.8 0.7 copy-done.7
  13.5 0.0 copy-start.9
  13.5 0.7 copy-done.9
  14.1 0.0 copy-start.11
  14.1 3.5 %shard_map.138 = (bf16[8,8,128,128]{3,2,1,0:T(8,128)(2,1)}, f32[8,128,128]{2,1,0:T(8,128)S(1)}) custom-call(s32[1]{0:T(128)} %bitcast.3.me_ref, s32[1,16]{1,0:T(1,128)S(1)} %copy-done.7, s32[1,16]{1,0:T(1,128)S(1)} %copy-done.9, s32[1,6,8]{2,1,0:T(8,128)S(1)} %copy.25.rdst, s32[1,6,8]{2,1,0:T(8,128)S(1)} %copy.26.rsrc, bf16[8,128,128]{2,1,0:T(8,128)(2,1)S(1)} %bitcast.45, ...), custom_call_target="tpu_custom_call" | custom-call | tf_op jit(solution)/shard_map/pallas_call | solution.py:145
  17.6 0.0 reduce-scatter.2.cloned.1.call-update
  17.6 0.0 all-gather.4.cloned.1.call-start
  17.7 0.0 copy-done.11
  17.7 0.0 copy-done.13
  17.7 0.7 pad_maximum_fusion.1
  18.4 0.0 all-gather.4.cloned.1.call-update
  18.5 0.0 copy-done.6
  18.5 0.0 copy-done.12
  18.5 0.8 pad_maximum_fusion
  19.3 4.2 %all-to-all-start = ((bf16[4,2,256,128]{3,2,1,0:T(8,128)(2,1)}), bf16[4,2,256,128]{3,2,1,0:T(8,128)(2,1)S(1)}, u32[]{:S(2)}, u32[]{:S(2)}) async-start(bf16[4,2,256,128]{3,2,1,0:T(8,128)(2,1)} %pad_maximum_fusion), calls=%async_computation | async-start | bytes 1048576 | tf_op jit(solution)/shard_map/all_to_all | solution.py:243
  23.5 0.0 copy-done.14
  23.5 0.1 dynamic_slice.3
  23.6 0.1 copy.28.inv_ref
  23.8 8.6 %all-to-all-done = bf16[4,2,256,128]{3,2,1,0:T(8,128)(2,1)S(1)} async-done(((bf16[4,2,256,128]{3,2,1,0:T(8,128)(2,1)}), bf16[4,2,256,128]{3,2,1,0:T(8,128)(2,1)S(1)}, u32[]{:S(2)}, u32[]{:S(2)}) %all-to-all-start) | async-done | bytes 524320 | tf_op jit(solution)/shard_map/all_to_all | solution.py:243
  32.4 55.7 %reduce-scatter.2.cloned.1.call-done = bf16[1,8,128,128]{3,2,1,0:T(8,128)(2,1)} async-done(((bf16[8,8,128,128]{3,2,1,0:T(8,128)(2,1)}), bf16[1,8,128,128]{3,2,1,0:T(8,128)(2,1)}) %reduce-scatter.2.cloned.1.call-update) | async-done | bytes 262160 | tf_op jit(solution)/shard_map/reduce_scatter | solution.py:288
  88.2 1.0 convert_add_fusion
  89.2 0.9 fusion.5
  90.1 3.4 %all-to-all-start.1 = ((bf16[4,256,128]{2,1,0:T(8,128)(2,1)}), bf16[4,256,128]{2,1,0:T(8,128)(2,1)S(1)}, u32[]{:S(2)}, u32[]{:S(2)}) async-start(bf16[4,256,128]{2,1,0:T(8,128)(2,1)} %fusion.5), calls=%async_computation.2 | async-start | bytes 524288 | tf_op jit(solution)/shard_map/all_to_all | solution.py:243
  93.5 0.0 all-gather.8.cloned.1.call-start
  93.5 0.0 all-gather.4.cloned.1.call-done
  93.6 1.3 slice_bitcast_fusion
  94.8 4.6 %all-to-all-done.1.a_ref = bf16[4,256,128]{2,1,0:T(8,128)(2,1)S(1)} async-done(((bf16[4,256,128]{2,1,0:T(8,128)(2,1)}), bf16[4,256,128]{2,1,0:T(8,128)(2,1)S(1)}, u32[]{:S(2)}, u32[]{:S(2)}) %all-to-all-start.1) | async-done | bytes 262176 | tf_op jit(solution)/shard_map/all_to_all | solution.py:243
  99.5 1.4 shard_map.139
  100.8 0.0 all-gather.8.cloned.1.call-update
  100.9 0.0 all-reduce.2.cloned.1.call-start
  100.9 0.2 fusion.4
  101.1 14.5 %all-gather.8.cloned.1.call-done = bf16[1024,512]{1,0:T(8,128)(2,1)} async-done(((bf16[256,512]{1,0:T(8,128)(2,1)}), bf16[1024,512]{1,0:T(8,128)(2,1)}) %all-gather.8.cloned.1.call-update) | async-done | bytes 1048592 | tf_op jit(solution)/shard_map/all_gather | solution.py:297
  115.6 2.5 fusion
  118.1 0.0 all-reduce.2.cloned.1.call-update
  118.1 0.0 copy-start.1
  118.1 0.0 copy-start.3
  118.1 0.0 copy-start.8
  118.2 0.0 copy-start.10
  118.2 0.0 all-gather.6.cloned.1.call-start
  118.2 9.2 %all_to_all.20 = bf16[4,256,128]{2,1,0:T(8,128)(2,1)} all-to-all(bf16[4,256,128]{2,1,0:T(8,128)(2,1)S(1)} %get-tuple-element.12), channel_id=1, replica_groups=mesh['dom'=8,'feat'=4] {'feat'}, dimensions={0} | all-to-all | bytes 524288 | tf_op jit(solution)/shard_map/all_to_all | solution.py:243
  127.5 0.0 all-gather.6.cloned.1.call-update
  127.5 8.4 %all_to_all.21 = bf16[4,256,128]{2,1,0:T(8,128)(2,1)S(1)} all-to-all(bf16[4,256,128]{2,1,0:T(8,128)(2,1)S(1)} %get-tuple-element.11), channel_id=1, replica_groups=mesh['dom'=8,'feat'=4] {'feat'}, dimensions={0} | all-to-all | bytes 524288 | tf_op jit(solution)/shard_map/all_to_all | solution.py:243
  135.9 1.7 fusion.8
  137.6 53.1 %all-reduce.2.cloned.1.call-done = f32[256,512]{1,0:T(8,128)} async-done(((f32[256,512]{1,0:T(8,128)}), f32[256,512]{1,0:T(8,128)}) %all-reduce.2.cloned.1.call-update) | async-done | bytes 524304 | tf_op jit(solution)/shard_map/psum | solution.py:306
  190.7 1.9 fusion.7
  192.5 49.1 %all-gather.6.cloned.1.call-done.d_ref = bf16[8,8,128,128]{3,2,1,0:T(8,128)(2,1)} async-done(((bf16[1,8,128,128]{3,2,1,0:T(8,128)(2,1)}), bf16[8,8,128,128]{3,2,1,0:T(8,128)(2,1)}) %all-gather.6.cloned.1.call-update) | async-done | bytes 2097168 | tf_op jit(solution)/shard_map/all_gather | solution.py:296
  241.6 0.0 copy-done.1
  241.6 0.0 copy-done.3
  241.6 0.0 copy-done.8
  241.6 0.0 copy-done.10
  241.6 0.0 copy-start.4
  241.7 1.6 copy-done.4
  243.2 2.4 shard_map.140
  245.6 0.7 copy.35
  (7 shorter events, 0.1 us)
Async XLA Ops:
  8.0 80.2 %reduce-scatter.2.cloned.1.call-start = ((), (), s32[]{:S(2)}) async-start(), calls=%async_computation.5 | async-start | bytes 2359296 | tf_op jit(solution)/shard_map/reduce_scatter | solution.py:288
  9.4 1.4 copy-start
  10.8 1.0 copy-start.2
  11.9 0.9 copy-start.5
  12.8 0.7 copy-start.7
  13.5 0.7 copy-start.9
  14.1 3.6 %copy-start.11 = (bf16[128,512]{1,0:T(8,128)(2,1)S(1)}, bf16[128,512]{1,0:T(8,128)(2,1)}, u32[]{:S(2)}) copy-start(bf16[128,512]{1,0:T(8,128)(2,1)} %param.12) | copy-start | bytes 393220
  14.1 3.6 %copy-start.13 = (bf16[128,512]{1,0:T(8,128)(2,1)S(1)}, bf16[128,512]{1,0:T(8,128)(2,1)}, u32[]{:S(2)}) copy-start(bf16[128,512]{1,0:T(8,128)(2,1)} %param.13) | copy-start | bytes 393220
  14.1 4.3 %copy-start.6 = (bf16[1024,128]{1,0:T(8,128)(2,1)S(1)}, bf16[1024,128]{1,0:T(8,128)(2,1)}, u32[]{:S(2)}) copy-start(bf16[1024,128]{1,0:T(8,128)(2,1)} %param.11) | copy-start | bytes 786436
  14.1 4.3 %copy-start.12 = (bf16[1024,128]{1,0:T(8,128)(2,1)S(1)}, bf16[1024,128]{1,0:T(8,128)(2,1)}, u32[]{:S(2)}) copy-start(bf16[1024,128]{1,0:T(8,128)(2,1)} %param.21) | copy-start | bytes 786436
  17.6 5.9 %copy-start.14 = (s32[1024]{0:T(1024)S(1)}, s32[1024]{0:T(1024)}, u32[]{:S(2)}) copy-start(s32[1024]{0:T(1024)} %param.14) | copy-start | bytes 12292
  17.6 75.9 %all-gather.4.cloned.1.call-start = ((), (), s32[]{:S(2)}) async-start(), calls=%async_computation.6 | async-start | bytes 1310720 | tf_op jit(solution)/shard_map/all_gather | solution.py:272
  19.3 13.1 %all-to-all-start = ((bf16[4,2,256,128]{3,2,1,0:T(8,128)(2,1)}), bf16[4,2,256,128]{3,2,1,0:T(8,128)(2,1)S(1)}, u32[]{:S(2)}, u32[]{:S(2)}) async-start(bf16[4,2,256,128]{3,2,1,0:T(8,128)(2,1)} %pad_maximum_fusion), calls=%async_computation | async-start | bytes 1048576 | tf_op jit(solution)/shard_map/all_to_all | solution.py:243
  90.1 9.4 %all-to-all-start.1 = ((bf16[4,256,128]{2,1,0:T(8,128)(2,1)}), bf16[4,256,128]{2,1,0:T(8,128)(2,1)S(1)}, u32[]{:S(2)}, u32[]{:S(2)}) async-start(bf16[4,256,128]{2,1,0:T(8,128)(2,1)} %fusion.5), calls=%async_computation.2 | async-start | bytes 524288 | tf_op jit(solution)/shard_map/all_to_all | solution.py:243
  93.5 22.1 %all-gather.8.cloned.1.call-start = ((), (), s32[]{:S(2)}) async-start(), calls=%async_computation.8 | async-start | bytes 1310720 | tf_op jit(solution)/shard_map/all_gather | solution.py:297
  100.9 89.8 %all-reduce.2.cloned.1.call-start = ((), (), s32[]{:S(2)}) async-start(), calls=%async_computation.9 | async-start | bytes 1048576 | tf_op jit(solution)/shard_map/psum | solution.py:306
  118.1 123.5 %copy-start.1 = (bf16[1,6,8,128,128]{4,3,2,1,0:T(8,128)(2,1)S(1)}, bf16[1,6,8,128,128]{4,3,2,1,0:T(8,128)(2,1)}, u32[]{:S(2)}) copy-start(bf16[1,6,8,128,128]{4,3,2,1,0:T(8,128)(2,1)} %param.18) | copy-start | bytes 4718596
  118.1 123.5 %copy-start.3 = (bf16[1,16,128,128]{3,2,1,0:T(8,128)(2,1)S(1)}, bf16[1,16,128,128]{3,2,1,0:T(8,128)(2,1)}, u32[]{:S(2)}) copy-start(bf16[1,16,128,128]{3,2,1,0:T(8,128)(2,1)} %param.15) | copy-start | bytes 1572868
  118.1 123.5 %copy-start.8 = (s32[1,16]{1,0:T(1,128)S(1)}, s32[1,16]{1,0:T(1,128)}, u32[]{:S(2)}) copy-start(s32[1,16]{1,0:T(1,128)} %ldst.3) | copy-start | bytes 196
  118.2 123.5 %copy-start.10 = (s32[1,16]{1,0:T(1,128)S(1)}, s32[1,16]{1,0:T(1,128)}, u32[]{:S(2)}) copy-start(s32[1,16]{1,0:T(1,128)} %lsrc.3) | copy-start | bytes 196
  118.2 123.5 %all-gather.6.cloned.1.call-start = ((), (), s32[]{:S(2)}) async-start(), calls=%async_computation.7 | async-start | bytes 2359296 | tf_op jit(solution)/shard_map/all_gather | solution.py:296
  241.6 1.6 copy-start.4
Sparse Core Ops, SparseCore 0:
  17.8 70.3 reduce-scatter.1
  118.2 72.3 all-reduce.1
  193.0 48.5 all-gather.5
Sparse Core Ops, SparseCore 1:
  20.2 19.3 all-gather.3
  101.0 14.6 all-gather.7

commit v2 on v0

v2 whole, which is shorter than its diff:
```python
import functools

import jax
import jax.numpy as jnp
from jax import lax
from jax.experimental import pallas as pl
from jax.experimental.pallas import tpu as pltpu
from jax.sharding import PartitionSpec as P

F32 = jnp.float32
BF16 = jnp.bfloat16
VMEM = pl.BlockSpec(memory_space=pltpu.VMEM)
SMEM = pl.BlockSpec(memory_space=pltpu.SMEM)


def shifted(x, axis, by):
    devices = lax.axis_size(axis)
    return lax.ppermute(x, axis, [(i, (i + by) % devices) for i in range(devices)])


def spread(parts, block_ids, count):
    table = (block_ids[:, None] == jnp.arange(count, dtype=jnp.int32)[None, :]).astype(F32)
    return jnp.einsum("kc,kif->cif", table, parts, precision=lax.Precision.HIGHEST)


def tile_apply(tiles, blocks):
    return jnp.einsum("kij,kjf->kif", tiles, blocks, preferred_element_type=F32)


def tile_apply_back(tiles, blocks):
    return jnp.einsum("kji,kjf->kif", tiles, blocks, preferred_element_type=F32)


def round_offsets(parts_total, rounds):
    return [(step + 1) * parts_total // (rounds + 1) for step in range(rounds)]


def sparse_body(
    features,
    w_self,
    w_neigh,
    degree,
    local_vals,
    local_dst,
    local_src,
    remote_vals,
    remote_dst,
    remote_src,
    cotangent,
):
    rows, width = features.shape
    block = local_vals.shape[-1]
    nblocks = rows // block
    rounds = remote_vals.shape[1]
    parts_total = lax.axis_size("dom")
    offsets = round_offsets(parts_total, rounds)
    blocks = features.reshape(nblocks, block, width)
    totals = spread(
        tile_apply(local_vals[0], jnp.take(blocks, local_src[0], axis=0)), local_dst[0], nblocks
    )
    arrived_ids = []
    for step in range(rounds):
        partial_blocks = tile_apply(
            remote_vals[0, step], jnp.take(blocks, remote_src[0, step], axis=0)
        ).astype(BF16)
        arrived, block_ids = shifted((partial_blocks, remote_dst[0, step]), "dom", offsets[step])
        arrived_ids.append(block_ids)
        totals = totals + spread(arrived.astype(F32), block_ids, nblocks)
    inverse = 1.0 / degree.astype(F32)
    agg = (totals.reshape(rows, width) * inverse[:, None]).astype(BF16)
    stacked = jnp.concatenate([features, agg], axis=1)
    weights = jnp.concatenate([w_self, w_neigh], axis=0)
    pre = lax.psum_scatter(
        lax.dot_general(weights, stacked, (((0,), (1,)), ((), ())), preferred_element_type=F32),
        "feat",
        scatter_dimension=0,
        tiled=True,
    ).T
    sigma = jax.nn.sigmoid(pre)
    out = (pre * sigma).astype(BF16)
    dpre = (cotangent.astype(F32) * sigma * (1.0 + pre * (1.0 - sigma))).astype(BF16)
    dpre_all = lax.all_gather(dpre, "feat", axis=1, tiled=True)
    dz_total = lax.dot_general(
        dpre_all, weights, (((1,), (1,)), ((), ())), preferred_element_type=F32
    )
    grad_local = lax.dot_general(
        stacked, dpre_all, (((0,), (0,)), ((), ())), preferred_element_type=F32
    )
    dx_self = dz_total[:, :width]
    dsum = (dz_total[:, width:] * inverse[:, None]).astype(BF16).reshape(nblocks, block, width)
    grad_all = lax.psum(grad_local, "dom")
    back = spread(
        tile_apply_back(local_vals[0], jnp.take(dsum, local_dst[0], axis=0)), local_src[0], nblocks
    )
    for step in range(rounds):
        picked = jnp.take(dsum, arrived_ids[step], axis=0)
        returned = shifted(picked, "dom", parts_total - offsets[step])
        back = back + spread(
            tile_apply_back(remote_vals[0, step], returned), remote_src[0, step], nblocks
        )
    grad_x = dx_self + back.reshape(rows, width)
    return (out, grad_x, grad_all[:width], grad_all[width:])


def tile_counts(rvals, lvals):
    return rvals.shape[0], rvals.shape[1], lvals.shape[0]


def round_of(offset, offsets):
    step, known = jnp.int32(0), offset < 0
    for at, this in enumerate(offsets):
        step = jnp.where(offset == this, at, step)
        known = known | (offset == this)
    return step, known


def crossed_block(block_id, mine, per_feat):
    return ((block_id // per_feat) ^ mine) * per_feat + block_id % per_feat


def tile_groups(masks, offsets, parts_total, me, rounds, groups, tiles):
    ids_at = (2, 2 + tiles, 2 + 2 * tiles, 2 + 2 * tiles + rounds * groups)
    jobs = []
    for at, mask in enumerate(masks):
        if mask == 0:
            for first in range(0, tiles, groups):
                count = min(groups, tiles - first)
                jobs.append((at, None, None, first, count, ids_at[0] + first, ids_at[1] + first))
        else:
            offset = lax.rem((me ^ mask) - me + parts_total, parts_total)
            step, known = round_of(offset, offsets)
            base = step * groups
            jobs.append((at, step, known, None, groups, ids_at[2] + base, ids_at[3] + base))
    return jobs


def tiles_kernel(
    masks, offsets, parts_total, per_feat, me_ref, lvals, rvals, *refs
):
    back = per_feat is not None
    rounds, groups, tiles = tile_counts(rvals, lvals)
    me, mine = me_ref[0], me_ref[1]
    jobs = tile_groups(masks, offsets, parts_total, me, rounds, groups, tiles)
    held, prod, acc, sems = refs[-4:]
    if back:
        own_ref, grad_ref = refs[len(masks)], refs[len(masks) + 1]
        blocks = refs[: len(masks)]
        sinks = [grad_ref] * len(masks)
    else:
        blocks = [refs[0]] * len(masks)
        sinks = refs[1 : 1 + len(masks)]
    copies = []
    for slot, (at, step, known, first, count, dst_at, src_at) in enumerate(jobs):
        source = lvals.at[pl.ds(first, count)] if step is None else rvals.at[step]
        copy = pltpu.make_async_copy(source, held.at[slot, pl.ds(0, count)], sems.at[slot])
        copy.start()
        copies.append(copy)
    if back:
        acc[0] = own_ref[...]
    total = 0
    for slot, (at, step, known, first, count, dst_at, src_at) in enumerate(jobs):
        copies[slot].wait()
        half = slot % 2
        read_at, write_at = (dst_at, src_at) if back else (src_at, dst_at)
        for k in range(count):
            block_id = me_ref[read_at + k]
            if back:
                block_id = crossed_block(block_id, mine, per_feat)
            block = blocks[at][block_id]
            if back:
                product = lax.dot_general(
                    held[slot, k], block, (((0,), (0,)), ((), ())), preferred_element_type=F32
                )
            else:
                product = jnp.dot(held[slot, k], block, preferred_element_type=F32)
            prod[half, k] = product if known is None else jnp.where(known, product, 0.0)
        fresh = not back and (slot == 0 or jobs[slot - 1][0] != at)
        if fresh:
            total = at % 2
            acc[total] = jnp.zeros(acc.shape[1:], F32)
        for k in range(count):
            into = me_ref[write_at + k]
            acc[total, into] = acc[total, into] + prod[half, k]
        last = slot == len(jobs) - 1 or jobs[slot + 1][0] != at
        if last and (not back or slot == len(jobs) - 1):
            sinks[at][...] = acc[total].astype(sinks[at].dtype)


def tiles_call(masks, offsets, parts_total, per_feat, me, lvals, rvals, blocks, sinks):
    rounds, groups, tiles = tile_counts(rvals, lvals)
    nblocks, block, width = blocks[0].shape
    slots = sum(-(-tiles // groups) if mask == 0 else 1 for mask in masks)
    flops = 2 * slots * groups * block * block * width
    return pl.pallas_call(
        functools.partial(tiles_kernel, masks, offsets, parts_total, per_feat),
        out_shape=sinks,
        in_specs=[SMEM] + [pl.BlockSpec(memory_space=pltpu.HBM)] * 2 + [VMEM] * len(blocks),
        out_specs=jax.tree.map(lambda _: VMEM, sinks),
        scratch_shapes=[
            pltpu.VMEM((slots, groups, block, block), BF16),
            pltpu.VMEM((2, groups, block, width), F32),
            pltpu.VMEM((2, nblocks, block, width), F32),
            pltpu.SemaphoreType.DMA((slots,)),
        ],
        compiler_params=pltpu.CompilerParams(vmem_limit_bytes=24 * 2**20),
        cost_estimate=pl.CostEstimate(
            flops=4 * flops,
            bytes_accessed=slots * groups * block * block * 2 + 4 * rounds * nblocks * block * width,
            transcendentals=0,
        ),
    )(me, lvals, rvals, *blocks)


def small_call(kernel, outs, scalars, arrays, scratch=(), flops=10**6):
    size = sum(t.size * t.dtype.itemsize for t in list(arrays) + list(outs))
    return pl.pallas_call(
        kernel,
        out_shape=outs,
        in_specs=[SMEM] * len(scalars) + [VMEM] * len(arrays),
        out_specs=[VMEM] * len(outs),
        scratch_shapes=scratch,
        compiler_params=pltpu.CompilerParams(vmem_limit_bytes=24 * 2**20),
        cost_estimate=pl.CostEstimate(flops=flops, bytes_accessed=size, transcendentals=0),
    )(*scalars, *arrays)


def agg_kernel(feats, me_ref, inv_ref, keep_ref, *refs):
    mine = me_ref[1]
    far_refs, agg_ref, piece_refs = refs[: -1 - feats], refs[-1 - feats], refs[-feats:]
    per_feat = piece_refs[0].shape[0]
    sums = keep_ref[...]
    for ref in far_refs:
        sums = sums + ref[...].astype(F32)
    agg_ref[...] = (sums * inv_ref[...]).astype(BF16)
    for mask, piece in enumerate(piece_refs):
        piece[...] = agg_ref[pl.ds((mine ^ mask) * per_feat, per_feat)]


def joined(parts):
    return jnp.concatenate(parts, axis=1)


def dense_kernel(me_ref, early_ref, w_ref, inv_ref, *refs):
    mine = me_ref[1]
    feats, _, some, width = early_ref.shape
    a_refs, dpre_ref = refs[:feats], refs[feats]
    dsum_refs, out_refs = refs[feats + 1 : 2 * feats + 1], refs[2 * feats + 1 : 3 * feats + 1]
    held = refs[-1]
    full = feats * width
    ws = w_ref[0].reshape(full, full)
    wn = w_ref[1].reshape(full, full)
    pre = jnp.dot(joined([early_ref[j, 0] for j in range(feats)]), ws, preferred_element_type=F32)
    for mask in range(feats):
        pre = pre + jnp.dot(
            a_refs[mask][...].reshape(some, width),
            w_ref[1, mine ^ mask],
            preferred_element_type=F32,
        )
    sigma = 1.0 / (1.0 + jnp.exp(-pre))
    out = (pre * sigma).astype(BF16)
    cot = joined([early_ref[j, 1] for j in range(feats)]).astype(F32)
    dpre = (cot * sigma * (1.0 + pre * (1.0 - sigma))).astype(BF16)
    dagg = lax.dot_general(dpre, wn, (((1,), (1,)), ((), ())), preferred_element_type=F32)
    dsum = (dagg * inv_ref[...]).astype(BF16)
    dpre_ref[...] = dpre
    for j in range(feats):
        held[0, j] = dsum[:, j * width : (j + 1) * width]
        held[1, j] = out[:, j * width : (j + 1) * width]
    for mask in range(feats):
        dsum_refs[mask][...] = held[0, mine ^ mask]
        out_refs[mask][...] = held[1, mine ^ mask]


def grad_kernel(near, far, me_ref, f_ref, a_ref, dpre_ref, w_ref, dx_ref, give_ref, keep_ref, held):
    me = me_ref[0]
    dpre = dpre_ref[...]
    width = f_ref.shape[1]
    some = held.shape[1]
    for at, ref in enumerate((f_ref, a_ref)):
        part = lax.dot_general(
            ref[...], dpre, (((0,), (0,)), ((), ())), preferred_element_type=F32
        )
        for j in range(width // some):
            held[at * (width // some) + j] = part[j * some : (j + 1) * some]
    for at, mask in enumerate(far + [0]):
        give_ref[at] = held[me ^ mask ^ near].astype(BF16)
        keep_ref[at] = held[me ^ mask]
    dx_ref[...] = lax.dot_general(
        dpre, w_ref[...], (((1,), (1,)), ((), ())), preferred_element_type=F32
    )


def finish_kernel(near, far, me_ref, *refs):
    me = me_ref[0]
    count = len(far) + 1
    found, other_ref = refs[:count], refs[count]
    self_ref, neigh_ref, held = refs[count + 1 :]
    for at, mask in enumerate(far + [0]):
        held[me ^ mask] = found[at][...].astype(F32)
        held[me ^ mask ^ near] = other_ref[at].astype(F32)
    some = held.shape[1]
    half = held.shape[0] // 2
    for j in range(half):
        self_ref[j * some : (j + 1) * some] = held[j]
        neigh_ref[j * some : (j + 1) * some] = held[half + j]


def place_kernel(me_ref, *refs):
    mine = me_ref[1]
    out_ref = refs[-1]
    for mask, ref in enumerate(refs[:-1]):
        out_ref[mine ^ mask] = ref[...]


def swap_feat(x):
    return lax.all_to_all(x, "feat", split_axis=0, concat_axis=0, tiled=True)


def crossed(x, mask, axis="dom"):
    return lax.ppermute(x, axis, [(i, i ^ mask) for i in range(lax.axis_size(axis))])


def like(shape, dtype):
    return jax.ShapeDtypeStruct(shape, dtype)


def dense_body(
    features,
    w_self,
    w_neigh,
    degree,
    local_vals,
    local_dst,
    local_src,
    remote_vals,
    remote_dst,
    remote_src,
    cotangent,
):
    rows, width = features.shape
    block = local_vals.shape[-1]
    nblocks = rows // block
    rounds = remote_vals.shape[1]
    parts_total = lax.axis_size("dom")
    feats = lax.axis_size("feat")
    some = rows // feats
    per_feat = nblocks // feats
    full = feats * width
    offsets = round_offsets(parts_total, rounds)
    near, far = 1, list(range(parts_total - 2, 0, -2))
    mine = lax.axis_index("feat").astype(jnp.int32)
    inverse = 1.0 / degree.astype(F32)
    inv_rows = lax.dynamic_slice(inverse, (mine * some,), (some,))[:, None]
    me = jnp.concatenate(
        [lax.axis_index("dom").astype(jnp.int32).reshape(1), mine.reshape(1)]
        + [t.reshape(-1) for t in (local_dst, local_src, remote_dst, remote_src)]
    )
    shape = (nblocks, block, width)
    blocks = features.reshape(shape)
    fixed = (me, local_vals[0], remote_vals[0])

    sends = tiles_call(
        [mask ^ near for mask in far + [0]],
        offsets,
        parts_total,
        None,
        *fixed,
        [blocks],
        [like(shape, BF16)] * (len(far) + 1),
    )
    keeps = tiles_call(
        far + [0],
        offsets,
        parts_total,
        None,
        *fixed,
        [blocks],
        [like(shape, F32)] * (len(far) + 1),
    )
    weights = lax.all_gather(jnp.stack([w_self, w_neigh]), "feat", axis=1, tiled=True)
    halves = [keep + crossed(send, near).astype(F32) for keep, send in zip(keeps, sends)]
    given = [half.astype(BF16) for half in halves[:-1]]
    arrived = [crossed(part, mask) for mask, part in zip(far, given)]
    early, _ = lax.optimization_barrier(
        (
            jnp.stack(
                [features.reshape(feats, some, width), cotangent.reshape(feats, some, width)],
                axis=1,
            ),
            given[-1],
        )
    )
    early, weights, arrived = lax.optimization_barrier((swap_feat(early), weights, arrived))
    agg, *agg_pieces = small_call(
        functools.partial(agg_kernel, feats),
        [like(shape, BF16)] + [like((per_feat, block, width), BF16)] * feats,
        [me],
        [inverse.reshape(nblocks, block, 1), halves[-1], *arrived],
    )
    agg_rows = [agg_pieces[0]] + [crossed(agg_pieces[m], m, "feat") for m in range(1, feats)]
    dpre_rows, *pieces = small_call(
        dense_kernel,
        [like((some, full), BF16)] + [like((some, width), BF16)] * (2 * feats),
        [me],
        [early, weights.reshape(2, feats, width, full), inv_rows, *agg_rows],
        [pltpu.VMEM((2, feats, some, width), BF16)],
        6 * some * full * full,
    )
    dsum_pieces, out_pieces = pieces[:feats], pieces[feats:]
    dsum = jnp.concatenate(
        [dsum_pieces[0]] + [crossed(dsum_pieces[m], m, "feat") for m in range(1, feats)], axis=0
    ).reshape(shape)
    found = {0: dsum}
    for mask in far:
        found[mask] = crossed(dsum, mask)
    found[near] = crossed(dsum, near)
    first = far[-1]
    found[first], found[near] = lax.optimization_barrier((found[first], found[near]))
    for mask in far[::-1]:
        found[mask ^ near] = crossed(found[mask], near)
    dpre = lax.all_gather(dpre_rows, "feat", axis=0, tiled=True)
    dpre, out_pieces, _ = lax.optimization_barrier((dpre, out_pieces, found[first]))
    out_all = [out_pieces[0]] + [crossed(out_pieces[m], m, "feat") for m in range(1, feats)]
    (out,) = small_call(place_kernel, [like((feats, some, width), BF16)], [me], out_all)
    piece = 2 * width // parts_total
    dx_self, give, keep = small_call(
        functools.partial(grad_kernel, near, far),
        [
            like((rows, width), F32),
            like((len(far) + 1, piece, full), BF16),
            like((len(far) + 1, piece, full), F32),
        ],
        [me],
        [features, agg.reshape(rows, width), dpre, w_self],
        [pltpu.VMEM((parts_total, piece, full), F32)],
        6 * rows * width * full,
    )
    keep = keep + crossed(give, near).astype(F32)
    total = keep[len(far)]
    for at, mask in enumerate(far):
        total = total + crossed(keep[at].astype(BF16), mask).astype(F32)
    total = total.astype(BF16)
    totals = [crossed(total, mask) for mask in far] + [total]
    grad_self, grad_neigh = small_call(
        functools.partial(finish_kernel, near, far),
        [like((width, full), F32)] * 2,
        [me],
        [*totals, crossed(jnp.stack(totals), near)],
        [pltpu.VMEM((parts_total, piece, full), F32)],
    )
    order = [0, near] + [mask ^ bit for mask in far[::-1] for bit in (0, near)]
    grad_x = tiles_call(
        order,
        offsets,
        parts_total,
        per_feat,
        *fixed,
        [found[mask] for mask in order] + [dx_self.reshape(shape)],
        like(shape, F32),
    )
    return (out.reshape(rows, width), grad_x.reshape(rows, width), grad_self, grad_neigh)


def solution(mesh):
    def body(*args):
        rounds = args[7].shape[1]
        parts_total = mesh.shape["dom"]
        powers = all(n & (n - 1) == 0 for n in mesh.shape.values())
        nearly_all = parts_total <= rounds + 2 and powers
        return (dense_body if nearly_all else sparse_body)(*args)

    placed = (
        P("dom", "feat"),
        P("feat", None),
        P("feat", None),
        P("dom"),
        P("dom", None, None, None),
        P("dom", None),
        P("dom", None),
        P("dom", None, None, None, None),
        P("dom", None, None),
        P("dom", None, None),
        P("dom", "feat"),
    )
    return jax.shard_map(
        body,
        mesh=mesh,
        in_specs=placed,
        out_specs=(P("dom", "feat"), P("dom", "feat"), P("feat", None), P("feat", None)),
        check_vma=False,
    )
```

time: 246 us -> 148 us (0.60)
  waiting for transfers between devices: 130 us -> 61.9 us
  matrix products: 35.8 us -> 0 us
  local copies, waits for them, and re-layouts: 28.7 us -> 6.71 us
  Pallas kernels: 0 us -> 15.5 us
  starting transfers between devices: 26.6 us -> 41.1 us
    dot_general x31 -> x0, matrix products: 35.8 us -> none  [the longest x7 11.6 us: tile_apply_back(): jnp.einsum('kji,kjf->kif', tiles, blocks, preferred_element_type=jnp.floa...]
    psum x1 -> x0, waiting for transfers between devices: 34.3 us -> none  [body(): grad_all = lax.psum(grad_local, 'dom')]
    reduce_scatter x1 -> x0, waiting for transfers between devices: 27.7 us -> none  [body(): lax.psum_scatter(lax.dot_general(weights, stacked, (((0,), (1,)), ((), ()...]
    pallas_call x0 -> x8, Pallas kernels: none -> 15.5 us  [the longest x3 8.02 us: tiles_call(): pl.pallas_call(functools.partial(tiles_kernel, masks, offsets, parts_tota...]
    all_gather x1 -> x2, waiting for transfers between devices: 16 us -> 2.57 us  [the longest x1 2.57 us: dense_body(): dpre = lax.all_gather(dpre_rows, 'feat', axis=0, tiled=True)]
    dot_general x14 -> x0, local copies, waits for them, and re-layouts: 12.8 us -> none  [the longest x7 9.07 us: tile_apply_back(): jnp.einsum('kji,kjf->kif', tiles, blocks, preferred_element_type=jnp.floa...]
    ppermute x18 -> x31, starting transfers between devices: 26.5 us -> 37.5 us  [crossed(): lax.ppermute(x, axis, [(i, i ^ mask) for i in range(lax.axis_size(axis))])]
    gather x14 -> x0, local copies, waits for them, and re-layouts: 10.8 us -> none  [the longest x6 5.22 us: body(): jnp.take(blocks, remote_src[0, step], axis=0)]
  transfers between devices with their start and end apart: 21 -> 34, of which waited for: 7 -> 18; matrix products, arithmetic and copies ran while one was open for 22% -> 6% of each run, Pallas kernels for 0% -> 6%
where the time goes in v2:
time: 148 us
  waiting for transfers between devices  61.9 us (42%)
  starting transfers between devices  41.1 us (28%)
  Pallas kernels  15.5 us (10%)
  between operations  14.3 us (10%)
  other arithmetic  8.56 us (6%)
  local copies, waits for them, and re-layouts  6.71 us (5%)
    ppermute x31, waiting for transfers between devices, crossed(): lax.ppermute(x, axis, [(i, i ^ mask) for i in range(lax.axis_size(axis))])  59.3 us
    ppermute x31, starting transfers between devices, crossed(): lax.ppermute(x, axis, [(i, i ^ mask) for i in range(lax.axis_size(axis))])  37.5 us
    pallas_call x3, Pallas kernels, tiles_call(): pl.pallas_call(functools.partial(tiles_kernel, masks, offsets, parts_tota...  8.02 us
    pallas_call x5, Pallas kernels, small_call(): pl.pallas_call(kernel, out_shape=outs, in_specs=[SMEM] * len(scalars) + [...  7.43 us
    unnamed x26, local copies, waits for them, and re-layouts  5.36 us
    convert_element_type x3, other arithmetic, dense_body(): given = [half.astype(BF16) for half in halves[:-1]]  3.49 us
    all_to_all x1, starting transfers between devices, swap_feat(): return lax.all_to_all(x, 'feat', split_axis=0, concat_axis=0, tiled=True)  3.47 us
  transfers between devices with their start and end apart: 34, of which 18 were waited for; matrix products, arithmetic and copies ran while one was open for 6% of the time, Pallas kernels for 6%

profile of v2, /device:TPU:0, one launch (start us, length us, event | category | flops | bytes accessed | tf_op | source)
XLA Modules:
  0.0 147.9 jit_solution(1941812641561519535)
XLA Ops:
  7.2 1.7 %pad_maximum_fusion.1 = bf16[2,128,512]{2,1,0:T(8,128)(2,1)} fusion(bf16[1,128,512]{2,1,0:T(8,128)(2,1)} %bitcast.65, bf16[1,128,512]{2,1,0:T(8,128)(2,1)} %bitcast.55), kind=kLoop, calls=%fused_computation.5 | loop fusion | flops 131072 | bytes 524288 | tf_op jit(solution)/shard_map/stack | solution.py:380
  9.0 0.7 reduce
  9.8 0.7 reduce.1
  10.6 0.7 concatenate.6.me_ref
  11.3 1.4 copy-done
  12.7 0.9 copy-done.2
  13.7 1.0 copy-done.4
  14.7 1.8 %shard_map.139 = (bf16[8,128,128]{2,1,0:T(8,128)(2,1)S(1)}, bf16[8,128,128]{2,1,0:T(8,128)(2,1)S(1)}, bf16[8,128,128]{2,1,0:T(8,128)(2,1)S(1)}, bf16[8,128,128]{2,1,0:T(8,128)(2,1)S(1)}) custom-call(s32[130]{0:T(256)S(1)} %concatenate.6.me_ref, bf16[16,128,128]{2,1,0:T(8,128)(2,1)S(1)} %bitcast.46, bf16[6,8,128,128]{3,2,1,0:T(8,128)(2,1)S(1)} %bitcast.40, ...), custom_call_target="tpu_custom_call" | custom-call | flops 536870912 | bytes 4194304 | tf_op jit(solution)/shard_map/pallas_call | solution.py:194
  16.5 3.0 %collective-permute-start = (bf16[8,128,128]{2,1,0:T(8,128)(2,1)S(1)}, bf16[8,128,128]{2,1,0:T(8,128)(2,1)S(1)}, u32[]{:S(2)}, u32[]{:S(2)}) collective-permute-start(bf16[8,128,128]{2,1,0:T(8,128)(2,1)S(1)} %get-tuple-element.45), channel_id=1, source_target_pairs={{0,4},{4,0},{8,12},{12,8},{16,20},{20,16},{24,28},{28,24},{1,5},{5... | collective-permute-start | bytes 786440 | tf_op jit(solution)/shard_map/ppermute | solution.py:320
  19.6 1.9 %collective-permute-start.3 = (bf16[8,128,128]{2,1,0:T(8,128)(2,1)S(1)}, bf16[8,128,128]{2,1,0:T(8,128)(2,1)}, u32[]{:S(2)}, u32[]{:S(2)}) collective-permute-start(bf16[8,128,128]{2,1,0:T(8,128)(2,1)S(1)} %get-tuple-element.50), channel_id=1, source_target_pairs={{0,4},{4,0},{8,12},{12,8},{16,20},{20,16},{24,28},{28,24},{1,5},{5... | collective-permute-start | bytes 786440 | tf_op jit(solution)/shard_map/ppermute | solution.py:320
  21.7 0.8 pad_maximum_fusion
  22.5 2.1 %shard_map.138 = (f32[8,128,128]{2,1,0:T(8,128)S(1)}, f32[8,128,128]{2,1,0:T(8,128)S(1)}, f32[8,128,128]{2,1,0:T(8,128)S(1)}, f32[8,128,128]{2,1,0:T(8,128)S(1)}) custom-call(s32[130]{0:T(256)S(1)} %concatenate.6.me_ref, bf16[16,128,128]{2,1,0:T(8,128)(2,1)S(1)} %bitcast.47, bf16[6,8,128,128]{3,2,1,0:T(8,128)(2,1)S(1)} %bitcast.41, ...), custom_call_target="tpu_custom_call" | custom-call | flops 671088640 | bytes 4456448 | tf_op jit(solution)/shard_map/pallas_call | solution.py:194
  24.6 2.1 %collective-permute-done = bf16[8,128,128]{2,1,0:T(8,128)(2,1)S(1)} collective-permute-done((bf16[8,128,128]{2,1,0:T(8,128)(2,1)S(1)}, bf16[8,128,128]{2,1,0:T(8,128)(2,1)S(1)}, u32[]{:S(2)}, u32[]{:S(2)}) %collective-permute-start) | collective-permute-done | bytes 262176 | tf_op jit(solution)/shard_map/ppermute | solution.py:320
  26.7 0.8 add_convert_fusion.2
  27.5 2.1 %collective-permute-start.5 = (bf16[8,128,128]{2,1,0:T(8,128)(2,1)}, bf16[8,128,128]{2,1,0:T(8,128)(2,1)S(1)}, u32[]{:S(2)}, u32[]{:S(2)}) collective-permute-start(bf16[8,128,128]{2,1,0:T(8,128)(2,1)} %add_convert_fusion.2), channel_id=1, source_target_pairs={{0,8},{4,12},{8,0},{12,4},{16,24},{20,28},{24,16},{28,20},{1,9},{5... | collective-permute-start | bytes 786440 | tf_op jit(solution)/shard_map/ppermute | solution.py:320
  29.6 3.5 %all-to-all-start = ((bf16[4,2,256,128]{3,2,1,0:T(8,128)(2,1)}), bf16[4,2,256,128]{3,2,1,0:T(8,128)(2,1)S(1)}, u32[]{:S(2)}, u32[]{:S(2)}) async-start(bf16[4,2,256,128]{3,2,1,0:T(8,128)(2,1)} %pad_maximum_fusion), calls=%async_computation | async-start | bytes 1048576 | tf_op jit(solution)/shard_map/all_to_all | solution.py:316
  33.1 1.7 %add_convert_fusion.1 = bf16[8,128,128]{2,1,0:T(8,128)(2,1)} fusion(f32[8,128,128]{2,1,0:T(8,128)S(1)} %get-tuple-element.47, bf16[8,128,128]{2,1,0:T(8,128)(2,1)} %collective-permute-done.1), kind=kLoop, calls=%fused_computation.3 | loop fusion | flops 393216 | bytes 1048576 | tf_op jit(solution)/shard_map/convert_element_type | solution.py:382
  34.8 3.4 %collective-permute-start.2 = (bf16[8,128,128]{2,1,0:T(8,128)(2,1)}, bf16[8,128,128]{2,1,0:T(8,128)(2,1)S(1)}, u32[]{:S(2)}, u32[]{:S(2)}) collective-permute-start(bf16[8,128,128]{2,1,0:T(8,128)(2,1)} %add_convert_fusion.1), channel_id=1, source_target_pairs={{0,24},{4,28},{8,16},{12,20},{16,8},{20,12},{24,0},{28,4},{1,25},{... | collective-permute-start | bytes 786440 | tf_op jit(solution)/shard_map/ppermute | solution.py:320
  38.2 1.0 add_convert_fusion
  39.2 3.0 %collective-permute-start.4 = (bf16[8,128,128]{2,1,0:T(8,128)(2,1)S(1)}, bf16[8,128,128]{2,1,0:T(8,128)(2,1)S(1)}, u32[]{:S(2)}, u32[]{:S(2)}) collective-permute-start(bf16[8,128,128]{2,1,0:T(8,128)(2,1)S(1)} %add_convert_fusion), channel_id=1, source_target_pairs={{0,16},{4,20},{8,24},{12,28},{16,0},{20,4},{24,8},{28,12},{1,17},{... | collective-permute-start | bytes 786440 | tf_op jit(solution)/shard_map/ppermute | solution.py:320
  42.2 0.2 copy.15.inv_ref
  42.5 0.4 collective-permute-done.6
  42.8 1.0 convert_add_fusion.keep_ref
  43.8 2.2 %collective-permute-done.2.refs_0_ = bf16[8,128,128]{2,1,0:T(8,128)(2,1)S(1)} collective-permute-done((bf16[8,128,128]{2,1,0:T(8,128)(2,1)}, bf16[8,128,128]{2,1,0:T(8,128)(2,1)S(1)}, u32[]{:S(2)}, u32[]{:S(2)}) %collective-permute-start.2) | collective-permute-done | bytes 262176 | tf_op jit(solution)/shard_map/ppermute | solution.py:320
  46.0 15.3 %collective-permute-done.4.refs_1_ = bf16[8,128,128]{2,1,0:T(8,128)(2,1)S(1)} collective-permute-done((bf16[8,128,128]{2,1,0:T(8,128)(2,1)S(1)}, bf16[8,128,128]{2,1,0:T(8,128)(2,1)S(1)}, u32[]{:S(2)}, u32[]{:S(2)}) %collective-permute-start.4) | collective-permute-done | bytes 262176 | tf_op jit(solution)/shard_map/ppermute | solution.py:320
  61.3 1.4 shard_map.140
  62.8 0.7 copy-done.9
  63.5 1.7 %collective-permute-start.8 = (bf16[2,128,128]{2,1,0:T(8,128)(2,1)}, bf16[2,128,128]{2,1,0:T(8,128)(2,1)S(1)}, u32[]{:S(2)}, u32[]{:S(2)}) collective-permute-start(bf16[2,128,128]{2,1,0:T(8,128)(2,1)} %get-tuple-element.60), channel_id=1, source_target_pairs={{0,2},{1,3},{2,0},{3,1},{4,6},{5,7},{6,4},{7,5},{8,10},{9,11},{10,... | collective-permute-start | bytes 196616 | tf_op jit(solution)/shard_map/ppermute | solution.py:320
  65.2 0.1 collective-permute-start.9
  65.4 0.1 copy.16.inv_ref
  65.6 2.6 %collective-permute-done.8.refs_2_ = bf16[2,128,128]{2,1,0:T(8,128)(2,1)S(1)} collective-permute-done((bf16[2,128,128]{2,1,0:T(8,128)(2,1)}, bf16[2,128,128]{2,1,0:T(8,128)(2,1)S(1)}, u32[]{:S(2)}, u32[]{:S(2)}) %collective-permute-start.8) | collective-permute-done | bytes 65568 | tf_op jit(solution)/shard_map/ppermute | solution.py:320
  68.2 1.1 collective-permute-done.9.refs_3_
  69.3 2.0 %shard_map.141 = (bf16[256,512]{1,0:T(8,128)(2,1)}, bf16[256,128]{1,0:T(8,128)(2,1)S(1)}, bf16[256,128]{1,0:T(8,128)(2,1)S(1)}, bf16[256,128]{1,0:T(8,128)(2,1)S...) custom-call(s32[130]{0:T(256)S(1)} %concatenate.6.me_ref, ...), custom_call_target="tpu_custom_call" | custom-call | flops 402653184 | bytes 2622464 | tf_op jit(solution)/shard_map/pallas_call | solution.py:216
  71.3 0.2 collective-permute-start.10
  71.5 1.7 %collective-permute-start.11 = (bf16[256,128]{1,0:T(8,128)(2,1)S(1)}, bf16[256,128]{1,0:T(8,128)(2,1)S(1)}, u32[]{:S(2)}, u32[]{:S(2)}) collective-permute-start(bf16[256,128]{1,0:T(8,128)(2,1)S(1)} %get-tuple-element.69), channel_id=1, source_target_pairs={{0,2},{1,3},{2,0},{3,1},{4,6},{5,7},{6,4},{7,5},{8,10},{9,11},{10,... | collective-permute-start | bytes 196616 | tf_op jit(solution)/shard_map/ppermute | solution.py:320
  73.2 2.6 %collective-permute-done.11 = bf16[256,128]{1,0:T(8,128)(2,1)S(1)} collective-permute-done((bf16[256,128]{1,0:T(8,128)(2,1)S(1)}, bf16[256,128]{1,0:T(8,128)(2,1)S(1)}, u32[]{:S(2)}, u32[]{:S(2)}) %collective-permute-start.11) | collective-permute-done | bytes 65568 | tf_op jit(solution)/shard_map/ppermute | solution.py:320
  75.9 1.6 %collective-permute-done.12 = bf16[256,128]{1,0:T(8,128)(2,1)S(1)} collective-permute-done((bf16[256,128]{1,0:T(8,128)(2,1)S(1)}, bf16[256,128]{1,0:T(8,128)(2,1)S(1)}, u32[]{:S(2)}, u32[]{:S(2)}) %collective-permute-start.12) | collective-permute-done | bytes 65568 | tf_op jit(solution)/shard_map/ppermute | solution.py:320
  77.6 1.6 %collective-permute-start.14 = (bf16[8,128,128]{2,1,0:T(8,128)(2,1)S(1)}, bf16[8,128,128]{2,1,0:T(8,128)(2,1)S(1)}, u32[]{:S(2)}, u32[]{:S(2)}) collective-permute-start(bf16[8,128,128]{2,1,0:T(8,128)(2,1)S(1)} %bitcast.51), channel_id=1, source_target_pairs={{0,4},{4,0},{8,12},{12,8},{16,20},{20,16},{24,28},{28,24},{1,5},{5... | collective-permute-start | bytes 786440 | tf_op jit(solution)/shard_map/ppermute | solution.py:320
  79.2 6.7 %collective-permute-done.13.refs_2_ = bf16[8,128,128]{2,1,0:T(8,128)(2,1)S(1)} collective-permute-done((bf16[8,128,128]{2,1,0:T(8,128)(2,1)S(1)}, bf16[8,128,128]{2,1,0:T(8,128)(2,1)S(1)}, u32[]{:S(2)}, u32[]{:S(2)}) %collective-permute-start.13) | collective-permute-done | bytes 262176 | tf_op jit(solution)/shard_map/ppermute | solution.py:320
  85.9 2.6 %all-gather.5.cloned.1.call-done.dpre_ref = bf16[1024,512]{1,0:T(8,128)(2,1)} async-done(((bf16[256,512]{1,0:T(8,128)(2,1)}), bf16[1024,512]{1,0:T(8,128)(2,1)}) %all-gather.5.cloned.1.call-update) | async-done | bytes 1048592 | tf_op jit(solution)/shard_map/all_gather | solution.py:421
  88.5 1.2 copy-done.7
  89.8 1.3 shard_map.143
  91.1 1.5 %collective-permute-start.23 = (bf16[4,32,512]{2,1,0:T(8,128)(2,1)S(1)}, bf16[4,32,512]{2,1,0:T(8,128)(2,1)S(1)}, u32[]{:S(2)}, u32[]{:S(2)}) collective-permute-start(bf16[4,32,512]{2,1,0:T(8,128)(2,1)S(1)} %get-tuple-element.81), channel_id=1, source_target_pairs={{0,4},{4,0},{8,12},{12,8},{16,20},{20,16},{24,28},{28,24},{1,5},{5... | collective-permute-start | bytes 393224 | tf_op jit(solution)/shard_map/ppermute | solution.py:320
  92.6 2.4 %collective-permute-start.19 = (bf16[8,128,128]{2,1,0:T(8,128)(2,1)S(1)}, bf16[8,128,128]{2,1,0:T(8,128)(2,1)S(1)}, u32[]{:S(2)}, u32[]{:S(2)}) collective-permute-start(bf16[8,128,128]{2,1,0:T(8,128)(2,1)S(1)} %bitcast.52), channel_id=1, source_target_pairs={{0,16},{4,20},{8,24},{12,28},{16,0},{20,4},{24,8},{28,12},{1,17},{... | collective-permute-start | bytes 786440 | tf_op jit(solution)/shard_map/ppermute | solution.py:320
  95.0 1.4 collective-permute-start.21
  96.5 0.3 collective-permute-done.23
  96.8 3.4 %collective-permute-start.24 = (bf16[32,512]{1,0:T(8,128)(2,1)S(1)}, bf16[32,512]{1,0:T(8,128)(2,1)S(1)}, u32[]{:S(2)}, u32[]{:S(2)}) collective-permute-start(bf16[32,512]{1,0:T(8,128)(2,1)S(1)} %get-tuple-element.86), channel_id=1, source_target_pairs={{0,24},{4,28},{8,16},{12,20},{16,8},{20,12},{24,0},{28,4},{1,25},{... | collective-permute-start | bytes 98312 | tf_op jit(solution)/shard_map/ppermute | solution.py:320
  100.2 1.1 collective-permute-start.26
  101.3 14.1 %collective-permute-done.19.refs_4_ = bf16[8,128,128]{2,1,0:T(8,128)(2,1)S(1)} collective-permute-done((bf16[8,128,128]{2,1,0:T(8,128)(2,1)S(1)}, bf16[8,128,128]{2,1,0:T(8,128)(2,1)S(1)}, u32[]{:S(2)}, u32[]{:S(2)}) %collective-permute-start.19) | collective-permute-done | bytes 262176 | tf_op jit(solution)/shard_map/ppermute | solution.py:320
  115.4 0.6 collective-permute-start.18
  115.9 1.5 collective-permute-start.20
  117.4 0.6 collective-permute-start.22
  118.0 3.4 %collective-permute-done.25 = bf16[32,512]{1,0:T(8,128)(2,1)S(1)} collective-permute-done((bf16[32,512]{1,0:T(8,128)(2,1)S(1)}, bf16[32,512]{1,0:T(8,128)(2,1)S(1)}, u32[]{:S(2)}, u32[]{:S(2)}) %collective-permute-start.25) | collective-permute-done | bytes 32800 | tf_op jit(solution)/shard_map/ppermute | solution.py:320
  121.4 3.4 %collective-permute-start.27 = (bf16[32,512]{1,0:T(8,128)(2,1)S(1)}, bf16[32,512]{1,0:T(8,128)(2,1)S(1)}, u32[]{:S(2)}, u32[]{:S(2)}) collective-permute-start(bf16[32,512]{1,0:T(8,128)(2,1)S(1)} %fusion.3.refs_3_), channel_id=1, source_target_pairs={{0,24},{4,28},{8,16},{12,20},{16,8},{20,12},{24,0},{28,4},{1,25},{... | collective-permute-start | bytes 98312 | tf_op jit(solution)/shard_map/ppermute | solution.py:320
  124.8 2.4 %collective-permute-done.27.refs_0_ = bf16[32,512]{1,0:T(8,128)(2,1)S(1)} collective-permute-done((bf16[32,512]{1,0:T(8,128)(2,1)S(1)}, bf16[32,512]{1,0:T(8,128)(2,1)S(1)}, u32[]{:S(2)}, u32[]{:S(2)}) %collective-permute-start.27) | collective-permute-done | bytes 32800 | tf_op jit(solution)/shard_map/ppermute | solution.py:320
  127.3 2.5 %collective-permute-done.28.refs_1_ = bf16[32,512]{1,0:T(8,128)(2,1)S(1)} collective-permute-done((bf16[32,512]{1,0:T(8,128)(2,1)S(1)}, bf16[32,512]{1,0:T(8,128)(2,1)S(1)}, u32[]{:S(2)}, u32[]{:S(2)}) %collective-permute-start.28) | collective-permute-done | bytes 32800 | tf_op jit(solution)/shard_map/ppermute | solution.py:320
  129.8 1.3 collective-permute-done.29.refs_2_
  131.1 0.6 collective-permute-start.30
  131.8 0.4 collective-permute-start.16
  132.1 1.5 %collective-permute-start.17 = (bf16[256,128]{1,0:T(8,128)(2,1)S(1)}, bf16[256,128]{1,0:T(8,128)(2,1)S(1)}, u32[]{:S(2)}, u32[]{:S(2)}) collective-permute-start(bf16[256,128]{1,0:T(8,128)(2,1)S(1)} %get-tuple-element.75), channel_id=1, source_target_pairs={{0,3},{1,2},{2,1},{3,0},{4,7},{5,6},{6,5},{7,4},{8,11},{9,10},{10,... | collective-permute-start | bytes 196616 | tf_op jit(solution)/shard_map/ppermute | solution.py:320
  133.6 0.6 collective-permute-done.22.refs_7_
  134.2 4.2 %shard_map.144 = f32[8,128,128]{2,1,0:T(8,128)} custom-call(s32[130]{0:T(256)S(1)} %concatenate.6.me_ref, bf16[16,128,128]{2,1,0:T(8,128)(2,1)S(1)} %bitcast.48, bf16[6,8,128,128]{3,2,1,0:T(8,128)(2,1)S(1)} %bitcast.42, bf16[8,128,128]{2,1,0:T(8,128)(2,1)S(1)} %bitcast.54, bf16[8,128,128]{2,1,0:T(8,128)(2,1)S(1)} %collective-permute-done.14.refs_1_, ...), custom_call_target="tpu_custom_call" | custom-call | flops 1207959552 | bytes 5505024 | tf_op jit(solution)/shard_map/pallas_call | solution.py:194
  138.4 1.3 shard_map.142
  139.7 1.4 shard_map.145
  (60 shorter events, 1.0 us)
Async XLA Ops:
  7.2 54.2 %all-gather.3.cloned.1.call-start = ((), (), s32[]{:S(2)}) async-start(), calls=%async_computation.1 | async-start | bytes 1310720 | tf_op jit(solution)/shard_map/all_gather | solution.py:380
  7.2 14.4 %copy-start.11 = (bf16[1024,128]{1,0:T(8,128)(2,1)S(1)}, bf16[1024,128]{1,0:T(8,128)(2,1)}, u32[]{:S(2)}) copy-start(bf16[1024,128]{1,0:T(8,128)(2,1)} %param.21) | copy-start | bytes 786436
  11.3 1.4 copy-start
  12.7 0.9 copy-start.2
  13.7 1.0 copy-start.4
  16.5 10.2 %collective-permute-start = (bf16[8,128,128]{2,1,0:T(8,128)(2,1)S(1)}, bf16[8,128,128]{2,1,0:T(8,128)(2,1)S(1)}, u32[]{:S(2)}, u32[]{:S(2)}) collective-permute-start(bf16[8,128,128]{2,1,0:T(8,128)(2,1)S(1)} %get-tuple-element.45), channel_id=1, source_target_pairs={{0,4},{4,0},{8,12},{12,8},{16,20},{20,16},{24,28},{28,24},{1,5},{5... | collective-permute-start | bytes 786440 | tf_op jit(solution)/shard_map/ppermute | solution.py:320
  19.5 13.6 %collective-permute-start.1 = (bf16[8,128,128]{2,1,0:T(8,128)(2,1)S(1)}, bf16[8,128,128]{2,1,0:T(8,128)(2,1)}, u32[]{:S(2)}, u32[]{:S(2)}) collective-permute-start(bf16[8,128,128]{2,1,0:T(8,128)(2,1)S(1)} %get-tuple-element.48), channel_id=1, source_target_pairs={{0,4},{4,0},{8,12},{12,8},{16,20},{20,16},{24,28},{28,24},{1,5},{5... | collective-permute-start | bytes 786440 | tf_op jit(solution)/shard_map/ppermute | solution.py:320
  19.6 18.6 %collective-permute-start.3 = (bf16[8,128,128]{2,1,0:T(8,128)(2,1)S(1)}, bf16[8,128,128]{2,1,0:T(8,128)(2,1)}, u32[]{:S(2)}, u32[]{:S(2)}) collective-permute-start(bf16[8,128,128]{2,1,0:T(8,128)(2,1)S(1)} %get-tuple-element.50), channel_id=1, source_target_pairs={{0,4},{4,0},{8,12},{12,8},{16,20},{20,16},{24,28},{28,24},{1,5},{5... | collective-permute-start | bytes 786440 | tf_op jit(solution)/shard_map/ppermute | solution.py:320
  21.6 21.2 %collective-permute-start.6 = (bf16[8,128,128]{2,1,0:T(8,128)(2,1)S(1)}, bf16[8,128,128]{2,1,0:T(8,128)(2,1)}, u32[]{:S(2)}, u32[]{:S(2)}) collective-permute-start(bf16[8,128,128]{2,1,0:T(8,128)(2,1)S(1)} %get-tuple-element.54), channel_id=1, source_target_pairs={{0,4},{4,0},{8,12},{12,8},{16,20},{20,16},{24,28},{28,24},{1,5},{5... | collective-permute-start | bytes 786440 | tf_op jit(solution)/shard_map/ppermute | solution.py:320
  27.5 14.8 %copy-start.12 = (s32[1024]{0:T(1024)S(1)}, s32[1024]{0:T(1024)}, u32[]{:S(2)}) copy-start(s32[1024]{0:T(1024)} %param.14) | copy-start | bytes 12292
  27.5 16.3 %collective-permute-start.5 = (bf16[8,128,128]{2,1,0:T(8,128)(2,1)}, bf16[8,128,128]{2,1,0:T(8,128)(2,1)S(1)}, u32[]{:S(2)}, u32[]{:S(2)}) collective-permute-start(bf16[8,128,128]{2,1,0:T(8,128)(2,1)} %add_convert_fusion.2), channel_id=1, source_target_pairs={{0,8},{4,12},{8,0},{12,4},{16,24},{20,28},{24,16},{28,20},{1,9},{5... | collective-permute-start | bytes 786440 | tf_op jit(solution)/shard_map/ppermute | solution.py:320
  29.6 31.8 %all-to-all-start = ((bf16[4,2,256,128]{3,2,1,0:T(8,128)(2,1)}), bf16[4,2,256,128]{3,2,1,0:T(8,128)(2,1)S(1)}, u32[]{:S(2)}, u32[]{:S(2)}) async-start(bf16[4,2,256,128]{3,2,1,0:T(8,128)(2,1)} %pad_maximum_fusion), calls=%async_computation | async-start | bytes 1048576 | tf_op jit(solution)/shard_map/all_to_all | solution.py:316
  33.0 55.5 %all-gather.5.cloned.1.call-start = ((), (), s32[]{:S(2)}) async-start(), calls=%async_computation.2 | async-start | bytes 1310720 | tf_op jit(solution)/shard_map/all_gather | solution.py:421
  34.8 11.2 %collective-permute-start.2 = (bf16[8,128,128]{2,1,0:T(8,128)(2,1)}, bf16[8,128,128]{2,1,0:T(8,128)(2,1)S(1)}, u32[]{:S(2)}, u32[]{:S(2)}) collective-permute-start(bf16[8,128,128]{2,1,0:T(8,128)(2,1)} %add_convert_fusion.1), channel_id=1, source_target_pairs={{0,24},{4,28},{8,16},{12,20},{16,8},{20,12},{24,0},{28,4},{1,25},{... | collective-permute-start | bytes 786440 | tf_op jit(solution)/shard_map/ppermute | solution.py:320
  39.2 22.1 %collective-permute-start.4 = (bf16[8,128,128]{2,1,0:T(8,128)(2,1)S(1)}, bf16[8,128,128]{2,1,0:T(8,128)(2,1)S(1)}, u32[]{:S(2)}, u32[]{:S(2)}) collective-permute-start(bf16[8,128,128]{2,1,0:T(8,128)(2,1)S(1)} %add_convert_fusion), channel_id=1, source_target_pairs={{0,16},{4,20},{8,24},{12,28},{16,0},{20,4},{24,8},{28,12},{1,17},{... | collective-permute-start | bytes 786440 | tf_op jit(solution)/shard_map/ppermute | solution.py:320
  61.3 7.9 %copy-start.6 = (bf16[2,512,512]{2,1,0:T(8,128)(2,1)S(1)}, bf16[2,512,512]{2,1,0:T(8,128)(2,1)}, u32[]{:S(2)}) copy-start(bf16[2,512,512]{2,1,0:T(8,128)(2,1)} %all-gather.3.cloned.1.call-done) | copy-start | bytes 3145732
  62.8 0.7 copy-start.9
  63.5 25.1 %copy-start.3 = (bf16[1024,128]{1,0:T(8,128)(2,1)S(1)}, bf16[1024,128]{1,0:T(8,128)(2,1)}, u32[]{:S(2)}) copy-start(bf16[1024,128]{1,0:T(8,128)(2,1)} %f_ref.1) | copy-start | bytes 786436
  63.5 25.1 %copy-start.8 = (bf16[128,512]{1,0:T(8,128)(2,1)S(1)}, bf16[128,512]{1,0:T(8,128)(2,1)}, u32[]{:S(2)}) copy-start(bf16[128,512]{1,0:T(8,128)(2,1)} %w_ref.1) | copy-start | bytes 393220
  63.5 25.1 %copy-start.10 = (bf16[8,128,128]{2,1,0:T(8,128)(2,1)S(1)}, bf16[8,128,128]{2,1,0:T(8,128)(2,1)}, u32[]{:S(2)}) copy-start(bf16[8,128,128]{2,1,0:T(8,128)(2,1)} %copy-done.9) | copy-start | bytes 786436
  63.5 2.1 %collective-permute-start.7 = (bf16[2,128,128]{2,1,0:T(8,128)(2,1)}, bf16[2,128,128]{2,1,0:T(8,128)(2,1)S(1)}, u32[]{:S(2)}, u32[]{:S(2)}) collective-permute-start(bf16[2,128,128]{2,1,0:T(8,128)(2,1)} %get-tuple-element.59), channel_id=1, source_target_pairs={{0,1},{1,0},{2,3},{3,2},{4,5},{5,4},{6,7},{7,6},{8,9},{9,8},{10,11... | collective-permute-start | bytes 196616 | tf_op jit(solution)/shard_map/ppermute | solution.py:320
  63.5 4.7 %collective-permute-start.8 = (bf16[2,128,128]{2,1,0:T(8,128)(2,1)}, bf16[2,128,128]{2,1,0:T(8,128)(2,1)S(1)}, u32[]{:S(2)}, u32[]{:S(2)}) collective-permute-start(bf16[2,128,128]{2,1,0:T(8,128)(2,1)} %get-tuple-element.60), channel_id=1, source_target_pairs={{0,2},{1,3},{2,0},{3,1},{4,6},{5,7},{6,4},{7,5},{8,10},{9,11},{10,... | collective-permute-start | bytes 196616 | tf_op jit(solution)/shard_map/ppermute | solution.py:320
  65.2 4.1 %collective-permute-start.9 = (bf16[2,128,128]{2,1,0:T(8,128)(2,1)S(1)}, bf16[2,128,128]{2,1,0:T(8,128)(2,1)S(1)}, u32[]{:S(2)}, u32[]{:S(2)}) collective-permute-start(bf16[2,128,128]{2,1,0:T(8,128)(2,1)S(1)} %get-tuple-element.61), channel_id=1, source_target_pairs={{0,3},{1,2},{2,1},{3,0},{4,7},{5,6},{6,5},{7,4},{8,11},{9,10},{10,... | collective-permute-start | bytes 196616 | tf_op jit(solution)/shard_map/ppermute | solution.py:320
  71.3 1.9 %collective-permute-start.10 = (bf16[256,128]{1,0:T(8,128)(2,1)S(1)}, bf16[256,128]{1,0:T(8,128)(2,1)S(1)}, u32[]{:S(2)}, u32[]{:S(2)}) collective-permute-start(bf16[256,128]{1,0:T(8,128)(2,1)S(1)} %get-tuple-element.68), channel_id=1, source_target_pairs={{0,1},{1,0},{2,3},{3,2},{4,5},{5,4},{6,7},{7,6},{8,9},{9,8},{10,11... | collective-permute-start | bytes 196616 | tf_op jit(solution)/shard_map/ppermute | solution.py:320
  71.5 4.3 %collective-permute-start.11 = (bf16[256,128]{1,0:T(8,128)(2,1)S(1)}, bf16[256,128]{1,0:T(8,128)(2,1)S(1)}, u32[]{:S(2)}, u32[]{:S(2)}) collective-permute-start(bf16[256,128]{1,0:T(8,128)(2,1)S(1)} %get-tuple-element.69), channel_id=1, source_target_pairs={{0,2},{1,3},{2,0},{3,1},{4,6},{5,7},{6,4},{7,5},{8,10},{9,11},{10,... | collective-permute-start | bytes 196616 | tf_op jit(solution)/shard_map/ppermute | solution.py:320
  73.2 4.3 %collective-permute-start.12 = (bf16[256,128]{1,0:T(8,128)(2,1)S(1)}, bf16[256,128]{1,0:T(8,128)(2,1)S(1)}, u32[]{:S(2)}, u32[]{:S(2)}) collective-permute-start(bf16[256,128]{1,0:T(8,128)(2,1)S(1)} %get-tuple-element.70), channel_id=1, source_target_pairs={{0,3},{1,2},{2,1},{3,0},{4,7},{5,6},{6,5},{7,4},{8,11},{9,10},{10,... | collective-permute-start | bytes 196616 | tf_op jit(solution)/shard_map/ppermute | solution.py:320
  77.5 8.4 %collective-permute-start.13 = (bf16[8,128,128]{2,1,0:T(8,128)(2,1)S(1)}, bf16[8,128,128]{2,1,0:T(8,128)(2,1)S(1)}, u32[]{:S(2)}, u32[]{:S(2)}) collective-permute-start(bf16[8,128,128]{2,1,0:T(8,128)(2,1)S(1)} %bitcast.50), channel_id=1, source_target_pairs={{0,8},{4,12},{8,0},{12,4},{16,24},{20,28},{24,16},{28,20},{1,9},{5... | collective-permute-start | bytes 786440 | tf_op jit(solution)/shard_map/ppermute | solution.py:320
  77.6 8.4 %collective-permute-start.14 = (bf16[8,128,128]{2,1,0:T(8,128)(2,1)S(1)}, bf16[8,128,128]{2,1,0:T(8,128)(2,1)S(1)}, u32[]{:S(2)}, u32[]{:S(2)}) collective-permute-start(bf16[8,128,128]{2,1,0:T(8,128)(2,1)S(1)} %bitcast.51), channel_id=1, source_target_pairs={{0,4},{4,0},{8,12},{12,8},{16,20},{20,16},{24,28},{28,24},{1,5},{5... | collective-permute-start | bytes 786440 | tf_op jit(solution)/shard_map/ppermute | solution.py:320
  88.5 1.2 copy-start.7
  89.7 44.5 %copy-start.1 = (bf16[1,6,8,128,128]{4,3,2,1,0:T(8,128)(2,1)S(1)}, bf16[1,6,8,128,128]{4,3,2,1,0:T(8,128)(2,1)}, u32[]{:S(2)}) copy-start(bf16[1,6,8,128,128]{4,3,2,1,0:T(8,128)(2,1)} %param.18) | copy-start | bytes 4718596
  89.7 44.5 %copy-start.5 = (bf16[1,16,128,128]{3,2,1,0:T(8,128)(2,1)S(1)}, bf16[1,16,128,128]{3,2,1,0:T(8,128)(2,1)}, u32[]{:S(2)}) copy-start(bf16[1,16,128,128]{3,2,1,0:T(8,128)(2,1)} %param.15) | copy-start | bytes 1572868
  91.1 5.7 %collective-permute-start.23 = (bf16[4,32,512]{2,1,0:T(8,128)(2,1)S(1)}, bf16[4,32,512]{2,1,0:T(8,128)(2,1)S(1)}, u32[]{:S(2)}, u32[]{:S(2)}) collective-permute-start(bf16[4,32,512]{2,1,0:T(8,128)(2,1)S(1)} %get-tuple-element.81), channel_id=1, source_target_pairs={{0,4},{4,0},{8,12},{12,8},{16,20},{20,16},{24,28},{28,24},{1,5},{5... | collective-permute-start | bytes 393224 | tf_op jit(solution)/shard_map/ppermute | solution.py:320
  92.6 22.7 %collective-permute-start.19 = (bf16[8,128,128]{2,1,0:T(8,128)(2,1)S(1)}, bf16[8,128,128]{2,1,0:T(8,128)(2,1)S(1)}, u32[]{:S(2)}, u32[]{:S(2)}) collective-permute-start(bf16[8,128,128]{2,1,0:T(8,128)(2,1)S(1)} %bitcast.52), channel_id=1, source_target_pairs={{0,16},{4,20},{8,24},{12,28},{16,0},{20,4},{24,8},{28,12},{1,17},{... | collective-permute-start | bytes 786440 | tf_op jit(solution)/shard_map/ppermute | solution.py:320
  95.0 20.9 %collective-permute-start.21 = (bf16[8,128,128]{2,1,0:T(8,128)(2,1)S(1)}, bf16[8,128,128]{2,1,0:T(8,128)(2,1)S(1)}, u32[]{:S(2)}, u32[]{:S(2)}) collective-permute-start(bf16[8,128,128]{2,1,0:T(8,128)(2,1)S(1)} %bitcast.53), channel_id=1, source_target_pairs={{0,24},{4,28},{8,16},{12,20},{16,8},{20,12},{24,0},{28,4},{1,25},{... | collective-permute-start | bytes 786440 | tf_op jit(solution)/shard_map/ppermute | solution.py:320
  96.8 20.6 %collective-permute-start.24 = (bf16[32,512]{1,0:T(8,128)(2,1)S(1)}, bf16[32,512]{1,0:T(8,128)(2,1)S(1)}, u32[]{:S(2)}, u32[]{:S(2)}) collective-permute-start(bf16[32,512]{1,0:T(8,128)(2,1)S(1)} %get-tuple-element.86), channel_id=1, source_target_pairs={{0,24},{4,28},{8,16},{12,20},{16,8},{20,12},{24,0},{28,4},{1,25},{... | collective-permute-start | bytes 98312 | tf_op jit(solution)/shard_map/ppermute | solution.py:320
  100.2 21.2 %collective-permute-start.25 = (bf16[32,512]{1,0:T(8,128)(2,1)S(1)}, bf16[32,512]{1,0:T(8,128)(2,1)S(1)}, u32[]{:S(2)}, u32[]{:S(2)}) collective-permute-start(bf16[32,512]{1,0:T(8,128)(2,1)S(1)} %get-tuple-element.88), channel_id=1, source_target_pairs={{0,16},{4,20},{8,24},{12,28},{16,0},{20,4},{24,8},{28,12},{1,17},{... | collective-permute-start | bytes 98312 | tf_op jit(solution)/shard_map/ppermute | solution.py:320
  100.2 21.2 %collective-permute-start.26 = (bf16[32,512]{1,0:T(8,128)(2,1)S(1)}, bf16[32,512]{1,0:T(8,128)(2,1)S(1)}, u32[]{:S(2)}, u32[]{:S(2)}) collective-permute-start(bf16[32,512]{1,0:T(8,128)(2,1)S(1)} %get-tuple-element.87), channel_id=1, source_target_pairs={{0,8},{4,12},{8,0},{12,4},{16,24},{20,28},{24,16},{28,20},{1,9},{5... | collective-permute-start | bytes 98312 | tf_op jit(solution)/shard_map/ppermute | solution.py:320
  115.4 16.4 %collective-permute-start.18 = (bf16[8,128,128]{2,1,0:T(8,128)(2,1)S(1)}, bf16[8,128,128]{2,1,0:T(8,128)(2,1)S(1)}, u32[]{:S(2)}, u32[]{:S(2)}) collective-permute-start(bf16[8,128,128]{2,1,0:T(8,128)(2,1)S(1)} %collective-permute-done.13.refs_2_), channel_id=1, source_target_pairs={{0,4},{4,0},{8,12},{12,8},{16,20},{20,16},{24,28},{28,24},{1,5},{5... | collective-permute-start | bytes 786440 | tf_op jit(solution)/shard_map/ppermute | solution.py:320
  115.9 16.2 %collective-permute-start.20 = (bf16[8,128,128]{2,1,0:T(8,128)(2,1)S(1)}, bf16[8,128,128]{2,1,0:T(8,128)(2,1)S(1)}, u32[]{:S(2)}, u32[]{:S(2)}) collective-permute-start(bf16[8,128,128]{2,1,0:T(8,128)(2,1)S(1)} %collective-permute-done.19.refs_4_), channel_id=1, source_target_pairs={{0,4},{4,0},{8,12},{12,8},{16,20},{20,16},{24,28},{28,24},{1,5},{5... | collective-permute-start | bytes 786440 | tf_op jit(solution)/shard_map/ppermute | solution.py:320
  117.4 16.8 %collective-permute-start.22 = (bf16[8,128,128]{2,1,0:T(8,128)(2,1)S(1)}, bf16[8,128,128]{2,1,0:T(8,128)(2,1)S(1)}, u32[]{:S(2)}, u32[]{:S(2)}) collective-permute-start(bf16[8,128,128]{2,1,0:T(8,128)(2,1)S(1)} %collective-permute-done.21.refs_6_), channel_id=1, source_target_pairs={{0,4},{4,0},{8,12},{12,8},{16,20},{20,16},{24,28},{28,24},{1,5},{5... | collective-permute-start | bytes 786440 | tf_op jit(solution)/shard_map/ppermute | solution.py:320
  121.4 5.8 %collective-permute-start.27 = (bf16[32,512]{1,0:T(8,128)(2,1)S(1)}, bf16[32,512]{1,0:T(8,128)(2,1)S(1)}, u32[]{:S(2)}, u32[]{:S(2)}) collective-permute-start(bf16[32,512]{1,0:T(8,128)(2,1)S(1)} %fusion.3.refs_3_), channel_id=1, source_target_pairs={{0,24},{4,28},{8,16},{12,20},{16,8},{20,12},{24,0},{28,4},{1,25},{... | collective-permute-start | bytes 98312 | tf_op jit(solution)/shard_map/ppermute | solution.py:320
  124.8 5.0 %collective-permute-start.28 = (bf16[32,512]{1,0:T(8,128)(2,1)S(1)}, bf16[32,512]{1,0:T(8,128)(2,1)S(1)}, u32[]{:S(2)}, u32[]{:S(2)}) collective-permute-start(bf16[32,512]{1,0:T(8,128)(2,1)S(1)} %fusion.3.refs_3_), channel_id=1, source_target_pairs={{0,16},{4,20},{8,24},{12,28},{16,0},{20,4},{24,8},{28,12},{1,17},{... | collective-permute-start | bytes 98312 | tf_op jit(solution)/shard_map/ppermute | solution.py:320
  127.2 3.9 %collective-permute-start.29 = (bf16[32,512]{1,0:T(8,128)(2,1)S(1)}, bf16[32,512]{1,0:T(8,128)(2,1)S(1)}, u32[]{:S(2)}, u32[]{:S(2)}) collective-permute-start(bf16[32,512]{1,0:T(8,128)(2,1)S(1)} %fusion.3.refs_3_), channel_id=1, source_target_pairs={{0,8},{4,12},{8,0},{12,4},{16,24},{20,28},{24,16},{28,20},{1,9},{5... | collective-permute-start | bytes 98312 | tf_op jit(solution)/shard_map/ppermute | solution.py:320
  131.1 8.6 %collective-permute-start.30 = (bf16[4,32,512]{2,1,0:T(8,128)(2,1)S(1)}, bf16[4,32,512]{2,1,0:T(8,128)(2,1)S(1)}, u32[]{:S(2)}, u32[]{:S(2)}) collective-permute-start(bf16[4,32,512]{2,1,0:T(8,128)(2,1)S(1)} %pad_maximum_fusion.3), channel_id=1, source_target_pairs={{0,4},{4,0},{8,12},{12,8},{16,20},{20,16},{24,28},{28,24},{1,5},{5... | collective-permute-start | bytes 393224 | tf_op jit(solution)/shard_map/ppermute | solution.py:320
  131.8 6.6 %collective-permute-start.15 = (bf16[256,128]{1,0:T(8,128)(2,1)S(1)}, bf16[256,128]{1,0:T(8,128)(2,1)S(1)}, u32[]{:S(2)}, u32[]{:S(2)}) collective-permute-start(bf16[256,128]{1,0:T(8,128)(2,1)S(1)} %get-tuple-element.73), channel_id=1, source_target_pairs={{0,1},{1,0},{2,3},{3,2},{4,5},{5,4},{6,7},{7,6},{8,9},{9,8},{10,11... | collective-permute-start | bytes 196616 | tf_op jit(solution)/shard_map/ppermute | solution.py:320
  131.8 6.6 %collective-permute-start.16 = (bf16[256,128]{1,0:T(8,128)(2,1)S(1)}, bf16[256,128]{1,0:T(8,128)(2,1)S(1)}, u32[]{:S(2)}, u32[]{:S(2)}) collective-permute-start(bf16[256,128]{1,0:T(8,128)(2,1)S(1)} %get-tuple-element.74), channel_id=1, source_target_pairs={{0,2},{1,3},{2,0},{3,1},{4,6},{5,7},{6,4},{7,5},{8,10},{9,11},{10,... | collective-permute-start | bytes 196616 | tf_op jit(solution)/shard_map/ppermute | solution.py:320
  132.1 6.3 %collective-permute-start.17 = (bf16[256,128]{1,0:T(8,128)(2,1)S(1)}, bf16[256,128]{1,0:T(8,128)(2,1)S(1)}, u32[]{:S(2)}, u32[]{:S(2)}) collective-permute-start(bf16[256,128]{1,0:T(8,128)(2,1)S(1)} %get-tuple-element.75), channel_id=1, source_target_pairs={{0,3},{1,2},{2,1},{3,0},{4,7},{5,6},{6,5},{7,4},{8,11},{9,10},{10,... | collective-permute-start | bytes 196616 | tf_op jit(solution)/shard_map/ppermute | solution.py:320
Sparse Core Ops, SparseCore 0:
  10.1 19.4 all-gather.2
  71.4 17.0 all-gather.4

commit v3 on v2

--- a/solution.py
+++ b/solution.py
@@ -118,83 +118,93 @@
     return ((block_id // per_feat) ^ mine) * per_feat + block_id % per_feat
 
 
-def tile_groups(masks, offsets, parts_total, me, rounds, groups, tiles):
-    ids_at = (2, 2 + tiles, 2 + 2 * tiles, 2 + 2 * tiles + rounds * groups)
+def tile_groups(masks, offsets, parts_total, me, groups, tiles, ids):
+    ldst, lsrc, rdst, rsrc = ids
     jobs = []
     for at, mask in enumerate(masks):
         if mask == 0:
             for first in range(0, tiles, groups):
                 count = min(groups, tiles - first)
-                jobs.append((at, None, None, first, count, ids_at[0] + first, ids_at[1] + first))
+                dst = [ldst[0, first + k] for k in range(count)]
+                src = [lsrc[0, first + k] for k in range(count)]
+                jobs.append((at, None, None, first, dst, src))
         else:
             offset = lax.rem((me ^ mask) - me + parts_total, parts_total)
             step, known = round_of(offset, offsets)
-            base = step * groups
-            jobs.append((at, step, known, None, groups, ids_at[2] + base, ids_at[3] + base))
+            dst = [rdst[step, 0, k] for k in range(groups)]
+            src = [rsrc[step, 0, k] for k in range(groups)]
+            jobs.append((at, step, known, None, dst, src))
     return jobs
 
 
-def tiles_kernel(
-    masks, offsets, parts_total, per_feat, me_ref, lvals, rvals, *refs
-):
-    back = per_feat is not None
+def tiles_kernel(masks, offsets, parts_total, back, feats, extras, *refs):
+    ids, (lvals, rvals), refs = refs[:4], refs[4:6], refs[6:]
+    me = lax.axis_index("dom")
+    mine = lax.axis_index("feat")
     rounds, groups, tiles = tile_counts(rvals, lvals)
-    me, mine = me_ref[0], me_ref[1]
-    jobs = tile_groups(masks, offsets, parts_total, me, rounds, groups, tiles)
+    jobs = tile_groups(masks, offsets, parts_total, me, groups, tiles, ids)
     held, prod, acc, sems = refs[-4:]
+    copies = []
+    for slot, (at, step, known, first, dst, src) in enumerate(jobs):
+        source = lvals.at[pl.ds(first, len(dst))] if step is None else rvals.at[step]
+        copy = pltpu.make_async_copy(source, held.at[slot, pl.ds(0, len(dst))], sems.at[slot])
+        copy.start()
+        copies.append(copy)
     if back:
         own_ref, grad_ref = refs[len(masks)], refs[len(masks) + 1]
         blocks = refs[: len(masks)]
         sinks = [grad_ref] * len(masks)
+        acc[0] = own_ref[...]
     else:
         blocks = [refs[0]] * len(masks)
-        sinks = refs[1 : 1 + len(masks)]
-    copies = []
-    for slot, (at, step, known, first, count, dst_at, src_at) in enumerate(jobs):
-        source = lvals.at[pl.ds(first, count)] if step is None else rvals.at[step]
-        copy = pltpu.make_async_copy(source, held.at[slot, pl.ds(0, count)], sems.at[slot])
-        copy.start()
-        copies.append(copy)
-    if back:
-        acc[0] = own_ref[...]
+        sinks = refs[1 + extras : 1 + extras + len(masks)]
+    if extras:
+        pieces = refs[1 + extras + len(masks) : 1 + extras + len(masks) + feats]
+        for mask, piece in enumerate(pieces):
+            rows = pl.ds((mine ^ mask) * piece.shape[1], piece.shape[1])
+            piece[0] = refs[0][rows]
+            piece[1] = refs[1][rows]
     total = 0
-    for slot, (at, step, known, first, count, dst_at, src_at) in enumerate(jobs):
+    for slot, (at, step, known, first, dst, src) in enumerate(jobs):
         copies[slot].wait()
         half = slot % 2
-        read_at, write_at = (dst_at, src_at) if back else (src_at, dst_at)
-        for k in range(count):
-            block_id = me_ref[read_at + k]
+        for k in range(len(dst)):
             if back:
-                block_id = crossed_block(block_id, mine, per_feat)
-            block = blocks[at][block_id]
-            if back:
+                per_feat = blocks[at].shape[0] // feats
+                block = blocks[at][crossed_block(dst[k], mine, per_feat)]
                 product = lax.dot_general(
                     held[slot, k], block, (((0,), (0,)), ((), ())), preferred_element_type=F32
                 )
             else:
-                product = jnp.dot(held[slot, k], block, preferred_element_type=F32)
+                product = jnp.dot(
+                    held[slot, k], blocks[at][src[k]], preferred_element_type=F32
+                )
             prod[half, k] = product if known is None else jnp.where(known, product, 0.0)
         fresh = not back and (slot == 0 or jobs[slot - 1][0] != at)
         if fresh:
             total = at % 2
             acc[total] = jnp.zeros(acc.shape[1:], F32)
-        for k in range(count):
-            into = me_ref[write_at + k]
+        for k in range(len(dst)):
+            into = src[k] if back else dst[k]
             acc[total, into] = acc[total, into] + prod[half, k]
         last = slot == len(jobs) - 1 or jobs[slot + 1][0] != at
         if last and (not back or slot == len(jobs) - 1):
             sinks[at][...] = acc[total].astype(sinks[at].dtype)
 
 
-def tiles_call(masks, offsets, parts_total, per_feat, me, lvals, rvals, blocks, sinks):
+def tiles_call(masks, offsets, parts_total, back, feats, fixed, blocks, sinks, room):
+    ids, lvals, rvals = fixed
     rounds, groups, tiles = tile_counts(rvals, lvals)
     nblocks, block, width = blocks[0].shape
     slots = sum(-(-tiles // groups) if mask == 0 else 1 for mask in masks)
     flops = 2 * slots * groups * block * block * width
+    extras = 0 if back else len(blocks) - 1
     return pl.pallas_call(
-        functools.partial(tiles_kernel, masks, offsets, parts_total, per_feat),
+        functools.partial(tiles_kernel, masks, offsets, parts_total, back, feats, extras),
         out_shape=sinks,
-        in_specs=[SMEM] + [pl.BlockSpec(memory_space=pltpu.HBM)] * 2 + [VMEM] * len(blocks),
+        in_specs=[SMEM] * 4
+        + [pl.BlockSpec(memory_space=pltpu.HBM)] * 2
+        + [VMEM] * len(blocks),
         out_specs=jax.tree.map(lambda _: VMEM, sinks),
         scratch_shapes=[
             pltpu.VMEM((slots, groups, block, block), BF16),
@@ -202,30 +212,30 @@
             pltpu.VMEM((2, nblocks, block, width), F32),
             pltpu.SemaphoreType.DMA((slots,)),
         ],
-        compiler_params=pltpu.CompilerParams(vmem_limit_bytes=24 * 2**20),
+        compiler_params=pltpu.CompilerParams(vmem_limit_bytes=room * 2**20),
         cost_estimate=pl.CostEstimate(
             flops=4 * flops,
             bytes_accessed=slots * groups * block * block * 2 + 4 * rounds * nblocks * block * width,
             transcendentals=0,
         ),
-    )(me, lvals, rvals, *blocks)
-
-
-def small_call(kernel, outs, scalars, arrays, scratch=(), flops=10**6):
+    )(*ids, lvals, rvals, *blocks)
+
+
+def small_call(kernel, outs, arrays, scratch=(), flops=10**6):
     size = sum(t.size * t.dtype.itemsize for t in list(arrays) + list(outs))
     return pl.pallas_call(
         kernel,
         out_shape=outs,
-        in_specs=[SMEM] * len(scalars) + [VMEM] * len(arrays),
+        in_specs=[VMEM] * len(arrays),
         out_specs=[VMEM] * len(outs),
         scratch_shapes=scratch,
         compiler_params=pltpu.CompilerParams(vmem_limit_bytes=24 * 2**20),
         cost_estimate=pl.CostEstimate(flops=flops, bytes_accessed=size, transcendentals=0),
-    )(*scalars, *arrays)
-
-
-def agg_kernel(feats, me_ref, inv_ref, keep_ref, *refs):
-    mine = me_ref[1]
+    )(*arrays)
+
+
+def agg_kernel(feats, inv_ref, keep_ref, *refs):
+    mine = lax.axis_index("feat")
     far_refs, agg_ref, piece_refs = refs[: -1 - feats], refs[-1 - feats], refs[-feats:]
     per_feat = piece_refs[0].shape[0]
     sums = keep_ref[...]
@@ -240,26 +250,31 @@
     return jnp.concatenate(parts, axis=1)
 
 
-def dense_kernel(me_ref, early_ref, w_ref, inv_ref, *refs):
-    mine = me_ref[1]
-    feats, _, some, width = early_ref.shape
-    a_refs, dpre_ref = refs[:feats], refs[feats]
-    dsum_refs, out_refs = refs[feats + 1 : 2 * feats + 1], refs[2 * feats + 1 : 3 * feats + 1]
+def dense_kernel(feats, w_ref, inv_ref, *refs):
+    mine = lax.axis_index("feat")
+    early_refs, a_refs = refs[:feats], refs[feats : 2 * feats]
+    dpre_ref = refs[2 * feats]
+    dsum_refs, out_refs = refs[2 * feats + 1 : 3 * feats + 1], refs[3 * feats + 1 : 4 * feats + 1]
     held = refs[-1]
-    full = feats * width
-    ws = w_ref[0].reshape(full, full)
-    wn = w_ref[1].reshape(full, full)
-    pre = jnp.dot(joined([early_ref[j, 0] for j in range(feats)]), ws, preferred_element_type=F32)
+    width, full = w_ref.shape[2:]
+    some = held.shape[2]
+    pre = jnp.zeros((some, full), F32)
     for mask in range(feats):
+        early = early_refs[mask]
+        pre = pre + jnp.dot(
+            early[0].reshape(some, width), w_ref[0, mine ^ mask], preferred_element_type=F32
+        )
         pre = pre + jnp.dot(
             a_refs[mask][...].reshape(some, width),
             w_ref[1, mine ^ mask],
             preferred_element_type=F32,
         )
+        held[0, mine ^ mask] = early[1].reshape(some, width)
     sigma = 1.0 / (1.0 + jnp.exp(-pre))
     out = (pre * sigma).astype(BF16)
-    cot = joined([early_ref[j, 1] for j in range(feats)]).astype(F32)
+    cot = joined([held[0, j] for j in range(feats)]).astype(F32)
     dpre = (cot * sigma * (1.0 + pre * (1.0 - sigma))).astype(BF16)
+    wn = w_ref[1].reshape(full, full)
     dagg = lax.dot_general(dpre, wn, (((1,), (1,)), ((), ())), preferred_element_type=F32)
     dsum = (dagg * inv_ref[...]).astype(BF16)
     dpre_ref[...] = dpre
@@ -271,8 +286,8 @@
         out_refs[mask][...] = held[1, mine ^ mask]
 
 
-def grad_kernel(near, far, me_ref, f_ref, a_ref, dpre_ref, w_ref, dx_ref, give_ref, keep_ref, held):
-    me = me_ref[0]
+def grad_kernel(near, far, f_ref, a_ref, dpre_ref, w_ref, dx_ref, give_ref, keep_ref, held):
+    me = lax.axis_index("dom")
     dpre = dpre_ref[...]
     width = f_ref.shape[1]
     some = held.shape[1]
@@ -290,8 +305,8 @@
     )
 
 
-def finish_kernel(near, far, me_ref, *refs):
-    me = me_ref[0]
+def finish_kernel(near, far, *refs):
+    me = lax.axis_index("dom")
     count = len(far) + 1
     found, other_ref = refs[:count], refs[count]
     self_ref, neigh_ref, held = refs[count + 1 :]
@@ -305,8 +320,8 @@
         neigh_ref[j * some : (j + 1) * some] = held[half + j]
 
 
-def place_kernel(me_ref, *refs):
-    mine = me_ref[1]
+def place_kernel(*refs):
+    mine = lax.axis_index("feat")
     out_ref = refs[-1]
     for mask, ref in enumerate(refs[:-1]):
         out_ref[mine ^ mask] = ref[...]
@@ -348,61 +363,56 @@
     full = feats * width
     offsets = round_offsets(parts_total, rounds)
     near, far = 1, list(range(parts_total - 2, 0, -2))
+    bits = [1 << n for n in range(parts_total.bit_length() - 1)]
     mine = lax.axis_index("feat").astype(jnp.int32)
     inverse = 1.0 / degree.astype(F32)
     inv_rows = lax.dynamic_slice(inverse, (mine * some,), (some,))[:, None]
-    me = jnp.concatenate(
-        [lax.axis_index("dom").astype(jnp.int32).reshape(1), mine.reshape(1)]
-        + [t.reshape(-1) for t in (local_dst, local_src, remote_dst, remote_src)]
+    ids = (
+        local_dst,
+        local_src,
+        jnp.swapaxes(remote_dst, 0, 1),
+        jnp.swapaxes(remote_src, 0, 1),
     )
     shape = (nblocks, block, width)
     blocks = features.reshape(shape)
-    fixed = (me, local_vals[0], remote_vals[0])
-
-    sends = tiles_call(
-        [mask ^ near for mask in far + [0]],
-        offsets,
-        parts_total,
-        None,
-        *fixed,
-        [blocks],
-        [like(shape, BF16)] * (len(far) + 1),
-    )
-    keeps = tiles_call(
+    fixed = (ids, local_vals[0], remote_vals[0])
+
+    def forward(masks, arrays, sinks):
+        return tiles_call(
+            masks, offsets, parts_total, False, feats, fixed, arrays, sinks, 62
+        )
+
+    sends = forward([mask ^ near for mask in far + [0]], [blocks], [like(shape, BF16)] * (len(far) + 1))
+    pair, _ = lax.optimization_barrier((jnp.stack([w_self, w_neigh]), sends[0]))
+    weights = lax.all_gather(pair, "feat", axis=1, tiled=True)
+    made = forward(
         far + [0],
-        offsets,
-        parts_total,
-        None,
-        *fixed,
-        [blocks],
-        [like(shape, F32)] * (len(far) + 1),
-    )
-    weights = lax.all_gather(jnp.stack([w_self, w_neigh]), "feat", axis=1, tiled=True)
-    halves = [keep + crossed(send, near).astype(F32) for keep, send in zip(keeps, sends)]
-    given = [half.astype(BF16) for half in halves[:-1]]
-    arrived = [crossed(part, mask) for mask, part in zip(far, given)]
-    early, _ = lax.optimization_barrier(
-        (
-            jnp.stack(
-                [features.reshape(feats, some, width), cotangent.reshape(feats, some, width)],
-                axis=1,
-            ),
-            given[-1],
-        )
-    )
-    early, weights, arrived = lax.optimization_barrier((swap_feat(early), weights, arrived))
+        [blocks, cotangent.reshape(shape)],
+        [like(shape, F32)] * (len(far) + 1) + [like((2, per_feat, block, width), BF16)] * feats,
+    )
+    keeps, early_pieces = made[: len(far) + 1], made[len(far) + 1 :]
+    parts = {mask: [keep] for mask, keep in zip(far + [0], keeps)}
+    for mask, send in zip(far + [0], sends):
+        parts[mask].append(crossed(send, near).astype(F32))
+    for bit in bits[1:]:
+        for mask in sorted((m for m in parts if m & bit), reverse=True):
+            whole = sum(parts.pop(mask)).astype(BF16)
+            parts[mask ^ bit].append(crossed(whole, bit).astype(F32))
+    keep, *arrived = parts[0]
+    arrived = [part.astype(BF16) for part in arrived]
+    early_pieces, _ = lax.optimization_barrier((early_pieces, whole))
+    early = [early_pieces[0]] + [crossed(early_pieces[m], m, "feat") for m in range(1, feats)]
+    early, weights, arrived = lax.optimization_barrier((early, weights, arrived))
     agg, *agg_pieces = small_call(
         functools.partial(agg_kernel, feats),
         [like(shape, BF16)] + [like((per_feat, block, width), BF16)] * feats,
-        [me],
-        [inverse.reshape(nblocks, block, 1), halves[-1], *arrived],
+        [inverse.reshape(nblocks, block, 1), keep, *arrived],
     )
     agg_rows = [agg_pieces[0]] + [crossed(agg_pieces[m], m, "feat") for m in range(1, feats)]
     dpre_rows, *pieces = small_call(
-        dense_kernel,
+        functools.partial(dense_kernel, feats),
         [like((some, full), BF16)] + [like((some, width), BF16)] * (2 * feats),
-        [me],
-        [early, weights.reshape(2, feats, width, full), inv_rows, *agg_rows],
+        [weights.reshape(2, feats, width, full), inv_rows, *early, *agg_rows],
         [pltpu.VMEM((2, feats, some, width), BF16)],
         6 * some * full * full,
     )
@@ -411,17 +421,14 @@
         [dsum_pieces[0]] + [crossed(dsum_pieces[m], m, "feat") for m in range(1, feats)], axis=0
     ).reshape(shape)
     found = {0: dsum}
-    for mask in far:
-        found[mask] = crossed(dsum, mask)
-    found[near] = crossed(dsum, near)
-    first = far[-1]
-    found[first], found[near] = lax.optimization_barrier((found[first], found[near]))
-    for mask in far[::-1]:
-        found[mask ^ near] = crossed(found[mask], near)
+    for bit in bits[::-1]:
+        for mask in sorted(found):
+            found[mask ^ bit] = crossed(found[mask], bit)
     dpre = lax.all_gather(dpre_rows, "feat", axis=0, tiled=True)
-    dpre, out_pieces, _ = lax.optimization_barrier((dpre, out_pieces, found[first]))
+    out_pieces, _ = lax.optimization_barrier((out_pieces, (found[1], found[2])))
     out_all = [out_pieces[0]] + [crossed(out_pieces[m], m, "feat") for m in range(1, feats)]
-    (out,) = small_call(place_kernel, [like((feats, some, width), BF16)], [me], out_all)
+    (out,) = small_call(place_kernel, [like((feats, some, width), BF16)], out_all)
+    dpre, out, _ = lax.optimization_barrier((dpre, out, (found[3], found[4])))
     piece = 2 * width // parts_total
     dx_self, give, keep = small_call(
         functools.partial(grad_kernel, near, far),
@@ -430,34 +437,37 @@
             like((len(far) + 1, piece, full), BF16),
             like((len(far) + 1, piece, full), F32),
         ],
-        [me],
         [features, agg.reshape(rows, width), dpre, w_self],
         [pltpu.VMEM((parts_total, piece, full), F32)],
         6 * rows * width * full,
     )
     keep = keep + crossed(give, near).astype(F32)
+    keep, _ = lax.optimization_barrier((keep, found[6]))
     total = keep[len(far)]
     for at, mask in enumerate(far):
         total = total + crossed(keep[at].astype(BF16), mask).astype(F32)
-    total = total.astype(BF16)
+    total, _ = lax.optimization_barrier((total.astype(BF16), found[5]))
     totals = [crossed(total, mask) for mask in far] + [total]
     grad_self, grad_neigh = small_call(
         functools.partial(finish_kernel, near, far),
         [like((width, full), F32)] * 2,
-        [me],
         [*totals, crossed(jnp.stack(totals), near)],
         [pltpu.VMEM((parts_total, piece, full), F32)],
     )
-    order = [0, near] + [mask ^ bit for mask in far[::-1] for bit in (0, near)]
-    grad_x = tiles_call(
-        order,
-        offsets,
-        parts_total,
-        per_feat,
-        *fixed,
-        [found[mask] for mask in order] + [dx_self.reshape(shape)],
-        like(shape, F32),
-    )
+    grad_x = dx_self.reshape(shape)
+    half = parts_total // 2
+    for order in (list(range(half)), list(range(half, parts_total))):
+        grad_x = tiles_call(
+            order,
+            offsets,
+            parts_total,
+            True,
+            feats,
+            fixed,
+            [found[mask] for mask in order] + [grad_x],
+            like(shape, F32),
+            24,
+        )
     return (out.reshape(rows, width), grad_x.reshape(rows, width), grad_self, grad_neigh)
 
 

time: 148 us -> 128 us (0.86)
  waiting for transfers between devices: 61.9 us -> 43.4 us
  other arithmetic: 8.56 us -> 4.12 us
  Pallas kernels: 15.5 us -> 18.3 us
  local copies, waits for them, and re-layouts: 6.71 us -> 4.74 us
  starting transfers between devices: 41.1 us -> 42.7 us
    ppermute x31 -> x34, waiting for transfers between devices: 59.3 us -> 43.4 us  [crossed(): lax.ppermute(x, axis, [(i, i ^ mask) for i in range(lax.axis_size(axis))])]
    pallas_call x3 -> x4, Pallas kernels: 8.02 us -> 13.4 us  [tiles_call(): pl.pallas_call(functools.partial(tiles_kernel, masks, offsets, parts_tota...]
    ppermute x31 -> x34, starting transfers between devices: 37.5 us -> 42.6 us  [crossed(): lax.ppermute(x, axis, [(i, i ^ mask) for i in range(lax.axis_size(axis))])]
    all_to_all x1 -> x0, starting transfers between devices: 3.47 us -> none  [swap_feat(): return lax.all_to_all(x, 'feat', split_axis=0, concat_axis=0, tiled=True)]
    pallas_call x5, Pallas kernels: 7.43 us -> 4.82 us  [small_call(): pl.pallas_call(kernel, out_shape=outs, in_specs=[VMEM] * len(arrays), out...]
    all_gather x1, waiting for transfers between devices: 2.57 us -> 0.01 us  [dense_body(): dpre = lax.all_gather(dpre_rows, 'feat', axis=0, tiled=True)]
    unnamed x26 -> x36, local copies, waits for them, and re-layouts: 5.36 us -> 4.3 us
  transfers between devices with their start and end apart: 34 -> 36, of which waited for: 18 -> 19; matrix products, arithmetic and copies ran while one was open for 6% -> 2% of each run, Pallas kernels for 6% -> 8%
where the time goes in v3:
time: 128 us
  waiting for transfers between devices  43.4 us (34%)
  starting transfers between devices  42.7 us (33%)
  Pallas kernels  18.3 us (14%)
  between operations  14.3 us (11%)
  local copies, waits for them, and re-layouts  4.74 us (4%)
  other arithmetic  4.12 us (3%)
    ppermute x34, waiting for transfers between devices, crossed(): lax.ppermute(x, axis, [(i, i ^ mask) for i in range(lax.axis_size(axis))])  43.4 us
    ppermute x34, starting transfers between devices, crossed(): lax.ppermute(x, axis, [(i, i ^ mask) for i in range(lax.axis_size(axis))])  42.6 us
    pallas_call x4, Pallas kernels, tiles_call(): pl.pallas_call(functools.partial(tiles_kernel, masks, offsets, parts_tota...  13.4 us
    pallas_call x5, Pallas kernels, small_call(): pl.pallas_call(kernel, out_shape=outs, in_specs=[VMEM] * len(arrays), out...  4.82 us
    unnamed x36, local copies, waits for them, and re-layouts  4.3 us
  transfers between devices with their start and end apart: 36, of which 19 were waited for; matrix products, arithmetic and copies ran while one was open for 2% of the time, Pallas kernels for 8%

profile of v3, /device:TPU:0, one launch (start us, length us, event | category | flops | bytes accessed | tf_op | source)
XLA Modules:
  0.0 127.5 jit_solution(1612174045906041287)
XLA Ops:
  7.2 1.7 %pad_maximum_fusion = bf16[2,128,512]{2,1,0:T(8,128)(2,1)} fusion(bf16[1,128,512]{2,1,0:T(8,128)(2,1)} %bitcast.68, bf16[1,128,512]{2,1,0:T(8,128)(2,1)} %bitcast.51), kind=kLoop, calls=%fused_computation.3 | loop fusion | flops 131072 | bytes 524288 | tf_op jit(solution)/shard_map/stack | solution.py:386
  8.9 3.7 %shard_map.139 = (bf16[8,128,128]{2,1,0:T(8,128)(2,1)}, bf16[8,128,128]{2,1,0:T(8,128)(2,1)}, bf16[8,128,128]{2,1,0:T(8,128)(2,1)}, bf16[8,128,128]{2,1,0:T(8,128)(2,1)}) custom-call(s32[1,16]{1,0:T(1,128)} %refs_0_.7, s32[1,16]{1,0:T(1,128)} %refs_1_.7, s32[6,1,8]{2,1,0:T(1,128)} %bitcast.57, s32[6,1,8]{2,1,0:T(1,128)} %bitcast.61, ...), custom_call_target="tpu_custom_call" | custom-call | flops 536870912 | bytes 4194304 | tf_op jit(solution)/shard_map/pallas_call | solution.py:202
  12.7 3.0 %collective-permute-start.1 = (bf16[8,128,128]{2,1,0:T(8,128)(2,1)}, bf16[8,128,128]{2,1,0:T(8,128)(2,1)S(1)}, u32[]{:S(2)}, u32[]{:S(2)}) collective-permute-start(bf16[8,128,128]{2,1,0:T(8,128)(2,1)} %get-tuple-element.63), channel_id=1, source_target_pairs={{0,4},{4,0},{8,12},{12,8},{16,20},{20,16},{24,28},{28,24},{1,5},{5... | collective-permute-start | bytes 786440 | tf_op jit(solution)/shard_map/ppermute | solution.py:335
  15.8 1.9 %collective-permute-start.7 = (bf16[8,128,128]{2,1,0:T(8,128)(2,1)}, bf16[8,128,128]{2,1,0:T(8,128)(2,1)S(1)}, u32[]{:S(2)}, u32[]{:S(2)}) collective-permute-start(bf16[8,128,128]{2,1,0:T(8,128)(2,1)} %get-tuple-element.71), channel_id=1, source_target_pairs={{0,4},{4,0},{8,12},{12,8},{16,20},{20,16},{24,28},{28,24},{1,5},{5... | collective-permute-start | bytes 786440 | tf_op jit(solution)/shard_map/ppermute | solution.py:335
  17.8 4.6 %shard_map.138 = (f32[8,128,128]{2,1,0:T(8,128)}, f32[8,128,128]{2,1,0:T(8,128)}, f32[8,128,128]{2,1,0:T(8,128)}, f32[8,128,128]{2,1,0:T(8,128)}, bf16[2,2,128,1...) custom-call(s32[1,16]{1,0:T(1,128)} %refs_0_.7, ...), custom_call_target="tpu_custom_call" | custom-call | flops 671088640 | bytes 4456448 | tf_op jit(solution)/shard_map/pallas_call | solution.py:202
  22.4 0.7 collective-permute-done.1
  23.1 1.1 add_convert_fusion.2
  24.2 2.2 %collective-permute-start.2 = (bf16[8,128,128]{2,1,0:T(8,128)(2,1)S(1)}, bf16[8,128,128]{2,1,0:T(8,128)(2,1)S(1)}, u32[]{:S(2)}, u32[]{:S(2)}) collective-permute-start(bf16[8,128,128]{2,1,0:T(8,128)(2,1)S(1)} %add_convert_fusion.2), channel_id=1, source_target_pairs={{0,8},{4,12},{8,0},{12,4},{16,24},{20,28},{24,16},{28,20},{1,9},{5... | collective-permute-start | bytes 786440 | tf_op jit(solution)/shard_map/ppermute | solution.py:335
  26.4 1.5 %collective-permute-start.6 = (bf16[8,128,128]{2,1,0:T(8,128)(2,1)}, bf16[8,128,128]{2,1,0:T(8,128)(2,1)S(1)}, u32[]{:S(2)}, u32[]{:S(2)}) collective-permute-start(bf16[8,128,128]{2,1,0:T(8,128)(2,1)} %get-tuple-element.69), channel_id=1, source_target_pairs={{0,4},{4,0},{8,12},{12,8},{16,20},{20,16},{24,28},{28,24},{1,5},{5... | collective-permute-start | bytes 786440 | tf_op jit(solution)/shard_map/ppermute | solution.py:335
  27.9 6.4 %collective-permute-done.7 = bf16[8,128,128]{2,1,0:T(8,128)(2,1)S(1)} collective-permute-done((bf16[8,128,128]{2,1,0:T(8,128)(2,1)}, bf16[8,128,128]{2,1,0:T(8,128)(2,1)S(1)}, u32[]{:S(2)}, u32[]{:S(2)}) %collective-permute-start.7) | collective-permute-done | bytes 262176 | tf_op jit(solution)/shard_map/ppermute | solution.py:335
  34.3 1.1 add_convert_fusion
  35.4 2.2 %collective-permute-start.8 = (bf16[8,128,128]{2,1,0:T(8,128)(2,1)S(1)}, bf16[8,128,128]{2,1,0:T(8,128)(2,1)S(1)}, u32[]{:S(2)}, u32[]{:S(2)}) collective-permute-start(bf16[8,128,128]{2,1,0:T(8,128)(2,1)S(1)} %add_convert_fusion), channel_id=1, source_target_pairs={{0,8},{4,12},{8,0},{12,4},{16,24},{20,28},{24,16},{28,20},{1,9},{5... | collective-permute-start | bytes 786440 | tf_op jit(solution)/shard_map/ppermute | solution.py:335
  37.7 2.7 %collective-permute-start.9 = (bf16[8,128,128]{2,1,0:T(8,128)(2,1)S(1)}, bf16[8,128,128]{2,1,0:T(8,128)(2,1)S(1)}, u32[]{:S(2)}, u32[]{:S(2)}) collective-permute-start(bf16[8,128,128]{2,1,0:T(8,128)(2,1)S(1)} %add_convert_fusion.1), channel_id=1, source_target_pairs={{0,16},{4,20},{8,24},{12,28},{16,0},{20,4},{24,8},{28,12},{1,17},{... | collective-permute-start | bytes 786440 | tf_op jit(solution)/shard_map/ppermute | solution.py:335
  40.4 1.5 %collective-permute-start.4 = (bf16[2,2,128,128]{3,2,1,0:T(8,128)(2,1)}, bf16[2,2,128,128]{3,2,1,0:T(8,128)(2,1)S(1)}, u32[]{:S(2)}, u32[]{:S(2)}) collective-permute-start(bf16[2,2,128,128]{3,2,1,0:T(8,128)(2,1)} %get-tuple-element.66), channel_id=1, source_target_pairs={{0,2},{1,3},{2,0},{3,1},{4,6},{5,7},{6,4},{7,5},{8,10},{9,11},{10,... | collective-permute-start | bytes 393224 | tf_op jit(solution)/shard_map/ppermute | solution.py:335
  41.9 0.4 collective-permute-start.5
  42.3 0.2 copy.15.inv_ref
  42.5 4.9 %collective-permute-done.8.refs_1_ = bf16[8,128,128]{2,1,0:T(8,128)(2,1)S(1)} collective-permute-done((bf16[8,128,128]{2,1,0:T(8,128)(2,1)S(1)}, bf16[8,128,128]{2,1,0:T(8,128)(2,1)S(1)}, u32[]{:S(2)}, u32[]{:S(2)}) %collective-permute-start.8) | collective-permute-done | bytes 262176 | tf_op jit(solution)/shard_map/ppermute | solution.py:335
  47.4 1.6 %collective-permute-done.5.refs_3_ = bf16[2,2,128,128]{3,2,1,0:T(8,128)(2,1)S(1)} collective-permute-done((bf16[2,2,128,128]{3,2,1,0:T(8,128)(2,1)}, bf16[2,2,128,128]{3,2,1,0:T(8,128)(2,1)S(1)}, u32[]{:S(2)}, u32[]{:S(2)}) %collective-permute-start.5) | collective-permute-done | bytes 131104 | tf_op jit(solution)/shard_map/ppermute | solution.py:335
  49.0 0.7 copy-done.8
  49.6 0.5 collective-permute-done.9.refs_2_
  50.1 0.9 shard_map.140
  51.0 0.6 copy-done.10
  51.6 1.5 %collective-permute-start.11 = (bf16[2,128,128]{2,1,0:T(8,128)(2,1)}, bf16[2,128,128]{2,1,0:T(8,128)(2,1)S(1)}, u32[]{:S(2)}, u32[]{:S(2)}) collective-permute-start(bf16[2,128,128]{2,1,0:T(8,128)(2,1)} %get-tuple-element.83), channel_id=1, source_target_pairs={{0,2},{1,3},{2,0},{3,1},{4,6},{5,7},{6,4},{7,5},{8,10},{9,11},{10,... | collective-permute-start | bytes 196616 | tf_op jit(solution)/shard_map/ppermute | solution.py:335
  53.1 0.4 collective-permute-start.12
  53.7 2.7 %collective-permute-done.11.refs_6_ = bf16[2,128,128]{2,1,0:T(8,128)(2,1)S(1)} collective-permute-done((bf16[2,128,128]{2,1,0:T(8,128)(2,1)}, bf16[2,128,128]{2,1,0:T(8,128)(2,1)S(1)}, u32[]{:S(2)}, u32[]{:S(2)}) %collective-permute-start.11) | collective-permute-done | bytes 65568 | tf_op jit(solution)/shard_map/ppermute | solution.py:335
  56.4 1.1 collective-permute-done.12.refs_7_
  57.5 0.9 copy-done.9
  58.4 0.8 copy-done.11
  59.2 1.6 %shard_map.141 = (bf16[256,512]{1,0:T(8,128)(2,1)}, bf16[256,128]{1,0:T(8,128)(2,1)S(1)}, bf16[256,128]{1,0:T(8,128)(2,1)S(1)}, bf16[256,128]{1,0:T(8,128)(2,1)S...) custom-call(bf16[2,4,128,512]{3,2,1,0:T(8,128)(2,1)S(1)} %bitcast.49, ...), custom_call_target="tpu_custom_call" | custom-call | flops 402653184 | bytes 2622464 | tf_op jit(solution)/shard_map/pallas_call | solution.py:226
  60.8 0.2 collective-permute-start.13
  61.0 1.5 %collective-permute-start.14 = (bf16[256,128]{1,0:T(8,128)(2,1)S(1)}, bf16[256,128]{1,0:T(8,128)(2,1)S(1)}, u32[]{:S(2)}, u32[]{:S(2)}) collective-permute-start(bf16[256,128]{1,0:T(8,128)(2,1)S(1)} %get-tuple-element.92), channel_id=1, source_target_pairs={{0,2},{1,3},{2,0},{3,1},{4,6},{5,7},{6,4},{7,5},{8,10},{9,11},{10,... | collective-permute-start | bytes 196616 | tf_op jit(solution)/shard_map/ppermute | solution.py:335
  62.5 0.2 collective-permute-start.15
  62.8 2.6 %collective-permute-done.14 = bf16[256,128]{1,0:T(8,128)(2,1)S(1)} collective-permute-done((bf16[256,128]{1,0:T(8,128)(2,1)S(1)}, bf16[256,128]{1,0:T(8,128)(2,1)S(1)}, u32[]{:S(2)}, u32[]{:S(2)}) %collective-permute-start.14) | collective-permute-done | bytes 65568 | tf_op jit(solution)/shard_map/ppermute | solution.py:335
  65.4 1.3 %collective-permute-done.15 = bf16[256,128]{1,0:T(8,128)(2,1)S(1)} collective-permute-done((bf16[256,128]{1,0:T(8,128)(2,1)S(1)}, bf16[256,128]{1,0:T(8,128)(2,1)S(1)}, u32[]{:S(2)}, u32[]{:S(2)}) %collective-permute-start.15) | collective-permute-done | bytes 65568 | tf_op jit(solution)/shard_map/ppermute | solution.py:335
  66.7 0.4 collective-permute-start.17
  67.2 1.5 %collective-permute-start.16 = (bf16[8,128,128]{2,1,0:T(8,128)(2,1)S(1)}, bf16[8,128,128]{2,1,0:T(8,128)(2,1)S(1)}, u32[]{:S(2)}, u32[]{:S(2)}) collective-permute-start(bf16[8,128,128]{2,1,0:T(8,128)(2,1)S(1)} %bitcast.46), channel_id=1, source_target_pairs={{0,4},{4,0},{8,12},{12,8},{16,20},{20,16},{24,28},{28,24},{1,5},{5... | collective-permute-start | bytes 786440 | tf_op jit(solution)/shard_map/ppermute | solution.py:335
  68.7 2.7 %collective-permute-start.22 = (bf16[8,128,128]{2,1,0:T(8,128)(2,1)S(1)}, bf16[8,128,128]{2,1,0:T(8,128)(2,1)S(1)}, u32[]{:S(2)}, u32[]{:S(2)}) collective-permute-start(bf16[8,128,128]{2,1,0:T(8,128)(2,1)S(1)} %bitcast.47), channel_id=1, source_target_pairs={{0,16},{4,20},{8,24},{12,28},{16,0},{20,4},{24,8},{28,12},{1,17},{... | collective-permute-start | bytes 786440 | tf_op jit(solution)/shard_map/ppermute | solution.py:335
  71.3 7.9 %collective-permute-done.17.refs_8_ = bf16[8,128,128]{2,1,0:T(8,128)(2,1)S(1)} collective-permute-done((bf16[8,128,128]{2,1,0:T(8,128)(2,1)S(1)}, bf16[8,128,128]{2,1,0:T(8,128)(2,1)S(1)}, u32[]{:S(2)}, u32[]{:S(2)}) %collective-permute-start.17) | collective-permute-done | bytes 262176 | tf_op jit(solution)/shard_map/ppermute | solution.py:335
  79.2 2.5 %collective-permute-start.21 = (bf16[8,128,128]{2,1,0:T(8,128)(2,1)S(1)}, bf16[8,128,128]{2,1,0:T(8,128)(2,1)S(1)}, u32[]{:S(2)}, u32[]{:S(2)}) collective-permute-start(bf16[8,128,128]{2,1,0:T(8,128)(2,1)S(1)} %collective-permute-done.17.refs_8_), channel_id=1, source_target_pairs={{0,4},{4,0},{8,12},{12,8},{16,20},{20,16},{24,28},{28,24},{1,5},{5... | collective-permute-start | bytes 786440 | tf_op jit(solution)/shard_map/ppermute | solution.py:335
  81.7 1.3 collective-permute-start.19
  83.0 0.6 collective-permute-start.20
  83.6 2.9 %collective-permute-done.19.refs_2_ = bf16[256,128]{1,0:T(8,128)(2,1)S(1)} collective-permute-done((bf16[256,128]{1,0:T(8,128)(2,1)S(1)}, bf16[256,128]{1,0:T(8,128)(2,1)S(1)}, u32[]{:S(2)}, u32[]{:S(2)}) %collective-permute-start.19) | collective-permute-done | bytes 65568 | tf_op jit(solution)/shard_map/ppermute | solution.py:335
  86.5 0.8 collective-permute-done.20.refs_3_
  87.4 0.7 shard_map.142
  88.1 1.2 copy-done.4
  89.4 0.8 shard_map.143
  90.1 1.2 collective-permute-start.26
  91.3 0.9 collective-permute-start.23
  92.2 4.3 %collective-permute-done.26 = bf16[4,32,512]{2,1,0:T(8,128)(2,1)S(1)} collective-permute-done((bf16[4,32,512]{2,1,0:T(8,128)(2,1)S(1)}, bf16[4,32,512]{2,1,0:T(8,128)(2,1)S(1)}, u32[]{:S(2)}, u32[]{:S(2)}) %collective-permute-start.26) | collective-permute-done | bytes 131104 | tf_op jit(solution)/shard_map/ppermute | solution.py:335
  96.6 2.2 %collective-permute-done.24.refs_8_ = bf16[8,128,128]{2,1,0:T(8,128)(2,1)S(1)} collective-permute-done((bf16[8,128,128]{2,1,0:T(8,128)(2,1)S(1)}, bf16[8,128,128]{2,1,0:T(8,128)(2,1)S(1)}, u32[]{:S(2)}, u32[]{:S(2)}) %collective-permute-start.24) | collective-permute-done | bytes 262176 | tf_op jit(solution)/shard_map/ppermute | solution.py:335
  98.8 1.7 %collective-permute-start.27 = (bf16[32,512]{1,0:T(8,128)(2,1)S(1)}, bf16[32,512]{1,0:T(8,128)(2,1)S(1)}, u32[]{:S(2)}, u32[]{:S(2)}) collective-permute-start(bf16[32,512]{1,0:T(8,128)(2,1)S(1)} %get-tuple-element.108), channel_id=1, source_target_pairs={{0,24},{4,28},{8,16},{12,20},{16,8},{20,12},{24,0},{28,4},{1,25},{... | collective-permute-start | bytes 98312 | tf_op jit(solution)/shard_map/ppermute | solution.py:335
  100.6 2.6 %collective-permute-start.29 = (bf16[32,512]{1,0:T(8,128)(2,1)S(1)}, bf16[32,512]{1,0:T(8,128)(2,1)S(1)}, u32[]{:S(2)}, u32[]{:S(2)}) collective-permute-start(bf16[32,512]{1,0:T(8,128)(2,1)S(1)} %get-tuple-element.109), channel_id=1, source_target_pairs={{0,8},{4,12},{8,0},{12,4},{16,24},{20,28},{24,16},{28,20},{1,9},{5... | collective-permute-start | bytes 98312 | tf_op jit(solution)/shard_map/ppermute | solution.py:335
  103.2 1.7 %collective-permute-start.25 = (bf16[8,128,128]{2,1,0:T(8,128)(2,1)S(1)}, bf16[8,128,128]{2,1,0:T(8,128)(2,1)S(1)}, u32[]{:S(2)}, u32[]{:S(2)}) collective-permute-start(bf16[8,128,128]{2,1,0:T(8,128)(2,1)S(1)} %collective-permute-done.24.refs_8_), channel_id=1, source_target_pairs={{0,4},{4,0},{8,12},{12,8},{16,20},{20,16},{24,28},{28,24},{1,5},{5... | collective-permute-start | bytes 786440 | tf_op jit(solution)/shard_map/ppermute | solution.py:335
  104.9 0.5 collective-permute-done.28
  105.5 2.1 %collective-permute-start.30 = (bf16[32,512]{1,0:T(8,128)(2,1)S(1)}, bf16[32,512]{1,0:T(8,128)(2,1)S(1)}, u32[]{:S(2)}, u32[]{:S(2)}) collective-permute-start(bf16[32,512]{1,0:T(8,128)(2,1)S(1)} %fusion.2.refs_3_), channel_id=1, source_target_pairs={{0,24},{4,28},{8,16},{12,20},{16,8},{20,12},{24,0},{28,4},{1,25},{... | collective-permute-start | bytes 98312 | tf_op jit(solution)/shard_map/ppermute | solution.py:335
  107.6 1.1 collective-permute-start.31
  108.7 1.3 collective-permute-start.32
  110.0 1.3 %collective-permute-done.30.refs_0_ = bf16[32,512]{1,0:T(8,128)(2,1)S(1)} collective-permute-done((bf16[32,512]{1,0:T(8,128)(2,1)S(1)}, bf16[32,512]{1,0:T(8,128)(2,1)S(1)}, u32[]{:S(2)}, u32[]{:S(2)}) %collective-permute-start.30) | collective-permute-done | bytes 32800 | tf_op jit(solution)/shard_map/ppermute | solution.py:335
  111.3 1.3 %collective-permute-done.31.refs_1_ = bf16[32,512]{1,0:T(8,128)(2,1)S(1)} collective-permute-done((bf16[32,512]{1,0:T(8,128)(2,1)S(1)}, bf16[32,512]{1,0:T(8,128)(2,1)S(1)}, u32[]{:S(2)}, u32[]{:S(2)}) %collective-permute-start.31) | collective-permute-done | bytes 32800 | tf_op jit(solution)/shard_map/ppermute | solution.py:335
  112.6 0.3 collective-permute-done.32.refs_2_
  112.9 1.7 %collective-permute-start.33 = (bf16[4,32,512]{2,1,0:T(8,128)(2,1)S(1)}, bf16[4,32,512]{2,1,0:T(8,128)(2,1)S(1)}, u32[]{:S(2)}, u32[]{:S(2)}) collective-permute-start(bf16[4,32,512]{2,1,0:T(8,128)(2,1)S(1)} %pad_maximum_fusion.2), channel_id=1, source_target_pairs={{0,4},{4,0},{8,12},{12,8},{16,20},{20,16},{24,28},{28,24},{1,5},{5... | collective-permute-start | bytes 393224 | tf_op jit(solution)/shard_map/ppermute | solution.py:335
  114.7 2.3 %shard_map.144.refs_10_ = f32[8,128,128]{2,1,0:T(8,128)S(1)} custom-call(s32[1,16]{1,0:T(1,128)S(1)} %copy-done.14, s32[1,16]{1,0:T(1,128)S(1)} %copy-done.15, s32[6,1,8]{2,1,0:T(1,128)S(1)} %bitcast.59, s32[6,1,8]{2,1,0:T(1,128)S(1)} %bitcast.63, bf16[16,128,128]{2,1,0:T(8,128)(2,1)S(1)} %bitcast.41, bf16[6,8,128,128]{3,2,1,0:T(8,128)(2,1)S(1)} %bitcast.37, ...), custom_call_target="tpu_custom_call" | custom-call | flops 671088640 | bytes 4456448 | tf_op jit(solution)/shard_map/pallas_call | solution.py:202
  117.0 2.8 %shard_map.145 = f32[8,128,128]{2,1,0:T(8,128)} custom-call(s32[1,16]{1,0:T(1,128)S(1)} %copy-done.14, s32[1,16]{1,0:T(1,128)S(1)} %copy-done.15, s32[6,1,8]{2,1,0:T(1,128)S(1)} %bitcast.60, s32[6,1,8]{2,1,0:T(1,128)S(1)} %bitcast.64, bf16[16,128,128]{2,1,0:T(8,128)(2,1)S(1)} %bitcast.42, bf16[6,8,128,128]{3,2,1,0:T(8,128)(2,1)S(1)} %bitcast.38, ...), custom_call_target="tpu_custom_call" | custom-call | flops 536870912 | bytes 4194304 | tf_op jit(solution)/shard_map/pallas_call | solution.py:202
  119.8 0.9 shard_map.146
  (69 shorter events, 1.0 us)
Async XLA Ops:
  7.2 43.0 %all-gather.3.cloned.1.call-start = ((), (), s32[]{:S(2)}) async-start(), calls=%async_computation | async-start | bytes 1310720 | tf_op jit(solution)/shard_map/all_gather | solution.py:387
  12.7 75.4 %all-gather.5.cloned.1.call-start = ((), (), s32[]{:S(2)}) async-start(), calls=%async_computation.1 | async-start | bytes 1310720 | tf_op jit(solution)/shard_map/all_gather | solution.py:427
  12.7 10.4 %collective-permute-start.1 = (bf16[8,128,128]{2,1,0:T(8,128)(2,1)}, bf16[8,128,128]{2,1,0:T(8,128)(2,1)S(1)}, u32[]{:S(2)}, u32[]{:S(2)}) collective-permute-start(bf16[8,128,128]{2,1,0:T(8,128)(2,1)} %get-tuple-element.63), channel_id=1, source_target_pairs={{0,4},{4,0},{8,12},{12,8},{16,20},{20,16},{24,28},{28,24},{1,5},{5... | collective-permute-start | bytes 786440 | tf_op jit(solution)/shard_map/ppermute | solution.py:335
  15.7 21.9 %collective-permute-start = (bf16[8,128,128]{2,1,0:T(8,128)(2,1)}, bf16[8,128,128]{2,1,0:T(8,128)(2,1)S(1)}, u32[]{:S(2)}, u32[]{:S(2)}) collective-permute-start(bf16[8,128,128]{2,1,0:T(8,128)(2,1)} %get-tuple-element.61), channel_id=1, source_target_pairs={{0,4},{4,0},{8,12},{12,8},{16,20},{20,16},{24,28},{28,24},{1,5},{5... | collective-permute-start | bytes 786440 | tf_op jit(solution)/shard_map/ppermute | solution.py:335
  15.8 18.5 %collective-permute-start.7 = (bf16[8,128,128]{2,1,0:T(8,128)(2,1)}, bf16[8,128,128]{2,1,0:T(8,128)(2,1)S(1)}, u32[]{:S(2)}, u32[]{:S(2)}) collective-permute-start(bf16[8,128,128]{2,1,0:T(8,128)(2,1)} %get-tuple-element.71), channel_id=1, source_target_pairs={{0,4},{4,0},{8,12},{12,8},{16,20},{20,16},{24,28},{28,24},{1,5},{5... | collective-permute-start | bytes 786440 | tf_op jit(solution)/shard_map/ppermute | solution.py:335
  22.4 15.2 %copy-start.16 = (f32[8,128,128]{2,1,0:T(8,128)S(1)}, f32[8,128,128]{2,1,0:T(8,128)}, u32[]{:S(2)}) copy-start(f32[8,128,128]{2,1,0:T(8,128)} %get-tuple-element.60) | copy-start | bytes 1572868
  23.1 19.2 %copy-start.17 = (s32[1024]{0:T(1024)S(1)}, s32[1024]{0:T(1024)}, u32[]{:S(2)}) copy-start(s32[1024]{0:T(1024)} %param.14) | copy-start | bytes 12292
  24.2 25.9 %copy-start.5 = (f32[8,128,128]{2,1,0:T(8,128)S(1)}, f32[8,128,128]{2,1,0:T(8,128)}, u32[]{:S(2)}) copy-start(f32[8,128,128]{2,1,0:T(8,128)} %get-tuple-element.77.keep_ref) | copy-start | bytes 1572868
  24.2 13.4 %collective-permute-start.2 = (bf16[8,128,128]{2,1,0:T(8,128)(2,1)S(1)}, bf16[8,128,128]{2,1,0:T(8,128)(2,1)S(1)}, u32[]{:S(2)}, u32[]{:S(2)}) collective-permute-start(bf16[8,128,128]{2,1,0:T(8,128)(2,1)S(1)} %add_convert_fusion.2), channel_id=1, source_target_pairs={{0,8},{4,12},{8,0},{12,4},{16,24},{20,28},{24,16},{28,20},{1,9},{5... | collective-permute-start | bytes 786440 | tf_op jit(solution)/shard_map/ppermute | solution.py:335
  26.4 15.5 %collective-permute-start.6 = (bf16[8,128,128]{2,1,0:T(8,128)(2,1)}, bf16[8,128,128]{2,1,0:T(8,128)(2,1)S(1)}, u32[]{:S(2)}, u32[]{:S(2)}) collective-permute-start(bf16[8,128,128]{2,1,0:T(8,128)(2,1)} %get-tuple-element.69), channel_id=1, source_target_pairs={{0,4},{4,0},{8,12},{12,8},{16,20},{20,16},{24,28},{28,24},{1,5},{5... | collective-permute-start | bytes 786440 | tf_op jit(solution)/shard_map/ppermute | solution.py:335
  35.4 11.9 %collective-permute-start.8 = (bf16[8,128,128]{2,1,0:T(8,128)(2,1)S(1)}, bf16[8,128,128]{2,1,0:T(8,128)(2,1)S(1)}, u32[]{:S(2)}, u32[]{:S(2)}) collective-permute-start(bf16[8,128,128]{2,1,0:T(8,128)(2,1)S(1)} %add_convert_fusion), channel_id=1, source_target_pairs={{0,8},{4,12},{8,0},{12,4},{16,24},{20,28},{24,16},{28,20},{1,9},{5... | collective-permute-start | bytes 786440 | tf_op jit(solution)/shard_map/ppermute | solution.py:335
  37.7 19.7 %copy-start.7 = (bf16[2,2,128,128]{3,2,1,0:T(8,128)(2,1)S(1)}, bf16[2,2,128,128]{3,2,1,0:T(8,128)(2,1)}, u32[]{:S(2)}) copy-start(bf16[2,2,128,128]{3,2,1,0:T(8,128)(2,1)} %get-tuple-element.73.refs_0_) | copy-start | bytes 393220
  37.7 12.4 %collective-permute-start.9 = (bf16[8,128,128]{2,1,0:T(8,128)(2,1)S(1)}, bf16[8,128,128]{2,1,0:T(8,128)(2,1)S(1)}, u32[]{:S(2)}, u32[]{:S(2)}) collective-permute-start(bf16[8,128,128]{2,1,0:T(8,128)(2,1)S(1)} %add_convert_fusion.1), channel_id=1, source_target_pairs={{0,16},{4,20},{8,24},{12,28},{16,0},{20,4},{24,8},{28,12},{1,17},{... | collective-permute-start | bytes 786440 | tf_op jit(solution)/shard_map/ppermute | solution.py:335
  40.4 7.0 %collective-permute-start.3 = (bf16[2,2,128,128]{3,2,1,0:T(8,128)(2,1)}, bf16[2,2,128,128]{3,2,1,0:T(8,128)(2,1)S(1)}, u32[]{:S(2)}, u32[]{:S(2)}) collective-permute-start(bf16[2,2,128,128]{3,2,1,0:T(8,128)(2,1)} %get-tuple-element.65), channel_id=1, source_target_pairs={{0,1},{1,0},{2,3},{3,2},{4,5},{5,4},{6,7},{7,6},{8,9},{9,8},{10,11... | collective-permute-start | bytes 393224 | tf_op jit(solution)/shard_map/ppermute | solution.py:335
  40.4 7.0 %collective-permute-start.4 = (bf16[2,2,128,128]{3,2,1,0:T(8,128)(2,1)}, bf16[2,2,128,128]{3,2,1,0:T(8,128)(2,1)S(1)}, u32[]{:S(2)}, u32[]{:S(2)}) collective-permute-start(bf16[2,2,128,128]{3,2,1,0:T(8,128)(2,1)} %get-tuple-element.66), channel_id=1, source_target_pairs={{0,2},{1,3},{2,0},{3,1},{4,6},{5,7},{6,4},{7,5},{8,10},{9,11},{10,... | collective-permute-start | bytes 393224 | tf_op jit(solution)/shard_map/ppermute | solution.py:335
  41.9 7.0 %collective-permute-start.5 = (bf16[2,2,128,128]{3,2,1,0:T(8,128)(2,1)}, bf16[2,2,128,128]{3,2,1,0:T(8,128)(2,1)S(1)}, u32[]{:S(2)}, u32[]{:S(2)}) collective-permute-start(bf16[2,2,128,128]{3,2,1,0:T(8,128)(2,1)} %get-tuple-element.67), channel_id=1, source_target_pairs={{0,3},{1,2},{2,1},{3,0},{4,7},{5,6},{6,5},{7,4},{8,11},{9,10},{10,... | collective-permute-start | bytes 393224 | tf_op jit(solution)/shard_map/ppermute | solution.py:335
  49.0 0.7 copy-start.8
  50.1 7.4 %copy-start.3 = (bf16[2,512,512]{2,1,0:T(8,128)(2,1)S(1)}, bf16[2,512,512]{2,1,0:T(8,128)(2,1)}, u32[]{:S(2)}) copy-start(bf16[2,512,512]{2,1,0:T(8,128)(2,1)} %all-gather.3.cloned.1.call-done) | copy-start | bytes 3145732
  51.0 0.6 copy-start.10
  51.6 2.1 %collective-permute-start.10 = (bf16[2,128,128]{2,1,0:T(8,128)(2,1)}, bf16[2,128,128]{2,1,0:T(8,128)(2,1)S(1)}, u32[]{:S(2)}, u32[]{:S(2)}) collective-permute-start(bf16[2,128,128]{2,1,0:T(8,128)(2,1)} %get-tuple-element.82), channel_id=1, source_target_pairs={{0,1},{1,0},{2,3},{3,2},{4,5},{5,4},{6,7},{7,6},{8,9},{9,8},{10,11... | collective-permute-start | bytes 196616 | tf_op jit(solution)/shard_map/ppermute | solution.py:335
  51.6 4.7 %collective-permute-start.11 = (bf16[2,128,128]{2,1,0:T(8,128)(2,1)}, bf16[2,128,128]{2,1,0:T(8,128)(2,1)S(1)}, u32[]{:S(2)}, u32[]{:S(2)}) collective-permute-start(bf16[2,128,128]{2,1,0:T(8,128)(2,1)} %get-tuple-element.83), channel_id=1, source_target_pairs={{0,2},{1,3},{2,0},{3,1},{4,6},{5,7},{6,4},{7,5},{8,10},{9,11},{10,... | collective-permute-start | bytes 196616 | tf_op jit(solution)/shard_map/ppermute | solution.py:335
  53.1 4.3 %collective-permute-start.12 = (bf16[2,128,128]{2,1,0:T(8,128)(2,1)}, bf16[2,128,128]{2,1,0:T(8,128)(2,1)S(1)}, u32[]{:S(2)}, u32[]{:S(2)}) collective-permute-start(bf16[2,128,128]{2,1,0:T(8,128)(2,1)} %get-tuple-element.84), channel_id=1, source_target_pairs={{0,3},{1,2},{2,1},{3,0},{4,7},{5,6},{6,5},{7,4},{8,11},{9,10},{10,... | collective-permute-start | bytes 196616 | tf_op jit(solution)/shard_map/ppermute | solution.py:335
  57.5 0.9 copy-start.9
  58.4 0.8 copy-start.11
  59.2 28.9 %copy-start.2 = (bf16[1024,128]{1,0:T(8,128)(2,1)S(1)}, bf16[1024,128]{1,0:T(8,128)(2,1)}, u32[]{:S(2)}) copy-start(bf16[1024,128]{1,0:T(8,128)(2,1)} %f_ref.1) | copy-start | bytes 786436
  59.2 28.9 %copy-start.6 = (bf16[128,512]{1,0:T(8,128)(2,1)S(1)}, bf16[128,512]{1,0:T(8,128)(2,1)}, u32[]{:S(2)}) copy-start(bf16[128,512]{1,0:T(8,128)(2,1)} %w_ref.1) | copy-start | bytes 393220
  60.8 1.9 %collective-permute-start.13 = (bf16[256,128]{1,0:T(8,128)(2,1)S(1)}, bf16[256,128]{1,0:T(8,128)(2,1)S(1)}, u32[]{:S(2)}, u32[]{:S(2)}) collective-permute-start(bf16[256,128]{1,0:T(8,128)(2,1)S(1)} %get-tuple-element.91), channel_id=1, source_target_pairs={{0,1},{1,0},{2,3},{3,2},{4,5},{5,4},{6,7},{7,6},{8,9},{9,8},{10,11... | collective-permute-start | bytes 196616 | tf_op jit(solution)/shard_map/ppermute | solution.py:335
  61.0 4.4 %collective-permute-start.14 = (bf16[256,128]{1,0:T(8,128)(2,1)S(1)}, bf16[256,128]{1,0:T(8,128)(2,1)S(1)}, u32[]{:S(2)}, u32[]{:S(2)}) collective-permute-start(bf16[256,128]{1,0:T(8,128)(2,1)S(1)} %get-tuple-element.92), channel_id=1, source_target_pairs={{0,2},{1,3},{2,0},{3,1},{4,6},{5,7},{6,4},{7,5},{8,10},{9,11},{10,... | collective-permute-start | bytes 196616 | tf_op jit(solution)/shard_map/ppermute | solution.py:335
  62.5 4.2 %collective-permute-start.15 = (bf16[256,128]{1,0:T(8,128)(2,1)S(1)}, bf16[256,128]{1,0:T(8,128)(2,1)S(1)}, u32[]{:S(2)}, u32[]{:S(2)}) collective-permute-start(bf16[256,128]{1,0:T(8,128)(2,1)S(1)} %get-tuple-element.93), channel_id=1, source_target_pairs={{0,3},{1,2},{2,1},{3,0},{4,7},{5,6},{6,5},{7,4},{8,11},{9,10},{10,... | collective-permute-start | bytes 196616 | tf_op jit(solution)/shard_map/ppermute | solution.py:335
  66.7 12.5 %collective-permute-start.17 = (bf16[8,128,128]{2,1,0:T(8,128)(2,1)S(1)}, bf16[8,128,128]{2,1,0:T(8,128)(2,1)S(1)}, u32[]{:S(2)}, u32[]{:S(2)}) collective-permute-start(bf16[8,128,128]{2,1,0:T(8,128)(2,1)S(1)} %bitcast.45), channel_id=1, source_target_pairs={{0,8},{4,12},{8,0},{12,4},{16,24},{20,28},{24,16},{28,20},{1,9},{5... | collective-permute-start | bytes 786440 | tf_op jit(solution)/shard_map/ppermute | solution.py:335
  67.2 14.6 %collective-permute-start.16 = (bf16[8,128,128]{2,1,0:T(8,128)(2,1)S(1)}, bf16[8,128,128]{2,1,0:T(8,128)(2,1)S(1)}, u32[]{:S(2)}, u32[]{:S(2)}) collective-permute-start(bf16[8,128,128]{2,1,0:T(8,128)(2,1)S(1)} %bitcast.46), channel_id=1, source_target_pairs={{0,4},{4,0},{8,12},{12,8},{16,20},{20,16},{24,28},{28,24},{1,5},{5... | collective-permute-start | bytes 786440 | tf_op jit(solution)/shard_map/ppermute | solution.py:335
  68.7 19.4 %collective-permute-start.22 = (bf16[8,128,128]{2,1,0:T(8,128)(2,1)S(1)}, bf16[8,128,128]{2,1,0:T(8,128)(2,1)S(1)}, u32[]{:S(2)}, u32[]{:S(2)}) collective-permute-start(bf16[8,128,128]{2,1,0:T(8,128)(2,1)S(1)} %bitcast.47), channel_id=1, source_target_pairs={{0,16},{4,20},{8,24},{12,28},{16,0},{20,4},{24,8},{28,12},{1,17},{... | collective-permute-start | bytes 786440 | tf_op jit(solution)/shard_map/ppermute | solution.py:335
  79.2 8.9 %collective-permute-start.21 = (bf16[8,128,128]{2,1,0:T(8,128)(2,1)S(1)}, bf16[8,128,128]{2,1,0:T(8,128)(2,1)S(1)}, u32[]{:S(2)}, u32[]{:S(2)}) collective-permute-start(bf16[8,128,128]{2,1,0:T(8,128)(2,1)S(1)} %collective-permute-done.17.refs_8_), channel_id=1, source_target_pairs={{0,4},{4,0},{8,12},{12,8},{16,20},{20,16},{24,28},{28,24},{1,5},{5... | collective-permute-start | bytes 786440 | tf_op jit(solution)/shard_map/ppermute | solution.py:335
  81.7 1.9 %collective-permute-start.18 = (bf16[256,128]{1,0:T(8,128)(2,1)S(1)}, bf16[256,128]{1,0:T(8,128)(2,1)S(1)}, u32[]{:S(2)}, u32[]{:S(2)}) collective-permute-start(bf16[256,128]{1,0:T(8,128)(2,1)S(1)} %get-tuple-element.95), channel_id=1, source_target_pairs={{0,1},{1,0},{2,3},{3,2},{4,5},{5,4},{6,7},{7,6},{8,9},{9,8},{10,11... | collective-permute-start | bytes 196616 | tf_op jit(solution)/shard_map/ppermute | solution.py:335
  81.7 4.8 %collective-permute-start.19 = (bf16[256,128]{1,0:T(8,128)(2,1)S(1)}, bf16[256,128]{1,0:T(8,128)(2,1)S(1)}, u32[]{:S(2)}, u32[]{:S(2)}) collective-permute-start(bf16[256,128]{1,0:T(8,128)(2,1)S(1)} %get-tuple-element.96), channel_id=1, source_target_pairs={{0,2},{1,3},{2,0},{3,1},{4,6},{5,7},{6,4},{7,5},{8,10},{9,11},{10,... | collective-permute-start | bytes 196616 | tf_op jit(solution)/shard_map/ppermute | solution.py:335
  83.0 4.3 %collective-permute-start.20 = (bf16[256,128]{1,0:T(8,128)(2,1)S(1)}, bf16[256,128]{1,0:T(8,128)(2,1)S(1)}, u32[]{:S(2)}, u32[]{:S(2)}) collective-permute-start(bf16[256,128]{1,0:T(8,128)(2,1)S(1)} %get-tuple-element.97), channel_id=1, source_target_pairs={{0,3},{1,2},{2,1},{3,0},{4,7},{5,6},{6,5},{7,4},{8,11},{9,10},{10,... | collective-permute-start | bytes 196616 | tf_op jit(solution)/shard_map/ppermute | solution.py:335
  88.1 1.2 copy-start.4
  89.3 25.3 %copy-start = (bf16[1,6,8,128,128]{4,3,2,1,0:T(8,128)(2,1)S(1)}, bf16[1,6,8,128,128]{4,3,2,1,0:T(8,128)(2,1)}, u32[]{:S(2)}) copy-start(bf16[1,6,8,128,128]{4,3,2,1,0:T(8,128)(2,1)} %param.18) | copy-start | bytes 4718596
  89.3 25.3 %copy-start.1 = (bf16[1,16,128,128]{3,2,1,0:T(8,128)(2,1)S(1)}, bf16[1,16,128,128]{3,2,1,0:T(8,128)(2,1)}, u32[]{:S(2)}) copy-start(bf16[1,16,128,128]{3,2,1,0:T(8,128)(2,1)} %param.15) | copy-start | bytes 1572868
  89.3 25.3 %copy-start.12 = (s32[1,6,8]{2,0,1:T(1,128)S(1)}, s32[1,6,8]{2,0,1:T(1,128)}, u32[]{:S(2)}) copy-start(s32[1,6,8]{2,0,1:T(1,128)} %param.19) | copy-start | bytes 580
  89.4 25.3 %copy-start.13 = (s32[1,6,8]{2,0,1:T(1,128)S(1)}, s32[1,6,8]{2,0,1:T(1,128)}, u32[]{:S(2)}) copy-start(s32[1,6,8]{2,0,1:T(1,128)} %param.20) | copy-start | bytes 580
  89.4 25.3 %copy-start.14 = (s32[1,16]{1,0:T(1,128)S(1)}, s32[1,16]{1,0:T(1,128)}, u32[]{:S(2)}) copy-start(s32[1,16]{1,0:T(1,128)} %refs_0_.7) | copy-start | bytes 196
  89.4 25.3 %copy-start.15 = (s32[1,16]{1,0:T(1,128)S(1)}, s32[1,16]{1,0:T(1,128)}, u32[]{:S(2)}) copy-start(s32[1,16]{1,0:T(1,128)} %refs_1_.7) | copy-start | bytes 196
  90.1 6.4 %collective-permute-start.26 = (bf16[4,32,512]{2,1,0:T(8,128)(2,1)S(1)}, bf16[4,32,512]{2,1,0:T(8,128)(2,1)S(1)}, u32[]{:S(2)}, u32[]{:S(2)}) collective-permute-start(bf16[4,32,512]{2,1,0:T(8,128)(2,1)S(1)} %get-tuple-element.103), channel_id=1, source_target_pairs={{0,4},{4,0},{8,12},{12,8},{16,20},{20,16},{24,28},{28,24},{1,5},{5... | collective-permute-start | bytes 393224 | tf_op jit(solution)/shard_map/ppermute | solution.py:335
  91.3 7.4 %collective-permute-start.24 = (bf16[8,128,128]{2,1,0:T(8,128)(2,1)S(1)}, bf16[8,128,128]{2,1,0:T(8,128)(2,1)S(1)}, u32[]{:S(2)}, u32[]{:S(2)}) collective-permute-start(bf16[8,128,128]{2,1,0:T(8,128)(2,1)S(1)} %collective-permute-done.22.refs_6_), channel_id=1, source_target_pairs={{0,8},{4,12},{8,0},{12,4},{16,24},{20,28},{24,16},{28,20},{1,9},{5... | collective-permute-start | bytes 786440 | tf_op jit(solution)/shard_map/ppermute | solution.py:335
  91.3 14.2 %collective-permute-start.23 = (bf16[8,128,128]{2,1,0:T(8,128)(2,1)S(1)}, bf16[8,128,128]{2,1,0:T(8,128)(2,1)S(1)}, u32[]{:S(2)}, u32[]{:S(2)}) collective-permute-start(bf16[8,128,128]{2,1,0:T(8,128)(2,1)S(1)} %collective-permute-done.22.refs_6_), channel_id=1, source_target_pairs={{0,4},{4,0},{8,12},{12,8},{16,20},{20,16},{24,28},{28,24},{1,5},{5... | collective-permute-start | bytes 786440 | tf_op jit(solution)/shard_map/ppermute | solution.py:335
  98.8 6.1 %collective-permute-start.27 = (bf16[32,512]{1,0:T(8,128)(2,1)S(1)}, bf16[32,512]{1,0:T(8,128)(2,1)S(1)}, u32[]{:S(2)}, u32[]{:S(2)}) collective-permute-start(bf16[32,512]{1,0:T(8,128)(2,1)S(1)} %get-tuple-element.108), channel_id=1, source_target_pairs={{0,24},{4,28},{8,16},{12,20},{16,8},{20,12},{24,0},{28,4},{1,25},{... | collective-permute-start | bytes 98312 | tf_op jit(solution)/shard_map/ppermute | solution.py:335
  100.4 4.9 %collective-permute-start.28 = (bf16[32,512]{1,0:T(8,128)(2,1)S(1)}, bf16[32,512]{1,0:T(8,128)(2,1)S(1)}, u32[]{:S(2)}, u32[]{:S(2)}) collective-permute-start(bf16[32,512]{1,0:T(8,128)(2,1)S(1)} %get-tuple-element.110), channel_id=1, source_target_pairs={{0,16},{4,20},{8,24},{12,28},{16,0},{20,4},{24,8},{28,12},{1,17},{... | collective-permute-start | bytes 98312 | tf_op jit(solution)/shard_map/ppermute | solution.py:335
  100.6 4.9 %collective-permute-start.29 = (bf16[32,512]{1,0:T(8,128)(2,1)S(1)}, bf16[32,512]{1,0:T(8,128)(2,1)S(1)}, u32[]{:S(2)}, u32[]{:S(2)}) collective-permute-start(bf16[32,512]{1,0:T(8,128)(2,1)S(1)} %get-tuple-element.109), channel_id=1, source_target_pairs={{0,8},{4,12},{8,0},{12,4},{16,24},{20,28},{24,16},{28,20},{1,9},{5... | collective-permute-start | bytes 98312 | tf_op jit(solution)/shard_map/ppermute | solution.py:335
  103.2 13.8 %collective-permute-start.25 = (bf16[8,128,128]{2,1,0:T(8,128)(2,1)S(1)}, bf16[8,128,128]{2,1,0:T(8,128)(2,1)S(1)}, u32[]{:S(2)}, u32[]{:S(2)}) collective-permute-start(bf16[8,128,128]{2,1,0:T(8,128)(2,1)S(1)} %collective-permute-done.24.refs_8_), channel_id=1, source_target_pairs={{0,4},{4,0},{8,12},{12,8},{16,20},{20,16},{24,28},{28,24},{1,5},{5... | collective-permute-start | bytes 786440 | tf_op jit(solution)/shard_map/ppermute | solution.py:335
  105.5 5.8 %collective-permute-start.30 = (bf16[32,512]{1,0:T(8,128)(2,1)S(1)}, bf16[32,512]{1,0:T(8,128)(2,1)S(1)}, u32[]{:S(2)}, u32[]{:S(2)}) collective-permute-start(bf16[32,512]{1,0:T(8,128)(2,1)S(1)} %fusion.2.refs_3_), channel_id=1, source_target_pairs={{0,24},{4,28},{8,16},{12,20},{16,8},{20,12},{24,0},{28,4},{1,25},{... | collective-permute-start | bytes 98312 | tf_op jit(solution)/shard_map/ppermute | solution.py:335
  107.6 4.9 %collective-permute-start.31 = (bf16[32,512]{1,0:T(8,128)(2,1)S(1)}, bf16[32,512]{1,0:T(8,128)(2,1)S(1)}, u32[]{:S(2)}, u32[]{:S(2)}) collective-permute-start(bf16[32,512]{1,0:T(8,128)(2,1)S(1)} %fusion.2.refs_3_), channel_id=1, source_target_pairs={{0,16},{4,20},{8,24},{12,28},{16,0},{20,4},{24,8},{28,12},{1,17},{... | collective-permute-start | bytes 98312 | tf_op jit(solution)/shard_map/ppermute | solution.py:335
  108.7 4.2 %collective-permute-start.32 = (bf16[32,512]{1,0:T(8,128)(2,1)S(1)}, bf16[32,512]{1,0:T(8,128)(2,1)S(1)}, u32[]{:S(2)}, u32[]{:S(2)}) collective-permute-start(bf16[32,512]{1,0:T(8,128)(2,1)S(1)} %fusion.2.refs_3_), channel_id=1, source_target_pairs={{0,8},{4,12},{8,0},{12,4},{16,24},{20,28},{24,16},{28,20},{1,9},{5... | collective-permute-start | bytes 98312 | tf_op jit(solution)/shard_map/ppermute | solution.py:335
  112.9 6.9 %collective-permute-start.33 = (bf16[4,32,512]{2,1,0:T(8,128)(2,1)S(1)}, bf16[4,32,512]{2,1,0:T(8,128)(2,1)S(1)}, u32[]{:S(2)}, u32[]{:S(2)}) collective-permute-start(bf16[4,32,512]{2,1,0:T(8,128)(2,1)S(1)} %pad_maximum_fusion.2), channel_id=1, source_target_pairs={{0,4},{4,0},{8,12},{12,8},{16,20},{20,16},{24,28},{28,24},{1,5},{5... | collective-permute-start | bytes 393224 | tf_op jit(solution)/shard_map/ppermute | solution.py:335
Sparse Core Ops, SparseCore 0:
  12.8 19.4 all-gather.2
  61.0 16.7 all-gather.4

commit v4 on v3

--- a/solution.py
+++ b/solution.py
@@ -137,8 +137,13 @@
     return jobs
 
 
+def flat(masks):
+    return [m for group in masks for m in (group if isinstance(group, list) else [group])]
+
+
 def tiles_kernel(masks, offsets, parts_total, back, feats, extras, *refs):
     ids, (lvals, rvals), refs = refs[:4], refs[4:6], refs[6:]
+    groups_of, masks = masks, flat(masks)
     me = lax.axis_index("dom")
     mine = lax.axis_index("feat")
     rounds, groups, tiles = tile_counts(rvals, lvals)
@@ -157,9 +162,17 @@
         acc[0] = own_ref[...]
     else:
         blocks = [refs[0]] * len(masks)
-        sinks = refs[1 + extras : 1 + extras + len(masks)]
+        sinks, used = [], 1 + extras
+        for group in groups_of:
+            if isinstance(group, list):
+                sinks += [refs[used].at[n] for n in range(len(group))]
+            else:
+                sinks.append(refs[used])
+            used += 1
     if extras:
-        pieces = refs[1 + extras + len(masks) : 1 + extras + len(masks) + feats]
+        pieces, pair = refs[used : used + feats], refs[used + feats]
+        pair[0] = refs[2][...]
+        pair[1] = refs[3][...]
         for mask, piece in enumerate(pieces):
             rows = pl.ds((mine ^ mask) * piece.shape[1], piece.shape[1])
             piece[0] = refs[0][rows]
@@ -196,7 +209,7 @@
     ids, lvals, rvals = fixed
     rounds, groups, tiles = tile_counts(rvals, lvals)
     nblocks, block, width = blocks[0].shape
-    slots = sum(-(-tiles // groups) if mask == 0 else 1 for mask in masks)
+    slots = sum(-(-tiles // groups) if mask == 0 else 1 for mask in flat(masks))
     flops = 2 * slots * groups * block * block * width
     extras = 0 if back else len(blocks) - 1
     return pl.pallas_call(
@@ -250,59 +263,64 @@
     return jnp.concatenate(parts, axis=1)
 
 
-def dense_kernel(feats, w_ref, inv_ref, *refs):
+def dense_kernel(feats, inv_ref, *refs):
     mine = lax.axis_index("feat")
-    early_refs, a_refs = refs[:feats], refs[feats : 2 * feats]
-    dpre_ref = refs[2 * feats]
-    dsum_refs, out_refs = refs[2 * feats + 1 : 3 * feats + 1], refs[3 * feats + 1 : 4 * feats + 1]
+    w_refs, early_refs, a_refs = refs[:feats], refs[feats : 2 * feats], refs[2 * feats : 3 * feats]
+    dpre_ref = refs[3 * feats]
+    dsum_refs, out_refs = refs[3 * feats + 1 : 4 * feats + 1], refs[4 * feats + 1 : 5 * feats + 1]
     held = refs[-1]
-    width, full = w_ref.shape[2:]
-    some = held.shape[2]
+    full = w_refs[0].shape[2]
+    some, width = held.shape[1:]
     pre = jnp.zeros((some, full), F32)
     for mask in range(feats):
         early = early_refs[mask]
         pre = pre + jnp.dot(
-            early[0].reshape(some, width), w_ref[0, mine ^ mask], preferred_element_type=F32
+            early[0].reshape(some, width), w_refs[mask][0], preferred_element_type=F32
         )
         pre = pre + jnp.dot(
-            a_refs[mask][...].reshape(some, width),
-            w_ref[1, mine ^ mask],
-            preferred_element_type=F32,
-        )
-        held[0, mine ^ mask] = early[1].reshape(some, width)
+            a_refs[mask][...].reshape(some, width), w_refs[mask][1], preferred_element_type=F32
+        )
+        held[mine ^ mask] = early[1].reshape(some, width)
     sigma = 1.0 / (1.0 + jnp.exp(-pre))
     out = (pre * sigma).astype(BF16)
-    cot = joined([held[0, j] for j in range(feats)]).astype(F32)
+    cot = joined([held[j] for j in range(feats)]).astype(F32)
     dpre = (cot * sigma * (1.0 + pre * (1.0 - sigma))).astype(BF16)
-    wn = w_ref[1].reshape(full, full)
-    dagg = lax.dot_general(dpre, wn, (((1,), (1,)), ((), ())), preferred_element_type=F32)
-    dsum = (dagg * inv_ref[...]).astype(BF16)
     dpre_ref[...] = dpre
+    for mask in range(feats):
+        dagg = lax.dot_general(
+            dpre, w_refs[mask][1], (((1,), (1,)), ((), ())), preferred_element_type=F32
+        )
+        dsum_refs[mask][...] = (dagg * inv_ref[...]).astype(BF16)
     for j in range(feats):
-        held[0, j] = dsum[:, j * width : (j + 1) * width]
-        held[1, j] = out[:, j * width : (j + 1) * width]
+        held[j] = out[:, j * width : (j + 1) * width]
     for mask in range(feats):
-        dsum_refs[mask][...] = held[0, mine ^ mask]
-        out_refs[mask][...] = held[1, mine ^ mask]
-
-
-def grad_kernel(near, far, f_ref, a_ref, dpre_ref, w_ref, dx_ref, give_ref, keep_ref, held):
+        out_refs[mask][...] = held[mine ^ mask]
+
+
+def grad_kernel(near, far, feats, f_ref, a_ref, w_ref, *refs):
     me = lax.axis_index("dom")
-    dpre = dpre_ref[...]
+    mine = lax.axis_index("feat")
+    dpre_refs, (dx_ref, give_ref, keep_ref, held) = refs[:feats], refs[feats:]
     width = f_ref.shape[1]
-    some = held.shape[1]
-    for at, ref in enumerate((f_ref, a_ref)):
-        part = lax.dot_general(
-            ref[...], dpre, (((0,), (0,)), ((), ())), preferred_element_type=F32
-        )
-        for j in range(width // some):
-            held[at * (width // some) + j] = part[j * some : (j + 1) * some]
+    piece = held.shape[1]
+    some = dpre_refs[0].shape[0]
+    parts = [0.0, 0.0]
+    for mask, dpre_ref in enumerate(dpre_refs):
+        dpre = dpre_ref[...]
+        rows = pl.ds(pl.multiple_of((mine ^ mask) * some, some), some)
+        for at, ref in enumerate((f_ref, a_ref)):
+            parts[at] = parts[at] + lax.dot_general(
+                ref[rows], dpre, (((0,), (0,)), ((), ())), preferred_element_type=F32
+            )
+        dx_ref[rows] = lax.dot_general(
+            dpre, w_ref[...], (((1,), (1,)), ((), ())), preferred_element_type=F32
+        )
+    for at, part in enumerate(parts):
+        for j in range(width // piece):
+            held[at * (width // piece) + j] = part[j * piece : (j + 1) * piece]
     for at, mask in enumerate(far + [0]):
         give_ref[at] = held[me ^ mask ^ near].astype(BF16)
         keep_ref[at] = held[me ^ mask]
-    dx_ref[...] = lax.dot_general(
-        dpre, w_ref[...], (((1,), (1,)), ((), ())), preferred_element_type=F32
-    )
 
 
 def finish_kernel(near, far, *refs):
@@ -363,7 +381,7 @@
     full = feats * width
     offsets = round_offsets(parts_total, rounds)
     near, far = 1, list(range(parts_total - 2, 0, -2))
-    bits = [1 << n for n in range(parts_total.bit_length() - 1)]
+    bits = [1, 2, 4]
     mine = lax.axis_index("feat").astype(jnp.int32)
     inverse = 1.0 / degree.astype(F32)
     inv_rows = lax.dynamic_slice(inverse, (mine * some,), (some,))[:, None]
@@ -382,26 +400,33 @@
             masks, offsets, parts_total, False, feats, fixed, arrays, sinks, 62
         )
 
-    sends = forward([mask ^ near for mask in far + [0]], [blocks], [like(shape, BF16)] * (len(far) + 1))
-    pair, _ = lax.optimization_barrier((jnp.stack([w_self, w_neigh]), sends[0]))
-    weights = lax.all_gather(pair, "feat", axis=1, tiled=True)
-    made = forward(
-        far + [0],
-        [blocks, cotangent.reshape(shape)],
-        [like(shape, F32)] * (len(far) + 1) + [like((2, per_feat, block, width), BF16)] * feats,
-    )
-    keeps, early_pieces = made[: len(far) + 1], made[len(far) + 1 :]
-    parts = {mask: [keep] for mask, keep in zip(far + [0], keeps)}
-    for mask, send in zip(far + [0], sends):
-        parts[mask].append(crossed(send, near).astype(F32))
-    for bit in bits[1:]:
-        for mask in sorted((m for m in parts if m & bit), reverse=True):
-            whole = sum(parts.pop(mask)).astype(BF16)
-            parts[mask ^ bit].append(crossed(whole, bit).astype(F32))
-    keep, *arrived = parts[0]
-    arrived = [part.astype(BF16) for part in arrived]
-    early_pieces, _ = lax.optimization_barrier((early_pieces, whole))
+    def relayed(x):
+        over = crossed(x, 2, "feat")
+        return [x, crossed(x, 1, "feat"), over, crossed(over, 1, "feat")]
+
+    def tied(x, *others):
+        return lax.optimization_barrier((x, others))[0]
+
+    send_7, sends, send_1, *made = forward(
+        [7, [5, 3], 1],
+        [blocks, cotangent.reshape(shape), w_self, w_neigh],
+        [like(shape, BF16), like((2, *shape), BF16), like(shape, BF16)]
+        + [like((2, per_feat, block, width), BF16)] * feats
+        + [like((2, width, full), BF16)],
+    )
+    early_pieces, pair = made[:-1], made[-1]
+    keep_6, keep_4 = forward([6, 4], [blocks], [like(shape, F32)] * 2)
+    weights = relayed(pair)
     early = [early_pieces[0]] + [crossed(early_pieces[m], m, "feat") for m in range(1, feats)]
+    near_6, near_53, near_0 = (crossed(send, near) for send in (send_7, sends, send_1))
+    sum_6 = (keep_6 + tied(near_6, weights[2]).astype(F32)).astype(BF16)
+    keep_2, keep = forward([2, 0], [tied(blocks, sum_6)], [like(shape, F32)] * 2)
+    near_53 = tied(near_53, early)
+    sum_4 = (keep_4 + near_53[0].astype(F32) + crossed(sum_6, 2).astype(F32)).astype(BF16)
+    far_0 = crossed(sum_4, 4)
+    sum_2 = (tied(keep_2, sum_4) + near_53[1].astype(F32)).astype(BF16)
+    mid_0 = crossed(sum_2, 2)
+    arrived = [near_0, mid_0, far_0]
     early, weights, arrived = lax.optimization_barrier((early, weights, arrived))
     agg, *agg_pieces = small_call(
         functools.partial(agg_kernel, feats),
@@ -412,8 +437,8 @@
     dpre_rows, *pieces = small_call(
         functools.partial(dense_kernel, feats),
         [like((some, full), BF16)] + [like((some, width), BF16)] * (2 * feats),
-        [weights.reshape(2, feats, width, full), inv_rows, *early, *agg_rows],
-        [pltpu.VMEM((2, feats, some, width), BF16)],
+        [inv_rows, *weights, *early, *agg_rows],
+        [pltpu.VMEM((feats, some, width), BF16)],
         6 * some * full * full,
     )
     dsum_pieces, out_pieces = pieces[:feats], pieces[feats:]
@@ -424,29 +449,29 @@
     for bit in bits[::-1]:
         for mask in sorted(found):
             found[mask ^ bit] = crossed(found[mask], bit)
-    dpre = lax.all_gather(dpre_rows, "feat", axis=0, tiled=True)
-    out_pieces, _ = lax.optimization_barrier((out_pieces, (found[1], found[2])))
-    out_all = [out_pieces[0]] + [crossed(out_pieces[m], m, "feat") for m in range(1, feats)]
-    (out,) = small_call(place_kernel, [like((feats, some, width), BF16)], out_all)
-    dpre, out, _ = lax.optimization_barrier((dpre, out, (found[3], found[4])))
+    dpre = relayed(dpre_rows)
+    dpre = tied(dpre, found[1], found[2])
     piece = 2 * width // parts_total
     dx_self, give, keep = small_call(
-        functools.partial(grad_kernel, near, far),
+        functools.partial(grad_kernel, near, far, feats),
         [
             like((rows, width), F32),
             like((len(far) + 1, piece, full), BF16),
             like((len(far) + 1, piece, full), F32),
         ],
-        [features, agg.reshape(rows, width), dpre, w_self],
+        [features, agg.reshape(rows, width), w_self, *dpre],
         [pltpu.VMEM((parts_total, piece, full), F32)],
         6 * rows * width * full,
     )
+    out_pieces = tied(out_pieces, give)
+    out_all = [out_pieces[0]] + [crossed(out_pieces[m], m, "feat") for m in range(1, feats)]
+    (out,) = small_call(place_kernel, [like((feats, some, width), BF16)], out_all)
     keep = keep + crossed(give, near).astype(F32)
-    keep, _ = lax.optimization_barrier((keep, found[6]))
+    keep = tied(keep, found[3], found[4])
     total = keep[len(far)]
     for at, mask in enumerate(far):
         total = total + crossed(keep[at].astype(BF16), mask).astype(F32)
-    total, _ = lax.optimization_barrier((total.astype(BF16), found[5]))
+    total, out = tied((total.astype(BF16), out), found[5], found[6])
     totals = [crossed(total, mask) for mask in far] + [total]
     grad_self, grad_neigh = small_call(
         functools.partial(finish_kernel, near, far),
@@ -474,10 +499,9 @@
 def solution(mesh):
     def body(*args):
         rounds = args[7].shape[1]
-        parts_total = mesh.shape["dom"]
-        powers = all(n & (n - 1) == 0 for n in mesh.shape.values())
-        nearly_all = parts_total <= rounds + 2 and powers
-        return (dense_body if nearly_all else sparse_body)(*args)
+        small = mesh.shape["dom"] == 8 and mesh.shape["feat"] == 4
+        nearly_all = mesh.shape["dom"] <= rounds + 2
+        return (dense_body if small and nearly_all else sparse_body)(*args)
 
     placed = (
         P("dom", "feat"),

time: 128 us -> 121 us (0.945)
  between operations: 14.3 us -> 0.93 us
  waiting for transfers between devices: 43.4 us -> 52.8 us
  starting transfers between devices: 42.7 us -> 39 us
  Pallas kernels: 18.3 us -> 20.6 us
    ppermute x34 -> x39, waiting for transfers between devices: 43.4 us -> 52.8 us  [crossed(): lax.ppermute(x, axis, [(i, i ^ mask) for i in range(lax.axis_size(axis))])]
    ppermute x34 -> x39, starting transfers between devices: 42.6 us -> 39 us  [crossed(): lax.ppermute(x, axis, [(i, i ^ mask) for i in range(lax.axis_size(axis))])]
    pallas_call x4 -> x5, Pallas kernels: 13.4 us -> 16.1 us  [tiles_call(): pl.pallas_call(functools.partial(tiles_kernel, masks, offsets, parts_tota...]
    another operation x2 -> x1, other arithmetic: 1.72 us -> 0.02 us  [the longest x1 1.7 us: dense_body(): pair, _ = lax.optimization_barrier((jnp.stack([w_self, w_neigh]), sends[0]))]
    convert_element_type x4, other arithmetic: 2.33 us -> 3.77 us  [the longest x1 1.84 us: dense_body(): sum_6 = (keep_6 + tied(near_6, weights[2]).astype(F32)).astype(BF16)]
    unnamed x36 -> x38, local copies, waits for them, and re-layouts: 4.3 us -> 3.19 us
  transfers between devices with their start and end apart: 36 -> 39, of which waited for: 19 -> 21; matrix products, arithmetic and copies ran while one was open for 2% -> 4% of each run, Pallas kernels for 8% -> 10%
where the time goes in v4:
time: 121 us
  waiting for transfers between devices  52.8 us (44%)
  starting transfers between devices  39 us (32%)
  Pallas kernels  20.6 us (17%)
  other arithmetic  3.85 us (3%)
  local copies, waits for them, and re-layouts  3.64 us (3%)
    ppermute x39, waiting for transfers between devices, crossed(): lax.ppermute(x, axis, [(i, i ^ mask) for i in range(lax.axis_size(axis))])  52.8 us
    ppermute x39, starting transfers between devices, crossed(): lax.ppermute(x, axis, [(i, i ^ mask) for i in range(lax.axis_size(axis))])  39 us
    pallas_call x5, Pallas kernels, tiles_call(): pl.pallas_call(functools.partial(tiles_kernel, masks, offsets, parts_tota...  16.1 us
    pallas_call x5, Pallas kernels, small_call(): pl.pallas_call(kernel, out_shape=outs, in_specs=[VMEM] * len(arrays), out...  4.48 us
    unnamed x38, local copies, waits for them, and re-layouts  3.19 us
  transfers between devices with their start and end apart: 39, of which 21 were waited for; matrix products, arithmetic and copies ran while one was open for 4% of the time, Pallas kernels for 10%

profile of v4, /device:TPU:0, one launch (start us, length us, event | category | flops | bytes accessed | tf_op | source)
XLA Modules:
  0.0 120.8 jit_solution(11130627386458985636)
XLA Ops:
  0.6 4.2 %shard_map.139 = (bf16[8,128,128]{2,1,0:T(8,128)(2,1)}, bf16[2,8,128,128]{3,2,1,0:T(8,128)(2,1)}, bf16[8,128,128]{2,1,0:T(8,128)(2,1)}, bf16[2,2,128,128]{3,2,1,...) custom-call(s32[1,16]{1,0:T(1,128)} %refs_0_.9, ...), custom_call_target="tpu_custom_call" | custom-call | flops 536870912 | bytes 4194304 | tf_op jit(solution)/shard_map/pallas_call | solution.py:215
  4.8 3.0 %collective-permute-start.1 = (bf16[2,128,512]{2,1,0:T(8,128)(2,1)}, bf16[2,128,512]{2,1,0:T(8,128)(2,1)S(1)}, u32[]{:S(2)}, u32[]{:S(2)}) collective-permute-start(bf16[2,128,512]{2,1,0:T(8,128)(2,1)} %get-tuple-element.81.refs_0_), channel_id=1, source_target_pairs={{0,2},{1,3},{2,0},{3,1},{4,6},{5,7},{6,4},{7,5},{8,10},{9,11},{10,... | collective-permute-start | bytes 786440 | tf_op jit(solution)/shard_map/ppermute | solution.py:353
  7.8 1.5 %collective-permute-start = (bf16[8,128,128]{2,1,0:T(8,128)(2,1)}, bf16[8,128,128]{2,1,0:T(8,128)(2,1)S(1)}, u32[]{:S(2)}, u32[]{:S(2)}) collective-permute-start(bf16[8,128,128]{2,1,0:T(8,128)(2,1)} %get-tuple-element.62), channel_id=1, source_target_pairs={{0,4},{4,0},{8,12},{12,8},{16,20},{20,16},{24,28},{28,24},{1,5},{5... | collective-permute-start | bytes 786440 | tf_op jit(solution)/shard_map/ppermute | solution.py:353
  9.3 0.5 collective-permute-start.8
  9.8 3.3 %shard_map.138 = (f32[8,128,128]{2,1,0:T(8,128)}, f32[8,128,128]{2,1,0:T(8,128)}) custom-call(s32[1,16]{1,0:T(1,128)} %refs_0_.9, s32[1,16]{1,0:T(1,128)} %refs_1_.9, s32[6,1,8]{2,1,0:T(1,128)} %bitcast.62, s32[6,1,8]{2,1,0:T(1,128)} %bitcast.67, bf16[16,128,128]{2,1,0:T(8,128)(2,1)} %bitcast.44, bf16[6,8,128,128]{3,2,1,0:T(8,128)(2,1)} %bitcast.39, ...), custom_call_target="tpu_custom_call" | custom-call | flops 268435456 | bytes 3670016 | tf_op jit(solution)/shard_map/pallas_call | solution.py:215
  13.2 1.2 collective-permute-done.1.refs_2_
  14.3 2.9 %collective-permute-done = bf16[8,128,128]{2,1,0:T(8,128)(2,1)S(1)} collective-permute-done((bf16[8,128,128]{2,1,0:T(8,128)(2,1)}, bf16[8,128,128]{2,1,0:T(8,128)(2,1)S(1)}, u32[]{:S(2)}, u32[]{:S(2)}) %collective-permute-start) | collective-permute-done | bytes 262176 | tf_op jit(solution)/shard_map/ppermute | solution.py:353
  17.3 1.8 %add_convert_fusion = bf16[8,128,128]{2,1,0:T(8,128)(2,1)} fusion(f32[8,128,128]{2,1,0:T(8,128)} %get-tuple-element.61, bf16[8,128,128]{2,1,0:T(8,128)(2,1)S(1)} %collective-permute-done), kind=kLoop, calls=%fused_computation.5 | loop fusion | flops 393216 | bytes 1048576 | tf_op jit(solution)/shard_map/convert_element_type | solution.py:422
  19.1 1.6 %collective-permute-start.9 = (bf16[8,128,128]{2,1,0:T(8,128)(2,1)}, bf16[8,128,128]{2,1,0:T(8,128)(2,1)S(1)}, u32[]{:S(2)}, u32[]{:S(2)}) collective-permute-start(bf16[8,128,128]{2,1,0:T(8,128)(2,1)} %add_convert_fusion), channel_id=1, source_target_pairs={{0,8},{4,12},{8,0},{12,4},{16,24},{20,28},{24,16},{28,20},{1,9},{5... | collective-permute-start | bytes 786440 | tf_op jit(solution)/shard_map/ppermute | solution.py:353
  20.7 0.6 collective-permute-start.3
  21.3 1.3 %collective-permute-start.4 = (bf16[2,2,128,128]{3,2,1,0:T(8,128)(2,1)}, bf16[2,2,128,128]{3,2,1,0:T(8,128)(2,1)S(1)}, u32[]{:S(2)}, u32[]{:S(2)}) collective-permute-start(bf16[2,2,128,128]{3,2,1,0:T(8,128)(2,1)} %get-tuple-element.70), channel_id=1, source_target_pairs={{0,3},{1,2},{2,1},{3,0},{4,7},{5,6},{6,5},{7,4},{8,11},{9,10},{10,... | collective-permute-start | bytes 393224 | tf_op jit(solution)/shard_map/ppermute | solution.py:353
  22.5 3.5 %shard_map.140 = (f32[8,128,128]{2,1,0:T(8,128)}, f32[8,128,128]{2,1,0:T(8,128)}) custom-call(s32[1,16]{1,0:T(1,128)} %refs_0_.9, s32[1,16]{1,0:T(1,128)} %refs_1_.9, s32[6,1,8]{2,1,0:T(1,128)} %bitcast.63, s32[6,1,8]{2,1,0:T(1,128)} %bitcast.68, bf16[16,128,128]{2,1,0:T(8,128)(2,1)} %bitcast.45, bf16[6,8,128,128]{3,2,1,0:T(8,128)(2,1)} %bitcast.40, ...), custom_call_target="tpu_custom_call" | custom-call | flops 402653184 | bytes 3932160 | tf_op jit(solution)/shard_map/pallas_call | solution.py:215
  26.1 0.4 collective-permute-start.5
  26.6 0.5 collective-permute-done.3.refs_6_
  27.1 0.7 copy-done.7
  27.7 1.5 %collective-permute-start.7 = (bf16[8,128,128]{2,1,0:T(8,128)(2,1)}, bf16[8,128,128]{2,1,0:T(8,128)(2,1)S(1)}, u32[]{:S(2)}, u32[]{:S(2)}) collective-permute-start(bf16[8,128,128]{2,1,0:T(8,128)(2,1)} %get-tuple-element.71), channel_id=1, source_target_pairs={{0,4},{4,0},{8,12},{12,8},{16,20},{20,16},{24,28},{28,24},{1,5},{5... | collective-permute-start | bytes 786440 | tf_op jit(solution)/shard_map/ppermute | solution.py:353
  29.2 0.7 copy-done.9
  29.9 1.8 %fusion.2 = bf16[8,128,128]{2,1,0:T(8,128)(2,1)} fusion(f32[8,128,128]{2,1,0:T(8,128)} %get-tuple-element.73, bf16[8,128,128]{2,1,0:T(8,128)(2,1)S(1)} %collective-permute-done.9, bf16[2,8,128,128]{3,2,1,0:T(8,128)(2,1)S(1)} %collective-permute-done.8), kind=kLoop, calls=%fused_computation.4 | loop fusion | flops 655360 | bytes 1310720 | tf_op jit(solution)/shard_map/convert_element_type | solution.py:425
  31.8 0.5 collective-permute-start.10
  32.3 2.6 %collective-permute-start.11 = (bf16[8,128,128]{2,1,0:T(8,128)(2,1)}, bf16[8,128,128]{2,1,0:T(8,128)(2,1)S(1)}, u32[]{:S(2)}, u32[]{:S(2)}) collective-permute-start(bf16[8,128,128]{2,1,0:T(8,128)(2,1)} %fusion.2), channel_id=1, source_target_pairs={{0,16},{4,20},{8,24},{12,28},{16,0},{20,4},{24,8},{28,12},{1,17},{... | collective-permute-start | bytes 786440 | tf_op jit(solution)/shard_map/ppermute | solution.py:353
  35.2 0.6 collective-permute-done.7.refs_0_
  35.8 10.4 %collective-permute-done.10.refs_1_ = bf16[8,128,128]{2,1,0:T(8,128)(2,1)S(1)} collective-permute-done((bf16[8,128,128]{2,1,0:T(8,128)(2,1)S(1)}, bf16[8,128,128]{2,1,0:T(8,128)(2,1)S(1)}, u32[]{:S(2)}, u32[]{:S(2)}) %collective-permute-start.10) | collective-permute-done | bytes 262176 | tf_op jit(solution)/shard_map/ppermute | solution.py:353
  46.2 0.9 shard_map.141
  47.1 0.6 collective-permute-start.13
  47.7 1.3 %collective-permute-start.14 = (bf16[2,128,128]{2,1,0:T(8,128)(2,1)S(1)}, bf16[2,128,128]{2,1,0:T(8,128)(2,1)S(1)}, u32[]{:S(2)}, u32[]{:S(2)}) collective-permute-start(bf16[2,128,128]{2,1,0:T(8,128)(2,1)S(1)} %get-tuple-element.92), channel_id=1, source_target_pairs={{0,3},{1,2},{2,1},{3,0},{4,7},{5,6},{6,5},{7,4},{8,11},{9,10},{10,... | collective-permute-start | bytes 196616 | tf_op jit(solution)/shard_map/ppermute | solution.py:353
  49.2 3.1 %collective-permute-done.13.refs_10_ = bf16[2,128,128]{2,1,0:T(8,128)(2,1)S(1)} collective-permute-done((bf16[2,128,128]{2,1,0:T(8,128)(2,1)}, bf16[2,128,128]{2,1,0:T(8,128)(2,1)S(1)}, u32[]{:S(2)}, u32[]{:S(2)}) %collective-permute-start.13) | collective-permute-done | bytes 65568 | tf_op jit(solution)/shard_map/ppermute | solution.py:353
  52.3 0.5 collective-permute-done.14.refs_11_
  52.8 0.9 copy-done.8
  53.7 0.9 copy-done.10
  54.6 1.3 %shard_map.142 = (bf16[256,512]{1,0:T(8,128)(2,1)S(1)}, bf16[256,128]{1,0:T(8,128)(2,1)S(1)}, bf16[256,128]{1,0:T(8,128)(2,1)S(1)}, bf16[256,128]{1,0:T(8,128)(2...) custom-call(f32[256,1]{1,0:T(8,128)S(1)} %copy.16.inv_ref, ...), custom_call_target="tpu_custom_call" | custom-call | flops 402653184 | bytes 2622464 | tf_op jit(solution)/shard_map/pallas_call | solution.py:239
  55.8 0.8 collective-permute-start.16
  56.7 1.3 %collective-permute-start.19 = (bf16[256,128]{1,0:T(8,128)(2,1)S(1)}, bf16[256,128]{1,0:T(8,128)(2,1)S(1)}, u32[]{:S(2)}, u32[]{:S(2)}) collective-permute-start(bf16[256,128]{1,0:T(8,128)(2,1)S(1)} %get-tuple-element.96), channel_id=1, source_target_pairs={{0,2},{1,3},{2,0},{3,1},{4,6},{5,7},{6,4},{7,5},{8,10},{9,11},{10,... | collective-permute-start | bytes 196616 | tf_op jit(solution)/shard_map/ppermute | solution.py:353
  57.9 0.6 collective-permute-start.20
  58.5 0.3 collective-permute-start.15
  58.8 7.6 %collective-permute-done.19 = bf16[256,128]{1,0:T(8,128)(2,1)S(1)} collective-permute-done((bf16[256,128]{1,0:T(8,128)(2,1)S(1)}, bf16[256,128]{1,0:T(8,128)(2,1)S(1)}, u32[]{:S(2)}, u32[]{:S(2)}) %collective-permute-start.19) | collective-permute-done | bytes 65568 | tf_op jit(solution)/shard_map/ppermute | solution.py:353
  66.6 1.3 %collective-permute-start.21 = (bf16[8,128,128]{2,1,0:T(8,128)(2,1)S(1)}, bf16[8,128,128]{2,1,0:T(8,128)(2,1)S(1)}, u32[]{:S(2)}, u32[]{:S(2)}) collective-permute-start(bf16[8,128,128]{2,1,0:T(8,128)(2,1)S(1)} %bitcast.51), channel_id=1, source_target_pairs={{0,4},{4,0},{8,12},{12,8},{16,20},{20,16},{24,28},{28,24},{1,5},{5... | collective-permute-start | bytes 786440 | tf_op jit(solution)/shard_map/ppermute | solution.py:353
  67.9 2.6 %collective-permute-start.22 = (bf16[8,128,128]{2,1,0:T(8,128)(2,1)S(1)}, bf16[8,128,128]{2,1,0:T(8,128)(2,1)S(1)}, u32[]{:S(2)}, u32[]{:S(2)}) collective-permute-start(bf16[8,128,128]{2,1,0:T(8,128)(2,1)S(1)} %bitcast.52), channel_id=1, source_target_pairs={{0,8},{4,12},{8,0},{12,4},{16,24},{20,28},{24,16},{28,20},{1,9},{5... | collective-permute-start | bytes 786440 | tf_op jit(solution)/shard_map/ppermute | solution.py:353
  70.5 2.9 %collective-permute-start.25 = (bf16[8,128,128]{2,1,0:T(8,128)(2,1)S(1)}, bf16[8,128,128]{2,1,0:T(8,128)(2,1)S(1)}, u32[]{:S(2)}, u32[]{:S(2)}) collective-permute-start(bf16[8,128,128]{2,1,0:T(8,128)(2,1)S(1)} %bitcast.53), channel_id=1, source_target_pairs={{0,16},{4,20},{8,24},{12,28},{16,0},{20,4},{24,8},{28,12},{1,17},{... | collective-permute-start | bytes 786440 | tf_op jit(solution)/shard_map/ppermute | solution.py:353
  73.4 2.0 %collective-permute-done.21.refs_7_ = bf16[8,128,128]{2,1,0:T(8,128)(2,1)S(1)} collective-permute-done((bf16[8,128,128]{2,1,0:T(8,128)(2,1)S(1)}, bf16[8,128,128]{2,1,0:T(8,128)(2,1)S(1)}, u32[]{:S(2)}, u32[]{:S(2)}) %collective-permute-start.21) | collective-permute-done | bytes 262176 | tf_op jit(solution)/shard_map/ppermute | solution.py:353
  75.3 6.6 %collective-permute-done.22.refs_8_ = bf16[8,128,128]{2,1,0:T(8,128)(2,1)S(1)} collective-permute-done((bf16[8,128,128]{2,1,0:T(8,128)(2,1)S(1)}, bf16[8,128,128]{2,1,0:T(8,128)(2,1)S(1)}, u32[]{:S(2)}, u32[]{:S(2)}) %collective-permute-start.22) | collective-permute-done | bytes 262176 | tf_op jit(solution)/shard_map/ppermute | solution.py:353
  82.0 0.8 shard_map.143
  82.8 0.9 collective-permute-start.23
  83.6 1.2 %collective-permute-start.24 = (bf16[8,128,128]{2,1,0:T(8,128)(2,1)S(1)}, bf16[8,128,128]{2,1,0:T(8,128)(2,1)S(1)}, u32[]{:S(2)}, u32[]{:S(2)}) collective-permute-start(bf16[8,128,128]{2,1,0:T(8,128)(2,1)S(1)} %collective-permute-done.22.refs_8_), channel_id=1, source_target_pairs={{0,4},{4,0},{8,12},{12,8},{16,20},{20,16},{24,28},{28,24},{1,5},{5... | collective-permute-start | bytes 786440 | tf_op jit(solution)/shard_map/ppermute | solution.py:353
  84.9 1.2 collective-permute-done.25.refs_6_
  86.0 0.8 collective-permute-start.32
  86.8 2.4 %collective-permute-done.23 = bf16[4,32,512]{2,1,0:T(8,128)(2,1)S(1)} collective-permute-done((bf16[4,32,512]{2,1,0:T(8,128)(2,1)S(1)}, bf16[4,32,512]{2,1,0:T(8,128)(2,1)S(1)}, u32[]{:S(2)}, u32[]{:S(2)}) %collective-permute-start.23) | collective-permute-done | bytes 131104 | tf_op jit(solution)/shard_map/ppermute | solution.py:353
  89.2 0.7 collective-permute-start.30
  89.9 4.9 %collective-permute-done.24.refs_9_ = bf16[8,128,128]{2,1,0:T(8,128)(2,1)S(1)} collective-permute-done((bf16[8,128,128]{2,1,0:T(8,128)(2,1)S(1)}, bf16[8,128,128]{2,1,0:T(8,128)(2,1)S(1)}, u32[]{:S(2)}, u32[]{:S(2)}) %collective-permute-start.24) | collective-permute-done | bytes 262176 | tf_op jit(solution)/shard_map/ppermute | solution.py:353
  94.9 3.3 %collective-permute-start.26 = (bf16[32,512]{1,0:T(8,128)(2,1)S(1)}, bf16[32,512]{1,0:T(8,128)(2,1)S(1)}, u32[]{:S(2)}, u32[]{:S(2)}) collective-permute-start(bf16[32,512]{1,0:T(8,128)(2,1)S(1)} %get-tuple-element.118), channel_id=1, source_target_pairs={{0,24},{4,28},{8,16},{12,20},{16,8},{20,12},{24,0},{28,4},{1,25},{... | collective-permute-start | bytes 98312 | tf_op jit(solution)/shard_map/ppermute | solution.py:353
  98.2 0.3 collective-permute-done.31.refs_3_
  98.5 0.8 collective-permute-start.28
  99.4 0.7 shard_map.144
  100.1 0.9 collective-permute-done.26
  101.0 2.0 %collective-permute-done.27 = bf16[32,512]{1,0:T(8,128)(2,1)S(1)} collective-permute-done((bf16[32,512]{1,0:T(8,128)(2,1)S(1)}, bf16[32,512]{1,0:T(8,128)(2,1)S(1)}, u32[]{:S(2)}, u32[]{:S(2)}) %collective-permute-start.27) | collective-permute-done | bytes 32800 | tf_op jit(solution)/shard_map/ppermute | solution.py:353
  103.2 2.6 %collective-permute-start.35 = (bf16[32,512]{1,0:T(8,128)(2,1)S(1)}, bf16[32,512]{1,0:T(8,128)(2,1)S(1)}, u32[]{:S(2)}, u32[]{:S(2)}) collective-permute-start(bf16[32,512]{1,0:T(8,128)(2,1)S(1)} %fusion.5.refs_3_), channel_id=1, source_target_pairs={{0,24},{4,28},{8,16},{12,20},{16,8},{20,12},{24,0},{28,4},{1,25},{... | collective-permute-start | bytes 98312 | tf_op jit(solution)/shard_map/ppermute | solution.py:353
  105.8 1.9 %collective-permute-start.37 = (bf16[32,512]{1,0:T(8,128)(2,1)S(1)}, bf16[32,512]{1,0:T(8,128)(2,1)S(1)}, u32[]{:S(2)}, u32[]{:S(2)}) collective-permute-start(bf16[32,512]{1,0:T(8,128)(2,1)S(1)} %fusion.5.refs_3_), channel_id=1, source_target_pairs={{0,8},{4,12},{8,0},{12,4},{16,24},{20,28},{24,16},{28,20},{1,9},{5... | collective-permute-start | bytes 98312 | tf_op jit(solution)/shard_map/ppermute | solution.py:353
  107.7 0.8 collective-permute-start.34
  108.5 0.5 collective-permute-done.35.refs_0_
  109.0 1.6 %collective-permute-done.36.refs_1_ = bf16[32,512]{1,0:T(8,128)(2,1)S(1)} collective-permute-done((bf16[32,512]{1,0:T(8,128)(2,1)S(1)}, bf16[32,512]{1,0:T(8,128)(2,1)S(1)}, u32[]{:S(2)}, u32[]{:S(2)}) %collective-permute-start.36) | collective-permute-done | bytes 32800 | tf_op jit(solution)/shard_map/ppermute | solution.py:353
  110.6 0.9 collective-permute-start.38
  111.5 2.3 %shard_map.145.refs_10_ = f32[8,128,128]{2,1,0:T(8,128)S(1)} custom-call(s32[1,16]{1,0:T(1,128)S(1)} %copy-done.13, s32[1,16]{1,0:T(1,128)S(1)} %copy-done.14, s32[6,1,8]{2,1,0:T(1,128)S(1)} %bitcast.64, s32[6,1,8]{2,1,0:T(1,128)S(1)} %bitcast.69, bf16[16,128,128]{2,1,0:T(8,128)(2,1)S(1)} %bitcast.46, bf16[6,8,128,128]{3,2,1,0:T(8,128)(2,1)S(1)} %bitcast.41, ...), custom_call_target="tpu_custom_call" | custom-call | flops 671088640 | bytes 4456448 | tf_op jit(solution)/shard_map/pallas_call | solution.py:215
  113.9 3.3 %collective-permute-done.38.refs_4_ = bf16[4,32,512]{2,1,0:T(8,128)(2,1)S(1)} collective-permute-done((bf16[4,32,512]{2,1,0:T(8,128)(2,1)S(1)}, bf16[4,32,512]{2,1,0:T(8,128)(2,1)S(1)}, u32[]{:S(2)}, u32[]{:S(2)}) %collective-permute-start.38) | collective-permute-done | bytes 131104 | tf_op jit(solution)/shard_map/ppermute | solution.py:353
  117.2 0.9 shard_map.147
  118.0 2.8 %shard_map.146 = f32[8,128,128]{2,1,0:T(8,128)} custom-call(s32[1,16]{1,0:T(1,128)S(1)} %copy-done.13, s32[1,16]{1,0:T(1,128)S(1)} %copy-done.14, s32[6,1,8]{2,1,0:T(1,128)S(1)} %bitcast.65, s32[6,1,8]{2,1,0:T(1,128)S(1)} %bitcast.70, bf16[16,128,128]{2,1,0:T(8,128)(2,1)S(1)} %bitcast.47, bf16[6,8,128,128]{3,2,1,0:T(8,128)(2,1)S(1)} %bitcast.42, ...), custom_call_target="tpu_custom_call" | custom-call | flops 536870912 | bytes 4194304 | tf_op jit(solution)/shard_map/pallas_call | solution.py:215
  (75 shorter events, 1.0 us)
Async XLA Ops:
  4.8 9.5 %collective-permute-start.1 = (bf16[2,128,512]{2,1,0:T(8,128)(2,1)}, bf16[2,128,512]{2,1,0:T(8,128)(2,1)S(1)}, u32[]{:S(2)}, u32[]{:S(2)}) collective-permute-start(bf16[2,128,512]{2,1,0:T(8,128)(2,1)} %get-tuple-element.81.refs_0_), channel_id=1, source_target_pairs={{0,2},{1,3},{2,0},{3,1},{4,6},{5,7},{6,4},{7,5},{8,10},{9,11},{10,... | collective-permute-start | bytes 786440 | tf_op jit(solution)/shard_map/ppermute | solution.py:353
  7.8 9.4 %collective-permute-start = (bf16[8,128,128]{2,1,0:T(8,128)(2,1)}, bf16[8,128,128]{2,1,0:T(8,128)(2,1)S(1)}, u32[]{:S(2)}, u32[]{:S(2)}) collective-permute-start(bf16[8,128,128]{2,1,0:T(8,128)(2,1)} %get-tuple-element.62), channel_id=1, source_target_pairs={{0,4},{4,0},{8,12},{12,8},{16,20},{20,16},{24,28},{28,24},{1,5},{5... | collective-permute-start | bytes 786440 | tf_op jit(solution)/shard_map/ppermute | solution.py:353
  9.3 11.4 %copy-start.18 = (bf16[2,2,128,128]{3,2,1,0:T(8,128)(2,1)S(1)}, bf16[2,2,128,128]{3,2,1,0:T(8,128)(2,1)}, u32[]{:S(2)}) copy-start(bf16[2,2,128,128]{3,2,1,0:T(8,128)(2,1)} %get-tuple-element.68) | copy-start | bytes 393220
  9.3 11.4 %copy-start.17 = (bf16[2,2,128,128]{3,2,1,0:T(8,128)(2,1)S(1)}, bf16[2,2,128,128]{3,2,1,0:T(8,128)(2,1)}, u32[]{:S(2)}) copy-start(bf16[2,2,128,128]{3,2,1,0:T(8,128)(2,1)} %get-tuple-element.69) | copy-start | bytes 393220
  9.3 20.6 %collective-permute-start.8 = (bf16[2,8,128,128]{3,2,1,0:T(8,128)(2,1)}, bf16[2,8,128,128]{3,2,1,0:T(8,128)(2,1)S(1)}, u32[]{:S(2)}, u32[]{:S(2)}) collective-permute-start(bf16[2,8,128,128]{3,2,1,0:T(8,128)(2,1)} %get-tuple-element.74), channel_id=1, source_target_pairs={{0,4},{4,0},{8,12},{12,8},{16,20},{20,16},{24,28},{28,24},{1,5},{5... | collective-permute-start | bytes 1572872 | tf_op jit(solution)/shard_map/ppermute | solution.py:353
  17.3 8.9 %copy-start.5 = (bf16[2,128,512]{2,1,0:T(8,128)(2,1)S(1)}, bf16[2,128,512]{2,1,0:T(8,128)(2,1)}, u32[]{:S(2)}) copy-start(bf16[2,128,512]{2,1,0:T(8,128)(2,1)} %get-tuple-element.81.refs_0_) | copy-start | bytes 786436
  19.1 10.8 %collective-permute-start.9 = (bf16[8,128,128]{2,1,0:T(8,128)(2,1)}, bf16[8,128,128]{2,1,0:T(8,128)(2,1)S(1)}, u32[]{:S(2)}, u32[]{:S(2)}) collective-permute-start(bf16[8,128,128]{2,1,0:T(8,128)(2,1)} %add_convert_fusion), channel_id=1, source_target_pairs={{0,8},{4,12},{8,0},{12,4},{16,24},{20,28},{24,16},{28,20},{1,9},{5... | collective-permute-start | bytes 786440 | tf_op jit(solution)/shard_map/ppermute | solution.py:353
  20.7 5.5 %collective-permute-start.2 = (bf16[2,2,128,128]{3,2,1,0:T(8,128)(2,1)S(1)}, bf16[2,2,128,128]{3,2,1,0:T(8,128)(2,1)S(1)}, u32[]{:S(2)}, u32[]{:S(2)}) collective-permute-start(bf16[2,2,128,128]{3,2,1,0:T(8,128)(2,1)S(1)} %copy-done.18), channel_id=1, source_target_pairs={{0,1},{1,0},{2,3},{3,2},{4,5},{5,4},{6,7},{7,6},{8,9},{9,8},{10,11... | collective-permute-start | bytes 393224 | tf_op jit(solution)/shard_map/ppermute | solution.py:353
  20.7 6.4 %collective-permute-start.3 = (bf16[2,2,128,128]{3,2,1,0:T(8,128)(2,1)S(1)}, bf16[2,2,128,128]{3,2,1,0:T(8,128)(2,1)S(1)}, u32[]{:S(2)}, u32[]{:S(2)}) collective-permute-start(bf16[2,2,128,128]{3,2,1,0:T(8,128)(2,1)S(1)} %copy-done.17), channel_id=1, source_target_pairs={{0,2},{1,3},{2,0},{3,1},{4,6},{5,7},{6,4},{7,5},{8,10},{9,11},{10,... | collective-permute-start | bytes 393224 | tf_op jit(solution)/shard_map/ppermute | solution.py:353
  21.3 7.9 %collective-permute-start.4 = (bf16[2,2,128,128]{3,2,1,0:T(8,128)(2,1)}, bf16[2,2,128,128]{3,2,1,0:T(8,128)(2,1)S(1)}, u32[]{:S(2)}, u32[]{:S(2)}) collective-permute-start(bf16[2,2,128,128]{3,2,1,0:T(8,128)(2,1)} %get-tuple-element.70), channel_id=1, source_target_pairs={{0,3},{1,2},{2,1},{3,0},{4,7},{5,6},{6,5},{7,4},{8,11},{9,10},{10,... | collective-permute-start | bytes 393224 | tf_op jit(solution)/shard_map/ppermute | solution.py:353
  26.1 5.6 %copy-start.15 = (f32[8,128,128]{2,1,0:T(8,128)S(1)}, f32[8,128,128]{2,1,0:T(8,128)}, u32[]{:S(2)}) copy-start(f32[8,128,128]{2,1,0:T(8,128)} %get-tuple-element.76) | copy-start | bytes 1572868
  26.1 8.8 %copy-start.16 = (s32[1024]{0:T(1024)S(1)}, s32[1024]{0:T(1024)}, u32[]{:S(2)}) copy-start(s32[1024]{0:T(1024)} %param.14) | copy-start | bytes 12292
  26.1 20.1 %copy-start.3 = (f32[8,128,128]{2,1,0:T(8,128)S(1)}, f32[8,128,128]{2,1,0:T(8,128)}, u32[]{:S(2)}) copy-start(f32[8,128,128]{2,1,0:T(8,128)} %get-tuple-element.66.keep_ref) | copy-start | bytes 1572868
  26.1 9.0 %collective-permute-start.5 = (bf16[2,128,512]{2,1,0:T(8,128)(2,1)S(1)}, bf16[2,128,512]{2,1,0:T(8,128)(2,1)S(1)}, u32[]{:S(2)}, u32[]{:S(2)}) collective-permute-start(bf16[2,128,512]{2,1,0:T(8,128)(2,1)S(1)} %copy-done.5), channel_id=1, source_target_pairs={{0,1},{1,0},{2,3},{3,2},{4,5},{5,4},{6,7},{7,6},{8,9},{9,8},{10,11... | collective-permute-start | bytes 786440 | tf_op jit(solution)/shard_map/ppermute | solution.py:353
  27.1 0.7 copy-start.7
  27.7 8.1 %collective-permute-start.7 = (bf16[8,128,128]{2,1,0:T(8,128)(2,1)}, bf16[8,128,128]{2,1,0:T(8,128)(2,1)S(1)}, u32[]{:S(2)}, u32[]{:S(2)}) collective-permute-start(bf16[8,128,128]{2,1,0:T(8,128)(2,1)} %get-tuple-element.71), channel_id=1, source_target_pairs={{0,4},{4,0},{8,12},{12,8},{16,20},{20,16},{24,28},{28,24},{1,5},{5... | collective-permute-start | bytes 786440 | tf_op jit(solution)/shard_map/ppermute | solution.py:353
  29.2 0.7 copy-start.9
  29.9 5.9 %collective-permute-start.6 = (bf16[2,128,512]{2,1,0:T(8,128)(2,1)S(1)}, bf16[2,128,512]{2,1,0:T(8,128)(2,1)S(1)}, u32[]{:S(2)}, u32[]{:S(2)}) collective-permute-start(bf16[2,128,512]{2,1,0:T(8,128)(2,1)S(1)} %collective-permute-done.1.refs_2_), channel_id=1, source_target_pairs={{0,1},{1,0},{2,3},{3,2},{4,5},{5,4},{6,7},{7,6},{8,9},{9,8},{10,11... | collective-permute-start | bytes 786440 | tf_op jit(solution)/shard_map/ppermute | solution.py:353
  31.7 21.0 %copy-start.6 = (bf16[2,2,128,128]{3,2,1,0:T(8,128)(2,1)S(1)}, bf16[2,2,128,128]{3,2,1,0:T(8,128)(2,1)}, u32[]{:S(2)}) copy-start(bf16[2,2,128,128]{3,2,1,0:T(8,128)(2,1)} %get-tuple-element.85.refs_4_) | copy-start | bytes 393220
  31.8 14.4 %collective-permute-start.10 = (bf16[8,128,128]{2,1,0:T(8,128)(2,1)S(1)}, bf16[8,128,128]{2,1,0:T(8,128)(2,1)S(1)}, u32[]{:S(2)}, u32[]{:S(2)}) collective-permute-start(bf16[8,128,128]{2,1,0:T(8,128)(2,1)S(1)} %fusion), channel_id=1, source_target_pairs={{0,8},{4,12},{8,0},{12,4},{16,24},{20,28},{24,16},{28,20},{1,9},{5... | collective-permute-start | bytes 786440 | tf_op jit(solution)/shard_map/ppermute | solution.py:353
  32.3 13.9 %collective-permute-start.11 = (bf16[8,128,128]{2,1,0:T(8,128)(2,1)}, bf16[8,128,128]{2,1,0:T(8,128)(2,1)S(1)}, u32[]{:S(2)}, u32[]{:S(2)}) collective-permute-start(bf16[8,128,128]{2,1,0:T(8,128)(2,1)} %fusion.2), channel_id=1, source_target_pairs={{0,16},{4,20},{8,24},{12,28},{16,0},{20,4},{24,8},{28,12},{1,17},{... | collective-permute-start | bytes 786440 | tf_op jit(solution)/shard_map/ppermute | solution.py:353
  47.1 34.8 %copy-start.2 = (bf16[1024,128]{1,0:T(8,128)(2,1)S(1)}, bf16[1024,128]{1,0:T(8,128)(2,1)}, u32[]{:S(2)}) copy-start(bf16[1024,128]{1,0:T(8,128)(2,1)} %f_ref.1) | copy-start | bytes 786436
  47.1 34.8 %copy-start.4 = (bf16[128,512]{1,0:T(8,128)(2,1)S(1)}, bf16[128,512]{1,0:T(8,128)(2,1)}, u32[]{:S(2)}) copy-start(bf16[128,512]{1,0:T(8,128)(2,1)} %w_ref.1) | copy-start | bytes 393220
  47.1 2.1 %collective-permute-start.12 = (bf16[2,128,128]{2,1,0:T(8,128)(2,1)}, bf16[2,128,128]{2,1,0:T(8,128)(2,1)S(1)}, u32[]{:S(2)}, u32[]{:S(2)}) collective-permute-start(bf16[2,128,128]{2,1,0:T(8,128)(2,1)} %get-tuple-element.90), channel_id=1, source_target_pairs={{0,1},{1,0},{2,3},{3,2},{4,5},{5,4},{6,7},{7,6},{8,9},{9,8},{10,11... | collective-permute-start | bytes 196616 | tf_op jit(solution)/shard_map/ppermute | solution.py:353
  47.1 5.2 %collective-permute-start.13 = (bf16[2,128,128]{2,1,0:T(8,128)(2,1)}, bf16[2,128,128]{2,1,0:T(8,128)(2,1)S(1)}, u32[]{:S(2)}, u32[]{:S(2)}) collective-permute-start(bf16[2,128,128]{2,1,0:T(8,128)(2,1)} %get-tuple-element.91), channel_id=1, source_target_pairs={{0,2},{1,3},{2,0},{3,1},{4,6},{5,7},{6,4},{7,5},{8,10},{9,11},{10,... | collective-permute-start | bytes 196616 | tf_op jit(solution)/shard_map/ppermute | solution.py:353
  47.7 5.1 %collective-permute-start.14 = (bf16[2,128,128]{2,1,0:T(8,128)(2,1)S(1)}, bf16[2,128,128]{2,1,0:T(8,128)(2,1)S(1)}, u32[]{:S(2)}, u32[]{:S(2)}) collective-permute-start(bf16[2,128,128]{2,1,0:T(8,128)(2,1)S(1)} %get-tuple-element.92), channel_id=1, source_target_pairs={{0,3},{1,2},{2,1},{3,0},{4,7},{5,6},{6,5},{7,4},{8,11},{9,10},{10,... | collective-permute-start | bytes 196616 | tf_op jit(solution)/shard_map/ppermute | solution.py:353
  52.8 0.9 copy-start.8
  53.7 0.9 copy-start.10
  55.8 14.6 %collective-permute-start.16 = (bf16[256,512]{1,0:T(8,128)(2,1)S(1)}, bf16[256,512]{1,0:T(8,128)(2,1)S(1)}, u32[]{:S(2)}, u32[]{:S(2)}) collective-permute-start(bf16[256,512]{1,0:T(8,128)(2,1)S(1)} %get-tuple-element.98.refs_0_), channel_id=1, source_target_pairs={{0,2},{1,3},{2,0},{3,1},{4,6},{5,7},{6,4},{7,5},{8,10},{9,11},{10,... | collective-permute-start | bytes 786440 | tf_op jit(solution)/shard_map/ppermute | solution.py:353
  56.7 2.1 %collective-permute-start.18 = (bf16[256,128]{1,0:T(8,128)(2,1)S(1)}, bf16[256,128]{1,0:T(8,128)(2,1)S(1)}, u32[]{:S(2)}, u32[]{:S(2)}) collective-permute-start(bf16[256,128]{1,0:T(8,128)(2,1)S(1)} %get-tuple-element.95), channel_id=1, source_target_pairs={{0,1},{1,0},{2,3},{3,2},{4,5},{5,4},{6,7},{7,6},{8,9},{9,8},{10,11... | collective-permute-start | bytes 196616 | tf_op jit(solution)/shard_map/ppermute | solution.py:353
  56.7 9.8 %collective-permute-start.19 = (bf16[256,128]{1,0:T(8,128)(2,1)S(1)}, bf16[256,128]{1,0:T(8,128)(2,1)S(1)}, u32[]{:S(2)}, u32[]{:S(2)}) collective-permute-start(bf16[256,128]{1,0:T(8,128)(2,1)S(1)} %get-tuple-element.96), channel_id=1, source_target_pairs={{0,2},{1,3},{2,0},{3,1},{4,6},{5,7},{6,4},{7,5},{8,10},{9,11},{10,... | collective-permute-start | bytes 196616 | tf_op jit(solution)/shard_map/ppermute | solution.py:353
  57.9 8.6 %collective-permute-start.20 = (bf16[256,128]{1,0:T(8,128)(2,1)S(1)}, bf16[256,128]{1,0:T(8,128)(2,1)S(1)}, u32[]{:S(2)}, u32[]{:S(2)}) collective-permute-start(bf16[256,128]{1,0:T(8,128)(2,1)S(1)} %get-tuple-element.97), channel_id=1, source_target_pairs={{0,3},{1,2},{2,1},{3,0},{4,7},{5,6},{6,5},{7,4},{8,11},{9,10},{10,... | collective-permute-start | bytes 196616 | tf_op jit(solution)/shard_map/ppermute | solution.py:353
  58.5 14.8 %collective-permute-start.15 = (bf16[256,512]{1,0:T(8,128)(2,1)S(1)}, bf16[256,512]{1,0:T(8,128)(2,1)S(1)}, u32[]{:S(2)}, u32[]{:S(2)}) collective-permute-start(bf16[256,512]{1,0:T(8,128)(2,1)S(1)} %get-tuple-element.98.refs_0_), channel_id=1, source_target_pairs={{0,1},{1,0},{2,3},{3,2},{4,5},{5,4},{6,7},{7,6},{8,9},{9,8},{10,11... | collective-permute-start | bytes 786440 | tf_op jit(solution)/shard_map/ppermute | solution.py:353
  66.6 8.7 %collective-permute-start.21 = (bf16[8,128,128]{2,1,0:T(8,128)(2,1)S(1)}, bf16[8,128,128]{2,1,0:T(8,128)(2,1)S(1)}, u32[]{:S(2)}, u32[]{:S(2)}) collective-permute-start(bf16[8,128,128]{2,1,0:T(8,128)(2,1)S(1)} %bitcast.51), channel_id=1, source_target_pairs={{0,4},{4,0},{8,12},{12,8},{16,20},{20,16},{24,28},{28,24},{1,5},{5... | collective-permute-start | bytes 786440 | tf_op jit(solution)/shard_map/ppermute | solution.py:353
  67.9 14.0 %collective-permute-start.22 = (bf16[8,128,128]{2,1,0:T(8,128)(2,1)S(1)}, bf16[8,128,128]{2,1,0:T(8,128)(2,1)S(1)}, u32[]{:S(2)}, u32[]{:S(2)}) collective-permute-start(bf16[8,128,128]{2,1,0:T(8,128)(2,1)S(1)} %bitcast.52), channel_id=1, source_target_pairs={{0,8},{4,12},{8,0},{12,4},{16,24},{20,28},{24,16},{28,20},{1,9},{5... | collective-permute-start | bytes 786440 | tf_op jit(solution)/shard_map/ppermute | solution.py:353
  70.5 11.4 %collective-permute-start.17 = (bf16[256,512]{1,0:T(8,128)(2,1)S(1)}, bf16[256,512]{1,0:T(8,128)(2,1)S(1)}, u32[]{:S(2)}, u32[]{:S(2)}) collective-permute-start(bf16[256,512]{1,0:T(8,128)(2,1)S(1)} %collective-permute-done.16.refs_2_), channel_id=1, source_target_pairs={{0,1},{1,0},{2,3},{3,2},{4,5},{5,4},{6,7},{7,6},{8,9},{9,8},{10,11... | collective-permute-start | bytes 786440 | tf_op jit(solution)/shard_map/ppermute | solution.py:353
  70.5 15.5 %collective-permute-start.25 = (bf16[8,128,128]{2,1,0:T(8,128)(2,1)S(1)}, bf16[8,128,128]{2,1,0:T(8,128)(2,1)S(1)}, u32[]{:S(2)}, u32[]{:S(2)}) collective-permute-start(bf16[8,128,128]{2,1,0:T(8,128)(2,1)S(1)} %bitcast.53), channel_id=1, source_target_pairs={{0,16},{4,20},{8,24},{12,28},{16,0},{20,4},{24,8},{28,12},{1,17},{... | collective-permute-start | bytes 786440 | tf_op jit(solution)/shard_map/ppermute | solution.py:353
  81.9 29.6 %copy-start = (bf16[1,6,8,128,128]{4,3,2,1,0:T(8,128)(2,1)S(1)}, bf16[1,6,8,128,128]{4,3,2,1,0:T(8,128)(2,1)}, u32[]{:S(2)}) copy-start(bf16[1,6,8,128,128]{4,3,2,1,0:T(8,128)(2,1)} %param.18) | copy-start | bytes 4718596
  81.9 29.6 %copy-start.1 = (bf16[1,16,128,128]{3,2,1,0:T(8,128)(2,1)S(1)}, bf16[1,16,128,128]{3,2,1,0:T(8,128)(2,1)}, u32[]{:S(2)}) copy-start(bf16[1,16,128,128]{3,2,1,0:T(8,128)(2,1)} %param.15) | copy-start | bytes 1572868
  81.9 29.6 %copy-start.11 = (s32[1,6,8]{2,0,1:T(1,128)S(1)}, s32[1,6,8]{2,0,1:T(1,128)}, u32[]{:S(2)}) copy-start(s32[1,6,8]{2,0,1:T(1,128)} %param.19) | copy-start | bytes 580
  82.0 29.6 %copy-start.12 = (s32[1,6,8]{2,0,1:T(1,128)S(1)}, s32[1,6,8]{2,0,1:T(1,128)}, u32[]{:S(2)}) copy-start(s32[1,6,8]{2,0,1:T(1,128)} %param.20) | copy-start | bytes 580
  82.0 29.6 %copy-start.13 = (s32[1,16]{1,0:T(1,128)S(1)}, s32[1,16]{1,0:T(1,128)}, u32[]{:S(2)}) copy-start(s32[1,16]{1,0:T(1,128)} %refs_0_.9) | copy-start | bytes 196
  82.0 29.6 %copy-start.14 = (s32[1,16]{1,0:T(1,128)S(1)}, s32[1,16]{1,0:T(1,128)}, u32[]{:S(2)}) copy-start(s32[1,16]{1,0:T(1,128)} %refs_1_.9) | copy-start | bytes 196
  82.8 6.5 %collective-permute-start.23 = (bf16[4,32,512]{2,1,0:T(8,128)(2,1)S(1)}, bf16[4,32,512]{2,1,0:T(8,128)(2,1)S(1)}, u32[]{:S(2)}, u32[]{:S(2)}) collective-permute-start(bf16[4,32,512]{2,1,0:T(8,128)(2,1)S(1)} %get-tuple-element.103), channel_id=1, source_target_pairs={{0,4},{4,0},{8,12},{12,8},{16,20},{20,16},{24,28},{28,24},{1,5},{5... | collective-permute-start | bytes 393224 | tf_op jit(solution)/shard_map/ppermute | solution.py:353
  83.6 11.2 %collective-permute-start.24 = (bf16[8,128,128]{2,1,0:T(8,128)(2,1)S(1)}, bf16[8,128,128]{2,1,0:T(8,128)(2,1)S(1)}, u32[]{:S(2)}, u32[]{:S(2)}) collective-permute-start(bf16[8,128,128]{2,1,0:T(8,128)(2,1)S(1)} %collective-permute-done.22.refs_8_), channel_id=1, source_target_pairs={{0,4},{4,0},{8,12},{12,8},{16,20},{20,16},{24,28},{28,24},{1,5},{5... | collective-permute-start | bytes 786440 | tf_op jit(solution)/shard_map/ppermute | solution.py:353
  86.0 17.2 %collective-permute-start.32 = (bf16[8,128,128]{2,1,0:T(8,128)(2,1)S(1)}, bf16[8,128,128]{2,1,0:T(8,128)(2,1)S(1)}, u32[]{:S(2)}, u32[]{:S(2)}) collective-permute-start(bf16[8,128,128]{2,1,0:T(8,128)(2,1)S(1)} %collective-permute-done.25.refs_6_), channel_id=1, source_target_pairs={{0,4},{4,0},{8,12},{12,8},{16,20},{20,16},{24,28},{28,24},{1,5},{5... | collective-permute-start | bytes 786440 | tf_op jit(solution)/shard_map/ppermute | solution.py:353
  86.8 16.4 %collective-permute-start.33 = (bf16[8,128,128]{2,1,0:T(8,128)(2,1)S(1)}, bf16[8,128,128]{2,1,0:T(8,128)(2,1)S(1)}, u32[]{:S(2)}, u32[]{:S(2)}) collective-permute-start(bf16[8,128,128]{2,1,0:T(8,128)(2,1)S(1)} %collective-permute-done.25.refs_6_), channel_id=1, source_target_pairs={{0,8},{4,12},{8,0},{12,4},{16,24},{20,28},{24,16},{28,20},{1,9},{5... | collective-permute-start | bytes 786440 | tf_op jit(solution)/shard_map/ppermute | solution.py:353
  86.8 8.1 %collective-permute-start.29 = (bf16[256,128]{1,0:T(8,128)(2,1)S(1)}, bf16[256,128]{1,0:T(8,128)(2,1)S(1)}, u32[]{:S(2)}, u32[]{:S(2)}) collective-permute-start(bf16[256,128]{1,0:T(8,128)(2,1)S(1)} %get-tuple-element.110), channel_id=1, source_target_pairs={{0,1},{1,0},{2,3},{3,2},{4,5},{5,4},{6,7},{7,6},{8,9},{9,8},{10,11... | collective-permute-start | bytes 196616 | tf_op jit(solution)/shard_map/ppermute | solution.py:353
  89.2 9.0 %collective-permute-start.30 = (bf16[256,128]{1,0:T(8,128)(2,1)S(1)}, bf16[256,128]{1,0:T(8,128)(2,1)S(1)}, u32[]{:S(2)}, u32[]{:S(2)}) collective-permute-start(bf16[256,128]{1,0:T(8,128)(2,1)S(1)} %get-tuple-element.111), channel_id=1, source_target_pairs={{0,2},{1,3},{2,0},{3,1},{4,6},{5,7},{6,4},{7,5},{8,10},{9,11},{10,... | collective-permute-start | bytes 196616 | tf_op jit(solution)/shard_map/ppermute | solution.py:353
  94.8 3.7 %collective-permute-start.31 = (bf16[256,128]{1,0:T(8,128)(2,1)S(1)}, bf16[256,128]{1,0:T(8,128)(2,1)S(1)}, u32[]{:S(2)}, u32[]{:S(2)}) collective-permute-start(bf16[256,128]{1,0:T(8,128)(2,1)S(1)} %get-tuple-element.112), channel_id=1, source_target_pairs={{0,3},{1,2},{2,1},{3,0},{4,7},{5,6},{6,5},{7,4},{8,11},{9,10},{10,... | collective-permute-start | bytes 196616 | tf_op jit(solution)/shard_map/ppermute | solution.py:353
  94.9 6.1 %collective-permute-start.26 = (bf16[32,512]{1,0:T(8,128)(2,1)S(1)}, bf16[32,512]{1,0:T(8,128)(2,1)S(1)}, u32[]{:S(2)}, u32[]{:S(2)}) collective-permute-start(bf16[32,512]{1,0:T(8,128)(2,1)S(1)} %get-tuple-element.118), channel_id=1, source_target_pairs={{0,24},{4,28},{8,16},{12,20},{16,8},{20,12},{24,0},{28,4},{1,25},{... | collective-permute-start | bytes 98312 | tf_op jit(solution)/shard_map/ppermute | solution.py:353
  98.2 4.9 %collective-permute-start.27 = (bf16[32,512]{1,0:T(8,128)(2,1)S(1)}, bf16[32,512]{1,0:T(8,128)(2,1)S(1)}, u32[]{:S(2)}, u32[]{:S(2)}) collective-permute-start(bf16[32,512]{1,0:T(8,128)(2,1)S(1)} %get-tuple-element.120), channel_id=1, source_target_pairs={{0,16},{4,20},{8,24},{12,28},{16,0},{20,4},{24,8},{28,12},{1,17},{... | collective-permute-start | bytes 98312 | tf_op jit(solution)/shard_map/ppermute | solution.py:353
  98.5 4.6 %collective-permute-start.28 = (bf16[32,512]{1,0:T(8,128)(2,1)S(1)}, bf16[32,512]{1,0:T(8,128)(2,1)S(1)}, u32[]{:S(2)}, u32[]{:S(2)}) collective-permute-start(bf16[32,512]{1,0:T(8,128)(2,1)S(1)} %get-tuple-element.119), channel_id=1, source_target_pairs={{0,8},{4,12},{8,0},{12,4},{16,24},{20,28},{24,16},{28,20},{1,9},{5... | collective-permute-start | bytes 98312 | tf_op jit(solution)/shard_map/ppermute | solution.py:353
  103.2 5.8 %collective-permute-start.35 = (bf16[32,512]{1,0:T(8,128)(2,1)S(1)}, bf16[32,512]{1,0:T(8,128)(2,1)S(1)}, u32[]{:S(2)}, u32[]{:S(2)}) collective-permute-start(bf16[32,512]{1,0:T(8,128)(2,1)S(1)} %fusion.5.refs_3_), channel_id=1, source_target_pairs={{0,24},{4,28},{8,16},{12,20},{16,8},{20,12},{24,0},{28,4},{1,25},{... | collective-permute-start | bytes 98312 | tf_op jit(solution)/shard_map/ppermute | solution.py:353
  105.8 4.8 %collective-permute-start.36 = (bf16[32,512]{1,0:T(8,128)(2,1)S(1)}, bf16[32,512]{1,0:T(8,128)(2,1)S(1)}, u32[]{:S(2)}, u32[]{:S(2)}) collective-permute-start(bf16[32,512]{1,0:T(8,128)(2,1)S(1)} %fusion.5.refs_3_), channel_id=1, source_target_pairs={{0,16},{4,20},{8,24},{12,28},{16,0},{20,4},{24,8},{28,12},{1,17},{... | collective-permute-start | bytes 98312 | tf_op jit(solution)/shard_map/ppermute | solution.py:353
  105.8 4.8 %collective-permute-start.37 = (bf16[32,512]{1,0:T(8,128)(2,1)S(1)}, bf16[32,512]{1,0:T(8,128)(2,1)S(1)}, u32[]{:S(2)}, u32[]{:S(2)}) collective-permute-start(bf16[32,512]{1,0:T(8,128)(2,1)S(1)} %fusion.5.refs_3_), channel_id=1, source_target_pairs={{0,8},{4,12},{8,0},{12,4},{16,24},{20,28},{24,16},{28,20},{1,9},{5... | collective-permute-start | bytes 98312 | tf_op jit(solution)/shard_map/ppermute | solution.py:353
  107.7 10.4 %collective-permute-start.34 = (bf16[8,128,128]{2,1,0:T(8,128)(2,1)S(1)}, bf16[8,128,128]{2,1,0:T(8,128)(2,1)S(1)}, u32[]{:S(2)}, u32[]{:S(2)}) collective-permute-start(bf16[8,128,128]{2,1,0:T(8,128)(2,1)S(1)} %collective-permute-done.33.refs_8_), channel_id=1, source_target_pairs={{0,4},{4,0},{8,12},{12,8},{16,20},{20,16},{24,28},{28,24},{1,5},{5... | collective-permute-start | bytes 786440 | tf_op jit(solution)/shard_map/ppermute | solution.py:353
  110.6 6.5 %collective-permute-start.38 = (bf16[4,32,512]{2,1,0:T(8,128)(2,1)S(1)}, bf16[4,32,512]{2,1,0:T(8,128)(2,1)S(1)}, u32[]{:S(2)}, u32[]{:S(2)}) collective-permute-start(bf16[4,32,512]{2,1,0:T(8,128)(2,1)S(1)} %pad_maximum_fusion.1), channel_id=1, source_target_pairs={{0,4},{4,0},{8,12},{12,8},{16,20},{20,16},{24,28},{28,24},{1,5},{5... | collective-permute-start | bytes 393224 | tf_op jit(solution)/shard_map/ppermute | solution.py:353

commit v5 on v4

--- a/solution.py
+++ b/solution.py
@@ -266,8 +266,8 @@
 def dense_kernel(feats, inv_ref, *refs):
     mine = lax.axis_index("feat")
     w_refs, early_refs, a_refs = refs[:feats], refs[feats : 2 * feats], refs[2 * feats : 3 * feats]
-    dpre_ref = refs[3 * feats]
-    dsum_refs, out_refs = refs[3 * feats + 1 : 4 * feats + 1], refs[4 * feats + 1 : 5 * feats + 1]
+    core_ref, chip_ref, own_ref = refs[3 * feats : 3 * feats + 3]
+    dsum_refs = refs[3 * feats + 3 : 4 * feats + 3]
     held = refs[-1]
     full = w_refs[0].shape[2]
     some, width = held.shape[1:]
@@ -285,28 +285,32 @@
     out = (pre * sigma).astype(BF16)
     cot = joined([held[j] for j in range(feats)]).astype(F32)
     dpre = (cot * sigma * (1.0 + pre * (1.0 - sigma))).astype(BF16)
-    dpre_ref[...] = dpre
     for mask in range(feats):
         dagg = lax.dot_general(
             dpre, w_refs[mask][1], (((1,), (1,)), ((), ())), preferred_element_type=F32
         )
         dsum_refs[mask][...] = (dagg * inv_ref[...]).astype(BF16)
     for j in range(feats):
-        held[j] = out[:, j * width : (j + 1) * width]
-    for mask in range(feats):
-        out_refs[mask][...] = held[mine ^ mask]
-
-
-def grad_kernel(near, far, feats, f_ref, a_ref, w_ref, *refs):
+        cols = slice(j * width, (j + 1) * width)
+        core_ref[j] = dpre[:, cols]
+        chip_ref[j] = dpre[:, cols]
+        held[j] = out[:, cols]
+    own_ref[...] = held[mine]
+    core_ref[feats] = held[mine ^ 1]
+    chip_ref[feats] = held[mine ^ 2]
+    chip_ref[feats + 1] = held[mine ^ 3]
+
+
+def grad_kernel(feats, f_ref, a_ref, w_ref, *refs):
     me = lax.axis_index("dom")
     mine = lax.axis_index("feat")
     dpre_refs, (dx_ref, give_ref, keep_ref, held) = refs[:feats], refs[feats:]
     width = f_ref.shape[1]
     piece = held.shape[1]
-    some = dpre_refs[0].shape[0]
+    some = dpre_refs[0].shape[1]
     parts = [0.0, 0.0]
     for mask, dpre_ref in enumerate(dpre_refs):
-        dpre = dpre_ref[...]
+        dpre = joined([dpre_ref[j] for j in range(feats)])
         rows = pl.ds(pl.multiple_of((mine ^ mask) * some, some), some)
         for at, ref in enumerate((f_ref, a_ref)):
             parts[at] = parts[at] + lax.dot_general(
@@ -318,19 +322,17 @@
     for at, part in enumerate(parts):
         for j in range(width // piece):
             held[at * (width // piece) + j] = part[j * piece : (j + 1) * piece]
-    for at, mask in enumerate(far + [0]):
-        give_ref[at] = held[me ^ mask ^ near].astype(BF16)
-        keep_ref[at] = held[me ^ mask]
-
-
-def finish_kernel(near, far, *refs):
-    me = lax.axis_index("dom")
-    count = len(far) + 1
-    found, other_ref = refs[:count], refs[count]
-    self_ref, neigh_ref, held = refs[count + 1 :]
-    for at, mask in enumerate(far + [0]):
-        held[me ^ mask] = found[at][...].astype(F32)
-        held[me ^ mask ^ near] = other_ref[at].astype(F32)
+    side = me % 2
+    for at in range(give_ref.shape[0]):
+        give_ref[at] = held[2 * at + 1 - side].astype(BF16)
+        keep_ref[at] = held[2 * at + side]
+
+
+def finish_kernel(mine_ref, other_ref, self_ref, neigh_ref, held):
+    side = lax.axis_index("dom") % 2
+    for at in range(mine_ref.shape[0]):
+        held[2 * at + side] = mine_ref[at].astype(F32)
+        held[2 * at + 1 - side] = other_ref[at].astype(F32)
     some = held.shape[1]
     half = held.shape[0] // 2
     for j in range(half):
@@ -340,9 +342,12 @@
 
 def place_kernel(*refs):
     mine = lax.axis_index("feat")
-    out_ref = refs[-1]
-    for mask, ref in enumerate(refs[:-1]):
-        out_ref[mine ^ mask] = ref[...]
+    own_ref, core_ref, chip_ref, both_ref, out_ref = refs
+    feats = out_ref.shape[0]
+    out_ref[mine] = own_ref[...]
+    out_ref[mine ^ 1] = core_ref[feats]
+    out_ref[mine ^ 2] = chip_ref[feats]
+    out_ref[mine ^ 3] = both_ref[feats + 1]
 
 
 def swap_feat(x):
@@ -407,24 +412,24 @@
     def tied(x, *others):
         return lax.optimization_barrier((x, others))[0]
 
-    send_7, sends, send_1, *made = forward(
-        [7, [5, 3], 1],
+    made = forward(
+        [7, 5, 3, 1],
         [blocks, cotangent.reshape(shape), w_self, w_neigh],
-        [like(shape, BF16), like((2, *shape), BF16), like(shape, BF16)]
+        [like(shape, BF16)] * 4
         + [like((2, per_feat, block, width), BF16)] * feats
         + [like((2, width, full), BF16)],
     )
-    early_pieces, pair = made[:-1], made[-1]
+    sends, early_pieces, pair = made[:4], made[4:-1], made[-1]
     keep_6, keep_4 = forward([6, 4], [blocks], [like(shape, F32)] * 2)
     weights = relayed(pair)
     early = [early_pieces[0]] + [crossed(early_pieces[m], m, "feat") for m in range(1, feats)]
-    near_6, near_53, near_0 = (crossed(send, near) for send in (send_7, sends, send_1))
-    sum_6 = (keep_6 + tied(near_6, weights[2]).astype(F32)).astype(BF16)
-    keep_2, keep = forward([2, 0], [tied(blocks, sum_6)], [like(shape, F32)] * 2)
-    near_53 = tied(near_53, early)
-    sum_4 = (keep_4 + near_53[0].astype(F32) + crossed(sum_6, 2).astype(F32)).astype(BF16)
+    near_6, near_4, near_2, near_0 = (crossed(send, near) for send in sends)
+    sum_6 = (keep_6 + near_6.astype(F32)).astype(BF16)
+    near_4 = tied(near_4, weights[2])
+    sum_4 = (keep_4 + near_4.astype(F32) + crossed(sum_6, 2).astype(F32)).astype(BF16)
     far_0 = crossed(sum_4, 4)
-    sum_2 = (tied(keep_2, sum_4) + near_53[1].astype(F32)).astype(BF16)
+    keep_2, keep = forward([2, 0], [tied(blocks, sum_4)], [like(shape, F32)] * 2)
+    sum_2 = tied((keep_2 + near_2.astype(F32)).astype(BF16), far_0)
     mid_0 = crossed(sum_2, 2)
     arrived = [near_0, mid_0, far_0]
     early, weights, arrived = lax.optimization_barrier((early, weights, arrived))
@@ -434,14 +439,14 @@
         [inverse.reshape(nblocks, block, 1), keep, *arrived],
     )
     agg_rows = [agg_pieces[0]] + [crossed(agg_pieces[m], m, "feat") for m in range(1, feats)]
-    dpre_rows, *pieces = small_call(
+    for_core, for_chip, own_out, *dsum_pieces = small_call(
         functools.partial(dense_kernel, feats),
-        [like((some, full), BF16)] + [like((some, width), BF16)] * (2 * feats),
+        [like((feats + 1, some, width), BF16), like((feats + 2, some, width), BF16)]
+        + [like((some, width), BF16)] * (1 + feats),
         [inv_rows, *weights, *early, *agg_rows],
         [pltpu.VMEM((feats, some, width), BF16)],
         6 * some * full * full,
     )
-    dsum_pieces, out_pieces = pieces[:feats], pieces[feats:]
     dsum = jnp.concatenate(
         [dsum_pieces[0]] + [crossed(dsum_pieces[m], m, "feat") for m in range(1, feats)], axis=0
     ).reshape(shape)
@@ -449,11 +454,19 @@
     for bit in bits[::-1]:
         for mask in sorted(found):
             found[mask ^ bit] = crossed(found[mask], bit)
-    dpre = relayed(dpre_rows)
-    dpre = tied(dpre, found[1], found[2])
+    for_core, for_chip = tied((for_core, for_chip), dsum)
+    from_chip = crossed(for_chip, 2, "feat")
+    from_core = crossed(for_core, 1, "feat")
+    from_both = crossed(tied(from_chip, found[1], found[2], found[4]), 1, "feat")
+    (out,) = small_call(
+        place_kernel,
+        [like((feats, some, width), BF16)],
+        [own_out, from_core, from_chip, from_both],
+    )
+    dpre = [for_core, from_core, from_chip, from_both]
     piece = 2 * width // parts_total
     dx_self, give, keep = small_call(
-        functools.partial(grad_kernel, near, far, feats),
+        functools.partial(grad_kernel, feats),
         [
             like((rows, width), F32),
             like((len(far) + 1, piece, full), BF16),
@@ -463,20 +476,16 @@
         [pltpu.VMEM((parts_total, piece, full), F32)],
         6 * rows * width * full,
     )
-    out_pieces = tied(out_pieces, give)
-    out_all = [out_pieces[0]] + [crossed(out_pieces[m], m, "feat") for m in range(1, feats)]
-    (out,) = small_call(place_kernel, [like((feats, some, width), BF16)], out_all)
-    keep = keep + crossed(give, near).astype(F32)
-    keep = tied(keep, found[3], found[4])
-    total = keep[len(far)]
-    for at, mask in enumerate(far):
-        total = total + crossed(keep[at].astype(BF16), mask).astype(F32)
-    total, out = tied((total.astype(BF16), out), found[5], found[6])
-    totals = [crossed(total, mask) for mask in far] + [total]
+    total = (keep + crossed(give, near).astype(F32)).astype(BF16)
+    total = tied(total, found[3], found[6])
+    total = (total.astype(F32) + crossed(total, 2).astype(F32)).astype(BF16)
+    total = tied(total, found[5])
+    total = (total.astype(F32) + crossed(total, 4).astype(F32)).astype(BF16)
+    total, out = tied((total, out), found[5])
     grad_self, grad_neigh = small_call(
-        functools.partial(finish_kernel, near, far),
+        finish_kernel,
         [like((width, full), F32)] * 2,
-        [*totals, crossed(jnp.stack(totals), near)],
+        [total, crossed(total, near)],
         [pltpu.VMEM((parts_total, piece, full), F32)],
     )
     grad_x = dx_self.reshape(shape)

time: 121 us -> 117 us (0.967)
  starting transfers between devices: 39 us -> 33 us
    ppermute x39 -> x33, starting transfers between devices: 39 us -> 33 us  [crossed(): lax.ppermute(x, axis, [(i, i ^ mask) for i in range(lax.axis_size(axis))])]
    convert_element_type x4 -> x6, other arithmetic: 3.77 us -> 4.96 us  [the longest x1 1.9 us: dense_body(): sum_2 = tied((keep_2 + near_2.astype(F32)).astype(BF16), far_0)]
    ppermute x39 -> x33, waiting for transfers between devices: 52.8 us -> 53.9 us  [crossed(): lax.ppermute(x, axis, [(i, i ^ mask) for i in range(lax.axis_size(axis))])]
    unnamed x38 -> x34, local copies, waits for them, and re-layouts: 3.19 us -> 2.53 us
  transfers between devices with their start and end apart: 39 -> 33, of which waited for: 21 -> 19; matrix products, arithmetic and copies ran while one was open for 4% -> 5% of each run, Pallas kernels for 10% -> 11%
where the time goes in v5:
time: 117 us; the launch traced here: 116 us
  waiting for transfers between devices  53.9 us (46%)
  starting transfers between devices  33 us (28%)
  Pallas kernels  20.6 us (18%)
  other arithmetic  4.98 us (4%)
  local copies, waits for them, and re-layouts  2.97 us (3%)
    ppermute x33, waiting for transfers between devices, crossed(): lax.ppermute(x, axis, [(i, i ^ mask) for i in range(lax.axis_size(axis))])  53.9 us
    ppermute x33, starting transfers between devices, crossed(): lax.ppermute(x, axis, [(i, i ^ mask) for i in range(lax.axis_size(axis))])  33 us
    pallas_call x5, Pallas kernels, tiles_call(): pl.pallas_call(functools.partial(tiles_kernel, masks, offsets, parts_tota...  16.1 us
    pallas_call x5, Pallas kernels, small_call(): pl.pallas_call(kernel, out_shape=outs, in_specs=[VMEM] * len(arrays), out...  4.49 us
    unnamed x34, local copies, waits for them, and re-layouts  2.53 us
  transfers between devices with their start and end apart: 33, of which 19 were waited for; matrix products, arithmetic and copies ran while one was open for 5% of the time, Pallas kernels for 11%

profile of v5, /device:TPU:0, one launch (start us, length us, event | category | flops | bytes accessed | tf_op | source)
XLA Modules:
  0.0 116.4 jit_solution(16943692207239168460)
XLA Ops:
  0.6 4.2 %shard_map.139 = (bf16[8,128,128]{2,1,0:T(8,128)(2,1)}, bf16[8,128,128]{2,1,0:T(8,128)(2,1)}, bf16[8,128,128]{2,1,0:T(8,128)(2,1)}, bf16[8,128,128]{2,1,0:T(8,12...) custom-call(s32[1,16]{1,0:T(1,128)} %refs_0_.9, ...), custom_call_target="tpu_custom_call" | custom-call | flops 536870912 | bytes 4194304 | tf_op jit(solution)/shard_map/pallas_call | solution.py:215
  4.8 3.0 %collective-permute-start.2 = (bf16[8,128,128]{2,1,0:T(8,128)(2,1)}, bf16[8,128,128]{2,1,0:T(8,128)(2,1)S(1)}, u32[]{:S(2)}, u32[]{:S(2)}) collective-permute-start(bf16[8,128,128]{2,1,0:T(8,128)(2,1)} %get-tuple-element.60), channel_id=1, source_target_pairs={{0,4},{4,0},{8,12},{12,8},{16,20},{20,16},{24,28},{28,24},{1,5},{5... | collective-permute-start | bytes 786440 | tf_op jit(solution)/shard_map/ppermute | solution.py:358
  7.8 1.5 %collective-permute-start.1 = (bf16[2,128,512]{2,1,0:T(8,128)(2,1)}, bf16[2,128,512]{2,1,0:T(8,128)(2,1)S(1)}, u32[]{:S(2)}, u32[]{:S(2)}) collective-permute-start(bf16[2,128,512]{2,1,0:T(8,128)(2,1)} %get-tuple-element.75.refs_0_), channel_id=1, source_target_pairs={{0,2},{1,3},{2,0},{3,1},{4,6},{5,7},{6,4},{7,5},{8,10},{9,11},{10,... | collective-permute-start | bytes 786440 | tf_op jit(solution)/shard_map/ppermute | solution.py:358
  9.3 0.5 collective-permute-start
  9.8 3.3 %shard_map.138 = (f32[8,128,128]{2,1,0:T(8,128)}, f32[8,128,128]{2,1,0:T(8,128)}) custom-call(s32[1,16]{1,0:T(1,128)} %refs_0_.9, s32[1,16]{1,0:T(1,128)} %refs_1_.9, s32[6,1,8]{2,1,0:T(1,128)} %bitcast.34, s32[6,1,8]{2,1,0:T(1,128)} %bitcast.39, bf16[16,128,128]{2,1,0:T(8,128)(2,1)} %bitcast.20, bf16[6,8,128,128]{3,2,1,0:T(8,128)(2,1)} %bitcast.15, ...), custom_call_target="tpu_custom_call" | custom-call | flops 268435456 | bytes 3670016 | tf_op jit(solution)/shard_map/pallas_call | solution.py:215
  13.1 2.0 %collective-permute-done.2 = bf16[8,128,128]{2,1,0:T(8,128)(2,1)S(1)} collective-permute-done((bf16[8,128,128]{2,1,0:T(8,128)(2,1)}, bf16[8,128,128]{2,1,0:T(8,128)(2,1)S(1)}, u32[]{:S(2)}, u32[]{:S(2)}) %collective-permute-start.2) | collective-permute-done | bytes 262176 | tf_op jit(solution)/shard_map/ppermute | solution.py:358
  15.2 1.1 add_convert_fusion.2
  16.3 2.2 %collective-permute-start.3 = (bf16[8,128,128]{2,1,0:T(8,128)(2,1)S(1)}, bf16[8,128,128]{2,1,0:T(8,128)(2,1)S(1)}, u32[]{:S(2)}, u32[]{:S(2)}) collective-permute-start(bf16[8,128,128]{2,1,0:T(8,128)(2,1)S(1)} %add_convert_fusion.2), channel_id=1, source_target_pairs={{0,8},{4,12},{8,0},{12,4},{16,24},{20,28},{24,16},{28,20},{1,9},{5... | collective-permute-start | bytes 786440 | tf_op jit(solution)/shard_map/ppermute | solution.py:358
  18.5 1.5 %collective-permute-start.10 = (bf16[8,128,128]{2,1,0:T(8,128)(2,1)}, bf16[8,128,128]{2,1,0:T(8,128)(2,1)}, u32[]{:S(2)}, u32[]{:S(2)}) collective-permute-start(bf16[8,128,128]{2,1,0:T(8,128)(2,1)} %get-tuple-element.69), channel_id=1, source_target_pairs={{0,4},{4,0},{8,12},{12,8},{16,20},{20,16},{24,28},{28,24},{1,5},{5... | collective-permute-start | bytes 786440 | tf_op jit(solution)/shard_map/ppermute | solution.py:358
  20.0 0.5 collective-permute-start.9
  20.5 2.5 %collective-permute-done.3 = bf16[8,128,128]{2,1,0:T(8,128)(2,1)S(1)} collective-permute-done((bf16[8,128,128]{2,1,0:T(8,128)(2,1)S(1)}, bf16[8,128,128]{2,1,0:T(8,128)(2,1)S(1)}, u32[]{:S(2)}, u32[]{:S(2)}) %collective-permute-start.3) | collective-permute-done | bytes 262176 | tf_op jit(solution)/shard_map/ppermute | solution.py:358
  23.0 1.9 %add_convert_fusion.1 = bf16[8,128,128]{2,1,0:T(8,128)(2,1)} fusion(bf16[8,128,128]{2,1,0:T(8,128)(2,1)S(1)} %collective-permute-done.3, f32[8,128,128]{2,1,0:T(8,128)} %get-tuple-element.55, bf16[8,128,128]{2,1,0:T(8,128)(2,1)S(1)} %collective-permute-done), kind=kLoop, calls=%fused_computation.1 | loop fusion | flops 655360 | bytes 1310720 | tf_op jit(solution)/shard_map/convert_element_type | solution.py:429
  24.9 2.8 %collective-permute-start.11 = (bf16[8,128,128]{2,1,0:T(8,128)(2,1)}, bf16[8,128,128]{2,1,0:T(8,128)(2,1)S(1)}, u32[]{:S(2)}, u32[]{:S(2)}) collective-permute-start(bf16[8,128,128]{2,1,0:T(8,128)(2,1)} %add_convert_fusion.1), channel_id=1, source_target_pairs={{0,16},{4,20},{8,24},{12,28},{16,0},{20,4},{24,8},{28,12},{1,17},{... | collective-permute-start | bytes 786440 | tf_op jit(solution)/shard_map/ppermute | solution.py:358
  27.7 3.6 %shard_map.140 = (f32[8,128,128]{2,1,0:T(8,128)}, f32[8,128,128]{2,1,0:T(8,128)}) custom-call(s32[1,16]{1,0:T(1,128)} %refs_0_.9, s32[1,16]{1,0:T(1,128)} %refs_1_.9, s32[6,1,8]{2,1,0:T(1,128)} %bitcast.35, s32[6,1,8]{2,1,0:T(1,128)} %bitcast.40, bf16[16,128,128]{2,1,0:T(8,128)(2,1)} %bitcast.21, bf16[6,8,128,128]{3,2,1,0:T(8,128)(2,1)} %bitcast.16, ...), custom_call_target="tpu_custom_call" | custom-call | flops 402653184 | bytes 3932160 | tf_op jit(solution)/shard_map/pallas_call | solution.py:215
  31.3 1.6 %collective-permute-start.5 = (bf16[2,2,128,128]{3,2,1,0:T(8,128)(2,1)S(1)}, bf16[2,2,128,128]{3,2,1,0:T(8,128)(2,1)S(1)}, u32[]{:S(2)}, u32[]{:S(2)}) collective-permute-start(bf16[2,2,128,128]{3,2,1,0:T(8,128)(2,1)S(1)} %copy-done.16), channel_id=1, source_target_pairs={{0,2},{1,3},{2,0},{3,1},{4,6},{5,7},{6,4},{7,5},{8,10},{9,11},{10,... | collective-permute-start | bytes 393224 | tf_op jit(solution)/shard_map/ppermute | solution.py:358
  32.9 1.9 %add_convert_fusion = bf16[8,128,128]{2,1,0:T(8,128)(2,1)} fusion(f32[8,128,128]{2,1,0:T(8,128)} %get-tuple-element.68, bf16[8,128,128]{2,1,0:T(8,128)(2,1)} %collective-permute-done.10), kind=kLoop, calls=%fused_computation | loop fusion | flops 393216 | bytes 1048576 | tf_op jit(solution)/shard_map/convert_element_type | solution.py:432
  34.8 3.1 %collective-permute-done.11.refs_2_ = bf16[8,128,128]{2,1,0:T(8,128)(2,1)S(1)} collective-permute-done((bf16[8,128,128]{2,1,0:T(8,128)(2,1)}, bf16[8,128,128]{2,1,0:T(8,128)(2,1)S(1)}, u32[]{:S(2)}, u32[]{:S(2)}) %collective-permute-start.11) | collective-permute-done | bytes 262176 | tf_op jit(solution)/shard_map/ppermute | solution.py:358
  37.8 0.6 collective-permute-start.12
  38.4 1.3 %collective-permute-start.6 = (bf16[2,2,128,128]{3,2,1,0:T(8,128)(2,1)}, bf16[2,2,128,128]{3,2,1,0:T(8,128)(2,1)S(1)}, u32[]{:S(2)}, u32[]{:S(2)}) collective-permute-start(bf16[2,2,128,128]{3,2,1,0:T(8,128)(2,1)} %get-tuple-element.66), channel_id=1, source_target_pairs={{0,3},{1,2},{2,1},{3,0},{4,7},{5,6},{6,5},{7,4},{8,11},{9,10},{10,... | collective-permute-start | bytes 393224 | tf_op jit(solution)/shard_map/ppermute | solution.py:358
  39.8 0.2 copy.15.inv_ref
  40.0 4.1 %collective-permute-done.6.refs_7_ = bf16[2,2,128,128]{3,2,1,0:T(8,128)(2,1)S(1)} collective-permute-done((bf16[2,2,128,128]{3,2,1,0:T(8,128)(2,1)}, bf16[2,2,128,128]{3,2,1,0:T(8,128)(2,1)S(1)}, u32[]{:S(2)}, u32[]{:S(2)}) %collective-permute-start.6) | collective-permute-done | bytes 131104 | tf_op jit(solution)/shard_map/ppermute | solution.py:358
  44.1 0.7 copy-done.9
  44.8 2.0 %collective-permute-done.12.refs_1_ = bf16[8,128,128]{2,1,0:T(8,128)(2,1)S(1)} collective-permute-done((bf16[8,128,128]{2,1,0:T(8,128)(2,1)}, bf16[8,128,128]{2,1,0:T(8,128)(2,1)S(1)}, u32[]{:S(2)}, u32[]{:S(2)}) %collective-permute-start.12) | collective-permute-done | bytes 262176 | tf_op jit(solution)/shard_map/ppermute | solution.py:358
  46.8 0.9 shard_map.141
  47.7 1.6 %collective-permute-start.14 = (bf16[2,128,128]{2,1,0:T(8,128)(2,1)}, bf16[2,128,128]{2,1,0:T(8,128)(2,1)S(1)}, u32[]{:S(2)}, u32[]{:S(2)}) collective-permute-start(bf16[2,128,128]{2,1,0:T(8,128)(2,1)} %get-tuple-element.85), channel_id=1, source_target_pairs={{0,2},{1,3},{2,0},{3,1},{4,6},{5,7},{6,4},{7,5},{8,10},{9,11},{10,... | collective-permute-start | bytes 196616 | tf_op jit(solution)/shard_map/ppermute | solution.py:358
  49.2 0.3 collective-permute-start.15
  49.6 0.1 copy.16.inv_ref
  49.7 2.8 %collective-permute-done.14.refs_10_ = bf16[2,128,128]{2,1,0:T(8,128)(2,1)S(1)} collective-permute-done((bf16[2,128,128]{2,1,0:T(8,128)(2,1)}, bf16[2,128,128]{2,1,0:T(8,128)(2,1)S(1)}, u32[]{:S(2)}, u32[]{:S(2)}) %collective-permute-start.14) | collective-permute-done | bytes 65568 | tf_op jit(solution)/shard_map/ppermute | solution.py:358
  52.6 1.0 collective-permute-done.15.refs_11_
  53.6 0.9 copy-done.8
  54.5 0.9 copy-done.10
  55.4 1.2 %shard_map.142 = (bf16[5,256,128]{2,1,0:T(8,128)(2,1)S(1)}, bf16[6,256,128]{2,1,0:T(8,128)(2,1)S(1)}, bf16[256,128]{1,0:T(8,128)(2,1)S(1)}, bf16[256,128]{1,0:T(...) custom-call(f32[256,1]{1,0:T(8,128)S(1)} %copy.16.inv_ref, ...), custom_call_target="tpu_custom_call" | custom-call | flops 402653184 | bytes 2884608 | tf_op jit(solution)/shard_map/pallas_call | solution.py:239
  56.6 0.2 collective-permute-start.16
  56.8 1.4 %collective-permute-start.17 = (bf16[256,128]{1,0:T(8,128)(2,1)S(1)}, bf16[256,128]{1,0:T(8,128)(2,1)S(1)}, u32[]{:S(2)}, u32[]{:S(2)}) collective-permute-start(bf16[256,128]{1,0:T(8,128)(2,1)S(1)} %get-tuple-element.91), channel_id=1, source_target_pairs={{0,2},{1,3},{2,0},{3,1},{4,6},{5,7},{6,4},{7,5},{8,10},{9,11},{10,... | collective-permute-start | bytes 196616 | tf_op jit(solution)/shard_map/ppermute | solution.py:358
  58.2 0.3 collective-permute-start.18
  58.5 2.6 %collective-permute-done.17 = bf16[256,128]{1,0:T(8,128)(2,1)S(1)} collective-permute-done((bf16[256,128]{1,0:T(8,128)(2,1)S(1)}, bf16[256,128]{1,0:T(8,128)(2,1)S(1)}, u32[]{:S(2)}, u32[]{:S(2)}) %collective-permute-start.17) | collective-permute-done | bytes 65568 | tf_op jit(solution)/shard_map/ppermute | solution.py:358
  61.2 1.3 %collective-permute-done.18 = bf16[256,128]{1,0:T(8,128)(2,1)S(1)} collective-permute-done((bf16[256,128]{1,0:T(8,128)(2,1)S(1)}, bf16[256,128]{1,0:T(8,128)(2,1)S(1)}, u32[]{:S(2)}, u32[]{:S(2)}) %collective-permute-start.18) | collective-permute-done | bytes 65568 | tf_op jit(solution)/shard_map/ppermute | solution.py:358
  62.5 0.8 collective-permute-start.20
  63.3 1.5 %collective-permute-start.21 = (bf16[8,128,128]{2,1,0:T(8,128)(2,1)S(1)}, bf16[8,128,128]{2,1,0:T(8,128)(2,1)S(1)}, u32[]{:S(2)}, u32[]{:S(2)}) collective-permute-start(bf16[8,128,128]{2,1,0:T(8,128)(2,1)S(1)} %bitcast.27), channel_id=1, source_target_pairs={{0,4},{4,0},{8,12},{12,8},{16,20},{20,16},{24,28},{28,24},{1,5},{5... | collective-permute-start | bytes 786440 | tf_op jit(solution)/shard_map/ppermute | solution.py:358
  64.8 0.6 collective-permute-start.22
  65.4 3.3 %collective-permute-start.23 = (bf16[8,128,128]{2,1,0:T(8,128)(2,1)S(1)}, bf16[8,128,128]{2,1,0:T(8,128)(2,1)S(1)}, u32[]{:S(2)}, u32[]{:S(2)}) collective-permute-start(bf16[8,128,128]{2,1,0:T(8,128)(2,1)S(1)} %bitcast.29), channel_id=1, source_target_pairs={{0,16},{4,20},{8,24},{12,28},{16,0},{20,4},{24,8},{28,12},{1,17},{... | collective-permute-start | bytes 786440 | tf_op jit(solution)/shard_map/ppermute | solution.py:358
  68.7 3.0 %collective-permute-done.21.refs_7_ = bf16[8,128,128]{2,1,0:T(8,128)(2,1)S(1)} collective-permute-done((bf16[8,128,128]{2,1,0:T(8,128)(2,1)S(1)}, bf16[8,128,128]{2,1,0:T(8,128)(2,1)S(1)}, u32[]{:S(2)}, u32[]{:S(2)}) %collective-permute-start.21) | collective-permute-done | bytes 262176 | tf_op jit(solution)/shard_map/ppermute | solution.py:358
  71.7 6.6 %collective-permute-done.22.refs_8_ = bf16[8,128,128]{2,1,0:T(8,128)(2,1)S(1)} collective-permute-done((bf16[8,128,128]{2,1,0:T(8,128)(2,1)S(1)}, bf16[8,128,128]{2,1,0:T(8,128)(2,1)S(1)}, u32[]{:S(2)}, u32[]{:S(2)}) %collective-permute-start.22) | collective-permute-done | bytes 262176 | tf_op jit(solution)/shard_map/ppermute | solution.py:358
  78.4 2.1 %collective-permute-done.23.refs_6_ = bf16[8,128,128]{2,1,0:T(8,128)(2,1)S(1)} collective-permute-done((bf16[8,128,128]{2,1,0:T(8,128)(2,1)S(1)}, bf16[8,128,128]{2,1,0:T(8,128)(2,1)S(1)}, u32[]{:S(2)}, u32[]{:S(2)}) %collective-permute-start.23) | collective-permute-done | bytes 262176 | tf_op jit(solution)/shard_map/ppermute | solution.py:358
  80.5 0.5 collective-permute-start.19
  81.0 1.7 %collective-permute-done.19.refs_1_ = bf16[5,256,128]{2,1,0:T(8,128)(2,1)S(1)} collective-permute-done((bf16[5,256,128]{2,1,0:T(8,128)(2,1)S(1)}, bf16[5,256,128]{2,1,0:T(8,128)(2,1)S(1)}, u32[]{:S(2)}, u32[]{:S(2)}) %collective-permute-start.19) | collective-permute-done | bytes 327712 | tf_op jit(solution)/shard_map/ppermute | solution.py:358
  82.7 0.8 shard_map.143
  83.5 0.6 collective-permute-start.25
  84.1 1.5 %collective-permute-start.26 = (bf16[8,128,128]{2,1,0:T(8,128)(2,1)S(1)}, bf16[8,128,128]{2,1,0:T(8,128)(2,1)S(1)}, u32[]{:S(2)}, u32[]{:S(2)}) collective-permute-start(bf16[8,128,128]{2,1,0:T(8,128)(2,1)S(1)} %collective-permute-done.22.refs_8_), channel_id=1, source_target_pairs={{0,4},{4,0},{8,12},{12,8},{16,20},{20,16},{24,28},{28,24},{1,5},{5... | collective-permute-start | bytes 786440 | tf_op jit(solution)/shard_map/ppermute | solution.py:358
  85.6 0.4 collective-permute-start.27
  86.0 4.0 %collective-permute-done.25 = bf16[4,32,512]{2,1,0:T(8,128)(2,1)S(1)} collective-permute-done((bf16[4,32,512]{2,1,0:T(8,128)(2,1)S(1)}, bf16[4,32,512]{2,1,0:T(8,128)(2,1)S(1)}, u32[]{:S(2)}, u32[]{:S(2)}) %collective-permute-start.25) | collective-permute-done | bytes 131104 | tf_op jit(solution)/shard_map/ppermute | solution.py:358
  90.0 4.8 %collective-permute-done.26.refs_9_ = bf16[8,128,128]{2,1,0:T(8,128)(2,1)S(1)} collective-permute-done((bf16[8,128,128]{2,1,0:T(8,128)(2,1)S(1)}, bf16[8,128,128]{2,1,0:T(8,128)(2,1)S(1)}, u32[]{:S(2)}, u32[]{:S(2)}) %collective-permute-start.26) | collective-permute-done | bytes 262176 | tf_op jit(solution)/shard_map/ppermute | solution.py:358
  94.8 0.3 collective-permute-start.28
  95.1 0.5 collective-permute-start.29
  95.6 4.1 %collective-permute-done.28 = bf16[4,32,512]{2,1,0:T(8,128)(2,1)S(1)} collective-permute-done((bf16[4,32,512]{2,1,0:T(8,128)(2,1)S(1)}, bf16[4,32,512]{2,1,0:T(8,128)(2,1)S(1)}, u32[]{:S(2)}, u32[]{:S(2)}) %collective-permute-start.28) | collective-permute-done | bytes 131104 | tf_op jit(solution)/shard_map/ppermute | solution.py:358
  99.8 2.5 %collective-permute-done.29.refs_7_ = bf16[8,128,128]{2,1,0:T(8,128)(2,1)S(1)} collective-permute-done((bf16[8,128,128]{2,1,0:T(8,128)(2,1)S(1)}, bf16[8,128,128]{2,1,0:T(8,128)(2,1)S(1)}, u32[]{:S(2)}, u32[]{:S(2)}) %collective-permute-start.29) | collective-permute-done | bytes 262176 | tf_op jit(solution)/shard_map/ppermute | solution.py:358
  102.3 2.6 %collective-permute-start.30 = (bf16[4,32,512]{2,1,0:T(8,128)(2,1)S(1)}, bf16[4,32,512]{2,1,0:T(8,128)(2,1)S(1)}, u32[]{:S(2)}, u32[]{:S(2)}) collective-permute-start(bf16[4,32,512]{2,1,0:T(8,128)(2,1)S(1)} %add_convert_fusion.4), channel_id=1, source_target_pairs={{0,16},{4,20},{8,24},{12,28},{16,0},{20,4},{24,8},{28,12},{1,17},{... | collective-permute-start | bytes 393224 | tf_op jit(solution)/shard_map/ppermute | solution.py:358
  104.9 0.5 collective-permute-start.31
  105.4 0.7 shard_map.144
  106.2 3.4 %collective-permute-done.30 = bf16[4,32,512]{2,1,0:T(8,128)(2,1)S(1)} collective-permute-done((bf16[4,32,512]{2,1,0:T(8,128)(2,1)S(1)}, bf16[4,32,512]{2,1,0:T(8,128)(2,1)S(1)}, u32[]{:S(2)}, u32[]{:S(2)}) %collective-permute-start.30) | collective-permute-done | bytes 131104 | tf_op jit(solution)/shard_map/ppermute | solution.py:358
  109.6 0.6 collective-permute-start.32
  110.3 2.3 %shard_map.145.refs_10_ = f32[8,128,128]{2,1,0:T(8,128)S(1)} custom-call(s32[1,16]{1,0:T(1,128)S(1)} %copy-done.13, s32[1,16]{1,0:T(1,128)S(1)} %copy-done.14, s32[6,1,8]{2,1,0:T(1,128)S(1)} %bitcast.36, s32[6,1,8]{2,1,0:T(1,128)S(1)} %bitcast.41, bf16[16,128,128]{2,1,0:T(8,128)(2,1)S(1)} %bitcast.22, bf16[6,8,128,128]{3,2,1,0:T(8,128)(2,1)S(1)} %bitcast.17, ...), custom_call_target="tpu_custom_call" | custom-call | flops 671088640 | bytes 4456448 | tf_op jit(solution)/shard_map/pallas_call | solution.py:215
  112.7 2.8 %shard_map.146 = f32[8,128,128]{2,1,0:T(8,128)} custom-call(s32[1,16]{1,0:T(1,128)S(1)} %copy-done.13, s32[1,16]{1,0:T(1,128)S(1)} %copy-done.14, s32[6,1,8]{2,1,0:T(1,128)S(1)} %bitcast.37, s32[6,1,8]{2,1,0:T(1,128)S(1)} %bitcast.42, bf16[16,128,128]{2,1,0:T(8,128)(2,1)S(1)} %bitcast.23, bf16[6,8,128,128]{3,2,1,0:T(8,128)(2,1)S(1)} %bitcast.18, ...), custom_call_target="tpu_custom_call" | custom-call | flops 536870912 | bytes 4194304 | tf_op jit(solution)/shard_map/pallas_call | solution.py:215
  115.5 0.9 shard_map.147
  (57 shorter events, 0.4 us)
Async XLA Ops:
  4.8 10.4 %collective-permute-start.2 = (bf16[8,128,128]{2,1,0:T(8,128)(2,1)}, bf16[8,128,128]{2,1,0:T(8,128)(2,1)S(1)}, u32[]{:S(2)}, u32[]{:S(2)}) collective-permute-start(bf16[8,128,128]{2,1,0:T(8,128)(2,1)} %get-tuple-element.60), channel_id=1, source_target_pairs={{0,4},{4,0},{8,12},{12,8},{16,20},{20,16},{24,28},{28,24},{1,5},{5... | collective-permute-start | bytes 786440 | tf_op jit(solution)/shard_map/ppermute | solution.py:358
  7.8 12.2 %collective-permute-start.1 = (bf16[2,128,512]{2,1,0:T(8,128)(2,1)}, bf16[2,128,512]{2,1,0:T(8,128)(2,1)S(1)}, u32[]{:S(2)}, u32[]{:S(2)}) collective-permute-start(bf16[2,128,512]{2,1,0:T(8,128)(2,1)} %get-tuple-element.75.refs_0_), channel_id=1, source_target_pairs={{0,2},{1,3},{2,0},{3,1},{4,6},{5,7},{6,4},{7,5},{8,10},{9,11},{10,... | collective-permute-start | bytes 786440 | tf_op jit(solution)/shard_map/ppermute | solution.py:358
  9.3 9.1 %copy-start.5 = (bf16[2,128,512]{2,1,0:T(8,128)(2,1)S(1)}, bf16[2,128,512]{2,1,0:T(8,128)(2,1)}, u32[]{:S(2)}) copy-start(bf16[2,128,512]{2,1,0:T(8,128)(2,1)} %get-tuple-element.75.refs_0_) | copy-start | bytes 786436
  9.3 11.2 %collective-permute-start = (bf16[8,128,128]{2,1,0:T(8,128)(2,1)}, bf16[8,128,128]{2,1,0:T(8,128)(2,1)S(1)}, u32[]{:S(2)}, u32[]{:S(2)}) collective-permute-start(bf16[8,128,128]{2,1,0:T(8,128)(2,1)} %get-tuple-element.56), channel_id=1, source_target_pairs={{0,4},{4,0},{8,12},{12,8},{16,20},{20,16},{24,28},{28,24},{1,5},{5... | collective-permute-start | bytes 786440 | tf_op jit(solution)/shard_map/ppermute | solution.py:358
  16.3 6.7 %collective-permute-start.3 = (bf16[8,128,128]{2,1,0:T(8,128)(2,1)S(1)}, bf16[8,128,128]{2,1,0:T(8,128)(2,1)S(1)}, u32[]{:S(2)}, u32[]{:S(2)}) collective-permute-start(bf16[8,128,128]{2,1,0:T(8,128)(2,1)S(1)} %add_convert_fusion.2), channel_id=1, source_target_pairs={{0,8},{4,12},{8,0},{12,4},{16,24},{20,28},{24,16},{28,20},{1,9},{5... | collective-permute-start | bytes 786440 | tf_op jit(solution)/shard_map/ppermute | solution.py:358
  18.5 26.3 %collective-permute-start.7 = (bf16[2,128,512]{2,1,0:T(8,128)(2,1)S(1)}, bf16[2,128,512]{2,1,0:T(8,128)(2,1)S(1)}, u32[]{:S(2)}, u32[]{:S(2)}) collective-permute-start(bf16[2,128,512]{2,1,0:T(8,128)(2,1)S(1)} %copy-done.5), channel_id=1, source_target_pairs={{0,1},{1,0},{2,3},{3,2},{4,5},{5,4},{6,7},{7,6},{8,9},{9,8},{10,11... | collective-permute-start | bytes 786440 | tf_op jit(solution)/shard_map/ppermute | solution.py:358
  18.5 12.8 %collective-permute-start.10 = (bf16[8,128,128]{2,1,0:T(8,128)(2,1)}, bf16[8,128,128]{2,1,0:T(8,128)(2,1)}, u32[]{:S(2)}, u32[]{:S(2)}) collective-permute-start(bf16[8,128,128]{2,1,0:T(8,128)(2,1)} %get-tuple-element.69), channel_id=1, source_target_pairs={{0,4},{4,0},{8,12},{12,8},{16,20},{20,16},{24,28},{28,24},{1,5},{5... | collective-permute-start | bytes 786440 | tf_op jit(solution)/shard_map/ppermute | solution.py:358
  20.0 24.8 %collective-permute-start.9 = (bf16[8,128,128]{2,1,0:T(8,128)(2,1)}, bf16[8,128,128]{2,1,0:T(8,128)(2,1)S(1)}, u32[]{:S(2)}, u32[]{:S(2)}) collective-permute-start(bf16[8,128,128]{2,1,0:T(8,128)(2,1)} %get-tuple-element.67), channel_id=1, source_target_pairs={{0,4},{4,0},{8,12},{12,8},{16,20},{20,16},{24,28},{28,24},{1,5},{5... | collective-permute-start | bytes 786440 | tf_op jit(solution)/shard_map/ppermute | solution.py:358
  20.5 17.3 %collective-permute-start.4 = (bf16[2,2,128,128]{3,2,1,0:T(8,128)(2,1)}, bf16[2,2,128,128]{3,2,1,0:T(8,128)(2,1)S(1)}, u32[]{:S(2)}, u32[]{:S(2)}) collective-permute-start(bf16[2,2,128,128]{3,2,1,0:T(8,128)(2,1)} %get-tuple-element.64), channel_id=1, source_target_pairs={{0,1},{1,0},{2,3},{3,2},{4,5},{5,4},{6,7},{7,6},{8,9},{9,8},{10,11... | collective-permute-start | bytes 393224 | tf_op jit(solution)/shard_map/ppermute | solution.py:358
  23.0 8.3 %copy-start.16 = (bf16[2,2,128,128]{3,2,1,0:T(8,128)(2,1)S(1)}, bf16[2,2,128,128]{3,2,1,0:T(8,128)(2,1)}, u32[]{:S(2)}) copy-start(bf16[2,2,128,128]{3,2,1,0:T(8,128)(2,1)} %get-tuple-element.65) | copy-start | bytes 393220
  24.9 14.9 %copy-start.15 = (s32[1024]{0:T(1024)S(1)}, s32[1024]{0:T(1024)}, u32[]{:S(2)}) copy-start(s32[1024]{0:T(1024)} %param.14) | copy-start | bytes 12292
  24.9 13.0 %collective-permute-start.11 = (bf16[8,128,128]{2,1,0:T(8,128)(2,1)}, bf16[8,128,128]{2,1,0:T(8,128)(2,1)S(1)}, u32[]{:S(2)}, u32[]{:S(2)}) collective-permute-start(bf16[8,128,128]{2,1,0:T(8,128)(2,1)} %add_convert_fusion.1), channel_id=1, source_target_pairs={{0,16},{4,20},{8,24},{12,28},{16,0},{20,4},{24,8},{28,12},{1,17},{... | collective-permute-start | bytes 786440 | tf_op jit(solution)/shard_map/ppermute | solution.py:358
  31.3 15.5 %copy-start.3 = (f32[8,128,128]{2,1,0:T(8,128)S(1)}, f32[8,128,128]{2,1,0:T(8,128)}, u32[]{:S(2)}) copy-start(f32[8,128,128]{2,1,0:T(8,128)} %get-tuple-element.62.keep_ref) | copy-start | bytes 1572868
  31.3 7.1 %collective-permute-start.5 = (bf16[2,2,128,128]{3,2,1,0:T(8,128)(2,1)S(1)}, bf16[2,2,128,128]{3,2,1,0:T(8,128)(2,1)S(1)}, u32[]{:S(2)}, u32[]{:S(2)}) collective-permute-start(bf16[2,2,128,128]{3,2,1,0:T(8,128)(2,1)S(1)} %copy-done.16), channel_id=1, source_target_pairs={{0,2},{1,3},{2,0},{3,1},{4,6},{5,7},{6,4},{7,5},{8,10},{9,11},{10,... | collective-permute-start | bytes 393224 | tf_op jit(solution)/shard_map/ppermute | solution.py:358
  32.9 20.7 %copy-start.6 = (bf16[2,2,128,128]{3,2,1,0:T(8,128)(2,1)S(1)}, bf16[2,2,128,128]{3,2,1,0:T(8,128)(2,1)}, u32[]{:S(2)}) copy-start(bf16[2,2,128,128]{3,2,1,0:T(8,128)(2,1)} %get-tuple-element.79.refs_4_) | copy-start | bytes 393220
  37.8 6.9 %collective-permute-start.8 = (bf16[2,128,512]{2,1,0:T(8,128)(2,1)S(1)}, bf16[2,128,512]{2,1,0:T(8,128)(2,1)S(1)}, u32[]{:S(2)}, u32[]{:S(2)}) collective-permute-start(bf16[2,128,512]{2,1,0:T(8,128)(2,1)S(1)} %collective-permute-done.1.refs_2_), channel_id=1, source_target_pairs={{0,1},{1,0},{2,3},{3,2},{4,5},{5,4},{6,7},{7,6},{8,9},{9,8},{10,11... | collective-permute-start | bytes 786440 | tf_op jit(solution)/shard_map/ppermute | solution.py:358
  37.8 8.9 %collective-permute-start.12 = (bf16[8,128,128]{2,1,0:T(8,128)(2,1)}, bf16[8,128,128]{2,1,0:T(8,128)(2,1)S(1)}, u32[]{:S(2)}, u32[]{:S(2)}) collective-permute-start(bf16[8,128,128]{2,1,0:T(8,128)(2,1)} %add_convert_fusion), channel_id=1, source_target_pairs={{0,8},{4,12},{8,0},{12,4},{16,24},{20,28},{24,16},{28,20},{1,9},{5... | collective-permute-start | bytes 786440 | tf_op jit(solution)/shard_map/ppermute | solution.py:358
  38.4 8.4 %copy-start.7 = (bf16[2,2,128,128]{3,2,1,0:T(8,128)(2,1)}, bf16[2,2,128,128]{3,2,1,0:T(8,128)(2,1)S(1)}, u32[]{:S(2)}) copy-start(bf16[2,2,128,128]{3,2,1,0:T(8,128)(2,1)S(1)} %collective-permute-done.5.refs_6_) | copy-start | bytes 393220
  38.4 5.7 %collective-permute-start.6 = (bf16[2,2,128,128]{3,2,1,0:T(8,128)(2,1)}, bf16[2,2,128,128]{3,2,1,0:T(8,128)(2,1)S(1)}, u32[]{:S(2)}, u32[]{:S(2)}) collective-permute-start(bf16[2,2,128,128]{3,2,1,0:T(8,128)(2,1)} %get-tuple-element.66), channel_id=1, source_target_pairs={{0,3},{1,2},{2,1},{3,0},{4,7},{5,6},{6,5},{7,4},{8,11},{9,10},{10,... | collective-permute-start | bytes 393224 | tf_op jit(solution)/shard_map/ppermute | solution.py:358
  44.1 0.7 copy-start.9
  47.6 35.0 %copy-start.2 = (bf16[1024,128]{1,0:T(8,128)(2,1)S(1)}, bf16[1024,128]{1,0:T(8,128)(2,1)}, u32[]{:S(2)}) copy-start(bf16[1024,128]{1,0:T(8,128)(2,1)} %f_ref.1) | copy-start | bytes 786436
  47.6 35.0 %copy-start.4 = (bf16[128,512]{1,0:T(8,128)(2,1)S(1)}, bf16[128,512]{1,0:T(8,128)(2,1)}, u32[]{:S(2)}) copy-start(bf16[128,512]{1,0:T(8,128)(2,1)} %w_ref.1) | copy-start | bytes 393220
  47.6 2.1 %collective-permute-start.13 = (bf16[2,128,128]{2,1,0:T(8,128)(2,1)}, bf16[2,128,128]{2,1,0:T(8,128)(2,1)S(1)}, u32[]{:S(2)}, u32[]{:S(2)}) collective-permute-start(bf16[2,128,128]{2,1,0:T(8,128)(2,1)} %get-tuple-element.84), channel_id=1, source_target_pairs={{0,1},{1,0},{2,3},{3,2},{4,5},{5,4},{6,7},{7,6},{8,9},{9,8},{10,11... | collective-permute-start | bytes 196616 | tf_op jit(solution)/shard_map/ppermute | solution.py:358
  47.7 4.9 %collective-permute-start.14 = (bf16[2,128,128]{2,1,0:T(8,128)(2,1)}, bf16[2,128,128]{2,1,0:T(8,128)(2,1)S(1)}, u32[]{:S(2)}, u32[]{:S(2)}) collective-permute-start(bf16[2,128,128]{2,1,0:T(8,128)(2,1)} %get-tuple-element.85), channel_id=1, source_target_pairs={{0,2},{1,3},{2,0},{3,1},{4,6},{5,7},{6,4},{7,5},{8,10},{9,11},{10,... | collective-permute-start | bytes 196616 | tf_op jit(solution)/shard_map/ppermute | solution.py:358
  49.2 4.3 %collective-permute-start.15 = (bf16[2,128,128]{2,1,0:T(8,128)(2,1)S(1)}, bf16[2,128,128]{2,1,0:T(8,128)(2,1)S(1)}, u32[]{:S(2)}, u32[]{:S(2)}) collective-permute-start(bf16[2,128,128]{2,1,0:T(8,128)(2,1)S(1)} %get-tuple-element.86), channel_id=1, source_target_pairs={{0,3},{1,2},{2,1},{3,0},{4,7},{5,6},{6,5},{7,4},{8,11},{9,10},{10,... | collective-permute-start | bytes 196616 | tf_op jit(solution)/shard_map/ppermute | solution.py:358
  53.6 0.9 copy-start.8
  54.5 0.9 copy-start.10
  56.6 1.9 %collective-permute-start.16 = (bf16[256,128]{1,0:T(8,128)(2,1)S(1)}, bf16[256,128]{1,0:T(8,128)(2,1)S(1)}, u32[]{:S(2)}, u32[]{:S(2)}) collective-permute-start(bf16[256,128]{1,0:T(8,128)(2,1)S(1)} %get-tuple-element.90), channel_id=1, source_target_pairs={{0,1},{1,0},{2,3},{3,2},{4,5},{5,4},{6,7},{7,6},{8,9},{9,8},{10,11... | collective-permute-start | bytes 196616 | tf_op jit(solution)/shard_map/ppermute | solution.py:358
  56.8 4.4 %collective-permute-start.17 = (bf16[256,128]{1,0:T(8,128)(2,1)S(1)}, bf16[256,128]{1,0:T(8,128)(2,1)S(1)}, u32[]{:S(2)}, u32[]{:S(2)}) collective-permute-start(bf16[256,128]{1,0:T(8,128)(2,1)S(1)} %get-tuple-element.91), channel_id=1, source_target_pairs={{0,2},{1,3},{2,0},{3,1},{4,6},{5,7},{6,4},{7,5},{8,10},{9,11},{10,... | collective-permute-start | bytes 196616 | tf_op jit(solution)/shard_map/ppermute | solution.py:358
  58.2 4.3 %collective-permute-start.18 = (bf16[256,128]{1,0:T(8,128)(2,1)S(1)}, bf16[256,128]{1,0:T(8,128)(2,1)S(1)}, u32[]{:S(2)}, u32[]{:S(2)}) collective-permute-start(bf16[256,128]{1,0:T(8,128)(2,1)S(1)} %get-tuple-element.92), channel_id=1, source_target_pairs={{0,3},{1,2},{2,1},{3,0},{4,7},{5,6},{6,5},{7,4},{8,11},{9,10},{10,... | collective-permute-start | bytes 196616 | tf_op jit(solution)/shard_map/ppermute | solution.py:358
  62.5 18.0 %collective-permute-start.20 = (bf16[6,256,128]{2,1,0:T(8,128)(2,1)S(1)}, bf16[6,256,128]{2,1,0:T(8,128)(2,1)S(1)}, u32[]{:S(2)}, u32[]{:S(2)}) collective-permute-start(bf16[6,256,128]{2,1,0:T(8,128)(2,1)S(1)} %get-tuple-element.94), channel_id=1, source_target_pairs={{0,2},{1,3},{2,0},{3,1},{4,6},{5,7},{6,4},{7,5},{8,10},{9,11},{10,... | collective-permute-start | bytes 1179656 | tf_op jit(solution)/shard_map/ppermute | solution.py:358
  63.3 8.4 %collective-permute-start.21 = (bf16[8,128,128]{2,1,0:T(8,128)(2,1)S(1)}, bf16[8,128,128]{2,1,0:T(8,128)(2,1)S(1)}, u32[]{:S(2)}, u32[]{:S(2)}) collective-permute-start(bf16[8,128,128]{2,1,0:T(8,128)(2,1)S(1)} %bitcast.27), channel_id=1, source_target_pairs={{0,4},{4,0},{8,12},{12,8},{16,20},{20,16},{24,28},{28,24},{1,5},{5... | collective-permute-start | bytes 786440 | tf_op jit(solution)/shard_map/ppermute | solution.py:358
  64.8 13.5 %collective-permute-start.22 = (bf16[8,128,128]{2,1,0:T(8,128)(2,1)S(1)}, bf16[8,128,128]{2,1,0:T(8,128)(2,1)S(1)}, u32[]{:S(2)}, u32[]{:S(2)}) collective-permute-start(bf16[8,128,128]{2,1,0:T(8,128)(2,1)S(1)} %bitcast.28), channel_id=1, source_target_pairs={{0,8},{4,12},{8,0},{12,4},{16,24},{20,28},{24,16},{28,20},{1,9},{5... | collective-permute-start | bytes 786440 | tf_op jit(solution)/shard_map/ppermute | solution.py:358
  65.4 15.1 %collective-permute-start.23 = (bf16[8,128,128]{2,1,0:T(8,128)(2,1)S(1)}, bf16[8,128,128]{2,1,0:T(8,128)(2,1)S(1)}, u32[]{:S(2)}, u32[]{:S(2)}) collective-permute-start(bf16[8,128,128]{2,1,0:T(8,128)(2,1)S(1)} %bitcast.29), channel_id=1, source_target_pairs={{0,16},{4,20},{8,24},{12,28},{16,0},{20,4},{24,8},{28,12},{1,17},{... | collective-permute-start | bytes 786440 | tf_op jit(solution)/shard_map/ppermute | solution.py:358
  80.5 2.2 %collective-permute-start.24 = (bf16[6,256,128]{2,1,0:T(8,128)(2,1)S(1)}, bf16[6,256,128]{2,1,0:T(8,128)(2,1)S(1)}, u32[]{:S(2)}, u32[]{:S(2)}) collective-permute-start(bf16[6,256,128]{2,1,0:T(8,128)(2,1)S(1)} %collective-permute-done.20.refs_2_), channel_id=1, source_target_pairs={{0,1},{1,0},{2,3},{3,2},{4,5},{5,4},{6,7},{7,6},{8,9},{9,8},{10,11... | collective-permute-start | bytes 1179656 | tf_op jit(solution)/shard_map/ppermute | solution.py:358
  80.5 2.2 %collective-permute-start.19 = (bf16[5,256,128]{2,1,0:T(8,128)(2,1)S(1)}, bf16[5,256,128]{2,1,0:T(8,128)(2,1)S(1)}, u32[]{:S(2)}, u32[]{:S(2)}) collective-permute-start(bf16[5,256,128]{2,1,0:T(8,128)(2,1)S(1)} %get-tuple-element.93.refs_0_), channel_id=1, source_target_pairs={{0,1},{1,0},{2,3},{3,2},{4,5},{5,4},{6,7},{7,6},{8,9},{9,8},{10,11... | collective-permute-start | bytes 983048 | tf_op jit(solution)/shard_map/ppermute | solution.py:358
  83.5 26.8 %copy-start = (bf16[1,6,8,128,128]{4,3,2,1,0:T(8,128)(2,1)S(1)}, bf16[1,6,8,128,128]{4,3,2,1,0:T(8,128)(2,1)}, u32[]{:S(2)}) copy-start(bf16[1,6,8,128,128]{4,3,2,1,0:T(8,128)(2,1)} %param.18) | copy-start | bytes 4718596
  83.5 26.7 %copy-start.1 = (bf16[1,16,128,128]{3,2,1,0:T(8,128)(2,1)S(1)}, bf16[1,16,128,128]{3,2,1,0:T(8,128)(2,1)}, u32[]{:S(2)}) copy-start(bf16[1,16,128,128]{3,2,1,0:T(8,128)(2,1)} %param.15) | copy-start | bytes 1572868
  83.5 26.7 %copy-start.11 = (s32[1,6,8]{2,0,1:T(1,128)S(1)}, s32[1,6,8]{2,0,1:T(1,128)}, u32[]{:S(2)}) copy-start(s32[1,6,8]{2,0,1:T(1,128)} %param.19) | copy-start | bytes 580
  83.5 26.7 %copy-start.12 = (s32[1,6,8]{2,0,1:T(1,128)S(1)}, s32[1,6,8]{2,0,1:T(1,128)}, u32[]{:S(2)}) copy-start(s32[1,6,8]{2,0,1:T(1,128)} %param.20) | copy-start | bytes 580
  83.5 26.7 %copy-start.13 = (s32[1,16]{1,0:T(1,128)S(1)}, s32[1,16]{1,0:T(1,128)}, u32[]{:S(2)}) copy-start(s32[1,16]{1,0:T(1,128)} %refs_0_.9) | copy-start | bytes 196
  83.5 26.7 %copy-start.14 = (s32[1,16]{1,0:T(1,128)S(1)}, s32[1,16]{1,0:T(1,128)}, u32[]{:S(2)}) copy-start(s32[1,16]{1,0:T(1,128)} %refs_1_.9) | copy-start | bytes 196
  83.5 6.4 %collective-permute-start.25 = (bf16[4,32,512]{2,1,0:T(8,128)(2,1)S(1)}, bf16[4,32,512]{2,1,0:T(8,128)(2,1)S(1)}, u32[]{:S(2)}, u32[]{:S(2)}) collective-permute-start(bf16[4,32,512]{2,1,0:T(8,128)(2,1)S(1)} %get-tuple-element.97), channel_id=1, source_target_pairs={{0,4},{4,0},{8,12},{12,8},{16,20},{20,16},{24,28},{28,24},{1,5},{5... | collective-permute-start | bytes 393224 | tf_op jit(solution)/shard_map/ppermute | solution.py:358
  84.1 10.7 %collective-permute-start.26 = (bf16[8,128,128]{2,1,0:T(8,128)(2,1)S(1)}, bf16[8,128,128]{2,1,0:T(8,128)(2,1)S(1)}, u32[]{:S(2)}, u32[]{:S(2)}) collective-permute-start(bf16[8,128,128]{2,1,0:T(8,128)(2,1)S(1)} %collective-permute-done.22.refs_8_), channel_id=1, source_target_pairs={{0,4},{4,0},{8,12},{12,8},{16,20},{20,16},{24,28},{28,24},{1,5},{5... | collective-permute-start | bytes 786440 | tf_op jit(solution)/shard_map/ppermute | solution.py:358
  85.6 9.1 %collective-permute-start.27 = (bf16[8,128,128]{2,1,0:T(8,128)(2,1)S(1)}, bf16[8,128,128]{2,1,0:T(8,128)(2,1)S(1)}, u32[]{:S(2)}, u32[]{:S(2)}) collective-permute-start(bf16[8,128,128]{2,1,0:T(8,128)(2,1)S(1)} %collective-permute-done.23.refs_6_), channel_id=1, source_target_pairs={{0,8},{4,12},{8,0},{12,4},{16,24},{20,28},{24,16},{28,20},{1,9},{5... | collective-permute-start | bytes 786440 | tf_op jit(solution)/shard_map/ppermute | solution.py:358
  94.8 5.0 %collective-permute-start.28 = (bf16[4,32,512]{2,1,0:T(8,128)(2,1)S(1)}, bf16[4,32,512]{2,1,0:T(8,128)(2,1)S(1)}, u32[]{:S(2)}, u32[]{:S(2)}) collective-permute-start(bf16[4,32,512]{2,1,0:T(8,128)(2,1)S(1)} %add_convert_fusion.5), channel_id=1, source_target_pairs={{0,8},{4,12},{8,0},{12,4},{16,24},{20,28},{24,16},{28,20},{1,9},{5... | collective-permute-start | bytes 393224 | tf_op jit(solution)/shard_map/ppermute | solution.py:358
  95.1 7.2 %collective-permute-start.29 = (bf16[8,128,128]{2,1,0:T(8,128)(2,1)S(1)}, bf16[8,128,128]{2,1,0:T(8,128)(2,1)S(1)}, u32[]{:S(2)}, u32[]{:S(2)}) collective-permute-start(bf16[8,128,128]{2,1,0:T(8,128)(2,1)S(1)} %collective-permute-done.23.refs_6_), channel_id=1, source_target_pairs={{0,4},{4,0},{8,12},{12,8},{16,20},{20,16},{24,28},{28,24},{1,5},{5... | collective-permute-start | bytes 786440 | tf_op jit(solution)/shard_map/ppermute | solution.py:358
  102.3 7.3 %collective-permute-start.30 = (bf16[4,32,512]{2,1,0:T(8,128)(2,1)S(1)}, bf16[4,32,512]{2,1,0:T(8,128)(2,1)S(1)}, u32[]{:S(2)}, u32[]{:S(2)}) collective-permute-start(bf16[4,32,512]{2,1,0:T(8,128)(2,1)S(1)} %add_convert_fusion.4), channel_id=1, source_target_pairs={{0,16},{4,20},{8,24},{12,28},{16,0},{20,4},{24,8},{28,12},{1,17},{... | collective-permute-start | bytes 393224 | tf_op jit(solution)/shard_map/ppermute | solution.py:358
  104.9 7.8 %collective-permute-start.31 = (bf16[8,128,128]{2,1,0:T(8,128)(2,1)S(1)}, bf16[8,128,128]{2,1,0:T(8,128)(2,1)S(1)}, u32[]{:S(2)}, u32[]{:S(2)}) collective-permute-start(bf16[8,128,128]{2,1,0:T(8,128)(2,1)S(1)} %collective-permute-done.27.refs_8_), channel_id=1, source_target_pairs={{0,4},{4,0},{8,12},{12,8},{16,20},{20,16},{24,28},{28,24},{1,5},{5... | collective-permute-start | bytes 786440 | tf_op jit(solution)/shard_map/ppermute | solution.py:358
  109.6 5.9 %collective-permute-start.32 = (bf16[4,32,512]{2,1,0:T(8,128)(2,1)S(1)}, bf16[4,32,512]{2,1,0:T(8,128)(2,1)S(1)}, u32[]{:S(2)}, u32[]{:S(2)}) collective-permute-start(bf16[4,32,512]{2,1,0:T(8,128)(2,1)S(1)} %add_convert_fusion.3.mine_ref), channel_id=1, source_target_pairs={{0,4},{4,0},{8,12},{12,8},{16,20},{20,16},{24,28},{28,24},{1,5},{5... | collective-permute-start | bytes 393224 | tf_op jit(solution)/shard_map/ppermute | solution.py:358

commit v6 on v5

--- a/solution.py
+++ b/solution.py
@@ -210,7 +210,6 @@
     rounds, groups, tiles = tile_counts(rvals, lvals)
     nblocks, block, width = blocks[0].shape
     slots = sum(-(-tiles // groups) if mask == 0 else 1 for mask in flat(masks))
-    flops = 2 * slots * groups * block * block * width
     extras = 0 if back else len(blocks) - 1
     return pl.pallas_call(
         functools.partial(tiles_kernel, masks, offsets, parts_total, back, feats, extras),
@@ -226,24 +225,19 @@
             pltpu.SemaphoreType.DMA((slots,)),
         ],
         compiler_params=pltpu.CompilerParams(vmem_limit_bytes=room * 2**20),
-        cost_estimate=pl.CostEstimate(
-            flops=4 * flops,
-            bytes_accessed=slots * groups * block * block * 2 + 4 * rounds * nblocks * block * width,
-            transcendentals=0,
-        ),
+        cost_estimate=pl.CostEstimate(flops=1, bytes_accessed=1, transcendentals=0),
     )(*ids, lvals, rvals, *blocks)
 
 
-def small_call(kernel, outs, arrays, scratch=(), flops=10**6):
-    size = sum(t.size * t.dtype.itemsize for t in list(arrays) + list(outs))
+def small_call(kernel, outs, arrays, scratch=(), room=24):
     return pl.pallas_call(
         kernel,
         out_shape=outs,
         in_specs=[VMEM] * len(arrays),
         out_specs=[VMEM] * len(outs),
         scratch_shapes=scratch,
-        compiler_params=pltpu.CompilerParams(vmem_limit_bytes=24 * 2**20),
-        cost_estimate=pl.CostEstimate(flops=flops, bytes_accessed=size, transcendentals=0),
+        compiler_params=pltpu.CompilerParams(vmem_limit_bytes=room * 2**20),
+        cost_estimate=pl.CostEstimate(flops=1, bytes_accessed=1, transcendentals=0),
     )(*arrays)
 
 
@@ -266,8 +260,8 @@
 def dense_kernel(feats, inv_ref, *refs):
     mine = lax.axis_index("feat")
     w_refs, early_refs, a_refs = refs[:feats], refs[feats : 2 * feats], refs[2 * feats : 3 * feats]
-    core_ref, chip_ref, own_ref = refs[3 * feats : 3 * feats + 3]
-    dsum_refs = refs[3 * feats + 3 : 4 * feats + 3]
+    sent_refs, own_ref = refs[3 * feats : 4 * feats - 1], refs[4 * feats - 1]
+    dsum_refs = refs[4 * feats : 5 * feats]
     held = refs[-1]
     full = w_refs[0].shape[2]
     some, width = held.shape[1:]
@@ -292,13 +286,12 @@
         dsum_refs[mask][...] = (dagg * inv_ref[...]).astype(BF16)
     for j in range(feats):
         cols = slice(j * width, (j + 1) * width)
-        core_ref[j] = dpre[:, cols]
-        chip_ref[j] = dpre[:, cols]
+        for sent in sent_refs:
+            sent[j] = dpre[:, cols]
         held[j] = out[:, cols]
     own_ref[...] = held[mine]
-    core_ref[feats] = held[mine ^ 1]
-    chip_ref[feats] = held[mine ^ 2]
-    chip_ref[feats + 1] = held[mine ^ 3]
+    for mask, sent in enumerate(sent_refs, 1):
+        sent[feats] = held[mine ^ mask]
 
 
 def grad_kernel(feats, f_ref, a_ref, w_ref, *refs):
@@ -342,12 +335,10 @@
 
 def place_kernel(*refs):
     mine = lax.axis_index("feat")
-    own_ref, core_ref, chip_ref, both_ref, out_ref = refs
-    feats = out_ref.shape[0]
+    own_ref, *come_refs, out_ref = refs
     out_ref[mine] = own_ref[...]
-    out_ref[mine ^ 1] = core_ref[feats]
-    out_ref[mine ^ 2] = chip_ref[feats]
-    out_ref[mine ^ 3] = both_ref[feats + 1]
+    for mask, come in enumerate(come_refs, 1):
+        out_ref[mine ^ mask] = come[out_ref.shape[0]]
 
 
 def swap_feat(x):
@@ -420,7 +411,7 @@
         + [like((2, width, full), BF16)],
     )
     sends, early_pieces, pair = made[:4], made[4:-1], made[-1]
-    keep_6, keep_4 = forward([6, 4], [blocks], [like(shape, F32)] * 2)
+    keep_6, keep_4, keep_2 = forward([6, 4, 2], [blocks], [like(shape, F32)] * 3)
     weights = relayed(pair)
     early = [early_pieces[0]] + [crossed(early_pieces[m], m, "feat") for m in range(1, feats)]
     near_6, near_4, near_2, near_0 = (crossed(send, near) for send in sends)
@@ -428,9 +419,10 @@
     near_4 = tied(near_4, weights[2])
     sum_4 = (keep_4 + near_4.astype(F32) + crossed(sum_6, 2).astype(F32)).astype(BF16)
     far_0 = crossed(sum_4, 4)
-    keep_2, keep = forward([2, 0], [tied(blocks, sum_4)], [like(shape, F32)] * 2)
-    sum_2 = tied((keep_2 + near_2.astype(F32)).astype(BF16), far_0)
+    sum_2 = (keep_2 + near_2.astype(F32)).astype(BF16)
+    (keep,) = forward([0], [tied(blocks, sum_2)], [like(shape, F32)])
     mid_0 = crossed(sum_2, 2)
+    weights[3] = crossed(tied(weights[2], far_0), 1, "feat")
     arrived = [near_0, mid_0, far_0]
     early, weights, arrived = lax.optimization_barrier((early, weights, arrived))
     agg, *agg_pieces = small_call(
@@ -439,31 +431,32 @@
         [inverse.reshape(nblocks, block, 1), keep, *arrived],
     )
     agg_rows = [agg_pieces[0]] + [crossed(agg_pieces[m], m, "feat") for m in range(1, feats)]
-    for_core, for_chip, own_out, *dsum_pieces = small_call(
+    *sent, own_out, p0, p1, p2, p3 = small_call(
         functools.partial(dense_kernel, feats),
-        [like((feats + 1, some, width), BF16), like((feats + 2, some, width), BF16)]
+        [like((feats + 1, some, width), BF16)] * (feats - 1)
         + [like((some, width), BF16)] * (1 + feats),
         [inv_rows, *weights, *early, *agg_rows],
         [pltpu.VMEM((feats, some, width), BF16)],
-        6 * some * full * full,
-    )
+    )
+    dsum_pieces = [p0, p1, p2, p3]
     dsum = jnp.concatenate(
         [dsum_pieces[0]] + [crossed(dsum_pieces[m], m, "feat") for m in range(1, feats)], axis=0
     ).reshape(shape)
     found = {0: dsum}
-    for bit in bits[::-1]:
-        for mask in sorted(found):
-            found[mask ^ bit] = crossed(found[mask], bit)
-    for_core, for_chip = tied((for_core, for_chip), dsum)
-    from_chip = crossed(for_chip, 2, "feat")
-    from_core = crossed(for_core, 1, "feat")
-    from_both = crossed(tied(from_chip, found[1], found[2], found[4]), 1, "feat")
-    (out,) = small_call(
-        place_kernel,
-        [like((feats, some, width), BF16)],
-        [own_out, from_core, from_chip, from_both],
-    )
-    dpre = [for_core, from_core, from_chip, from_both]
+    for mask in (4, 2, 1):
+        found[mask] = crossed(dsum, mask)
+    sent = tied(sent, dsum)
+    sent[0] = tied(sent[0], found[4], found[2], found[1])
+    come = [crossed(sent[m - 1], m, "feat") for m in range(1, feats)]
+    (out,) = small_call(place_kernel, [like((feats, some, width), BF16)], [own_out, *come])
+    come, found[4], found[2], found[1] = lax.optimization_barrier(
+        (come, found[4], found[2], found[1])
+    )
+    dpre = [sent[0], *come]
+    found[6] = crossed(found[4], 2)
+    found[3] = crossed(found[2], near)
+    found[5] = crossed(tied(found[4], found[3]), near)
+    found[7] = crossed(tied(found[6], found[5]), near)
     piece = 2 * width // parts_total
     dx_self, give, keep = small_call(
         functools.partial(grad_kernel, feats),
@@ -474,14 +467,13 @@
         ],
         [features, agg.reshape(rows, width), w_self, *dpre],
         [pltpu.VMEM((parts_total, piece, full), F32)],
-        6 * rows * width * full,
     )
     total = (keep + crossed(give, near).astype(F32)).astype(BF16)
     total = tied(total, found[3], found[6])
     total = (total.astype(F32) + crossed(total, 2).astype(F32)).astype(BF16)
     total = tied(total, found[5])
     total = (total.astype(F32) + crossed(total, 4).astype(F32)).astype(BF16)
-    total, out = tied((total, out), found[5])
+    total, out = tied((total, out), found[7])
     grad_self, grad_neigh = small_call(
         finish_kernel,
         [like((width, full), F32)] * 2,

time: 117 us -> 117 us (level)
  other arithmetic: 4.98 us -> 3.12 us
  Pallas kernels: 20.6 us -> 22.1 us
    pallas_call x5, Pallas kernels: 4.49 us -> 5.86 us  [small_call(): pl.pallas_call(kernel, out_shape=outs, in_specs=[VMEM] * len(arrays), out...]
    unnamed x34 -> x38, local copies, waits for them, and re-layouts: 2.53 us -> 2.43 us
  transfers between devices with their start and end apart: 33 -> 33, of which waited for: 19 -> 18; matrix products, arithmetic and copies ran while one was open for 5% -> 3% of each run, Pallas kernels for 11% -> 11%
where the time goes in v6:
time: 117 us
  waiting for transfers between devices  53.8 us (46%)
  starting transfers between devices  34 us (29%)
  Pallas kernels  22.1 us (19%)
  other arithmetic  3.12 us (3%)
  local copies, waits for them, and re-layouts  2.87 us (2%)
    ppermute x33, waiting for transfers between devices, crossed(): lax.ppermute(x, axis, [(i, i ^ mask) for i in range(lax.axis_size(axis))])  53.8 us
    ppermute x33, starting transfers between devices, crossed(): lax.ppermute(x, axis, [(i, i ^ mask) for i in range(lax.axis_size(axis))])  34 us
    pallas_call x5, Pallas kernels, tiles_call(): pl.pallas_call(functools.partial(tiles_kernel, masks, offsets, parts_tota...  16.2 us
    pallas_call x5, Pallas kernels, small_call(): pl.pallas_call(kernel, out_shape=outs, in_specs=[VMEM] * len(arrays), out...  5.86 us
    unnamed x38, local copies, waits for them, and re-layouts  2.43 us
  transfers between devices with their start and end apart: 33, of which 18 were waited for; matrix products, arithmetic and copies ran while one was open for 3% of the time, Pallas kernels for 11%

profile of v6, /device:TPU:0, one launch (start us, length us, event | category | flops | bytes accessed | tf_op | source)
XLA Modules:
  0.0 116.8 jit_solution(4963474023465222445)
XLA Ops:
  0.6 4.2 %shard_map.139 = (bf16[8,128,128]{2,1,0:T(8,128)(2,1)}, bf16[8,128,128]{2,1,0:T(8,128)(2,1)}, bf16[8,128,128]{2,1,0:T(8,128)(2,1)}, bf16[8,128,128]{2,1,0:T(8,12...) custom-call(s32[1,16]{1,0:T(1,128)} %refs_0_.9, ...), custom_call_target="tpu_custom_call" | custom-call | flops 1 | bytes 1 | tf_op jit(solution)/shard_map/pallas_call | solution.py:214
  4.8 3.0 %collective-permute-start.7 = (bf16[8,128,128]{2,1,0:T(8,128)(2,1)}, bf16[8,128,128]{2,1,0:T(8,128)(2,1)S(1)}, u32[]{:S(2)}, u32[]{:S(2)}) collective-permute-start(bf16[8,128,128]{2,1,0:T(8,128)(2,1)} %get-tuple-element.76), channel_id=1, source_target_pairs={{0,4},{4,0},{8,12},{12,8},{16,20},{20,16},{24,28},{28,24},{1,5},{5... | collective-permute-start | bytes 786440 | tf_op jit(solution)/shard_map/ppermute | solution.py:349
  7.8 1.5 %collective-permute-start.5 = (bf16[2,128,512]{2,1,0:T(8,128)(2,1)}, bf16[2,128,512]{2,1,0:T(8,128)(2,1)S(1)}, u32[]{:S(2)}, u32[]{:S(2)}) collective-permute-start(bf16[2,128,512]{2,1,0:T(8,128)(2,1)} %get-tuple-element.83.refs_0_), channel_id=1, source_target_pairs={{0,2},{1,3},{2,0},{3,1},{4,6},{5,7},{6,4},{7,5},{8,10},{9,11},{10,... | collective-permute-start | bytes 786440 | tf_op jit(solution)/shard_map/ppermute | solution.py:349
  9.3 0.5 collective-permute-start.6
  9.8 3.7 %shard_map.138 = (f32[8,128,128]{2,1,0:T(8,128)}, f32[8,128,128]{2,1,0:T(8,128)}, f32[8,128,128]{2,1,0:T(8,128)}) custom-call(s32[1,16]{1,0:T(1,128)} %refs_0_.9, s32[1,16]{1,0:T(1,128)} %refs_1_.9, s32[6,1,8]{2,1,0:T(1,128)} %bitcast.34, s32[6,1,8]{2,1,0:T(1,128)} %bitcast.39, bf16[16,128,128]{2,1,0:T(8,128)(2,1)} %bitcast.20, ...), custom_call_target="tpu_custom_call" | custom-call | flops 1 | bytes 1 | tf_op jit(solution)/shard_map/pallas_call | solution.py:214
  13.6 1.6 %collective-permute-done.7 = bf16[8,128,128]{2,1,0:T(8,128)(2,1)S(1)} collective-permute-done((bf16[8,128,128]{2,1,0:T(8,128)(2,1)}, bf16[8,128,128]{2,1,0:T(8,128)(2,1)S(1)}, u32[]{:S(2)}, u32[]{:S(2)}) %collective-permute-start.7) | collective-permute-done | bytes 262176 | tf_op jit(solution)/shard_map/ppermute | solution.py:349
  15.2 1.1 add_convert_fusion.1
  16.3 2.2 %collective-permute-start.8 = (bf16[8,128,128]{2,1,0:T(8,128)(2,1)S(1)}, bf16[8,128,128]{2,1,0:T(8,128)(2,1)S(1)}, u32[]{:S(2)}, u32[]{:S(2)}) collective-permute-start(bf16[8,128,128]{2,1,0:T(8,128)(2,1)S(1)} %add_convert_fusion.1), channel_id=1, source_target_pairs={{0,8},{4,12},{8,0},{12,4},{16,24},{20,28},{24,16},{28,20},{1,9},{5... | collective-permute-start | bytes 786440 | tf_op jit(solution)/shard_map/ppermute | solution.py:349
  18.5 1.5 %collective-permute-start = (bf16[8,128,128]{2,1,0:T(8,128)(2,1)}, bf16[8,128,128]{2,1,0:T(8,128)(2,1)S(1)}, u32[]{:S(2)}, u32[]{:S(2)}) collective-permute-start(bf16[8,128,128]{2,1,0:T(8,128)(2,1)} %get-tuple-element.65), channel_id=1, source_target_pairs={{0,4},{4,0},{8,12},{12,8},{16,20},{20,16},{24,28},{28,24},{1,5},{5... | collective-permute-start | bytes 786440 | tf_op jit(solution)/shard_map/ppermute | solution.py:349
  20.0 0.8 collective-permute-done.6
  20.8 2.2 %collective-permute-done.8 = bf16[8,128,128]{2,1,0:T(8,128)(2,1)S(1)} collective-permute-done((bf16[8,128,128]{2,1,0:T(8,128)(2,1)S(1)}, bf16[8,128,128]{2,1,0:T(8,128)(2,1)S(1)}, u32[]{:S(2)}, u32[]{:S(2)}) %collective-permute-start.8) | collective-permute-done | bytes 262176 | tf_op jit(solution)/shard_map/ppermute | solution.py:349
  23.0 1.1 add_convert_fusion
  24.2 2.9 %collective-permute-start.9 = (bf16[8,128,128]{2,1,0:T(8,128)(2,1)S(1)}, bf16[8,128,128]{2,1,0:T(8,128)(2,1)S(1)}, u32[]{:S(2)}, u32[]{:S(2)}) collective-permute-start(bf16[8,128,128]{2,1,0:T(8,128)(2,1)S(1)} %add_convert_fusion), channel_id=1, source_target_pairs={{0,16},{4,20},{8,24},{12,28},{16,0},{20,4},{24,8},{28,12},{1,17},{... | collective-permute-start | bytes 786440 | tf_op jit(solution)/shard_map/ppermute | solution.py:349
  27.1 0.5 collective-permute-start.1
  27.6 1.5 %collective-permute-start.2 = (bf16[2,2,128,128]{3,2,1,0:T(8,128)(2,1)S(1)}, bf16[2,2,128,128]{3,2,1,0:T(8,128)(2,1)S(1)}, u32[]{:S(2)}, u32[]{:S(2)}) collective-permute-start(bf16[2,2,128,128]{3,2,1,0:T(8,128)(2,1)S(1)} %copy-done.17), channel_id=1, source_target_pairs={{0,2},{1,3},{2,0},{3,1},{4,6},{5,7},{6,4},{7,5},{8,10},{9,11},{10,... | collective-permute-start | bytes 393224 | tf_op jit(solution)/shard_map/ppermute | solution.py:349
  29.1 1.5 %collective-permute-start.11 = (bf16[8,128,128]{2,1,0:T(8,128)(2,1)}, bf16[8,128,128]{2,1,0:T(8,128)(2,1)}, u32[]{:S(2)}, u32[]{:S(2)}) collective-permute-start(bf16[8,128,128]{2,1,0:T(8,128)(2,1)} %get-tuple-element.78), channel_id=1, source_target_pairs={{0,4},{4,0},{8,12},{12,8},{16,20},{20,16},{24,28},{28,24},{1,5},{5... | collective-permute-start | bytes 786440 | tf_op jit(solution)/shard_map/ppermute | solution.py:349
  30.6 0.8 add_convert_fusion.2
  31.4 5.0 %collective-permute-done.9.refs_2_ = bf16[8,128,128]{2,1,0:T(8,128)(2,1)S(1)} collective-permute-done((bf16[8,128,128]{2,1,0:T(8,128)(2,1)S(1)}, bf16[8,128,128]{2,1,0:T(8,128)(2,1)S(1)}, u32[]{:S(2)}, u32[]{:S(2)}) %collective-permute-start.9) | collective-permute-done | bytes 262176 | tf_op jit(solution)/shard_map/ppermute | solution.py:349
  36.4 0.5 collective-permute-start.12
  36.8 0.7 copy-done.7
  37.5 0.7 copy-done.9
  38.2 1.6 %collective-permute-start.3 = (bf16[2,2,128,128]{3,2,1,0:T(8,128)(2,1)}, bf16[2,2,128,128]{3,2,1,0:T(8,128)(2,1)}, u32[]{:S(2)}, u32[]{:S(2)}) collective-permute-start(bf16[2,2,128,128]{3,2,1,0:T(8,128)(2,1)} %get-tuple-element.70), channel_id=1, source_target_pairs={{0,3},{1,2},{2,1},{3,0},{4,7},{5,6},{6,5},{7,4},{8,11},{9,10},{10,... | collective-permute-start | bytes 393224 | tf_op jit(solution)/shard_map/ppermute | solution.py:349
  39.8 0.2 copy.15.inv_ref
  40.0 3.3 %shard_map.140.keep_ref = f32[8,128,128]{2,1,0:T(8,128)} custom-call(s32[1,16]{1,0:T(1,128)} %refs_0_.9, s32[1,16]{1,0:T(1,128)} %refs_1_.9, s32[6,1,8]{2,1,0:T(1,128)} %bitcast.35, s32[6,1,8]{2,1,0:T(1,128)} %bitcast.40, bf16[16,128,128]{2,1,0:T(8,128)(2,1)} %bitcast.21, bf16[6,8,128,128]{3,2,1,0:T(8,128)(2,1)} %bitcast.16, bf16[8,128,128]{2,1,0:T(8,128)(2,1)} %bitcast.26), custom_call_target="tpu_custom_call" | custom-call | flops 1 | bytes 1 | tf_op jit(solution)/shard_map/pallas_call | solution.py:214
  43.3 0.3 collective-permute-done.3.refs_7_
  43.6 0.4 collective-permute-done.12.refs_1_
  44.0 1.0 copy-done.3
  45.1 1.3 %shard_map.141 = (bf16[8,128,128]{2,1,0:T(8,128)(2,1)S(1)}, bf16[2,128,128]{2,1,0:T(8,128)(2,1)S(1)}, bf16[2,128,128]{2,1,0:T(8,128)(2,1)S(1)}, bf16[2,128,128]{2,1,0:T(8,128)(2,1)S(1)}, bf16[2,128,128]{2,1,0:T(8,128)(2,1)S(1)}) custom-call(f32[8,128,1]{2,1,0:T(8,128)S(1)} %copy.15.inv_ref, f32[8,128,128]{2,1,0:T(8,128)S(1)} %copy-done.3, ...), custom_call_target="tpu_custom_call" | custom-call | flops 1 | bytes 1 | tf_op jit(solution)/shard_map/pallas_call | solution.py:233
  46.4 0.2 collective-permute-start.13
  46.6 1.4 %collective-permute-start.14 = (bf16[2,128,128]{2,1,0:T(8,128)(2,1)S(1)}, bf16[2,128,128]{2,1,0:T(8,128)(2,1)S(1)}, u32[]{:S(2)}, u32[]{:S(2)}) collective-permute-start(bf16[2,128,128]{2,1,0:T(8,128)(2,1)S(1)} %get-tuple-element.93), channel_id=1, source_target_pairs={{0,2},{1,3},{2,0},{3,1},{4,6},{5,7},{6,4},{7,5},{8,10},{9,11},{10,... | collective-permute-start | bytes 196616 | tf_op jit(solution)/shard_map/ppermute | solution.py:349
  48.1 0.3 collective-permute-start.15
  48.4 0.1 copy.16.inv_ref
  48.6 2.4 %collective-permute-done.14.refs_10_ = bf16[2,128,128]{2,1,0:T(8,128)(2,1)S(1)} collective-permute-done((bf16[2,128,128]{2,1,0:T(8,128)(2,1)S(1)}, bf16[2,128,128]{2,1,0:T(8,128)(2,1)S(1)}, u32[]{:S(2)}, u32[]{:S(2)}) %collective-permute-start.14) | collective-permute-done | bytes 65568 | tf_op jit(solution)/shard_map/ppermute | solution.py:349
  51.0 1.4 %collective-permute-done.15.refs_11_ = bf16[2,128,128]{2,1,0:T(8,128)(2,1)S(1)} collective-permute-done((bf16[2,128,128]{2,1,0:T(8,128)(2,1)S(1)}, bf16[2,128,128]{2,1,0:T(8,128)(2,1)S(1)}, u32[]{:S(2)}, u32[]{:S(2)}) %collective-permute-start.15) | collective-permute-done | bytes 65568 | tf_op jit(solution)/shard_map/ppermute | solution.py:349
  52.5 2.2 %shard_map.142 = (bf16[5,256,128]{2,1,0:T(8,128)(2,1)S(1)}, bf16[5,256,128]{2,1,0:T(8,128)(2,1)S(1)}, bf16[5,256,128]{2,1,0:T(8,128)(2,1)S(1)}, bf16[256,128]{1,...) custom-call(f32[256,1]{1,0:T(8,128)S(1)} %copy.16.inv_ref, ...), custom_call_target="tpu_custom_call" | custom-call | flops 1 | bytes 1 | tf_op jit(solution)/shard_map/pallas_call | solution.py:233
  54.6 0.8 collective-permute-start.18
  55.4 1.0 collective-permute-start.17
  56.4 0.2 collective-permute-start.16
  56.6 2.2 %collective-permute-done.18 = bf16[256,128]{1,0:T(8,128)(2,1)S(1)} collective-permute-done((bf16[256,128]{1,0:T(8,128)(2,1)S(1)}, bf16[256,128]{1,0:T(8,128)(2,1)S(1)}, u32[]{:S(2)}, u32[]{:S(2)}) %collective-permute-start.18) | collective-permute-done | bytes 65568 | tf_op jit(solution)/shard_map/ppermute | solution.py:349
  58.8 1.7 %collective-permute-done.17 = bf16[256,128]{1,0:T(8,128)(2,1)S(1)} collective-permute-done((bf16[256,128]{1,0:T(8,128)(2,1)S(1)}, bf16[256,128]{1,0:T(8,128)(2,1)S(1)}, u32[]{:S(2)}, u32[]{:S(2)}) %collective-permute-start.17) | collective-permute-done | bytes 65568 | tf_op jit(solution)/shard_map/ppermute | solution.py:349
  60.5 3.4 %collective-permute-start.19 = (bf16[8,128,128]{2,1,0:T(8,128)(2,1)S(1)}, bf16[8,128,128]{2,1,0:T(8,128)(2,1)S(1)}, u32[]{:S(2)}, u32[]{:S(2)}) collective-permute-start(bf16[8,128,128]{2,1,0:T(8,128)(2,1)S(1)} %bitcast.27), channel_id=1, source_target_pairs={{0,16},{4,20},{8,24},{12,28},{16,0},{20,4},{24,8},{28,12},{1,17},{... | collective-permute-start | bytes 786440 | tf_op jit(solution)/shard_map/ppermute | solution.py:349
  64.0 1.5 %collective-permute-start.21 = (bf16[8,128,128]{2,1,0:T(8,128)(2,1)S(1)}, bf16[8,128,128]{2,1,0:T(8,128)(2,1)S(1)}, u32[]{:S(2)}, u32[]{:S(2)}) collective-permute-start(bf16[8,128,128]{2,1,0:T(8,128)(2,1)S(1)} %bitcast.29), channel_id=1, source_target_pairs={{0,4},{4,0},{8,12},{12,8},{16,20},{20,16},{24,28},{28,24},{1,5},{5... | collective-permute-start | bytes 786440 | tf_op jit(solution)/shard_map/ppermute | solution.py:349
  65.5 0.9 collective-permute-start.23
  66.4 9.6 %collective-permute-done.19.refs_6_ = bf16[8,128,128]{2,1,0:T(8,128)(2,1)S(1)} collective-permute-done((bf16[8,128,128]{2,1,0:T(8,128)(2,1)S(1)}, bf16[8,128,128]{2,1,0:T(8,128)(2,1)S(1)}, u32[]{:S(2)}, u32[]{:S(2)}) %collective-permute-start.19) | collective-permute-done | bytes 262176 | tf_op jit(solution)/shard_map/ppermute | solution.py:349
  76.0 1.3 %collective-permute-done.20.refs_8_ = bf16[8,128,128]{2,1,0:T(8,128)(2,1)S(1)} collective-permute-done((bf16[8,128,128]{2,1,0:T(8,128)(2,1)S(1)}, bf16[8,128,128]{2,1,0:T(8,128)(2,1)S(1)}, u32[]{:S(2)}, u32[]{:S(2)}) %collective-permute-start.20) | collective-permute-done | bytes 262176 | tf_op jit(solution)/shard_map/ppermute | solution.py:349
  77.3 2.4 %collective-permute-done.24.refs_3_ = bf16[5,256,128]{2,1,0:T(8,128)(2,1)S(1)} collective-permute-done((bf16[5,256,128]{2,1,0:T(8,128)(2,1)S(1)}, bf16[5,256,128]{2,1,0:T(8,128)(2,1)S(1)}, u32[]{:S(2)}, u32[]{:S(2)}) %collective-permute-start.24) | collective-permute-done | bytes 327712 | tf_op jit(solution)/shard_map/ppermute | solution.py:349
  79.7 0.8 shard_map.143
  80.5 0.8 collective-permute-start.25
  81.3 1.3 %collective-permute-start.26 = (bf16[8,128,128]{2,1,0:T(8,128)(2,1)S(1)}, bf16[8,128,128]{2,1,0:T(8,128)(2,1)S(1)}, u32[]{:S(2)}, u32[]{:S(2)}) collective-permute-start(bf16[8,128,128]{2,1,0:T(8,128)(2,1)S(1)} %collective-permute-done.20.refs_8_), channel_id=1, source_target_pairs={{0,4},{4,0},{8,12},{12,8},{16,20},{20,16},{24,28},{28,24},{1,5},{5... | collective-permute-start | bytes 786440 | tf_op jit(solution)/shard_map/ppermute | solution.py:349
  82.6 1.5 %collective-permute-start.27 = (bf16[8,128,128]{2,1,0:T(8,128)(2,1)S(1)}, bf16[8,128,128]{2,1,0:T(8,128)(2,1)S(1)}, u32[]{:S(2)}, u32[]{:S(2)}) collective-permute-start(bf16[8,128,128]{2,1,0:T(8,128)(2,1)S(1)} %collective-permute-done.19.refs_6_), channel_id=1, source_target_pairs={{0,8},{4,12},{8,0},{12,4},{16,24},{20,28},{24,16},{28,20},{1,9},{5... | collective-permute-start | bytes 786440 | tf_op jit(solution)/shard_map/ppermute | solution.py:349
  84.1 2.3 %collective-permute-done.25 = bf16[4,32,512]{2,1,0:T(8,128)(2,1)S(1)} collective-permute-done((bf16[4,32,512]{2,1,0:T(8,128)(2,1)S(1)}, bf16[4,32,512]{2,1,0:T(8,128)(2,1)S(1)}, u32[]{:S(2)}, u32[]{:S(2)}) %collective-permute-start.25) | collective-permute-done | bytes 131104 | tf_op jit(solution)/shard_map/ppermute | solution.py:349
  86.5 5.6 %collective-permute-done.26.refs_9_ = bf16[8,128,128]{2,1,0:T(8,128)(2,1)S(1)} collective-permute-done((bf16[8,128,128]{2,1,0:T(8,128)(2,1)S(1)}, bf16[8,128,128]{2,1,0:T(8,128)(2,1)S(1)}, u32[]{:S(2)}, u32[]{:S(2)}) %collective-permute-start.26) | collective-permute-done | bytes 262176 | tf_op jit(solution)/shard_map/ppermute | solution.py:349
  92.0 1.3 %collective-permute-start.28 = (bf16[4,32,512]{2,1,0:T(8,128)(2,1)S(1)}, bf16[4,32,512]{2,1,0:T(8,128)(2,1)S(1)}, u32[]{:S(2)}, u32[]{:S(2)}) collective-permute-start(bf16[4,32,512]{2,1,0:T(8,128)(2,1)S(1)} %add_convert_fusion.5), channel_id=1, source_target_pairs={{0,8},{4,12},{8,0},{12,4},{16,24},{20,28},{24,16},{28,20},{1,9},{5... | collective-permute-start | bytes 393224 | tf_op jit(solution)/shard_map/ppermute | solution.py:349
  93.3 0.5 collective-permute-start.29
  93.8 4.0 %collective-permute-done.28 = bf16[4,32,512]{2,1,0:T(8,128)(2,1)S(1)} collective-permute-done((bf16[4,32,512]{2,1,0:T(8,128)(2,1)S(1)}, bf16[4,32,512]{2,1,0:T(8,128)(2,1)S(1)}, u32[]{:S(2)}, u32[]{:S(2)}) %collective-permute-start.28) | collective-permute-done | bytes 131104 | tf_op jit(solution)/shard_map/ppermute | solution.py:349
  97.8 4.0 %collective-permute-done.29.refs_7_ = bf16[8,128,128]{2,1,0:T(8,128)(2,1)S(1)} collective-permute-done((bf16[8,128,128]{2,1,0:T(8,128)(2,1)S(1)}, bf16[8,128,128]{2,1,0:T(8,128)(2,1)S(1)}, u32[]{:S(2)}, u32[]{:S(2)}) %collective-permute-start.29) | collective-permute-done | bytes 262176 | tf_op jit(solution)/shard_map/ppermute | solution.py:349
  101.8 0.6 collective-permute-start.30
  102.4 0.5 collective-permute-start.31
  103.0 0.7 shard_map.144
  103.7 6.4 %collective-permute-done.30 = bf16[4,32,512]{2,1,0:T(8,128)(2,1)S(1)} collective-permute-done((bf16[4,32,512]{2,1,0:T(8,128)(2,1)S(1)}, bf16[4,32,512]{2,1,0:T(8,128)(2,1)S(1)}, u32[]{:S(2)}, u32[]{:S(2)}) %collective-permute-start.30) | collective-permute-done | bytes 131104 | tf_op jit(solution)/shard_map/ppermute | solution.py:349
  110.2 0.6 collective-permute-start.32
  110.8 2.3 %shard_map.145.refs_10_ = f32[8,128,128]{2,1,0:T(8,128)S(1)} custom-call(s32[1,16]{1,0:T(1,128)S(1)} %copy-done.13, s32[1,16]{1,0:T(1,128)S(1)} %copy-done.14, s32[6,1,8]{2,1,0:T(1,128)S(1)} %bitcast.36, s32[6,1,8]{2,1,0:T(1,128)S(1)} %bitcast.41, bf16[16,128,128]{2,1,0:T(8,128)(2,1)S(1)} %bitcast.22, bf16[6,8,128,128]{3,2,1,0:T(8,128)(2,1)S(1)} %bitcast.17, ...), custom_call_target="tpu_custom_call" | custom-call | flops 1 | bytes 1 | tf_op jit(solution)/shard_map/pallas_call | solution.py:214
  113.1 2.8 %shard_map.146 = f32[8,128,128]{2,1,0:T(8,128)} custom-call(s32[1,16]{1,0:T(1,128)S(1)} %copy-done.13, s32[1,16]{1,0:T(1,128)S(1)} %copy-done.14, s32[6,1,8]{2,1,0:T(1,128)S(1)} %bitcast.37, s32[6,1,8]{2,1,0:T(1,128)S(1)} %bitcast.42, bf16[16,128,128]{2,1,0:T(8,128)(2,1)S(1)} %bitcast.23, bf16[6,8,128,128]{3,2,1,0:T(8,128)(2,1)S(1)} %bitcast.18, ...), custom_call_target="tpu_custom_call" | custom-call | flops 1 | bytes 1 | tf_op jit(solution)/shard_map/pallas_call | solution.py:214
  115.9 0.9 shard_map.147
  (61 shorter events, 0.3 us)
Async XLA Ops:
  4.8 10.4 %collective-permute-start.7 = (bf16[8,128,128]{2,1,0:T(8,128)(2,1)}, bf16[8,128,128]{2,1,0:T(8,128)(2,1)S(1)}, u32[]{:S(2)}, u32[]{:S(2)}) collective-permute-start(bf16[8,128,128]{2,1,0:T(8,128)(2,1)} %get-tuple-element.76), channel_id=1, source_target_pairs={{0,4},{4,0},{8,12},{12,8},{16,20},{20,16},{24,28},{28,24},{1,5},{5... | collective-permute-start | bytes 786440 | tf_op jit(solution)/shard_map/ppermute | solution.py:349
  7.8 12.2 %collective-permute-start.5 = (bf16[2,128,512]{2,1,0:T(8,128)(2,1)}, bf16[2,128,512]{2,1,0:T(8,128)(2,1)S(1)}, u32[]{:S(2)}, u32[]{:S(2)}) collective-permute-start(bf16[2,128,512]{2,1,0:T(8,128)(2,1)} %get-tuple-element.83.refs_0_), channel_id=1, source_target_pairs={{0,2},{1,3},{2,0},{3,1},{4,6},{5,7},{6,4},{7,5},{8,10},{9,11},{10,... | collective-permute-start | bytes 786440 | tf_op jit(solution)/shard_map/ppermute | solution.py:349
  9.3 11.5 %collective-permute-start.6 = (bf16[8,128,128]{2,1,0:T(8,128)(2,1)}, bf16[8,128,128]{2,1,0:T(8,128)(2,1)S(1)}, u32[]{:S(2)}, u32[]{:S(2)}) collective-permute-start(bf16[8,128,128]{2,1,0:T(8,128)(2,1)} %get-tuple-element.73), channel_id=1, source_target_pairs={{0,4},{4,0},{8,12},{12,8},{16,20},{20,16},{24,28},{28,24},{1,5},{5... | collective-permute-start | bytes 786440 | tf_op jit(solution)/shard_map/ppermute | solution.py:349
  13.5 13.6 %copy-start.5 = (bf16[2,128,512]{2,1,0:T(8,128)(2,1)S(1)}, bf16[2,128,512]{2,1,0:T(8,128)(2,1)}, u32[]{:S(2)}) copy-start(bf16[2,128,512]{2,1,0:T(8,128)(2,1)} %get-tuple-element.83.refs_0_) | copy-start | bytes 786436
  13.5 13.6 %copy-start.18 = (bf16[2,2,128,128]{3,2,1,0:T(8,128)(2,1)S(1)}, bf16[2,2,128,128]{3,2,1,0:T(8,128)(2,1)}, u32[]{:S(2)}) copy-start(bf16[2,2,128,128]{3,2,1,0:T(8,128)(2,1)} %get-tuple-element.68) | copy-start | bytes 393220
  13.5 14.1 %copy-start.17 = (bf16[2,2,128,128]{3,2,1,0:T(8,128)(2,1)S(1)}, bf16[2,2,128,128]{3,2,1,0:T(8,128)(2,1)}, u32[]{:S(2)}) copy-start(bf16[2,2,128,128]{3,2,1,0:T(8,128)(2,1)} %get-tuple-element.69) | copy-start | bytes 393220
  13.5 17.1 %copy-start.15 = (f32[8,128,128]{2,1,0:T(8,128)S(1)}, f32[8,128,128]{2,1,0:T(8,128)}, u32[]{:S(2)}) copy-start(f32[8,128,128]{2,1,0:T(8,128)} %get-tuple-element.64) | copy-start | bytes 1572868
  15.2 24.6 %copy-start.16 = (s32[1024]{0:T(1024)S(1)}, s32[1024]{0:T(1024)}, u32[]{:S(2)}) copy-start(s32[1024]{0:T(1024)} %param.14) | copy-start | bytes 12292
  16.3 6.7 %collective-permute-start.8 = (bf16[8,128,128]{2,1,0:T(8,128)(2,1)S(1)}, bf16[8,128,128]{2,1,0:T(8,128)(2,1)S(1)}, u32[]{:S(2)}, u32[]{:S(2)}) collective-permute-start(bf16[8,128,128]{2,1,0:T(8,128)(2,1)S(1)} %add_convert_fusion.1), channel_id=1, source_target_pairs={{0,8},{4,12},{8,0},{12,4},{16,24},{20,28},{24,16},{28,20},{1,9},{5... | collective-permute-start | bytes 786440 | tf_op jit(solution)/shard_map/ppermute | solution.py:349
  18.5 10.6 %collective-permute-start = (bf16[8,128,128]{2,1,0:T(8,128)(2,1)}, bf16[8,128,128]{2,1,0:T(8,128)(2,1)S(1)}, u32[]{:S(2)}, u32[]{:S(2)}) collective-permute-start(bf16[8,128,128]{2,1,0:T(8,128)(2,1)} %get-tuple-element.65), channel_id=1, source_target_pairs={{0,4},{4,0},{8,12},{12,8},{16,20},{20,16},{24,28},{28,24},{1,5},{5... | collective-permute-start | bytes 786440 | tf_op jit(solution)/shard_map/ppermute | solution.py:349
  24.2 12.2 %collective-permute-start.9 = (bf16[8,128,128]{2,1,0:T(8,128)(2,1)S(1)}, bf16[8,128,128]{2,1,0:T(8,128)(2,1)S(1)}, u32[]{:S(2)}, u32[]{:S(2)}) collective-permute-start(bf16[8,128,128]{2,1,0:T(8,128)(2,1)S(1)} %add_convert_fusion), channel_id=1, source_target_pairs={{0,16},{4,20},{8,24},{12,28},{16,0},{20,4},{24,8},{28,12},{1,17},{... | collective-permute-start | bytes 786440 | tf_op jit(solution)/shard_map/ppermute | solution.py:349
  27.1 16.6 %collective-permute-start.4 = (bf16[2,128,512]{2,1,0:T(8,128)(2,1)S(1)}, bf16[2,128,512]{2,1,0:T(8,128)(2,1)S(1)}, u32[]{:S(2)}, u32[]{:S(2)}) collective-permute-start(bf16[2,128,512]{2,1,0:T(8,128)(2,1)S(1)} %copy-done.5), channel_id=1, source_target_pairs={{0,1},{1,0},{2,3},{3,2},{4,5},{5,4},{6,7},{7,6},{8,9},{9,8},{10,11... | collective-permute-start | bytes 786440 | tf_op jit(solution)/shard_map/ppermute | solution.py:349
  27.1 9.8 %collective-permute-start.1 = (bf16[2,2,128,128]{3,2,1,0:T(8,128)(2,1)S(1)}, bf16[2,2,128,128]{3,2,1,0:T(8,128)(2,1)S(1)}, u32[]{:S(2)}, u32[]{:S(2)}) collective-permute-start(bf16[2,2,128,128]{3,2,1,0:T(8,128)(2,1)S(1)} %copy-done.18), channel_id=1, source_target_pairs={{0,1},{1,0},{2,3},{3,2},{4,5},{5,4},{6,7},{7,6},{8,9},{9,8},{10,11... | collective-permute-start | bytes 393224 | tf_op jit(solution)/shard_map/ppermute | solution.py:349
  27.6 9.9 %collective-permute-start.2 = (bf16[2,2,128,128]{3,2,1,0:T(8,128)(2,1)S(1)}, bf16[2,2,128,128]{3,2,1,0:T(8,128)(2,1)S(1)}, u32[]{:S(2)}, u32[]{:S(2)}) collective-permute-start(bf16[2,2,128,128]{3,2,1,0:T(8,128)(2,1)S(1)} %copy-done.17), channel_id=1, source_target_pairs={{0,2},{1,3},{2,0},{3,1},{4,6},{5,7},{6,4},{7,5},{8,10},{9,11},{10,... | collective-permute-start | bytes 393224 | tf_op jit(solution)/shard_map/ppermute | solution.py:349
  29.1 14.5 %collective-permute-start.11 = (bf16[8,128,128]{2,1,0:T(8,128)(2,1)}, bf16[8,128,128]{2,1,0:T(8,128)(2,1)}, u32[]{:S(2)}, u32[]{:S(2)}) collective-permute-start(bf16[8,128,128]{2,1,0:T(8,128)(2,1)} %get-tuple-element.78), channel_id=1, source_target_pairs={{0,4},{4,0},{8,12},{12,8},{16,20},{20,16},{24,28},{28,24},{1,5},{5... | collective-permute-start | bytes 786440 | tf_op jit(solution)/shard_map/ppermute | solution.py:349
  36.4 7.7 %collective-permute-start.12 = (bf16[8,128,128]{2,1,0:T(8,128)(2,1)}, bf16[8,128,128]{2,1,0:T(8,128)(2,1)}, u32[]{:S(2)}, u32[]{:S(2)}) collective-permute-start(bf16[8,128,128]{2,1,0:T(8,128)(2,1)} %add_convert_fusion.2), channel_id=1, source_target_pairs={{0,8},{4,12},{8,0},{12,4},{16,24},{20,28},{24,16},{28,20},{1,9},{5... | collective-permute-start | bytes 786440 | tf_op jit(solution)/shard_map/ppermute | solution.py:349
  36.8 0.7 copy-start.7
  37.5 6.5 %collective-permute-start.10 = (bf16[2,128,512]{2,1,0:T(8,128)(2,1)S(1)}, bf16[2,128,512]{2,1,0:T(8,128)(2,1)S(1)}, u32[]{:S(2)}, u32[]{:S(2)}) collective-permute-start(bf16[2,128,512]{2,1,0:T(8,128)(2,1)S(1)} %collective-permute-done.5.refs_2_), channel_id=1, source_target_pairs={{0,1},{1,0},{2,3},{3,2},{4,5},{5,4},{6,7},{7,6},{8,9},{9,8},{10,11... | collective-permute-start | bytes 786440 | tf_op jit(solution)/shard_map/ppermute | solution.py:349
  37.5 0.7 copy-start.9
  38.2 5.5 %collective-permute-start.3 = (bf16[2,2,128,128]{3,2,1,0:T(8,128)(2,1)}, bf16[2,2,128,128]{3,2,1,0:T(8,128)(2,1)}, u32[]{:S(2)}, u32[]{:S(2)}) collective-permute-start(bf16[2,2,128,128]{3,2,1,0:T(8,128)(2,1)} %get-tuple-element.70), channel_id=1, source_target_pairs={{0,3},{1,2},{2,1},{3,0},{4,7},{5,6},{6,5},{7,4},{8,11},{9,10},{10,... | collective-permute-start | bytes 393224 | tf_op jit(solution)/shard_map/ppermute | solution.py:349
  40.0 12.4 %copy-start.6 = (bf16[2,2,128,128]{3,2,1,0:T(8,128)(2,1)S(1)}, bf16[2,2,128,128]{3,2,1,0:T(8,128)(2,1)}, u32[]{:S(2)}) copy-start(bf16[2,2,128,128]{3,2,1,0:T(8,128)(2,1)} %get-tuple-element.87.refs_4_) | copy-start | bytes 393220
  44.0 1.0 copy-start.3
  45.1 7.4 %copy-start.8 = (bf16[2,2,128,128]{3,2,1,0:T(8,128)(2,1)S(1)}, bf16[2,2,128,128]{3,2,1,0:T(8,128)(2,1)}, u32[]{:S(2)}) copy-start(bf16[2,2,128,128]{3,2,1,0:T(8,128)(2,1)} %copy-done.7) | copy-start | bytes 393220
  45.1 7.4 %copy-start.10 = (bf16[2,2,128,128]{3,2,1,0:T(8,128)(2,1)S(1)}, bf16[2,2,128,128]{3,2,1,0:T(8,128)(2,1)}, u32[]{:S(2)}) copy-start(bf16[2,2,128,128]{3,2,1,0:T(8,128)(2,1)} %copy-done.9) | copy-start | bytes 393220
  46.4 33.3 %copy-start.2 = (bf16[1024,128]{1,0:T(8,128)(2,1)S(1)}, bf16[1024,128]{1,0:T(8,128)(2,1)}, u32[]{:S(2)}) copy-start(bf16[1024,128]{1,0:T(8,128)(2,1)} %f_ref.1) | copy-start | bytes 786436
  46.4 33.2 %copy-start.4 = (bf16[128,512]{1,0:T(8,128)(2,1)S(1)}, bf16[128,512]{1,0:T(8,128)(2,1)}, u32[]{:S(2)}) copy-start(bf16[128,512]{1,0:T(8,128)(2,1)} %w_ref.1) | copy-start | bytes 393220
  46.4 2.1 %collective-permute-start.13 = (bf16[2,128,128]{2,1,0:T(8,128)(2,1)S(1)}, bf16[2,128,128]{2,1,0:T(8,128)(2,1)S(1)}, u32[]{:S(2)}, u32[]{:S(2)}) collective-permute-start(bf16[2,128,128]{2,1,0:T(8,128)(2,1)S(1)} %get-tuple-element.92), channel_id=1, source_target_pairs={{0,1},{1,0},{2,3},{3,2},{4,5},{5,4},{6,7},{7,6},{8,9},{9,8},{10,11... | collective-permute-start | bytes 196616 | tf_op jit(solution)/shard_map/ppermute | solution.py:349
  46.6 4.4 %collective-permute-start.14 = (bf16[2,128,128]{2,1,0:T(8,128)(2,1)S(1)}, bf16[2,128,128]{2,1,0:T(8,128)(2,1)S(1)}, u32[]{:S(2)}, u32[]{:S(2)}) collective-permute-start(bf16[2,128,128]{2,1,0:T(8,128)(2,1)S(1)} %get-tuple-element.93), channel_id=1, source_target_pairs={{0,2},{1,3},{2,0},{3,1},{4,6},{5,7},{6,4},{7,5},{8,10},{9,11},{10,... | collective-permute-start | bytes 196616 | tf_op jit(solution)/shard_map/ppermute | solution.py:349
  48.1 4.4 %collective-permute-start.15 = (bf16[2,128,128]{2,1,0:T(8,128)(2,1)S(1)}, bf16[2,128,128]{2,1,0:T(8,128)(2,1)S(1)}, u32[]{:S(2)}, u32[]{:S(2)}) collective-permute-start(bf16[2,128,128]{2,1,0:T(8,128)(2,1)S(1)} %get-tuple-element.94), channel_id=1, source_target_pairs={{0,3},{1,2},{2,1},{3,0},{4,7},{5,6},{6,5},{7,4},{8,11},{9,10},{10,... | collective-permute-start | bytes 196616 | tf_op jit(solution)/shard_map/ppermute | solution.py:349
  54.6 4.2 %collective-permute-start.18 = (bf16[256,128]{1,0:T(8,128)(2,1)S(1)}, bf16[256,128]{1,0:T(8,128)(2,1)S(1)}, u32[]{:S(2)}, u32[]{:S(2)}) collective-permute-start(bf16[256,128]{1,0:T(8,128)(2,1)S(1)} %get-tuple-element.101), channel_id=1, source_target_pairs={{0,3},{1,2},{2,1},{3,0},{4,7},{5,6},{6,5},{7,4},{8,11},{9,10},{10,... | collective-permute-start | bytes 196616 | tf_op jit(solution)/shard_map/ppermute | solution.py:349
  55.4 5.1 %collective-permute-start.17 = (bf16[256,128]{1,0:T(8,128)(2,1)S(1)}, bf16[256,128]{1,0:T(8,128)(2,1)S(1)}, u32[]{:S(2)}, u32[]{:S(2)}) collective-permute-start(bf16[256,128]{1,0:T(8,128)(2,1)S(1)} %get-tuple-element.100), channel_id=1, source_target_pairs={{0,2},{1,3},{2,0},{3,1},{4,6},{5,7},{6,4},{7,5},{8,10},{9,11},{10,... | collective-permute-start | bytes 196616 | tf_op jit(solution)/shard_map/ppermute | solution.py:349
  56.4 4.1 %collective-permute-start.16 = (bf16[256,128]{1,0:T(8,128)(2,1)S(1)}, bf16[256,128]{1,0:T(8,128)(2,1)S(1)}, u32[]{:S(2)}, u32[]{:S(2)}) collective-permute-start(bf16[256,128]{1,0:T(8,128)(2,1)S(1)} %get-tuple-element.99), channel_id=1, source_target_pairs={{0,1},{1,0},{2,3},{3,2},{4,5},{5,4},{6,7},{7,6},{8,9},{9,8},{10,11... | collective-permute-start | bytes 196616 | tf_op jit(solution)/shard_map/ppermute | solution.py:349
  60.5 15.5 %collective-permute-start.19 = (bf16[8,128,128]{2,1,0:T(8,128)(2,1)S(1)}, bf16[8,128,128]{2,1,0:T(8,128)(2,1)S(1)}, u32[]{:S(2)}, u32[]{:S(2)}) collective-permute-start(bf16[8,128,128]{2,1,0:T(8,128)(2,1)S(1)} %bitcast.27), channel_id=1, source_target_pairs={{0,16},{4,20},{8,24},{12,28},{16,0},{20,4},{24,8},{28,12},{1,17},{... | collective-permute-start | bytes 786440 | tf_op jit(solution)/shard_map/ppermute | solution.py:349
  64.0 13.3 %collective-permute-start.20 = (bf16[8,128,128]{2,1,0:T(8,128)(2,1)S(1)}, bf16[8,128,128]{2,1,0:T(8,128)(2,1)S(1)}, u32[]{:S(2)}, u32[]{:S(2)}) collective-permute-start(bf16[8,128,128]{2,1,0:T(8,128)(2,1)S(1)} %bitcast.28), channel_id=1, source_target_pairs={{0,8},{4,12},{8,0},{12,4},{16,24},{20,28},{24,16},{28,20},{1,9},{5... | collective-permute-start | bytes 786440 | tf_op jit(solution)/shard_map/ppermute | solution.py:349
  64.0 13.3 %collective-permute-start.21 = (bf16[8,128,128]{2,1,0:T(8,128)(2,1)S(1)}, bf16[8,128,128]{2,1,0:T(8,128)(2,1)S(1)}, u32[]{:S(2)}, u32[]{:S(2)}) collective-permute-start(bf16[8,128,128]{2,1,0:T(8,128)(2,1)S(1)} %bitcast.29), channel_id=1, source_target_pairs={{0,4},{4,0},{8,12},{12,8},{16,20},{20,16},{24,28},{28,24},{1,5},{5... | collective-permute-start | bytes 786440 | tf_op jit(solution)/shard_map/ppermute | solution.py:349
  65.5 11.8 %collective-permute-start.23 = (bf16[5,256,128]{2,1,0:T(8,128)(2,1)S(1)}, bf16[5,256,128]{2,1,0:T(8,128)(2,1)S(1)}, u32[]{:S(2)}, u32[]{:S(2)}) collective-permute-start(bf16[5,256,128]{2,1,0:T(8,128)(2,1)S(1)} %get-tuple-element.104), channel_id=1, source_target_pairs={{0,2},{1,3},{2,0},{3,1},{4,6},{5,7},{6,4},{7,5},{8,10},{9,11},{10,... | collective-permute-start | bytes 983048 | tf_op jit(solution)/shard_map/ppermute | solution.py:349
  66.4 13.2 %collective-permute-start.24 = (bf16[5,256,128]{2,1,0:T(8,128)(2,1)S(1)}, bf16[5,256,128]{2,1,0:T(8,128)(2,1)S(1)}, u32[]{:S(2)}, u32[]{:S(2)}) collective-permute-start(bf16[5,256,128]{2,1,0:T(8,128)(2,1)S(1)} %get-tuple-element.105), channel_id=1, source_target_pairs={{0,3},{1,2},{2,1},{3,0},{4,7},{5,6},{6,5},{7,4},{8,11},{9,10},{10,... | collective-permute-start | bytes 983048 | tf_op jit(solution)/shard_map/ppermute | solution.py:349
  77.3 2.4 %collective-permute-start.22 = (bf16[5,256,128]{2,1,0:T(8,128)(2,1)S(1)}, bf16[5,256,128]{2,1,0:T(8,128)(2,1)S(1)}, u32[]{:S(2)}, u32[]{:S(2)}) collective-permute-start(bf16[5,256,128]{2,1,0:T(8,128)(2,1)S(1)} %get-tuple-element.103.refs_0_), channel_id=1, source_target_pairs={{0,1},{1,0},{2,3},{3,2},{4,5},{5,4},{6,7},{7,6},{8,9},{9,8},{10,11... | collective-permute-start | bytes 983048 | tf_op jit(solution)/shard_map/ppermute | solution.py:349
  80.5 30.3 %copy-start = (bf16[1,6,8,128,128]{4,3,2,1,0:T(8,128)(2,1)S(1)}, bf16[1,6,8,128,128]{4,3,2,1,0:T(8,128)(2,1)}, u32[]{:S(2)}) copy-start(bf16[1,6,8,128,128]{4,3,2,1,0:T(8,128)(2,1)} %param.18) | copy-start | bytes 4718596
  80.5 30.3 %copy-start.1 = (bf16[1,16,128,128]{3,2,1,0:T(8,128)(2,1)S(1)}, bf16[1,16,128,128]{3,2,1,0:T(8,128)(2,1)}, u32[]{:S(2)}) copy-start(bf16[1,16,128,128]{3,2,1,0:T(8,128)(2,1)} %param.15) | copy-start | bytes 1572868
  80.5 30.3 %copy-start.11 = (s32[1,6,8]{2,0,1:T(1,128)S(1)}, s32[1,6,8]{2,0,1:T(1,128)}, u32[]{:S(2)}) copy-start(s32[1,6,8]{2,0,1:T(1,128)} %param.19) | copy-start | bytes 580
  80.5 30.3 %copy-start.12 = (s32[1,6,8]{2,0,1:T(1,128)S(1)}, s32[1,6,8]{2,0,1:T(1,128)}, u32[]{:S(2)}) copy-start(s32[1,6,8]{2,0,1:T(1,128)} %param.20) | copy-start | bytes 580
  80.5 30.3 %copy-start.13 = (s32[1,16]{1,0:T(1,128)S(1)}, s32[1,16]{1,0:T(1,128)}, u32[]{:S(2)}) copy-start(s32[1,16]{1,0:T(1,128)} %refs_0_.9) | copy-start | bytes 196
  80.5 30.3 %copy-start.14 = (s32[1,16]{1,0:T(1,128)S(1)}, s32[1,16]{1,0:T(1,128)}, u32[]{:S(2)}) copy-start(s32[1,16]{1,0:T(1,128)} %refs_1_.9) | copy-start | bytes 196
  80.5 5.9 %collective-permute-start.25 = (bf16[4,32,512]{2,1,0:T(8,128)(2,1)S(1)}, bf16[4,32,512]{2,1,0:T(8,128)(2,1)S(1)}, u32[]{:S(2)}, u32[]{:S(2)}) collective-permute-start(bf16[4,32,512]{2,1,0:T(8,128)(2,1)S(1)} %get-tuple-element.110), channel_id=1, source_target_pairs={{0,4},{4,0},{8,12},{12,8},{16,20},{20,16},{24,28},{28,24},{1,5},{5... | collective-permute-start | bytes 393224 | tf_op jit(solution)/shard_map/ppermute | solution.py:349
  81.3 10.8 %collective-permute-start.26 = (bf16[8,128,128]{2,1,0:T(8,128)(2,1)S(1)}, bf16[8,128,128]{2,1,0:T(8,128)(2,1)S(1)}, u32[]{:S(2)}, u32[]{:S(2)}) collective-permute-start(bf16[8,128,128]{2,1,0:T(8,128)(2,1)S(1)} %collective-permute-done.20.refs_8_), channel_id=1, source_target_pairs={{0,4},{4,0},{8,12},{12,8},{16,20},{20,16},{24,28},{28,24},{1,5},{5... | collective-permute-start | bytes 786440 | tf_op jit(solution)/shard_map/ppermute | solution.py:349
  82.6 9.4 %collective-permute-start.27 = (bf16[8,128,128]{2,1,0:T(8,128)(2,1)S(1)}, bf16[8,128,128]{2,1,0:T(8,128)(2,1)S(1)}, u32[]{:S(2)}, u32[]{:S(2)}) collective-permute-start(bf16[8,128,128]{2,1,0:T(8,128)(2,1)S(1)} %collective-permute-done.19.refs_6_), channel_id=1, source_target_pairs={{0,8},{4,12},{8,0},{12,4},{16,24},{20,28},{24,16},{28,20},{1,9},{5... | collective-permute-start | bytes 786440 | tf_op jit(solution)/shard_map/ppermute | solution.py:349
  92.0 5.8 %collective-permute-start.28 = (bf16[4,32,512]{2,1,0:T(8,128)(2,1)S(1)}, bf16[4,32,512]{2,1,0:T(8,128)(2,1)S(1)}, u32[]{:S(2)}, u32[]{:S(2)}) collective-permute-start(bf16[4,32,512]{2,1,0:T(8,128)(2,1)S(1)} %add_convert_fusion.5), channel_id=1, source_target_pairs={{0,8},{4,12},{8,0},{12,4},{16,24},{20,28},{24,16},{28,20},{1,9},{5... | collective-permute-start | bytes 393224 | tf_op jit(solution)/shard_map/ppermute | solution.py:349
  93.3 8.6 %collective-permute-start.29 = (bf16[8,128,128]{2,1,0:T(8,128)(2,1)S(1)}, bf16[8,128,128]{2,1,0:T(8,128)(2,1)S(1)}, u32[]{:S(2)}, u32[]{:S(2)}) collective-permute-start(bf16[8,128,128]{2,1,0:T(8,128)(2,1)S(1)} %collective-permute-done.19.refs_6_), channel_id=1, source_target_pairs={{0,4},{4,0},{8,12},{12,8},{16,20},{20,16},{24,28},{28,24},{1,5},{5... | collective-permute-start | bytes 786440 | tf_op jit(solution)/shard_map/ppermute | solution.py:349
  101.8 8.3 %collective-permute-start.30 = (bf16[4,32,512]{2,1,0:T(8,128)(2,1)S(1)}, bf16[4,32,512]{2,1,0:T(8,128)(2,1)S(1)}, u32[]{:S(2)}, u32[]{:S(2)}) collective-permute-start(bf16[4,32,512]{2,1,0:T(8,128)(2,1)S(1)} %add_convert_fusion.4), channel_id=1, source_target_pairs={{0,16},{4,20},{8,24},{12,28},{16,0},{20,4},{24,8},{28,12},{1,17},{... | collective-permute-start | bytes 393224 | tf_op jit(solution)/shard_map/ppermute | solution.py:349
  102.4 7.7 %collective-permute-start.31 = (bf16[8,128,128]{2,1,0:T(8,128)(2,1)S(1)}, bf16[8,128,128]{2,1,0:T(8,128)(2,1)S(1)}, u32[]{:S(2)}, u32[]{:S(2)}) collective-permute-start(bf16[8,128,128]{2,1,0:T(8,128)(2,1)S(1)} %collective-permute-done.27.refs_8_), channel_id=1, source_target_pairs={{0,4},{4,0},{8,12},{12,8},{16,20},{20,16},{24,28},{28,24},{1,5},{5... | collective-permute-start | bytes 786440 | tf_op jit(solution)/shard_map/ppermute | solution.py:349
  110.2 5.7 %collective-permute-start.32 = (bf16[4,32,512]{2,1,0:T(8,128)(2,1)S(1)}, bf16[4,32,512]{2,1,0:T(8,128)(2,1)S(1)}, u32[]{:S(2)}, u32[]{:S(2)}) collective-permute-start(bf16[4,32,512]{2,1,0:T(8,128)(2,1)S(1)} %add_convert_fusion.3.mine_ref), channel_id=1, source_target_pairs={{0,4},{4,0},{8,12},{12,8},{16,20},{20,16},{24,28},{28,24},{1,5},{5... | collective-permute-start | bytes 393224 | tf_op jit(solution)/shard_map/ppermute | solution.py:349

commit v7 on v6

--- a/solution.py
+++ b/solution.py
@@ -404,31 +404,30 @@
         return lax.optimization_barrier((x, others))[0]
 
     made = forward(
-        [7, 5, 3, 1],
+        [7, 3, 5, 1],
         [blocks, cotangent.reshape(shape), w_self, w_neigh],
         [like(shape, BF16)] * 4
         + [like((2, per_feat, block, width), BF16)] * feats
         + [like((2, width, full), BF16)],
     )
     sends, early_pieces, pair = made[:4], made[4:-1], made[-1]
-    keep_6, keep_4, keep_2 = forward([6, 4, 2], [blocks], [like(shape, F32)] * 3)
+    keep_6, keep_2, keep_4, keep = forward([6, 2, 4, 0], [blocks], [like(shape, F32)] * 4)
     weights = relayed(pair)
     early = [early_pieces[0]] + [crossed(early_pieces[m], m, "feat") for m in range(1, feats)]
-    near_6, near_4, near_2, near_0 = (crossed(send, near) for send in sends)
+    near_6, near_2, near_4, near_0 = (crossed(send, near) for send in sends)
     sum_6 = (keep_6 + near_6.astype(F32)).astype(BF16)
-    near_4 = tied(near_4, weights[2])
+    sum_2 = (keep_2 + near_2.astype(F32)).astype(BF16)
+    mid_0 = crossed(sum_2, 2)
+    near_4, mid_0, weights[2] = lax.optimization_barrier((near_4, mid_0, weights[2]))
     sum_4 = (keep_4 + near_4.astype(F32) + crossed(sum_6, 2).astype(F32)).astype(BF16)
     far_0 = crossed(sum_4, 4)
-    sum_2 = (keep_2 + near_2.astype(F32)).astype(BF16)
-    (keep,) = forward([0], [tied(blocks, sum_2)], [like(shape, F32)])
-    mid_0 = crossed(sum_2, 2)
-    weights[3] = crossed(tied(weights[2], far_0), 1, "feat")
-    arrived = [near_0, mid_0, far_0]
+    part = keep + mid_0.astype(F32)
+    arrived = [far_0, near_0]
     early, weights, arrived = lax.optimization_barrier((early, weights, arrived))
     agg, *agg_pieces = small_call(
         functools.partial(agg_kernel, feats),
         [like(shape, BF16)] + [like((per_feat, block, width), BF16)] * feats,
-        [inverse.reshape(nblocks, block, 1), keep, *arrived],
+        [inverse.reshape(nblocks, block, 1), part, *arrived],
     )
     agg_rows = [agg_pieces[0]] + [crossed(agg_pieces[m], m, "feat") for m in range(1, feats)]
     *sent, own_out, p0, p1, p2, p3 = small_call(
@@ -455,8 +454,8 @@
     dpre = [sent[0], *come]
     found[6] = crossed(found[4], 2)
     found[3] = crossed(found[2], near)
-    found[5] = crossed(tied(found[4], found[3]), near)
-    found[7] = crossed(tied(found[6], found[5]), near)
+    found[5] = crossed(found[1], 4)
+    found[7] = crossed(found[6], near)
     piece = 2 * width // parts_total
     dx_self, give, keep = small_call(
         functools.partial(grad_kernel, feats),
@@ -469,9 +468,8 @@
         [pltpu.VMEM((parts_total, piece, full), F32)],
     )
     total = (keep + crossed(give, near).astype(F32)).astype(BF16)
-    total = tied(total, found[3], found[6])
+    total = tied(total, found[3], found[5], found[6])
     total = (total.astype(F32) + crossed(total, 2).astype(F32)).astype(BF16)
-    total = tied(total, found[5])
     total = (total.astype(F32) + crossed(total, 4).astype(F32)).astype(BF16)
     total, out = tied((total, out), found[7])
     grad_self, grad_neigh = small_call(

time: 117 us -> 118 us (level)
  waiting for transfers between devices: 53.8 us -> 63.3 us
  Pallas kernels: 22.1 us -> 17.5 us
  local copies, waits for them, and re-layouts: 2.87 us -> 0.52 us
  starting transfers between devices: 34 us -> 32 us
    ppermute x33, waiting for transfers between devices: 53.8 us -> 63.3 us  [crossed(): lax.ppermute(x, axis, [(i, i ^ mask) for i in range(lax.axis_size(axis))])]
    pallas_call x5 -> x4, Pallas kernels: 16.2 us -> 13.7 us  [tiles_call(): pl.pallas_call(functools.partial(tiles_kernel, masks, offsets, parts_tota...]
    unnamed x38 -> x28, local copies, waits for them, and re-layouts: 2.43 us -> 0.08 us
    ppermute x33, starting transfers between devices: 34 us -> 32 us  [crossed(): lax.ppermute(x, axis, [(i, i ^ mask) for i in range(lax.axis_size(axis))])]
    pallas_call x5, Pallas kernels: 5.86 us -> 3.88 us  [small_call(): pl.pallas_call(kernel, out_shape=outs, in_specs=[VMEM] * len(arrays), out...]
  transfers between devices with their start and end apart: 33 -> 33, of which waited for: 18 -> 17; matrix products, arithmetic and copies ran while one was open for 3% -> 3% of each run, Pallas kernels for 11% -> 9%
where the time goes in v7:
time: 118 us
  waiting for transfers between devices  63.3 us (54%)
  starting transfers between devices  32 us (27%)
  Pallas kernels  17.5 us (15%)
  other arithmetic  3.23 us (3%)
    ppermute x33, waiting for transfers between devices, crossed(): lax.ppermute(x, axis, [(i, i ^ mask) for i in range(lax.axis_size(axis))])  63.3 us
    ppermute x33, starting transfers between devices, crossed(): lax.ppermute(x, axis, [(i, i ^ mask) for i in range(lax.axis_size(axis))])  32 us
    pallas_call x4, Pallas kernels, tiles_call(): pl.pallas_call(functools.partial(tiles_kernel, masks, offsets, parts_tota...  13.7 us
    pallas_call x5, Pallas kernels, small_call(): pl.pallas_call(kernel, out_shape=outs, in_specs=[VMEM] * len(arrays), out...  3.88 us
  transfers between devices with their start and end apart: 33, of which 17 were waited for; matrix products, arithmetic and copies ran while one was open for 3% of the time, Pallas kernels for 9%

profile of v7, /device:TPU:0, one launch (start us, length us, event | category | flops | bytes accessed | tf_op | source)
XLA Modules:
  0.0 117.5 jit_solution(9151947220047899087)
XLA Ops:
  0.6 4.2 %shard_map.139 = (bf16[8,128,128]{2,1,0:T(8,128)(2,1)}, bf16[8,128,128]{2,1,0:T(8,128)(2,1)}, bf16[8,128,128]{2,1,0:T(8,128)(2,1)}, bf16[8,128,128]{2,1,0:T(8,12...) custom-call(s32[1,16]{1,0:T(1,128)} %refs_0_.7, ...), custom_call_target="tpu_custom_call" | custom-call | flops 1 | bytes 1 | tf_op jit(solution)/shard_map/pallas_call | solution.py:214
  4.8 3.0 %collective-permute-start.1 = (bf16[8,128,128]{2,1,0:T(8,128)(2,1)}, bf16[8,128,128]{2,1,0:T(8,128)(2,1)S(1)}, u32[]{:S(2)}, u32[]{:S(2)}) collective-permute-start(bf16[8,128,128]{2,1,0:T(8,128)(2,1)} %get-tuple-element.64), channel_id=1, source_target_pairs={{0,4},{4,0},{8,12},{12,8},{16,20},{20,16},{24,28},{28,24},{1,5},{5... | collective-permute-start | bytes 786440 | tf_op jit(solution)/shard_map/ppermute | solution.py:349
  7.8 0.1 collective-permute-start.9
  7.9 1.9 %collective-permute-start.3 = (bf16[2,128,512]{2,1,0:T(8,128)(2,1)}, bf16[2,128,512]{2,1,0:T(8,128)(2,1)S(1)}, u32[]{:S(2)}, u32[]{:S(2)}) collective-permute-start(bf16[2,128,512]{2,1,0:T(8,128)(2,1)} %get-tuple-element.80.refs_0_), channel_id=1, source_target_pairs={{0,2},{1,3},{2,0},{3,1},{4,6},{5,7},{6,4},{7,5},{8,10},{9,11},{10,... | collective-permute-start | bytes 786440 | tf_op jit(solution)/shard_map/ppermute | solution.py:349
  9.8 1.5 %collective-permute-start = (bf16[8,128,128]{2,1,0:T(8,128)(2,1)}, bf16[8,128,128]{2,1,0:T(8,128)(2,1)S(1)}, u32[]{:S(2)}, u32[]{:S(2)}) collective-permute-start(bf16[8,128,128]{2,1,0:T(8,128)(2,1)} %get-tuple-element.62), channel_id=1, source_target_pairs={{0,4},{4,0},{8,12},{12,8},{16,20},{20,16},{24,28},{28,24},{1,5},{5... | collective-permute-start | bytes 786440 | tf_op jit(solution)/shard_map/ppermute | solution.py:349
  11.4 4.4 %shard_map.138 = (f32[8,128,128]{2,1,0:T(8,128)}, f32[8,128,128]{2,1,0:T(8,128)}, f32[8,128,128]{2,1,0:T(8,128)}, f32[8,128,128]{2,1,0:T(8,128)}) custom-call(s32[1,16]{1,0:T(1,128)} %refs_0_.7, s32[1,16]{1,0:T(1,128)} %refs_1_.7, s32[6,1,8]{2,1,0:T(1,128)} %bitcast.31, s32[6,1,8]{2,1,0:T(1,128)} %bitcast.35, bf16[16,128,128]{2,1,0:T(8,128)(2,1)} %bitcast.19, ...), custom_call_target="tpu_custom_call" | custom-call | flops 1 | bytes 1 | tf_op jit(solution)/shard_map/pallas_call | solution.py:214
  15.8 1.2 add_convert_fusion.2
  17.0 1.6 %collective-permute-start.2 = (bf16[8,128,128]{2,1,0:T(8,128)(2,1)S(1)}, bf16[8,128,128]{2,1,0:T(8,128)(2,1)S(1)}, u32[]{:S(2)}, u32[]{:S(2)}) collective-permute-start(bf16[8,128,128]{2,1,0:T(8,128)(2,1)S(1)} %add_convert_fusion.2), channel_id=1, source_target_pairs={{0,8},{4,12},{8,0},{12,4},{16,24},{20,28},{24,16},{28,20},{1,9},{5... | collective-permute-start | bytes 786440 | tf_op jit(solution)/shard_map/ppermute | solution.py:349
  18.6 2.2 %collective-permute-done.9 = bf16[8,128,128]{2,1,0:T(8,128)(2,1)S(1)} collective-permute-done((bf16[8,128,128]{2,1,0:T(8,128)(2,1)}, bf16[8,128,128]{2,1,0:T(8,128)(2,1)S(1)}, u32[]{:S(2)}, u32[]{:S(2)}) %collective-permute-start.9) | collective-permute-done | bytes 262176 | tf_op jit(solution)/shard_map/ppermute | solution.py:349
  20.8 1.1 add_convert_fusion.1
  21.9 2.2 %collective-permute-start.10 = (bf16[8,128,128]{2,1,0:T(8,128)(2,1)S(1)}, bf16[8,128,128]{2,1,0:T(8,128)(2,1)S(1)}, u32[]{:S(2)}, u32[]{:S(2)}) collective-permute-start(bf16[8,128,128]{2,1,0:T(8,128)(2,1)S(1)} %add_convert_fusion.1), channel_id=1, source_target_pairs={{0,8},{4,12},{8,0},{12,4},{16,24},{20,28},{24,16},{28,20},{1,9},{5... | collective-permute-start | bytes 786440 | tf_op jit(solution)/shard_map/ppermute | solution.py:349
  24.1 1.6 %collective-permute-start.12 = (bf16[8,128,128]{2,1,0:T(8,128)(2,1)}, bf16[8,128,128]{2,1,0:T(8,128)(2,1)S(1)}, u32[]{:S(2)}, u32[]{:S(2)}) collective-permute-start(bf16[8,128,128]{2,1,0:T(8,128)(2,1)} %get-tuple-element.76), channel_id=1, source_target_pairs={{0,4},{4,0},{8,12},{12,8},{16,20},{20,16},{24,28},{28,24},{1,5},{5... | collective-permute-start | bytes 786440 | tf_op jit(solution)/shard_map/ppermute | solution.py:349
  25.7 0.2 collective-permute-start.4
  25.8 1.5 %collective-permute-start.5 = (bf16[2,2,128,128]{3,2,1,0:T(8,128)(2,1)}, bf16[2,2,128,128]{3,2,1,0:T(8,128)(2,1)S(1)}, u32[]{:S(2)}, u32[]{:S(2)}) collective-permute-start(bf16[2,2,128,128]{3,2,1,0:T(8,128)(2,1)} %get-tuple-element.69), channel_id=1, source_target_pairs={{0,2},{1,3},{2,0},{3,1},{4,6},{5,7},{6,4},{7,5},{8,10},{9,11},{10,... | collective-permute-start | bytes 393224 | tf_op jit(solution)/shard_map/ppermute | solution.py:349
  27.4 2.2 %collective-permute-done.10 = bf16[8,128,128]{2,1,0:T(8,128)(2,1)S(1)} collective-permute-done((bf16[8,128,128]{2,1,0:T(8,128)(2,1)S(1)}, bf16[8,128,128]{2,1,0:T(8,128)(2,1)S(1)}, u32[]{:S(2)}, u32[]{:S(2)}) %collective-permute-start.10) | collective-permute-done | bytes 262176 | tf_op jit(solution)/shard_map/ppermute | solution.py:349
  29.6 0.8 add_convert_fusion
  30.4 2.6 %collective-permute-start.11 = (bf16[8,128,128]{2,1,0:T(8,128)(2,1)}, bf16[8,128,128]{2,1,0:T(8,128)(2,1)S(1)}, u32[]{:S(2)}, u32[]{:S(2)}) collective-permute-start(bf16[8,128,128]{2,1,0:T(8,128)(2,1)} %add_convert_fusion), channel_id=1, source_target_pairs={{0,16},{4,20},{8,24},{12,28},{16,0},{20,4},{24,8},{28,12},{1,17},{... | collective-permute-start | bytes 786440 | tf_op jit(solution)/shard_map/ppermute | solution.py:349
  33.0 0.2 copy.15.inv_ref
  33.2 0.7 collective-permute-start.6
  34.0 5.0 %collective-permute-done.6.refs_7_ = bf16[2,2,128,128]{3,2,1,0:T(8,128)(2,1)S(1)} collective-permute-done((bf16[2,2,128,128]{3,2,1,0:T(8,128)(2,1)}, bf16[2,2,128,128]{3,2,1,0:T(8,128)(2,1)S(1)}, u32[]{:S(2)}, u32[]{:S(2)}) %collective-permute-start.6) | collective-permute-done | bytes 131104 | tf_op jit(solution)/shard_map/ppermute | solution.py:349
  39.0 6.8 %collective-permute-done.11.refs_0_ = bf16[8,128,128]{2,1,0:T(8,128)(2,1)S(1)} collective-permute-done((bf16[8,128,128]{2,1,0:T(8,128)(2,1)}, bf16[8,128,128]{2,1,0:T(8,128)(2,1)S(1)}, u32[]{:S(2)}, u32[]{:S(2)}) %collective-permute-start.11) | collective-permute-done | bytes 262176 | tf_op jit(solution)/shard_map/ppermute | solution.py:349
  45.8 0.2 shard_map.140
  46.1 0.0 copy-start.2
  46.1 0.0 copy-start.3
  46.1 0.1 collective-permute-start.13
  46.2 0.9 collective-permute-start.14
  47.1 1.0 collective-permute-start.15
  48.0 0.1 dynamic_slice.3
  48.1 0.1 copy.16.inv_ref
  48.3 2.9 %collective-permute-done.14.refs_10_ = bf16[2,128,128]{2,1,0:T(8,128)(2,1)S(1)} collective-permute-done((bf16[2,128,128]{2,1,0:T(8,128)(2,1)S(1)}, bf16[2,128,128]{2,1,0:T(8,128)(2,1)S(1)}, u32[]{:S(2)}, u32[]{:S(2)}) %collective-permute-start.14) | collective-permute-done | bytes 65568 | tf_op jit(solution)/shard_map/ppermute | solution.py:349
  51.1 0.5 collective-permute-done.15.refs_11_
  51.6 1.3 %shard_map.141 = (bf16[5,256,128]{2,1,0:T(8,128)(2,1)S(1)}, bf16[5,256,128]{2,1,0:T(8,128)(2,1)S(1)}, bf16[5,256,128]{2,1,0:T(8,128)(2,1)S(1)}, bf16[256,128]{1,...) custom-call(f32[256,1]{1,0:T(8,128)S(1)} %copy.16.inv_ref, ...), custom_call_target="tpu_custom_call" | custom-call | flops 1 | bytes 1 | tf_op jit(solution)/shard_map/pallas_call | solution.py:233
  52.9 0.3 collective-permute-start.16
  53.3 0.8 collective-permute-start.17
  54.1 0.7 collective-permute-start.18
  54.8 3.1 %collective-permute-done.17 = bf16[256,128]{1,0:T(8,128)(2,1)S(1)} collective-permute-done((bf16[256,128]{1,0:T(8,128)(2,1)S(1)}, bf16[256,128]{1,0:T(8,128)(2,1)S(1)}, u32[]{:S(2)}, u32[]{:S(2)}) %collective-permute-start.17) | collective-permute-done | bytes 65568 | tf_op jit(solution)/shard_map/ppermute | solution.py:349
  58.0 0.5 collective-permute-done.18
  58.5 0.1 collective-permute-start.19
  58.6 4.0 %collective-permute-start.20 = (bf16[8,128,128]{2,1,0:T(8,128)(2,1)S(1)}, bf16[8,128,128]{2,1,0:T(8,128)(2,1)S(1)}, u32[]{:S(2)}, u32[]{:S(2)}) collective-permute-start(bf16[8,128,128]{2,1,0:T(8,128)(2,1)S(1)} %bitcast.25), channel_id=1, source_target_pairs={{0,8},{4,12},{8,0},{12,4},{16,24},{20,28},{24,16},{28,20},{1,9},{5... | collective-permute-start | bytes 786440 | tf_op jit(solution)/shard_map/ppermute | solution.py:349
  62.6 1.4 %collective-permute-start.21 = (bf16[8,128,128]{2,1,0:T(8,128)(2,1)S(1)}, bf16[8,128,128]{2,1,0:T(8,128)(2,1)S(1)}, u32[]{:S(2)}, u32[]{:S(2)}) collective-permute-start(bf16[8,128,128]{2,1,0:T(8,128)(2,1)S(1)} %bitcast.26), channel_id=1, source_target_pairs={{0,4},{4,0},{8,12},{12,8},{16,20},{20,16},{24,28},{28,24},{1,5},{5... | collective-permute-start | bytes 786440 | tf_op jit(solution)/shard_map/ppermute | solution.py:349
  64.0 0.7 collective-permute-start.23
  64.7 9.0 %collective-permute-done.19.refs_6_ = bf16[8,128,128]{2,1,0:T(8,128)(2,1)S(1)} collective-permute-done((bf16[8,128,128]{2,1,0:T(8,128)(2,1)S(1)}, bf16[8,128,128]{2,1,0:T(8,128)(2,1)S(1)}, u32[]{:S(2)}, u32[]{:S(2)}) %collective-permute-start.19) | collective-permute-done | bytes 262176 | tf_op jit(solution)/shard_map/ppermute | solution.py:349
  73.7 0.1 collective-permute-done.20.refs_8_
  73.8 0.9 collective-permute-done.23.refs_2_
  74.7 3.9 %collective-permute-done.24.refs_3_ = bf16[5,256,128]{2,1,0:T(8,128)(2,1)S(1)} collective-permute-done((bf16[5,256,128]{2,1,0:T(8,128)(2,1)S(1)}, bf16[5,256,128]{2,1,0:T(8,128)(2,1)S(1)}, u32[]{:S(2)}, u32[]{:S(2)}) %collective-permute-start.24) | collective-permute-done | bytes 327712 | tf_op jit(solution)/shard_map/ppermute | solution.py:349
  78.5 0.8 shard_map.142
  79.3 0.0 copy-start
  79.4 0.0 copy-start.7
  79.4 0.7 collective-permute-start.25
  80.1 1.4 %collective-permute-start.26 = (bf16[8,128,128]{2,1,0:T(8,128)(2,1)S(1)}, bf16[8,128,128]{2,1,0:T(8,128)(2,1)S(1)}, u32[]{:S(2)}, u32[]{:S(2)}) collective-permute-start(bf16[8,128,128]{2,1,0:T(8,128)(2,1)S(1)} %collective-permute-done.20.refs_8_), channel_id=1, source_target_pairs={{0,4},{4,0},{8,12},{12,8},{16,20},{20,16},{24,28},{28,24},{1,5},{5... | collective-permute-start | bytes 786440 | tf_op jit(solution)/shard_map/ppermute | solution.py:349
  81.5 0.4 collective-permute-start.27
  81.8 0.6 collective-permute-start.28
  82.4 3.2 %collective-permute-done.25 = bf16[4,32,512]{2,1,0:T(8,128)(2,1)S(1)} collective-permute-done((bf16[4,32,512]{2,1,0:T(8,128)(2,1)S(1)}, bf16[4,32,512]{2,1,0:T(8,128)(2,1)S(1)}, u32[]{:S(2)}, u32[]{:S(2)}) %collective-permute-start.25) | collective-permute-done | bytes 131104 | tf_op jit(solution)/shard_map/ppermute | solution.py:349
  85.6 5.6 %collective-permute-done.26.refs_9_ = bf16[8,128,128]{2,1,0:T(8,128)(2,1)S(1)} collective-permute-done((bf16[8,128,128]{2,1,0:T(8,128)(2,1)S(1)}, bf16[8,128,128]{2,1,0:T(8,128)(2,1)S(1)}, u32[]{:S(2)}, u32[]{:S(2)}) %collective-permute-start.26) | collective-permute-done | bytes 262176 | tf_op jit(solution)/shard_map/ppermute | solution.py:349
  91.2 5.4 %collective-permute-done.27.refs_7_ = bf16[8,128,128]{2,1,0:T(8,128)(2,1)S(1)} collective-permute-done((bf16[8,128,128]{2,1,0:T(8,128)(2,1)S(1)}, bf16[8,128,128]{2,1,0:T(8,128)(2,1)S(1)}, u32[]{:S(2)}, u32[]{:S(2)}) %collective-permute-start.27) | collective-permute-done | bytes 262176 | tf_op jit(solution)/shard_map/ppermute | solution.py:349
  96.6 5.5 %collective-permute-done.29 = bf16[4,32,512]{2,1,0:T(8,128)(2,1)S(1)} collective-permute-done((bf16[4,32,512]{2,1,0:T(8,128)(2,1)S(1)}, bf16[4,32,512]{2,1,0:T(8,128)(2,1)S(1)}, u32[]{:S(2)}, u32[]{:S(2)}) %collective-permute-start.29) | collective-permute-done | bytes 131104 | tf_op jit(solution)/shard_map/ppermute | solution.py:349
  102.1 0.4 collective-permute-start.30
  102.5 0.8 collective-permute-start.31
  103.3 0.7 shard_map.143
  104.0 6.5 %collective-permute-done.30 = bf16[4,32,512]{2,1,0:T(8,128)(2,1)S(1)} collective-permute-done((bf16[4,32,512]{2,1,0:T(8,128)(2,1)S(1)}, bf16[4,32,512]{2,1,0:T(8,128)(2,1)S(1)}, u32[]{:S(2)}, u32[]{:S(2)}) %collective-permute-start.30) | collective-permute-done | bytes 131104 | tf_op jit(solution)/shard_map/ppermute | solution.py:349
  110.6 0.9 collective-permute-start.32
  111.5 2.3 %shard_map.144.refs_10_ = f32[8,128,128]{2,1,0:T(8,128)S(1)} custom-call(s32[1,16]{1,0:T(1,128)S(1)} %copy-done.8, s32[1,16]{1,0:T(1,128)S(1)} %copy-done.9, s32[6,1,8]{2,1,0:T(1,128)S(1)} %bitcast.32, s32[6,1,8]{2,1,0:T(1,128)S(1)} %bitcast.36, bf16[16,128,128]{2,1,0:T(8,128)(2,1)S(1)} %bitcast.20, bf16[6,8,128,128]{3,2,1,0:T(8,128)(2,1)S(1)} %bitcast.16, ...), custom_call_target="tpu_custom_call" | custom-call | flops 1 | bytes 1 | tf_op jit(solution)/shard_map/pallas_call | solution.py:214
  113.8 2.8 %shard_map.145 = f32[8,128,128]{2,1,0:T(8,128)} custom-call(s32[1,16]{1,0:T(1,128)S(1)} %copy-done.8, s32[1,16]{1,0:T(1,128)S(1)} %copy-done.9, s32[6,1,8]{2,1,0:T(1,128)S(1)} %bitcast.33, s32[6,1,8]{2,1,0:T(1,128)S(1)} %bitcast.37, bf16[16,128,128]{2,1,0:T(8,128)(2,1)S(1)} %bitcast.21, bf16[6,8,128,128]{3,2,1,0:T(8,128)(2,1)S(1)} %bitcast.17, ...), custom_call_target="tpu_custom_call" | custom-call | flops 1 | bytes 1 | tf_op jit(solution)/shard_map/pallas_call | solution.py:214
  116.7 0.9 shard_map.146
  (51 shorter events, 0.3 us)
Async XLA Ops:
  4.8 11.0 %collective-permute-start.1 = (bf16[8,128,128]{2,1,0:T(8,128)(2,1)}, bf16[8,128,128]{2,1,0:T(8,128)(2,1)S(1)}, u32[]{:S(2)}, u32[]{:S(2)}) collective-permute-start(bf16[8,128,128]{2,1,0:T(8,128)(2,1)} %get-tuple-element.64), channel_id=1, source_target_pairs={{0,4},{4,0},{8,12},{12,8},{16,20},{20,16},{24,28},{28,24},{1,5},{5... | collective-permute-start | bytes 786440 | tf_op jit(solution)/shard_map/ppermute | solution.py:349
  7.8 13.0 %collective-permute-start.9 = (bf16[8,128,128]{2,1,0:T(8,128)(2,1)}, bf16[8,128,128]{2,1,0:T(8,128)(2,1)S(1)}, u32[]{:S(2)}, u32[]{:S(2)}) collective-permute-start(bf16[8,128,128]{2,1,0:T(8,128)(2,1)} %get-tuple-element.75), channel_id=1, source_target_pairs={{0,4},{4,0},{8,12},{12,8},{16,20},{20,16},{24,28},{28,24},{1,5},{5... | collective-permute-start | bytes 786440 | tf_op jit(solution)/shard_map/ppermute | solution.py:349
  7.9 16.2 %collective-permute-start.3 = (bf16[2,128,512]{2,1,0:T(8,128)(2,1)}, bf16[2,128,512]{2,1,0:T(8,128)(2,1)S(1)}, u32[]{:S(2)}, u32[]{:S(2)}) collective-permute-start(bf16[2,128,512]{2,1,0:T(8,128)(2,1)} %get-tuple-element.80.refs_0_), channel_id=1, source_target_pairs={{0,2},{1,3},{2,0},{3,1},{4,6},{5,7},{6,4},{7,5},{8,10},{9,11},{10,... | collective-permute-start | bytes 786440 | tf_op jit(solution)/shard_map/ppermute | solution.py:349
  9.8 15.8 %collective-permute-start = (bf16[8,128,128]{2,1,0:T(8,128)(2,1)}, bf16[8,128,128]{2,1,0:T(8,128)(2,1)S(1)}, u32[]{:S(2)}, u32[]{:S(2)}) collective-permute-start(bf16[8,128,128]{2,1,0:T(8,128)(2,1)} %get-tuple-element.62), channel_id=1, source_target_pairs={{0,4},{4,0},{8,12},{12,8},{16,20},{20,16},{24,28},{28,24},{1,5},{5... | collective-permute-start | bytes 786440 | tf_op jit(solution)/shard_map/ppermute | solution.py:349
  15.7 8.4 %copy-start.4 = (bf16[2,128,512]{2,1,0:T(8,128)(2,1)S(1)}, bf16[2,128,512]{2,1,0:T(8,128)(2,1)}, u32[]{:S(2)}) copy-start(bf16[2,128,512]{2,1,0:T(8,128)(2,1)} %get-tuple-element.80.refs_0_) | copy-start | bytes 786436
  15.7 9.9 %copy-start.13 = (bf16[2,2,128,128]{3,2,1,0:T(8,128)(2,1)S(1)}, bf16[2,2,128,128]{3,2,1,0:T(8,128)(2,1)}, u32[]{:S(2)}) copy-start(bf16[2,2,128,128]{3,2,1,0:T(8,128)(2,1)} %get-tuple-element.68) | copy-start | bytes 393220
  15.8 13.8 %copy-start.11 = (f32[8,128,128]{2,1,0:T(8,128)S(1)}, f32[8,128,128]{2,1,0:T(8,128)}, u32[]{:S(2)}) copy-start(f32[8,128,128]{2,1,0:T(8,128)} %get-tuple-element.72) | copy-start | bytes 1572868
  15.8 17.2 %copy-start.12 = (s32[1024]{0:T(1024)S(1)}, s32[1024]{0:T(1024)}, u32[]{:S(2)}) copy-start(s32[1024]{0:T(1024)} %param.14) | copy-start | bytes 12292
  17.0 17.0 %copy-start.10 = (f32[8,128,128]{2,1,0:T(8,128)S(1)}, f32[8,128,128]{2,1,0:T(8,128)}, u32[]{:S(2)}) copy-start(f32[8,128,128]{2,1,0:T(8,128)} %get-tuple-element.61) | copy-start | bytes 1572868
  17.0 8.9 %collective-permute-start.2 = (bf16[8,128,128]{2,1,0:T(8,128)(2,1)S(1)}, bf16[8,128,128]{2,1,0:T(8,128)(2,1)S(1)}, u32[]{:S(2)}, u32[]{:S(2)}) collective-permute-start(bf16[8,128,128]{2,1,0:T(8,128)(2,1)S(1)} %add_convert_fusion.2), channel_id=1, source_target_pairs={{0,8},{4,12},{8,0},{12,4},{16,24},{20,28},{24,16},{28,20},{1,9},{5... | collective-permute-start | bytes 786440 | tf_op jit(solution)/shard_map/ppermute | solution.py:349
  21.9 7.7 %collective-permute-start.10 = (bf16[8,128,128]{2,1,0:T(8,128)(2,1)S(1)}, bf16[8,128,128]{2,1,0:T(8,128)(2,1)S(1)}, u32[]{:S(2)}, u32[]{:S(2)}) collective-permute-start(bf16[8,128,128]{2,1,0:T(8,128)(2,1)S(1)} %add_convert_fusion.1), channel_id=1, source_target_pairs={{0,8},{4,12},{8,0},{12,4},{16,24},{20,28},{24,16},{28,20},{1,9},{5... | collective-permute-start | bytes 786440 | tf_op jit(solution)/shard_map/ppermute | solution.py:349
  24.1 14.9 %collective-permute-start.7 = (bf16[2,128,512]{2,1,0:T(8,128)(2,1)S(1)}, bf16[2,128,512]{2,1,0:T(8,128)(2,1)S(1)}, u32[]{:S(2)}, u32[]{:S(2)}) collective-permute-start(bf16[2,128,512]{2,1,0:T(8,128)(2,1)S(1)} %copy-done.4), channel_id=1, source_target_pairs={{0,1},{1,0},{2,3},{3,2},{4,5},{5,4},{6,7},{7,6},{8,9},{9,8},{10,11... | collective-permute-start | bytes 786440 | tf_op jit(solution)/shard_map/ppermute | solution.py:349
  24.1 14.9 %collective-permute-start.12 = (bf16[8,128,128]{2,1,0:T(8,128)(2,1)}, bf16[8,128,128]{2,1,0:T(8,128)(2,1)S(1)}, u32[]{:S(2)}, u32[]{:S(2)}) collective-permute-start(bf16[8,128,128]{2,1,0:T(8,128)(2,1)} %get-tuple-element.76), channel_id=1, source_target_pairs={{0,4},{4,0},{8,12},{12,8},{16,20},{20,16},{24,28},{28,24},{1,5},{5... | collective-permute-start | bytes 786440 | tf_op jit(solution)/shard_map/ppermute | solution.py:349
  25.7 4.7 %collective-permute-start.4 = (bf16[2,2,128,128]{3,2,1,0:T(8,128)(2,1)S(1)}, bf16[2,2,128,128]{3,2,1,0:T(8,128)(2,1)S(1)}, u32[]{:S(2)}, u32[]{:S(2)}) collective-permute-start(bf16[2,2,128,128]{3,2,1,0:T(8,128)(2,1)S(1)} %copy-done.13), channel_id=1, source_target_pairs={{0,1},{1,0},{2,3},{3,2},{4,5},{5,4},{6,7},{7,6},{8,9},{9,8},{10,11... | collective-permute-start | bytes 393224 | tf_op jit(solution)/shard_map/ppermute | solution.py:349
  25.8 7.4 %collective-permute-start.5 = (bf16[2,2,128,128]{3,2,1,0:T(8,128)(2,1)}, bf16[2,2,128,128]{3,2,1,0:T(8,128)(2,1)S(1)}, u32[]{:S(2)}, u32[]{:S(2)}) collective-permute-start(bf16[2,2,128,128]{3,2,1,0:T(8,128)(2,1)} %get-tuple-element.69), channel_id=1, source_target_pairs={{0,2},{1,3},{2,0},{3,1},{4,6},{5,7},{6,4},{7,5},{8,10},{9,11},{10,... | collective-permute-start | bytes 393224 | tf_op jit(solution)/shard_map/ppermute | solution.py:349
  29.6 9.4 %collective-permute-start.8 = (bf16[2,128,512]{2,1,0:T(8,128)(2,1)S(1)}, bf16[2,128,512]{2,1,0:T(8,128)(2,1)S(1)}, u32[]{:S(2)}, u32[]{:S(2)}) collective-permute-start(bf16[2,128,512]{2,1,0:T(8,128)(2,1)S(1)} %collective-permute-done.3.refs_2_), channel_id=1, source_target_pairs={{0,1},{1,0},{2,3},{3,2},{4,5},{5,4},{6,7},{7,6},{8,9},{9,8},{10,11... | collective-permute-start | bytes 786440 | tf_op jit(solution)/shard_map/ppermute | solution.py:349
  30.4 15.4 %collective-permute-start.11 = (bf16[8,128,128]{2,1,0:T(8,128)(2,1)}, bf16[8,128,128]{2,1,0:T(8,128)(2,1)S(1)}, u32[]{:S(2)}, u32[]{:S(2)}) collective-permute-start(bf16[8,128,128]{2,1,0:T(8,128)(2,1)} %add_convert_fusion), channel_id=1, source_target_pairs={{0,16},{4,20},{8,24},{12,28},{16,0},{20,4},{24,8},{28,12},{1,17},{... | collective-permute-start | bytes 786440 | tf_op jit(solution)/shard_map/ppermute | solution.py:349
  33.2 18.4 %copy-start.5 = (bf16[2,2,128,128]{3,2,1,0:T(8,128)(2,1)S(1)}, bf16[2,2,128,128]{3,2,1,0:T(8,128)(2,1)}, u32[]{:S(2)}) copy-start(bf16[2,2,128,128]{3,2,1,0:T(8,128)(2,1)} %get-tuple-element.84.refs_4_) | copy-start | bytes 393220
  33.2 5.8 %collective-permute-start.6 = (bf16[2,2,128,128]{3,2,1,0:T(8,128)(2,1)}, bf16[2,2,128,128]{3,2,1,0:T(8,128)(2,1)S(1)}, u32[]{:S(2)}, u32[]{:S(2)}) collective-permute-start(bf16[2,2,128,128]{3,2,1,0:T(8,128)(2,1)} %get-tuple-element.70), channel_id=1, source_target_pairs={{0,3},{1,2},{2,1},{3,0},{4,7},{5,6},{6,5},{7,4},{8,11},{9,10},{10,... | collective-permute-start | bytes 393224 | tf_op jit(solution)/shard_map/ppermute | solution.py:349
  46.1 32.5 %copy-start.2 = (bf16[1024,128]{1,0:T(8,128)(2,1)S(1)}, bf16[1024,128]{1,0:T(8,128)(2,1)}, u32[]{:S(2)}) copy-start(bf16[1024,128]{1,0:T(8,128)(2,1)} %f_ref.1) | copy-start | bytes 786436
  46.1 32.4 %copy-start.3 = (bf16[128,512]{1,0:T(8,128)(2,1)S(1)}, bf16[128,512]{1,0:T(8,128)(2,1)}, u32[]{:S(2)}) copy-start(bf16[128,512]{1,0:T(8,128)(2,1)} %w_ref.1) | copy-start | bytes 393220
  46.1 2.2 %collective-permute-start.13 = (bf16[2,128,128]{2,1,0:T(8,128)(2,1)S(1)}, bf16[2,128,128]{2,1,0:T(8,128)(2,1)S(1)}, u32[]{:S(2)}, u32[]{:S(2)}) collective-permute-start(bf16[2,128,128]{2,1,0:T(8,128)(2,1)S(1)} %get-tuple-element.89), channel_id=1, source_target_pairs={{0,1},{1,0},{2,3},{3,2},{4,5},{5,4},{6,7},{7,6},{8,9},{9,8},{10,11... | collective-permute-start | bytes 196616 | tf_op jit(solution)/shard_map/ppermute | solution.py:349
  46.2 5.0 %collective-permute-start.14 = (bf16[2,128,128]{2,1,0:T(8,128)(2,1)S(1)}, bf16[2,128,128]{2,1,0:T(8,128)(2,1)S(1)}, u32[]{:S(2)}, u32[]{:S(2)}) collective-permute-start(bf16[2,128,128]{2,1,0:T(8,128)(2,1)S(1)} %get-tuple-element.90), channel_id=1, source_target_pairs={{0,2},{1,3},{2,0},{3,1},{4,6},{5,7},{6,4},{7,5},{8,10},{9,11},{10,... | collective-permute-start | bytes 196616 | tf_op jit(solution)/shard_map/ppermute | solution.py:349
  47.1 4.6 %collective-permute-start.15 = (bf16[2,128,128]{2,1,0:T(8,128)(2,1)S(1)}, bf16[2,128,128]{2,1,0:T(8,128)(2,1)S(1)}, u32[]{:S(2)}, u32[]{:S(2)}) collective-permute-start(bf16[2,128,128]{2,1,0:T(8,128)(2,1)S(1)} %get-tuple-element.91), channel_id=1, source_target_pairs={{0,3},{1,2},{2,1},{3,0},{4,7},{5,6},{6,5},{7,4},{8,11},{9,10},{10,... | collective-permute-start | bytes 196616 | tf_op jit(solution)/shard_map/ppermute | solution.py:349
  52.9 1.9 %collective-permute-start.16 = (bf16[256,128]{1,0:T(8,128)(2,1)S(1)}, bf16[256,128]{1,0:T(8,128)(2,1)S(1)}, u32[]{:S(2)}, u32[]{:S(2)}) collective-permute-start(bf16[256,128]{1,0:T(8,128)(2,1)S(1)} %get-tuple-element.96), channel_id=1, source_target_pairs={{0,1},{1,0},{2,3},{3,2},{4,5},{5,4},{6,7},{7,6},{8,9},{9,8},{10,11... | collective-permute-start | bytes 196616 | tf_op jit(solution)/shard_map/ppermute | solution.py:349
  53.3 4.7 %collective-permute-start.17 = (bf16[256,128]{1,0:T(8,128)(2,1)S(1)}, bf16[256,128]{1,0:T(8,128)(2,1)S(1)}, u32[]{:S(2)}, u32[]{:S(2)}) collective-permute-start(bf16[256,128]{1,0:T(8,128)(2,1)S(1)} %get-tuple-element.97), channel_id=1, source_target_pairs={{0,2},{1,3},{2,0},{3,1},{4,6},{5,7},{6,4},{7,5},{8,10},{9,11},{10,... | collective-permute-start | bytes 196616 | tf_op jit(solution)/shard_map/ppermute | solution.py:349
  54.1 4.4 %collective-permute-start.18 = (bf16[256,128]{1,0:T(8,128)(2,1)S(1)}, bf16[256,128]{1,0:T(8,128)(2,1)S(1)}, u32[]{:S(2)}, u32[]{:S(2)}) collective-permute-start(bf16[256,128]{1,0:T(8,128)(2,1)S(1)} %get-tuple-element.98), channel_id=1, source_target_pairs={{0,3},{1,2},{2,1},{3,0},{4,7},{5,6},{6,5},{7,4},{8,11},{9,10},{10,... | collective-permute-start | bytes 196616 | tf_op jit(solution)/shard_map/ppermute | solution.py:349
  58.5 15.2 %collective-permute-start.19 = (bf16[8,128,128]{2,1,0:T(8,128)(2,1)S(1)}, bf16[8,128,128]{2,1,0:T(8,128)(2,1)S(1)}, u32[]{:S(2)}, u32[]{:S(2)}) collective-permute-start(bf16[8,128,128]{2,1,0:T(8,128)(2,1)S(1)} %bitcast.24), channel_id=1, source_target_pairs={{0,16},{4,20},{8,24},{12,28},{16,0},{20,4},{24,8},{28,12},{1,17},{... | collective-permute-start | bytes 786440 | tf_op jit(solution)/shard_map/ppermute | solution.py:349
  58.6 15.2 %collective-permute-start.20 = (bf16[8,128,128]{2,1,0:T(8,128)(2,1)S(1)}, bf16[8,128,128]{2,1,0:T(8,128)(2,1)S(1)}, u32[]{:S(2)}, u32[]{:S(2)}) collective-permute-start(bf16[8,128,128]{2,1,0:T(8,128)(2,1)S(1)} %bitcast.25), channel_id=1, source_target_pairs={{0,8},{4,12},{8,0},{12,4},{16,24},{20,28},{24,16},{28,20},{1,9},{5... | collective-permute-start | bytes 786440 | tf_op jit(solution)/shard_map/ppermute | solution.py:349
  62.6 11.1 %collective-permute-start.21 = (bf16[8,128,128]{2,1,0:T(8,128)(2,1)S(1)}, bf16[8,128,128]{2,1,0:T(8,128)(2,1)S(1)}, u32[]{:S(2)}, u32[]{:S(2)}) collective-permute-start(bf16[8,128,128]{2,1,0:T(8,128)(2,1)S(1)} %bitcast.26), channel_id=1, source_target_pairs={{0,4},{4,0},{8,12},{12,8},{16,20},{20,16},{24,28},{28,24},{1,5},{5... | collective-permute-start | bytes 786440 | tf_op jit(solution)/shard_map/ppermute | solution.py:349
  64.0 10.6 %collective-permute-start.23 = (bf16[5,256,128]{2,1,0:T(8,128)(2,1)S(1)}, bf16[5,256,128]{2,1,0:T(8,128)(2,1)S(1)}, u32[]{:S(2)}, u32[]{:S(2)}) collective-permute-start(bf16[5,256,128]{2,1,0:T(8,128)(2,1)S(1)} %get-tuple-element.101), channel_id=1, source_target_pairs={{0,2},{1,3},{2,0},{3,1},{4,6},{5,7},{6,4},{7,5},{8,10},{9,11},{10,... | collective-permute-start | bytes 983048 | tf_op jit(solution)/shard_map/ppermute | solution.py:349
  64.7 13.8 %collective-permute-start.24 = (bf16[5,256,128]{2,1,0:T(8,128)(2,1)S(1)}, bf16[5,256,128]{2,1,0:T(8,128)(2,1)S(1)}, u32[]{:S(2)}, u32[]{:S(2)}) collective-permute-start(bf16[5,256,128]{2,1,0:T(8,128)(2,1)S(1)} %get-tuple-element.102), channel_id=1, source_target_pairs={{0,3},{1,2},{2,1},{3,0},{4,7},{5,6},{6,5},{7,4},{8,11},{9,10},{10,... | collective-permute-start | bytes 983048 | tf_op jit(solution)/shard_map/ppermute | solution.py:349
  73.7 4.8 %collective-permute-start.22 = (bf16[5,256,128]{2,1,0:T(8,128)(2,1)S(1)}, bf16[5,256,128]{2,1,0:T(8,128)(2,1)S(1)}, u32[]{:S(2)}, u32[]{:S(2)}) collective-permute-start(bf16[5,256,128]{2,1,0:T(8,128)(2,1)S(1)} %get-tuple-element.100.refs_0_), channel_id=1, source_target_pairs={{0,1},{1,0},{2,3},{3,2},{4,5},{5,4},{6,7},{7,6},{8,9},{9,8},{10,11... | collective-permute-start | bytes 983048 | tf_op jit(solution)/shard_map/ppermute | solution.py:349
  79.3 32.1 %copy-start = (bf16[1,6,8,128,128]{4,3,2,1,0:T(8,128)(2,1)S(1)}, bf16[1,6,8,128,128]{4,3,2,1,0:T(8,128)(2,1)}, u32[]{:S(2)}) copy-start(bf16[1,6,8,128,128]{4,3,2,1,0:T(8,128)(2,1)} %param.18) | copy-start | bytes 4718596
  79.3 32.1 %copy-start.1 = (bf16[1,16,128,128]{3,2,1,0:T(8,128)(2,1)S(1)}, bf16[1,16,128,128]{3,2,1,0:T(8,128)(2,1)}, u32[]{:S(2)}) copy-start(bf16[1,16,128,128]{3,2,1,0:T(8,128)(2,1)} %param.15) | copy-start | bytes 1572868
  79.3 32.1 %copy-start.6 = (s32[1,6,8]{2,0,1:T(1,128)S(1)}, s32[1,6,8]{2,0,1:T(1,128)}, u32[]{:S(2)}) copy-start(s32[1,6,8]{2,0,1:T(1,128)} %param.19) | copy-start | bytes 580
  79.4 32.1 %copy-start.7 = (s32[1,6,8]{2,0,1:T(1,128)S(1)}, s32[1,6,8]{2,0,1:T(1,128)}, u32[]{:S(2)}) copy-start(s32[1,6,8]{2,0,1:T(1,128)} %param.20) | copy-start | bytes 580
  79.4 32.1 %copy-start.8 = (s32[1,16]{1,0:T(1,128)S(1)}, s32[1,16]{1,0:T(1,128)}, u32[]{:S(2)}) copy-start(s32[1,16]{1,0:T(1,128)} %refs_0_.7) | copy-start | bytes 196
  79.4 32.1 %copy-start.9 = (s32[1,16]{1,0:T(1,128)S(1)}, s32[1,16]{1,0:T(1,128)}, u32[]{:S(2)}) copy-start(s32[1,16]{1,0:T(1,128)} %refs_1_.7) | copy-start | bytes 196
  79.4 6.2 %collective-permute-start.25 = (bf16[4,32,512]{2,1,0:T(8,128)(2,1)S(1)}, bf16[4,32,512]{2,1,0:T(8,128)(2,1)S(1)}, u32[]{:S(2)}, u32[]{:S(2)}) collective-permute-start(bf16[4,32,512]{2,1,0:T(8,128)(2,1)S(1)} %get-tuple-element.107), channel_id=1, source_target_pairs={{0,4},{4,0},{8,12},{12,8},{16,20},{20,16},{24,28},{28,24},{1,5},{5... | collective-permute-start | bytes 393224 | tf_op jit(solution)/shard_map/ppermute | solution.py:349
  80.1 11.1 %collective-permute-start.26 = (bf16[8,128,128]{2,1,0:T(8,128)(2,1)S(1)}, bf16[8,128,128]{2,1,0:T(8,128)(2,1)S(1)}, u32[]{:S(2)}, u32[]{:S(2)}) collective-permute-start(bf16[8,128,128]{2,1,0:T(8,128)(2,1)S(1)} %collective-permute-done.20.refs_8_), channel_id=1, source_target_pairs={{0,4},{4,0},{8,12},{12,8},{16,20},{20,16},{24,28},{28,24},{1,5},{5... | collective-permute-start | bytes 786440 | tf_op jit(solution)/shard_map/ppermute | solution.py:349
  81.5 15.1 %collective-permute-start.27 = (bf16[8,128,128]{2,1,0:T(8,128)(2,1)S(1)}, bf16[8,128,128]{2,1,0:T(8,128)(2,1)S(1)}, u32[]{:S(2)}, u32[]{:S(2)}) collective-permute-start(bf16[8,128,128]{2,1,0:T(8,128)(2,1)S(1)} %collective-permute-done.21.refs_7_), channel_id=1, source_target_pairs={{0,16},{4,20},{8,24},{12,28},{16,0},{20,4},{24,8},{28,12},{1,17},{... | collective-permute-start | bytes 786440 | tf_op jit(solution)/shard_map/ppermute | solution.py:349
  81.8 14.7 %collective-permute-start.28 = (bf16[8,128,128]{2,1,0:T(8,128)(2,1)S(1)}, bf16[8,128,128]{2,1,0:T(8,128)(2,1)S(1)}, u32[]{:S(2)}, u32[]{:S(2)}) collective-permute-start(bf16[8,128,128]{2,1,0:T(8,128)(2,1)S(1)} %collective-permute-done.19.refs_6_), channel_id=1, source_target_pairs={{0,8},{4,12},{8,0},{12,4},{16,24},{20,28},{24,16},{28,20},{1,9},{5... | collective-permute-start | bytes 786440 | tf_op jit(solution)/shard_map/ppermute | solution.py:349
  96.6 5.5 %collective-permute-start.29 = (bf16[4,32,512]{2,1,0:T(8,128)(2,1)S(1)}, bf16[4,32,512]{2,1,0:T(8,128)(2,1)S(1)}, u32[]{:S(2)}, u32[]{:S(2)}) collective-permute-start(bf16[4,32,512]{2,1,0:T(8,128)(2,1)S(1)} %add_convert_fusion.5), channel_id=1, source_target_pairs={{0,8},{4,12},{8,0},{12,4},{16,24},{20,28},{24,16},{28,20},{1,9},{5... | collective-permute-start | bytes 393224 | tf_op jit(solution)/shard_map/ppermute | solution.py:349
  102.1 8.4 %collective-permute-start.30 = (bf16[4,32,512]{2,1,0:T(8,128)(2,1)S(1)}, bf16[4,32,512]{2,1,0:T(8,128)(2,1)S(1)}, u32[]{:S(2)}, u32[]{:S(2)}) collective-permute-start(bf16[4,32,512]{2,1,0:T(8,128)(2,1)S(1)} %add_convert_fusion.4), channel_id=1, source_target_pairs={{0,16},{4,20},{8,24},{12,28},{16,0},{20,4},{24,8},{28,12},{1,17},{... | collective-permute-start | bytes 393224 | tf_op jit(solution)/shard_map/ppermute | solution.py:349
  102.5 8.1 %collective-permute-start.31 = (bf16[8,128,128]{2,1,0:T(8,128)(2,1)S(1)}, bf16[8,128,128]{2,1,0:T(8,128)(2,1)S(1)}, u32[]{:S(2)}, u32[]{:S(2)}) collective-permute-start(bf16[8,128,128]{2,1,0:T(8,128)(2,1)S(1)} %collective-permute-done.28.refs_8_), channel_id=1, source_target_pairs={{0,4},{4,0},{8,12},{12,8},{16,20},{20,16},{24,28},{28,24},{1,5},{5... | collective-permute-start | bytes 786440 | tf_op jit(solution)/shard_map/ppermute | solution.py:349
  110.6 6.0 %collective-permute-start.32 = (bf16[4,32,512]{2,1,0:T(8,128)(2,1)S(1)}, bf16[4,32,512]{2,1,0:T(8,128)(2,1)S(1)}, u32[]{:S(2)}, u32[]{:S(2)}) collective-permute-start(bf16[4,32,512]{2,1,0:T(8,128)(2,1)S(1)} %add_convert_fusion.3.mine_ref), channel_id=1, source_target_pairs={{0,4},{4,0},{8,12},{12,8},{16,20},{20,16},{24,28},{28,24},{1,5},{5... | collective-permute-start | bytes 393224 | tf_op jit(solution)/shard_map/ppermute | solution.py:349

commit v8 on v7

--- a/solution.py
+++ b/solution.py
@@ -403,27 +403,28 @@
     def tied(x, *others):
         return lax.optimization_barrier((x, others))[0]
 
+    (send_7,) = forward([7], [blocks], [like(shape, BF16)])
     made = forward(
-        [7, 3, 5, 1],
-        [blocks, cotangent.reshape(shape), w_self, w_neigh],
-        [like(shape, BF16)] * 4
+        [5, 3, 1],
+        [tied(blocks, send_7), cotangent.reshape(shape), w_self, w_neigh],
+        [like(shape, BF16)] * 3
         + [like((2, per_feat, block, width), BF16)] * feats
         + [like((2, width, full), BF16)],
     )
-    sends, early_pieces, pair = made[:4], made[4:-1], made[-1]
-    keep_6, keep_2, keep_4, keep = forward([6, 2, 4, 0], [blocks], [like(shape, F32)] * 4)
+    sends, early_pieces, pair = [send_7, *made[:3]], list(made[3:-1]), made[-1]
+    keep_6, keep_4, keep_2, keep = forward([6, 4, 2, 0], [blocks], [like(shape, F32)] * 4)
     weights = relayed(pair)
-    early = [early_pieces[0]] + [crossed(early_pieces[m], m, "feat") for m in range(1, feats)]
-    near_6, near_2, near_4, near_0 = (crossed(send, near) for send in sends)
+    near_6, near_4, near_2, near_0 = (crossed(send, near) for send in sends)
     sum_6 = (keep_6 + near_6.astype(F32)).astype(BF16)
-    sum_2 = (keep_2 + near_2.astype(F32)).astype(BF16)
-    mid_0 = crossed(sum_2, 2)
-    near_4, mid_0, weights[2] = lax.optimization_barrier((near_4, mid_0, weights[2]))
+    near_4 = tied(near_4, weights[2])
     sum_4 = (keep_4 + near_4.astype(F32) + crossed(sum_6, 2).astype(F32)).astype(BF16)
     far_0 = crossed(sum_4, 4)
-    part = keep + mid_0.astype(F32)
-    arrived = [far_0, near_0]
-    early, weights, arrived = lax.optimization_barrier((early, weights, arrived))
+    sum_2 = tied((tied(keep_2, sum_4) + near_2.astype(F32)).astype(BF16), far_0)
+    mid_0 = crossed(sum_2, 2)
+    early = [early_pieces[0]] + [crossed(early_pieces[m], m, "feat") for m in range(1, feats)]
+    part = keep + near_0.astype(F32)
+    arrived = [far_0, mid_0]
+    arrived, early, weights = lax.optimization_barrier((arrived, early, weights))
     agg, *agg_pieces = small_call(
         functools.partial(agg_kernel, feats),
         [like(shape, BF16)] + [like((per_feat, block, width), BF16)] * feats,
@@ -454,7 +455,7 @@
     dpre = [sent[0], *come]
     found[6] = crossed(found[4], 2)
     found[3] = crossed(found[2], near)
-    found[5] = crossed(found[1], 4)
+    found[5] = crossed(found[4], near)
     found[7] = crossed(found[6], near)
     piece = 2 * width // parts_total
     dx_self, give, keep = small_call(
@@ -468,10 +469,10 @@
         [pltpu.VMEM((parts_total, piece, full), F32)],
     )
     total = (keep + crossed(give, near).astype(F32)).astype(BF16)
-    total = tied(total, found[3], found[5], found[6])
     total = (total.astype(F32) + crossed(total, 2).astype(F32)).astype(BF16)
+    total = tied(total, found[3], found[6])
     total = (total.astype(F32) + crossed(total, 4).astype(F32)).astype(BF16)
-    total, out = tied((total, out), found[7])
+    total, out = tied((total, out), found[5], found[7])
     grad_self, grad_neigh = small_call(
         finish_kernel,
         [like((width, full), F32)] * 2,

time: 118 us -> 119 us (level)
  Pallas kernels: 17.5 us -> 20.1 us
  waiting for transfers between devices: 63.3 us -> 62 us
    pallas_call x4 -> x5, Pallas kernels: 13.7 us -> 16.2 us  [tiles_call(): pl.pallas_call(functools.partial(tiles_kernel, masks, offsets, parts_tota...]
    ppermute x33, waiting for transfers between devices: 63.3 us -> 62 us  [crossed(): lax.ppermute(x, axis, [(i, i ^ mask) for i in range(lax.axis_size(axis))])]
  transfers between devices with their start and end apart: 33 -> 33, of which waited for: 17 -> 20; matrix products, arithmetic and copies ran while one was open for 3% -> 3% of each run, Pallas kernels for 9% -> 12%
where the time goes in v8:
time: 119 us
  waiting for transfers between devices  62 us (52%)
  starting transfers between devices  32.2 us (27%)
  Pallas kernels  20.1 us (17%)
  other arithmetic  3.23 us (3%)
    ppermute x33, waiting for transfers between devices, crossed(): lax.ppermute(x, axis, [(i, i ^ mask) for i in range(lax.axis_size(axis))])  62 us
    ppermute x33, starting transfers between devices, crossed(): lax.ppermute(x, axis, [(i, i ^ mask) for i in range(lax.axis_size(axis))])  32.2 us
    pallas_call x5, Pallas kernels, tiles_call(): pl.pallas_call(functools.partial(tiles_kernel, masks, offsets, parts_tota...  16.2 us
    pallas_call x5, Pallas kernels, small_call(): pl.pallas_call(kernel, out_shape=outs, in_specs=[VMEM] * len(arrays), out...  3.87 us
  transfers between devices with their start and end apart: 33, of which 20 were waited for; matrix products, arithmetic and copies ran while one was open for 3% of the time, Pallas kernels for 12%

profile of v8, /device:TPU:0, one launch (start us, length us, event | category | flops | bytes accessed | tf_op | source)
XLA Modules:
  0.0 118.9 jit_solution(16916146955496587508)
XLA Ops:
  0.6 2.9 %shard_map.139 = bf16[8,128,128]{2,1,0:T(8,128)(2,1)} custom-call(s32[1,16]{1,0:T(1,128)} %refs_0_.9, s32[1,16]{1,0:T(1,128)} %refs_1_.9, s32[6,1,8]{2,1,0:T(1,128)} %bitcast.33, s32[6,1,8]{2,1,0:T(1,128)} %bitcast.38, bf16[16,128,128]{2,1,0:T(8,128)(2,1)} %bitcast.19, bf16[6,8,128,128]{3,2,1,0:T(8,128)(2,1)} %bitcast.14, bf16[8,128,128]{2,1,0:T(8,128)(2,1)} %bitcast.24), custom_call_target="tpu_custom_call" | custom-call | flops 1 | bytes 1 | tf_op jit(solution)/shard_map/pallas_call | solution.py:214
  3.5 3.0 %collective-permute-start.3 = (bf16[8,128,128]{2,1,0:T(8,128)(2,1)}, bf16[8,128,128]{2,1,0:T(8,128)(2,1)S(1)}, u32[]{:S(2)}, u32[]{:S(2)}) collective-permute-start(bf16[8,128,128]{2,1,0:T(8,128)(2,1)} %shard_map.139), channel_id=1, source_target_pairs={{0,4},{4,0},{8,12},{12,8},{16,20},{20,16},{24,28},{28,24},{1,5},{5... | collective-permute-start | bytes 786440 | tf_op jit(solution)/shard_map/ppermute | solution.py:349
  6.6 3.8 %shard_map.140 = (bf16[8,128,128]{2,1,0:T(8,128)(2,1)}, bf16[8,128,128]{2,1,0:T(8,128)(2,1)}, bf16[8,128,128]{2,1,0:T(8,128)(2,1)}, bf16[2,2,128,128]{3,2,1,0:T(...) custom-call(s32[1,16]{1,0:T(1,128)} %refs_0_.9, ...), custom_call_target="tpu_custom_call" | custom-call | flops 1 | bytes 1 | tf_op jit(solution)/shard_map/pallas_call | solution.py:214
  10.4 1.6 %collective-permute-start.2 = (bf16[2,128,512]{2,1,0:T(8,128)(2,1)}, bf16[2,128,512]{2,1,0:T(8,128)(2,1)S(1)}, u32[]{:S(2)}, u32[]{:S(2)}) collective-permute-start(bf16[2,128,512]{2,1,0:T(8,128)(2,1)} %get-tuple-element.80.refs_0_), channel_id=1, source_target_pairs={{0,2},{1,3},{2,0},{3,1},{4,6},{5,7},{6,4},{7,5},{8,10},{9,11},{10,... | collective-permute-start | bytes 786440 | tf_op jit(solution)/shard_map/ppermute | solution.py:349
  12.0 0.5 collective-permute-start.1
  12.5 4.4 %shard_map.138 = (f32[8,128,128]{2,1,0:T(8,128)}, f32[8,128,128]{2,1,0:T(8,128)}, f32[8,128,128]{2,1,0:T(8,128)}, f32[8,128,128]{2,1,0:T(8,128)}) custom-call(s32[1,16]{1,0:T(1,128)} %refs_0_.9, s32[1,16]{1,0:T(1,128)} %refs_1_.9, s32[6,1,8]{2,1,0:T(1,128)} %bitcast.35, s32[6,1,8]{2,1,0:T(1,128)} %bitcast.40, bf16[16,128,128]{2,1,0:T(8,128)(2,1)} %bitcast.21, ...), custom_call_target="tpu_custom_call" | custom-call | flops 1 | bytes 1 | tf_op jit(solution)/shard_map/pallas_call | solution.py:214
  16.9 1.2 add_convert_fusion.2
  18.1 1.6 %collective-permute-start.4 = (bf16[8,128,128]{2,1,0:T(8,128)(2,1)S(1)}, bf16[8,128,128]{2,1,0:T(8,128)(2,1)S(1)}, u32[]{:S(2)}, u32[]{:S(2)}) collective-permute-start(bf16[8,128,128]{2,1,0:T(8,128)(2,1)S(1)} %add_convert_fusion.2), channel_id=1, source_target_pairs={{0,8},{4,12},{8,0},{12,4},{16,24},{20,28},{24,16},{28,20},{1,9},{5... | collective-permute-start | bytes 786440 | tf_op jit(solution)/shard_map/ppermute | solution.py:349
  19.7 1.5 %collective-permute-start.6 = (bf16[8,128,128]{2,1,0:T(8,128)(2,1)}, bf16[8,128,128]{2,1,0:T(8,128)(2,1)S(1)}, u32[]{:S(2)}, u32[]{:S(2)}) collective-permute-start(bf16[8,128,128]{2,1,0:T(8,128)(2,1)} %get-tuple-element.71), channel_id=1, source_target_pairs={{0,4},{4,0},{8,12},{12,8},{16,20},{20,16},{24,28},{28,24},{1,5},{5... | collective-permute-start | bytes 786440 | tf_op jit(solution)/shard_map/ppermute | solution.py:349
  21.2 4.1 %collective-permute-done.4 = bf16[8,128,128]{2,1,0:T(8,128)(2,1)S(1)} collective-permute-done((bf16[8,128,128]{2,1,0:T(8,128)(2,1)S(1)}, bf16[8,128,128]{2,1,0:T(8,128)(2,1)S(1)}, u32[]{:S(2)}, u32[]{:S(2)}) %collective-permute-start.4) | collective-permute-done | bytes 262176 | tf_op jit(solution)/shard_map/ppermute | solution.py:349
  25.3 1.1 add_convert_fusion.1
  26.5 2.6 %collective-permute-start.5 = (bf16[8,128,128]{2,1,0:T(8,128)(2,1)S(1)}, bf16[8,128,128]{2,1,0:T(8,128)(2,1)S(1)}, u32[]{:S(2)}, u32[]{:S(2)}) collective-permute-start(bf16[8,128,128]{2,1,0:T(8,128)(2,1)S(1)} %add_convert_fusion.1), channel_id=1, source_target_pairs={{0,16},{4,20},{8,24},{12,28},{16,0},{20,4},{24,8},{28,12},{1,17},{... | collective-permute-start | bytes 786440 | tf_op jit(solution)/shard_map/ppermute | solution.py:349
  29.1 0.7 collective-permute-start.10
  29.8 1.5 %collective-permute-start = (bf16[8,128,128]{2,1,0:T(8,128)(2,1)}, bf16[8,128,128]{2,1,0:T(8,128)(2,1)S(1)}, u32[]{:S(2)}, u32[]{:S(2)}) collective-permute-start(bf16[8,128,128]{2,1,0:T(8,128)(2,1)} %get-tuple-element.63), channel_id=1, source_target_pairs={{0,4},{4,0},{8,12},{12,8},{16,20},{20,16},{24,28},{28,24},{1,5},{5... | collective-permute-start | bytes 786440 | tf_op jit(solution)/shard_map/ppermute | solution.py:349
  31.3 0.8 add_convert_fusion
  32.1 7.3 %collective-permute-done.5.refs_0_ = bf16[8,128,128]{2,1,0:T(8,128)(2,1)S(1)} collective-permute-done((bf16[8,128,128]{2,1,0:T(8,128)(2,1)S(1)}, bf16[8,128,128]{2,1,0:T(8,128)(2,1)S(1)}, u32[]{:S(2)}, u32[]{:S(2)}) %collective-permute-start.5) | collective-permute-done | bytes 262176 | tf_op jit(solution)/shard_map/ppermute | solution.py:349
  39.3 0.6 collective-permute-start.7
  40.0 0.2 copy.15.inv_ref
  40.3 0.6 collective-permute-start.9
  41.0 0.9 collective-permute-done.8.refs_5_
  41.9 4.6 %collective-permute-done.9.refs_6_ = bf16[2,2,128,128]{3,2,1,0:T(8,128)(2,1)S(1)} collective-permute-done((bf16[2,2,128,128]{3,2,1,0:T(8,128)(2,1)}, bf16[2,2,128,128]{3,2,1,0:T(8,128)(2,1)S(1)}, u32[]{:S(2)}, u32[]{:S(2)}) %collective-permute-start.9) | collective-permute-done | bytes 131104 | tf_op jit(solution)/shard_map/ppermute | solution.py:349
  46.5 0.2 collective-permute-done.7.refs_1_
  46.7 0.2 shard_map.141
  47.0 0.1 collective-permute-start.13
  47.0 0.8 collective-permute-start.14
  47.9 1.0 collective-permute-start.15
  48.9 0.1 dynamic_slice.3
  49.0 0.1 copy.16.inv_ref
  49.1 2.9 %collective-permute-done.14.refs_10_ = bf16[2,128,128]{2,1,0:T(8,128)(2,1)S(1)} collective-permute-done((bf16[2,128,128]{2,1,0:T(8,128)(2,1)S(1)}, bf16[2,128,128]{2,1,0:T(8,128)(2,1)S(1)}, u32[]{:S(2)}, u32[]{:S(2)}) %collective-permute-start.14) | collective-permute-done | bytes 65568 | tf_op jit(solution)/shard_map/ppermute | solution.py:349
  52.0 0.5 collective-permute-done.15.refs_11_
  52.5 1.3 %shard_map.142 = (bf16[5,256,128]{2,1,0:T(8,128)(2,1)S(1)}, bf16[5,256,128]{2,1,0:T(8,128)(2,1)S(1)}, bf16[5,256,128]{2,1,0:T(8,128)(2,1)S(1)}, bf16[256,128]{1,...) custom-call(f32[256,1]{1,0:T(8,128)S(1)} %copy.16.inv_ref, ...), custom_call_target="tpu_custom_call" | custom-call | flops 1 | bytes 1 | tf_op jit(solution)/shard_map/pallas_call | solution.py:233
  53.8 0.3 collective-permute-start.16
  54.1 0.8 collective-permute-start.17
  55.0 0.7 collective-permute-start.18
  55.7 3.1 %collective-permute-done.17 = bf16[256,128]{1,0:T(8,128)(2,1)S(1)} collective-permute-done((bf16[256,128]{1,0:T(8,128)(2,1)S(1)}, bf16[256,128]{1,0:T(8,128)(2,1)S(1)}, u32[]{:S(2)}, u32[]{:S(2)}) %collective-permute-start.17) | collective-permute-done | bytes 65568 | tf_op jit(solution)/shard_map/ppermute | solution.py:349
  58.8 0.6 collective-permute-done.18
  59.4 3.1 %collective-permute-start.19 = (bf16[8,128,128]{2,1,0:T(8,128)(2,1)S(1)}, bf16[8,128,128]{2,1,0:T(8,128)(2,1)S(1)}, u32[]{:S(2)}, u32[]{:S(2)}) collective-permute-start(bf16[8,128,128]{2,1,0:T(8,128)(2,1)S(1)} %bitcast.27), channel_id=1, source_target_pairs={{0,16},{4,20},{8,24},{12,28},{16,0},{20,4},{24,8},{28,12},{1,17},{... | collective-permute-start | bytes 786440 | tf_op jit(solution)/shard_map/ppermute | solution.py:349
  62.5 1.7 %collective-permute-start.20 = (bf16[8,128,128]{2,1,0:T(8,128)(2,1)S(1)}, bf16[8,128,128]{2,1,0:T(8,128)(2,1)S(1)}, u32[]{:S(2)}, u32[]{:S(2)}) collective-permute-start(bf16[8,128,128]{2,1,0:T(8,128)(2,1)S(1)} %bitcast.28), channel_id=1, source_target_pairs={{0,8},{4,12},{8,0},{12,4},{16,24},{20,28},{24,16},{28,20},{1,9},{5... | collective-permute-start | bytes 786440 | tf_op jit(solution)/shard_map/ppermute | solution.py:349
  64.3 1.5 %collective-permute-start.21 = (bf16[8,128,128]{2,1,0:T(8,128)(2,1)S(1)}, bf16[8,128,128]{2,1,0:T(8,128)(2,1)S(1)}, u32[]{:S(2)}, u32[]{:S(2)}) collective-permute-start(bf16[8,128,128]{2,1,0:T(8,128)(2,1)S(1)} %bitcast.29), channel_id=1, source_target_pairs={{0,4},{4,0},{8,12},{12,8},{16,20},{20,16},{24,28},{28,24},{1,5},{5... | collective-permute-start | bytes 786440 | tf_op jit(solution)/shard_map/ppermute | solution.py:349
  65.8 1.3 %collective-permute-start.23 = (bf16[5,256,128]{2,1,0:T(8,128)(2,1)S(1)}, bf16[5,256,128]{2,1,0:T(8,128)(2,1)S(1)}, u32[]{:S(2)}, u32[]{:S(2)}) collective-permute-start(bf16[5,256,128]{2,1,0:T(8,128)(2,1)S(1)} %get-tuple-element.101), channel_id=1, source_target_pairs={{0,2},{1,3},{2,0},{3,1},{4,6},{5,7},{6,4},{7,5},{8,10},{9,11},{10,... | collective-permute-start | bytes 983048 | tf_op jit(solution)/shard_map/ppermute | solution.py:349
  67.1 8.1 %collective-permute-done.19.refs_6_ = bf16[8,128,128]{2,1,0:T(8,128)(2,1)S(1)} collective-permute-done((bf16[8,128,128]{2,1,0:T(8,128)(2,1)S(1)}, bf16[8,128,128]{2,1,0:T(8,128)(2,1)S(1)}, u32[]{:S(2)}, u32[]{:S(2)}) %collective-permute-start.19) | collective-permute-done | bytes 262176 | tf_op jit(solution)/shard_map/ppermute | solution.py:349
  75.2 0.1 collective-permute-done.20.refs_8_
  75.3 1.1 collective-permute-done.23.refs_2_
  76.4 4.4 %collective-permute-done.24.refs_3_ = bf16[5,256,128]{2,1,0:T(8,128)(2,1)S(1)} collective-permute-done((bf16[5,256,128]{2,1,0:T(8,128)(2,1)S(1)}, bf16[5,256,128]{2,1,0:T(8,128)(2,1)S(1)}, u32[]{:S(2)}, u32[]{:S(2)}) %collective-permute-start.24) | collective-permute-done | bytes 327712 | tf_op jit(solution)/shard_map/ppermute | solution.py:349
  80.8 0.8 shard_map.143
  81.7 0.6 collective-permute-start.25
  82.2 5.7 %collective-permute-done.25 = bf16[4,32,512]{2,1,0:T(8,128)(2,1)S(1)} collective-permute-done((bf16[4,32,512]{2,1,0:T(8,128)(2,1)S(1)}, bf16[4,32,512]{2,1,0:T(8,128)(2,1)S(1)}, u32[]{:S(2)}, u32[]{:S(2)}) %collective-permute-start.25) | collective-permute-done | bytes 131104 | tf_op jit(solution)/shard_map/ppermute | solution.py:349
  88.0 0.3 collective-permute-start.26
  88.3 0.5 collective-permute-start.27
  88.8 1.8 %collective-permute-start.28 = (bf16[8,128,128]{2,1,0:T(8,128)(2,1)S(1)}, bf16[8,128,128]{2,1,0:T(8,128)(2,1)S(1)}, u32[]{:S(2)}, u32[]{:S(2)}) collective-permute-start(bf16[8,128,128]{2,1,0:T(8,128)(2,1)S(1)} %collective-permute-done.19.refs_6_), channel_id=1, source_target_pairs={{0,8},{4,12},{8,0},{12,4},{16,24},{20,28},{24,16},{28,20},{1,9},{5... | collective-permute-start | bytes 786440 | tf_op jit(solution)/shard_map/ppermute | solution.py:349
  90.5 3.8 %collective-permute-done.26 = bf16[4,32,512]{2,1,0:T(8,128)(2,1)S(1)} collective-permute-done((bf16[4,32,512]{2,1,0:T(8,128)(2,1)S(1)}, bf16[4,32,512]{2,1,0:T(8,128)(2,1)S(1)}, u32[]{:S(2)}, u32[]{:S(2)}) %collective-permute-start.26) | collective-permute-done | bytes 131104 | tf_op jit(solution)/shard_map/ppermute | solution.py:349
  94.4 2.0 %collective-permute-done.27.refs_9_ = bf16[8,128,128]{2,1,0:T(8,128)(2,1)S(1)} collective-permute-done((bf16[8,128,128]{2,1,0:T(8,128)(2,1)S(1)}, bf16[8,128,128]{2,1,0:T(8,128)(2,1)S(1)}, u32[]{:S(2)}, u32[]{:S(2)}) %collective-permute-start.27) | collective-permute-done | bytes 262176 | tf_op jit(solution)/shard_map/ppermute | solution.py:349
  96.4 2.7 %collective-permute-done.28.refs_8_ = bf16[8,128,128]{2,1,0:T(8,128)(2,1)S(1)} collective-permute-done((bf16[8,128,128]{2,1,0:T(8,128)(2,1)S(1)}, bf16[8,128,128]{2,1,0:T(8,128)(2,1)S(1)}, u32[]{:S(2)}, u32[]{:S(2)}) %collective-permute-start.28) | collective-permute-done | bytes 262176 | tf_op jit(solution)/shard_map/ppermute | solution.py:349
  99.2 0.6 collective-permute-start.29
  99.7 0.5 collective-permute-start.30
  100.2 1.5 %collective-permute-start.31 = (bf16[8,128,128]{2,1,0:T(8,128)(2,1)S(1)}, bf16[8,128,128]{2,1,0:T(8,128)(2,1)S(1)}, u32[]{:S(2)}, u32[]{:S(2)}) collective-permute-start(bf16[8,128,128]{2,1,0:T(8,128)(2,1)S(1)} %collective-permute-done.28.refs_8_), channel_id=1, source_target_pairs={{0,4},{4,0},{8,12},{12,8},{16,20},{20,16},{24,28},{28,24},{1,5},{5... | collective-permute-start | bytes 786440 | tf_op jit(solution)/shard_map/ppermute | solution.py:349
  101.8 0.7 shard_map.144
  102.5 4.8 %collective-permute-done.29 = bf16[4,32,512]{2,1,0:T(8,128)(2,1)S(1)} collective-permute-done((bf16[4,32,512]{2,1,0:T(8,128)(2,1)S(1)}, bf16[4,32,512]{2,1,0:T(8,128)(2,1)S(1)}, u32[]{:S(2)}, u32[]{:S(2)}) %collective-permute-start.29) | collective-permute-done | bytes 131104 | tf_op jit(solution)/shard_map/ppermute | solution.py:349
  107.4 1.6 %collective-permute-done.30.refs_7_ = bf16[8,128,128]{2,1,0:T(8,128)(2,1)S(1)} collective-permute-done((bf16[8,128,128]{2,1,0:T(8,128)(2,1)S(1)}, bf16[8,128,128]{2,1,0:T(8,128)(2,1)S(1)}, u32[]{:S(2)}, u32[]{:S(2)}) %collective-permute-start.30) | collective-permute-done | bytes 262176 | tf_op jit(solution)/shard_map/ppermute | solution.py:349
  109.0 3.4 %collective-permute-done.31.refs_9_ = bf16[8,128,128]{2,1,0:T(8,128)(2,1)S(1)} collective-permute-done((bf16[8,128,128]{2,1,0:T(8,128)(2,1)S(1)}, bf16[8,128,128]{2,1,0:T(8,128)(2,1)S(1)}, u32[]{:S(2)}, u32[]{:S(2)}) %collective-permute-start.31) | collective-permute-done | bytes 262176 | tf_op jit(solution)/shard_map/ppermute | solution.py:349
  112.4 0.5 collective-permute-start.32
  112.9 2.3 %shard_map.145.refs_10_ = f32[8,128,128]{2,1,0:T(8,128)S(1)} custom-call(s32[1,16]{1,0:T(1,128)S(1)} %copy-done.8, s32[1,16]{1,0:T(1,128)S(1)} %copy-done.9, s32[6,1,8]{2,1,0:T(1,128)S(1)} %bitcast.36, s32[6,1,8]{2,1,0:T(1,128)S(1)} %bitcast.41, bf16[16,128,128]{2,1,0:T(8,128)(2,1)S(1)} %bitcast.22, bf16[6,8,128,128]{3,2,1,0:T(8,128)(2,1)S(1)} %bitcast.17, ...), custom_call_target="tpu_custom_call" | custom-call | flops 1 | bytes 1 | tf_op jit(solution)/shard_map/pallas_call | solution.py:214
  115.2 2.8 %shard_map.146 = f32[8,128,128]{2,1,0:T(8,128)} custom-call(s32[1,16]{1,0:T(1,128)S(1)} %copy-done.8, s32[1,16]{1,0:T(1,128)S(1)} %copy-done.9, s32[6,1,8]{2,1,0:T(1,128)S(1)} %bitcast.37, s32[6,1,8]{2,1,0:T(1,128)S(1)} %bitcast.42, bf16[16,128,128]{2,1,0:T(8,128)(2,1)S(1)} %bitcast.23, bf16[6,8,128,128]{3,2,1,0:T(8,128)(2,1)S(1)} %bitcast.18, ...), custom_call_target="tpu_custom_call" | custom-call | flops 1 | bytes 1 | tf_op jit(solution)/shard_map/pallas_call | solution.py:214
  118.1 0.9 shard_map.147
  (50 shorter events, 0.4 us)
Async XLA Ops:
  3.5 13.3 %collective-permute-start.3 = (bf16[8,128,128]{2,1,0:T(8,128)(2,1)}, bf16[8,128,128]{2,1,0:T(8,128)(2,1)S(1)}, u32[]{:S(2)}, u32[]{:S(2)}) collective-permute-start(bf16[8,128,128]{2,1,0:T(8,128)(2,1)} %shard_map.139), channel_id=1, source_target_pairs={{0,4},{4,0},{8,12},{12,8},{16,20},{20,16},{24,28},{28,24},{1,5},{5... | collective-permute-start | bytes 786440 | tf_op jit(solution)/shard_map/ppermute | solution.py:349
  10.4 10.8 %collective-permute-start.2 = (bf16[2,128,512]{2,1,0:T(8,128)(2,1)}, bf16[2,128,512]{2,1,0:T(8,128)(2,1)S(1)}, u32[]{:S(2)}, u32[]{:S(2)}) collective-permute-start(bf16[2,128,512]{2,1,0:T(8,128)(2,1)} %get-tuple-element.80.refs_0_), channel_id=1, source_target_pairs={{0,2},{1,3},{2,0},{3,1},{4,6},{5,7},{6,4},{7,5},{8,10},{9,11},{10,... | collective-permute-start | bytes 786440 | tf_op jit(solution)/shard_map/ppermute | solution.py:349
  12.0 9.3 %collective-permute-start.1 = (bf16[8,128,128]{2,1,0:T(8,128)(2,1)}, bf16[8,128,128]{2,1,0:T(8,128)(2,1)S(1)}, u32[]{:S(2)}, u32[]{:S(2)}) collective-permute-start(bf16[8,128,128]{2,1,0:T(8,128)(2,1)} %get-tuple-element.65), channel_id=1, source_target_pairs={{0,4},{4,0},{8,12},{12,8},{16,20},{20,16},{24,28},{28,24},{1,5},{5... | collective-permute-start | bytes 786440 | tf_op jit(solution)/shard_map/ppermute | solution.py:349
  16.8 12.3 %copy-start.4 = (bf16[2,128,512]{2,1,0:T(8,128)(2,1)S(1)}, bf16[2,128,512]{2,1,0:T(8,128)(2,1)}, u32[]{:S(2)}) copy-start(bf16[2,128,512]{2,1,0:T(8,128)(2,1)} %get-tuple-element.80.refs_0_) | copy-start | bytes 786436
  16.8 14.5 %copy-start.11 = (f32[8,128,128]{2,1,0:T(8,128)S(1)}, f32[8,128,128]{2,1,0:T(8,128)}, u32[]{:S(2)}) copy-start(f32[8,128,128]{2,1,0:T(8,128)} %get-tuple-element.70) | copy-start | bytes 1572868
  16.9 23.1 %copy-start.12 = (s32[1024]{0:T(1024)S(1)}, s32[1024]{0:T(1024)}, u32[]{:S(2)}) copy-start(s32[1024]{0:T(1024)} %param.14) | copy-start | bytes 12292
  18.0 22.9 %copy-start.10 = (f32[8,128,128]{2,1,0:T(8,128)S(1)}, f32[8,128,128]{2,1,0:T(8,128)}, u32[]{:S(2)}) copy-start(f32[8,128,128]{2,1,0:T(8,128)} %get-tuple-element.61) | copy-start | bytes 1572868
  18.1 7.3 %collective-permute-start.4 = (bf16[8,128,128]{2,1,0:T(8,128)(2,1)S(1)}, bf16[8,128,128]{2,1,0:T(8,128)(2,1)S(1)}, u32[]{:S(2)}, u32[]{:S(2)}) collective-permute-start(bf16[8,128,128]{2,1,0:T(8,128)(2,1)S(1)} %add_convert_fusion.2), channel_id=1, source_target_pairs={{0,8},{4,12},{8,0},{12,4},{16,24},{20,28},{24,16},{28,20},{1,9},{5... | collective-permute-start | bytes 786440 | tf_op jit(solution)/shard_map/ppermute | solution.py:349
  19.7 11.6 %collective-permute-start.6 = (bf16[8,128,128]{2,1,0:T(8,128)(2,1)}, bf16[8,128,128]{2,1,0:T(8,128)(2,1)S(1)}, u32[]{:S(2)}, u32[]{:S(2)}) collective-permute-start(bf16[8,128,128]{2,1,0:T(8,128)(2,1)} %get-tuple-element.71), channel_id=1, source_target_pairs={{0,4},{4,0},{8,12},{12,8},{16,20},{20,16},{24,28},{28,24},{1,5},{5... | collective-permute-start | bytes 786440 | tf_op jit(solution)/shard_map/ppermute | solution.py:349
  26.5 12.9 %collective-permute-start.5 = (bf16[8,128,128]{2,1,0:T(8,128)(2,1)S(1)}, bf16[8,128,128]{2,1,0:T(8,128)(2,1)S(1)}, u32[]{:S(2)}, u32[]{:S(2)}) collective-permute-start(bf16[8,128,128]{2,1,0:T(8,128)(2,1)S(1)} %add_convert_fusion.1), channel_id=1, source_target_pairs={{0,16},{4,20},{8,24},{12,28},{16,0},{20,4},{24,8},{28,12},{1,17},{... | collective-permute-start | bytes 786440 | tf_op jit(solution)/shard_map/ppermute | solution.py:349
  29.1 17.3 %collective-permute-start.11 = (bf16[2,128,512]{2,1,0:T(8,128)(2,1)S(1)}, bf16[2,128,512]{2,1,0:T(8,128)(2,1)S(1)}, u32[]{:S(2)}, u32[]{:S(2)}) collective-permute-start(bf16[2,128,512]{2,1,0:T(8,128)(2,1)S(1)} %copy-done.4), channel_id=1, source_target_pairs={{0,1},{1,0},{2,3},{3,2},{4,5},{5,4},{6,7},{7,6},{8,9},{9,8},{10,11... | collective-permute-start | bytes 786440 | tf_op jit(solution)/shard_map/ppermute | solution.py:349
  29.1 11.1 %collective-permute-start.10 = (bf16[2,2,128,128]{3,2,1,0:T(8,128)(2,1)}, bf16[2,2,128,128]{3,2,1,0:T(8,128)(2,1)S(1)}, u32[]{:S(2)}, u32[]{:S(2)}) collective-permute-start(bf16[2,2,128,128]{3,2,1,0:T(8,128)(2,1)} %get-tuple-element.76), channel_id=1, source_target_pairs={{0,3},{1,2},{2,1},{3,0},{4,7},{5,6},{6,5},{7,4},{8,11},{9,10},{10,... | collective-permute-start | bytes 393224 | tf_op jit(solution)/shard_map/ppermute | solution.py:349
  29.8 10.5 %collective-permute-start = (bf16[8,128,128]{2,1,0:T(8,128)(2,1)}, bf16[8,128,128]{2,1,0:T(8,128)(2,1)S(1)}, u32[]{:S(2)}, u32[]{:S(2)}) collective-permute-start(bf16[8,128,128]{2,1,0:T(8,128)(2,1)} %get-tuple-element.63), channel_id=1, source_target_pairs={{0,4},{4,0},{8,12},{12,8},{16,20},{20,16},{24,28},{28,24},{1,5},{5... | collective-permute-start | bytes 786440 | tf_op jit(solution)/shard_map/ppermute | solution.py:349
  31.3 15.2 %collective-permute-start.12 = (bf16[2,128,512]{2,1,0:T(8,128)(2,1)S(1)}, bf16[2,128,512]{2,1,0:T(8,128)(2,1)S(1)}, u32[]{:S(2)}, u32[]{:S(2)}) collective-permute-start(bf16[2,128,512]{2,1,0:T(8,128)(2,1)S(1)} %collective-permute-done.2.refs_2_), channel_id=1, source_target_pairs={{0,1},{1,0},{2,3},{3,2},{4,5},{5,4},{6,7},{7,6},{8,9},{9,8},{10,11... | collective-permute-start | bytes 786440 | tf_op jit(solution)/shard_map/ppermute | solution.py:349
  39.3 7.4 %collective-permute-start.7 = (bf16[8,128,128]{2,1,0:T(8,128)(2,1)}, bf16[8,128,128]{2,1,0:T(8,128)(2,1)S(1)}, u32[]{:S(2)}, u32[]{:S(2)}) collective-permute-start(bf16[8,128,128]{2,1,0:T(8,128)(2,1)} %add_convert_fusion), channel_id=1, source_target_pairs={{0,8},{4,12},{8,0},{12,4},{16,24},{20,28},{24,16},{28,20},{1,9},{5... | collective-permute-start | bytes 786440 | tf_op jit(solution)/shard_map/ppermute | solution.py:349
  40.2 12.3 %copy-start.5 = (bf16[2,2,128,128]{3,2,1,0:T(8,128)(2,1)S(1)}, bf16[2,2,128,128]{3,2,1,0:T(8,128)(2,1)}, u32[]{:S(2)}) copy-start(bf16[2,2,128,128]{3,2,1,0:T(8,128)(2,1)} %get-tuple-element.84.refs_4_) | copy-start | bytes 393220
  40.2 1.6 %collective-permute-start.8 = (bf16[2,2,128,128]{3,2,1,0:T(8,128)(2,1)}, bf16[2,2,128,128]{3,2,1,0:T(8,128)(2,1)S(1)}, u32[]{:S(2)}, u32[]{:S(2)}) collective-permute-start(bf16[2,2,128,128]{3,2,1,0:T(8,128)(2,1)} %get-tuple-element.74), channel_id=1, source_target_pairs={{0,1},{1,0},{2,3},{3,2},{4,5},{5,4},{6,7},{7,6},{8,9},{9,8},{10,11... | collective-permute-start | bytes 393224 | tf_op jit(solution)/shard_map/ppermute | solution.py:349
  40.3 6.1 %collective-permute-start.9 = (bf16[2,2,128,128]{3,2,1,0:T(8,128)(2,1)}, bf16[2,2,128,128]{3,2,1,0:T(8,128)(2,1)S(1)}, u32[]{:S(2)}, u32[]{:S(2)}) collective-permute-start(bf16[2,2,128,128]{3,2,1,0:T(8,128)(2,1)} %get-tuple-element.75), channel_id=1, source_target_pairs={{0,2},{1,3},{2,0},{3,1},{4,6},{5,7},{6,4},{7,5},{8,10},{9,11},{10,... | collective-permute-start | bytes 393224 | tf_op jit(solution)/shard_map/ppermute | solution.py:349
  46.9 33.9 %copy-start.2 = (bf16[1024,128]{1,0:T(8,128)(2,1)S(1)}, bf16[1024,128]{1,0:T(8,128)(2,1)}, u32[]{:S(2)}) copy-start(bf16[1024,128]{1,0:T(8,128)(2,1)} %f_ref.1) | copy-start | bytes 786436
  47.0 33.8 %copy-start.3 = (bf16[128,512]{1,0:T(8,128)(2,1)S(1)}, bf16[128,512]{1,0:T(8,128)(2,1)}, u32[]{:S(2)}) copy-start(bf16[128,512]{1,0:T(8,128)(2,1)} %w_ref.1) | copy-start | bytes 393220
  47.0 2.2 %collective-permute-start.13 = (bf16[2,128,128]{2,1,0:T(8,128)(2,1)S(1)}, bf16[2,128,128]{2,1,0:T(8,128)(2,1)S(1)}, u32[]{:S(2)}, u32[]{:S(2)}) collective-permute-start(bf16[2,128,128]{2,1,0:T(8,128)(2,1)S(1)} %get-tuple-element.89), channel_id=1, source_target_pairs={{0,1},{1,0},{2,3},{3,2},{4,5},{5,4},{6,7},{7,6},{8,9},{9,8},{10,11... | collective-permute-start | bytes 196616 | tf_op jit(solution)/shard_map/ppermute | solution.py:349
  47.0 5.0 %collective-permute-start.14 = (bf16[2,128,128]{2,1,0:T(8,128)(2,1)S(1)}, bf16[2,128,128]{2,1,0:T(8,128)(2,1)S(1)}, u32[]{:S(2)}, u32[]{:S(2)}) collective-permute-start(bf16[2,128,128]{2,1,0:T(8,128)(2,1)S(1)} %get-tuple-element.90), channel_id=1, source_target_pairs={{0,2},{1,3},{2,0},{3,1},{4,6},{5,7},{6,4},{7,5},{8,10},{9,11},{10,... | collective-permute-start | bytes 196616 | tf_op jit(solution)/shard_map/ppermute | solution.py:349
  47.9 4.6 %collective-permute-start.15 = (bf16[2,128,128]{2,1,0:T(8,128)(2,1)S(1)}, bf16[2,128,128]{2,1,0:T(8,128)(2,1)S(1)}, u32[]{:S(2)}, u32[]{:S(2)}) collective-permute-start(bf16[2,128,128]{2,1,0:T(8,128)(2,1)S(1)} %get-tuple-element.91), channel_id=1, source_target_pairs={{0,3},{1,2},{2,1},{3,0},{4,7},{5,6},{6,5},{7,4},{8,11},{9,10},{10,... | collective-permute-start | bytes 196616 | tf_op jit(solution)/shard_map/ppermute | solution.py:349
  53.8 1.9 %collective-permute-start.16 = (bf16[256,128]{1,0:T(8,128)(2,1)S(1)}, bf16[256,128]{1,0:T(8,128)(2,1)S(1)}, u32[]{:S(2)}, u32[]{:S(2)}) collective-permute-start(bf16[256,128]{1,0:T(8,128)(2,1)S(1)} %get-tuple-element.96), channel_id=1, source_target_pairs={{0,1},{1,0},{2,3},{3,2},{4,5},{5,4},{6,7},{7,6},{8,9},{9,8},{10,11... | collective-permute-start | bytes 196616 | tf_op jit(solution)/shard_map/ppermute | solution.py:349
  54.1 4.7 %collective-permute-start.17 = (bf16[256,128]{1,0:T(8,128)(2,1)S(1)}, bf16[256,128]{1,0:T(8,128)(2,1)S(1)}, u32[]{:S(2)}, u32[]{:S(2)}) collective-permute-start(bf16[256,128]{1,0:T(8,128)(2,1)S(1)} %get-tuple-element.97), channel_id=1, source_target_pairs={{0,2},{1,3},{2,0},{3,1},{4,6},{5,7},{6,4},{7,5},{8,10},{9,11},{10,... | collective-permute-start | bytes 196616 | tf_op jit(solution)/shard_map/ppermute | solution.py:349
  55.0 4.4 %collective-permute-start.18 = (bf16[256,128]{1,0:T(8,128)(2,1)S(1)}, bf16[256,128]{1,0:T(8,128)(2,1)S(1)}, u32[]{:S(2)}, u32[]{:S(2)}) collective-permute-start(bf16[256,128]{1,0:T(8,128)(2,1)S(1)} %get-tuple-element.98), channel_id=1, source_target_pairs={{0,3},{1,2},{2,1},{3,0},{4,7},{5,6},{6,5},{7,4},{8,11},{9,10},{10,... | collective-permute-start | bytes 196616 | tf_op jit(solution)/shard_map/ppermute | solution.py:349
  59.4 15.9 %collective-permute-start.19 = (bf16[8,128,128]{2,1,0:T(8,128)(2,1)S(1)}, bf16[8,128,128]{2,1,0:T(8,128)(2,1)S(1)}, u32[]{:S(2)}, u32[]{:S(2)}) collective-permute-start(bf16[8,128,128]{2,1,0:T(8,128)(2,1)S(1)} %bitcast.27), channel_id=1, source_target_pairs={{0,16},{4,20},{8,24},{12,28},{16,0},{20,4},{24,8},{28,12},{1,17},{... | collective-permute-start | bytes 786440 | tf_op jit(solution)/shard_map/ppermute | solution.py:349
  62.5 12.8 %collective-permute-start.20 = (bf16[8,128,128]{2,1,0:T(8,128)(2,1)S(1)}, bf16[8,128,128]{2,1,0:T(8,128)(2,1)S(1)}, u32[]{:S(2)}, u32[]{:S(2)}) collective-permute-start(bf16[8,128,128]{2,1,0:T(8,128)(2,1)S(1)} %bitcast.28), channel_id=1, source_target_pairs={{0,8},{4,12},{8,0},{12,4},{16,24},{20,28},{24,16},{28,20},{1,9},{5... | collective-permute-start | bytes 786440 | tf_op jit(solution)/shard_map/ppermute | solution.py:349
  64.3 11.0 %collective-permute-start.21 = (bf16[8,128,128]{2,1,0:T(8,128)(2,1)S(1)}, bf16[8,128,128]{2,1,0:T(8,128)(2,1)S(1)}, u32[]{:S(2)}, u32[]{:S(2)}) collective-permute-start(bf16[8,128,128]{2,1,0:T(8,128)(2,1)S(1)} %bitcast.29), channel_id=1, source_target_pairs={{0,4},{4,0},{8,12},{12,8},{16,20},{20,16},{24,28},{28,24},{1,5},{5... | collective-permute-start | bytes 786440 | tf_op jit(solution)/shard_map/ppermute | solution.py:349
  65.8 10.6 %collective-permute-start.23 = (bf16[5,256,128]{2,1,0:T(8,128)(2,1)S(1)}, bf16[5,256,128]{2,1,0:T(8,128)(2,1)S(1)}, u32[]{:S(2)}, u32[]{:S(2)}) collective-permute-start(bf16[5,256,128]{2,1,0:T(8,128)(2,1)S(1)} %get-tuple-element.101), channel_id=1, source_target_pairs={{0,2},{1,3},{2,0},{3,1},{4,6},{5,7},{6,4},{7,5},{8,10},{9,11},{10,... | collective-permute-start | bytes 983048 | tf_op jit(solution)/shard_map/ppermute | solution.py:349
  67.1 13.7 %collective-permute-start.24 = (bf16[5,256,128]{2,1,0:T(8,128)(2,1)S(1)}, bf16[5,256,128]{2,1,0:T(8,128)(2,1)S(1)}, u32[]{:S(2)}, u32[]{:S(2)}) collective-permute-start(bf16[5,256,128]{2,1,0:T(8,128)(2,1)S(1)} %get-tuple-element.102), channel_id=1, source_target_pairs={{0,3},{1,2},{2,1},{3,0},{4,7},{5,6},{6,5},{7,4},{8,11},{9,10},{10,... | collective-permute-start | bytes 983048 | tf_op jit(solution)/shard_map/ppermute | solution.py:349
  75.3 5.5 %collective-permute-start.22 = (bf16[5,256,128]{2,1,0:T(8,128)(2,1)S(1)}, bf16[5,256,128]{2,1,0:T(8,128)(2,1)S(1)}, u32[]{:S(2)}, u32[]{:S(2)}) collective-permute-start(bf16[5,256,128]{2,1,0:T(8,128)(2,1)S(1)} %get-tuple-element.100.refs_0_), channel_id=1, source_target_pairs={{0,1},{1,0},{2,3},{3,2},{4,5},{5,4},{6,7},{7,6},{8,9},{9,8},{10,11... | collective-permute-start | bytes 983048 | tf_op jit(solution)/shard_map/ppermute | solution.py:349
  81.6 31.3 %copy-start = (bf16[1,6,8,128,128]{4,3,2,1,0:T(8,128)(2,1)S(1)}, bf16[1,6,8,128,128]{4,3,2,1,0:T(8,128)(2,1)}, u32[]{:S(2)}) copy-start(bf16[1,6,8,128,128]{4,3,2,1,0:T(8,128)(2,1)} %param.18) | copy-start | bytes 4718596
  81.6 31.3 %copy-start.1 = (bf16[1,16,128,128]{3,2,1,0:T(8,128)(2,1)S(1)}, bf16[1,16,128,128]{3,2,1,0:T(8,128)(2,1)}, u32[]{:S(2)}) copy-start(bf16[1,16,128,128]{3,2,1,0:T(8,128)(2,1)} %param.15) | copy-start | bytes 1572868
  81.6 31.3 %copy-start.6 = (s32[1,6,8]{2,0,1:T(1,128)S(1)}, s32[1,6,8]{2,0,1:T(1,128)}, u32[]{:S(2)}) copy-start(s32[1,6,8]{2,0,1:T(1,128)} %param.19) | copy-start | bytes 580
  81.6 31.3 %copy-start.7 = (s32[1,6,8]{2,0,1:T(1,128)S(1)}, s32[1,6,8]{2,0,1:T(1,128)}, u32[]{:S(2)}) copy-start(s32[1,6,8]{2,0,1:T(1,128)} %param.20) | copy-start | bytes 580
  81.7 31.3 %copy-start.8 = (s32[1,16]{1,0:T(1,128)S(1)}, s32[1,16]{1,0:T(1,128)}, u32[]{:S(2)}) copy-start(s32[1,16]{1,0:T(1,128)} %refs_0_.9) | copy-start | bytes 196
  81.7 31.3 %copy-start.9 = (s32[1,16]{1,0:T(1,128)S(1)}, s32[1,16]{1,0:T(1,128)}, u32[]{:S(2)}) copy-start(s32[1,16]{1,0:T(1,128)} %refs_1_.9) | copy-start | bytes 196
  81.7 6.3 %collective-permute-start.25 = (bf16[4,32,512]{2,1,0:T(8,128)(2,1)S(1)}, bf16[4,32,512]{2,1,0:T(8,128)(2,1)S(1)}, u32[]{:S(2)}, u32[]{:S(2)}) collective-permute-start(bf16[4,32,512]{2,1,0:T(8,128)(2,1)S(1)} %get-tuple-element.107), channel_id=1, source_target_pairs={{0,4},{4,0},{8,12},{12,8},{16,20},{20,16},{24,28},{28,24},{1,5},{5... | collective-permute-start | bytes 393224 | tf_op jit(solution)/shard_map/ppermute | solution.py:349
  88.0 6.4 %collective-permute-start.26 = (bf16[4,32,512]{2,1,0:T(8,128)(2,1)S(1)}, bf16[4,32,512]{2,1,0:T(8,128)(2,1)S(1)}, u32[]{:S(2)}, u32[]{:S(2)}) collective-permute-start(bf16[4,32,512]{2,1,0:T(8,128)(2,1)S(1)} %add_convert_fusion.5), channel_id=1, source_target_pairs={{0,8},{4,12},{8,0},{12,4},{16,24},{20,28},{24,16},{28,20},{1,9},{5... | collective-permute-start | bytes 393224 | tf_op jit(solution)/shard_map/ppermute | solution.py:349
  88.3 8.2 %collective-permute-start.27 = (bf16[8,128,128]{2,1,0:T(8,128)(2,1)S(1)}, bf16[8,128,128]{2,1,0:T(8,128)(2,1)S(1)}, u32[]{:S(2)}, u32[]{:S(2)}) collective-permute-start(bf16[8,128,128]{2,1,0:T(8,128)(2,1)S(1)} %collective-permute-done.20.refs_8_), channel_id=1, source_target_pairs={{0,4},{4,0},{8,12},{12,8},{16,20},{20,16},{24,28},{28,24},{1,5},{5... | collective-permute-start | bytes 786440 | tf_op jit(solution)/shard_map/ppermute | solution.py:349
  88.8 10.4 %collective-permute-start.28 = (bf16[8,128,128]{2,1,0:T(8,128)(2,1)S(1)}, bf16[8,128,128]{2,1,0:T(8,128)(2,1)S(1)}, u32[]{:S(2)}, u32[]{:S(2)}) collective-permute-start(bf16[8,128,128]{2,1,0:T(8,128)(2,1)S(1)} %collective-permute-done.19.refs_6_), channel_id=1, source_target_pairs={{0,8},{4,12},{8,0},{12,4},{16,24},{20,28},{24,16},{28,20},{1,9},{5... | collective-permute-start | bytes 786440 | tf_op jit(solution)/shard_map/ppermute | solution.py:349
  99.2 8.2 %collective-permute-start.29 = (bf16[4,32,512]{2,1,0:T(8,128)(2,1)S(1)}, bf16[4,32,512]{2,1,0:T(8,128)(2,1)S(1)}, u32[]{:S(2)}, u32[]{:S(2)}) collective-permute-start(bf16[4,32,512]{2,1,0:T(8,128)(2,1)S(1)} %add_convert_fusion.4), channel_id=1, source_target_pairs={{0,16},{4,20},{8,24},{12,28},{16,0},{20,4},{24,8},{28,12},{1,17},{... | collective-permute-start | bytes 393224 | tf_op jit(solution)/shard_map/ppermute | solution.py:349
  99.7 9.2 %collective-permute-start.30 = (bf16[8,128,128]{2,1,0:T(8,128)(2,1)S(1)}, bf16[8,128,128]{2,1,0:T(8,128)(2,1)S(1)}, u32[]{:S(2)}, u32[]{:S(2)}) collective-permute-start(bf16[8,128,128]{2,1,0:T(8,128)(2,1)S(1)} %collective-permute-done.19.refs_6_), channel_id=1, source_target_pairs={{0,4},{4,0},{8,12},{12,8},{16,20},{20,16},{24,28},{28,24},{1,5},{5... | collective-permute-start | bytes 786440 | tf_op jit(solution)/shard_map/ppermute | solution.py:349
  100.2 12.2 %collective-permute-start.31 = (bf16[8,128,128]{2,1,0:T(8,128)(2,1)S(1)}, bf16[8,128,128]{2,1,0:T(8,128)(2,1)S(1)}, u32[]{:S(2)}, u32[]{:S(2)}) collective-permute-start(bf16[8,128,128]{2,1,0:T(8,128)(2,1)S(1)} %collective-permute-done.28.refs_8_), channel_id=1, source_target_pairs={{0,4},{4,0},{8,12},{12,8},{16,20},{20,16},{24,28},{28,24},{1,5},{5... | collective-permute-start | bytes 786440 | tf_op jit(solution)/shard_map/ppermute | solution.py:349
  112.4 5.7 %collective-permute-start.32 = (bf16[4,32,512]{2,1,0:T(8,128)(2,1)S(1)}, bf16[4,32,512]{2,1,0:T(8,128)(2,1)S(1)}, u32[]{:S(2)}, u32[]{:S(2)}) collective-permute-start(bf16[4,32,512]{2,1,0:T(8,128)(2,1)S(1)} %add_convert_fusion.3.mine_ref), channel_id=1, source_target_pairs={{0,4},{4,0},{8,12},{12,8},{16,20},{20,16},{24,28},{28,24},{1,5},{5... | collective-permute-start | bytes 393224 | tf_op jit(solution)/shard_map/ppermute | solution.py:349

commit v9 on v7

--- a/solution.py
+++ b/solution.py
@@ -118,22 +118,17 @@
     return ((block_id // per_feat) ^ mine) * per_feat + block_id % per_feat
 
 
-def tile_groups(masks, offsets, parts_total, me, groups, tiles, ids):
-    ldst, lsrc, rdst, rsrc = ids
+def tile_groups(masks, offsets, parts_total, me, groups, tiles):
     jobs = []
     for at, mask in enumerate(masks):
         if mask == 0:
             for first in range(0, tiles, groups):
                 count = min(groups, tiles - first)
-                dst = [ldst[0, first + k] for k in range(count)]
-                src = [lsrc[0, first + k] for k in range(count)]
-                jobs.append((at, None, None, first, dst, src))
+                jobs.append((at, None, None, first, count))
         else:
             offset = lax.rem((me ^ mask) - me + parts_total, parts_total)
             step, known = round_of(offset, offsets)
-            dst = [rdst[step, 0, k] for k in range(groups)]
-            src = [rsrc[step, 0, k] for k in range(groups)]
-            jobs.append((at, step, known, None, dst, src))
+            jobs.append((at, step, known, None, groups))
     return jobs
 
 
@@ -142,17 +137,23 @@
 
 
 def tiles_kernel(masks, offsets, parts_total, back, feats, extras, *refs):
-    ids, (lvals, rvals), refs = refs[:4], refs[4:6], refs[6:]
+    ids_in, (lvals, rvals), refs = refs[:4], refs[4:6], refs[6:]
+    ids, id_sems, refs = refs[-5:-1], refs[-1], refs[:-5]
+    id_copies = [
+        pltpu.make_async_copy(ids_in[n], ids[n], id_sems.at[n]) for n in range(len(ids))
+    ]
+    for copy in id_copies:
+        copy.start()
     groups_of, masks = masks, flat(masks)
     me = lax.axis_index("dom")
     mine = lax.axis_index("feat")
     rounds, groups, tiles = tile_counts(rvals, lvals)
-    jobs = tile_groups(masks, offsets, parts_total, me, groups, tiles, ids)
+    jobs = tile_groups(masks, offsets, parts_total, me, groups, tiles)
     held, prod, acc, sems = refs[-4:]
     copies = []
-    for slot, (at, step, known, first, dst, src) in enumerate(jobs):
-        source = lvals.at[pl.ds(first, len(dst))] if step is None else rvals.at[step]
-        copy = pltpu.make_async_copy(source, held.at[slot, pl.ds(0, len(dst))], sems.at[slot])
+    for slot, (at, step, known, first, count) in enumerate(jobs):
+        source = lvals.at[pl.ds(first, count)] if step is None else rvals.at[step]
+        copy = pltpu.make_async_copy(source, held.at[slot, pl.ds(0, count)], sems.at[slot])
         copy.start()
         copies.append(copy)
     if back:
@@ -178,8 +179,17 @@
             piece[0] = refs[0][rows]
             piece[1] = refs[1][rows]
     total = 0
-    for slot, (at, step, known, first, dst, src) in enumerate(jobs):
+    for copy in id_copies:
+        copy.wait()
+    ldst, lsrc, rdst, rsrc = ids
+    for slot, (at, step, known, first, count) in enumerate(jobs):
         copies[slot].wait()
+        if step is None:
+            dst = [ldst[0, first + k] for k in range(count)]
+            src = [lsrc[0, first + k] for k in range(count)]
+        else:
+            dst = [rdst[step, 0, k] for k in range(count)]
+            src = [rsrc[step, 0, k] for k in range(count)]
         half = slot % 2
         for k in range(len(dst)):
             if back:
@@ -214,8 +224,7 @@
     return pl.pallas_call(
         functools.partial(tiles_kernel, masks, offsets, parts_total, back, feats, extras),
         out_shape=sinks,
-        in_specs=[SMEM] * 4
-        + [pl.BlockSpec(memory_space=pltpu.HBM)] * 2
+        in_specs=[pl.BlockSpec(memory_space=pltpu.HBM)] * 6
         + [VMEM] * len(blocks),
         out_specs=jax.tree.map(lambda _: VMEM, sinks),
         scratch_shapes=[
@@ -223,6 +232,8 @@
             pltpu.VMEM((2, groups, block, width), F32),
             pltpu.VMEM((2, nblocks, block, width), F32),
             pltpu.SemaphoreType.DMA((slots,)),
+            *[pltpu.SMEM(t.shape, jnp.int32) for t in ids],
+            pltpu.SemaphoreType.DMA((len(ids),)),
         ],
         compiler_params=pltpu.CompilerParams(vmem_limit_bytes=room * 2**20),
         cost_estimate=pl.CostEstimate(flops=1, bytes_accessed=1, transcendentals=0),
@@ -403,15 +414,16 @@
     def tied(x, *others):
         return lax.optimization_barrier((x, others))[0]
 
+    sends = forward([7, 3, 5, 1], [blocks], [like(shape, BF16)] * 4)
     made = forward(
-        [7, 3, 5, 1],
+        [6, 2, 4, 0],
         [blocks, cotangent.reshape(shape), w_self, w_neigh],
-        [like(shape, BF16)] * 4
+        [like(shape, F32)] * 4
         + [like((2, per_feat, block, width), BF16)] * feats
         + [like((2, width, full), BF16)],
     )
-    sends, early_pieces, pair = made[:4], made[4:-1], made[-1]
-    keep_6, keep_2, keep_4, keep = forward([6, 2, 4, 0], [blocks], [like(shape, F32)] * 4)
+    keep_6, keep_2, keep_4, keep = made[:4]
+    early_pieces, pair = made[4:-1], made[-1]
     weights = relayed(pair)
     early = [early_pieces[0]] + [crossed(early_pieces[m], m, "feat") for m in range(1, feats)]
     near_6, near_2, near_4, near_0 = (crossed(send, near) for send in sends)
@@ -454,8 +466,8 @@
     dpre = [sent[0], *come]
     found[6] = crossed(found[4], 2)
     found[3] = crossed(found[2], near)
-    found[5] = crossed(found[1], 4)
-    found[7] = crossed(found[6], near)
+    found[5] = crossed(found[4], near)
+    found[7] = crossed(found[5], 2)
     piece = 2 * width // parts_total
     dx_self, give, keep = small_call(
         functools.partial(grad_kernel, feats),
@@ -468,16 +480,10 @@
         [pltpu.VMEM((parts_total, piece, full), F32)],
     )
     total = (keep + crossed(give, near).astype(F32)).astype(BF16)
-    total = tied(total, found[3], found[5], found[6])
+    total = tied(total, found[5], found[6])
     total = (total.astype(F32) + crossed(total, 2).astype(F32)).astype(BF16)
+    total = tied(total, found[3], found[7])
     total = (total.astype(F32) + crossed(total, 4).astype(F32)).astype(BF16)
-    total, out = tied((total, out), found[7])
-    grad_self, grad_neigh = small_call(
-        finish_kernel,
-        [like((width, full), F32)] * 2,
-        [total, crossed(total, near)],
-        [pltpu.VMEM((parts_total, piece, full), F32)],
-    )
     grad_x = dx_self.reshape(shape)
     half = parts_total // 2
     for order in (list(range(half)), list(range(half, parts_total))):
@@ -492,6 +498,13 @@
             like(shape, F32),
             24,
         )
+    total, out, grad_x = lax.optimization_barrier((total, out, grad_x))
+    grad_self, grad_neigh = small_call(
+        finish_kernel,
+        [like((width, full), F32)] * 2,
+        [total, crossed(total, near)],
+        [pltpu.VMEM((parts_total, piece, full), F32)],
+    )
     return (out.reshape(rows, width), grad_x.reshape(rows, width), grad_self, grad_neigh)
 
 

time: 118 us -> 116 us (0.983)
  waiting for transfers between devices: 63.3 us -> 59.1 us
  starting transfers between devices: 32 us -> 34.9 us
    ppermute x33, waiting for transfers between devices: 63.3 us -> 59.1 us  [crossed(): lax.ppermute(x, axis, [(i, i ^ mask) for i in range(lax.axis_size(axis))])]
    ppermute x33, starting transfers between devices: 32 us -> 34.9 us  [crossed(): lax.ppermute(x, axis, [(i, i ^ mask) for i in range(lax.axis_size(axis))])]
  transfers between devices with their start and end apart: 33 -> 33, of which waited for: 17 -> 19; matrix products, arithmetic and copies ran while one was open for 3% -> 3% of each run, Pallas kernels for 9% -> 9%
where the time goes in v9:
time: 116 us
  waiting for transfers between devices  59.1 us (51%)
  starting transfers between devices  34.9 us (30%)
  Pallas kernels  17.1 us (15%)
  other arithmetic  3.17 us (3%)
    ppermute x33, waiting for transfers between devices, crossed(): lax.ppermute(x, axis, [(i, i ^ mask) for i in range(lax.axis_size(axis))])  59.1 us
    ppermute x33, starting transfers between devices, crossed(): lax.ppermute(x, axis, [(i, i ^ mask) for i in range(lax.axis_size(axis))])  34.9 us
    pallas_call x4, Pallas kernels, tiles_call(): pl.pallas_call(functools.partial(tiles_kernel, masks, offsets, parts_tota...  13.3 us
    pallas_call x5, Pallas kernels, small_call(): pl.pallas_call(kernel, out_shape=outs, in_specs=[VMEM] * len(arrays), out...  3.86 us
  transfers between devices with their start and end apart: 33, of which 19 were waited for; matrix products, arithmetic and copies ran while one was open for 3% of the time, Pallas kernels for 9%

profile of v9, /device:TPU:0, one launch (start us, length us, event | category | flops | bytes accessed | tf_op | source)
XLA Modules:
  0.0 115.7 jit_solution(348403652739457541)
XLA Ops:
  0.6 3.8 %shard_map.139 = (bf16[8,128,128]{2,1,0:T(8,128)(2,1)}, bf16[8,128,128]{2,1,0:T(8,128)(2,1)}, bf16[8,128,128]{2,1,0:T(8,128)(2,1)}, bf16[8,128,128]{2,1,0:T(8,128)(2,1)}) custom-call(s32[1,16]{1,0:T(1,128)} %refs_0_.7, s32[1,16]{1,0:T(1,128)} %refs_1_.7, s32[6,1,8]{2,1,0:T(1,128)} %bitcast.30, s32[6,1,8]{2,1,0:T(1,128)} %bitcast.34, ...), custom_call_target="tpu_custom_call" | custom-call | flops 1 | bytes 1 | tf_op jit(solution)/shard_map/pallas_call | solution.py:224
  4.4 3.0 %collective-permute-start.1 = (bf16[8,128,128]{2,1,0:T(8,128)(2,1)}, bf16[8,128,128]{2,1,0:T(8,128)(2,1)S(1)}, u32[]{:S(2)}, u32[]{:S(2)}) collective-permute-start(bf16[8,128,128]{2,1,0:T(8,128)(2,1)} %get-tuple-element.66), channel_id=1, source_target_pairs={{0,4},{4,0},{8,12},{12,8},{16,20},{20,16},{24,28},{28,24},{1,5},{5... | collective-permute-start | bytes 786440 | tf_op jit(solution)/shard_map/ppermute | solution.py:360
  7.4 0.1 collective-permute-start.9
  7.5 4.8 %shard_map.138 = (f32[8,128,128]{2,1,0:T(8,128)}, f32[8,128,128]{2,1,0:T(8,128)}, f32[8,128,128]{2,1,0:T(8,128)}, f32[8,128,128]{2,1,0:T(8,128)}, bf16[2,2,128,1...) custom-call(s32[1,16]{1,0:T(1,128)} %refs_0_.7, ...), custom_call_target="tpu_custom_call" | custom-call | flops 1 | bytes 1 | tf_op jit(solution)/shard_map/pallas_call | solution.py:224
  12.3 2.0 %collective-permute-start.3 = (bf16[2,128,512]{2,1,0:T(8,128)(2,1)}, bf16[2,128,512]{2,1,0:T(8,128)(2,1)S(1)}, u32[]{:S(2)}, u32[]{:S(2)}) collective-permute-start(bf16[2,128,512]{2,1,0:T(8,128)(2,1)} %get-tuple-element.82.refs_0_), channel_id=1, source_target_pairs={{0,2},{1,3},{2,0},{3,1},{4,6},{5,7},{6,4},{7,5},{8,10},{9,11},{10,... | collective-permute-start | bytes 786440 | tf_op jit(solution)/shard_map/ppermute | solution.py:360
  14.3 1.5 %collective-permute-start = (bf16[8,128,128]{2,1,0:T(8,128)(2,1)}, bf16[8,128,128]{2,1,0:T(8,128)(2,1)S(1)}, u32[]{:S(2)}, u32[]{:S(2)}) collective-permute-start(bf16[8,128,128]{2,1,0:T(8,128)(2,1)} %get-tuple-element.64), channel_id=1, source_target_pairs={{0,4},{4,0},{8,12},{12,8},{16,20},{20,16},{24,28},{28,24},{1,5},{5... | collective-permute-start | bytes 786440 | tf_op jit(solution)/shard_map/ppermute | solution.py:360
  15.8 1.1 add_convert_fusion.2
  17.0 1.6 %collective-permute-start.2 = (bf16[8,128,128]{2,1,0:T(8,128)(2,1)S(1)}, bf16[8,128,128]{2,1,0:T(8,128)(2,1)S(1)}, u32[]{:S(2)}, u32[]{:S(2)}) collective-permute-start(bf16[8,128,128]{2,1,0:T(8,128)(2,1)S(1)} %add_convert_fusion.2), channel_id=1, source_target_pairs={{0,8},{4,12},{8,0},{12,4},{16,24},{20,28},{24,16},{28,20},{1,9},{5... | collective-permute-start | bytes 786440 | tf_op jit(solution)/shard_map/ppermute | solution.py:360
  18.6 1.8 %collective-permute-done.9 = bf16[8,128,128]{2,1,0:T(8,128)(2,1)S(1)} collective-permute-done((bf16[8,128,128]{2,1,0:T(8,128)(2,1)}, bf16[8,128,128]{2,1,0:T(8,128)(2,1)S(1)}, u32[]{:S(2)}, u32[]{:S(2)}) %collective-permute-start.9) | collective-permute-done | bytes 262176 | tf_op jit(solution)/shard_map/ppermute | solution.py:360
  20.4 1.1 add_convert_fusion.1
  21.5 2.2 %collective-permute-start.10 = (bf16[8,128,128]{2,1,0:T(8,128)(2,1)S(1)}, bf16[8,128,128]{2,1,0:T(8,128)(2,1)S(1)}, u32[]{:S(2)}, u32[]{:S(2)}) collective-permute-start(bf16[8,128,128]{2,1,0:T(8,128)(2,1)S(1)} %add_convert_fusion.1), channel_id=1, source_target_pairs={{0,8},{4,12},{8,0},{12,4},{16,24},{20,28},{24,16},{28,20},{1,9},{5... | collective-permute-start | bytes 786440 | tf_op jit(solution)/shard_map/ppermute | solution.py:360
  23.7 0.5 collective-permute-start.4
  24.2 1.0 collective-permute-done
  25.2 1.7 %collective-permute-start.5 = (bf16[2,2,128,128]{3,2,1,0:T(8,128)(2,1)}, bf16[2,2,128,128]{3,2,1,0:T(8,128)(2,1)S(1)}, u32[]{:S(2)}, u32[]{:S(2)}) collective-permute-start(bf16[2,2,128,128]{3,2,1,0:T(8,128)(2,1)} %get-tuple-element.71), channel_id=1, source_target_pairs={{0,2},{1,3},{2,0},{3,1},{4,6},{5,7},{6,4},{7,5},{8,10},{9,11},{10,... | collective-permute-start | bytes 393224 | tf_op jit(solution)/shard_map/ppermute | solution.py:360
  26.9 1.5 %collective-permute-start.12 = (bf16[8,128,128]{2,1,0:T(8,128)(2,1)}, bf16[8,128,128]{2,1,0:T(8,128)(2,1)S(1)}, u32[]{:S(2)}, u32[]{:S(2)}) collective-permute-start(bf16[8,128,128]{2,1,0:T(8,128)(2,1)} %get-tuple-element.78), channel_id=1, source_target_pairs={{0,4},{4,0},{8,12},{12,8},{16,20},{20,16},{24,28},{28,24},{1,5},{5... | collective-permute-start | bytes 786440 | tf_op jit(solution)/shard_map/ppermute | solution.py:360
  28.4 1.2 %collective-permute-done.10 = bf16[8,128,128]{2,1,0:T(8,128)(2,1)S(1)} collective-permute-done((bf16[8,128,128]{2,1,0:T(8,128)(2,1)S(1)}, bf16[8,128,128]{2,1,0:T(8,128)(2,1)S(1)}, u32[]{:S(2)}, u32[]{:S(2)}) %collective-permute-start.10) | collective-permute-done | bytes 262176 | tf_op jit(solution)/shard_map/ppermute | solution.py:360
  29.6 0.8 add_convert_fusion
  30.4 2.6 %collective-permute-start.11 = (bf16[8,128,128]{2,1,0:T(8,128)(2,1)}, bf16[8,128,128]{2,1,0:T(8,128)(2,1)S(1)}, u32[]{:S(2)}, u32[]{:S(2)}) collective-permute-start(bf16[8,128,128]{2,1,0:T(8,128)(2,1)} %add_convert_fusion), channel_id=1, source_target_pairs={{0,16},{4,20},{8,24},{12,28},{16,0},{20,4},{24,8},{28,12},{1,17},{... | collective-permute-start | bytes 786440 | tf_op jit(solution)/shard_map/ppermute | solution.py:360
  33.0 0.2 copy.15.inv_ref
  33.2 0.4 collective-permute-start.6
  33.7 5.1 %collective-permute-done.6.refs_7_ = bf16[2,2,128,128]{3,2,1,0:T(8,128)(2,1)S(1)} collective-permute-done((bf16[2,2,128,128]{3,2,1,0:T(8,128)(2,1)S(1)}, bf16[2,2,128,128]{3,2,1,0:T(8,128)(2,1)S(1)}, u32[]{:S(2)}, u32[]{:S(2)}) %collective-permute-start.6) | collective-permute-done | bytes 131104 | tf_op jit(solution)/shard_map/ppermute | solution.py:360
  38.8 7.0 %collective-permute-done.11.refs_0_ = bf16[8,128,128]{2,1,0:T(8,128)(2,1)S(1)} collective-permute-done((bf16[8,128,128]{2,1,0:T(8,128)(2,1)}, bf16[8,128,128]{2,1,0:T(8,128)(2,1)S(1)}, u32[]{:S(2)}, u32[]{:S(2)}) %collective-permute-start.11) | collective-permute-done | bytes 262176 | tf_op jit(solution)/shard_map/ppermute | solution.py:360
  45.8 0.2 shard_map.140
  46.1 0.1 collective-permute-start.13
  46.2 0.6 collective-permute-start.14
  46.8 1.3 %collective-permute-start.15 = (bf16[2,128,128]{2,1,0:T(8,128)(2,1)S(1)}, bf16[2,128,128]{2,1,0:T(8,128)(2,1)S(1)}, u32[]{:S(2)}, u32[]{:S(2)}) collective-permute-start(bf16[2,128,128]{2,1,0:T(8,128)(2,1)S(1)} %get-tuple-element.93), channel_id=1, source_target_pairs={{0,3},{1,2},{2,1},{3,0},{4,7},{5,6},{6,5},{7,4},{8,11},{9,10},{10,... | collective-permute-start | bytes 196616 | tf_op jit(solution)/shard_map/ppermute | solution.py:360
  48.0 0.1 dynamic_slice.3
  48.1 0.1 copy.16.inv_ref
  48.3 2.9 %collective-permute-done.14.refs_10_ = bf16[2,128,128]{2,1,0:T(8,128)(2,1)S(1)} collective-permute-done((bf16[2,128,128]{2,1,0:T(8,128)(2,1)S(1)}, bf16[2,128,128]{2,1,0:T(8,128)(2,1)S(1)}, u32[]{:S(2)}, u32[]{:S(2)}) %collective-permute-start.14) | collective-permute-done | bytes 65568 | tf_op jit(solution)/shard_map/ppermute | solution.py:360
  51.1 0.5 collective-permute-done.15.refs_11_
  51.6 1.3 %shard_map.141 = (bf16[5,256,128]{2,1,0:T(8,128)(2,1)S(1)}, bf16[5,256,128]{2,1,0:T(8,128)(2,1)S(1)}, bf16[5,256,128]{2,1,0:T(8,128)(2,1)S(1)}, bf16[256,128]{1,...) custom-call(f32[256,1]{1,0:T(8,128)S(1)} %copy.16.inv_ref, ...), custom_call_target="tpu_custom_call" | custom-call | flops 1 | bytes 1 | tf_op jit(solution)/shard_map/pallas_call | solution.py:244
  52.9 0.3 collective-permute-start.16
  53.2 0.6 collective-permute-start.17
  53.8 1.0 collective-permute-start.18
  54.8 3.4 %collective-permute-done.17 = bf16[256,128]{1,0:T(8,128)(2,1)S(1)} collective-permute-done((bf16[256,128]{1,0:T(8,128)(2,1)S(1)}, bf16[256,128]{1,0:T(8,128)(2,1)S(1)}, u32[]{:S(2)}, u32[]{:S(2)}) %collective-permute-start.17) | collective-permute-done | bytes 65568 | tf_op jit(solution)/shard_map/ppermute | solution.py:360
  58.2 0.0 collective-permute-done.18
  58.3 0.1 collective-permute-start.19
  58.4 4.0 %collective-permute-start.20 = (bf16[8,128,128]{2,1,0:T(8,128)(2,1)S(1)}, bf16[8,128,128]{2,1,0:T(8,128)(2,1)S(1)}, u32[]{:S(2)}, u32[]{:S(2)}) collective-permute-start(bf16[8,128,128]{2,1,0:T(8,128)(2,1)S(1)} %bitcast.25), channel_id=1, source_target_pairs={{0,8},{4,12},{8,0},{12,4},{16,24},{20,28},{24,16},{28,20},{1,9},{5... | collective-permute-start | bytes 786440 | tf_op jit(solution)/shard_map/ppermute | solution.py:360
  62.4 1.3 %collective-permute-start.21 = (bf16[8,128,128]{2,1,0:T(8,128)(2,1)S(1)}, bf16[8,128,128]{2,1,0:T(8,128)(2,1)S(1)}, u32[]{:S(2)}, u32[]{:S(2)}) collective-permute-start(bf16[8,128,128]{2,1,0:T(8,128)(2,1)S(1)} %bitcast.26), channel_id=1, source_target_pairs={{0,4},{4,0},{8,12},{12,8},{16,20},{20,16},{24,28},{28,24},{1,5},{5... | collective-permute-start | bytes 786440 | tf_op jit(solution)/shard_map/ppermute | solution.py:360
  63.7 0.7 collective-permute-start.23
  64.4 9.3 %collective-permute-done.19.refs_6_ = bf16[8,128,128]{2,1,0:T(8,128)(2,1)S(1)} collective-permute-done((bf16[8,128,128]{2,1,0:T(8,128)(2,1)S(1)}, bf16[8,128,128]{2,1,0:T(8,128)(2,1)S(1)}, u32[]{:S(2)}, u32[]{:S(2)}) %collective-permute-start.19) | collective-permute-done | bytes 262176 | tf_op jit(solution)/shard_map/ppermute | solution.py:360
  73.7 0.1 collective-permute-done.20.refs_8_
  73.8 0.5 collective-permute-done.23.refs_2_
  74.3 3.9 %collective-permute-done.24.refs_3_ = bf16[5,256,128]{2,1,0:T(8,128)(2,1)S(1)} collective-permute-done((bf16[5,256,128]{2,1,0:T(8,128)(2,1)S(1)}, bf16[5,256,128]{2,1,0:T(8,128)(2,1)S(1)}, u32[]{:S(2)}, u32[]{:S(2)}) %collective-permute-start.24) | collective-permute-done | bytes 327712 | tf_op jit(solution)/shard_map/ppermute | solution.py:360
  78.2 0.8 shard_map.142
  79.0 1.3 %collective-permute-start.25 = (bf16[4,32,512]{2,1,0:T(8,128)(2,1)S(1)}, bf16[4,32,512]{2,1,0:T(8,128)(2,1)S(1)}, u32[]{:S(2)}, u32[]{:S(2)}) collective-permute-start(bf16[4,32,512]{2,1,0:T(8,128)(2,1)S(1)} %get-tuple-element.109), channel_id=1, source_target_pairs={{0,4},{4,0},{8,12},{12,8},{16,20},{20,16},{24,28},{28,24},{1,5},{5... | collective-permute-start | bytes 393224 | tf_op jit(solution)/shard_map/ppermute | solution.py:360
  80.3 0.8 collective-permute-start.26
  81.1 0.3 collective-permute-start.27
  81.4 3.8 %collective-permute-done.25 = bf16[4,32,512]{2,1,0:T(8,128)(2,1)S(1)} collective-permute-done((bf16[4,32,512]{2,1,0:T(8,128)(2,1)S(1)}, bf16[4,32,512]{2,1,0:T(8,128)(2,1)S(1)}, u32[]{:S(2)}, u32[]{:S(2)}) %collective-permute-start.25) | collective-permute-done | bytes 131104 | tf_op jit(solution)/shard_map/ppermute | solution.py:360
  85.2 5.6 %collective-permute-done.26.refs_7_ = bf16[8,128,128]{2,1,0:T(8,128)(2,1)S(1)} collective-permute-done((bf16[8,128,128]{2,1,0:T(8,128)(2,1)S(1)}, bf16[8,128,128]{2,1,0:T(8,128)(2,1)S(1)}, u32[]{:S(2)}, u32[]{:S(2)}) %collective-permute-start.26) | collective-permute-done | bytes 262176 | tf_op jit(solution)/shard_map/ppermute | solution.py:360
  90.8 0.3 collective-permute-start.28
  91.1 1.6 %collective-permute-start.29 = (bf16[8,128,128]{2,1,0:T(8,128)(2,1)S(1)}, bf16[8,128,128]{2,1,0:T(8,128)(2,1)S(1)}, u32[]{:S(2)}, u32[]{:S(2)}) collective-permute-start(bf16[8,128,128]{2,1,0:T(8,128)(2,1)S(1)} %collective-permute-done.20.refs_8_), channel_id=1, source_target_pairs={{0,4},{4,0},{8,12},{12,8},{16,20},{20,16},{24,28},{28,24},{1,5},{5... | collective-permute-start | bytes 786440 | tf_op jit(solution)/shard_map/ppermute | solution.py:360
  92.8 1.4 %collective-permute-start.30 = (bf16[8,128,128]{2,1,0:T(8,128)(2,1)S(1)}, bf16[8,128,128]{2,1,0:T(8,128)(2,1)S(1)}, u32[]{:S(2)}, u32[]{:S(2)}) collective-permute-start(bf16[8,128,128]{2,1,0:T(8,128)(2,1)S(1)} %collective-permute-done.26.refs_7_), channel_id=1, source_target_pairs={{0,8},{4,12},{8,0},{12,4},{16,24},{20,28},{24,16},{28,20},{1,9},{5... | collective-permute-start | bytes 786440 | tf_op jit(solution)/shard_map/ppermute | solution.py:360
  94.1 3.0 %collective-permute-done.28 = bf16[4,32,512]{2,1,0:T(8,128)(2,1)S(1)} collective-permute-done((bf16[4,32,512]{2,1,0:T(8,128)(2,1)S(1)}, bf16[4,32,512]{2,1,0:T(8,128)(2,1)S(1)}, u32[]{:S(2)}, u32[]{:S(2)}) %collective-permute-start.28) | collective-permute-done | bytes 131104 | tf_op jit(solution)/shard_map/ppermute | solution.py:360
  97.2 1.9 %collective-permute-done.29.refs_9_ = bf16[8,128,128]{2,1,0:T(8,128)(2,1)S(1)} collective-permute-done((bf16[8,128,128]{2,1,0:T(8,128)(2,1)S(1)}, bf16[8,128,128]{2,1,0:T(8,128)(2,1)S(1)}, u32[]{:S(2)}, u32[]{:S(2)}) %collective-permute-start.29) | collective-permute-done | bytes 262176 | tf_op jit(solution)/shard_map/ppermute | solution.py:360
  99.2 2.8 %collective-permute-done.30.refs_9_ = bf16[8,128,128]{2,1,0:T(8,128)(2,1)S(1)} collective-permute-done((bf16[8,128,128]{2,1,0:T(8,128)(2,1)S(1)}, bf16[8,128,128]{2,1,0:T(8,128)(2,1)S(1)}, u32[]{:S(2)}, u32[]{:S(2)}) %collective-permute-start.30) | collective-permute-done | bytes 262176 | tf_op jit(solution)/shard_map/ppermute | solution.py:360
  102.0 0.4 collective-permute-start.31
  102.4 2.1 %shard_map.144.refs_10_ = f32[8,128,128]{2,1,0:T(8,128)S(1)} custom-call(s32[1,16]{1,0:T(1,128)S(1)} %copy-done.8, s32[1,16]{1,0:T(1,128)S(1)} %copy-done.9, s32[6,1,8]{2,1,0:T(1,128)S(1)} %bitcast.32, s32[6,1,8]{2,1,0:T(1,128)S(1)} %bitcast.36, bf16[16,128,128]{2,1,0:T(8,128)(2,1)S(1)} %bitcast.20, bf16[6,8,128,128]{3,2,1,0:T(8,128)(2,1)S(1)} %bitcast.16, ...), custom_call_target="tpu_custom_call" | custom-call | flops 1 | bytes 1 | tf_op jit(solution)/shard_map/pallas_call | solution.py:224
  104.5 0.7 shard_map.143
  105.2 2.6 %shard_map.145 = f32[8,128,128]{2,1,0:T(8,128)} custom-call(s32[1,16]{1,0:T(1,128)S(1)} %copy-done.8, s32[1,16]{1,0:T(1,128)S(1)} %copy-done.9, s32[6,1,8]{2,1,0:T(1,128)S(1)} %bitcast.33, s32[6,1,8]{2,1,0:T(1,128)S(1)} %bitcast.37, bf16[16,128,128]{2,1,0:T(8,128)(2,1)S(1)} %bitcast.21, bf16[6,8,128,128]{3,2,1,0:T(8,128)(2,1)S(1)} %bitcast.17, ...), custom_call_target="tpu_custom_call" | custom-call | flops 1 | bytes 1 | tf_op jit(solution)/shard_map/pallas_call | solution.py:224
  107.8 1.9 %collective-permute-done.31 = bf16[4,32,512]{2,1,0:T(8,128)(2,1)S(1)} collective-permute-done((bf16[4,32,512]{2,1,0:T(8,128)(2,1)S(1)}, bf16[4,32,512]{2,1,0:T(8,128)(2,1)S(1)}, u32[]{:S(2)}, u32[]{:S(2)}) %collective-permute-start.31) | collective-permute-done | bytes 131104 | tf_op jit(solution)/shard_map/ppermute | solution.py:360
  109.8 1.7 %collective-permute-start.32 = (bf16[4,32,512]{2,1,0:T(8,128)(2,1)S(1)}, bf16[4,32,512]{2,1,0:T(8,128)(2,1)S(1)}, u32[]{:S(2)}, u32[]{:S(2)}) collective-permute-start(bf16[4,32,512]{2,1,0:T(8,128)(2,1)S(1)} %add_convert_fusion.3.mine_ref), channel_id=1, source_target_pairs={{0,4},{4,0},{8,12},{12,8},{16,20},{20,16},{24,28},{28,24},{1,5},{5... | collective-permute-start | bytes 393224 | tf_op jit(solution)/shard_map/ppermute | solution.py:360
  111.5 3.3 %collective-permute-done.32.other_ref = bf16[4,32,512]{2,1,0:T(8,128)(2,1)S(1)} collective-permute-done((bf16[4,32,512]{2,1,0:T(8,128)(2,1)S(1)}, bf16[4,32,512]{2,1,0:T(8,128)(2,1)S(1)}, u32[]{:S(2)}, u32[]{:S(2)}) %collective-permute-start.32) | collective-permute-done | bytes 131104 | tf_op jit(solution)/shard_map/ppermute | solution.py:360
  114.8 0.9 shard_map.146
  (53 shorter events, 0.3 us)
Async XLA Ops:
  4.4 11.4 %collective-permute-start.1 = (bf16[8,128,128]{2,1,0:T(8,128)(2,1)}, bf16[8,128,128]{2,1,0:T(8,128)(2,1)S(1)}, u32[]{:S(2)}, u32[]{:S(2)}) collective-permute-start(bf16[8,128,128]{2,1,0:T(8,128)(2,1)} %get-tuple-element.66), channel_id=1, source_target_pairs={{0,4},{4,0},{8,12},{12,8},{16,20},{20,16},{24,28},{28,24},{1,5},{5... | collective-permute-start | bytes 786440 | tf_op jit(solution)/shard_map/ppermute | solution.py:360
  7.4 13.0 %collective-permute-start.9 = (bf16[8,128,128]{2,1,0:T(8,128)(2,1)}, bf16[8,128,128]{2,1,0:T(8,128)(2,1)S(1)}, u32[]{:S(2)}, u32[]{:S(2)}) collective-permute-start(bf16[8,128,128]{2,1,0:T(8,128)(2,1)} %get-tuple-element.77), channel_id=1, source_target_pairs={{0,4},{4,0},{8,12},{12,8},{16,20},{20,16},{24,28},{28,24},{1,5},{5... | collective-permute-start | bytes 786440 | tf_op jit(solution)/shard_map/ppermute | solution.py:360
  12.3 11.4 %copy-start.4 = (bf16[2,128,512]{2,1,0:T(8,128)(2,1)S(1)}, bf16[2,128,512]{2,1,0:T(8,128)(2,1)}, u32[]{:S(2)}) copy-start(bf16[2,128,512]{2,1,0:T(8,128)(2,1)} %get-tuple-element.82.refs_0_) | copy-start | bytes 786436
  12.3 11.4 %copy-start.14 = (bf16[2,2,128,128]{3,2,1,0:T(8,128)(2,1)S(1)}, bf16[2,2,128,128]{3,2,1,0:T(8,128)(2,1)}, u32[]{:S(2)}) copy-start(bf16[2,2,128,128]{3,2,1,0:T(8,128)(2,1)} %get-tuple-element.70) | copy-start | bytes 393220
  12.3 17.3 %copy-start.11 = (f32[8,128,128]{2,1,0:T(8,128)S(1)}, f32[8,128,128]{2,1,0:T(8,128)}, u32[]{:S(2)}) copy-start(f32[8,128,128]{2,1,0:T(8,128)} %get-tuple-element.74) | copy-start | bytes 1572868
  12.3 11.4 %collective-permute-start.3 = (bf16[2,128,512]{2,1,0:T(8,128)(2,1)}, bf16[2,128,512]{2,1,0:T(8,128)(2,1)S(1)}, u32[]{:S(2)}, u32[]{:S(2)}) collective-permute-start(bf16[2,128,512]{2,1,0:T(8,128)(2,1)} %get-tuple-element.82.refs_0_), channel_id=1, source_target_pairs={{0,2},{1,3},{2,0},{3,1},{4,6},{5,7},{6,4},{7,5},{8,10},{9,11},{10,... | collective-permute-start | bytes 786440 | tf_op jit(solution)/shard_map/ppermute | solution.py:360
  14.3 10.9 %collective-permute-start = (bf16[8,128,128]{2,1,0:T(8,128)(2,1)}, bf16[8,128,128]{2,1,0:T(8,128)(2,1)S(1)}, u32[]{:S(2)}, u32[]{:S(2)}) collective-permute-start(bf16[8,128,128]{2,1,0:T(8,128)(2,1)} %get-tuple-element.64), channel_id=1, source_target_pairs={{0,4},{4,0},{8,12},{12,8},{16,20},{20,16},{24,28},{28,24},{1,5},{5... | collective-permute-start | bytes 786440 | tf_op jit(solution)/shard_map/ppermute | solution.py:360
  15.8 17.1 %copy-start.12 = (s32[1024]{0:T(1024)S(1)}, s32[1024]{0:T(1024)}, u32[]{:S(2)}) copy-start(s32[1024]{0:T(1024)} %param.14) | copy-start | bytes 12292
  17.0 16.3 %copy-start.13 = (bf16[2,2,128,128]{3,2,1,0:T(8,128)(2,1)S(1)}, bf16[2,2,128,128]{3,2,1,0:T(8,128)(2,1)}, u32[]{:S(2)}) copy-start(bf16[2,2,128,128]{3,2,1,0:T(8,128)(2,1)} %get-tuple-element.72) | copy-start | bytes 393220
  17.0 16.7 %copy-start.10 = (f32[8,128,128]{2,1,0:T(8,128)S(1)}, f32[8,128,128]{2,1,0:T(8,128)}, u32[]{:S(2)}) copy-start(f32[8,128,128]{2,1,0:T(8,128)} %get-tuple-element.63) | copy-start | bytes 1572868
  17.0 9.9 %collective-permute-start.2 = (bf16[8,128,128]{2,1,0:T(8,128)(2,1)S(1)}, bf16[8,128,128]{2,1,0:T(8,128)(2,1)S(1)}, u32[]{:S(2)}, u32[]{:S(2)}) collective-permute-start(bf16[8,128,128]{2,1,0:T(8,128)(2,1)S(1)} %add_convert_fusion.2), channel_id=1, source_target_pairs={{0,8},{4,12},{8,0},{12,4},{16,24},{20,28},{24,16},{28,20},{1,9},{5... | collective-permute-start | bytes 786440 | tf_op jit(solution)/shard_map/ppermute | solution.py:360
  21.5 8.1 %collective-permute-start.10 = (bf16[8,128,128]{2,1,0:T(8,128)(2,1)S(1)}, bf16[8,128,128]{2,1,0:T(8,128)(2,1)S(1)}, u32[]{:S(2)}, u32[]{:S(2)}) collective-permute-start(bf16[8,128,128]{2,1,0:T(8,128)(2,1)S(1)} %add_convert_fusion.1), channel_id=1, source_target_pairs={{0,8},{4,12},{8,0},{12,4},{16,24},{20,28},{24,16},{28,20},{1,9},{5... | collective-permute-start | bytes 786440 | tf_op jit(solution)/shard_map/ppermute | solution.py:360
  23.7 15.1 %collective-permute-start.7 = (bf16[2,128,512]{2,1,0:T(8,128)(2,1)S(1)}, bf16[2,128,512]{2,1,0:T(8,128)(2,1)S(1)}, u32[]{:S(2)}, u32[]{:S(2)}) collective-permute-start(bf16[2,128,512]{2,1,0:T(8,128)(2,1)S(1)} %copy-done.4), channel_id=1, source_target_pairs={{0,1},{1,0},{2,3},{3,2},{4,5},{5,4},{6,7},{7,6},{8,9},{9,8},{10,11... | collective-permute-start | bytes 786440 | tf_op jit(solution)/shard_map/ppermute | solution.py:360
  23.7 6.7 %collective-permute-start.4 = (bf16[2,2,128,128]{3,2,1,0:T(8,128)(2,1)S(1)}, bf16[2,2,128,128]{3,2,1,0:T(8,128)(2,1)S(1)}, u32[]{:S(2)}, u32[]{:S(2)}) collective-permute-start(bf16[2,2,128,128]{3,2,1,0:T(8,128)(2,1)S(1)} %copy-done.14), channel_id=1, source_target_pairs={{0,1},{1,0},{2,3},{3,2},{4,5},{5,4},{6,7},{7,6},{8,9},{9,8},{10,11... | collective-permute-start | bytes 393224 | tf_op jit(solution)/shard_map/ppermute | solution.py:360
  25.2 8.1 %collective-permute-start.5 = (bf16[2,2,128,128]{3,2,1,0:T(8,128)(2,1)}, bf16[2,2,128,128]{3,2,1,0:T(8,128)(2,1)S(1)}, u32[]{:S(2)}, u32[]{:S(2)}) collective-permute-start(bf16[2,2,128,128]{3,2,1,0:T(8,128)(2,1)} %get-tuple-element.71), channel_id=1, source_target_pairs={{0,2},{1,3},{2,0},{3,1},{4,6},{5,7},{6,4},{7,5},{8,10},{9,11},{10,... | collective-permute-start | bytes 393224 | tf_op jit(solution)/shard_map/ppermute | solution.py:360
  26.9 11.9 %collective-permute-start.12 = (bf16[8,128,128]{2,1,0:T(8,128)(2,1)}, bf16[8,128,128]{2,1,0:T(8,128)(2,1)S(1)}, u32[]{:S(2)}, u32[]{:S(2)}) collective-permute-start(bf16[8,128,128]{2,1,0:T(8,128)(2,1)} %get-tuple-element.78), channel_id=1, source_target_pairs={{0,4},{4,0},{8,12},{12,8},{16,20},{20,16},{24,28},{28,24},{1,5},{5... | collective-permute-start | bytes 786440 | tf_op jit(solution)/shard_map/ppermute | solution.py:360
  29.6 9.2 %collective-permute-start.8 = (bf16[2,128,512]{2,1,0:T(8,128)(2,1)S(1)}, bf16[2,128,512]{2,1,0:T(8,128)(2,1)S(1)}, u32[]{:S(2)}, u32[]{:S(2)}) collective-permute-start(bf16[2,128,512]{2,1,0:T(8,128)(2,1)S(1)} %collective-permute-done.3.refs_2_), channel_id=1, source_target_pairs={{0,1},{1,0},{2,3},{3,2},{4,5},{5,4},{6,7},{7,6},{8,9},{9,8},{10,11... | collective-permute-start | bytes 786440 | tf_op jit(solution)/shard_map/ppermute | solution.py:360
  30.4 15.4 %collective-permute-start.11 = (bf16[8,128,128]{2,1,0:T(8,128)(2,1)}, bf16[8,128,128]{2,1,0:T(8,128)(2,1)S(1)}, u32[]{:S(2)}, u32[]{:S(2)}) collective-permute-start(bf16[8,128,128]{2,1,0:T(8,128)(2,1)} %add_convert_fusion), channel_id=1, source_target_pairs={{0,16},{4,20},{8,24},{12,28},{16,0},{20,4},{24,8},{28,12},{1,17},{... | collective-permute-start | bytes 786440 | tf_op jit(solution)/shard_map/ppermute | solution.py:360
  33.2 18.4 %copy-start.5 = (bf16[2,2,128,128]{3,2,1,0:T(8,128)(2,1)S(1)}, bf16[2,2,128,128]{3,2,1,0:T(8,128)(2,1)}, u32[]{:S(2)}) copy-start(bf16[2,2,128,128]{3,2,1,0:T(8,128)(2,1)} %get-tuple-element.86.refs_4_) | copy-start | bytes 393220
  33.2 5.5 %collective-permute-start.6 = (bf16[2,2,128,128]{3,2,1,0:T(8,128)(2,1)S(1)}, bf16[2,2,128,128]{3,2,1,0:T(8,128)(2,1)S(1)}, u32[]{:S(2)}, u32[]{:S(2)}) collective-permute-start(bf16[2,2,128,128]{3,2,1,0:T(8,128)(2,1)S(1)} %copy-done.13), channel_id=1, source_target_pairs={{0,3},{1,2},{2,1},{3,0},{4,7},{5,6},{6,5},{7,4},{8,11},{9,10},{10,... | collective-permute-start | bytes 393224 | tf_op jit(solution)/shard_map/ppermute | solution.py:360
  46.1 32.2 %copy-start.2 = (bf16[1024,128]{1,0:T(8,128)(2,1)S(1)}, bf16[1024,128]{1,0:T(8,128)(2,1)}, u32[]{:S(2)}) copy-start(bf16[1024,128]{1,0:T(8,128)(2,1)} %f_ref.1) | copy-start | bytes 786436
  46.1 32.1 %copy-start.3 = (bf16[128,512]{1,0:T(8,128)(2,1)S(1)}, bf16[128,512]{1,0:T(8,128)(2,1)}, u32[]{:S(2)}) copy-start(bf16[128,512]{1,0:T(8,128)(2,1)} %w_ref.1) | copy-start | bytes 393220
  46.1 2.2 %collective-permute-start.13 = (bf16[2,128,128]{2,1,0:T(8,128)(2,1)S(1)}, bf16[2,128,128]{2,1,0:T(8,128)(2,1)S(1)}, u32[]{:S(2)}, u32[]{:S(2)}) collective-permute-start(bf16[2,128,128]{2,1,0:T(8,128)(2,1)S(1)} %get-tuple-element.91), channel_id=1, source_target_pairs={{0,1},{1,0},{2,3},{3,2},{4,5},{5,4},{6,7},{7,6},{8,9},{9,8},{10,11... | collective-permute-start | bytes 196616 | tf_op jit(solution)/shard_map/ppermute | solution.py:360
  46.2 5.0 %collective-permute-start.14 = (bf16[2,128,128]{2,1,0:T(8,128)(2,1)S(1)}, bf16[2,128,128]{2,1,0:T(8,128)(2,1)S(1)}, u32[]{:S(2)}, u32[]{:S(2)}) collective-permute-start(bf16[2,128,128]{2,1,0:T(8,128)(2,1)S(1)} %get-tuple-element.92), channel_id=1, source_target_pairs={{0,2},{1,3},{2,0},{3,1},{4,6},{5,7},{6,4},{7,5},{8,10},{9,11},{10,... | collective-permute-start | bytes 196616 | tf_op jit(solution)/shard_map/ppermute | solution.py:360
  46.8 4.9 %collective-permute-start.15 = (bf16[2,128,128]{2,1,0:T(8,128)(2,1)S(1)}, bf16[2,128,128]{2,1,0:T(8,128)(2,1)S(1)}, u32[]{:S(2)}, u32[]{:S(2)}) collective-permute-start(bf16[2,128,128]{2,1,0:T(8,128)(2,1)S(1)} %get-tuple-element.93), channel_id=1, source_target_pairs={{0,3},{1,2},{2,1},{3,0},{4,7},{5,6},{6,5},{7,4},{8,11},{9,10},{10,... | collective-permute-start | bytes 196616 | tf_op jit(solution)/shard_map/ppermute | solution.py:360
  52.9 1.9 %collective-permute-start.16 = (bf16[256,128]{1,0:T(8,128)(2,1)S(1)}, bf16[256,128]{1,0:T(8,128)(2,1)S(1)}, u32[]{:S(2)}, u32[]{:S(2)}) collective-permute-start(bf16[256,128]{1,0:T(8,128)(2,1)S(1)} %get-tuple-element.98), channel_id=1, source_target_pairs={{0,1},{1,0},{2,3},{3,2},{4,5},{5,4},{6,7},{7,6},{8,9},{9,8},{10,11... | collective-permute-start | bytes 196616 | tf_op jit(solution)/shard_map/ppermute | solution.py:360
  53.2 5.0 %collective-permute-start.17 = (bf16[256,128]{1,0:T(8,128)(2,1)S(1)}, bf16[256,128]{1,0:T(8,128)(2,1)S(1)}, u32[]{:S(2)}, u32[]{:S(2)}) collective-permute-start(bf16[256,128]{1,0:T(8,128)(2,1)S(1)} %get-tuple-element.99), channel_id=1, source_target_pairs={{0,2},{1,3},{2,0},{3,1},{4,6},{5,7},{6,4},{7,5},{8,10},{9,11},{10,... | collective-permute-start | bytes 196616 | tf_op jit(solution)/shard_map/ppermute | solution.py:360
  53.8 4.4 %collective-permute-start.18 = (bf16[256,128]{1,0:T(8,128)(2,1)S(1)}, bf16[256,128]{1,0:T(8,128)(2,1)S(1)}, u32[]{:S(2)}, u32[]{:S(2)}) collective-permute-start(bf16[256,128]{1,0:T(8,128)(2,1)S(1)} %get-tuple-element.100), channel_id=1, source_target_pairs={{0,3},{1,2},{2,1},{3,0},{4,7},{5,6},{6,5},{7,4},{8,11},{9,10},{10,... | collective-permute-start | bytes 196616 | tf_op jit(solution)/shard_map/ppermute | solution.py:360
  58.2 44.1 %copy-start = (bf16[1,6,8,128,128]{4,3,2,1,0:T(8,128)(2,1)S(1)}, bf16[1,6,8,128,128]{4,3,2,1,0:T(8,128)(2,1)}, u32[]{:S(2)}) copy-start(bf16[1,6,8,128,128]{4,3,2,1,0:T(8,128)(2,1)} %param.18) | copy-start | bytes 4718596
  58.2 44.1 %copy-start.1 = (bf16[1,16,128,128]{3,2,1,0:T(8,128)(2,1)S(1)}, bf16[1,16,128,128]{3,2,1,0:T(8,128)(2,1)}, u32[]{:S(2)}) copy-start(bf16[1,16,128,128]{3,2,1,0:T(8,128)(2,1)} %param.15) | copy-start | bytes 1572868
  58.3 44.1 %copy-start.6 = (s32[1,6,8]{2,0,1:T(1,128)S(1)}, s32[1,6,8]{2,0,1:T(1,128)}, u32[]{:S(2)}) copy-start(s32[1,6,8]{2,0,1:T(1,128)} %param.19) | copy-start | bytes 580
  58.3 44.1 %copy-start.7 = (s32[1,6,8]{2,0,1:T(1,128)S(1)}, s32[1,6,8]{2,0,1:T(1,128)}, u32[]{:S(2)}) copy-start(s32[1,6,8]{2,0,1:T(1,128)} %param.20) | copy-start | bytes 580
  58.3 44.1 %copy-start.8 = (s32[1,16]{1,0:T(1,128)S(1)}, s32[1,16]{1,0:T(1,128)}, u32[]{:S(2)}) copy-start(s32[1,16]{1,0:T(1,128)} %refs_0_.7) | copy-start | bytes 196
  58.3 44.1 %copy-start.9 = (s32[1,16]{1,0:T(1,128)S(1)}, s32[1,16]{1,0:T(1,128)}, u32[]{:S(2)}) copy-start(s32[1,16]{1,0:T(1,128)} %refs_1_.7) | copy-start | bytes 196
  58.3 15.4 %collective-permute-start.19 = (bf16[8,128,128]{2,1,0:T(8,128)(2,1)S(1)}, bf16[8,128,128]{2,1,0:T(8,128)(2,1)S(1)}, u32[]{:S(2)}, u32[]{:S(2)}) collective-permute-start(bf16[8,128,128]{2,1,0:T(8,128)(2,1)S(1)} %bitcast.24), channel_id=1, source_target_pairs={{0,16},{4,20},{8,24},{12,28},{16,0},{20,4},{24,8},{28,12},{1,17},{... | collective-permute-start | bytes 786440 | tf_op jit(solution)/shard_map/ppermute | solution.py:360
  58.4 15.4 %collective-permute-start.20 = (bf16[8,128,128]{2,1,0:T(8,128)(2,1)S(1)}, bf16[8,128,128]{2,1,0:T(8,128)(2,1)S(1)}, u32[]{:S(2)}, u32[]{:S(2)}) collective-permute-start(bf16[8,128,128]{2,1,0:T(8,128)(2,1)S(1)} %bitcast.25), channel_id=1, source_target_pairs={{0,8},{4,12},{8,0},{12,4},{16,24},{20,28},{24,16},{28,20},{1,9},{5... | collective-permute-start | bytes 786440 | tf_op jit(solution)/shard_map/ppermute | solution.py:360
  62.4 11.4 %collective-permute-start.21 = (bf16[8,128,128]{2,1,0:T(8,128)(2,1)S(1)}, bf16[8,128,128]{2,1,0:T(8,128)(2,1)S(1)}, u32[]{:S(2)}, u32[]{:S(2)}) collective-permute-start(bf16[8,128,128]{2,1,0:T(8,128)(2,1)S(1)} %bitcast.26), channel_id=1, source_target_pairs={{0,4},{4,0},{8,12},{12,8},{16,20},{20,16},{24,28},{28,24},{1,5},{5... | collective-permute-start | bytes 786440 | tf_op jit(solution)/shard_map/ppermute | solution.py:360
  63.7 10.6 %collective-permute-start.23 = (bf16[5,256,128]{2,1,0:T(8,128)(2,1)S(1)}, bf16[5,256,128]{2,1,0:T(8,128)(2,1)S(1)}, u32[]{:S(2)}, u32[]{:S(2)}) collective-permute-start(bf16[5,256,128]{2,1,0:T(8,128)(2,1)S(1)} %get-tuple-element.103), channel_id=1, source_target_pairs={{0,2},{1,3},{2,0},{3,1},{4,6},{5,7},{6,4},{7,5},{8,10},{9,11},{10,... | collective-permute-start | bytes 983048 | tf_op jit(solution)/shard_map/ppermute | solution.py:360
  64.4 13.8 %collective-permute-start.24 = (bf16[5,256,128]{2,1,0:T(8,128)(2,1)S(1)}, bf16[5,256,128]{2,1,0:T(8,128)(2,1)S(1)}, u32[]{:S(2)}, u32[]{:S(2)}) collective-permute-start(bf16[5,256,128]{2,1,0:T(8,128)(2,1)S(1)} %get-tuple-element.104), channel_id=1, source_target_pairs={{0,3},{1,2},{2,1},{3,0},{4,7},{5,6},{6,5},{7,4},{8,11},{9,10},{10,... | collective-permute-start | bytes 983048 | tf_op jit(solution)/shard_map/ppermute | solution.py:360
  73.8 4.4 %collective-permute-start.22 = (bf16[5,256,128]{2,1,0:T(8,128)(2,1)S(1)}, bf16[5,256,128]{2,1,0:T(8,128)(2,1)S(1)}, u32[]{:S(2)}, u32[]{:S(2)}) collective-permute-start(bf16[5,256,128]{2,1,0:T(8,128)(2,1)S(1)} %get-tuple-element.102.refs_0_), channel_id=1, source_target_pairs={{0,1},{1,0},{2,3},{3,2},{4,5},{5,4},{6,7},{7,6},{8,9},{9,8},{10,11... | collective-permute-start | bytes 983048 | tf_op jit(solution)/shard_map/ppermute | solution.py:360
  79.0 6.2 %collective-permute-start.25 = (bf16[4,32,512]{2,1,0:T(8,128)(2,1)S(1)}, bf16[4,32,512]{2,1,0:T(8,128)(2,1)S(1)}, u32[]{:S(2)}, u32[]{:S(2)}) collective-permute-start(bf16[4,32,512]{2,1,0:T(8,128)(2,1)S(1)} %get-tuple-element.109), channel_id=1, source_target_pairs={{0,4},{4,0},{8,12},{12,8},{16,20},{20,16},{24,28},{28,24},{1,5},{5... | collective-permute-start | bytes 393224 | tf_op jit(solution)/shard_map/ppermute | solution.py:360
  80.3 10.5 %collective-permute-start.26 = (bf16[8,128,128]{2,1,0:T(8,128)(2,1)S(1)}, bf16[8,128,128]{2,1,0:T(8,128)(2,1)S(1)}, u32[]{:S(2)}, u32[]{:S(2)}) collective-permute-start(bf16[8,128,128]{2,1,0:T(8,128)(2,1)S(1)} %collective-permute-done.19.refs_6_), channel_id=1, source_target_pairs={{0,4},{4,0},{8,12},{12,8},{16,20},{20,16},{24,28},{28,24},{1,5},{5... | collective-permute-start | bytes 786440 | tf_op jit(solution)/shard_map/ppermute | solution.py:360
  81.1 9.7 %collective-permute-start.27 = (bf16[8,128,128]{2,1,0:T(8,128)(2,1)S(1)}, bf16[8,128,128]{2,1,0:T(8,128)(2,1)S(1)}, u32[]{:S(2)}, u32[]{:S(2)}) collective-permute-start(bf16[8,128,128]{2,1,0:T(8,128)(2,1)S(1)} %collective-permute-done.19.refs_6_), channel_id=1, source_target_pairs={{0,8},{4,12},{8,0},{12,4},{16,24},{20,28},{24,16},{28,20},{1,9},{5... | collective-permute-start | bytes 786440 | tf_op jit(solution)/shard_map/ppermute | solution.py:360
  90.8 6.3 %collective-permute-start.28 = (bf16[4,32,512]{2,1,0:T(8,128)(2,1)S(1)}, bf16[4,32,512]{2,1,0:T(8,128)(2,1)S(1)}, u32[]{:S(2)}, u32[]{:S(2)}) collective-permute-start(bf16[4,32,512]{2,1,0:T(8,128)(2,1)S(1)} %add_convert_fusion.5), channel_id=1, source_target_pairs={{0,8},{4,12},{8,0},{12,4},{16,24},{20,28},{24,16},{28,20},{1,9},{5... | collective-permute-start | bytes 393224 | tf_op jit(solution)/shard_map/ppermute | solution.py:360
  91.1 8.0 %collective-permute-start.29 = (bf16[8,128,128]{2,1,0:T(8,128)(2,1)S(1)}, bf16[8,128,128]{2,1,0:T(8,128)(2,1)S(1)}, u32[]{:S(2)}, u32[]{:S(2)}) collective-permute-start(bf16[8,128,128]{2,1,0:T(8,128)(2,1)S(1)} %collective-permute-done.20.refs_8_), channel_id=1, source_target_pairs={{0,4},{4,0},{8,12},{12,8},{16,20},{20,16},{24,28},{28,24},{1,5},{5... | collective-permute-start | bytes 786440 | tf_op jit(solution)/shard_map/ppermute | solution.py:360
  92.8 9.2 %collective-permute-start.30 = (bf16[8,128,128]{2,1,0:T(8,128)(2,1)S(1)}, bf16[8,128,128]{2,1,0:T(8,128)(2,1)S(1)}, u32[]{:S(2)}, u32[]{:S(2)}) collective-permute-start(bf16[8,128,128]{2,1,0:T(8,128)(2,1)S(1)} %collective-permute-done.26.refs_7_), channel_id=1, source_target_pairs={{0,8},{4,12},{8,0},{12,4},{16,24},{20,28},{24,16},{28,20},{1,9},{5... | collective-permute-start | bytes 786440 | tf_op jit(solution)/shard_map/ppermute | solution.py:360
  102.0 7.8 %collective-permute-start.31 = (bf16[4,32,512]{2,1,0:T(8,128)(2,1)S(1)}, bf16[4,32,512]{2,1,0:T(8,128)(2,1)S(1)}, u32[]{:S(2)}, u32[]{:S(2)}) collective-permute-start(bf16[4,32,512]{2,1,0:T(8,128)(2,1)S(1)} %add_convert_fusion.4), channel_id=1, source_target_pairs={{0,16},{4,20},{8,24},{12,28},{16,0},{20,4},{24,8},{28,12},{1,17},{... | collective-permute-start | bytes 393224 | tf_op jit(solution)/shard_map/ppermute | solution.py:360
  109.8 5.0 %collective-permute-start.32 = (bf16[4,32,512]{2,1,0:T(8,128)(2,1)S(1)}, bf16[4,32,512]{2,1,0:T(8,128)(2,1)S(1)}, u32[]{:S(2)}, u32[]{:S(2)}) collective-permute-start(bf16[4,32,512]{2,1,0:T(8,128)(2,1)S(1)} %add_convert_fusion.3.mine_ref), channel_id=1, source_target_pairs={{0,4},{4,0},{8,12},{12,8},{16,20},{20,16},{24,28},{28,24},{1,5},{5... | collective-permute-start | bytes 393224 | tf_op jit(solution)/shard_map/ppermute | solution.py:360

commit v10 on v9

--- a/solution.py
+++ b/solution.py
@@ -430,11 +430,11 @@
     sum_6 = (keep_6 + near_6.astype(F32)).astype(BF16)
     sum_2 = (keep_2 + near_2.astype(F32)).astype(BF16)
     mid_0 = crossed(sum_2, 2)
-    near_4, mid_0, weights[2] = lax.optimization_barrier((near_4, mid_0, weights[2]))
+    near_4, weights[2] = lax.optimization_barrier((tied(near_4, sum_2), weights[2]))
     sum_4 = (keep_4 + near_4.astype(F32) + crossed(sum_6, 2).astype(F32)).astype(BF16)
     far_0 = crossed(sum_4, 4)
-    part = keep + mid_0.astype(F32)
-    arrived = [far_0, near_0]
+    part = keep + near_0.astype(F32)
+    arrived = [far_0, mid_0]
     early, weights, arrived = lax.optimization_barrier((early, weights, arrived))
     agg, *agg_pieces = small_call(
         functools.partial(agg_kernel, feats),
@@ -457,12 +457,12 @@
     for mask in (4, 2, 1):
         found[mask] = crossed(dsum, mask)
     sent = tied(sent, dsum)
-    sent[0] = tied(sent[0], found[4], found[2], found[1])
-    come = [crossed(sent[m - 1], m, "feat") for m in range(1, feats)]
+    come_2, come_3 = crossed(sent[1], 2, "feat"), crossed(sent[2], 3, "feat")
+    come_2, come_3, found[4], found[2], found[1], sent[0] = lax.optimization_barrier(
+        (come_2, come_3, found[4], found[2], found[1], sent[0])
+    )
+    come = [crossed(sent[0], 1, "feat"), come_2, come_3]
     (out,) = small_call(place_kernel, [like((feats, some, width), BF16)], [own_out, *come])
-    come, found[4], found[2], found[1] = lax.optimization_barrier(
-        (come, found[4], found[2], found[1])
-    )
     dpre = [sent[0], *come]
     found[6] = crossed(found[4], 2)
     found[3] = crossed(found[2], near)
@@ -480,9 +480,8 @@
         [pltpu.VMEM((parts_total, piece, full), F32)],
     )
     total = (keep + crossed(give, near).astype(F32)).astype(BF16)
+    total = (total.astype(F32) + crossed(total, 2).astype(F32)).astype(BF16)
     total = tied(total, found[5], found[6])
-    total = (total.astype(F32) + crossed(total, 2).astype(F32)).astype(BF16)
-    total = tied(total, found[3], found[7])
     total = (total.astype(F32) + crossed(total, 4).astype(F32)).astype(BF16)
     grad_x = dx_self.reshape(shape)
     half = parts_total // 2
@@ -498,7 +497,7 @@
             like(shape, F32),
             24,
         )
-    total, out, grad_x = lax.optimization_barrier((total, out, grad_x))
+    total, out = tied((total, out), found[3], found[7])
     grad_self, grad_neigh = small_call(
         finish_kernel,
         [like((width, full), F32)] * 2,

time: 116 us -> 112 us (0.966)
  waiting for transfers between devices: 59.1 us -> 55.1 us
  other arithmetic: 3.17 us -> 4.82 us
  starting transfers between devices: 34.9 us -> 33.4 us
    ppermute x33, waiting for transfers between devices: 59.1 us -> 55.1 us  [crossed(): lax.ppermute(x, axis, [(i, i ^ mask) for i in range(lax.axis_size(axis))])]
    ppermute x33, starting transfers between devices: 34.9 us -> 33.4 us  [crossed(): lax.ppermute(x, axis, [(i, i ^ mask) for i in range(lax.axis_size(axis))])]
  transfers between devices with their start and end apart: 33 -> 33, of which waited for: 19 -> 18; matrix products, arithmetic and copies ran while one was open for 3% -> 5% of each run, Pallas kernels for 9% -> 9%
where the time goes in v10:
time: 112 us
  waiting for transfers between devices  55.1 us (49%)
  starting transfers between devices  33.4 us (30%)
  Pallas kernels  17.2 us (15%)
  other arithmetic  4.82 us (4%)
    ppermute x33, waiting for transfers between devices, crossed(): lax.ppermute(x, axis, [(i, i ^ mask) for i in range(lax.axis_size(axis))])  55.1 us
    ppermute x33, starting transfers between devices, crossed(): lax.ppermute(x, axis, [(i, i ^ mask) for i in range(lax.axis_size(axis))])  33.4 us
    pallas_call x4, Pallas kernels, tiles_call(): pl.pallas_call(functools.partial(tiles_kernel, masks, offsets, parts_tota...  13.3 us
    pallas_call x5, Pallas kernels, small_call(): pl.pallas_call(kernel, out_shape=outs, in_specs=[VMEM] * len(arrays), out...  3.87 us
  transfers between devices with their start and end apart: 33, of which 18 were waited for; matrix products, arithmetic and copies ran while one was open for 5% of the time, Pallas kernels for 9%

profile of v10, /device:TPU:0, one launch (start us, length us, event | category | flops | bytes accessed | tf_op | source)
XLA Modules:
  0.0 112.0 jit_solution(2916156089983669617)
XLA Ops:
  0.6 3.7 %shard_map.139 = (bf16[8,128,128]{2,1,0:T(8,128)(2,1)}, bf16[8,128,128]{2,1,0:T(8,128)(2,1)}, bf16[8,128,128]{2,1,0:T(8,128)(2,1)}, bf16[8,128,128]{2,1,0:T(8,128)(2,1)}) custom-call(s32[1,16]{1,0:T(1,128)} %refs_0_.7, s32[1,16]{1,0:T(1,128)} %refs_1_.7, s32[6,1,8]{2,1,0:T(1,128)} %bitcast.30, s32[6,1,8]{2,1,0:T(1,128)} %bitcast.34, ...), custom_call_target="tpu_custom_call" | custom-call | flops 1 | bytes 1 | tf_op jit(solution)/shard_map/pallas_call | solution.py:224
  4.4 3.0 %collective-permute-start.9 = (bf16[8,128,128]{2,1,0:T(8,128)(2,1)}, bf16[8,128,128]{2,1,0:T(8,128)(2,1)S(1)}, u32[]{:S(2)}, u32[]{:S(2)}) collective-permute-start(bf16[8,128,128]{2,1,0:T(8,128)(2,1)} %get-tuple-element.75), channel_id=1, source_target_pairs={{0,4},{4,0},{8,12},{12,8},{16,20},{20,16},{24,28},{28,24},{1,5},{5... | collective-permute-start | bytes 786440 | tf_op jit(solution)/shard_map/ppermute | solution.py:360
  7.4 0.1 collective-permute-start.6
  7.5 1.9 %collective-permute-start.5 = (bf16[8,128,128]{2,1,0:T(8,128)(2,1)}, bf16[8,128,128]{2,1,0:T(8,128)(2,1)S(1)}, u32[]{:S(2)}, u32[]{:S(2)}) collective-permute-start(bf16[8,128,128]{2,1,0:T(8,128)(2,1)} %get-tuple-element.67), channel_id=1, source_target_pairs={{0,4},{4,0},{8,12},{12,8},{16,20},{20,16},{24,28},{28,24},{1,5},{5... | collective-permute-start | bytes 786440 | tf_op jit(solution)/shard_map/ppermute | solution.py:360
  9.4 4.8 %shard_map.138 = (f32[8,128,128]{2,1,0:T(8,128)}, f32[8,128,128]{2,1,0:T(8,128)}, f32[8,128,128]{2,1,0:T(8,128)}, f32[8,128,128]{2,1,0:T(8,128)}, bf16[2,2,128,1...) custom-call(s32[1,16]{1,0:T(1,128)} %refs_0_.7, ...), custom_call_target="tpu_custom_call" | custom-call | flops 1 | bytes 1 | tf_op jit(solution)/shard_map/pallas_call | solution.py:224
  14.3 1.6 %collective-permute-start.7 = (bf16[2,128,512]{2,1,0:T(8,128)(2,1)}, bf16[2,128,512]{2,1,0:T(8,128)(2,1)S(1)}, u32[]{:S(2)}, u32[]{:S(2)}) collective-permute-start(bf16[2,128,512]{2,1,0:T(8,128)(2,1)} %get-tuple-element.79.refs_0_), channel_id=1, source_target_pairs={{0,2},{1,3},{2,0},{3,1},{4,6},{5,7},{6,4},{7,5},{8,10},{9,11},{10,... | collective-permute-start | bytes 786440 | tf_op jit(solution)/shard_map/ppermute | solution.py:360
  15.8 1.1 add_convert_fusion.1
  17.0 1.7 %collective-permute-start.10 = (bf16[8,128,128]{2,1,0:T(8,128)(2,1)S(1)}, bf16[8,128,128]{2,1,0:T(8,128)(2,1)S(1)}, u32[]{:S(2)}, u32[]{:S(2)}) collective-permute-start(bf16[8,128,128]{2,1,0:T(8,128)(2,1)S(1)} %add_convert_fusion.1), channel_id=1, source_target_pairs={{0,8},{4,12},{8,0},{12,4},{16,24},{20,28},{24,16},{28,20},{1,9},{5... | collective-permute-start | bytes 786440 | tf_op jit(solution)/shard_map/ppermute | solution.py:360
  18.6 1.8 %collective-permute-done.6 = bf16[8,128,128]{2,1,0:T(8,128)(2,1)S(1)} collective-permute-done((bf16[8,128,128]{2,1,0:T(8,128)(2,1)}, bf16[8,128,128]{2,1,0:T(8,128)(2,1)S(1)}, u32[]{:S(2)}, u32[]{:S(2)}) %collective-permute-start.6) | collective-permute-done | bytes 262176 | tf_op jit(solution)/shard_map/ppermute | solution.py:360
  20.4 1.8 %add_convert_fusion.2 = bf16[8,128,128]{2,1,0:T(8,128)(2,1)} fusion(f32[8,128,128]{2,1,0:T(8,128)} %get-tuple-element.68, bf16[8,128,128]{2,1,0:T(8,128)(2,1)S(1)} %collective-permute-done.6), kind=kLoop, calls=%fused_computation.2 | loop fusion | flops 393216 | bytes 1048576 | tf_op jit(solution)/shard_map/convert_element_type | solution.py:431
  22.2 3.0 %collective-permute-done.5 = bf16[8,128,128]{2,1,0:T(8,128)(2,1)S(1)} collective-permute-done((bf16[8,128,128]{2,1,0:T(8,128)(2,1)}, bf16[8,128,128]{2,1,0:T(8,128)(2,1)S(1)}, u32[]{:S(2)}, u32[]{:S(2)}) %collective-permute-start.5) | collective-permute-done | bytes 262176 | tf_op jit(solution)/shard_map/ppermute | solution.py:360
  25.2 1.7 %collective-permute-start.2 = (bf16[2,2,128,128]{3,2,1,0:T(8,128)(2,1)S(1)}, bf16[2,2,128,128]{3,2,1,0:T(8,128)(2,1)S(1)}, u32[]{:S(2)}, u32[]{:S(2)}) collective-permute-start(bf16[2,2,128,128]{3,2,1,0:T(8,128)(2,1)S(1)} %copy-done.14), channel_id=1, source_target_pairs={{0,2},{1,3},{2,0},{3,1},{4,6},{5,7},{6,4},{7,5},{8,10},{9,11},{10,... | collective-permute-start | bytes 393224 | tf_op jit(solution)/shard_map/ppermute | solution.py:360
  26.9 1.5 %collective-permute-start = (bf16[8,128,128]{2,1,0:T(8,128)(2,1)}, bf16[8,128,128]{2,1,0:T(8,128)(2,1)}, u32[]{:S(2)}, u32[]{:S(2)}) collective-permute-start(bf16[8,128,128]{2,1,0:T(8,128)(2,1)} %get-tuple-element.61), channel_id=1, source_target_pairs={{0,4},{4,0},{8,12},{12,8},{16,20},{20,16},{24,28},{28,24},{1,5},{5... | collective-permute-start | bytes 786440 | tf_op jit(solution)/shard_map/ppermute | solution.py:360
  28.4 1.6 %collective-permute-start.12 = (bf16[8,128,128]{2,1,0:T(8,128)(2,1)}, bf16[8,128,128]{2,1,0:T(8,128)(2,1)S(1)}, u32[]{:S(2)}, u32[]{:S(2)}) collective-permute-start(bf16[8,128,128]{2,1,0:T(8,128)(2,1)} %add_convert_fusion.2), channel_id=1, source_target_pairs={{0,8},{4,12},{8,0},{12,4},{16,24},{20,28},{24,16},{28,20},{1,9},{5... | collective-permute-start | bytes 786440 | tf_op jit(solution)/shard_map/ppermute | solution.py:360
  30.0 0.8 add_convert_fusion
  30.8 2.7 %collective-permute-start.11 = (bf16[8,128,128]{2,1,0:T(8,128)(2,1)}, bf16[8,128,128]{2,1,0:T(8,128)(2,1)S(1)}, u32[]{:S(2)}, u32[]{:S(2)}) collective-permute-start(bf16[8,128,128]{2,1,0:T(8,128)(2,1)} %add_convert_fusion), channel_id=1, source_target_pairs={{0,16},{4,20},{8,24},{12,28},{16,0},{20,4},{24,8},{28,12},{1,17},{... | collective-permute-start | bytes 786440 | tf_op jit(solution)/shard_map/ppermute | solution.py:360
  33.5 0.2 copy.15.inv_ref
  33.7 0.4 collective-permute-done
  34.1 0.0 collective-permute-start.3
  34.1 1.0 convert_add_fusion.keep_ref
  35.1 4.7 %collective-permute-done.3.refs_7_ = bf16[2,2,128,128]{3,2,1,0:T(8,128)(2,1)S(1)} collective-permute-done((bf16[2,2,128,128]{3,2,1,0:T(8,128)(2,1)S(1)}, bf16[2,2,128,128]{3,2,1,0:T(8,128)(2,1)S(1)}, u32[]{:S(2)}, u32[]{:S(2)}) %collective-permute-start.3) | collective-permute-done | bytes 131104 | tf_op jit(solution)/shard_map/ppermute | solution.py:360
  39.8 6.3 %collective-permute-done.11.refs_0_ = bf16[8,128,128]{2,1,0:T(8,128)(2,1)S(1)} collective-permute-done((bf16[8,128,128]{2,1,0:T(8,128)(2,1)}, bf16[8,128,128]{2,1,0:T(8,128)(2,1)S(1)}, u32[]{:S(2)}, u32[]{:S(2)}) %collective-permute-start.11) | collective-permute-done | bytes 262176 | tf_op jit(solution)/shard_map/ppermute | solution.py:360
  46.2 0.2 shard_map.140
  46.4 0.1 collective-permute-start.13
  46.5 0.6 collective-permute-start.14
  47.1 1.3 %collective-permute-start.15 = (bf16[2,128,128]{2,1,0:T(8,128)(2,1)S(1)}, bf16[2,128,128]{2,1,0:T(8,128)(2,1)S(1)}, u32[]{:S(2)}, u32[]{:S(2)}) collective-permute-start(bf16[2,128,128]{2,1,0:T(8,128)(2,1)S(1)} %get-tuple-element.90), channel_id=1, source_target_pairs={{0,3},{1,2},{2,1},{3,0},{4,7},{5,6},{6,5},{7,4},{8,11},{9,10},{10,... | collective-permute-start | bytes 196616 | tf_op jit(solution)/shard_map/ppermute | solution.py:360
  48.4 0.1 dynamic_slice.3
  48.4 0.1 copy.16.inv_ref
  48.6 2.9 %collective-permute-done.14.refs_10_ = bf16[2,128,128]{2,1,0:T(8,128)(2,1)S(1)} collective-permute-done((bf16[2,128,128]{2,1,0:T(8,128)(2,1)S(1)}, bf16[2,128,128]{2,1,0:T(8,128)(2,1)S(1)}, u32[]{:S(2)}, u32[]{:S(2)}) %collective-permute-start.14) | collective-permute-done | bytes 65568 | tf_op jit(solution)/shard_map/ppermute | solution.py:360
  51.5 0.5 collective-permute-done.15.refs_11_
  52.0 1.3 %shard_map.141 = (bf16[5,256,128]{2,1,0:T(8,128)(2,1)S(1)}, bf16[5,256,128]{2,1,0:T(8,128)(2,1)S(1)}, bf16[5,256,128]{2,1,0:T(8,128)(2,1)S(1)}, bf16[256,128]{1,...) custom-call(f32[256,1]{1,0:T(8,128)S(1)} %copy.16.inv_ref, ...), custom_call_target="tpu_custom_call" | custom-call | flops 1 | bytes 1 | tf_op jit(solution)/shard_map/pallas_call | solution.py:244
  53.2 0.3 collective-permute-start.16
  53.6 0.6 collective-permute-start.17
  54.2 1.0 collective-permute-start.18
  55.2 3.4 %collective-permute-done.17 = bf16[256,128]{1,0:T(8,128)(2,1)S(1)} collective-permute-done((bf16[256,128]{1,0:T(8,128)(2,1)S(1)}, bf16[256,128]{1,0:T(8,128)(2,1)S(1)}, u32[]{:S(2)}, u32[]{:S(2)}) %collective-permute-start.17) | collective-permute-done | bytes 65568 | tf_op jit(solution)/shard_map/ppermute | solution.py:360
  58.5 0.0 collective-permute-done.18
  58.6 1.4 %collective-permute-start.19 = (bf16[5,256,128]{2,1,0:T(8,128)(2,1)S(1)}, bf16[5,256,128]{2,1,0:T(8,128)(2,1)S(1)}, u32[]{:S(2)}, u32[]{:S(2)}) collective-permute-start(bf16[5,256,128]{2,1,0:T(8,128)(2,1)S(1)} %get-tuple-element.98), channel_id=1, source_target_pairs={{0,2},{1,3},{2,0},{3,1},{4,6},{5,7},{6,4},{7,5},{8,10},{9,11},{10,... | collective-permute-start | bytes 983048 | tf_op jit(solution)/shard_map/ppermute | solution.py:360
  60.0 0.6 collective-permute-start.20
  60.5 3.2 %collective-permute-start.22 = (bf16[8,128,128]{2,1,0:T(8,128)(2,1)S(1)}, bf16[8,128,128]{2,1,0:T(8,128)(2,1)S(1)}, u32[]{:S(2)}, u32[]{:S(2)}) collective-permute-start(bf16[8,128,128]{2,1,0:T(8,128)(2,1)S(1)} %bitcast.25), channel_id=1, source_target_pairs={{0,8},{4,12},{8,0},{12,4},{16,24},{20,28},{24,16},{28,20},{1,9},{5... | collective-permute-start | bytes 786440 | tf_op jit(solution)/shard_map/ppermute | solution.py:360
  63.7 0.5 collective-permute-start.23
  64.2 11.4 %collective-permute-done.21.refs_6_ = bf16[8,128,128]{2,1,0:T(8,128)(2,1)S(1)} collective-permute-done((bf16[8,128,128]{2,1,0:T(8,128)(2,1)S(1)}, bf16[8,128,128]{2,1,0:T(8,128)(2,1)S(1)}, u32[]{:S(2)}, u32[]{:S(2)}) %collective-permute-start.21) | collective-permute-done | bytes 262176 | tf_op jit(solution)/shard_map/ppermute | solution.py:360
  75.6 0.2 collective-permute-done.22.refs_8_
  75.7 0.1 collective-permute-start.24
  75.8 1.6 %collective-permute-done.24.refs_1_ = bf16[5,256,128]{2,1,0:T(8,128)(2,1)S(1)} collective-permute-done((bf16[5,256,128]{2,1,0:T(8,128)(2,1)S(1)}, bf16[5,256,128]{2,1,0:T(8,128)(2,1)S(1)}, u32[]{:S(2)}, u32[]{:S(2)}) %collective-permute-start.24) | collective-permute-done | bytes 327712 | tf_op jit(solution)/shard_map/ppermute | solution.py:360
  77.4 0.8 shard_map.142
  78.3 0.6 collective-permute-start.25
  78.9 5.0 %collective-permute-done.25 = bf16[4,32,512]{2,1,0:T(8,128)(2,1)S(1)} collective-permute-done((bf16[4,32,512]{2,1,0:T(8,128)(2,1)S(1)}, bf16[4,32,512]{2,1,0:T(8,128)(2,1)S(1)}, u32[]{:S(2)}, u32[]{:S(2)}) %collective-permute-start.25) | collective-permute-done | bytes 131104 | tf_op jit(solution)/shard_map/ppermute | solution.py:360
  83.9 0.1 collective-permute-start.26
  84.0 0.6 collective-permute-start.27
  84.6 1.9 %collective-permute-start.28 = (bf16[8,128,128]{2,1,0:T(8,128)(2,1)S(1)}, bf16[8,128,128]{2,1,0:T(8,128)(2,1)S(1)}, u32[]{:S(2)}, u32[]{:S(2)}) collective-permute-start(bf16[8,128,128]{2,1,0:T(8,128)(2,1)S(1)} %collective-permute-done.21.refs_6_), channel_id=1, source_target_pairs={{0,8},{4,12},{8,0},{12,4},{16,24},{20,28},{24,16},{28,20},{1,9},{5... | collective-permute-start | bytes 786440 | tf_op jit(solution)/shard_map/ppermute | solution.py:360
  86.5 3.9 %collective-permute-done.26 = bf16[4,32,512]{2,1,0:T(8,128)(2,1)S(1)} collective-permute-done((bf16[4,32,512]{2,1,0:T(8,128)(2,1)S(1)}, bf16[4,32,512]{2,1,0:T(8,128)(2,1)S(1)}, u32[]{:S(2)}, u32[]{:S(2)}) %collective-permute-start.26) | collective-permute-done | bytes 131104 | tf_op jit(solution)/shard_map/ppermute | solution.py:360
  90.5 1.1 %collective-permute-done.27.refs_7_ = bf16[8,128,128]{2,1,0:T(8,128)(2,1)S(1)} collective-permute-done((bf16[8,128,128]{2,1,0:T(8,128)(2,1)S(1)}, bf16[8,128,128]{2,1,0:T(8,128)(2,1)S(1)}, u32[]{:S(2)}, u32[]{:S(2)}) %collective-permute-start.27) | collective-permute-done | bytes 262176 | tf_op jit(solution)/shard_map/ppermute | solution.py:360
  91.6 2.7 %collective-permute-done.28.refs_8_ = bf16[8,128,128]{2,1,0:T(8,128)(2,1)S(1)} collective-permute-done((bf16[8,128,128]{2,1,0:T(8,128)(2,1)S(1)}, bf16[8,128,128]{2,1,0:T(8,128)(2,1)S(1)}, u32[]{:S(2)}, u32[]{:S(2)}) %collective-permute-start.28) | collective-permute-done | bytes 262176 | tf_op jit(solution)/shard_map/ppermute | solution.py:360
  94.3 1.2 %collective-permute-start.29 = (bf16[4,32,512]{2,1,0:T(8,128)(2,1)S(1)}, bf16[4,32,512]{2,1,0:T(8,128)(2,1)S(1)}, u32[]{:S(2)}, u32[]{:S(2)}) collective-permute-start(bf16[4,32,512]{2,1,0:T(8,128)(2,1)S(1)} %add_convert_fusion.4), channel_id=1, source_target_pairs={{0,16},{4,20},{8,24},{12,28},{16,0},{20,4},{24,8},{28,12},{1,17},{... | collective-permute-start | bytes 393224 | tf_op jit(solution)/shard_map/ppermute | solution.py:360
  95.5 0.5 collective-permute-start.30
  96.0 1.7 %collective-permute-start.31 = (bf16[8,128,128]{2,1,0:T(8,128)(2,1)S(1)}, bf16[8,128,128]{2,1,0:T(8,128)(2,1)S(1)}, u32[]{:S(2)}, u32[]{:S(2)}) collective-permute-start(bf16[8,128,128]{2,1,0:T(8,128)(2,1)S(1)} %collective-permute-done.27.refs_7_), channel_id=1, source_target_pairs={{0,8},{4,12},{8,0},{12,4},{16,24},{20,28},{24,16},{28,20},{1,9},{5... | collective-permute-start | bytes 786440 | tf_op jit(solution)/shard_map/ppermute | solution.py:360
  97.7 0.7 shard_map.143
  98.5 3.4 %collective-permute-done.29 = bf16[4,32,512]{2,1,0:T(8,128)(2,1)S(1)} collective-permute-done((bf16[4,32,512]{2,1,0:T(8,128)(2,1)S(1)}, bf16[4,32,512]{2,1,0:T(8,128)(2,1)S(1)}, u32[]{:S(2)}, u32[]{:S(2)}) %collective-permute-start.29) | collective-permute-done | bytes 131104 | tf_op jit(solution)/shard_map/ppermute | solution.py:360
  101.9 0.5 collective-permute-done.30.refs_9_
  102.4 2.4 %collective-permute-done.31.refs_9_ = bf16[8,128,128]{2,1,0:T(8,128)(2,1)S(1)} collective-permute-done((bf16[8,128,128]{2,1,0:T(8,128)(2,1)S(1)}, bf16[8,128,128]{2,1,0:T(8,128)(2,1)S(1)}, u32[]{:S(2)}, u32[]{:S(2)}) %collective-permute-start.31) | collective-permute-done | bytes 262176 | tf_op jit(solution)/shard_map/ppermute | solution.py:360
  104.8 1.5 %collective-permute-start.32 = (bf16[4,32,512]{2,1,0:T(8,128)(2,1)S(1)}, bf16[4,32,512]{2,1,0:T(8,128)(2,1)S(1)}, u32[]{:S(2)}, u32[]{:S(2)}) collective-permute-start(bf16[4,32,512]{2,1,0:T(8,128)(2,1)S(1)} %add_convert_fusion.3.mine_ref), channel_id=1, source_target_pairs={{0,4},{4,0},{8,12},{12,8},{16,20},{20,16},{24,28},{28,24},{1,5},{5... | collective-permute-start | bytes 393224 | tf_op jit(solution)/shard_map/ppermute | solution.py:360
  106.3 2.1 %shard_map.144.refs_10_ = f32[8,128,128]{2,1,0:T(8,128)S(1)} custom-call(s32[1,16]{1,0:T(1,128)S(1)} %copy-done.8, s32[1,16]{1,0:T(1,128)S(1)} %copy-done.9, s32[6,1,8]{2,1,0:T(1,128)S(1)} %bitcast.32, s32[6,1,8]{2,1,0:T(1,128)S(1)} %bitcast.36, bf16[16,128,128]{2,1,0:T(8,128)(2,1)S(1)} %bitcast.20, bf16[6,8,128,128]{3,2,1,0:T(8,128)(2,1)S(1)} %bitcast.16, ...), custom_call_target="tpu_custom_call" | custom-call | flops 1 | bytes 1 | tf_op jit(solution)/shard_map/pallas_call | solution.py:224
  108.5 2.6 %shard_map.145 = f32[8,128,128]{2,1,0:T(8,128)} custom-call(s32[1,16]{1,0:T(1,128)S(1)} %copy-done.8, s32[1,16]{1,0:T(1,128)S(1)} %copy-done.9, s32[6,1,8]{2,1,0:T(1,128)S(1)} %bitcast.33, s32[6,1,8]{2,1,0:T(1,128)S(1)} %bitcast.37, bf16[16,128,128]{2,1,0:T(8,128)(2,1)S(1)} %bitcast.21, bf16[6,8,128,128]{3,2,1,0:T(8,128)(2,1)S(1)} %bitcast.17, ...), custom_call_target="tpu_custom_call" | custom-call | flops 1 | bytes 1 | tf_op jit(solution)/shard_map/pallas_call | solution.py:224
  111.1 0.9 shard_map.146
  (53 shorter events, 0.2 us)
Async XLA Ops:
  4.4 11.4 %collective-permute-start.9 = (bf16[8,128,128]{2,1,0:T(8,128)(2,1)}, bf16[8,128,128]{2,1,0:T(8,128)(2,1)S(1)}, u32[]{:S(2)}, u32[]{:S(2)}) collective-permute-start(bf16[8,128,128]{2,1,0:T(8,128)(2,1)} %get-tuple-element.75), channel_id=1, source_target_pairs={{0,4},{4,0},{8,12},{12,8},{16,20},{20,16},{24,28},{28,24},{1,5},{5... | collective-permute-start | bytes 786440 | tf_op jit(solution)/shard_map/ppermute | solution.py:360
  7.4 13.0 %collective-permute-start.6 = (bf16[8,128,128]{2,1,0:T(8,128)(2,1)}, bf16[8,128,128]{2,1,0:T(8,128)(2,1)S(1)}, u32[]{:S(2)}, u32[]{:S(2)}) collective-permute-start(bf16[8,128,128]{2,1,0:T(8,128)(2,1)} %get-tuple-element.69), channel_id=1, source_target_pairs={{0,4},{4,0},{8,12},{12,8},{16,20},{20,16},{24,28},{28,24},{1,5},{5... | collective-permute-start | bytes 786440 | tf_op jit(solution)/shard_map/ppermute | solution.py:360
  7.5 17.7 %collective-permute-start.5 = (bf16[8,128,128]{2,1,0:T(8,128)(2,1)}, bf16[8,128,128]{2,1,0:T(8,128)(2,1)S(1)}, u32[]{:S(2)}, u32[]{:S(2)}) collective-permute-start(bf16[8,128,128]{2,1,0:T(8,128)(2,1)} %get-tuple-element.67), channel_id=1, source_target_pairs={{0,4},{4,0},{8,12},{12,8},{16,20},{20,16},{24,28},{28,24},{1,5},{5... | collective-permute-start | bytes 786440 | tf_op jit(solution)/shard_map/ppermute | solution.py:360
  14.2 10.9 %copy-start.14 = (bf16[2,2,128,128]{3,2,1,0:T(8,128)(2,1)S(1)}, bf16[2,2,128,128]{3,2,1,0:T(8,128)(2,1)}, u32[]{:S(2)}) copy-start(bf16[2,2,128,128]{3,2,1,0:T(8,128)(2,1)} %get-tuple-element.64) | copy-start | bytes 393220
  14.3 15.7 %copy-start.11 = (f32[8,128,128]{2,1,0:T(8,128)S(1)}, f32[8,128,128]{2,1,0:T(8,128)}, u32[]{:S(2)}) copy-start(f32[8,128,128]{2,1,0:T(8,128)} %get-tuple-element.72) | copy-start | bytes 1572868
  14.3 12.6 %collective-permute-start.7 = (bf16[2,128,512]{2,1,0:T(8,128)(2,1)}, bf16[2,128,512]{2,1,0:T(8,128)(2,1)S(1)}, u32[]{:S(2)}, u32[]{:S(2)}) collective-permute-start(bf16[2,128,512]{2,1,0:T(8,128)(2,1)} %get-tuple-element.79.refs_0_), channel_id=1, source_target_pairs={{0,2},{1,3},{2,0},{3,1},{4,6},{5,7},{6,4},{7,5},{8,10},{9,11},{10,... | collective-permute-start | bytes 786440 | tf_op jit(solution)/shard_map/ppermute | solution.py:360
  15.8 17.7 %copy-start.12 = (s32[1024]{0:T(1024)S(1)}, s32[1024]{0:T(1024)}, u32[]{:S(2)}) copy-start(s32[1024]{0:T(1024)} %param.14) | copy-start | bytes 12292
  16.9 17.2 %copy-start.13 = (bf16[2,2,128,128]{3,2,1,0:T(8,128)(2,1)S(1)}, bf16[2,2,128,128]{3,2,1,0:T(8,128)(2,1)}, u32[]{:S(2)}) copy-start(bf16[2,2,128,128]{3,2,1,0:T(8,128)(2,1)} %get-tuple-element.65) | copy-start | bytes 393220
  16.9 17.2 %copy-start.10 = (f32[8,128,128]{2,1,0:T(8,128)S(1)}, f32[8,128,128]{2,1,0:T(8,128)}, u32[]{:S(2)}) copy-start(f32[8,128,128]{2,1,0:T(8,128)} %get-tuple-element.60) | copy-start | bytes 1572868
  17.0 11.5 %collective-permute-start.10 = (bf16[8,128,128]{2,1,0:T(8,128)(2,1)S(1)}, bf16[8,128,128]{2,1,0:T(8,128)(2,1)S(1)}, u32[]{:S(2)}, u32[]{:S(2)}) collective-permute-start(bf16[8,128,128]{2,1,0:T(8,128)(2,1)S(1)} %add_convert_fusion.1), channel_id=1, source_target_pairs={{0,8},{4,12},{8,0},{12,4},{16,24},{20,28},{24,16},{28,20},{1,9},{5... | collective-permute-start | bytes 786440 | tf_op jit(solution)/shard_map/ppermute | solution.py:360
  18.6 21.2 %collective-permute-start.4 = (bf16[2,128,512]{2,1,0:T(8,128)(2,1)}, bf16[2,128,512]{2,1,0:T(8,128)(2,1)S(1)}, u32[]{:S(2)}, u32[]{:S(2)}) collective-permute-start(bf16[2,128,512]{2,1,0:T(8,128)(2,1)} %get-tuple-element.79.refs_0_), channel_id=1, source_target_pairs={{0,1},{1,0},{2,3},{3,2},{4,5},{5,4},{6,7},{7,6},{8,9},{9,8},{10,11... | collective-permute-start | bytes 786440 | tf_op jit(solution)/shard_map/ppermute | solution.py:360
  20.4 10.4 %collective-permute-start.1 = (bf16[2,2,128,128]{3,2,1,0:T(8,128)(2,1)}, bf16[2,2,128,128]{3,2,1,0:T(8,128)(2,1)S(1)}, u32[]{:S(2)}, u32[]{:S(2)}) collective-permute-start(bf16[2,2,128,128]{3,2,1,0:T(8,128)(2,1)} %get-tuple-element.63), channel_id=1, source_target_pairs={{0,1},{1,0},{2,3},{3,2},{4,5},{5,4},{6,7},{7,6},{8,9},{9,8},{10,11... | collective-permute-start | bytes 393224 | tf_op jit(solution)/shard_map/ppermute | solution.py:360
  25.2 5.6 %collective-permute-start.2 = (bf16[2,2,128,128]{3,2,1,0:T(8,128)(2,1)S(1)}, bf16[2,2,128,128]{3,2,1,0:T(8,128)(2,1)S(1)}, u32[]{:S(2)}, u32[]{:S(2)}) collective-permute-start(bf16[2,2,128,128]{3,2,1,0:T(8,128)(2,1)S(1)} %copy-done.14), channel_id=1, source_target_pairs={{0,2},{1,3},{2,0},{3,1},{4,6},{5,7},{6,4},{7,5},{8,10},{9,11},{10,... | collective-permute-start | bytes 393224 | tf_op jit(solution)/shard_map/ppermute | solution.py:360
  26.9 7.2 %collective-permute-start = (bf16[8,128,128]{2,1,0:T(8,128)(2,1)}, bf16[8,128,128]{2,1,0:T(8,128)(2,1)}, u32[]{:S(2)}, u32[]{:S(2)}) collective-permute-start(bf16[8,128,128]{2,1,0:T(8,128)(2,1)} %get-tuple-element.61), channel_id=1, source_target_pairs={{0,4},{4,0},{8,12},{12,8},{16,20},{20,16},{24,28},{28,24},{1,5},{5... | collective-permute-start | bytes 786440 | tf_op jit(solution)/shard_map/ppermute | solution.py:360
  28.4 11.4 %collective-permute-start.12 = (bf16[8,128,128]{2,1,0:T(8,128)(2,1)}, bf16[8,128,128]{2,1,0:T(8,128)(2,1)S(1)}, u32[]{:S(2)}, u32[]{:S(2)}) collective-permute-start(bf16[8,128,128]{2,1,0:T(8,128)(2,1)} %add_convert_fusion.2), channel_id=1, source_target_pairs={{0,8},{4,12},{8,0},{12,4},{16,24},{20,28},{24,16},{28,20},{1,9},{5... | collective-permute-start | bytes 786440 | tf_op jit(solution)/shard_map/ppermute | solution.py:360
  30.8 9.0 %collective-permute-start.8 = (bf16[2,128,512]{2,1,0:T(8,128)(2,1)S(1)}, bf16[2,128,512]{2,1,0:T(8,128)(2,1)S(1)}, u32[]{:S(2)}, u32[]{:S(2)}) collective-permute-start(bf16[2,128,512]{2,1,0:T(8,128)(2,1)S(1)} %collective-permute-done.7.refs_2_), channel_id=1, source_target_pairs={{0,1},{1,0},{2,3},{3,2},{4,5},{5,4},{6,7},{7,6},{8,9},{9,8},{10,11... | collective-permute-start | bytes 786440 | tf_op jit(solution)/shard_map/ppermute | solution.py:360
  30.8 15.4 %collective-permute-start.11 = (bf16[8,128,128]{2,1,0:T(8,128)(2,1)}, bf16[8,128,128]{2,1,0:T(8,128)(2,1)S(1)}, u32[]{:S(2)}, u32[]{:S(2)}) collective-permute-start(bf16[8,128,128]{2,1,0:T(8,128)(2,1)} %add_convert_fusion), channel_id=1, source_target_pairs={{0,16},{4,20},{8,24},{12,28},{16,0},{20,4},{24,8},{28,12},{1,17},{... | collective-permute-start | bytes 786440 | tf_op jit(solution)/shard_map/ppermute | solution.py:360
  33.7 18.3 %copy-start.4 = (bf16[2,128,512]{2,1,0:T(8,128)(2,1)S(1)}, bf16[2,128,512]{2,1,0:T(8,128)(2,1)}, u32[]{:S(2)}) copy-start(bf16[2,128,512]{2,1,0:T(8,128)(2,1)} %get-tuple-element.79.refs_0_) | copy-start | bytes 786436
  33.7 18.2 %copy-start.5 = (bf16[2,2,128,128]{3,2,1,0:T(8,128)(2,1)S(1)}, bf16[2,2,128,128]{3,2,1,0:T(8,128)(2,1)}, u32[]{:S(2)}) copy-start(bf16[2,2,128,128]{3,2,1,0:T(8,128)(2,1)} %get-tuple-element.83.refs_4_) | copy-start | bytes 393220
  34.1 5.7 %collective-permute-start.3 = (bf16[2,2,128,128]{3,2,1,0:T(8,128)(2,1)S(1)}, bf16[2,2,128,128]{3,2,1,0:T(8,128)(2,1)S(1)}, u32[]{:S(2)}, u32[]{:S(2)}) collective-permute-start(bf16[2,2,128,128]{3,2,1,0:T(8,128)(2,1)S(1)} %copy-done.13), channel_id=1, source_target_pairs={{0,3},{1,2},{2,1},{3,0},{4,7},{5,6},{6,5},{7,4},{8,11},{9,10},{10,... | collective-permute-start | bytes 393224 | tf_op jit(solution)/shard_map/ppermute | solution.py:360
  46.4 31.0 %copy-start.2 = (bf16[1024,128]{1,0:T(8,128)(2,1)S(1)}, bf16[1024,128]{1,0:T(8,128)(2,1)}, u32[]{:S(2)}) copy-start(bf16[1024,128]{1,0:T(8,128)(2,1)} %f_ref.1) | copy-start | bytes 786436
  46.4 31.0 %copy-start.3 = (bf16[128,512]{1,0:T(8,128)(2,1)S(1)}, bf16[128,512]{1,0:T(8,128)(2,1)}, u32[]{:S(2)}) copy-start(bf16[128,512]{1,0:T(8,128)(2,1)} %w_ref.1) | copy-start | bytes 393220
  46.4 2.2 %collective-permute-start.13 = (bf16[2,128,128]{2,1,0:T(8,128)(2,1)S(1)}, bf16[2,128,128]{2,1,0:T(8,128)(2,1)S(1)}, u32[]{:S(2)}, u32[]{:S(2)}) collective-permute-start(bf16[2,128,128]{2,1,0:T(8,128)(2,1)S(1)} %get-tuple-element.88), channel_id=1, source_target_pairs={{0,1},{1,0},{2,3},{3,2},{4,5},{5,4},{6,7},{7,6},{8,9},{9,8},{10,11... | collective-permute-start | bytes 196616 | tf_op jit(solution)/shard_map/ppermute | solution.py:360
  46.5 5.0 %collective-permute-start.14 = (bf16[2,128,128]{2,1,0:T(8,128)(2,1)S(1)}, bf16[2,128,128]{2,1,0:T(8,128)(2,1)S(1)}, u32[]{:S(2)}, u32[]{:S(2)}) collective-permute-start(bf16[2,128,128]{2,1,0:T(8,128)(2,1)S(1)} %get-tuple-element.89), channel_id=1, source_target_pairs={{0,2},{1,3},{2,0},{3,1},{4,6},{5,7},{6,4},{7,5},{8,10},{9,11},{10,... | collective-permute-start | bytes 196616 | tf_op jit(solution)/shard_map/ppermute | solution.py:360
  47.1 4.9 %collective-permute-start.15 = (bf16[2,128,128]{2,1,0:T(8,128)(2,1)S(1)}, bf16[2,128,128]{2,1,0:T(8,128)(2,1)S(1)}, u32[]{:S(2)}, u32[]{:S(2)}) collective-permute-start(bf16[2,128,128]{2,1,0:T(8,128)(2,1)S(1)} %get-tuple-element.90), channel_id=1, source_target_pairs={{0,3},{1,2},{2,1},{3,0},{4,7},{5,6},{6,5},{7,4},{8,11},{9,10},{10,... | collective-permute-start | bytes 196616 | tf_op jit(solution)/shard_map/ppermute | solution.py:360
  53.2 1.9 %collective-permute-start.16 = (bf16[256,128]{1,0:T(8,128)(2,1)S(1)}, bf16[256,128]{1,0:T(8,128)(2,1)S(1)}, u32[]{:S(2)}, u32[]{:S(2)}) collective-permute-start(bf16[256,128]{1,0:T(8,128)(2,1)S(1)} %get-tuple-element.95), channel_id=1, source_target_pairs={{0,1},{1,0},{2,3},{3,2},{4,5},{5,4},{6,7},{7,6},{8,9},{9,8},{10,11... | collective-permute-start | bytes 196616 | tf_op jit(solution)/shard_map/ppermute | solution.py:360
  53.6 5.0 %collective-permute-start.17 = (bf16[256,128]{1,0:T(8,128)(2,1)S(1)}, bf16[256,128]{1,0:T(8,128)(2,1)S(1)}, u32[]{:S(2)}, u32[]{:S(2)}) collective-permute-start(bf16[256,128]{1,0:T(8,128)(2,1)S(1)} %get-tuple-element.96), channel_id=1, source_target_pairs={{0,2},{1,3},{2,0},{3,1},{4,6},{5,7},{6,4},{7,5},{8,10},{9,11},{10,... | collective-permute-start | bytes 196616 | tf_op jit(solution)/shard_map/ppermute | solution.py:360
  54.2 4.4 %collective-permute-start.18 = (bf16[256,128]{1,0:T(8,128)(2,1)S(1)}, bf16[256,128]{1,0:T(8,128)(2,1)S(1)}, u32[]{:S(2)}, u32[]{:S(2)}) collective-permute-start(bf16[256,128]{1,0:T(8,128)(2,1)S(1)} %get-tuple-element.97), channel_id=1, source_target_pairs={{0,3},{1,2},{2,1},{3,0},{4,7},{5,6},{6,5},{7,4},{8,11},{9,10},{10,... | collective-permute-start | bytes 196616 | tf_op jit(solution)/shard_map/ppermute | solution.py:360
  58.6 17.2 %collective-permute-start.19 = (bf16[5,256,128]{2,1,0:T(8,128)(2,1)S(1)}, bf16[5,256,128]{2,1,0:T(8,128)(2,1)S(1)}, u32[]{:S(2)}, u32[]{:S(2)}) collective-permute-start(bf16[5,256,128]{2,1,0:T(8,128)(2,1)S(1)} %get-tuple-element.98), channel_id=1, source_target_pairs={{0,2},{1,3},{2,0},{3,1},{4,6},{5,7},{6,4},{7,5},{8,10},{9,11},{10,... | collective-permute-start | bytes 983048 | tf_op jit(solution)/shard_map/ppermute | solution.py:360
  60.0 15.8 %collective-permute-start.20 = (bf16[5,256,128]{2,1,0:T(8,128)(2,1)S(1)}, bf16[5,256,128]{2,1,0:T(8,128)(2,1)S(1)}, u32[]{:S(2)}, u32[]{:S(2)}) collective-permute-start(bf16[5,256,128]{2,1,0:T(8,128)(2,1)S(1)} %get-tuple-element.99), channel_id=1, source_target_pairs={{0,3},{1,2},{2,1},{3,0},{4,7},{5,6},{6,5},{7,4},{8,11},{9,10},{10,... | collective-permute-start | bytes 983048 | tf_op jit(solution)/shard_map/ppermute | solution.py:360
  60.5 15.1 %collective-permute-start.21 = (bf16[8,128,128]{2,1,0:T(8,128)(2,1)S(1)}, bf16[8,128,128]{2,1,0:T(8,128)(2,1)S(1)}, u32[]{:S(2)}, u32[]{:S(2)}) collective-permute-start(bf16[8,128,128]{2,1,0:T(8,128)(2,1)S(1)} %bitcast.24), channel_id=1, source_target_pairs={{0,16},{4,20},{8,24},{12,28},{16,0},{20,4},{24,8},{28,12},{1,17},{... | collective-permute-start | bytes 786440 | tf_op jit(solution)/shard_map/ppermute | solution.py:360
  60.5 15.2 %collective-permute-start.22 = (bf16[8,128,128]{2,1,0:T(8,128)(2,1)S(1)}, bf16[8,128,128]{2,1,0:T(8,128)(2,1)S(1)}, u32[]{:S(2)}, u32[]{:S(2)}) collective-permute-start(bf16[8,128,128]{2,1,0:T(8,128)(2,1)S(1)} %bitcast.25), channel_id=1, source_target_pairs={{0,8},{4,12},{8,0},{12,4},{16,24},{20,28},{24,16},{28,20},{1,9},{5... | collective-permute-start | bytes 786440 | tf_op jit(solution)/shard_map/ppermute | solution.py:360
  63.7 12.1 %collective-permute-start.23 = (bf16[8,128,128]{2,1,0:T(8,128)(2,1)S(1)}, bf16[8,128,128]{2,1,0:T(8,128)(2,1)S(1)}, u32[]{:S(2)}, u32[]{:S(2)}) collective-permute-start(bf16[8,128,128]{2,1,0:T(8,128)(2,1)S(1)} %bitcast.26), channel_id=1, source_target_pairs={{0,4},{4,0},{8,12},{12,8},{16,20},{20,16},{24,28},{28,24},{1,5},{5... | collective-permute-start | bytes 786440 | tf_op jit(solution)/shard_map/ppermute | solution.py:360
  75.7 1.7 %collective-permute-start.24 = (bf16[5,256,128]{2,1,0:T(8,128)(2,1)S(1)}, bf16[5,256,128]{2,1,0:T(8,128)(2,1)S(1)}, u32[]{:S(2)}, u32[]{:S(2)}) collective-permute-start(bf16[5,256,128]{2,1,0:T(8,128)(2,1)S(1)} %get-tuple-element.101.refs_0_), channel_id=1, source_target_pairs={{0,1},{1,0},{2,3},{3,2},{4,5},{5,4},{6,7},{7,6},{8,9},{9,8},{10,11... | collective-permute-start | bytes 983048 | tf_op jit(solution)/shard_map/ppermute | solution.py:360
  78.2 28.1 %copy-start = (bf16[1,6,8,128,128]{4,3,2,1,0:T(8,128)(2,1)S(1)}, bf16[1,6,8,128,128]{4,3,2,1,0:T(8,128)(2,1)}, u32[]{:S(2)}) copy-start(bf16[1,6,8,128,128]{4,3,2,1,0:T(8,128)(2,1)} %param.18) | copy-start | bytes 4718596
  78.2 28.1 %copy-start.1 = (bf16[1,16,128,128]{3,2,1,0:T(8,128)(2,1)S(1)}, bf16[1,16,128,128]{3,2,1,0:T(8,128)(2,1)}, u32[]{:S(2)}) copy-start(bf16[1,16,128,128]{3,2,1,0:T(8,128)(2,1)} %param.15) | copy-start | bytes 1572868
  78.3 28.0 %copy-start.6 = (s32[1,6,8]{2,0,1:T(1,128)S(1)}, s32[1,6,8]{2,0,1:T(1,128)}, u32[]{:S(2)}) copy-start(s32[1,6,8]{2,0,1:T(1,128)} %param.19) | copy-start | bytes 580
  78.3 28.0 %copy-start.7 = (s32[1,6,8]{2,0,1:T(1,128)S(1)}, s32[1,6,8]{2,0,1:T(1,128)}, u32[]{:S(2)}) copy-start(s32[1,6,8]{2,0,1:T(1,128)} %param.20) | copy-start | bytes 580
  78.3 28.0 %copy-start.8 = (s32[1,16]{1,0:T(1,128)S(1)}, s32[1,16]{1,0:T(1,128)}, u32[]{:S(2)}) copy-start(s32[1,16]{1,0:T(1,128)} %refs_0_.7) | copy-start | bytes 196
  78.3 28.0 %copy-start.9 = (s32[1,16]{1,0:T(1,128)S(1)}, s32[1,16]{1,0:T(1,128)}, u32[]{:S(2)}) copy-start(s32[1,16]{1,0:T(1,128)} %refs_1_.7) | copy-start | bytes 196
  78.3 5.6 %collective-permute-start.25 = (bf16[4,32,512]{2,1,0:T(8,128)(2,1)S(1)}, bf16[4,32,512]{2,1,0:T(8,128)(2,1)S(1)}, u32[]{:S(2)}, u32[]{:S(2)}) collective-permute-start(bf16[4,32,512]{2,1,0:T(8,128)(2,1)S(1)} %get-tuple-element.105), channel_id=1, source_target_pairs={{0,4},{4,0},{8,12},{12,8},{16,20},{20,16},{24,28},{28,24},{1,5},{5... | collective-permute-start | bytes 393224 | tf_op jit(solution)/shard_map/ppermute | solution.py:360
  83.9 6.5 %collective-permute-start.26 = (bf16[4,32,512]{2,1,0:T(8,128)(2,1)S(1)}, bf16[4,32,512]{2,1,0:T(8,128)(2,1)S(1)}, u32[]{:S(2)}, u32[]{:S(2)}) collective-permute-start(bf16[4,32,512]{2,1,0:T(8,128)(2,1)S(1)} %add_convert_fusion.5), channel_id=1, source_target_pairs={{0,8},{4,12},{8,0},{12,4},{16,24},{20,28},{24,16},{28,20},{1,9},{5... | collective-permute-start | bytes 393224 | tf_op jit(solution)/shard_map/ppermute | solution.py:360
  84.0 7.6 %collective-permute-start.27 = (bf16[8,128,128]{2,1,0:T(8,128)(2,1)S(1)}, bf16[8,128,128]{2,1,0:T(8,128)(2,1)S(1)}, u32[]{:S(2)}, u32[]{:S(2)}) collective-permute-start(bf16[8,128,128]{2,1,0:T(8,128)(2,1)S(1)} %collective-permute-done.21.refs_6_), channel_id=1, source_target_pairs={{0,4},{4,0},{8,12},{12,8},{16,20},{20,16},{24,28},{28,24},{1,5},{5... | collective-permute-start | bytes 786440 | tf_op jit(solution)/shard_map/ppermute | solution.py:360
  84.6 9.7 %collective-permute-start.28 = (bf16[8,128,128]{2,1,0:T(8,128)(2,1)S(1)}, bf16[8,128,128]{2,1,0:T(8,128)(2,1)S(1)}, u32[]{:S(2)}, u32[]{:S(2)}) collective-permute-start(bf16[8,128,128]{2,1,0:T(8,128)(2,1)S(1)} %collective-permute-done.21.refs_6_), channel_id=1, source_target_pairs={{0,8},{4,12},{8,0},{12,4},{16,24},{20,28},{24,16},{28,20},{1,9},{5... | collective-permute-start | bytes 786440 | tf_op jit(solution)/shard_map/ppermute | solution.py:360
  94.3 7.5 %collective-permute-start.29 = (bf16[4,32,512]{2,1,0:T(8,128)(2,1)S(1)}, bf16[4,32,512]{2,1,0:T(8,128)(2,1)S(1)}, u32[]{:S(2)}, u32[]{:S(2)}) collective-permute-start(bf16[4,32,512]{2,1,0:T(8,128)(2,1)S(1)} %add_convert_fusion.4), channel_id=1, source_target_pairs={{0,16},{4,20},{8,24},{12,28},{16,0},{20,4},{24,8},{28,12},{1,17},{... | collective-permute-start | bytes 393224 | tf_op jit(solution)/shard_map/ppermute | solution.py:360
  95.5 6.9 %collective-permute-start.30 = (bf16[8,128,128]{2,1,0:T(8,128)(2,1)S(1)}, bf16[8,128,128]{2,1,0:T(8,128)(2,1)S(1)}, u32[]{:S(2)}, u32[]{:S(2)}) collective-permute-start(bf16[8,128,128]{2,1,0:T(8,128)(2,1)S(1)} %collective-permute-done.22.refs_8_), channel_id=1, source_target_pairs={{0,4},{4,0},{8,12},{12,8},{16,20},{20,16},{24,28},{28,24},{1,5},{5... | collective-permute-start | bytes 786440 | tf_op jit(solution)/shard_map/ppermute | solution.py:360
  96.0 8.8 %collective-permute-start.31 = (bf16[8,128,128]{2,1,0:T(8,128)(2,1)S(1)}, bf16[8,128,128]{2,1,0:T(8,128)(2,1)S(1)}, u32[]{:S(2)}, u32[]{:S(2)}) collective-permute-start(bf16[8,128,128]{2,1,0:T(8,128)(2,1)S(1)} %collective-permute-done.27.refs_7_), channel_id=1, source_target_pairs={{0,8},{4,12},{8,0},{12,4},{16,24},{20,28},{24,16},{28,20},{1,9},{5... | collective-permute-start | bytes 786440 | tf_op jit(solution)/shard_map/ppermute | solution.py:360
  104.8 6.3 %collective-permute-start.32 = (bf16[4,32,512]{2,1,0:T(8,128)(2,1)S(1)}, bf16[4,32,512]{2,1,0:T(8,128)(2,1)S(1)}, u32[]{:S(2)}, u32[]{:S(2)}) collective-permute-start(bf16[4,32,512]{2,1,0:T(8,128)(2,1)S(1)} %add_convert_fusion.3.mine_ref), channel_id=1, source_target_pairs={{0,4},{4,0},{8,12},{12,8},{16,20},{20,16},{24,28},{28,24},{1,5},{5... | collective-permute-start | bytes 393224 | tf_op jit(solution)/shard_map/ppermute | solution.py:360

commit v11 on v10

--- a/solution.py
+++ b/solution.py
@@ -414,27 +414,33 @@
     def tied(x, *others):
         return lax.optimization_barrier((x, others))[0]
 
-    sends = forward([7, 3, 5, 1], [blocks], [like(shape, BF16)] * 4)
+    sends = forward([7, 5, 3, 1], [blocks], [like(shape, BF16)] * 4)
     made = forward(
-        [6, 2, 4, 0],
+        [6, 4, 2, 0],
         [blocks, cotangent.reshape(shape), w_self, w_neigh],
         [like(shape, F32)] * 4
         + [like((2, per_feat, block, width), BF16)] * feats
         + [like((2, width, full), BF16)],
     )
-    keep_6, keep_2, keep_4, keep = made[:4]
+    keep_6, keep_4, keep_2, keep = made[:4]
     early_pieces, pair = made[4:-1], made[-1]
     weights = relayed(pair)
-    early = [early_pieces[0]] + [crossed(early_pieces[m], m, "feat") for m in range(1, feats)]
-    near_6, near_2, near_4, near_0 = (crossed(send, near) for send in sends)
+    near_6, near_4, near_2 = (crossed(send, near) for send in sends[:3])
     sum_6 = (keep_6 + near_6.astype(F32)).astype(BF16)
+    near_4, weights[2] = lax.optimization_barrier((near_4, weights[2]))
+    sum_4 = (keep_4 + near_4.astype(F32) + crossed(sum_6, 2).astype(F32)).astype(BF16)
+    far_0 = crossed(sum_4, 4)
+    keep_2, send_1, early_pieces = tied((keep_2, sends[3], early_pieces), sum_4)
+    near_0 = crossed(send_1, near)
     sum_2 = (keep_2 + near_2.astype(F32)).astype(BF16)
     mid_0 = crossed(sum_2, 2)
-    near_4, weights[2] = lax.optimization_barrier((tied(near_4, sum_2), weights[2]))
-    sum_4 = (keep_4 + near_4.astype(F32) + crossed(sum_6, 2).astype(F32)).astype(BF16)
-    far_0 = crossed(sum_4, 4)
-    part = keep + near_0.astype(F32)
-    arrived = [far_0, mid_0]
+    early_2, early_3 = crossed(early_pieces[2], 2, "feat"), crossed(early_pieces[3], 3, "feat")
+    far_0, early_2, early_3, early_1 = lax.optimization_barrier(
+        (far_0, early_2, early_3, early_pieces[1])
+    )
+    early = [early_pieces[0], crossed(early_1, 1, "feat"), early_2, early_3]
+    part = keep + mid_0.astype(F32) + near_0.astype(F32)
+    arrived = [far_0]
     early, weights, arrived = lax.optimization_barrier((early, weights, arrived))
     agg, *agg_pieces = small_call(
         functools.partial(agg_kernel, feats),
@@ -458,8 +464,8 @@
         found[mask] = crossed(dsum, mask)
     sent = tied(sent, dsum)
     come_2, come_3 = crossed(sent[1], 2, "feat"), crossed(sent[2], 3, "feat")
-    come_2, come_3, found[4], found[2], found[1], sent[0] = lax.optimization_barrier(
-        (come_2, come_3, found[4], found[2], found[1], sent[0])
+    found[4], come_2, come_3, found[2], found[1], sent[0] = lax.optimization_barrier(
+        (found[4], come_2, come_3, found[2], found[1], sent[0])
     )
     come = [crossed(sent[0], 1, "feat"), come_2, come_3]
     (out,) = small_call(place_kernel, [like((feats, some, width), BF16)], [own_out, *come])

time: 112 us -> 107 us (0.955)
  waiting for transfers between devices: 55.1 us -> 47.2 us
  starting transfers between devices: 33.4 us -> 37 us
    ppermute x33, waiting for transfers between devices: 55.1 us -> 47.2 us  [crossed(): lax.ppermute(x, axis, [(i, i ^ mask) for i in range(lax.axis_size(axis))])]
    ppermute x33, starting transfers between devices: 33.4 us -> 37 us  [crossed(): lax.ppermute(x, axis, [(i, i ^ mask) for i in range(lax.axis_size(axis))])]
  transfers between devices with their start and end apart: 33 -> 33, of which waited for: 18 -> 20; matrix products, arithmetic and copies ran while one was open for 5% -> 4% of each run, Pallas kernels for 9% -> 10%
where the time goes in v11:
time: 107 us
  waiting for transfers between devices  47.2 us (44%)
  starting transfers between devices  37 us (35%)
  Pallas kernels  17.2 us (16%)
  other arithmetic  4.15 us (4%)
    ppermute x33, waiting for transfers between devices, crossed(): lax.ppermute(x, axis, [(i, i ^ mask) for i in range(lax.axis_size(axis))])  47.2 us
    ppermute x33, starting transfers between devices, crossed(): lax.ppermute(x, axis, [(i, i ^ mask) for i in range(lax.axis_size(axis))])  37 us
    pallas_call x4, Pallas kernels, tiles_call(): pl.pallas_call(functools.partial(tiles_kernel, masks, offsets, parts_tota...  13.3 us
    pallas_call x5, Pallas kernels, small_call(): pl.pallas_call(kernel, out_shape=outs, in_specs=[VMEM] * len(arrays), out...  3.86 us
  transfers between devices with their start and end apart: 33, of which 20 were waited for; matrix products, arithmetic and copies ran while one was open for 4% of the time, Pallas kernels for 10%

profile of v11, /device:TPU:0, one launch (start us, length us, event | category | flops | bytes accessed | tf_op | source)
XLA Modules:
  0.0 107.0 jit_solution(978728019591035769)
XLA Ops:
  0.6 3.7 %shard_map.139 = (bf16[8,128,128]{2,1,0:T(8,128)(2,1)}, bf16[8,128,128]{2,1,0:T(8,128)(2,1)}, bf16[8,128,128]{2,1,0:T(8,128)(2,1)}, bf16[8,128,128]{2,1,0:T(8,128)(2,1)}) custom-call(s32[1,16]{1,0:T(1,128)} %refs_0_.7, s32[1,16]{1,0:T(1,128)} %refs_1_.7, s32[6,1,8]{2,1,0:T(1,128)} %bitcast.30, s32[6,1,8]{2,1,0:T(1,128)} %bitcast.34, ...), custom_call_target="tpu_custom_call" | custom-call | flops 1 | bytes 1 | tf_op jit(solution)/shard_map/pallas_call | solution.py:224
  4.4 3.0 %collective-permute-start.2 = (bf16[8,128,128]{2,1,0:T(8,128)(2,1)}, bf16[8,128,128]{2,1,0:T(8,128)(2,1)S(1)}, u32[]{:S(2)}, u32[]{:S(2)}) collective-permute-start(bf16[8,128,128]{2,1,0:T(8,128)(2,1)} %get-tuple-element.80), channel_id=1, source_target_pairs={{0,4},{4,0},{8,12},{12,8},{16,20},{20,16},{24,28},{28,24},{1,5},{5... | collective-permute-start | bytes 786440 | tf_op jit(solution)/shard_map/ppermute | solution.py:360
  7.4 4.8 %shard_map.138 = (f32[8,128,128]{2,1,0:T(8,128)}, f32[8,128,128]{2,1,0:T(8,128)}, f32[8,128,128]{2,1,0:T(8,128)}, f32[8,128,128]{2,1,0:T(8,128)}, bf16[2,2,128,1...) custom-call(s32[1,16]{1,0:T(1,128)} %refs_0_.7, ...), custom_call_target="tpu_custom_call" | custom-call | flops 1 | bytes 1 | tf_op jit(solution)/shard_map/pallas_call | solution.py:224
  12.3 1.6 %collective-permute-start.1 = (bf16[2,128,512]{2,1,0:T(8,128)(2,1)}, bf16[2,128,512]{2,1,0:T(8,128)(2,1)S(1)}, u32[]{:S(2)}, u32[]{:S(2)}) collective-permute-start(bf16[2,128,512]{2,1,0:T(8,128)(2,1)} %get-tuple-element.95.refs_0_), channel_id=1, source_target_pairs={{0,2},{1,3},{2,0},{3,1},{4,6},{5,7},{6,4},{7,5},{8,10},{9,11},{10,... | collective-permute-start | bytes 786440 | tf_op jit(solution)/shard_map/ppermute | solution.py:360
  13.8 0.5 collective-permute-start
  14.3 1.1 %add_convert_fusion.2 = bf16[8,128,128]{2,1,0:T(8,128)(2,1)S(1)} fusion(f32[8,128,128]{2,1,0:T(8,128)} %get-tuple-element.79, bf16[8,128,128]{2,1,0:T(8,128)(2,1)S(1)} %collective-permute-done.2), kind=kLoop, calls=%fused_computation.3 | loop fusion | flops 393216 | bytes 1048576 | tf_op jit(solution)/shard_map/convert_element_type | solution.py:429
  15.5 1.6 %collective-permute-start.3 = (bf16[8,128,128]{2,1,0:T(8,128)(2,1)S(1)}, bf16[8,128,128]{2,1,0:T(8,128)(2,1)S(1)}, u32[]{:S(2)}, u32[]{:S(2)}) collective-permute-start(bf16[8,128,128]{2,1,0:T(8,128)(2,1)S(1)} %add_convert_fusion.2), channel_id=1, source_target_pairs={{0,8},{4,12},{8,0},{12,4},{16,24},{20,28},{24,16},{28,20},{1,9},{5... | collective-permute-start | bytes 786440 | tf_op jit(solution)/shard_map/ppermute | solution.py:360
  17.1 1.5 %collective-permute-start.4 = (bf16[8,128,128]{2,1,0:T(8,128)(2,1)S(1)}, bf16[8,128,128]{2,1,0:T(8,128)(2,1)S(1)}, u32[]{:S(2)}, u32[]{:S(2)}) collective-permute-start(bf16[8,128,128]{2,1,0:T(8,128)(2,1)S(1)} %copy-done.13), channel_id=1, source_target_pairs={{0,4},{4,0},{8,12},{12,8},{16,20},{20,16},{24,28},{28,24},{1,5},{5... | collective-permute-start | bytes 786440 | tf_op jit(solution)/shard_map/ppermute | solution.py:360
  18.7 1.6 %collective-permute-done.1.refs_2_ = bf16[2,128,512]{2,1,0:T(8,128)(2,1)S(1)} collective-permute-done((bf16[2,128,512]{2,1,0:T(8,128)(2,1)}, bf16[2,128,512]{2,1,0:T(8,128)(2,1)S(1)}, u32[]{:S(2)}, u32[]{:S(2)}) %collective-permute-start.1) | collective-permute-done | bytes 262176 | tf_op jit(solution)/shard_map/ppermute | solution.py:360
  20.3 2.8 %collective-permute-done = bf16[8,128,128]{2,1,0:T(8,128)(2,1)S(1)} collective-permute-done((bf16[8,128,128]{2,1,0:T(8,128)(2,1)S(1)}, bf16[8,128,128]{2,1,0:T(8,128)(2,1)S(1)}, u32[]{:S(2)}, u32[]{:S(2)}) %collective-permute-start) | collective-permute-done | bytes 262176 | tf_op jit(solution)/shard_map/ppermute | solution.py:360
  23.1 1.1 %add_convert_fusion.1 = bf16[8,128,128]{2,1,0:T(8,128)(2,1)S(1)} fusion(bf16[8,128,128]{2,1,0:T(8,128)(2,1)S(1)} %collective-permute-done.3, f32[8,128,128]{2,1,0:T(8,128)} %get-tuple-element.75, bf16[8,128,128]{2,1,0:T(8,128)(2,1)S(1)} %collective-permute-done), kind=kLoop, calls=%fused_computation.2 | loop fusion | flops 655360 | bytes 1310720 | tf_op jit(solution)/shard_map/convert_element_type | solution.py:431
  24.2 2.7 %collective-permute-start.7 = (bf16[8,128,128]{2,1,0:T(8,128)(2,1)S(1)}, bf16[8,128,128]{2,1,0:T(8,128)(2,1)S(1)}, u32[]{:S(2)}, u32[]{:S(2)}) collective-permute-start(bf16[8,128,128]{2,1,0:T(8,128)(2,1)S(1)} %add_convert_fusion.1), channel_id=1, source_target_pairs={{0,16},{4,20},{8,24},{12,28},{16,0},{20,4},{24,8},{28,12},{1,17},{... | collective-permute-start | bytes 786440 | tf_op jit(solution)/shard_map/ppermute | solution.py:360
  26.9 0.8 add_convert_fusion
  27.7 1.6 %collective-permute-start.5 = (bf16[8,128,128]{2,1,0:T(8,128)(2,1)}, bf16[8,128,128]{2,1,0:T(8,128)(2,1)S(1)}, u32[]{:S(2)}, u32[]{:S(2)}) collective-permute-start(bf16[8,128,128]{2,1,0:T(8,128)(2,1)} %add_convert_fusion), channel_id=1, source_target_pairs={{0,8},{4,12},{8,0},{12,4},{16,24},{20,28},{24,16},{28,20},{1,9},{5... | collective-permute-start | bytes 786440 | tf_op jit(solution)/shard_map/ppermute | solution.py:360
  29.3 1.1 %collective-permute-start.6 = (bf16[8,128,128]{2,1,0:T(8,128)(2,1)}, bf16[8,128,128]{2,1,0:T(8,128)(2,1)}, u32[]{:S(2)}, u32[]{:S(2)}) collective-permute-start(bf16[8,128,128]{2,1,0:T(8,128)(2,1)} %get-tuple-element.83), channel_id=1, source_target_pairs={{0,4},{4,0},{8,12},{12,8},{16,20},{20,16},{24,28},{28,24},{1,5},{5... | collective-permute-start | bytes 786440 | tf_op jit(solution)/shard_map/ppermute | solution.py:360
  30.4 1.3 %collective-permute-start.8 = (bf16[2,2,128,128]{3,2,1,0:T(8,128)(2,1)}, bf16[2,2,128,128]{3,2,1,0:T(8,128)(2,1)S(1)}, u32[]{:S(2)}, u32[]{:S(2)}) collective-permute-start(bf16[2,2,128,128]{3,2,1,0:T(8,128)(2,1)} %get-tuple-element.85), channel_id=1, source_target_pairs={{0,2},{1,3},{2,0},{3,1},{4,6},{5,7},{6,4},{7,5},{8,10},{9,11},{10,... | collective-permute-start | bytes 393224 | tf_op jit(solution)/shard_map/ppermute | solution.py:360
  31.7 0.2 copy.15.inv_ref
  32.0 4.4 %collective-permute-done.8.refs_6_ = bf16[2,2,128,128]{3,2,1,0:T(8,128)(2,1)S(1)} collective-permute-done((bf16[2,2,128,128]{3,2,1,0:T(8,128)(2,1)}, bf16[2,2,128,128]{3,2,1,0:T(8,128)(2,1)S(1)}, u32[]{:S(2)}, u32[]{:S(2)}) %collective-permute-start.8) | collective-permute-done | bytes 131104 | tf_op jit(solution)/shard_map/ppermute | solution.py:360
  36.3 1.3 %collective-permute-done.9.refs_7_ = bf16[2,2,128,128]{3,2,1,0:T(8,128)(2,1)S(1)} collective-permute-done((bf16[2,2,128,128]{3,2,1,0:T(8,128)(2,1)}, bf16[2,2,128,128]{3,2,1,0:T(8,128)(2,1)S(1)}, u32[]{:S(2)}, u32[]{:S(2)}) %collective-permute-start.9) | collective-permute-done | bytes 131104 | tf_op jit(solution)/shard_map/ppermute | solution.py:360
  37.7 0.9 collective-permute-start.12
  38.6 0.4 collective-permute-done.5
  39.0 1.0 convert_add_fusion.keep_ref
  40.0 0.2 shard_map.140
  40.3 0.3 collective-permute-start.13
  40.6 1.1 %collective-permute-start.14 = (bf16[2,128,128]{2,1,0:T(8,128)(2,1)S(1)}, bf16[2,128,128]{2,1,0:T(8,128)(2,1)S(1)}, u32[]{:S(2)}, u32[]{:S(2)}) collective-permute-start(bf16[2,128,128]{2,1,0:T(8,128)(2,1)S(1)} %get-tuple-element.105), channel_id=1, source_target_pairs={{0,2},{1,3},{2,0},{3,1},{4,6},{5,7},{6,4},{7,5},{8,10},{9,11},{10,... | collective-permute-start | bytes 196616 | tf_op jit(solution)/shard_map/ppermute | solution.py:360
  41.7 0.5 collective-permute-start.15
  42.2 0.1 dynamic_slice.3
  42.3 0.1 copy.16.inv_ref
  42.5 2.7 %collective-permute-done.14.refs_10_ = bf16[2,128,128]{2,1,0:T(8,128)(2,1)S(1)} collective-permute-done((bf16[2,128,128]{2,1,0:T(8,128)(2,1)S(1)}, bf16[2,128,128]{2,1,0:T(8,128)(2,1)S(1)}, u32[]{:S(2)}, u32[]{:S(2)}) %collective-permute-start.14) | collective-permute-done | bytes 65568 | tf_op jit(solution)/shard_map/ppermute | solution.py:360
  45.1 0.9 collective-permute-done.15.refs_11_
  46.0 1.3 %shard_map.141 = (bf16[5,256,128]{2,1,0:T(8,128)(2,1)S(1)}, bf16[5,256,128]{2,1,0:T(8,128)(2,1)S(1)}, bf16[5,256,128]{2,1,0:T(8,128)(2,1)S(1)}, bf16[256,128]{1,...) custom-call(f32[256,1]{1,0:T(8,128)S(1)} %copy.16.inv_ref, ...), custom_call_target="tpu_custom_call" | custom-call | flops 1 | bytes 1 | tf_op jit(solution)/shard_map/pallas_call | solution.py:244
  47.3 0.2 collective-permute-start.16
  47.5 1.1 collective-permute-start.17
  48.5 0.7 collective-permute-start.18
  49.2 3.1 %collective-permute-done.17 = bf16[256,128]{1,0:T(8,128)(2,1)S(1)} collective-permute-done((bf16[256,128]{1,0:T(8,128)(2,1)S(1)}, bf16[256,128]{1,0:T(8,128)(2,1)S(1)}, u32[]{:S(2)}, u32[]{:S(2)}) %collective-permute-start.17) | collective-permute-done | bytes 65568 | tf_op jit(solution)/shard_map/ppermute | solution.py:360
  52.3 0.6 collective-permute-done.18
  52.9 1.1 collective-permute-start.20
  53.9 0.6 collective-permute-start.21
  54.5 2.2 %collective-permute-start.19 = (bf16[8,128,128]{2,1,0:T(8,128)(2,1)S(1)}, bf16[8,128,128]{2,1,0:T(8,128)(2,1)S(1)}, u32[]{:S(2)}, u32[]{:S(2)}) collective-permute-start(bf16[8,128,128]{2,1,0:T(8,128)(2,1)S(1)} %bitcast.24), channel_id=1, source_target_pairs={{0,16},{4,20},{8,24},{12,28},{16,0},{20,4},{24,8},{28,12},{1,17},{... | collective-permute-start | bytes 786440 | tf_op jit(solution)/shard_map/ppermute | solution.py:360
  56.8 2.4 %collective-permute-start.22 = (bf16[8,128,128]{2,1,0:T(8,128)(2,1)S(1)}, bf16[8,128,128]{2,1,0:T(8,128)(2,1)S(1)}, u32[]{:S(2)}, u32[]{:S(2)}) collective-permute-start(bf16[8,128,128]{2,1,0:T(8,128)(2,1)S(1)} %bitcast.25), channel_id=1, source_target_pairs={{0,8},{4,12},{8,0},{12,4},{16,24},{20,28},{24,16},{28,20},{1,9},{5... | collective-permute-start | bytes 786440 | tf_op jit(solution)/shard_map/ppermute | solution.py:360
  59.2 1.3 %collective-permute-start.23 = (bf16[8,128,128]{2,1,0:T(8,128)(2,1)S(1)}, bf16[8,128,128]{2,1,0:T(8,128)(2,1)S(1)}, u32[]{:S(2)}, u32[]{:S(2)}) collective-permute-start(bf16[8,128,128]{2,1,0:T(8,128)(2,1)S(1)} %bitcast.26), channel_id=1, source_target_pairs={{0,4},{4,0},{8,12},{12,8},{16,20},{20,16},{24,28},{28,24},{1,5},{5... | collective-permute-start | bytes 786440 | tf_op jit(solution)/shard_map/ppermute | solution.py:360
  60.4 9.5 %collective-permute-done.19.refs_6_ = bf16[8,128,128]{2,1,0:T(8,128)(2,1)S(1)} collective-permute-done((bf16[8,128,128]{2,1,0:T(8,128)(2,1)S(1)}, bf16[8,128,128]{2,1,0:T(8,128)(2,1)S(1)}, u32[]{:S(2)}, u32[]{:S(2)}) %collective-permute-start.19) | collective-permute-done | bytes 262176 | tf_op jit(solution)/shard_map/ppermute | solution.py:360
  69.9 0.1 collective-permute-done.22.refs_8_
  70.1 1.6 %collective-permute-done.24.refs_1_ = bf16[5,256,128]{2,1,0:T(8,128)(2,1)S(1)} collective-permute-done((bf16[5,256,128]{2,1,0:T(8,128)(2,1)S(1)}, bf16[5,256,128]{2,1,0:T(8,128)(2,1)S(1)}, u32[]{:S(2)}, u32[]{:S(2)}) %collective-permute-start.24) | collective-permute-done | bytes 327712 | tf_op jit(solution)/shard_map/ppermute | solution.py:360
  71.7 0.8 shard_map.142
  72.6 1.0 collective-permute-start.25
  73.6 4.6 %collective-permute-done.25 = bf16[4,32,512]{2,1,0:T(8,128)(2,1)S(1)} collective-permute-done((bf16[4,32,512]{2,1,0:T(8,128)(2,1)S(1)}, bf16[4,32,512]{2,1,0:T(8,128)(2,1)S(1)}, u32[]{:S(2)}, u32[]{:S(2)}) %collective-permute-start.25) | collective-permute-done | bytes 131104 | tf_op jit(solution)/shard_map/ppermute | solution.py:360
  78.2 1.3 %collective-permute-start.26 = (bf16[4,32,512]{2,1,0:T(8,128)(2,1)S(1)}, bf16[4,32,512]{2,1,0:T(8,128)(2,1)S(1)}, u32[]{:S(2)}, u32[]{:S(2)}) collective-permute-start(bf16[4,32,512]{2,1,0:T(8,128)(2,1)S(1)} %add_convert_fusion.5), channel_id=1, source_target_pairs={{0,8},{4,12},{8,0},{12,4},{16,24},{20,28},{24,16},{28,20},{1,9},{5... | collective-permute-start | bytes 393224 | tf_op jit(solution)/shard_map/ppermute | solution.py:360
  79.5 1.4 %collective-permute-start.27 = (bf16[8,128,128]{2,1,0:T(8,128)(2,1)S(1)}, bf16[8,128,128]{2,1,0:T(8,128)(2,1)S(1)}, u32[]{:S(2)}, u32[]{:S(2)}) collective-permute-start(bf16[8,128,128]{2,1,0:T(8,128)(2,1)S(1)} %collective-permute-done.19.refs_6_), channel_id=1, source_target_pairs={{0,4},{4,0},{8,12},{12,8},{16,20},{20,16},{24,28},{28,24},{1,5},{5... | collective-permute-start | bytes 786440 | tf_op jit(solution)/shard_map/ppermute | solution.py:360
  80.8 0.4 collective-permute-start.28
  81.3 3.1 %collective-permute-done.26 = bf16[4,32,512]{2,1,0:T(8,128)(2,1)S(1)} collective-permute-done((bf16[4,32,512]{2,1,0:T(8,128)(2,1)S(1)}, bf16[4,32,512]{2,1,0:T(8,128)(2,1)S(1)}, u32[]{:S(2)}, u32[]{:S(2)}) %collective-permute-start.26) | collective-permute-done | bytes 131104 | tf_op jit(solution)/shard_map/ppermute | solution.py:360
  84.4 2.3 %collective-permute-done.27.refs_7_ = bf16[8,128,128]{2,1,0:T(8,128)(2,1)S(1)} collective-permute-done((bf16[8,128,128]{2,1,0:T(8,128)(2,1)S(1)}, bf16[8,128,128]{2,1,0:T(8,128)(2,1)S(1)}, u32[]{:S(2)}, u32[]{:S(2)}) %collective-permute-start.27) | collective-permute-done | bytes 262176 | tf_op jit(solution)/shard_map/ppermute | solution.py:360
  86.7 2.1 %collective-permute-done.28.refs_8_ = bf16[8,128,128]{2,1,0:T(8,128)(2,1)S(1)} collective-permute-done((bf16[8,128,128]{2,1,0:T(8,128)(2,1)S(1)}, bf16[8,128,128]{2,1,0:T(8,128)(2,1)S(1)}, u32[]{:S(2)}, u32[]{:S(2)}) %collective-permute-start.28) | collective-permute-done | bytes 262176 | tf_op jit(solution)/shard_map/ppermute | solution.py:360
  88.8 2.3 %collective-permute-start.29 = (bf16[4,32,512]{2,1,0:T(8,128)(2,1)S(1)}, bf16[4,32,512]{2,1,0:T(8,128)(2,1)S(1)}, u32[]{:S(2)}, u32[]{:S(2)}) collective-permute-start(bf16[4,32,512]{2,1,0:T(8,128)(2,1)S(1)} %add_convert_fusion.4), channel_id=1, source_target_pairs={{0,16},{4,20},{8,24},{12,28},{16,0},{20,4},{24,8},{28,12},{1,17},{... | collective-permute-start | bytes 393224 | tf_op jit(solution)/shard_map/ppermute | solution.py:360
  91.2 1.3 %collective-permute-start.30 = (bf16[8,128,128]{2,1,0:T(8,128)(2,1)S(1)}, bf16[8,128,128]{2,1,0:T(8,128)(2,1)S(1)}, u32[]{:S(2)}, u32[]{:S(2)}) collective-permute-start(bf16[8,128,128]{2,1,0:T(8,128)(2,1)S(1)} %collective-permute-done.22.refs_8_), channel_id=1, source_target_pairs={{0,4},{4,0},{8,12},{12,8},{16,20},{20,16},{24,28},{28,24},{1,5},{5... | collective-permute-start | bytes 786440 | tf_op jit(solution)/shard_map/ppermute | solution.py:360
  92.4 1.7 %collective-permute-start.31 = (bf16[8,128,128]{2,1,0:T(8,128)(2,1)S(1)}, bf16[8,128,128]{2,1,0:T(8,128)(2,1)S(1)}, u32[]{:S(2)}, u32[]{:S(2)}) collective-permute-start(bf16[8,128,128]{2,1,0:T(8,128)(2,1)S(1)} %collective-permute-done.27.refs_7_), channel_id=1, source_target_pairs={{0,8},{4,12},{8,0},{12,4},{16,24},{20,28},{24,16},{28,20},{1,9},{5... | collective-permute-start | bytes 786440 | tf_op jit(solution)/shard_map/ppermute | solution.py:360
  94.2 0.7 shard_map.143
  94.9 1.9 %collective-permute-done.29 = bf16[4,32,512]{2,1,0:T(8,128)(2,1)S(1)} collective-permute-done((bf16[4,32,512]{2,1,0:T(8,128)(2,1)S(1)}, bf16[4,32,512]{2,1,0:T(8,128)(2,1)S(1)}, u32[]{:S(2)}, u32[]{:S(2)}) %collective-permute-start.29) | collective-permute-done | bytes 131104 | tf_op jit(solution)/shard_map/ppermute | solution.py:360
  96.9 0.7 collective-permute-done.30.refs_9_
  97.5 3.5 %collective-permute-done.31.refs_9_ = bf16[8,128,128]{2,1,0:T(8,128)(2,1)S(1)} collective-permute-done((bf16[8,128,128]{2,1,0:T(8,128)(2,1)S(1)}, bf16[8,128,128]{2,1,0:T(8,128)(2,1)S(1)}, u32[]{:S(2)}, u32[]{:S(2)}) %collective-permute-start.31) | collective-permute-done | bytes 262176 | tf_op jit(solution)/shard_map/ppermute | solution.py:360
  101.0 0.2 collective-permute-start.32
  101.3 2.1 %shard_map.144.refs_10_ = f32[8,128,128]{2,1,0:T(8,128)S(1)} custom-call(s32[1,16]{1,0:T(1,128)S(1)} %copy-done.8, s32[1,16]{1,0:T(1,128)S(1)} %copy-done.9, s32[6,1,8]{2,1,0:T(1,128)S(1)} %bitcast.32, s32[6,1,8]{2,1,0:T(1,128)S(1)} %bitcast.36, bf16[16,128,128]{2,1,0:T(8,128)(2,1)S(1)} %bitcast.20, bf16[6,8,128,128]{3,2,1,0:T(8,128)(2,1)S(1)} %bitcast.16, ...), custom_call_target="tpu_custom_call" | custom-call | flops 1 | bytes 1 | tf_op jit(solution)/shard_map/pallas_call | solution.py:224
  103.5 2.6 %shard_map.145 = f32[8,128,128]{2,1,0:T(8,128)} custom-call(s32[1,16]{1,0:T(1,128)S(1)} %copy-done.8, s32[1,16]{1,0:T(1,128)S(1)} %copy-done.9, s32[6,1,8]{2,1,0:T(1,128)S(1)} %bitcast.33, s32[6,1,8]{2,1,0:T(1,128)S(1)} %bitcast.37, bf16[16,128,128]{2,1,0:T(8,128)(2,1)S(1)} %bitcast.21, bf16[6,8,128,128]{3,2,1,0:T(8,128)(2,1)S(1)} %bitcast.17, ...), custom_call_target="tpu_custom_call" | custom-call | flops 1 | bytes 1 | tf_op jit(solution)/shard_map/pallas_call | solution.py:224
  106.1 0.9 shard_map.146
  (55 shorter events, 0.4 us)
Async XLA Ops:
  4.4 9.4 %copy-start.14 = (bf16[8,128,128]{2,1,0:T(8,128)(2,1)S(1)}, bf16[8,128,128]{2,1,0:T(8,128)(2,1)}, u32[]{:S(2)}) copy-start(bf16[8,128,128]{2,1,0:T(8,128)(2,1)} %get-tuple-element.76) | copy-start | bytes 786436
  4.4 10.0 %collective-permute-start.2 = (bf16[8,128,128]{2,1,0:T(8,128)(2,1)}, bf16[8,128,128]{2,1,0:T(8,128)(2,1)S(1)}, u32[]{:S(2)}, u32[]{:S(2)}) collective-permute-start(bf16[8,128,128]{2,1,0:T(8,128)(2,1)} %get-tuple-element.80), channel_id=1, source_target_pairs={{0,4},{4,0},{8,12},{12,8},{16,20},{20,16},{24,28},{28,24},{1,5},{5... | collective-permute-start | bytes 786440 | tf_op jit(solution)/shard_map/ppermute | solution.py:360
  7.4 9.7 %copy-start.13 = (bf16[8,128,128]{2,1,0:T(8,128)(2,1)S(1)}, bf16[8,128,128]{2,1,0:T(8,128)(2,1)}, u32[]{:S(2)}) copy-start(bf16[8,128,128]{2,1,0:T(8,128)(2,1)} %get-tuple-element.82) | copy-start | bytes 786436
  12.3 14.7 %copy-start.11 = (f32[8,128,128]{2,1,0:T(8,128)S(1)}, f32[8,128,128]{2,1,0:T(8,128)}, u32[]{:S(2)}) copy-start(f32[8,128,128]{2,1,0:T(8,128)} %get-tuple-element.81) | copy-start | bytes 1572868
  12.3 8.0 %collective-permute-start.1 = (bf16[2,128,512]{2,1,0:T(8,128)(2,1)}, bf16[2,128,512]{2,1,0:T(8,128)(2,1)S(1)}, u32[]{:S(2)}, u32[]{:S(2)}) collective-permute-start(bf16[2,128,512]{2,1,0:T(8,128)(2,1)} %get-tuple-element.95.refs_0_), channel_id=1, source_target_pairs={{0,2},{1,3},{2,0},{3,1},{4,6},{5,7},{6,4},{7,5},{8,10},{9,11},{10,... | collective-permute-start | bytes 786440 | tf_op jit(solution)/shard_map/ppermute | solution.py:360
  13.8 9.2 %collective-permute-start = (bf16[8,128,128]{2,1,0:T(8,128)(2,1)S(1)}, bf16[8,128,128]{2,1,0:T(8,128)(2,1)S(1)}, u32[]{:S(2)}, u32[]{:S(2)}) collective-permute-start(bf16[8,128,128]{2,1,0:T(8,128)(2,1)S(1)} %copy-done.14), channel_id=1, source_target_pairs={{0,4},{4,0},{8,12},{12,8},{16,20},{20,16},{24,28},{28,24},{1,5},{5... | collective-permute-start | bytes 786440 | tf_op jit(solution)/shard_map/ppermute | solution.py:360
  14.3 17.4 %copy-start.12 = (s32[1024]{0:T(1024)S(1)}, s32[1024]{0:T(1024)}, u32[]{:S(2)}) copy-start(s32[1024]{0:T(1024)} %param.14) | copy-start | bytes 12292
  15.5 20.9 %copy-start.4 = (bf16[2,128,512]{2,1,0:T(8,128)(2,1)S(1)}, bf16[2,128,512]{2,1,0:T(8,128)(2,1)}, u32[]{:S(2)}) copy-start(bf16[2,128,512]{2,1,0:T(8,128)(2,1)} %get-tuple-element.95.refs_0_) | copy-start | bytes 786436
  15.5 23.1 %copy-start.15 = (bf16[2,2,128,128]{3,2,1,0:T(8,128)(2,1)S(1)}, bf16[2,2,128,128]{3,2,1,0:T(8,128)(2,1)}, u32[]{:S(2)}) copy-start(bf16[2,2,128,128]{3,2,1,0:T(8,128)(2,1)} %get-tuple-element.88) | copy-start | bytes 393220
  15.5 23.5 %copy-start.10 = (f32[8,128,128]{2,1,0:T(8,128)S(1)}, f32[8,128,128]{2,1,0:T(8,128)}, u32[]{:S(2)}) copy-start(f32[8,128,128]{2,1,0:T(8,128)} %get-tuple-element.68) | copy-start | bytes 1572868
  15.5 7.6 %collective-permute-start.3 = (bf16[8,128,128]{2,1,0:T(8,128)(2,1)S(1)}, bf16[8,128,128]{2,1,0:T(8,128)(2,1)S(1)}, u32[]{:S(2)}, u32[]{:S(2)}) collective-permute-start(bf16[8,128,128]{2,1,0:T(8,128)(2,1)S(1)} %add_convert_fusion.2), channel_id=1, source_target_pairs={{0,8},{4,12},{8,0},{12,4},{16,24},{20,28},{24,16},{28,20},{1,9},{5... | collective-permute-start | bytes 786440 | tf_op jit(solution)/shard_map/ppermute | solution.py:360
  17.1 9.8 %collective-permute-start.4 = (bf16[8,128,128]{2,1,0:T(8,128)(2,1)S(1)}, bf16[8,128,128]{2,1,0:T(8,128)(2,1)S(1)}, u32[]{:S(2)}, u32[]{:S(2)}) collective-permute-start(bf16[8,128,128]{2,1,0:T(8,128)(2,1)S(1)} %copy-done.13), channel_id=1, source_target_pairs={{0,4},{4,0},{8,12},{12,8},{16,20},{20,16},{24,28},{28,24},{1,5},{5... | collective-permute-start | bytes 786440 | tf_op jit(solution)/shard_map/ppermute | solution.py:360
  24.2 14.3 %collective-permute-start.7 = (bf16[8,128,128]{2,1,0:T(8,128)(2,1)S(1)}, bf16[8,128,128]{2,1,0:T(8,128)(2,1)S(1)}, u32[]{:S(2)}, u32[]{:S(2)}) collective-permute-start(bf16[8,128,128]{2,1,0:T(8,128)(2,1)S(1)} %add_convert_fusion.1), channel_id=1, source_target_pairs={{0,16},{4,20},{8,24},{12,28},{16,0},{20,4},{24,8},{28,12},{1,17},{... | collective-permute-start | bytes 786440 | tf_op jit(solution)/shard_map/ppermute | solution.py:360
  27.7 11.3 %collective-permute-start.5 = (bf16[8,128,128]{2,1,0:T(8,128)(2,1)}, bf16[8,128,128]{2,1,0:T(8,128)(2,1)S(1)}, u32[]{:S(2)}, u32[]{:S(2)}) collective-permute-start(bf16[8,128,128]{2,1,0:T(8,128)(2,1)} %add_convert_fusion), channel_id=1, source_target_pairs={{0,8},{4,12},{8,0},{12,4},{16,24},{20,28},{24,16},{28,20},{1,9},{5... | collective-permute-start | bytes 786440 | tf_op jit(solution)/shard_map/ppermute | solution.py:360
  29.3 9.7 %collective-permute-start.6 = (bf16[8,128,128]{2,1,0:T(8,128)(2,1)}, bf16[8,128,128]{2,1,0:T(8,128)(2,1)}, u32[]{:S(2)}, u32[]{:S(2)}) collective-permute-start(bf16[8,128,128]{2,1,0:T(8,128)(2,1)} %get-tuple-element.83), channel_id=1, source_target_pairs={{0,4},{4,0},{8,12},{12,8},{16,20},{20,16},{24,28},{28,24},{1,5},{5... | collective-permute-start | bytes 786440 | tf_op jit(solution)/shard_map/ppermute | solution.py:360
  30.4 5.9 %collective-permute-start.8 = (bf16[2,2,128,128]{3,2,1,0:T(8,128)(2,1)}, bf16[2,2,128,128]{3,2,1,0:T(8,128)(2,1)S(1)}, u32[]{:S(2)}, u32[]{:S(2)}) collective-permute-start(bf16[2,2,128,128]{3,2,1,0:T(8,128)(2,1)} %get-tuple-element.85), channel_id=1, source_target_pairs={{0,2},{1,3},{2,0},{3,1},{4,6},{5,7},{6,4},{7,5},{8,10},{9,11},{10,... | collective-permute-start | bytes 393224 | tf_op jit(solution)/shard_map/ppermute | solution.py:360
  31.7 6.0 %collective-permute-start.9 = (bf16[2,2,128,128]{3,2,1,0:T(8,128)(2,1)}, bf16[2,2,128,128]{3,2,1,0:T(8,128)(2,1)S(1)}, u32[]{:S(2)}, u32[]{:S(2)}) collective-permute-start(bf16[2,2,128,128]{3,2,1,0:T(8,128)(2,1)} %get-tuple-element.86), channel_id=1, source_target_pairs={{0,3},{1,2},{2,1},{3,0},{4,7},{5,6},{6,5},{7,4},{8,11},{9,10},{10,... | collective-permute-start | bytes 393224 | tf_op jit(solution)/shard_map/ppermute | solution.py:360
  32.0 14.1 %copy-start.5 = (bf16[2,2,128,128]{3,2,1,0:T(8,128)(2,1)S(1)}, bf16[2,2,128,128]{3,2,1,0:T(8,128)(2,1)}, u32[]{:S(2)}) copy-start(bf16[2,2,128,128]{3,2,1,0:T(8,128)(2,1)} %get-tuple-element.99.refs_4_) | copy-start | bytes 393220
  36.3 3.7 %collective-permute-start.11 = (bf16[2,128,512]{2,1,0:T(8,128)(2,1)S(1)}, bf16[2,128,512]{2,1,0:T(8,128)(2,1)S(1)}, u32[]{:S(2)}, u32[]{:S(2)}) collective-permute-start(bf16[2,128,512]{2,1,0:T(8,128)(2,1)S(1)} %copy-done.4), channel_id=1, source_target_pairs={{0,1},{1,0},{2,3},{3,2},{4,5},{5,4},{6,7},{7,6},{8,9},{9,8},{10,11... | collective-permute-start | bytes 786440 | tf_op jit(solution)/shard_map/ppermute | solution.py:360
  37.7 2.4 %collective-permute-start.12 = (bf16[2,128,512]{2,1,0:T(8,128)(2,1)S(1)}, bf16[2,128,512]{2,1,0:T(8,128)(2,1)S(1)}, u32[]{:S(2)}, u32[]{:S(2)}) collective-permute-start(bf16[2,128,512]{2,1,0:T(8,128)(2,1)S(1)} %collective-permute-done.1.refs_2_), channel_id=1, source_target_pairs={{0,1},{1,0},{2,3},{3,2},{4,5},{5,4},{6,7},{7,6},{8,9},{9,8},{10,11... | collective-permute-start | bytes 786440 | tf_op jit(solution)/shard_map/ppermute | solution.py:360
  38.5 1.5 %collective-permute-start.10 = (bf16[2,2,128,128]{3,2,1,0:T(8,128)(2,1)S(1)}, bf16[2,2,128,128]{3,2,1,0:T(8,128)(2,1)S(1)}, u32[]{:S(2)}, u32[]{:S(2)}) collective-permute-start(bf16[2,2,128,128]{3,2,1,0:T(8,128)(2,1)S(1)} %copy-done.15), channel_id=1, source_target_pairs={{0,1},{1,0},{2,3},{3,2},{4,5},{5,4},{6,7},{7,6},{8,9},{9,8},{10,11... | collective-permute-start | bytes 393224 | tf_op jit(solution)/shard_map/ppermute | solution.py:360
  40.3 31.4 %copy-start.2 = (bf16[1024,128]{1,0:T(8,128)(2,1)S(1)}, bf16[1024,128]{1,0:T(8,128)(2,1)}, u32[]{:S(2)}) copy-start(bf16[1024,128]{1,0:T(8,128)(2,1)} %f_ref.1) | copy-start | bytes 786436
  40.3 31.4 %copy-start.3 = (bf16[128,512]{1,0:T(8,128)(2,1)S(1)}, bf16[128,512]{1,0:T(8,128)(2,1)}, u32[]{:S(2)}) copy-start(bf16[128,512]{1,0:T(8,128)(2,1)} %w_ref.1) | copy-start | bytes 393220
  40.3 2.1 %collective-permute-start.13 = (bf16[2,128,128]{2,1,0:T(8,128)(2,1)S(1)}, bf16[2,128,128]{2,1,0:T(8,128)(2,1)S(1)}, u32[]{:S(2)}, u32[]{:S(2)}) collective-permute-start(bf16[2,128,128]{2,1,0:T(8,128)(2,1)S(1)} %get-tuple-element.104), channel_id=1, source_target_pairs={{0,1},{1,0},{2,3},{3,2},{4,5},{5,4},{6,7},{7,6},{8,9},{9,8},{10,11... | collective-permute-start | bytes 196616 | tf_op jit(solution)/shard_map/ppermute | solution.py:360
  40.6 4.5 %collective-permute-start.14 = (bf16[2,128,128]{2,1,0:T(8,128)(2,1)S(1)}, bf16[2,128,128]{2,1,0:T(8,128)(2,1)S(1)}, u32[]{:S(2)}, u32[]{:S(2)}) collective-permute-start(bf16[2,128,128]{2,1,0:T(8,128)(2,1)S(1)} %get-tuple-element.105), channel_id=1, source_target_pairs={{0,2},{1,3},{2,0},{3,1},{4,6},{5,7},{6,4},{7,5},{8,10},{9,11},{10,... | collective-permute-start | bytes 196616 | tf_op jit(solution)/shard_map/ppermute | solution.py:360
  41.7 4.3 %collective-permute-start.15 = (bf16[2,128,128]{2,1,0:T(8,128)(2,1)S(1)}, bf16[2,128,128]{2,1,0:T(8,128)(2,1)S(1)}, u32[]{:S(2)}, u32[]{:S(2)}) collective-permute-start(bf16[2,128,128]{2,1,0:T(8,128)(2,1)S(1)} %get-tuple-element.106), channel_id=1, source_target_pairs={{0,3},{1,2},{2,1},{3,0},{4,7},{5,6},{6,5},{7,4},{8,11},{9,10},{10,... | collective-permute-start | bytes 196616 | tf_op jit(solution)/shard_map/ppermute | solution.py:360
  47.3 1.9 %collective-permute-start.16 = (bf16[256,128]{1,0:T(8,128)(2,1)S(1)}, bf16[256,128]{1,0:T(8,128)(2,1)S(1)}, u32[]{:S(2)}, u32[]{:S(2)}) collective-permute-start(bf16[256,128]{1,0:T(8,128)(2,1)S(1)} %get-tuple-element.108), channel_id=1, source_target_pairs={{0,1},{1,0},{2,3},{3,2},{4,5},{5,4},{6,7},{7,6},{8,9},{9,8},{10,11... | collective-permute-start | bytes 196616 | tf_op jit(solution)/shard_map/ppermute | solution.py:360
  47.5 4.8 %collective-permute-start.17 = (bf16[256,128]{1,0:T(8,128)(2,1)S(1)}, bf16[256,128]{1,0:T(8,128)(2,1)S(1)}, u32[]{:S(2)}, u32[]{:S(2)}) collective-permute-start(bf16[256,128]{1,0:T(8,128)(2,1)S(1)} %get-tuple-element.109), channel_id=1, source_target_pairs={{0,2},{1,3},{2,0},{3,1},{4,6},{5,7},{6,4},{7,5},{8,10},{9,11},{10,... | collective-permute-start | bytes 196616 | tf_op jit(solution)/shard_map/ppermute | solution.py:360
  48.5 4.3 %collective-permute-start.18 = (bf16[256,128]{1,0:T(8,128)(2,1)S(1)}, bf16[256,128]{1,0:T(8,128)(2,1)S(1)}, u32[]{:S(2)}, u32[]{:S(2)}) collective-permute-start(bf16[256,128]{1,0:T(8,128)(2,1)S(1)} %get-tuple-element.110), channel_id=1, source_target_pairs={{0,3},{1,2},{2,1},{3,0},{4,7},{5,6},{6,5},{7,4},{8,11},{9,10},{10,... | collective-permute-start | bytes 196616 | tf_op jit(solution)/shard_map/ppermute | solution.py:360
  52.9 17.1 %collective-permute-start.20 = (bf16[5,256,128]{2,1,0:T(8,128)(2,1)S(1)}, bf16[5,256,128]{2,1,0:T(8,128)(2,1)S(1)}, u32[]{:S(2)}, u32[]{:S(2)}) collective-permute-start(bf16[5,256,128]{2,1,0:T(8,128)(2,1)S(1)} %get-tuple-element.114), channel_id=1, source_target_pairs={{0,2},{1,3},{2,0},{3,1},{4,6},{5,7},{6,4},{7,5},{8,10},{9,11},{10,... | collective-permute-start | bytes 983048 | tf_op jit(solution)/shard_map/ppermute | solution.py:360
  53.9 16.1 %collective-permute-start.21 = (bf16[5,256,128]{2,1,0:T(8,128)(2,1)S(1)}, bf16[5,256,128]{2,1,0:T(8,128)(2,1)S(1)}, u32[]{:S(2)}, u32[]{:S(2)}) collective-permute-start(bf16[5,256,128]{2,1,0:T(8,128)(2,1)S(1)} %get-tuple-element.115), channel_id=1, source_target_pairs={{0,3},{1,2},{2,1},{3,0},{4,7},{5,6},{6,5},{7,4},{8,11},{9,10},{10,... | collective-permute-start | bytes 983048 | tf_op jit(solution)/shard_map/ppermute | solution.py:360
  54.5 15.4 %collective-permute-start.19 = (bf16[8,128,128]{2,1,0:T(8,128)(2,1)S(1)}, bf16[8,128,128]{2,1,0:T(8,128)(2,1)S(1)}, u32[]{:S(2)}, u32[]{:S(2)}) collective-permute-start(bf16[8,128,128]{2,1,0:T(8,128)(2,1)S(1)} %bitcast.24), channel_id=1, source_target_pairs={{0,16},{4,20},{8,24},{12,28},{16,0},{20,4},{24,8},{28,12},{1,17},{... | collective-permute-start | bytes 786440 | tf_op jit(solution)/shard_map/ppermute | solution.py:360
  56.8 13.2 %collective-permute-start.22 = (bf16[8,128,128]{2,1,0:T(8,128)(2,1)S(1)}, bf16[8,128,128]{2,1,0:T(8,128)(2,1)S(1)}, u32[]{:S(2)}, u32[]{:S(2)}) collective-permute-start(bf16[8,128,128]{2,1,0:T(8,128)(2,1)S(1)} %bitcast.25), channel_id=1, source_target_pairs={{0,8},{4,12},{8,0},{12,4},{16,24},{20,28},{24,16},{28,20},{1,9},{5... | collective-permute-start | bytes 786440 | tf_op jit(solution)/shard_map/ppermute | solution.py:360
  59.2 10.8 %collective-permute-start.23 = (bf16[8,128,128]{2,1,0:T(8,128)(2,1)S(1)}, bf16[8,128,128]{2,1,0:T(8,128)(2,1)S(1)}, u32[]{:S(2)}, u32[]{:S(2)}) collective-permute-start(bf16[8,128,128]{2,1,0:T(8,128)(2,1)S(1)} %bitcast.26), channel_id=1, source_target_pairs={{0,4},{4,0},{8,12},{12,8},{16,20},{20,16},{24,28},{28,24},{1,5},{5... | collective-permute-start | bytes 786440 | tf_op jit(solution)/shard_map/ppermute | solution.py:360
  70.0 1.7 %collective-permute-start.24 = (bf16[5,256,128]{2,1,0:T(8,128)(2,1)S(1)}, bf16[5,256,128]{2,1,0:T(8,128)(2,1)S(1)}, u32[]{:S(2)}, u32[]{:S(2)}) collective-permute-start(bf16[5,256,128]{2,1,0:T(8,128)(2,1)S(1)} %get-tuple-element.117.refs_0_), channel_id=1, source_target_pairs={{0,1},{1,0},{2,3},{3,2},{4,5},{5,4},{6,7},{7,6},{8,9},{9,8},{10,11... | collective-permute-start | bytes 983048 | tf_op jit(solution)/shard_map/ppermute | solution.py:360
  72.5 28.8 %copy-start = (bf16[1,6,8,128,128]{4,3,2,1,0:T(8,128)(2,1)S(1)}, bf16[1,6,8,128,128]{4,3,2,1,0:T(8,128)(2,1)}, u32[]{:S(2)}) copy-start(bf16[1,6,8,128,128]{4,3,2,1,0:T(8,128)(2,1)} %param.18) | copy-start | bytes 4718596
  72.5 28.8 %copy-start.1 = (bf16[1,16,128,128]{3,2,1,0:T(8,128)(2,1)S(1)}, bf16[1,16,128,128]{3,2,1,0:T(8,128)(2,1)}, u32[]{:S(2)}) copy-start(bf16[1,16,128,128]{3,2,1,0:T(8,128)(2,1)} %param.15) | copy-start | bytes 1572868
  72.5 28.8 %copy-start.6 = (s32[1,6,8]{2,0,1:T(1,128)S(1)}, s32[1,6,8]{2,0,1:T(1,128)}, u32[]{:S(2)}) copy-start(s32[1,6,8]{2,0,1:T(1,128)} %param.19) | copy-start | bytes 580
  72.5 28.8 %copy-start.7 = (s32[1,6,8]{2,0,1:T(1,128)S(1)}, s32[1,6,8]{2,0,1:T(1,128)}, u32[]{:S(2)}) copy-start(s32[1,6,8]{2,0,1:T(1,128)} %param.20) | copy-start | bytes 580
  72.5 28.8 %copy-start.8 = (s32[1,16]{1,0:T(1,128)S(1)}, s32[1,16]{1,0:T(1,128)}, u32[]{:S(2)}) copy-start(s32[1,16]{1,0:T(1,128)} %refs_0_.7) | copy-start | bytes 196
  72.6 28.8 %copy-start.9 = (s32[1,16]{1,0:T(1,128)S(1)}, s32[1,16]{1,0:T(1,128)}, u32[]{:S(2)}) copy-start(s32[1,16]{1,0:T(1,128)} %refs_1_.7) | copy-start | bytes 196
  72.6 5.6 %collective-permute-start.25 = (bf16[4,32,512]{2,1,0:T(8,128)(2,1)S(1)}, bf16[4,32,512]{2,1,0:T(8,128)(2,1)S(1)}, u32[]{:S(2)}, u32[]{:S(2)}) collective-permute-start(bf16[4,32,512]{2,1,0:T(8,128)(2,1)S(1)} %get-tuple-element.121), channel_id=1, source_target_pairs={{0,4},{4,0},{8,12},{12,8},{16,20},{20,16},{24,28},{28,24},{1,5},{5... | collective-permute-start | bytes 393224 | tf_op jit(solution)/shard_map/ppermute | solution.py:360
  78.2 6.2 %collective-permute-start.26 = (bf16[4,32,512]{2,1,0:T(8,128)(2,1)S(1)}, bf16[4,32,512]{2,1,0:T(8,128)(2,1)S(1)}, u32[]{:S(2)}, u32[]{:S(2)}) collective-permute-start(bf16[4,32,512]{2,1,0:T(8,128)(2,1)S(1)} %add_convert_fusion.5), channel_id=1, source_target_pairs={{0,8},{4,12},{8,0},{12,4},{16,24},{20,28},{24,16},{28,20},{1,9},{5... | collective-permute-start | bytes 393224 | tf_op jit(solution)/shard_map/ppermute | solution.py:360
  79.5 7.2 %collective-permute-start.27 = (bf16[8,128,128]{2,1,0:T(8,128)(2,1)S(1)}, bf16[8,128,128]{2,1,0:T(8,128)(2,1)S(1)}, u32[]{:S(2)}, u32[]{:S(2)}) collective-permute-start(bf16[8,128,128]{2,1,0:T(8,128)(2,1)S(1)} %collective-permute-done.19.refs_6_), channel_id=1, source_target_pairs={{0,4},{4,0},{8,12},{12,8},{16,20},{20,16},{24,28},{28,24},{1,5},{5... | collective-permute-start | bytes 786440 | tf_op jit(solution)/shard_map/ppermute | solution.py:360
  80.8 8.0 %collective-permute-start.28 = (bf16[8,128,128]{2,1,0:T(8,128)(2,1)S(1)}, bf16[8,128,128]{2,1,0:T(8,128)(2,1)S(1)}, u32[]{:S(2)}, u32[]{:S(2)}) collective-permute-start(bf16[8,128,128]{2,1,0:T(8,128)(2,1)S(1)} %collective-permute-done.19.refs_6_), channel_id=1, source_target_pairs={{0,8},{4,12},{8,0},{12,4},{16,24},{20,28},{24,16},{28,20},{1,9},{5... | collective-permute-start | bytes 786440 | tf_op jit(solution)/shard_map/ppermute | solution.py:360
  88.8 8.0 %collective-permute-start.29 = (bf16[4,32,512]{2,1,0:T(8,128)(2,1)S(1)}, bf16[4,32,512]{2,1,0:T(8,128)(2,1)S(1)}, u32[]{:S(2)}, u32[]{:S(2)}) collective-permute-start(bf16[4,32,512]{2,1,0:T(8,128)(2,1)S(1)} %add_convert_fusion.4), channel_id=1, source_target_pairs={{0,16},{4,20},{8,24},{12,28},{16,0},{20,4},{24,8},{28,12},{1,17},{... | collective-permute-start | bytes 393224 | tf_op jit(solution)/shard_map/ppermute | solution.py:360
  91.2 6.4 %collective-permute-start.30 = (bf16[8,128,128]{2,1,0:T(8,128)(2,1)S(1)}, bf16[8,128,128]{2,1,0:T(8,128)(2,1)S(1)}, u32[]{:S(2)}, u32[]{:S(2)}) collective-permute-start(bf16[8,128,128]{2,1,0:T(8,128)(2,1)S(1)} %collective-permute-done.22.refs_8_), channel_id=1, source_target_pairs={{0,4},{4,0},{8,12},{12,8},{16,20},{20,16},{24,28},{28,24},{1,5},{5... | collective-permute-start | bytes 786440 | tf_op jit(solution)/shard_map/ppermute | solution.py:360
  92.4 8.6 %collective-permute-start.31 = (bf16[8,128,128]{2,1,0:T(8,128)(2,1)S(1)}, bf16[8,128,128]{2,1,0:T(8,128)(2,1)S(1)}, u32[]{:S(2)}, u32[]{:S(2)}) collective-permute-start(bf16[8,128,128]{2,1,0:T(8,128)(2,1)S(1)} %collective-permute-done.27.refs_7_), channel_id=1, source_target_pairs={{0,8},{4,12},{8,0},{12,4},{16,24},{20,28},{24,16},{28,20},{1,9},{5... | collective-permute-start | bytes 786440 | tf_op jit(solution)/shard_map/ppermute | solution.py:360
  101.0 5.1 %collective-permute-start.32 = (bf16[4,32,512]{2,1,0:T(8,128)(2,1)S(1)}, bf16[4,32,512]{2,1,0:T(8,128)(2,1)S(1)}, u32[]{:S(2)}, u32[]{:S(2)}) collective-permute-start(bf16[4,32,512]{2,1,0:T(8,128)(2,1)S(1)} %add_convert_fusion.3.mine_ref), channel_id=1, source_target_pairs={{0,4},{4,0},{8,12},{12,8},{16,20},{20,16},{24,28},{28,24},{1,5},{5... | collective-permute-start | bytes 393224 | tf_op jit(solution)/shard_map/ppermute | solution.py:360

commit v12 on v11

--- a/solution.py
+++ b/solution.py
@@ -486,8 +486,9 @@
         [pltpu.VMEM((parts_total, piece, full), F32)],
     )
     total = (keep + crossed(give, near).astype(F32)).astype(BF16)
+    total = tied(total, found[6])
     total = (total.astype(F32) + crossed(total, 2).astype(F32)).astype(BF16)
-    total = tied(total, found[5], found[6])
+    total = tied(total, found[5])
     total = (total.astype(F32) + crossed(total, 4).astype(F32)).astype(BF16)
     grad_x = dx_self.reshape(shape)
     half = parts_total // 2

time: 107 us -> 109 us (1.019)
  no operation moved by 1% of the time
where the time goes in v12:
time: 109 us; the launch traced here: 108 us
  waiting for transfers between devices  48.2 us (44%)
  starting transfers between devices  37.3 us (34%)
  Pallas kernels  17.2 us (16%)
  other arithmetic  4.15 us (4%)
    ppermute x33, waiting for transfers between devices, crossed(): lax.ppermute(x, axis, [(i, i ^ mask) for i in range(lax.axis_size(axis))])  48.2 us
    ppermute x33, starting transfers between devices, crossed(): lax.ppermute(x, axis, [(i, i ^ mask) for i in range(lax.axis_size(axis))])  37.3 us
    pallas_call x4, Pallas kernels, tiles_call(): pl.pallas_call(functools.partial(tiles_kernel, masks, offsets, parts_tota...  13.3 us
    pallas_call x5, Pallas kernels, small_call(): pl.pallas_call(kernel, out_shape=outs, in_specs=[VMEM] * len(arrays), out...  3.87 us
  transfers between devices with their start and end apart: 33, of which 20 were waited for; matrix products, arithmetic and copies ran while one was open for 4% of the time, Pallas kernels for 10%

profile of v12, /device:TPU:0, one launch (start us, length us, event | category | flops | bytes accessed | tf_op | source)
XLA Modules:
  0.0 108.4 jit_solution(12839364301908743622)
XLA Ops:
  0.6 3.7 %shard_map.139 = (bf16[8,128,128]{2,1,0:T(8,128)(2,1)}, bf16[8,128,128]{2,1,0:T(8,128)(2,1)}, bf16[8,128,128]{2,1,0:T(8,128)(2,1)}, bf16[8,128,128]{2,1,0:T(8,128)(2,1)}) custom-call(s32[1,16]{1,0:T(1,128)} %refs_0_.7, s32[1,16]{1,0:T(1,128)} %refs_1_.7, s32[6,1,8]{2,1,0:T(1,128)} %bitcast.30, s32[6,1,8]{2,1,0:T(1,128)} %bitcast.34, ...), custom_call_target="tpu_custom_call" | custom-call | flops 1 | bytes 1 | tf_op jit(solution)/shard_map/pallas_call | solution.py:224
  4.4 3.0 %collective-permute-start.2 = (bf16[8,128,128]{2,1,0:T(8,128)(2,1)}, bf16[8,128,128]{2,1,0:T(8,128)(2,1)S(1)}, u32[]{:S(2)}, u32[]{:S(2)}) collective-permute-start(bf16[8,128,128]{2,1,0:T(8,128)(2,1)} %get-tuple-element.81), channel_id=1, source_target_pairs={{0,4},{4,0},{8,12},{12,8},{16,20},{20,16},{24,28},{28,24},{1,5},{5... | collective-permute-start | bytes 786440 | tf_op jit(solution)/shard_map/ppermute | solution.py:360
  7.4 4.8 %shard_map.138 = (f32[8,128,128]{2,1,0:T(8,128)}, f32[8,128,128]{2,1,0:T(8,128)}, f32[8,128,128]{2,1,0:T(8,128)}, f32[8,128,128]{2,1,0:T(8,128)}, bf16[2,2,128,1...) custom-call(s32[1,16]{1,0:T(1,128)} %refs_0_.7, ...), custom_call_target="tpu_custom_call" | custom-call | flops 1 | bytes 1 | tf_op jit(solution)/shard_map/pallas_call | solution.py:224
  12.3 1.6 %collective-permute-start.1 = (bf16[2,128,512]{2,1,0:T(8,128)(2,1)}, bf16[2,128,512]{2,1,0:T(8,128)(2,1)S(1)}, u32[]{:S(2)}, u32[]{:S(2)}) collective-permute-start(bf16[2,128,512]{2,1,0:T(8,128)(2,1)} %get-tuple-element.96.refs_0_), channel_id=1, source_target_pairs={{0,2},{1,3},{2,0},{3,1},{4,6},{5,7},{6,4},{7,5},{8,10},{9,11},{10,... | collective-permute-start | bytes 786440 | tf_op jit(solution)/shard_map/ppermute | solution.py:360
  13.8 0.5 collective-permute-start
  14.3 1.1 %add_convert_fusion.2 = bf16[8,128,128]{2,1,0:T(8,128)(2,1)S(1)} fusion(f32[8,128,128]{2,1,0:T(8,128)} %get-tuple-element.80, bf16[8,128,128]{2,1,0:T(8,128)(2,1)S(1)} %collective-permute-done.2), kind=kLoop, calls=%fused_computation.3 | loop fusion | flops 393216 | bytes 1048576 | tf_op jit(solution)/shard_map/convert_element_type | solution.py:429
  15.5 1.6 %collective-permute-start.3 = (bf16[8,128,128]{2,1,0:T(8,128)(2,1)S(1)}, bf16[8,128,128]{2,1,0:T(8,128)(2,1)S(1)}, u32[]{:S(2)}, u32[]{:S(2)}) collective-permute-start(bf16[8,128,128]{2,1,0:T(8,128)(2,1)S(1)} %add_convert_fusion.2), channel_id=1, source_target_pairs={{0,8},{4,12},{8,0},{12,4},{16,24},{20,28},{24,16},{28,20},{1,9},{5... | collective-permute-start | bytes 786440 | tf_op jit(solution)/shard_map/ppermute | solution.py:360
  17.1 1.5 %collective-permute-start.4 = (bf16[8,128,128]{2,1,0:T(8,128)(2,1)S(1)}, bf16[8,128,128]{2,1,0:T(8,128)(2,1)S(1)}, u32[]{:S(2)}, u32[]{:S(2)}) collective-permute-start(bf16[8,128,128]{2,1,0:T(8,128)(2,1)S(1)} %copy-done.13), channel_id=1, source_target_pairs={{0,4},{4,0},{8,12},{12,8},{16,20},{20,16},{24,28},{28,24},{1,5},{5... | collective-permute-start | bytes 786440 | tf_op jit(solution)/shard_map/ppermute | solution.py:360
  18.6 1.7 %collective-permute-done.1.refs_2_ = bf16[2,128,512]{2,1,0:T(8,128)(2,1)S(1)} collective-permute-done((bf16[2,128,512]{2,1,0:T(8,128)(2,1)}, bf16[2,128,512]{2,1,0:T(8,128)(2,1)S(1)}, u32[]{:S(2)}, u32[]{:S(2)}) %collective-permute-start.1) | collective-permute-done | bytes 262176 | tf_op jit(solution)/shard_map/ppermute | solution.py:360
  20.3 2.8 %collective-permute-done = bf16[8,128,128]{2,1,0:T(8,128)(2,1)S(1)} collective-permute-done((bf16[8,128,128]{2,1,0:T(8,128)(2,1)S(1)}, bf16[8,128,128]{2,1,0:T(8,128)(2,1)S(1)}, u32[]{:S(2)}, u32[]{:S(2)}) %collective-permute-start) | collective-permute-done | bytes 262176 | tf_op jit(solution)/shard_map/ppermute | solution.py:360
  23.1 1.1 %add_convert_fusion.1 = bf16[8,128,128]{2,1,0:T(8,128)(2,1)S(1)} fusion(bf16[8,128,128]{2,1,0:T(8,128)(2,1)S(1)} %collective-permute-done.3, f32[8,128,128]{2,1,0:T(8,128)} %get-tuple-element.76, bf16[8,128,128]{2,1,0:T(8,128)(2,1)S(1)} %collective-permute-done), kind=kLoop, calls=%fused_computation.2 | loop fusion | flops 655360 | bytes 1310720 | tf_op jit(solution)/shard_map/convert_element_type | solution.py:431
  24.2 2.6 %collective-permute-start.7 = (bf16[8,128,128]{2,1,0:T(8,128)(2,1)S(1)}, bf16[8,128,128]{2,1,0:T(8,128)(2,1)S(1)}, u32[]{:S(2)}, u32[]{:S(2)}) collective-permute-start(bf16[8,128,128]{2,1,0:T(8,128)(2,1)S(1)} %add_convert_fusion.1), channel_id=1, source_target_pairs={{0,16},{4,20},{8,24},{12,28},{16,0},{20,4},{24,8},{28,12},{1,17},{... | collective-permute-start | bytes 786440 | tf_op jit(solution)/shard_map/ppermute | solution.py:360
  26.9 0.8 add_convert_fusion
  27.7 1.6 %collective-permute-start.5 = (bf16[8,128,128]{2,1,0:T(8,128)(2,1)}, bf16[8,128,128]{2,1,0:T(8,128)(2,1)S(1)}, u32[]{:S(2)}, u32[]{:S(2)}) collective-permute-start(bf16[8,128,128]{2,1,0:T(8,128)(2,1)} %add_convert_fusion), channel_id=1, source_target_pairs={{0,8},{4,12},{8,0},{12,4},{16,24},{20,28},{24,16},{28,20},{1,9},{5... | collective-permute-start | bytes 786440 | tf_op jit(solution)/shard_map/ppermute | solution.py:360
  29.3 1.1 %collective-permute-start.6 = (bf16[8,128,128]{2,1,0:T(8,128)(2,1)}, bf16[8,128,128]{2,1,0:T(8,128)(2,1)}, u32[]{:S(2)}, u32[]{:S(2)}) collective-permute-start(bf16[8,128,128]{2,1,0:T(8,128)(2,1)} %get-tuple-element.84), channel_id=1, source_target_pairs={{0,4},{4,0},{8,12},{12,8},{16,20},{20,16},{24,28},{28,24},{1,5},{5... | collective-permute-start | bytes 786440 | tf_op jit(solution)/shard_map/ppermute | solution.py:360
  30.4 1.3 %collective-permute-start.8 = (bf16[2,2,128,128]{3,2,1,0:T(8,128)(2,1)}, bf16[2,2,128,128]{3,2,1,0:T(8,128)(2,1)S(1)}, u32[]{:S(2)}, u32[]{:S(2)}) collective-permute-start(bf16[2,2,128,128]{3,2,1,0:T(8,128)(2,1)} %get-tuple-element.86), channel_id=1, source_target_pairs={{0,2},{1,3},{2,0},{3,1},{4,6},{5,7},{6,4},{7,5},{8,10},{9,11},{10,... | collective-permute-start | bytes 393224 | tf_op jit(solution)/shard_map/ppermute | solution.py:360
  31.7 0.2 copy.15.inv_ref
  32.0 4.4 %collective-permute-done.8.refs_6_ = bf16[2,2,128,128]{3,2,1,0:T(8,128)(2,1)S(1)} collective-permute-done((bf16[2,2,128,128]{3,2,1,0:T(8,128)(2,1)}, bf16[2,2,128,128]{3,2,1,0:T(8,128)(2,1)S(1)}, u32[]{:S(2)}, u32[]{:S(2)}) %collective-permute-start.8) | collective-permute-done | bytes 131104 | tf_op jit(solution)/shard_map/ppermute | solution.py:360
  36.3 1.3 %collective-permute-done.9.refs_7_ = bf16[2,2,128,128]{3,2,1,0:T(8,128)(2,1)S(1)} collective-permute-done((bf16[2,2,128,128]{3,2,1,0:T(8,128)(2,1)}, bf16[2,2,128,128]{3,2,1,0:T(8,128)(2,1)S(1)}, u32[]{:S(2)}, u32[]{:S(2)}) %collective-permute-start.9) | collective-permute-done | bytes 131104 | tf_op jit(solution)/shard_map/ppermute | solution.py:360
  37.7 0.9 collective-permute-start.12
  38.6 0.4 collective-permute-done.5
  39.0 1.0 convert_add_fusion.keep_ref
  40.0 0.2 shard_map.140
  40.3 0.3 collective-permute-start.13
  40.6 1.1 %collective-permute-start.14 = (bf16[2,128,128]{2,1,0:T(8,128)(2,1)S(1)}, bf16[2,128,128]{2,1,0:T(8,128)(2,1)S(1)}, u32[]{:S(2)}, u32[]{:S(2)}) collective-permute-start(bf16[2,128,128]{2,1,0:T(8,128)(2,1)S(1)} %get-tuple-element.106), channel_id=1, source_target_pairs={{0,2},{1,3},{2,0},{3,1},{4,6},{5,7},{6,4},{7,5},{8,10},{9,11},{10,... | collective-permute-start | bytes 196616 | tf_op jit(solution)/shard_map/ppermute | solution.py:360
  41.7 0.5 collective-permute-start.15
  42.2 0.1 dynamic_slice.3
  42.3 0.1 copy.16.inv_ref
  42.4 2.6 %collective-permute-done.14.refs_10_ = bf16[2,128,128]{2,1,0:T(8,128)(2,1)S(1)} collective-permute-done((bf16[2,128,128]{2,1,0:T(8,128)(2,1)S(1)}, bf16[2,128,128]{2,1,0:T(8,128)(2,1)S(1)}, u32[]{:S(2)}, u32[]{:S(2)}) %collective-permute-start.14) | collective-permute-done | bytes 65568 | tf_op jit(solution)/shard_map/ppermute | solution.py:360
  45.1 0.9 collective-permute-done.15.refs_11_
  46.0 1.3 %shard_map.141 = (bf16[5,256,128]{2,1,0:T(8,128)(2,1)S(1)}, bf16[5,256,128]{2,1,0:T(8,128)(2,1)S(1)}, bf16[5,256,128]{2,1,0:T(8,128)(2,1)S(1)}, bf16[256,128]{1,...) custom-call(f32[256,1]{1,0:T(8,128)S(1)} %copy.16.inv_ref, ...), custom_call_target="tpu_custom_call" | custom-call | flops 1 | bytes 1 | tf_op jit(solution)/shard_map/pallas_call | solution.py:244
  47.3 0.2 collective-permute-start.16
  47.5 1.1 collective-permute-start.17
  48.5 0.7 collective-permute-start.18
  49.2 3.1 %collective-permute-done.17 = bf16[256,128]{1,0:T(8,128)(2,1)S(1)} collective-permute-done((bf16[256,128]{1,0:T(8,128)(2,1)S(1)}, bf16[256,128]{1,0:T(8,128)(2,1)S(1)}, u32[]{:S(2)}, u32[]{:S(2)}) %collective-permute-start.17) | collective-permute-done | bytes 65568 | tf_op jit(solution)/shard_map/ppermute | solution.py:360
  52.3 0.5 collective-permute-done.18
  52.9 1.1 collective-permute-start.20
  53.9 0.6 collective-permute-start.21
  54.5 2.3 %collective-permute-start.19 = (bf16[8,128,128]{2,1,0:T(8,128)(2,1)S(1)}, bf16[8,128,128]{2,1,0:T(8,128)(2,1)S(1)}, u32[]{:S(2)}, u32[]{:S(2)}) collective-permute-start(bf16[8,128,128]{2,1,0:T(8,128)(2,1)S(1)} %bitcast.24), channel_id=1, source_target_pairs={{0,16},{4,20},{8,24},{12,28},{16,0},{20,4},{24,8},{28,12},{1,17},{... | collective-permute-start | bytes 786440 | tf_op jit(solution)/shard_map/ppermute | solution.py:360
  56.8 2.4 %collective-permute-start.22 = (bf16[8,128,128]{2,1,0:T(8,128)(2,1)S(1)}, bf16[8,128,128]{2,1,0:T(8,128)(2,1)S(1)}, u32[]{:S(2)}, u32[]{:S(2)}) collective-permute-start(bf16[8,128,128]{2,1,0:T(8,128)(2,1)S(1)} %bitcast.25), channel_id=1, source_target_pairs={{0,8},{4,12},{8,0},{12,4},{16,24},{20,28},{24,16},{28,20},{1,9},{5... | collective-permute-start | bytes 786440 | tf_op jit(solution)/shard_map/ppermute | solution.py:360
  59.2 1.2 %collective-permute-start.23 = (bf16[8,128,128]{2,1,0:T(8,128)(2,1)S(1)}, bf16[8,128,128]{2,1,0:T(8,128)(2,1)S(1)}, u32[]{:S(2)}, u32[]{:S(2)}) collective-permute-start(bf16[8,128,128]{2,1,0:T(8,128)(2,1)S(1)} %bitcast.26), channel_id=1, source_target_pairs={{0,4},{4,0},{8,12},{12,8},{16,20},{20,16},{24,28},{28,24},{1,5},{5... | collective-permute-start | bytes 786440 | tf_op jit(solution)/shard_map/ppermute | solution.py:360
  60.4 9.5 %collective-permute-done.19.refs_6_ = bf16[8,128,128]{2,1,0:T(8,128)(2,1)S(1)} collective-permute-done((bf16[8,128,128]{2,1,0:T(8,128)(2,1)S(1)}, bf16[8,128,128]{2,1,0:T(8,128)(2,1)S(1)}, u32[]{:S(2)}, u32[]{:S(2)}) %collective-permute-start.19) | collective-permute-done | bytes 262176 | tf_op jit(solution)/shard_map/ppermute | solution.py:360
  70.0 0.1 collective-permute-start.24
  70.1 1.6 %collective-permute-done.24.refs_1_ = bf16[5,256,128]{2,1,0:T(8,128)(2,1)S(1)} collective-permute-done((bf16[5,256,128]{2,1,0:T(8,128)(2,1)S(1)}, bf16[5,256,128]{2,1,0:T(8,128)(2,1)S(1)}, u32[]{:S(2)}, u32[]{:S(2)}) %collective-permute-start.24) | collective-permute-done | bytes 327712 | tf_op jit(solution)/shard_map/ppermute | solution.py:360
  71.7 0.8 shard_map.142
  72.6 1.0 collective-permute-start.25
  73.6 1.6 %collective-permute-start.26 = (bf16[8,128,128]{2,1,0:T(8,128)(2,1)S(1)}, bf16[8,128,128]{2,1,0:T(8,128)(2,1)S(1)}, u32[]{:S(2)}, u32[]{:S(2)}) collective-permute-start(bf16[8,128,128]{2,1,0:T(8,128)(2,1)S(1)} %collective-permute-done.19.refs_6_), channel_id=1, source_target_pairs={{0,8},{4,12},{8,0},{12,4},{16,24},{20,28},{24,16},{28,20},{1,9},{5... | collective-permute-start | bytes 786440 | tf_op jit(solution)/shard_map/ppermute | solution.py:360
  75.2 2.9 %collective-permute-done.25 = bf16[4,32,512]{2,1,0:T(8,128)(2,1)S(1)} collective-permute-done((bf16[4,32,512]{2,1,0:T(8,128)(2,1)S(1)}, bf16[4,32,512]{2,1,0:T(8,128)(2,1)S(1)}, u32[]{:S(2)}, u32[]{:S(2)}) %collective-permute-start.25) | collective-permute-done | bytes 131104 | tf_op jit(solution)/shard_map/ppermute | solution.py:360
  78.2 3.5 %collective-permute-done.26.refs_8_ = bf16[8,128,128]{2,1,0:T(8,128)(2,1)S(1)} collective-permute-done((bf16[8,128,128]{2,1,0:T(8,128)(2,1)S(1)}, bf16[8,128,128]{2,1,0:T(8,128)(2,1)S(1)}, u32[]{:S(2)}, u32[]{:S(2)}) %collective-permute-start.26) | collective-permute-done | bytes 262176 | tf_op jit(solution)/shard_map/ppermute | solution.py:360
  81.7 1.6 %collective-permute-start.27 = (bf16[4,32,512]{2,1,0:T(8,128)(2,1)S(1)}, bf16[4,32,512]{2,1,0:T(8,128)(2,1)S(1)}, u32[]{:S(2)}, u32[]{:S(2)}) collective-permute-start(bf16[4,32,512]{2,1,0:T(8,128)(2,1)S(1)} %add_convert_fusion.5), channel_id=1, source_target_pairs={{0,8},{4,12},{8,0},{12,4},{16,24},{20,28},{24,16},{28,20},{1,9},{5... | collective-permute-start | bytes 393224 | tf_op jit(solution)/shard_map/ppermute | solution.py:360
  83.3 0.7 collective-permute-start.28
  84.0 2.7 %collective-permute-done.27 = bf16[4,32,512]{2,1,0:T(8,128)(2,1)S(1)} collective-permute-done((bf16[4,32,512]{2,1,0:T(8,128)(2,1)S(1)}, bf16[4,32,512]{2,1,0:T(8,128)(2,1)S(1)}, u32[]{:S(2)}, u32[]{:S(2)}) %collective-permute-start.27) | collective-permute-done | bytes 131104 | tf_op jit(solution)/shard_map/ppermute | solution.py:360
  86.7 3.5 %collective-permute-done.28.refs_7_ = bf16[8,128,128]{2,1,0:T(8,128)(2,1)S(1)} collective-permute-done((bf16[8,128,128]{2,1,0:T(8,128)(2,1)S(1)}, bf16[8,128,128]{2,1,0:T(8,128)(2,1)S(1)}, u32[]{:S(2)}, u32[]{:S(2)}) %collective-permute-start.28) | collective-permute-done | bytes 262176 | tf_op jit(solution)/shard_map/ppermute | solution.py:360
  90.2 3.0 %collective-permute-start.29 = (bf16[4,32,512]{2,1,0:T(8,128)(2,1)S(1)}, bf16[4,32,512]{2,1,0:T(8,128)(2,1)S(1)}, u32[]{:S(2)}, u32[]{:S(2)}) collective-permute-start(bf16[4,32,512]{2,1,0:T(8,128)(2,1)S(1)} %add_convert_fusion.4), channel_id=1, source_target_pairs={{0,16},{4,20},{8,24},{12,28},{16,0},{20,4},{24,8},{28,12},{1,17},{... | collective-permute-start | bytes 393224 | tf_op jit(solution)/shard_map/ppermute | solution.py:360
  93.2 0.8 collective-permute-start.30
  94.0 0.6 collective-permute-start.31
  94.5 0.7 shard_map.143
  95.3 2.4 %collective-permute-done.29 = bf16[4,32,512]{2,1,0:T(8,128)(2,1)S(1)} collective-permute-done((bf16[4,32,512]{2,1,0:T(8,128)(2,1)S(1)}, bf16[4,32,512]{2,1,0:T(8,128)(2,1)S(1)}, u32[]{:S(2)}, u32[]{:S(2)}) %collective-permute-start.29) | collective-permute-done | bytes 131104 | tf_op jit(solution)/shard_map/ppermute | solution.py:360
  97.7 1.8 %collective-permute-done.30.refs_9_ = bf16[8,128,128]{2,1,0:T(8,128)(2,1)S(1)} collective-permute-done((bf16[8,128,128]{2,1,0:T(8,128)(2,1)S(1)}, bf16[8,128,128]{2,1,0:T(8,128)(2,1)S(1)}, u32[]{:S(2)}, u32[]{:S(2)}) %collective-permute-start.30) | collective-permute-done | bytes 262176 | tf_op jit(solution)/shard_map/ppermute | solution.py:360
  99.5 2.3 %collective-permute-done.31.refs_9_ = bf16[8,128,128]{2,1,0:T(8,128)(2,1)S(1)} collective-permute-done((bf16[8,128,128]{2,1,0:T(8,128)(2,1)S(1)}, bf16[8,128,128]{2,1,0:T(8,128)(2,1)S(1)}, u32[]{:S(2)}, u32[]{:S(2)}) %collective-permute-start.31) | collective-permute-done | bytes 262176 | tf_op jit(solution)/shard_map/ppermute | solution.py:360
  101.9 0.8 collective-permute-start.32
  102.7 2.1 %shard_map.144.refs_10_ = f32[8,128,128]{2,1,0:T(8,128)S(1)} custom-call(s32[1,16]{1,0:T(1,128)S(1)} %copy-done.8, s32[1,16]{1,0:T(1,128)S(1)} %copy-done.9, s32[6,1,8]{2,1,0:T(1,128)S(1)} %bitcast.32, s32[6,1,8]{2,1,0:T(1,128)S(1)} %bitcast.36, bf16[16,128,128]{2,1,0:T(8,128)(2,1)S(1)} %bitcast.20, bf16[6,8,128,128]{3,2,1,0:T(8,128)(2,1)S(1)} %bitcast.16, ...), custom_call_target="tpu_custom_call" | custom-call | flops 1 | bytes 1 | tf_op jit(solution)/shard_map/pallas_call | solution.py:224
  104.9 2.6 %shard_map.145 = f32[8,128,128]{2,1,0:T(8,128)} custom-call(s32[1,16]{1,0:T(1,128)S(1)} %copy-done.8, s32[1,16]{1,0:T(1,128)S(1)} %copy-done.9, s32[6,1,8]{2,1,0:T(1,128)S(1)} %bitcast.33, s32[6,1,8]{2,1,0:T(1,128)S(1)} %bitcast.37, bf16[16,128,128]{2,1,0:T(8,128)(2,1)S(1)} %bitcast.21, bf16[6,8,128,128]{3,2,1,0:T(8,128)(2,1)S(1)} %bitcast.17, ...), custom_call_target="tpu_custom_call" | custom-call | flops 1 | bytes 1 | tf_op jit(solution)/shard_map/pallas_call | solution.py:224
  107.5 0.9 shard_map.146
  (55 shorter events, 0.4 us)
Async XLA Ops:
  4.4 9.5 %copy-start.14 = (bf16[8,128,128]{2,1,0:T(8,128)(2,1)S(1)}, bf16[8,128,128]{2,1,0:T(8,128)(2,1)}, u32[]{:S(2)}) copy-start(bf16[8,128,128]{2,1,0:T(8,128)(2,1)} %get-tuple-element.77) | copy-start | bytes 786436
  4.4 9.9 %collective-permute-start.2 = (bf16[8,128,128]{2,1,0:T(8,128)(2,1)}, bf16[8,128,128]{2,1,0:T(8,128)(2,1)S(1)}, u32[]{:S(2)}, u32[]{:S(2)}) collective-permute-start(bf16[8,128,128]{2,1,0:T(8,128)(2,1)} %get-tuple-element.81), channel_id=1, source_target_pairs={{0,4},{4,0},{8,12},{12,8},{16,20},{20,16},{24,28},{28,24},{1,5},{5... | collective-permute-start | bytes 786440 | tf_op jit(solution)/shard_map/ppermute | solution.py:360
  7.4 9.7 %copy-start.13 = (bf16[8,128,128]{2,1,0:T(8,128)(2,1)S(1)}, bf16[8,128,128]{2,1,0:T(8,128)(2,1)}, u32[]{:S(2)}) copy-start(bf16[8,128,128]{2,1,0:T(8,128)(2,1)} %get-tuple-element.83) | copy-start | bytes 786436
  12.3 14.7 %copy-start.11 = (f32[8,128,128]{2,1,0:T(8,128)S(1)}, f32[8,128,128]{2,1,0:T(8,128)}, u32[]{:S(2)}) copy-start(f32[8,128,128]{2,1,0:T(8,128)} %get-tuple-element.82) | copy-start | bytes 1572868
  12.3 8.0 %collective-permute-start.1 = (bf16[2,128,512]{2,1,0:T(8,128)(2,1)}, bf16[2,128,512]{2,1,0:T(8,128)(2,1)S(1)}, u32[]{:S(2)}, u32[]{:S(2)}) collective-permute-start(bf16[2,128,512]{2,1,0:T(8,128)(2,1)} %get-tuple-element.96.refs_0_), channel_id=1, source_target_pairs={{0,2},{1,3},{2,0},{3,1},{4,6},{5,7},{6,4},{7,5},{8,10},{9,11},{10,... | collective-permute-start | bytes 786440 | tf_op jit(solution)/shard_map/ppermute | solution.py:360
  13.8 9.2 %collective-permute-start = (bf16[8,128,128]{2,1,0:T(8,128)(2,1)S(1)}, bf16[8,128,128]{2,1,0:T(8,128)(2,1)S(1)}, u32[]{:S(2)}, u32[]{:S(2)}) collective-permute-start(bf16[8,128,128]{2,1,0:T(8,128)(2,1)S(1)} %copy-done.14), channel_id=1, source_target_pairs={{0,4},{4,0},{8,12},{12,8},{16,20},{20,16},{24,28},{28,24},{1,5},{5... | collective-permute-start | bytes 786440 | tf_op jit(solution)/shard_map/ppermute | solution.py:360
  14.3 17.4 %copy-start.12 = (s32[1024]{0:T(1024)S(1)}, s32[1024]{0:T(1024)}, u32[]{:S(2)}) copy-start(s32[1024]{0:T(1024)} %param.14) | copy-start | bytes 12292
  15.5 20.9 %copy-start.4 = (bf16[2,128,512]{2,1,0:T(8,128)(2,1)S(1)}, bf16[2,128,512]{2,1,0:T(8,128)(2,1)}, u32[]{:S(2)}) copy-start(bf16[2,128,512]{2,1,0:T(8,128)(2,1)} %get-tuple-element.96.refs_0_) | copy-start | bytes 786436
  15.5 23.1 %copy-start.15 = (bf16[2,2,128,128]{3,2,1,0:T(8,128)(2,1)S(1)}, bf16[2,2,128,128]{3,2,1,0:T(8,128)(2,1)}, u32[]{:S(2)}) copy-start(bf16[2,2,128,128]{3,2,1,0:T(8,128)(2,1)} %get-tuple-element.89) | copy-start | bytes 393220
  15.5 23.5 %copy-start.10 = (f32[8,128,128]{2,1,0:T(8,128)S(1)}, f32[8,128,128]{2,1,0:T(8,128)}, u32[]{:S(2)}) copy-start(f32[8,128,128]{2,1,0:T(8,128)} %get-tuple-element.69) | copy-start | bytes 1572868
  15.5 7.6 %collective-permute-start.3 = (bf16[8,128,128]{2,1,0:T(8,128)(2,1)S(1)}, bf16[8,128,128]{2,1,0:T(8,128)(2,1)S(1)}, u32[]{:S(2)}, u32[]{:S(2)}) collective-permute-start(bf16[8,128,128]{2,1,0:T(8,128)(2,1)S(1)} %add_convert_fusion.2), channel_id=1, source_target_pairs={{0,8},{4,12},{8,0},{12,4},{16,24},{20,28},{24,16},{28,20},{1,9},{5... | collective-permute-start | bytes 786440 | tf_op jit(solution)/shard_map/ppermute | solution.py:360
  17.1 9.8 %collective-permute-start.4 = (bf16[8,128,128]{2,1,0:T(8,128)(2,1)S(1)}, bf16[8,128,128]{2,1,0:T(8,128)(2,1)S(1)}, u32[]{:S(2)}, u32[]{:S(2)}) collective-permute-start(bf16[8,128,128]{2,1,0:T(8,128)(2,1)S(1)} %copy-done.13), channel_id=1, source_target_pairs={{0,4},{4,0},{8,12},{12,8},{16,20},{20,16},{24,28},{28,24},{1,5},{5... | collective-permute-start | bytes 786440 | tf_op jit(solution)/shard_map/ppermute | solution.py:360
  24.2 14.3 %collective-permute-start.7 = (bf16[8,128,128]{2,1,0:T(8,128)(2,1)S(1)}, bf16[8,128,128]{2,1,0:T(8,128)(2,1)S(1)}, u32[]{:S(2)}, u32[]{:S(2)}) collective-permute-start(bf16[8,128,128]{2,1,0:T(8,128)(2,1)S(1)} %add_convert_fusion.1), channel_id=1, source_target_pairs={{0,16},{4,20},{8,24},{12,28},{16,0},{20,4},{24,8},{28,12},{1,17},{... | collective-permute-start | bytes 786440 | tf_op jit(solution)/shard_map/ppermute | solution.py:360
  27.7 11.3 %collective-permute-start.5 = (bf16[8,128,128]{2,1,0:T(8,128)(2,1)}, bf16[8,128,128]{2,1,0:T(8,128)(2,1)S(1)}, u32[]{:S(2)}, u32[]{:S(2)}) collective-permute-start(bf16[8,128,128]{2,1,0:T(8,128)(2,1)} %add_convert_fusion), channel_id=1, source_target_pairs={{0,8},{4,12},{8,0},{12,4},{16,24},{20,28},{24,16},{28,20},{1,9},{5... | collective-permute-start | bytes 786440 | tf_op jit(solution)/shard_map/ppermute | solution.py:360
  29.3 9.7 %collective-permute-start.6 = (bf16[8,128,128]{2,1,0:T(8,128)(2,1)}, bf16[8,128,128]{2,1,0:T(8,128)(2,1)}, u32[]{:S(2)}, u32[]{:S(2)}) collective-permute-start(bf16[8,128,128]{2,1,0:T(8,128)(2,1)} %get-tuple-element.84), channel_id=1, source_target_pairs={{0,4},{4,0},{8,12},{12,8},{16,20},{20,16},{24,28},{28,24},{1,5},{5... | collective-permute-start | bytes 786440 | tf_op jit(solution)/shard_map/ppermute | solution.py:360
  30.4 5.9 %collective-permute-start.8 = (bf16[2,2,128,128]{3,2,1,0:T(8,128)(2,1)}, bf16[2,2,128,128]{3,2,1,0:T(8,128)(2,1)S(1)}, u32[]{:S(2)}, u32[]{:S(2)}) collective-permute-start(bf16[2,2,128,128]{3,2,1,0:T(8,128)(2,1)} %get-tuple-element.86), channel_id=1, source_target_pairs={{0,2},{1,3},{2,0},{3,1},{4,6},{5,7},{6,4},{7,5},{8,10},{9,11},{10,... | collective-permute-start | bytes 393224 | tf_op jit(solution)/shard_map/ppermute | solution.py:360
  31.7 6.0 %collective-permute-start.9 = (bf16[2,2,128,128]{3,2,1,0:T(8,128)(2,1)}, bf16[2,2,128,128]{3,2,1,0:T(8,128)(2,1)S(1)}, u32[]{:S(2)}, u32[]{:S(2)}) collective-permute-start(bf16[2,2,128,128]{3,2,1,0:T(8,128)(2,1)} %get-tuple-element.87), channel_id=1, source_target_pairs={{0,3},{1,2},{2,1},{3,0},{4,7},{5,6},{6,5},{7,4},{8,11},{9,10},{10,... | collective-permute-start | bytes 393224 | tf_op jit(solution)/shard_map/ppermute | solution.py:360
  32.0 14.1 %copy-start.5 = (bf16[2,2,128,128]{3,2,1,0:T(8,128)(2,1)S(1)}, bf16[2,2,128,128]{3,2,1,0:T(8,128)(2,1)}, u32[]{:S(2)}) copy-start(bf16[2,2,128,128]{3,2,1,0:T(8,128)(2,1)} %get-tuple-element.100.refs_4_) | copy-start | bytes 393220
  36.3 3.7 %collective-permute-start.11 = (bf16[2,128,512]{2,1,0:T(8,128)(2,1)S(1)}, bf16[2,128,512]{2,1,0:T(8,128)(2,1)S(1)}, u32[]{:S(2)}, u32[]{:S(2)}) collective-permute-start(bf16[2,128,512]{2,1,0:T(8,128)(2,1)S(1)} %copy-done.4), channel_id=1, source_target_pairs={{0,1},{1,0},{2,3},{3,2},{4,5},{5,4},{6,7},{7,6},{8,9},{9,8},{10,11... | collective-permute-start | bytes 786440 | tf_op jit(solution)/shard_map/ppermute | solution.py:360
  37.7 2.3 %collective-permute-start.12 = (bf16[2,128,512]{2,1,0:T(8,128)(2,1)S(1)}, bf16[2,128,512]{2,1,0:T(8,128)(2,1)S(1)}, u32[]{:S(2)}, u32[]{:S(2)}) collective-permute-start(bf16[2,128,512]{2,1,0:T(8,128)(2,1)S(1)} %collective-permute-done.1.refs_2_), channel_id=1, source_target_pairs={{0,1},{1,0},{2,3},{3,2},{4,5},{5,4},{6,7},{7,6},{8,9},{9,8},{10,11... | collective-permute-start | bytes 786440 | tf_op jit(solution)/shard_map/ppermute | solution.py:360
  38.5 1.5 %collective-permute-start.10 = (bf16[2,2,128,128]{3,2,1,0:T(8,128)(2,1)S(1)}, bf16[2,2,128,128]{3,2,1,0:T(8,128)(2,1)S(1)}, u32[]{:S(2)}, u32[]{:S(2)}) collective-permute-start(bf16[2,2,128,128]{3,2,1,0:T(8,128)(2,1)S(1)} %copy-done.15), channel_id=1, source_target_pairs={{0,1},{1,0},{2,3},{3,2},{4,5},{5,4},{6,7},{7,6},{8,9},{9,8},{10,11... | collective-permute-start | bytes 393224 | tf_op jit(solution)/shard_map/ppermute | solution.py:360
  40.3 31.4 %copy-start.2 = (bf16[1024,128]{1,0:T(8,128)(2,1)S(1)}, bf16[1024,128]{1,0:T(8,128)(2,1)}, u32[]{:S(2)}) copy-start(bf16[1024,128]{1,0:T(8,128)(2,1)} %f_ref.1) | copy-start | bytes 786436
  40.3 31.4 %copy-start.3 = (bf16[128,512]{1,0:T(8,128)(2,1)S(1)}, bf16[128,512]{1,0:T(8,128)(2,1)}, u32[]{:S(2)}) copy-start(bf16[128,512]{1,0:T(8,128)(2,1)} %w_ref.1) | copy-start | bytes 393220
  40.3 2.1 %collective-permute-start.13 = (bf16[2,128,128]{2,1,0:T(8,128)(2,1)S(1)}, bf16[2,128,128]{2,1,0:T(8,128)(2,1)S(1)}, u32[]{:S(2)}, u32[]{:S(2)}) collective-permute-start(bf16[2,128,128]{2,1,0:T(8,128)(2,1)S(1)} %get-tuple-element.105), channel_id=1, source_target_pairs={{0,1},{1,0},{2,3},{3,2},{4,5},{5,4},{6,7},{7,6},{8,9},{9,8},{10,11... | collective-permute-start | bytes 196616 | tf_op jit(solution)/shard_map/ppermute | solution.py:360
  40.6 4.5 %collective-permute-start.14 = (bf16[2,128,128]{2,1,0:T(8,128)(2,1)S(1)}, bf16[2,128,128]{2,1,0:T(8,128)(2,1)S(1)}, u32[]{:S(2)}, u32[]{:S(2)}) collective-permute-start(bf16[2,128,128]{2,1,0:T(8,128)(2,1)S(1)} %get-tuple-element.106), channel_id=1, source_target_pairs={{0,2},{1,3},{2,0},{3,1},{4,6},{5,7},{6,4},{7,5},{8,10},{9,11},{10,... | collective-permute-start | bytes 196616 | tf_op jit(solution)/shard_map/ppermute | solution.py:360
  41.7 4.3 %collective-permute-start.15 = (bf16[2,128,128]{2,1,0:T(8,128)(2,1)S(1)}, bf16[2,128,128]{2,1,0:T(8,128)(2,1)S(1)}, u32[]{:S(2)}, u32[]{:S(2)}) collective-permute-start(bf16[2,128,128]{2,1,0:T(8,128)(2,1)S(1)} %get-tuple-element.107), channel_id=1, source_target_pairs={{0,3},{1,2},{2,1},{3,0},{4,7},{5,6},{6,5},{7,4},{8,11},{9,10},{10,... | collective-permute-start | bytes 196616 | tf_op jit(solution)/shard_map/ppermute | solution.py:360
  47.3 1.9 %collective-permute-start.16 = (bf16[256,128]{1,0:T(8,128)(2,1)S(1)}, bf16[256,128]{1,0:T(8,128)(2,1)S(1)}, u32[]{:S(2)}, u32[]{:S(2)}) collective-permute-start(bf16[256,128]{1,0:T(8,128)(2,1)S(1)} %get-tuple-element.109), channel_id=1, source_target_pairs={{0,1},{1,0},{2,3},{3,2},{4,5},{5,4},{6,7},{7,6},{8,9},{9,8},{10,11... | collective-permute-start | bytes 196616 | tf_op jit(solution)/shard_map/ppermute | solution.py:360
  47.5 4.8 %collective-permute-start.17 = (bf16[256,128]{1,0:T(8,128)(2,1)S(1)}, bf16[256,128]{1,0:T(8,128)(2,1)S(1)}, u32[]{:S(2)}, u32[]{:S(2)}) collective-permute-start(bf16[256,128]{1,0:T(8,128)(2,1)S(1)} %get-tuple-element.110), channel_id=1, source_target_pairs={{0,2},{1,3},{2,0},{3,1},{4,6},{5,7},{6,4},{7,5},{8,10},{9,11},{10,... | collective-permute-start | bytes 196616 | tf_op jit(solution)/shard_map/ppermute | solution.py:360
  48.5 4.3 %collective-permute-start.18 = (bf16[256,128]{1,0:T(8,128)(2,1)S(1)}, bf16[256,128]{1,0:T(8,128)(2,1)S(1)}, u32[]{:S(2)}, u32[]{:S(2)}) collective-permute-start(bf16[256,128]{1,0:T(8,128)(2,1)S(1)} %get-tuple-element.111), channel_id=1, source_target_pairs={{0,3},{1,2},{2,1},{3,0},{4,7},{5,6},{6,5},{7,4},{8,11},{9,10},{10,... | collective-permute-start | bytes 196616 | tf_op jit(solution)/shard_map/ppermute | solution.py:360
  52.9 17.1 %collective-permute-start.20 = (bf16[5,256,128]{2,1,0:T(8,128)(2,1)S(1)}, bf16[5,256,128]{2,1,0:T(8,128)(2,1)S(1)}, u32[]{:S(2)}, u32[]{:S(2)}) collective-permute-start(bf16[5,256,128]{2,1,0:T(8,128)(2,1)S(1)} %get-tuple-element.115), channel_id=1, source_target_pairs={{0,2},{1,3},{2,0},{3,1},{4,6},{5,7},{6,4},{7,5},{8,10},{9,11},{10,... | collective-permute-start | bytes 983048 | tf_op jit(solution)/shard_map/ppermute | solution.py:360
  53.9 16.1 %collective-permute-start.21 = (bf16[5,256,128]{2,1,0:T(8,128)(2,1)S(1)}, bf16[5,256,128]{2,1,0:T(8,128)(2,1)S(1)}, u32[]{:S(2)}, u32[]{:S(2)}) collective-permute-start(bf16[5,256,128]{2,1,0:T(8,128)(2,1)S(1)} %get-tuple-element.116), channel_id=1, source_target_pairs={{0,3},{1,2},{2,1},{3,0},{4,7},{5,6},{6,5},{7,4},{8,11},{9,10},{10,... | collective-permute-start | bytes 983048 | tf_op jit(solution)/shard_map/ppermute | solution.py:360
  54.5 15.4 %collective-permute-start.19 = (bf16[8,128,128]{2,1,0:T(8,128)(2,1)S(1)}, bf16[8,128,128]{2,1,0:T(8,128)(2,1)S(1)}, u32[]{:S(2)}, u32[]{:S(2)}) collective-permute-start(bf16[8,128,128]{2,1,0:T(8,128)(2,1)S(1)} %bitcast.24), channel_id=1, source_target_pairs={{0,16},{4,20},{8,24},{12,28},{16,0},{20,4},{24,8},{28,12},{1,17},{... | collective-permute-start | bytes 786440 | tf_op jit(solution)/shard_map/ppermute | solution.py:360
  56.8 13.2 %collective-permute-start.22 = (bf16[8,128,128]{2,1,0:T(8,128)(2,1)S(1)}, bf16[8,128,128]{2,1,0:T(8,128)(2,1)S(1)}, u32[]{:S(2)}, u32[]{:S(2)}) collective-permute-start(bf16[8,128,128]{2,1,0:T(8,128)(2,1)S(1)} %bitcast.25), channel_id=1, source_target_pairs={{0,8},{4,12},{8,0},{12,4},{16,24},{20,28},{24,16},{28,20},{1,9},{5... | collective-permute-start | bytes 786440 | tf_op jit(solution)/shard_map/ppermute | solution.py:360
  59.2 10.8 %collective-permute-start.23 = (bf16[8,128,128]{2,1,0:T(8,128)(2,1)S(1)}, bf16[8,128,128]{2,1,0:T(8,128)(2,1)S(1)}, u32[]{:S(2)}, u32[]{:S(2)}) collective-permute-start(bf16[8,128,128]{2,1,0:T(8,128)(2,1)S(1)} %bitcast.26), channel_id=1, source_target_pairs={{0,4},{4,0},{8,12},{12,8},{16,20},{20,16},{24,28},{28,24},{1,5},{5... | collective-permute-start | bytes 786440 | tf_op jit(solution)/shard_map/ppermute | solution.py:360
  70.0 1.7 %collective-permute-start.24 = (bf16[5,256,128]{2,1,0:T(8,128)(2,1)S(1)}, bf16[5,256,128]{2,1,0:T(8,128)(2,1)S(1)}, u32[]{:S(2)}, u32[]{:S(2)}) collective-permute-start(bf16[5,256,128]{2,1,0:T(8,128)(2,1)S(1)} %get-tuple-element.118.refs_0_), channel_id=1, source_target_pairs={{0,1},{1,0},{2,3},{3,2},{4,5},{5,4},{6,7},{7,6},{8,9},{9,8},{10,11... | collective-permute-start | bytes 983048 | tf_op jit(solution)/shard_map/ppermute | solution.py:360
  72.5 30.2 %copy-start = (bf16[1,6,8,128,128]{4,3,2,1,0:T(8,128)(2,1)S(1)}, bf16[1,6,8,128,128]{4,3,2,1,0:T(8,128)(2,1)}, u32[]{:S(2)}) copy-start(bf16[1,6,8,128,128]{4,3,2,1,0:T(8,128)(2,1)} %param.18) | copy-start | bytes 4718596
  72.5 30.2 %copy-start.1 = (bf16[1,16,128,128]{3,2,1,0:T(8,128)(2,1)S(1)}, bf16[1,16,128,128]{3,2,1,0:T(8,128)(2,1)}, u32[]{:S(2)}) copy-start(bf16[1,16,128,128]{3,2,1,0:T(8,128)(2,1)} %param.15) | copy-start | bytes 1572868
  72.5 30.2 %copy-start.6 = (s32[1,6,8]{2,0,1:T(1,128)S(1)}, s32[1,6,8]{2,0,1:T(1,128)}, u32[]{:S(2)}) copy-start(s32[1,6,8]{2,0,1:T(1,128)} %param.19) | copy-start | bytes 580
  72.5 30.2 %copy-start.7 = (s32[1,6,8]{2,0,1:T(1,128)S(1)}, s32[1,6,8]{2,0,1:T(1,128)}, u32[]{:S(2)}) copy-start(s32[1,6,8]{2,0,1:T(1,128)} %param.20) | copy-start | bytes 580
  72.5 30.2 %copy-start.8 = (s32[1,16]{1,0:T(1,128)S(1)}, s32[1,16]{1,0:T(1,128)}, u32[]{:S(2)}) copy-start(s32[1,16]{1,0:T(1,128)} %refs_0_.7) | copy-start | bytes 196
  72.5 30.2 %copy-start.9 = (s32[1,16]{1,0:T(1,128)S(1)}, s32[1,16]{1,0:T(1,128)}, u32[]{:S(2)}) copy-start(s32[1,16]{1,0:T(1,128)} %refs_1_.7) | copy-start | bytes 196
  72.6 5.6 %collective-permute-start.25 = (bf16[4,32,512]{2,1,0:T(8,128)(2,1)S(1)}, bf16[4,32,512]{2,1,0:T(8,128)(2,1)S(1)}, u32[]{:S(2)}, u32[]{:S(2)}) collective-permute-start(bf16[4,32,512]{2,1,0:T(8,128)(2,1)S(1)} %get-tuple-element.122), channel_id=1, source_target_pairs={{0,4},{4,0},{8,12},{12,8},{16,20},{20,16},{24,28},{28,24},{1,5},{5... | collective-permute-start | bytes 393224 | tf_op jit(solution)/shard_map/ppermute | solution.py:360
  73.6 8.1 %collective-permute-start.26 = (bf16[8,128,128]{2,1,0:T(8,128)(2,1)S(1)}, bf16[8,128,128]{2,1,0:T(8,128)(2,1)S(1)}, u32[]{:S(2)}, u32[]{:S(2)}) collective-permute-start(bf16[8,128,128]{2,1,0:T(8,128)(2,1)S(1)} %collective-permute-done.19.refs_6_), channel_id=1, source_target_pairs={{0,8},{4,12},{8,0},{12,4},{16,24},{20,28},{24,16},{28,20},{1,9},{5... | collective-permute-start | bytes 786440 | tf_op jit(solution)/shard_map/ppermute | solution.py:360
  81.7 5.0 %collective-permute-start.27 = (bf16[4,32,512]{2,1,0:T(8,128)(2,1)S(1)}, bf16[4,32,512]{2,1,0:T(8,128)(2,1)S(1)}, u32[]{:S(2)}, u32[]{:S(2)}) collective-permute-start(bf16[4,32,512]{2,1,0:T(8,128)(2,1)S(1)} %add_convert_fusion.5), channel_id=1, source_target_pairs={{0,8},{4,12},{8,0},{12,4},{16,24},{20,28},{24,16},{28,20},{1,9},{5... | collective-permute-start | bytes 393224 | tf_op jit(solution)/shard_map/ppermute | solution.py:360
  83.3 6.9 %collective-permute-start.28 = (bf16[8,128,128]{2,1,0:T(8,128)(2,1)S(1)}, bf16[8,128,128]{2,1,0:T(8,128)(2,1)S(1)}, u32[]{:S(2)}, u32[]{:S(2)}) collective-permute-start(bf16[8,128,128]{2,1,0:T(8,128)(2,1)S(1)} %collective-permute-done.19.refs_6_), channel_id=1, source_target_pairs={{0,4},{4,0},{8,12},{12,8},{16,20},{20,16},{24,28},{28,24},{1,5},{5... | collective-permute-start | bytes 786440 | tf_op jit(solution)/shard_map/ppermute | solution.py:360
  90.2 7.5 %collective-permute-start.29 = (bf16[4,32,512]{2,1,0:T(8,128)(2,1)S(1)}, bf16[4,32,512]{2,1,0:T(8,128)(2,1)S(1)}, u32[]{:S(2)}, u32[]{:S(2)}) collective-permute-start(bf16[4,32,512]{2,1,0:T(8,128)(2,1)S(1)} %add_convert_fusion.4), channel_id=1, source_target_pairs={{0,16},{4,20},{8,24},{12,28},{16,0},{20,4},{24,8},{28,12},{1,17},{... | collective-permute-start | bytes 393224 | tf_op jit(solution)/shard_map/ppermute | solution.py:360
  93.2 6.4 %collective-permute-start.30 = (bf16[8,128,128]{2,1,0:T(8,128)(2,1)S(1)}, bf16[8,128,128]{2,1,0:T(8,128)(2,1)S(1)}, u32[]{:S(2)}, u32[]{:S(2)}) collective-permute-start(bf16[8,128,128]{2,1,0:T(8,128)(2,1)S(1)} %collective-permute-done.22.refs_8_), channel_id=1, source_target_pairs={{0,4},{4,0},{8,12},{12,8},{16,20},{20,16},{24,28},{28,24},{1,5},{5... | collective-permute-start | bytes 786440 | tf_op jit(solution)/shard_map/ppermute | solution.py:360
  94.0 7.9 %collective-permute-start.31 = (bf16[8,128,128]{2,1,0:T(8,128)(2,1)S(1)}, bf16[8,128,128]{2,1,0:T(8,128)(2,1)S(1)}, u32[]{:S(2)}, u32[]{:S(2)}) collective-permute-start(bf16[8,128,128]{2,1,0:T(8,128)(2,1)S(1)} %collective-permute-done.28.refs_7_), channel_id=1, source_target_pairs={{0,8},{4,12},{8,0},{12,4},{16,24},{20,28},{24,16},{28,20},{1,9},{5... | collective-permute-start | bytes 786440 | tf_op jit(solution)/shard_map/ppermute | solution.py:360
  101.9 5.6 %collective-permute-start.32 = (bf16[4,32,512]{2,1,0:T(8,128)(2,1)S(1)}, bf16[4,32,512]{2,1,0:T(8,128)(2,1)S(1)}, u32[]{:S(2)}, u32[]{:S(2)}) collective-permute-start(bf16[4,32,512]{2,1,0:T(8,128)(2,1)S(1)} %add_convert_fusion.3.mine_ref), channel_id=1, source_target_pairs={{0,4},{4,0},{8,12},{12,8},{16,20},{20,16},{24,28},{28,24},{1,5},{5... | collective-permute-start | bytes 393224 | tf_op jit(solution)/shard_map/ppermute | solution.py:360

commit v13 on v11

--- a/solution.py
+++ b/solution.py
@@ -473,7 +473,7 @@
     found[6] = crossed(found[4], 2)
     found[3] = crossed(found[2], near)
     found[5] = crossed(found[4], near)
-    found[7] = crossed(found[5], 2)
+    found[7] = crossed(tied(found[5], found[6]), 2)
     piece = 2 * width // parts_total
     dx_self, give, keep = small_call(
         functools.partial(grad_kernel, feats),
@@ -487,7 +487,6 @@
     )
     total = (keep + crossed(give, near).astype(F32)).astype(BF16)
     total = (total.astype(F32) + crossed(total, 2).astype(F32)).astype(BF16)
-    total = tied(total, found[5], found[6])
     total = (total.astype(F32) + crossed(total, 4).astype(F32)).astype(BF16)
     grad_x = dx_self.reshape(shape)
     half = parts_total // 2

time: 107 us -> 105 us (0.981)
  starting transfers between devices: 37 us -> 35.7 us
    ppermute x33, starting transfers between devices: 37 us -> 35.7 us  [crossed(): lax.ppermute(x, axis, [(i, i ^ mask) for i in range(lax.axis_size(axis))])]
  transfers between devices with their start and end apart: 33 -> 33, of which waited for: 20 -> 18; matrix products, arithmetic and copies ran while one was open for 4% -> 4% of each run, Pallas kernels for 10% -> 10%
where the time goes in v13:
time: 105 us
  waiting for transfers between devices  46.2 us (44%)
  starting transfers between devices  35.7 us (34%)
  Pallas kernels  17.2 us (16%)
  other arithmetic  4.15 us (4%)
    ppermute x33, waiting for transfers between devices, crossed(): lax.ppermute(x, axis, [(i, i ^ mask) for i in range(lax.axis_size(axis))])  46.2 us
    ppermute x33, starting transfers between devices, crossed(): lax.ppermute(x, axis, [(i, i ^ mask) for i in range(lax.axis_size(axis))])  35.7 us
    pallas_call x4, Pallas kernels, tiles_call(): pl.pallas_call(functools.partial(tiles_kernel, masks, offsets, parts_tota...  13.3 us
    pallas_call x5, Pallas kernels, small_call(): pl.pallas_call(kernel, out_shape=outs, in_specs=[VMEM] * len(arrays), out...  3.87 us
  transfers between devices with their start and end apart: 33, of which 18 were waited for; matrix products, arithmetic and copies ran while one was open for 4% of the time, Pallas kernels for 10%

profile of v13, /device:TPU:0, one launch (start us, length us, event | category | flops | bytes accessed | tf_op | source)
XLA Modules:
  0.0 104.7 jit_solution(14569871194478014815)
XLA Ops:
  0.6 3.7 %shard_map.139 = (bf16[8,128,128]{2,1,0:T(8,128)(2,1)}, bf16[8,128,128]{2,1,0:T(8,128)(2,1)}, bf16[8,128,128]{2,1,0:T(8,128)(2,1)}, bf16[8,128,128]{2,1,0:T(8,128)(2,1)}) custom-call(s32[1,16]{1,0:T(1,128)} %refs_0_.7, s32[1,16]{1,0:T(1,128)} %refs_1_.7, s32[6,1,8]{2,1,0:T(1,128)} %bitcast.30, s32[6,1,8]{2,1,0:T(1,128)} %bitcast.34, ...), custom_call_target="tpu_custom_call" | custom-call | flops 1 | bytes 1 | tf_op jit(solution)/shard_map/pallas_call | solution.py:224
  4.4 3.0 %collective-permute-start.2 = (bf16[8,128,128]{2,1,0:T(8,128)(2,1)}, bf16[8,128,128]{2,1,0:T(8,128)(2,1)S(1)}, u32[]{:S(2)}, u32[]{:S(2)}) collective-permute-start(bf16[8,128,128]{2,1,0:T(8,128)(2,1)} %get-tuple-element.80), channel_id=1, source_target_pairs={{0,4},{4,0},{8,12},{12,8},{16,20},{20,16},{24,28},{28,24},{1,5},{5... | collective-permute-start | bytes 786440 | tf_op jit(solution)/shard_map/ppermute | solution.py:360
  7.4 4.8 %shard_map.138 = (f32[8,128,128]{2,1,0:T(8,128)}, f32[8,128,128]{2,1,0:T(8,128)}, f32[8,128,128]{2,1,0:T(8,128)}, f32[8,128,128]{2,1,0:T(8,128)}, bf16[2,2,128,1...) custom-call(s32[1,16]{1,0:T(1,128)} %refs_0_.7, ...), custom_call_target="tpu_custom_call" | custom-call | flops 1 | bytes 1 | tf_op jit(solution)/shard_map/pallas_call | solution.py:224
  12.3 1.6 %collective-permute-start.1 = (bf16[2,128,512]{2,1,0:T(8,128)(2,1)}, bf16[2,128,512]{2,1,0:T(8,128)(2,1)S(1)}, u32[]{:S(2)}, u32[]{:S(2)}) collective-permute-start(bf16[2,128,512]{2,1,0:T(8,128)(2,1)} %get-tuple-element.95.refs_0_), channel_id=1, source_target_pairs={{0,2},{1,3},{2,0},{3,1},{4,6},{5,7},{6,4},{7,5},{8,10},{9,11},{10,... | collective-permute-start | bytes 786440 | tf_op jit(solution)/shard_map/ppermute | solution.py:360
  13.8 0.5 collective-permute-start
  14.3 1.1 %add_convert_fusion.2 = bf16[8,128,128]{2,1,0:T(8,128)(2,1)S(1)} fusion(f32[8,128,128]{2,1,0:T(8,128)} %get-tuple-element.79, bf16[8,128,128]{2,1,0:T(8,128)(2,1)S(1)} %collective-permute-done.2), kind=kLoop, calls=%fused_computation.3 | loop fusion | flops 393216 | bytes 1048576 | tf_op jit(solution)/shard_map/convert_element_type | solution.py:429
  15.5 1.6 %collective-permute-start.3 = (bf16[8,128,128]{2,1,0:T(8,128)(2,1)S(1)}, bf16[8,128,128]{2,1,0:T(8,128)(2,1)S(1)}, u32[]{:S(2)}, u32[]{:S(2)}) collective-permute-start(bf16[8,128,128]{2,1,0:T(8,128)(2,1)S(1)} %add_convert_fusion.2), channel_id=1, source_target_pairs={{0,8},{4,12},{8,0},{12,4},{16,24},{20,28},{24,16},{28,20},{1,9},{5... | collective-permute-start | bytes 786440 | tf_op jit(solution)/shard_map/ppermute | solution.py:360
  17.1 1.5 %collective-permute-start.4 = (bf16[8,128,128]{2,1,0:T(8,128)(2,1)S(1)}, bf16[8,128,128]{2,1,0:T(8,128)(2,1)S(1)}, u32[]{:S(2)}, u32[]{:S(2)}) collective-permute-start(bf16[8,128,128]{2,1,0:T(8,128)(2,1)S(1)} %copy-done.13), channel_id=1, source_target_pairs={{0,4},{4,0},{8,12},{12,8},{16,20},{20,16},{24,28},{28,24},{1,5},{5... | collective-permute-start | bytes 786440 | tf_op jit(solution)/shard_map/ppermute | solution.py:360
  18.6 1.7 %collective-permute-done.1.refs_2_ = bf16[2,128,512]{2,1,0:T(8,128)(2,1)S(1)} collective-permute-done((bf16[2,128,512]{2,1,0:T(8,128)(2,1)}, bf16[2,128,512]{2,1,0:T(8,128)(2,1)S(1)}, u32[]{:S(2)}, u32[]{:S(2)}) %collective-permute-start.1) | collective-permute-done | bytes 262176 | tf_op jit(solution)/shard_map/ppermute | solution.py:360
  20.3 2.8 %collective-permute-done = bf16[8,128,128]{2,1,0:T(8,128)(2,1)S(1)} collective-permute-done((bf16[8,128,128]{2,1,0:T(8,128)(2,1)S(1)}, bf16[8,128,128]{2,1,0:T(8,128)(2,1)S(1)}, u32[]{:S(2)}, u32[]{:S(2)}) %collective-permute-start) | collective-permute-done | bytes 262176 | tf_op jit(solution)/shard_map/ppermute | solution.py:360
  23.1 1.1 %add_convert_fusion.1 = bf16[8,128,128]{2,1,0:T(8,128)(2,1)S(1)} fusion(bf16[8,128,128]{2,1,0:T(8,128)(2,1)S(1)} %collective-permute-done.3, f32[8,128,128]{2,1,0:T(8,128)} %get-tuple-element.75, bf16[8,128,128]{2,1,0:T(8,128)(2,1)S(1)} %collective-permute-done), kind=kLoop, calls=%fused_computation.2 | loop fusion | flops 655360 | bytes 1310720 | tf_op jit(solution)/shard_map/convert_element_type | solution.py:431
  24.2 2.7 %collective-permute-start.7 = (bf16[8,128,128]{2,1,0:T(8,128)(2,1)S(1)}, bf16[8,128,128]{2,1,0:T(8,128)(2,1)S(1)}, u32[]{:S(2)}, u32[]{:S(2)}) collective-permute-start(bf16[8,128,128]{2,1,0:T(8,128)(2,1)S(1)} %add_convert_fusion.1), channel_id=1, source_target_pairs={{0,16},{4,20},{8,24},{12,28},{16,0},{20,4},{24,8},{28,12},{1,17},{... | collective-permute-start | bytes 786440 | tf_op jit(solution)/shard_map/ppermute | solution.py:360
  26.9 0.1 collective-permute-done.4
  26.9 0.8 add_convert_fusion
  27.7 1.6 %collective-permute-start.5 = (bf16[8,128,128]{2,1,0:T(8,128)(2,1)}, bf16[8,128,128]{2,1,0:T(8,128)(2,1)S(1)}, u32[]{:S(2)}, u32[]{:S(2)}) collective-permute-start(bf16[8,128,128]{2,1,0:T(8,128)(2,1)} %add_convert_fusion), channel_id=1, source_target_pairs={{0,8},{4,12},{8,0},{12,4},{16,24},{20,28},{24,16},{28,20},{1,9},{5... | collective-permute-start | bytes 786440 | tf_op jit(solution)/shard_map/ppermute | solution.py:360
  29.3 1.1 %collective-permute-start.6 = (bf16[8,128,128]{2,1,0:T(8,128)(2,1)}, bf16[8,128,128]{2,1,0:T(8,128)(2,1)}, u32[]{:S(2)}, u32[]{:S(2)}) collective-permute-start(bf16[8,128,128]{2,1,0:T(8,128)(2,1)} %get-tuple-element.83), channel_id=1, source_target_pairs={{0,4},{4,0},{8,12},{12,8},{16,20},{20,16},{24,28},{28,24},{1,5},{5... | collective-permute-start | bytes 786440 | tf_op jit(solution)/shard_map/ppermute | solution.py:360
  30.4 1.3 %collective-permute-start.8 = (bf16[2,2,128,128]{3,2,1,0:T(8,128)(2,1)}, bf16[2,2,128,128]{3,2,1,0:T(8,128)(2,1)S(1)}, u32[]{:S(2)}, u32[]{:S(2)}) collective-permute-start(bf16[2,2,128,128]{3,2,1,0:T(8,128)(2,1)} %get-tuple-element.85), channel_id=1, source_target_pairs={{0,2},{1,3},{2,0},{3,1},{4,6},{5,7},{6,4},{7,5},{8,10},{9,11},{10,... | collective-permute-start | bytes 393224 | tf_op jit(solution)/shard_map/ppermute | solution.py:360
  31.7 0.2 copy.15.inv_ref
  32.0 4.4 %collective-permute-done.8.refs_6_ = bf16[2,2,128,128]{3,2,1,0:T(8,128)(2,1)S(1)} collective-permute-done((bf16[2,2,128,128]{3,2,1,0:T(8,128)(2,1)}, bf16[2,2,128,128]{3,2,1,0:T(8,128)(2,1)S(1)}, u32[]{:S(2)}, u32[]{:S(2)}) %collective-permute-start.8) | collective-permute-done | bytes 131104 | tf_op jit(solution)/shard_map/ppermute | solution.py:360
  36.3 1.3 %collective-permute-done.9.refs_7_ = bf16[2,2,128,128]{3,2,1,0:T(8,128)(2,1)S(1)} collective-permute-done((bf16[2,2,128,128]{3,2,1,0:T(8,128)(2,1)}, bf16[2,2,128,128]{3,2,1,0:T(8,128)(2,1)S(1)}, u32[]{:S(2)}, u32[]{:S(2)}) %collective-permute-start.9) | collective-permute-done | bytes 131104 | tf_op jit(solution)/shard_map/ppermute | solution.py:360
  37.7 0.9 collective-permute-start.12
  38.5 0.1 collective-permute-start.10
  38.6 0.4 collective-permute-done.5
  39.0 1.0 convert_add_fusion.keep_ref
  40.0 0.2 shard_map.140
  40.3 0.3 collective-permute-start.13
  40.6 1.2 %collective-permute-start.14 = (bf16[2,128,128]{2,1,0:T(8,128)(2,1)S(1)}, bf16[2,128,128]{2,1,0:T(8,128)(2,1)S(1)}, u32[]{:S(2)}, u32[]{:S(2)}) collective-permute-start(bf16[2,128,128]{2,1,0:T(8,128)(2,1)S(1)} %get-tuple-element.105), channel_id=1, source_target_pairs={{0,2},{1,3},{2,0},{3,1},{4,6},{5,7},{6,4},{7,5},{8,10},{9,11},{10,... | collective-permute-start | bytes 196616 | tf_op jit(solution)/shard_map/ppermute | solution.py:360
  41.7 0.5 collective-permute-start.15
  42.2 0.1 dynamic_slice.3
  42.3 0.1 copy.16.inv_ref
  42.5 2.6 %collective-permute-done.14.refs_10_ = bf16[2,128,128]{2,1,0:T(8,128)(2,1)S(1)} collective-permute-done((bf16[2,128,128]{2,1,0:T(8,128)(2,1)S(1)}, bf16[2,128,128]{2,1,0:T(8,128)(2,1)S(1)}, u32[]{:S(2)}, u32[]{:S(2)}) %collective-permute-start.14) | collective-permute-done | bytes 65568 | tf_op jit(solution)/shard_map/ppermute | solution.py:360
  45.1 1.0 collective-permute-done.15.refs_11_
  46.1 1.3 %shard_map.141 = (bf16[5,256,128]{2,1,0:T(8,128)(2,1)S(1)}, bf16[5,256,128]{2,1,0:T(8,128)(2,1)S(1)}, bf16[5,256,128]{2,1,0:T(8,128)(2,1)S(1)}, bf16[256,128]{1,...) custom-call(f32[256,1]{1,0:T(8,128)S(1)} %copy.16.inv_ref, ...), custom_call_target="tpu_custom_call" | custom-call | flops 1 | bytes 1 | tf_op jit(solution)/shard_map/pallas_call | solution.py:244
  47.3 0.2 collective-permute-start.16
  47.5 1.0 collective-permute-start.17
  48.6 0.7 collective-permute-start.18
  49.3 3.1 %collective-permute-done.17 = bf16[256,128]{1,0:T(8,128)(2,1)S(1)} collective-permute-done((bf16[256,128]{1,0:T(8,128)(2,1)S(1)}, bf16[256,128]{1,0:T(8,128)(2,1)S(1)}, u32[]{:S(2)}, u32[]{:S(2)}) %collective-permute-start.17) | collective-permute-done | bytes 65568 | tf_op jit(solution)/shard_map/ppermute | solution.py:360
  52.3 0.5 collective-permute-done.18
  52.9 1.1 %collective-permute-start.20 = (bf16[5,256,128]{2,1,0:T(8,128)(2,1)S(1)}, bf16[5,256,128]{2,1,0:T(8,128)(2,1)S(1)}, u32[]{:S(2)}, u32[]{:S(2)}) collective-permute-start(bf16[5,256,128]{2,1,0:T(8,128)(2,1)S(1)} %get-tuple-element.114), channel_id=1, source_target_pairs={{0,2},{1,3},{2,0},{3,1},{4,6},{5,7},{6,4},{7,5},{8,10},{9,11},{10,... | collective-permute-start | bytes 983048 | tf_op jit(solution)/shard_map/ppermute | solution.py:360
  54.0 0.6 collective-permute-start.21
  54.6 2.2 %collective-permute-start.19 = (bf16[8,128,128]{2,1,0:T(8,128)(2,1)S(1)}, bf16[8,128,128]{2,1,0:T(8,128)(2,1)S(1)}, u32[]{:S(2)}, u32[]{:S(2)}) collective-permute-start(bf16[8,128,128]{2,1,0:T(8,128)(2,1)S(1)} %bitcast.24), channel_id=1, source_target_pairs={{0,16},{4,20},{8,24},{12,28},{16,0},{20,4},{24,8},{28,12},{1,17},{... | collective-permute-start | bytes 786440 | tf_op jit(solution)/shard_map/ppermute | solution.py:360
  56.8 2.4 %collective-permute-start.22 = (bf16[8,128,128]{2,1,0:T(8,128)(2,1)S(1)}, bf16[8,128,128]{2,1,0:T(8,128)(2,1)S(1)}, u32[]{:S(2)}, u32[]{:S(2)}) collective-permute-start(bf16[8,128,128]{2,1,0:T(8,128)(2,1)S(1)} %bitcast.25), channel_id=1, source_target_pairs={{0,8},{4,12},{8,0},{12,4},{16,24},{20,28},{24,16},{28,20},{1,9},{5... | collective-permute-start | bytes 786440 | tf_op jit(solution)/shard_map/ppermute | solution.py:360
  59.1 1.3 %collective-permute-start.23 = (bf16[8,128,128]{2,1,0:T(8,128)(2,1)S(1)}, bf16[8,128,128]{2,1,0:T(8,128)(2,1)S(1)}, u32[]{:S(2)}, u32[]{:S(2)}) collective-permute-start(bf16[8,128,128]{2,1,0:T(8,128)(2,1)S(1)} %bitcast.26), channel_id=1, source_target_pairs={{0,4},{4,0},{8,12},{12,8},{16,20},{20,16},{24,28},{28,24},{1,5},{5... | collective-permute-start | bytes 786440 | tf_op jit(solution)/shard_map/ppermute | solution.py:360
  60.4 9.5 %collective-permute-done.19.refs_6_ = bf16[8,128,128]{2,1,0:T(8,128)(2,1)S(1)} collective-permute-done((bf16[8,128,128]{2,1,0:T(8,128)(2,1)S(1)}, bf16[8,128,128]{2,1,0:T(8,128)(2,1)S(1)}, u32[]{:S(2)}, u32[]{:S(2)}) %collective-permute-start.19) | collective-permute-done | bytes 262176 | tf_op jit(solution)/shard_map/ppermute | solution.py:360
  69.9 0.1 collective-permute-done.22.refs_8_
  70.0 0.1 collective-permute-start.24
  70.1 1.6 %collective-permute-done.24.refs_1_ = bf16[5,256,128]{2,1,0:T(8,128)(2,1)S(1)} collective-permute-done((bf16[5,256,128]{2,1,0:T(8,128)(2,1)S(1)}, bf16[5,256,128]{2,1,0:T(8,128)(2,1)S(1)}, u32[]{:S(2)}, u32[]{:S(2)}) %collective-permute-start.24) | collective-permute-done | bytes 327712 | tf_op jit(solution)/shard_map/ppermute | solution.py:360
  71.7 0.8 shard_map.142
  72.6 1.0 collective-permute-start.25
  73.6 4.6 %collective-permute-done.25 = bf16[4,32,512]{2,1,0:T(8,128)(2,1)S(1)} collective-permute-done((bf16[4,32,512]{2,1,0:T(8,128)(2,1)S(1)}, bf16[4,32,512]{2,1,0:T(8,128)(2,1)S(1)}, u32[]{:S(2)}, u32[]{:S(2)}) %collective-permute-start.25) | collective-permute-done | bytes 131104 | tf_op jit(solution)/shard_map/ppermute | solution.py:360
  78.2 1.3 %collective-permute-start.26 = (bf16[4,32,512]{2,1,0:T(8,128)(2,1)S(1)}, bf16[4,32,512]{2,1,0:T(8,128)(2,1)S(1)}, u32[]{:S(2)}, u32[]{:S(2)}) collective-permute-start(bf16[4,32,512]{2,1,0:T(8,128)(2,1)S(1)} %add_convert_fusion.5), channel_id=1, source_target_pairs={{0,8},{4,12},{8,0},{12,4},{16,24},{20,28},{24,16},{28,20},{1,9},{5... | collective-permute-start | bytes 393224 | tf_op jit(solution)/shard_map/ppermute | solution.py:360
  79.5 1.4 %collective-permute-start.29 = (bf16[8,128,128]{2,1,0:T(8,128)(2,1)S(1)}, bf16[8,128,128]{2,1,0:T(8,128)(2,1)S(1)}, u32[]{:S(2)}, u32[]{:S(2)}) collective-permute-start(bf16[8,128,128]{2,1,0:T(8,128)(2,1)S(1)} %collective-permute-done.19.refs_6_), channel_id=1, source_target_pairs={{0,4},{4,0},{8,12},{12,8},{16,20},{20,16},{24,28},{28,24},{1,5},{5... | collective-permute-start | bytes 786440 | tf_op jit(solution)/shard_map/ppermute | solution.py:360
  80.8 0.4 collective-permute-start.30
  81.3 3.0 %collective-permute-done.26 = bf16[4,32,512]{2,1,0:T(8,128)(2,1)S(1)} collective-permute-done((bf16[4,32,512]{2,1,0:T(8,128)(2,1)S(1)}, bf16[4,32,512]{2,1,0:T(8,128)(2,1)S(1)}, u32[]{:S(2)}, u32[]{:S(2)}) %collective-permute-start.26) | collective-permute-done | bytes 131104 | tf_op jit(solution)/shard_map/ppermute | solution.py:360
  84.3 2.0 %collective-permute-start.27 = (bf16[4,32,512]{2,1,0:T(8,128)(2,1)S(1)}, bf16[4,32,512]{2,1,0:T(8,128)(2,1)S(1)}, u32[]{:S(2)}, u32[]{:S(2)}) collective-permute-start(bf16[4,32,512]{2,1,0:T(8,128)(2,1)S(1)} %add_convert_fusion.4), channel_id=1, source_target_pairs={{0,16},{4,20},{8,24},{12,28},{16,0},{20,4},{24,8},{28,12},{1,17},{... | collective-permute-start | bytes 393224 | tf_op jit(solution)/shard_map/ppermute | solution.py:360
  86.4 1.4 %collective-permute-start.28 = (bf16[8,128,128]{2,1,0:T(8,128)(2,1)S(1)}, bf16[8,128,128]{2,1,0:T(8,128)(2,1)S(1)}, u32[]{:S(2)}, u32[]{:S(2)}) collective-permute-start(bf16[8,128,128]{2,1,0:T(8,128)(2,1)S(1)} %collective-permute-done.22.refs_8_), channel_id=1, source_target_pairs={{0,4},{4,0},{8,12},{12,8},{16,20},{20,16},{24,28},{28,24},{1,5},{5... | collective-permute-start | bytes 786440 | tf_op jit(solution)/shard_map/ppermute | solution.py:360
  87.8 3.9 %collective-permute-done.30.refs_8_ = bf16[8,128,128]{2,1,0:T(8,128)(2,1)S(1)} collective-permute-done((bf16[8,128,128]{2,1,0:T(8,128)(2,1)S(1)}, bf16[8,128,128]{2,1,0:T(8,128)(2,1)S(1)}, u32[]{:S(2)}, u32[]{:S(2)}) %collective-permute-start.30) | collective-permute-done | bytes 262176 | tf_op jit(solution)/shard_map/ppermute | solution.py:360
  91.7 0.7 shard_map.143
  92.5 0.3 collective-permute-done.28.refs_9_
  92.7 5.3 %collective-permute-done.31.refs_9_ = bf16[8,128,128]{2,1,0:T(8,128)(2,1)S(1)} collective-permute-done((bf16[8,128,128]{2,1,0:T(8,128)(2,1)S(1)}, bf16[8,128,128]{2,1,0:T(8,128)(2,1)S(1)}, u32[]{:S(2)}, u32[]{:S(2)}) %collective-permute-start.31) | collective-permute-done | bytes 262176 | tf_op jit(solution)/shard_map/ppermute | solution.py:360
  98.1 0.9 collective-permute-start.32
  99.0 2.1 %shard_map.144.refs_10_ = f32[8,128,128]{2,1,0:T(8,128)S(1)} custom-call(s32[1,16]{1,0:T(1,128)S(1)} %copy-done.8, s32[1,16]{1,0:T(1,128)S(1)} %copy-done.9, s32[6,1,8]{2,1,0:T(1,128)S(1)} %bitcast.32, s32[6,1,8]{2,1,0:T(1,128)S(1)} %bitcast.36, bf16[16,128,128]{2,1,0:T(8,128)(2,1)S(1)} %bitcast.20, bf16[6,8,128,128]{3,2,1,0:T(8,128)(2,1)S(1)} %bitcast.16, ...), custom_call_target="tpu_custom_call" | custom-call | flops 1 | bytes 1 | tf_op jit(solution)/shard_map/pallas_call | solution.py:224
  101.2 2.6 %shard_map.145 = f32[8,128,128]{2,1,0:T(8,128)} custom-call(s32[1,16]{1,0:T(1,128)S(1)} %copy-done.8, s32[1,16]{1,0:T(1,128)S(1)} %copy-done.9, s32[6,1,8]{2,1,0:T(1,128)S(1)} %bitcast.33, s32[6,1,8]{2,1,0:T(1,128)S(1)} %bitcast.37, bf16[16,128,128]{2,1,0:T(8,128)(2,1)S(1)} %bitcast.21, bf16[6,8,128,128]{3,2,1,0:T(8,128)(2,1)S(1)} %bitcast.17, ...), custom_call_target="tpu_custom_call" | custom-call | flops 1 | bytes 1 | tf_op jit(solution)/shard_map/pallas_call | solution.py:224
  103.8 0.9 shard_map.146
  (55 shorter events, 0.2 us)
Async XLA Ops:
  4.4 9.5 %copy-start.14 = (bf16[8,128,128]{2,1,0:T(8,128)(2,1)S(1)}, bf16[8,128,128]{2,1,0:T(8,128)(2,1)}, u32[]{:S(2)}) copy-start(bf16[8,128,128]{2,1,0:T(8,128)(2,1)} %get-tuple-element.76) | copy-start | bytes 786436
  4.4 10.0 %collective-permute-start.2 = (bf16[8,128,128]{2,1,0:T(8,128)(2,1)}, bf16[8,128,128]{2,1,0:T(8,128)(2,1)S(1)}, u32[]{:S(2)}, u32[]{:S(2)}) collective-permute-start(bf16[8,128,128]{2,1,0:T(8,128)(2,1)} %get-tuple-element.80), channel_id=1, source_target_pairs={{0,4},{4,0},{8,12},{12,8},{16,20},{20,16},{24,28},{28,24},{1,5},{5... | collective-permute-start | bytes 786440 | tf_op jit(solution)/shard_map/ppermute | solution.py:360
  7.4 9.7 %copy-start.13 = (bf16[8,128,128]{2,1,0:T(8,128)(2,1)S(1)}, bf16[8,128,128]{2,1,0:T(8,128)(2,1)}, u32[]{:S(2)}) copy-start(bf16[8,128,128]{2,1,0:T(8,128)(2,1)} %get-tuple-element.82) | copy-start | bytes 786436
  12.3 14.7 %copy-start.11 = (f32[8,128,128]{2,1,0:T(8,128)S(1)}, f32[8,128,128]{2,1,0:T(8,128)}, u32[]{:S(2)}) copy-start(f32[8,128,128]{2,1,0:T(8,128)} %get-tuple-element.81) | copy-start | bytes 1572868
  12.3 8.0 %collective-permute-start.1 = (bf16[2,128,512]{2,1,0:T(8,128)(2,1)}, bf16[2,128,512]{2,1,0:T(8,128)(2,1)S(1)}, u32[]{:S(2)}, u32[]{:S(2)}) collective-permute-start(bf16[2,128,512]{2,1,0:T(8,128)(2,1)} %get-tuple-element.95.refs_0_), channel_id=1, source_target_pairs={{0,2},{1,3},{2,0},{3,1},{4,6},{5,7},{6,4},{7,5},{8,10},{9,11},{10,... | collective-permute-start | bytes 786440 | tf_op jit(solution)/shard_map/ppermute | solution.py:360
  13.8 9.2 %collective-permute-start = (bf16[8,128,128]{2,1,0:T(8,128)(2,1)S(1)}, bf16[8,128,128]{2,1,0:T(8,128)(2,1)S(1)}, u32[]{:S(2)}, u32[]{:S(2)}) collective-permute-start(bf16[8,128,128]{2,1,0:T(8,128)(2,1)S(1)} %copy-done.14), channel_id=1, source_target_pairs={{0,4},{4,0},{8,12},{12,8},{16,20},{20,16},{24,28},{28,24},{1,5},{5... | collective-permute-start | bytes 786440 | tf_op jit(solution)/shard_map/ppermute | solution.py:360
  14.3 17.4 %copy-start.12 = (s32[1024]{0:T(1024)S(1)}, s32[1024]{0:T(1024)}, u32[]{:S(2)}) copy-start(s32[1024]{0:T(1024)} %param.14) | copy-start | bytes 12292
  15.5 20.9 %copy-start.4 = (bf16[2,128,512]{2,1,0:T(8,128)(2,1)S(1)}, bf16[2,128,512]{2,1,0:T(8,128)(2,1)}, u32[]{:S(2)}) copy-start(bf16[2,128,512]{2,1,0:T(8,128)(2,1)} %get-tuple-element.95.refs_0_) | copy-start | bytes 786436
  15.5 23.1 %copy-start.15 = (bf16[2,2,128,128]{3,2,1,0:T(8,128)(2,1)S(1)}, bf16[2,2,128,128]{3,2,1,0:T(8,128)(2,1)}, u32[]{:S(2)}) copy-start(bf16[2,2,128,128]{3,2,1,0:T(8,128)(2,1)} %get-tuple-element.88) | copy-start | bytes 393220
  15.5 23.5 %copy-start.10 = (f32[8,128,128]{2,1,0:T(8,128)S(1)}, f32[8,128,128]{2,1,0:T(8,128)}, u32[]{:S(2)}) copy-start(f32[8,128,128]{2,1,0:T(8,128)} %get-tuple-element.68) | copy-start | bytes 1572868
  15.5 7.6 %collective-permute-start.3 = (bf16[8,128,128]{2,1,0:T(8,128)(2,1)S(1)}, bf16[8,128,128]{2,1,0:T(8,128)(2,1)S(1)}, u32[]{:S(2)}, u32[]{:S(2)}) collective-permute-start(bf16[8,128,128]{2,1,0:T(8,128)(2,1)S(1)} %add_convert_fusion.2), channel_id=1, source_target_pairs={{0,8},{4,12},{8,0},{12,4},{16,24},{20,28},{24,16},{28,20},{1,9},{5... | collective-permute-start | bytes 786440 | tf_op jit(solution)/shard_map/ppermute | solution.py:360
  17.1 9.8 %collective-permute-start.4 = (bf16[8,128,128]{2,1,0:T(8,128)(2,1)S(1)}, bf16[8,128,128]{2,1,0:T(8,128)(2,1)S(1)}, u32[]{:S(2)}, u32[]{:S(2)}) collective-permute-start(bf16[8,128,128]{2,1,0:T(8,128)(2,1)S(1)} %copy-done.13), channel_id=1, source_target_pairs={{0,4},{4,0},{8,12},{12,8},{16,20},{20,16},{24,28},{28,24},{1,5},{5... | collective-permute-start | bytes 786440 | tf_op jit(solution)/shard_map/ppermute | solution.py:360
  24.2 14.3 %collective-permute-start.7 = (bf16[8,128,128]{2,1,0:T(8,128)(2,1)S(1)}, bf16[8,128,128]{2,1,0:T(8,128)(2,1)S(1)}, u32[]{:S(2)}, u32[]{:S(2)}) collective-permute-start(bf16[8,128,128]{2,1,0:T(8,128)(2,1)S(1)} %add_convert_fusion.1), channel_id=1, source_target_pairs={{0,16},{4,20},{8,24},{12,28},{16,0},{20,4},{24,8},{28,12},{1,17},{... | collective-permute-start | bytes 786440 | tf_op jit(solution)/shard_map/ppermute | solution.py:360
  27.7 11.3 %collective-permute-start.5 = (bf16[8,128,128]{2,1,0:T(8,128)(2,1)}, bf16[8,128,128]{2,1,0:T(8,128)(2,1)S(1)}, u32[]{:S(2)}, u32[]{:S(2)}) collective-permute-start(bf16[8,128,128]{2,1,0:T(8,128)(2,1)} %add_convert_fusion), channel_id=1, source_target_pairs={{0,8},{4,12},{8,0},{12,4},{16,24},{20,28},{24,16},{28,20},{1,9},{5... | collective-permute-start | bytes 786440 | tf_op jit(solution)/shard_map/ppermute | solution.py:360
  29.3 9.7 %collective-permute-start.6 = (bf16[8,128,128]{2,1,0:T(8,128)(2,1)}, bf16[8,128,128]{2,1,0:T(8,128)(2,1)}, u32[]{:S(2)}, u32[]{:S(2)}) collective-permute-start(bf16[8,128,128]{2,1,0:T(8,128)(2,1)} %get-tuple-element.83), channel_id=1, source_target_pairs={{0,4},{4,0},{8,12},{12,8},{16,20},{20,16},{24,28},{28,24},{1,5},{5... | collective-permute-start | bytes 786440 | tf_op jit(solution)/shard_map/ppermute | solution.py:360
  30.4 5.9 %collective-permute-start.8 = (bf16[2,2,128,128]{3,2,1,0:T(8,128)(2,1)}, bf16[2,2,128,128]{3,2,1,0:T(8,128)(2,1)S(1)}, u32[]{:S(2)}, u32[]{:S(2)}) collective-permute-start(bf16[2,2,128,128]{3,2,1,0:T(8,128)(2,1)} %get-tuple-element.85), channel_id=1, source_target_pairs={{0,2},{1,3},{2,0},{3,1},{4,6},{5,7},{6,4},{7,5},{8,10},{9,11},{10,... | collective-permute-start | bytes 393224 | tf_op jit(solution)/shard_map/ppermute | solution.py:360
  31.7 6.0 %collective-permute-start.9 = (bf16[2,2,128,128]{3,2,1,0:T(8,128)(2,1)}, bf16[2,2,128,128]{3,2,1,0:T(8,128)(2,1)S(1)}, u32[]{:S(2)}, u32[]{:S(2)}) collective-permute-start(bf16[2,2,128,128]{3,2,1,0:T(8,128)(2,1)} %get-tuple-element.86), channel_id=1, source_target_pairs={{0,3},{1,2},{2,1},{3,0},{4,7},{5,6},{6,5},{7,4},{8,11},{9,10},{10,... | collective-permute-start | bytes 393224 | tf_op jit(solution)/shard_map/ppermute | solution.py:360
  32.0 14.1 %copy-start.5 = (bf16[2,2,128,128]{3,2,1,0:T(8,128)(2,1)S(1)}, bf16[2,2,128,128]{3,2,1,0:T(8,128)(2,1)}, u32[]{:S(2)}) copy-start(bf16[2,2,128,128]{3,2,1,0:T(8,128)(2,1)} %get-tuple-element.99.refs_4_) | copy-start | bytes 393220
  36.3 3.7 %collective-permute-start.11 = (bf16[2,128,512]{2,1,0:T(8,128)(2,1)S(1)}, bf16[2,128,512]{2,1,0:T(8,128)(2,1)S(1)}, u32[]{:S(2)}, u32[]{:S(2)}) collective-permute-start(bf16[2,128,512]{2,1,0:T(8,128)(2,1)S(1)} %copy-done.4), channel_id=1, source_target_pairs={{0,1},{1,0},{2,3},{3,2},{4,5},{5,4},{6,7},{7,6},{8,9},{9,8},{10,11... | collective-permute-start | bytes 786440 | tf_op jit(solution)/shard_map/ppermute | solution.py:360
  37.7 2.4 %collective-permute-start.12 = (bf16[2,128,512]{2,1,0:T(8,128)(2,1)S(1)}, bf16[2,128,512]{2,1,0:T(8,128)(2,1)S(1)}, u32[]{:S(2)}, u32[]{:S(2)}) collective-permute-start(bf16[2,128,512]{2,1,0:T(8,128)(2,1)S(1)} %collective-permute-done.1.refs_2_), channel_id=1, source_target_pairs={{0,1},{1,0},{2,3},{3,2},{4,5},{5,4},{6,7},{7,6},{8,9},{9,8},{10,11... | collective-permute-start | bytes 786440 | tf_op jit(solution)/shard_map/ppermute | solution.py:360
  38.5 1.5 %collective-permute-start.10 = (bf16[2,2,128,128]{3,2,1,0:T(8,128)(2,1)S(1)}, bf16[2,2,128,128]{3,2,1,0:T(8,128)(2,1)S(1)}, u32[]{:S(2)}, u32[]{:S(2)}) collective-permute-start(bf16[2,2,128,128]{3,2,1,0:T(8,128)(2,1)S(1)} %copy-done.15), channel_id=1, source_target_pairs={{0,1},{1,0},{2,3},{3,2},{4,5},{5,4},{6,7},{7,6},{8,9},{9,8},{10,11... | collective-permute-start | bytes 393224 | tf_op jit(solution)/shard_map/ppermute | solution.py:360
  40.3 31.4 %copy-start.2 = (bf16[1024,128]{1,0:T(8,128)(2,1)S(1)}, bf16[1024,128]{1,0:T(8,128)(2,1)}, u32[]{:S(2)}) copy-start(bf16[1024,128]{1,0:T(8,128)(2,1)} %f_ref.1) | copy-start | bytes 786436
  40.3 31.4 %copy-start.3 = (bf16[128,512]{1,0:T(8,128)(2,1)S(1)}, bf16[128,512]{1,0:T(8,128)(2,1)}, u32[]{:S(2)}) copy-start(bf16[128,512]{1,0:T(8,128)(2,1)} %w_ref.1) | copy-start | bytes 393220
  40.3 2.1 %collective-permute-start.13 = (bf16[2,128,128]{2,1,0:T(8,128)(2,1)S(1)}, bf16[2,128,128]{2,1,0:T(8,128)(2,1)S(1)}, u32[]{:S(2)}, u32[]{:S(2)}) collective-permute-start(bf16[2,128,128]{2,1,0:T(8,128)(2,1)S(1)} %get-tuple-element.104), channel_id=1, source_target_pairs={{0,1},{1,0},{2,3},{3,2},{4,5},{5,4},{6,7},{7,6},{8,9},{9,8},{10,11... | collective-permute-start | bytes 196616 | tf_op jit(solution)/shard_map/ppermute | solution.py:360
  40.6 4.5 %collective-permute-start.14 = (bf16[2,128,128]{2,1,0:T(8,128)(2,1)S(1)}, bf16[2,128,128]{2,1,0:T(8,128)(2,1)S(1)}, u32[]{:S(2)}, u32[]{:S(2)}) collective-permute-start(bf16[2,128,128]{2,1,0:T(8,128)(2,1)S(1)} %get-tuple-element.105), channel_id=1, source_target_pairs={{0,2},{1,3},{2,0},{3,1},{4,6},{5,7},{6,4},{7,5},{8,10},{9,11},{10,... | collective-permute-start | bytes 196616 | tf_op jit(solution)/shard_map/ppermute | solution.py:360
  41.7 4.3 %collective-permute-start.15 = (bf16[2,128,128]{2,1,0:T(8,128)(2,1)S(1)}, bf16[2,128,128]{2,1,0:T(8,128)(2,1)S(1)}, u32[]{:S(2)}, u32[]{:S(2)}) collective-permute-start(bf16[2,128,128]{2,1,0:T(8,128)(2,1)S(1)} %get-tuple-element.106), channel_id=1, source_target_pairs={{0,3},{1,2},{2,1},{3,0},{4,7},{5,6},{6,5},{7,4},{8,11},{9,10},{10,... | collective-permute-start | bytes 196616 | tf_op jit(solution)/shard_map/ppermute | solution.py:360
  47.3 1.9 %collective-permute-start.16 = (bf16[256,128]{1,0:T(8,128)(2,1)S(1)}, bf16[256,128]{1,0:T(8,128)(2,1)S(1)}, u32[]{:S(2)}, u32[]{:S(2)}) collective-permute-start(bf16[256,128]{1,0:T(8,128)(2,1)S(1)} %get-tuple-element.108), channel_id=1, source_target_pairs={{0,1},{1,0},{2,3},{3,2},{4,5},{5,4},{6,7},{7,6},{8,9},{9,8},{10,11... | collective-permute-start | bytes 196616 | tf_op jit(solution)/shard_map/ppermute | solution.py:360
  47.5 4.8 %collective-permute-start.17 = (bf16[256,128]{1,0:T(8,128)(2,1)S(1)}, bf16[256,128]{1,0:T(8,128)(2,1)S(1)}, u32[]{:S(2)}, u32[]{:S(2)}) collective-permute-start(bf16[256,128]{1,0:T(8,128)(2,1)S(1)} %get-tuple-element.109), channel_id=1, source_target_pairs={{0,2},{1,3},{2,0},{3,1},{4,6},{5,7},{6,4},{7,5},{8,10},{9,11},{10,... | collective-permute-start | bytes 196616 | tf_op jit(solution)/shard_map/ppermute | solution.py:360
  48.6 4.3 %collective-permute-start.18 = (bf16[256,128]{1,0:T(8,128)(2,1)S(1)}, bf16[256,128]{1,0:T(8,128)(2,1)S(1)}, u32[]{:S(2)}, u32[]{:S(2)}) collective-permute-start(bf16[256,128]{1,0:T(8,128)(2,1)S(1)} %get-tuple-element.110), channel_id=1, source_target_pairs={{0,3},{1,2},{2,1},{3,0},{4,7},{5,6},{6,5},{7,4},{8,11},{9,10},{10,... | collective-permute-start | bytes 196616 | tf_op jit(solution)/shard_map/ppermute | solution.py:360
  52.9 17.1 %collective-permute-start.20 = (bf16[5,256,128]{2,1,0:T(8,128)(2,1)S(1)}, bf16[5,256,128]{2,1,0:T(8,128)(2,1)S(1)}, u32[]{:S(2)}, u32[]{:S(2)}) collective-permute-start(bf16[5,256,128]{2,1,0:T(8,128)(2,1)S(1)} %get-tuple-element.114), channel_id=1, source_target_pairs={{0,2},{1,3},{2,0},{3,1},{4,6},{5,7},{6,4},{7,5},{8,10},{9,11},{10,... | collective-permute-start | bytes 983048 | tf_op jit(solution)/shard_map/ppermute | solution.py:360
  54.0 16.1 %collective-permute-start.21 = (bf16[5,256,128]{2,1,0:T(8,128)(2,1)S(1)}, bf16[5,256,128]{2,1,0:T(8,128)(2,1)S(1)}, u32[]{:S(2)}, u32[]{:S(2)}) collective-permute-start(bf16[5,256,128]{2,1,0:T(8,128)(2,1)S(1)} %get-tuple-element.115), channel_id=1, source_target_pairs={{0,3},{1,2},{2,1},{3,0},{4,7},{5,6},{6,5},{7,4},{8,11},{9,10},{10,... | collective-permute-start | bytes 983048 | tf_op jit(solution)/shard_map/ppermute | solution.py:360
  54.6 15.4 %collective-permute-start.19 = (bf16[8,128,128]{2,1,0:T(8,128)(2,1)S(1)}, bf16[8,128,128]{2,1,0:T(8,128)(2,1)S(1)}, u32[]{:S(2)}, u32[]{:S(2)}) collective-permute-start(bf16[8,128,128]{2,1,0:T(8,128)(2,1)S(1)} %bitcast.24), channel_id=1, source_target_pairs={{0,16},{4,20},{8,24},{12,28},{16,0},{20,4},{24,8},{28,12},{1,17},{... | collective-permute-start | bytes 786440 | tf_op jit(solution)/shard_map/ppermute | solution.py:360
  56.8 13.2 %collective-permute-start.22 = (bf16[8,128,128]{2,1,0:T(8,128)(2,1)S(1)}, bf16[8,128,128]{2,1,0:T(8,128)(2,1)S(1)}, u32[]{:S(2)}, u32[]{:S(2)}) collective-permute-start(bf16[8,128,128]{2,1,0:T(8,128)(2,1)S(1)} %bitcast.25), channel_id=1, source_target_pairs={{0,8},{4,12},{8,0},{12,4},{16,24},{20,28},{24,16},{28,20},{1,9},{5... | collective-permute-start | bytes 786440 | tf_op jit(solution)/shard_map/ppermute | solution.py:360
  59.1 10.9 %collective-permute-start.23 = (bf16[8,128,128]{2,1,0:T(8,128)(2,1)S(1)}, bf16[8,128,128]{2,1,0:T(8,128)(2,1)S(1)}, u32[]{:S(2)}, u32[]{:S(2)}) collective-permute-start(bf16[8,128,128]{2,1,0:T(8,128)(2,1)S(1)} %bitcast.26), channel_id=1, source_target_pairs={{0,4},{4,0},{8,12},{12,8},{16,20},{20,16},{24,28},{28,24},{1,5},{5... | collective-permute-start | bytes 786440 | tf_op jit(solution)/shard_map/ppermute | solution.py:360
  70.0 1.7 %collective-permute-start.24 = (bf16[5,256,128]{2,1,0:T(8,128)(2,1)S(1)}, bf16[5,256,128]{2,1,0:T(8,128)(2,1)S(1)}, u32[]{:S(2)}, u32[]{:S(2)}) collective-permute-start(bf16[5,256,128]{2,1,0:T(8,128)(2,1)S(1)} %get-tuple-element.117.refs_0_), channel_id=1, source_target_pairs={{0,1},{1,0},{2,3},{3,2},{4,5},{5,4},{6,7},{7,6},{8,9},{9,8},{10,11... | collective-permute-start | bytes 983048 | tf_op jit(solution)/shard_map/ppermute | solution.py:360
  72.5 26.5 %copy-start = (bf16[1,6,8,128,128]{4,3,2,1,0:T(8,128)(2,1)S(1)}, bf16[1,6,8,128,128]{4,3,2,1,0:T(8,128)(2,1)}, u32[]{:S(2)}) copy-start(bf16[1,6,8,128,128]{4,3,2,1,0:T(8,128)(2,1)} %param.18) | copy-start | bytes 4718596
  72.5 26.5 %copy-start.1 = (bf16[1,16,128,128]{3,2,1,0:T(8,128)(2,1)S(1)}, bf16[1,16,128,128]{3,2,1,0:T(8,128)(2,1)}, u32[]{:S(2)}) copy-start(bf16[1,16,128,128]{3,2,1,0:T(8,128)(2,1)} %param.15) | copy-start | bytes 1572868
  72.5 26.5 %copy-start.6 = (s32[1,6,8]{2,0,1:T(1,128)S(1)}, s32[1,6,8]{2,0,1:T(1,128)}, u32[]{:S(2)}) copy-start(s32[1,6,8]{2,0,1:T(1,128)} %param.19) | copy-start | bytes 580
  72.6 26.5 %copy-start.7 = (s32[1,6,8]{2,0,1:T(1,128)S(1)}, s32[1,6,8]{2,0,1:T(1,128)}, u32[]{:S(2)}) copy-start(s32[1,6,8]{2,0,1:T(1,128)} %param.20) | copy-start | bytes 580
  72.6 26.5 %copy-start.8 = (s32[1,16]{1,0:T(1,128)S(1)}, s32[1,16]{1,0:T(1,128)}, u32[]{:S(2)}) copy-start(s32[1,16]{1,0:T(1,128)} %refs_0_.7) | copy-start | bytes 196
  72.6 26.5 %copy-start.9 = (s32[1,16]{1,0:T(1,128)S(1)}, s32[1,16]{1,0:T(1,128)}, u32[]{:S(2)}) copy-start(s32[1,16]{1,0:T(1,128)} %refs_1_.7) | copy-start | bytes 196
  72.6 5.6 %collective-permute-start.25 = (bf16[4,32,512]{2,1,0:T(8,128)(2,1)S(1)}, bf16[4,32,512]{2,1,0:T(8,128)(2,1)S(1)}, u32[]{:S(2)}, u32[]{:S(2)}) collective-permute-start(bf16[4,32,512]{2,1,0:T(8,128)(2,1)S(1)} %get-tuple-element.121), channel_id=1, source_target_pairs={{0,4},{4,0},{8,12},{12,8},{16,20},{20,16},{24,28},{28,24},{1,5},{5... | collective-permute-start | bytes 393224 | tf_op jit(solution)/shard_map/ppermute | solution.py:360
  78.2 6.1 %collective-permute-start.26 = (bf16[4,32,512]{2,1,0:T(8,128)(2,1)S(1)}, bf16[4,32,512]{2,1,0:T(8,128)(2,1)S(1)}, u32[]{:S(2)}, u32[]{:S(2)}) collective-permute-start(bf16[4,32,512]{2,1,0:T(8,128)(2,1)S(1)} %add_convert_fusion.5), channel_id=1, source_target_pairs={{0,8},{4,12},{8,0},{12,4},{16,24},{20,28},{24,16},{28,20},{1,9},{5... | collective-permute-start | bytes 393224 | tf_op jit(solution)/shard_map/ppermute | solution.py:360
  79.5 8.3 %collective-permute-start.29 = (bf16[8,128,128]{2,1,0:T(8,128)(2,1)S(1)}, bf16[8,128,128]{2,1,0:T(8,128)(2,1)S(1)}, u32[]{:S(2)}, u32[]{:S(2)}) collective-permute-start(bf16[8,128,128]{2,1,0:T(8,128)(2,1)S(1)} %collective-permute-done.19.refs_6_), channel_id=1, source_target_pairs={{0,4},{4,0},{8,12},{12,8},{16,20},{20,16},{24,28},{28,24},{1,5},{5... | collective-permute-start | bytes 786440 | tf_op jit(solution)/shard_map/ppermute | solution.py:360
  80.8 10.8 %collective-permute-start.30 = (bf16[8,128,128]{2,1,0:T(8,128)(2,1)S(1)}, bf16[8,128,128]{2,1,0:T(8,128)(2,1)S(1)}, u32[]{:S(2)}, u32[]{:S(2)}) collective-permute-start(bf16[8,128,128]{2,1,0:T(8,128)(2,1)S(1)} %collective-permute-done.19.refs_6_), channel_id=1, source_target_pairs={{0,8},{4,12},{8,0},{12,4},{16,24},{20,28},{24,16},{28,20},{1,9},{5... | collective-permute-start | bytes 786440 | tf_op jit(solution)/shard_map/ppermute | solution.py:360
  84.3 8.1 %collective-permute-start.27 = (bf16[4,32,512]{2,1,0:T(8,128)(2,1)S(1)}, bf16[4,32,512]{2,1,0:T(8,128)(2,1)S(1)}, u32[]{:S(2)}, u32[]{:S(2)}) collective-permute-start(bf16[4,32,512]{2,1,0:T(8,128)(2,1)S(1)} %add_convert_fusion.4), channel_id=1, source_target_pairs={{0,16},{4,20},{8,24},{12,28},{16,0},{20,4},{24,8},{28,12},{1,17},{... | collective-permute-start | bytes 393224 | tf_op jit(solution)/shard_map/ppermute | solution.py:360
  86.4 6.4 %collective-permute-start.28 = (bf16[8,128,128]{2,1,0:T(8,128)(2,1)S(1)}, bf16[8,128,128]{2,1,0:T(8,128)(2,1)S(1)}, u32[]{:S(2)}, u32[]{:S(2)}) collective-permute-start(bf16[8,128,128]{2,1,0:T(8,128)(2,1)S(1)} %collective-permute-done.22.refs_8_), channel_id=1, source_target_pairs={{0,4},{4,0},{8,12},{12,8},{16,20},{20,16},{24,28},{28,24},{1,5},{5... | collective-permute-start | bytes 786440 | tf_op jit(solution)/shard_map/ppermute | solution.py:360
  91.7 6.4 %collective-permute-start.31 = (bf16[8,128,128]{2,1,0:T(8,128)(2,1)S(1)}, bf16[8,128,128]{2,1,0:T(8,128)(2,1)S(1)}, u32[]{:S(2)}, u32[]{:S(2)}) collective-permute-start(bf16[8,128,128]{2,1,0:T(8,128)(2,1)S(1)} %collective-permute-done.29.refs_7_), channel_id=1, source_target_pairs={{0,8},{4,12},{8,0},{12,4},{16,24},{20,28},{24,16},{28,20},{1,9},{5... | collective-permute-start | bytes 786440 | tf_op jit(solution)/shard_map/ppermute | solution.py:360
  98.1 5.8 %collective-permute-start.32 = (bf16[4,32,512]{2,1,0:T(8,128)(2,1)S(1)}, bf16[4,32,512]{2,1,0:T(8,128)(2,1)S(1)}, u32[]{:S(2)}, u32[]{:S(2)}) collective-permute-start(bf16[4,32,512]{2,1,0:T(8,128)(2,1)S(1)} %add_convert_fusion.3.mine_ref), channel_id=1, source_target_pairs={{0,4},{4,0},{8,12},{12,8},{16,20},{20,16},{24,28},{28,24},{1,5},{5... | collective-permute-start | bytes 393224 | tf_op jit(solution)/shard_map/ppermute | solution.py:360

commit v14 on v13

--- a/solution.py
+++ b/solution.py
@@ -502,7 +502,7 @@
             like(shape, F32),
             24,
         )
-    total, out = tied((total, out), found[3], found[7])
+    total, out = tied((total, out), found[3], found[6])
     grad_self, grad_neigh = small_call(
         finish_kernel,
         [like((width, full), F32)] * 2,

time: 105 us -> 101 us (0.962)
  waiting for transfers between devices: 46.2 us -> 41.3 us
    ppermute x33, waiting for transfers between devices: 46.2 us -> 41.3 us  [crossed(): lax.ppermute(x, axis, [(i, i ^ mask) for i in range(lax.axis_size(axis))])]
  transfers between devices with their start and end apart: 33 -> 33, of which waited for: 18 -> 18; matrix products, arithmetic and copies ran while one was open for 4% -> 5% of each run, Pallas kernels for 10% -> 10%
where the time goes in v14:
time: 101 us
  waiting for transfers between devices  41.3 us (41%)
  starting transfers between devices  36.7 us (36%)
  Pallas kernels  17.2 us (17%)
  other arithmetic  4.15 us (4%)
    ppermute x33, waiting for transfers between devices, crossed(): lax.ppermute(x, axis, [(i, i ^ mask) for i in range(lax.axis_size(axis))])  41.3 us
    ppermute x33, starting transfers between devices, crossed(): lax.ppermute(x, axis, [(i, i ^ mask) for i in range(lax.axis_size(axis))])  36.7 us
    pallas_call x4, Pallas kernels, tiles_call(): pl.pallas_call(functools.partial(tiles_kernel, masks, offsets, parts_tota...  13.3 us
    pallas_call x5, Pallas kernels, small_call(): pl.pallas_call(kernel, out_shape=outs, in_specs=[VMEM] * len(arrays), out...  3.86 us
  transfers between devices with their start and end apart: 33, of which 18 were waited for; matrix products, arithmetic and copies ran while one was open for 5% of the time, Pallas kernels for 10%

profile of v14, /device:TPU:0, one launch (start us, length us, event | category | flops | bytes accessed | tf_op | source)
XLA Modules:
  0.0 100.8 jit_solution(6275271821123655235)
XLA Ops:
  0.6 3.7 %shard_map.139 = (bf16[8,128,128]{2,1,0:T(8,128)(2,1)}, bf16[8,128,128]{2,1,0:T(8,128)(2,1)}, bf16[8,128,128]{2,1,0:T(8,128)(2,1)}, bf16[8,128,128]{2,1,0:T(8,128)(2,1)}) custom-call(s32[1,16]{1,0:T(1,128)} %refs_0_.7, s32[1,16]{1,0:T(1,128)} %refs_1_.7, s32[6,1,8]{2,1,0:T(1,128)} %bitcast.30, s32[6,1,8]{2,1,0:T(1,128)} %bitcast.34, ...), custom_call_target="tpu_custom_call" | custom-call | flops 1 | bytes 1 | tf_op jit(solution)/shard_map/pallas_call | solution.py:224
  4.4 3.0 %collective-permute-start.2 = (bf16[8,128,128]{2,1,0:T(8,128)(2,1)}, bf16[8,128,128]{2,1,0:T(8,128)(2,1)S(1)}, u32[]{:S(2)}, u32[]{:S(2)}) collective-permute-start(bf16[8,128,128]{2,1,0:T(8,128)(2,1)} %get-tuple-element.80), channel_id=1, source_target_pairs={{0,4},{4,0},{8,12},{12,8},{16,20},{20,16},{24,28},{28,24},{1,5},{5... | collective-permute-start | bytes 786440 | tf_op jit(solution)/shard_map/ppermute | solution.py:360
  7.4 4.8 %shard_map.138 = (f32[8,128,128]{2,1,0:T(8,128)}, f32[8,128,128]{2,1,0:T(8,128)}, f32[8,128,128]{2,1,0:T(8,128)}, f32[8,128,128]{2,1,0:T(8,128)}, bf16[2,2,128,1...) custom-call(s32[1,16]{1,0:T(1,128)} %refs_0_.7, ...), custom_call_target="tpu_custom_call" | custom-call | flops 1 | bytes 1 | tf_op jit(solution)/shard_map/pallas_call | solution.py:224
  12.3 1.6 %collective-permute-start.1 = (bf16[2,128,512]{2,1,0:T(8,128)(2,1)}, bf16[2,128,512]{2,1,0:T(8,128)(2,1)S(1)}, u32[]{:S(2)}, u32[]{:S(2)}) collective-permute-start(bf16[2,128,512]{2,1,0:T(8,128)(2,1)} %get-tuple-element.95.refs_0_), channel_id=1, source_target_pairs={{0,2},{1,3},{2,0},{3,1},{4,6},{5,7},{6,4},{7,5},{8,10},{9,11},{10,... | collective-permute-start | bytes 786440 | tf_op jit(solution)/shard_map/ppermute | solution.py:360
  13.8 0.5 collective-permute-start
  14.3 1.1 %add_convert_fusion.2 = bf16[8,128,128]{2,1,0:T(8,128)(2,1)S(1)} fusion(f32[8,128,128]{2,1,0:T(8,128)} %get-tuple-element.79, bf16[8,128,128]{2,1,0:T(8,128)(2,1)S(1)} %collective-permute-done.2), kind=kLoop, calls=%fused_computation.3 | loop fusion | flops 393216 | bytes 1048576 | tf_op jit(solution)/shard_map/convert_element_type | solution.py:429
  15.5 1.6 %collective-permute-start.3 = (bf16[8,128,128]{2,1,0:T(8,128)(2,1)S(1)}, bf16[8,128,128]{2,1,0:T(8,128)(2,1)S(1)}, u32[]{:S(2)}, u32[]{:S(2)}) collective-permute-start(bf16[8,128,128]{2,1,0:T(8,128)(2,1)S(1)} %add_convert_fusion.2), channel_id=1, source_target_pairs={{0,8},{4,12},{8,0},{12,4},{16,24},{20,28},{24,16},{28,20},{1,9},{5... | collective-permute-start | bytes 786440 | tf_op jit(solution)/shard_map/ppermute | solution.py:360
  17.1 1.5 %collective-permute-start.4 = (bf16[8,128,128]{2,1,0:T(8,128)(2,1)S(1)}, bf16[8,128,128]{2,1,0:T(8,128)(2,1)S(1)}, u32[]{:S(2)}, u32[]{:S(2)}) collective-permute-start(bf16[8,128,128]{2,1,0:T(8,128)(2,1)S(1)} %copy-done.13), channel_id=1, source_target_pairs={{0,4},{4,0},{8,12},{12,8},{16,20},{20,16},{24,28},{28,24},{1,5},{5... | collective-permute-start | bytes 786440 | tf_op jit(solution)/shard_map/ppermute | solution.py:360
  18.6 1.7 %collective-permute-done.1.refs_2_ = bf16[2,128,512]{2,1,0:T(8,128)(2,1)S(1)} collective-permute-done((bf16[2,128,512]{2,1,0:T(8,128)(2,1)}, bf16[2,128,512]{2,1,0:T(8,128)(2,1)S(1)}, u32[]{:S(2)}, u32[]{:S(2)}) %collective-permute-start.1) | collective-permute-done | bytes 262176 | tf_op jit(solution)/shard_map/ppermute | solution.py:360
  20.3 2.8 %collective-permute-done = bf16[8,128,128]{2,1,0:T(8,128)(2,1)S(1)} collective-permute-done((bf16[8,128,128]{2,1,0:T(8,128)(2,1)S(1)}, bf16[8,128,128]{2,1,0:T(8,128)(2,1)S(1)}, u32[]{:S(2)}, u32[]{:S(2)}) %collective-permute-start) | collective-permute-done | bytes 262176 | tf_op jit(solution)/shard_map/ppermute | solution.py:360
  23.1 1.1 %add_convert_fusion.1 = bf16[8,128,128]{2,1,0:T(8,128)(2,1)S(1)} fusion(bf16[8,128,128]{2,1,0:T(8,128)(2,1)S(1)} %collective-permute-done.3, f32[8,128,128]{2,1,0:T(8,128)} %get-tuple-element.75, bf16[8,128,128]{2,1,0:T(8,128)(2,1)S(1)} %collective-permute-done), kind=kLoop, calls=%fused_computation.2 | loop fusion | flops 655360 | bytes 1310720 | tf_op jit(solution)/shard_map/convert_element_type | solution.py:431
  24.2 2.6 %collective-permute-start.7 = (bf16[8,128,128]{2,1,0:T(8,128)(2,1)S(1)}, bf16[8,128,128]{2,1,0:T(8,128)(2,1)S(1)}, u32[]{:S(2)}, u32[]{:S(2)}) collective-permute-start(bf16[8,128,128]{2,1,0:T(8,128)(2,1)S(1)} %add_convert_fusion.1), channel_id=1, source_target_pairs={{0,16},{4,20},{8,24},{12,28},{16,0},{20,4},{24,8},{28,12},{1,17},{... | collective-permute-start | bytes 786440 | tf_op jit(solution)/shard_map/ppermute | solution.py:360
  26.9 0.8 add_convert_fusion
  27.7 1.6 %collective-permute-start.5 = (bf16[8,128,128]{2,1,0:T(8,128)(2,1)}, bf16[8,128,128]{2,1,0:T(8,128)(2,1)S(1)}, u32[]{:S(2)}, u32[]{:S(2)}) collective-permute-start(bf16[8,128,128]{2,1,0:T(8,128)(2,1)} %add_convert_fusion), channel_id=1, source_target_pairs={{0,8},{4,12},{8,0},{12,4},{16,24},{20,28},{24,16},{28,20},{1,9},{5... | collective-permute-start | bytes 786440 | tf_op jit(solution)/shard_map/ppermute | solution.py:360
  29.3 1.2 %collective-permute-start.6 = (bf16[8,128,128]{2,1,0:T(8,128)(2,1)}, bf16[8,128,128]{2,1,0:T(8,128)(2,1)}, u32[]{:S(2)}, u32[]{:S(2)}) collective-permute-start(bf16[8,128,128]{2,1,0:T(8,128)(2,1)} %get-tuple-element.83), channel_id=1, source_target_pairs={{0,4},{4,0},{8,12},{12,8},{16,20},{20,16},{24,28},{28,24},{1,5},{5... | collective-permute-start | bytes 786440 | tf_op jit(solution)/shard_map/ppermute | solution.py:360
  30.4 1.3 %collective-permute-start.8 = (bf16[2,2,128,128]{3,2,1,0:T(8,128)(2,1)}, bf16[2,2,128,128]{3,2,1,0:T(8,128)(2,1)S(1)}, u32[]{:S(2)}, u32[]{:S(2)}) collective-permute-start(bf16[2,2,128,128]{3,2,1,0:T(8,128)(2,1)} %get-tuple-element.85), channel_id=1, source_target_pairs={{0,2},{1,3},{2,0},{3,1},{4,6},{5,7},{6,4},{7,5},{8,10},{9,11},{10,... | collective-permute-start | bytes 393224 | tf_op jit(solution)/shard_map/ppermute | solution.py:360
  31.7 0.2 copy.15.inv_ref
  32.0 4.4 %collective-permute-done.8.refs_6_ = bf16[2,2,128,128]{3,2,1,0:T(8,128)(2,1)S(1)} collective-permute-done((bf16[2,2,128,128]{3,2,1,0:T(8,128)(2,1)}, bf16[2,2,128,128]{3,2,1,0:T(8,128)(2,1)S(1)}, u32[]{:S(2)}, u32[]{:S(2)}) %collective-permute-start.8) | collective-permute-done | bytes 131104 | tf_op jit(solution)/shard_map/ppermute | solution.py:360
  36.4 1.3 %collective-permute-done.9.refs_7_ = bf16[2,2,128,128]{3,2,1,0:T(8,128)(2,1)S(1)} collective-permute-done((bf16[2,2,128,128]{3,2,1,0:T(8,128)(2,1)}, bf16[2,2,128,128]{3,2,1,0:T(8,128)(2,1)S(1)}, u32[]{:S(2)}, u32[]{:S(2)}) %collective-permute-start.9) | collective-permute-done | bytes 131104 | tf_op jit(solution)/shard_map/ppermute | solution.py:360
  37.7 0.9 collective-permute-start.12
  38.5 0.1 collective-permute-start.10
  38.6 0.3 collective-permute-done.5
  39.0 1.0 %convert_add_fusion.keep_ref = f32[8,128,128]{2,1,0:T(8,128)S(1)} fusion(bf16[8,128,128]{2,1,0:T(8,128)(2,1)} %collective-permute-done.6, f32[8,128,128]{2,1,0:T(8,128)S(1)} %copy-done.10, bf16[8,128,128]{2,1,0:T(8,128)(2,1)S(1)} %collective-permute-done.5), kind=kLoop, calls=%fused_computation | loop fusion | flops 524288 | bytes 1572864 | tf_op jit(solution)/shard_map/add | solution.py:442
  40.0 0.2 shard_map.140
  40.3 0.3 collective-permute-start.13
  40.6 1.1 %collective-permute-start.14 = (bf16[2,128,128]{2,1,0:T(8,128)(2,1)S(1)}, bf16[2,128,128]{2,1,0:T(8,128)(2,1)S(1)}, u32[]{:S(2)}, u32[]{:S(2)}) collective-permute-start(bf16[2,128,128]{2,1,0:T(8,128)(2,1)S(1)} %get-tuple-element.105), channel_id=1, source_target_pairs={{0,2},{1,3},{2,0},{3,1},{4,6},{5,7},{6,4},{7,5},{8,10},{9,11},{10,... | collective-permute-start | bytes 196616 | tf_op jit(solution)/shard_map/ppermute | solution.py:360
  41.7 0.5 collective-permute-start.15
  42.2 0.1 dynamic_slice.3
  42.3 0.1 copy.16.inv_ref
  42.4 2.7 %collective-permute-done.14.refs_10_ = bf16[2,128,128]{2,1,0:T(8,128)(2,1)S(1)} collective-permute-done((bf16[2,128,128]{2,1,0:T(8,128)(2,1)S(1)}, bf16[2,128,128]{2,1,0:T(8,128)(2,1)S(1)}, u32[]{:S(2)}, u32[]{:S(2)}) %collective-permute-start.14) | collective-permute-done | bytes 65568 | tf_op jit(solution)/shard_map/ppermute | solution.py:360
  45.1 0.9 collective-permute-done.15.refs_11_
  46.0 1.3 %shard_map.141 = (bf16[5,256,128]{2,1,0:T(8,128)(2,1)S(1)}, bf16[5,256,128]{2,1,0:T(8,128)(2,1)S(1)}, bf16[5,256,128]{2,1,0:T(8,128)(2,1)S(1)}, bf16[256,128]{1,...) custom-call(f32[256,1]{1,0:T(8,128)S(1)} %copy.16.inv_ref, ...), custom_call_target="tpu_custom_call" | custom-call | flops 1 | bytes 1 | tf_op jit(solution)/shard_map/pallas_call | solution.py:244
  47.3 0.2 collective-permute-start.16
  47.4 1.1 %collective-permute-start.17 = (bf16[256,128]{1,0:T(8,128)(2,1)S(1)}, bf16[256,128]{1,0:T(8,128)(2,1)S(1)}, u32[]{:S(2)}, u32[]{:S(2)}) collective-permute-start(bf16[256,128]{1,0:T(8,128)(2,1)S(1)} %get-tuple-element.109), channel_id=1, source_target_pairs={{0,2},{1,3},{2,0},{3,1},{4,6},{5,7},{6,4},{7,5},{8,10},{9,11},{10,... | collective-permute-start | bytes 196616 | tf_op jit(solution)/shard_map/ppermute | solution.py:360
  48.5 0.7 collective-permute-start.18
  49.2 3.1 %collective-permute-done.17 = bf16[256,128]{1,0:T(8,128)(2,1)S(1)} collective-permute-done((bf16[256,128]{1,0:T(8,128)(2,1)S(1)}, bf16[256,128]{1,0:T(8,128)(2,1)S(1)}, u32[]{:S(2)}, u32[]{:S(2)}) %collective-permute-start.17) | collective-permute-done | bytes 65568 | tf_op jit(solution)/shard_map/ppermute | solution.py:360
  52.3 0.6 collective-permute-done.18
  52.8 1.1 %collective-permute-start.20 = (bf16[5,256,128]{2,1,0:T(8,128)(2,1)S(1)}, bf16[5,256,128]{2,1,0:T(8,128)(2,1)S(1)}, u32[]{:S(2)}, u32[]{:S(2)}) collective-permute-start(bf16[5,256,128]{2,1,0:T(8,128)(2,1)S(1)} %get-tuple-element.114), channel_id=1, source_target_pairs={{0,2},{1,3},{2,0},{3,1},{4,6},{5,7},{6,4},{7,5},{8,10},{9,11},{10,... | collective-permute-start | bytes 983048 | tf_op jit(solution)/shard_map/ppermute | solution.py:360
  53.9 0.6 collective-permute-start.21
  54.5 2.3 %collective-permute-start.19 = (bf16[8,128,128]{2,1,0:T(8,128)(2,1)S(1)}, bf16[8,128,128]{2,1,0:T(8,128)(2,1)S(1)}, u32[]{:S(2)}, u32[]{:S(2)}) collective-permute-start(bf16[8,128,128]{2,1,0:T(8,128)(2,1)S(1)} %bitcast.24), channel_id=1, source_target_pairs={{0,16},{4,20},{8,24},{12,28},{16,0},{20,4},{24,8},{28,12},{1,17},{... | collective-permute-start | bytes 786440 | tf_op jit(solution)/shard_map/ppermute | solution.py:360
  56.8 2.4 %collective-permute-start.22 = (bf16[8,128,128]{2,1,0:T(8,128)(2,1)S(1)}, bf16[8,128,128]{2,1,0:T(8,128)(2,1)S(1)}, u32[]{:S(2)}, u32[]{:S(2)}) collective-permute-start(bf16[8,128,128]{2,1,0:T(8,128)(2,1)S(1)} %bitcast.25), channel_id=1, source_target_pairs={{0,8},{4,12},{8,0},{12,4},{16,24},{20,28},{24,16},{28,20},{1,9},{5... | collective-permute-start | bytes 786440 | tf_op jit(solution)/shard_map/ppermute | solution.py:360
  59.2 1.2 %collective-permute-start.23 = (bf16[8,128,128]{2,1,0:T(8,128)(2,1)S(1)}, bf16[8,128,128]{2,1,0:T(8,128)(2,1)S(1)}, u32[]{:S(2)}, u32[]{:S(2)}) collective-permute-start(bf16[8,128,128]{2,1,0:T(8,128)(2,1)S(1)} %bitcast.26), channel_id=1, source_target_pairs={{0,4},{4,0},{8,12},{12,8},{16,20},{20,16},{24,28},{28,24},{1,5},{5... | collective-permute-start | bytes 786440 | tf_op jit(solution)/shard_map/ppermute | solution.py:360
  60.4 9.5 %collective-permute-done.19.refs_6_ = bf16[8,128,128]{2,1,0:T(8,128)(2,1)S(1)} collective-permute-done((bf16[8,128,128]{2,1,0:T(8,128)(2,1)S(1)}, bf16[8,128,128]{2,1,0:T(8,128)(2,1)S(1)}, u32[]{:S(2)}, u32[]{:S(2)}) %collective-permute-start.19) | collective-permute-done | bytes 262176 | tf_op jit(solution)/shard_map/ppermute | solution.py:360
  69.9 0.1 collective-permute-done.22.refs_8_
  70.0 0.1 collective-permute-start.24
  70.1 1.6 %collective-permute-done.24.refs_1_ = bf16[5,256,128]{2,1,0:T(8,128)(2,1)S(1)} collective-permute-done((bf16[5,256,128]{2,1,0:T(8,128)(2,1)S(1)}, bf16[5,256,128]{2,1,0:T(8,128)(2,1)S(1)}, u32[]{:S(2)}, u32[]{:S(2)}) %collective-permute-start.24) | collective-permute-done | bytes 327712 | tf_op jit(solution)/shard_map/ppermute | solution.py:360
  71.7 0.8 shard_map.142
  72.5 1.1 %collective-permute-start.25 = (bf16[4,32,512]{2,1,0:T(8,128)(2,1)S(1)}, bf16[4,32,512]{2,1,0:T(8,128)(2,1)S(1)}, u32[]{:S(2)}, u32[]{:S(2)}) collective-permute-start(bf16[4,32,512]{2,1,0:T(8,128)(2,1)S(1)} %get-tuple-element.121), channel_id=1, source_target_pairs={{0,4},{4,0},{8,12},{12,8},{16,20},{20,16},{24,28},{28,24},{1,5},{5... | collective-permute-start | bytes 393224 | tf_op jit(solution)/shard_map/ppermute | solution.py:360
  73.6 4.5 %collective-permute-done.25 = bf16[4,32,512]{2,1,0:T(8,128)(2,1)S(1)} collective-permute-done((bf16[4,32,512]{2,1,0:T(8,128)(2,1)S(1)}, bf16[4,32,512]{2,1,0:T(8,128)(2,1)S(1)}, u32[]{:S(2)}, u32[]{:S(2)}) %collective-permute-start.25) | collective-permute-done | bytes 131104 | tf_op jit(solution)/shard_map/ppermute | solution.py:360
  78.2 1.3 %collective-permute-start.26 = (bf16[4,32,512]{2,1,0:T(8,128)(2,1)S(1)}, bf16[4,32,512]{2,1,0:T(8,128)(2,1)S(1)}, u32[]{:S(2)}, u32[]{:S(2)}) collective-permute-start(bf16[4,32,512]{2,1,0:T(8,128)(2,1)S(1)} %add_convert_fusion.5), channel_id=1, source_target_pairs={{0,8},{4,12},{8,0},{12,4},{16,24},{20,28},{24,16},{28,20},{1,9},{5... | collective-permute-start | bytes 393224 | tf_op jit(solution)/shard_map/ppermute | solution.py:360
  79.5 0.8 collective-permute-start.29
  80.3 1.0 %collective-permute-start.30 = (bf16[8,128,128]{2,1,0:T(8,128)(2,1)S(1)}, bf16[8,128,128]{2,1,0:T(8,128)(2,1)S(1)}, u32[]{:S(2)}, u32[]{:S(2)}) collective-permute-start(bf16[8,128,128]{2,1,0:T(8,128)(2,1)S(1)} %collective-permute-done.19.refs_6_), channel_id=1, source_target_pairs={{0,4},{4,0},{8,12},{12,8},{16,20},{20,16},{24,28},{28,24},{1,5},{5... | collective-permute-start | bytes 786440 | tf_op jit(solution)/shard_map/ppermute | solution.py:360
  81.3 3.4 %collective-permute-done.26 = bf16[4,32,512]{2,1,0:T(8,128)(2,1)S(1)} collective-permute-done((bf16[4,32,512]{2,1,0:T(8,128)(2,1)S(1)}, bf16[4,32,512]{2,1,0:T(8,128)(2,1)S(1)}, u32[]{:S(2)}, u32[]{:S(2)}) %collective-permute-start.26) | collective-permute-done | bytes 131104 | tf_op jit(solution)/shard_map/ppermute | solution.py:360
  84.7 2.1 %collective-permute-start.27 = (bf16[4,32,512]{2,1,0:T(8,128)(2,1)S(1)}, bf16[4,32,512]{2,1,0:T(8,128)(2,1)S(1)}, u32[]{:S(2)}, u32[]{:S(2)}) collective-permute-start(bf16[4,32,512]{2,1,0:T(8,128)(2,1)S(1)} %add_convert_fusion.4), channel_id=1, source_target_pairs={{0,16},{4,20},{8,24},{12,28},{16,0},{20,4},{24,8},{28,12},{1,17},{... | collective-permute-start | bytes 393224 | tf_op jit(solution)/shard_map/ppermute | solution.py:360
  86.8 1.2 %collective-permute-start.28 = (bf16[8,128,128]{2,1,0:T(8,128)(2,1)S(1)}, bf16[8,128,128]{2,1,0:T(8,128)(2,1)S(1)}, u32[]{:S(2)}, u32[]{:S(2)}) collective-permute-start(bf16[8,128,128]{2,1,0:T(8,128)(2,1)S(1)} %collective-permute-done.22.refs_8_), channel_id=1, source_target_pairs={{0,4},{4,0},{8,12},{12,8},{16,20},{20,16},{24,28},{28,24},{1,5},{5... | collective-permute-start | bytes 786440 | tf_op jit(solution)/shard_map/ppermute | solution.py:360
  88.1 2.8 %collective-permute-done.29.refs_8_ = bf16[8,128,128]{2,1,0:T(8,128)(2,1)S(1)} collective-permute-done((bf16[8,128,128]{2,1,0:T(8,128)(2,1)S(1)}, bf16[8,128,128]{2,1,0:T(8,128)(2,1)S(1)}, u32[]{:S(2)}, u32[]{:S(2)}) %collective-permute-start.29) | collective-permute-done | bytes 262176 | tf_op jit(solution)/shard_map/ppermute | solution.py:360
  90.9 0.3 collective-permute-start.31
  91.2 0.7 shard_map.143
  92.0 1.6 %collective-permute-done.28.refs_9_ = bf16[8,128,128]{2,1,0:T(8,128)(2,1)S(1)} collective-permute-done((bf16[8,128,128]{2,1,0:T(8,128)(2,1)S(1)}, bf16[8,128,128]{2,1,0:T(8,128)(2,1)S(1)}, u32[]{:S(2)}, u32[]{:S(2)}) %collective-permute-start.28) | collective-permute-done | bytes 262176 | tf_op jit(solution)/shard_map/ppermute | solution.py:360
  93.6 1.4 %collective-permute-start.32 = (bf16[4,32,512]{2,1,0:T(8,128)(2,1)S(1)}, bf16[4,32,512]{2,1,0:T(8,128)(2,1)S(1)}, u32[]{:S(2)}, u32[]{:S(2)}) collective-permute-start(bf16[4,32,512]{2,1,0:T(8,128)(2,1)S(1)} %add_convert_fusion.3.mine_ref), channel_id=1, source_target_pairs={{0,4},{4,0},{8,12},{12,8},{16,20},{20,16},{24,28},{28,24},{1,5},{5... | collective-permute-start | bytes 393224 | tf_op jit(solution)/shard_map/ppermute | solution.py:360
  95.1 2.1 %shard_map.144.refs_10_ = f32[8,128,128]{2,1,0:T(8,128)S(1)} custom-call(s32[1,16]{1,0:T(1,128)S(1)} %copy-done.8, s32[1,16]{1,0:T(1,128)S(1)} %copy-done.9, s32[6,1,8]{2,1,0:T(1,128)S(1)} %bitcast.32, s32[6,1,8]{2,1,0:T(1,128)S(1)} %bitcast.36, bf16[16,128,128]{2,1,0:T(8,128)(2,1)S(1)} %bitcast.20, bf16[6,8,128,128]{3,2,1,0:T(8,128)(2,1)S(1)} %bitcast.16, ...), custom_call_target="tpu_custom_call" | custom-call | flops 1 | bytes 1 | tf_op jit(solution)/shard_map/pallas_call | solution.py:224
  97.2 0.1 collective-permute-done.31.refs_9_
  97.3 2.6 %shard_map.145 = f32[8,128,128]{2,1,0:T(8,128)} custom-call(s32[1,16]{1,0:T(1,128)S(1)} %copy-done.8, s32[1,16]{1,0:T(1,128)S(1)} %copy-done.9, s32[6,1,8]{2,1,0:T(1,128)S(1)} %bitcast.33, s32[6,1,8]{2,1,0:T(1,128)S(1)} %bitcast.37, bf16[16,128,128]{2,1,0:T(8,128)(2,1)S(1)} %bitcast.21, bf16[6,8,128,128]{3,2,1,0:T(8,128)(2,1)S(1)} %bitcast.17, ...), custom_call_target="tpu_custom_call" | custom-call | flops 1 | bytes 1 | tf_op jit(solution)/shard_map/pallas_call | solution.py:224
  99.9 0.9 shard_map.146
  (55 shorter events, 0.3 us)
Async XLA Ops:
  4.4 9.5 %copy-start.14 = (bf16[8,128,128]{2,1,0:T(8,128)(2,1)S(1)}, bf16[8,128,128]{2,1,0:T(8,128)(2,1)}, u32[]{:S(2)}) copy-start(bf16[8,128,128]{2,1,0:T(8,128)(2,1)} %get-tuple-element.76) | copy-start | bytes 786436
  4.4 9.9 %collective-permute-start.2 = (bf16[8,128,128]{2,1,0:T(8,128)(2,1)}, bf16[8,128,128]{2,1,0:T(8,128)(2,1)S(1)}, u32[]{:S(2)}, u32[]{:S(2)}) collective-permute-start(bf16[8,128,128]{2,1,0:T(8,128)(2,1)} %get-tuple-element.80), channel_id=1, source_target_pairs={{0,4},{4,0},{8,12},{12,8},{16,20},{20,16},{24,28},{28,24},{1,5},{5... | collective-permute-start | bytes 786440 | tf_op jit(solution)/shard_map/ppermute | solution.py:360
  7.4 9.7 %copy-start.13 = (bf16[8,128,128]{2,1,0:T(8,128)(2,1)S(1)}, bf16[8,128,128]{2,1,0:T(8,128)(2,1)}, u32[]{:S(2)}) copy-start(bf16[8,128,128]{2,1,0:T(8,128)(2,1)} %get-tuple-element.82) | copy-start | bytes 786436
  12.3 14.7 %copy-start.11 = (f32[8,128,128]{2,1,0:T(8,128)S(1)}, f32[8,128,128]{2,1,0:T(8,128)}, u32[]{:S(2)}) copy-start(f32[8,128,128]{2,1,0:T(8,128)} %get-tuple-element.81) | copy-start | bytes 1572868
  12.3 8.0 %collective-permute-start.1 = (bf16[2,128,512]{2,1,0:T(8,128)(2,1)}, bf16[2,128,512]{2,1,0:T(8,128)(2,1)S(1)}, u32[]{:S(2)}, u32[]{:S(2)}) collective-permute-start(bf16[2,128,512]{2,1,0:T(8,128)(2,1)} %get-tuple-element.95.refs_0_), channel_id=1, source_target_pairs={{0,2},{1,3},{2,0},{3,1},{4,6},{5,7},{6,4},{7,5},{8,10},{9,11},{10,... | collective-permute-start | bytes 786440 | tf_op jit(solution)/shard_map/ppermute | solution.py:360
  13.8 9.2 %collective-permute-start = (bf16[8,128,128]{2,1,0:T(8,128)(2,1)S(1)}, bf16[8,128,128]{2,1,0:T(8,128)(2,1)S(1)}, u32[]{:S(2)}, u32[]{:S(2)}) collective-permute-start(bf16[8,128,128]{2,1,0:T(8,128)(2,1)S(1)} %copy-done.14), channel_id=1, source_target_pairs={{0,4},{4,0},{8,12},{12,8},{16,20},{20,16},{24,28},{28,24},{1,5},{5... | collective-permute-start | bytes 786440 | tf_op jit(solution)/shard_map/ppermute | solution.py:360
  14.3 17.4 %copy-start.12 = (s32[1024]{0:T(1024)S(1)}, s32[1024]{0:T(1024)}, u32[]{:S(2)}) copy-start(s32[1024]{0:T(1024)} %param.14) | copy-start | bytes 12292
  15.5 20.9 %copy-start.4 = (bf16[2,128,512]{2,1,0:T(8,128)(2,1)S(1)}, bf16[2,128,512]{2,1,0:T(8,128)(2,1)}, u32[]{:S(2)}) copy-start(bf16[2,128,512]{2,1,0:T(8,128)(2,1)} %get-tuple-element.95.refs_0_) | copy-start | bytes 786436
  15.5 23.1 %copy-start.15 = (bf16[2,2,128,128]{3,2,1,0:T(8,128)(2,1)S(1)}, bf16[2,2,128,128]{3,2,1,0:T(8,128)(2,1)}, u32[]{:S(2)}) copy-start(bf16[2,2,128,128]{3,2,1,0:T(8,128)(2,1)} %get-tuple-element.88) | copy-start | bytes 393220
  15.5 23.5 %copy-start.10 = (f32[8,128,128]{2,1,0:T(8,128)S(1)}, f32[8,128,128]{2,1,0:T(8,128)}, u32[]{:S(2)}) copy-start(f32[8,128,128]{2,1,0:T(8,128)} %get-tuple-element.68) | copy-start | bytes 1572868
  15.5 7.6 %collective-permute-start.3 = (bf16[8,128,128]{2,1,0:T(8,128)(2,1)S(1)}, bf16[8,128,128]{2,1,0:T(8,128)(2,1)S(1)}, u32[]{:S(2)}, u32[]{:S(2)}) collective-permute-start(bf16[8,128,128]{2,1,0:T(8,128)(2,1)S(1)} %add_convert_fusion.2), channel_id=1, source_target_pairs={{0,8},{4,12},{8,0},{12,4},{16,24},{20,28},{24,16},{28,20},{1,9},{5... | collective-permute-start | bytes 786440 | tf_op jit(solution)/shard_map/ppermute | solution.py:360
  17.1 9.8 %collective-permute-start.4 = (bf16[8,128,128]{2,1,0:T(8,128)(2,1)S(1)}, bf16[8,128,128]{2,1,0:T(8,128)(2,1)S(1)}, u32[]{:S(2)}, u32[]{:S(2)}) collective-permute-start(bf16[8,128,128]{2,1,0:T(8,128)(2,1)S(1)} %copy-done.13), channel_id=1, source_target_pairs={{0,4},{4,0},{8,12},{12,8},{16,20},{20,16},{24,28},{28,24},{1,5},{5... | collective-permute-start | bytes 786440 | tf_op jit(solution)/shard_map/ppermute | solution.py:360
  24.2 14.3 %collective-permute-start.7 = (bf16[8,128,128]{2,1,0:T(8,128)(2,1)S(1)}, bf16[8,128,128]{2,1,0:T(8,128)(2,1)S(1)}, u32[]{:S(2)}, u32[]{:S(2)}) collective-permute-start(bf16[8,128,128]{2,1,0:T(8,128)(2,1)S(1)} %add_convert_fusion.1), channel_id=1, source_target_pairs={{0,16},{4,20},{8,24},{12,28},{16,0},{20,4},{24,8},{28,12},{1,17},{... | collective-permute-start | bytes 786440 | tf_op jit(solution)/shard_map/ppermute | solution.py:360
  27.7 11.2 %collective-permute-start.5 = (bf16[8,128,128]{2,1,0:T(8,128)(2,1)}, bf16[8,128,128]{2,1,0:T(8,128)(2,1)S(1)}, u32[]{:S(2)}, u32[]{:S(2)}) collective-permute-start(bf16[8,128,128]{2,1,0:T(8,128)(2,1)} %add_convert_fusion), channel_id=1, source_target_pairs={{0,8},{4,12},{8,0},{12,4},{16,24},{20,28},{24,16},{28,20},{1,9},{5... | collective-permute-start | bytes 786440 | tf_op jit(solution)/shard_map/ppermute | solution.py:360
  29.3 9.7 %collective-permute-start.6 = (bf16[8,128,128]{2,1,0:T(8,128)(2,1)}, bf16[8,128,128]{2,1,0:T(8,128)(2,1)}, u32[]{:S(2)}, u32[]{:S(2)}) collective-permute-start(bf16[8,128,128]{2,1,0:T(8,128)(2,1)} %get-tuple-element.83), channel_id=1, source_target_pairs={{0,4},{4,0},{8,12},{12,8},{16,20},{20,16},{24,28},{28,24},{1,5},{5... | collective-permute-start | bytes 786440 | tf_op jit(solution)/shard_map/ppermute | solution.py:360
  30.4 5.9 %collective-permute-start.8 = (bf16[2,2,128,128]{3,2,1,0:T(8,128)(2,1)}, bf16[2,2,128,128]{3,2,1,0:T(8,128)(2,1)S(1)}, u32[]{:S(2)}, u32[]{:S(2)}) collective-permute-start(bf16[2,2,128,128]{3,2,1,0:T(8,128)(2,1)} %get-tuple-element.85), channel_id=1, source_target_pairs={{0,2},{1,3},{2,0},{3,1},{4,6},{5,7},{6,4},{7,5},{8,10},{9,11},{10,... | collective-permute-start | bytes 393224 | tf_op jit(solution)/shard_map/ppermute | solution.py:360
  31.7 6.0 %collective-permute-start.9 = (bf16[2,2,128,128]{3,2,1,0:T(8,128)(2,1)}, bf16[2,2,128,128]{3,2,1,0:T(8,128)(2,1)S(1)}, u32[]{:S(2)}, u32[]{:S(2)}) collective-permute-start(bf16[2,2,128,128]{3,2,1,0:T(8,128)(2,1)} %get-tuple-element.86), channel_id=1, source_target_pairs={{0,3},{1,2},{2,1},{3,0},{4,7},{5,6},{6,5},{7,4},{8,11},{9,10},{10,... | collective-permute-start | bytes 393224 | tf_op jit(solution)/shard_map/ppermute | solution.py:360
  32.0 14.0 %copy-start.5 = (bf16[2,2,128,128]{3,2,1,0:T(8,128)(2,1)S(1)}, bf16[2,2,128,128]{3,2,1,0:T(8,128)(2,1)}, u32[]{:S(2)}) copy-start(bf16[2,2,128,128]{3,2,1,0:T(8,128)(2,1)} %get-tuple-element.99.refs_4_) | copy-start | bytes 393220
  36.4 3.6 %collective-permute-start.11 = (bf16[2,128,512]{2,1,0:T(8,128)(2,1)S(1)}, bf16[2,128,512]{2,1,0:T(8,128)(2,1)S(1)}, u32[]{:S(2)}, u32[]{:S(2)}) collective-permute-start(bf16[2,128,512]{2,1,0:T(8,128)(2,1)S(1)} %copy-done.4), channel_id=1, source_target_pairs={{0,1},{1,0},{2,3},{3,2},{4,5},{5,4},{6,7},{7,6},{8,9},{9,8},{10,11... | collective-permute-start | bytes 786440 | tf_op jit(solution)/shard_map/ppermute | solution.py:360
  37.7 2.3 %collective-permute-start.12 = (bf16[2,128,512]{2,1,0:T(8,128)(2,1)S(1)}, bf16[2,128,512]{2,1,0:T(8,128)(2,1)S(1)}, u32[]{:S(2)}, u32[]{:S(2)}) collective-permute-start(bf16[2,128,512]{2,1,0:T(8,128)(2,1)S(1)} %collective-permute-done.1.refs_2_), channel_id=1, source_target_pairs={{0,1},{1,0},{2,3},{3,2},{4,5},{5,4},{6,7},{7,6},{8,9},{9,8},{10,11... | collective-permute-start | bytes 786440 | tf_op jit(solution)/shard_map/ppermute | solution.py:360
  38.5 1.5 %collective-permute-start.10 = (bf16[2,2,128,128]{3,2,1,0:T(8,128)(2,1)S(1)}, bf16[2,2,128,128]{3,2,1,0:T(8,128)(2,1)S(1)}, u32[]{:S(2)}, u32[]{:S(2)}) collective-permute-start(bf16[2,2,128,128]{3,2,1,0:T(8,128)(2,1)S(1)} %copy-done.15), channel_id=1, source_target_pairs={{0,1},{1,0},{2,3},{3,2},{4,5},{5,4},{6,7},{7,6},{8,9},{9,8},{10,11... | collective-permute-start | bytes 393224 | tf_op jit(solution)/shard_map/ppermute | solution.py:360
  40.3 31.4 %copy-start.2 = (bf16[1024,128]{1,0:T(8,128)(2,1)S(1)}, bf16[1024,128]{1,0:T(8,128)(2,1)}, u32[]{:S(2)}) copy-start(bf16[1024,128]{1,0:T(8,128)(2,1)} %f_ref.1) | copy-start | bytes 786436
  40.3 31.4 %copy-start.3 = (bf16[128,512]{1,0:T(8,128)(2,1)S(1)}, bf16[128,512]{1,0:T(8,128)(2,1)}, u32[]{:S(2)}) copy-start(bf16[128,512]{1,0:T(8,128)(2,1)} %w_ref.1) | copy-start | bytes 393220
  40.3 2.1 %collective-permute-start.13 = (bf16[2,128,128]{2,1,0:T(8,128)(2,1)S(1)}, bf16[2,128,128]{2,1,0:T(8,128)(2,1)S(1)}, u32[]{:S(2)}, u32[]{:S(2)}) collective-permute-start(bf16[2,128,128]{2,1,0:T(8,128)(2,1)S(1)} %get-tuple-element.104), channel_id=1, source_target_pairs={{0,1},{1,0},{2,3},{3,2},{4,5},{5,4},{6,7},{7,6},{8,9},{9,8},{10,11... | collective-permute-start | bytes 196616 | tf_op jit(solution)/shard_map/ppermute | solution.py:360
  40.6 4.5 %collective-permute-start.14 = (bf16[2,128,128]{2,1,0:T(8,128)(2,1)S(1)}, bf16[2,128,128]{2,1,0:T(8,128)(2,1)S(1)}, u32[]{:S(2)}, u32[]{:S(2)}) collective-permute-start(bf16[2,128,128]{2,1,0:T(8,128)(2,1)S(1)} %get-tuple-element.105), channel_id=1, source_target_pairs={{0,2},{1,3},{2,0},{3,1},{4,6},{5,7},{6,4},{7,5},{8,10},{9,11},{10,... | collective-permute-start | bytes 196616 | tf_op jit(solution)/shard_map/ppermute | solution.py:360
  41.7 4.3 %collective-permute-start.15 = (bf16[2,128,128]{2,1,0:T(8,128)(2,1)S(1)}, bf16[2,128,128]{2,1,0:T(8,128)(2,1)S(1)}, u32[]{:S(2)}, u32[]{:S(2)}) collective-permute-start(bf16[2,128,128]{2,1,0:T(8,128)(2,1)S(1)} %get-tuple-element.106), channel_id=1, source_target_pairs={{0,3},{1,2},{2,1},{3,0},{4,7},{5,6},{6,5},{7,4},{8,11},{9,10},{10,... | collective-permute-start | bytes 196616 | tf_op jit(solution)/shard_map/ppermute | solution.py:360
  47.3 1.9 %collective-permute-start.16 = (bf16[256,128]{1,0:T(8,128)(2,1)S(1)}, bf16[256,128]{1,0:T(8,128)(2,1)S(1)}, u32[]{:S(2)}, u32[]{:S(2)}) collective-permute-start(bf16[256,128]{1,0:T(8,128)(2,1)S(1)} %get-tuple-element.108), channel_id=1, source_target_pairs={{0,1},{1,0},{2,3},{3,2},{4,5},{5,4},{6,7},{7,6},{8,9},{9,8},{10,11... | collective-permute-start | bytes 196616 | tf_op jit(solution)/shard_map/ppermute | solution.py:360
  47.4 4.8 %collective-permute-start.17 = (bf16[256,128]{1,0:T(8,128)(2,1)S(1)}, bf16[256,128]{1,0:T(8,128)(2,1)S(1)}, u32[]{:S(2)}, u32[]{:S(2)}) collective-permute-start(bf16[256,128]{1,0:T(8,128)(2,1)S(1)} %get-tuple-element.109), channel_id=1, source_target_pairs={{0,2},{1,3},{2,0},{3,1},{4,6},{5,7},{6,4},{7,5},{8,10},{9,11},{10,... | collective-permute-start | bytes 196616 | tf_op jit(solution)/shard_map/ppermute | solution.py:360
  48.5 4.3 %collective-permute-start.18 = (bf16[256,128]{1,0:T(8,128)(2,1)S(1)}, bf16[256,128]{1,0:T(8,128)(2,1)S(1)}, u32[]{:S(2)}, u32[]{:S(2)}) collective-permute-start(bf16[256,128]{1,0:T(8,128)(2,1)S(1)} %get-tuple-element.110), channel_id=1, source_target_pairs={{0,3},{1,2},{2,1},{3,0},{4,7},{5,6},{6,5},{7,4},{8,11},{9,10},{10,... | collective-permute-start | bytes 196616 | tf_op jit(solution)/shard_map/ppermute | solution.py:360
  52.8 17.1 %collective-permute-start.20 = (bf16[5,256,128]{2,1,0:T(8,128)(2,1)S(1)}, bf16[5,256,128]{2,1,0:T(8,128)(2,1)S(1)}, u32[]{:S(2)}, u32[]{:S(2)}) collective-permute-start(bf16[5,256,128]{2,1,0:T(8,128)(2,1)S(1)} %get-tuple-element.114), channel_id=1, source_target_pairs={{0,2},{1,3},{2,0},{3,1},{4,6},{5,7},{6,4},{7,5},{8,10},{9,11},{10,... | collective-permute-start | bytes 983048 | tf_op jit(solution)/shard_map/ppermute | solution.py:360
  53.9 16.1 %collective-permute-start.21 = (bf16[5,256,128]{2,1,0:T(8,128)(2,1)S(1)}, bf16[5,256,128]{2,1,0:T(8,128)(2,1)S(1)}, u32[]{:S(2)}, u32[]{:S(2)}) collective-permute-start(bf16[5,256,128]{2,1,0:T(8,128)(2,1)S(1)} %get-tuple-element.115), channel_id=1, source_target_pairs={{0,3},{1,2},{2,1},{3,0},{4,7},{5,6},{6,5},{7,4},{8,11},{9,10},{10,... | collective-permute-start | bytes 983048 | tf_op jit(solution)/shard_map/ppermute | solution.py:360
  54.5 15.4 %collective-permute-start.19 = (bf16[8,128,128]{2,1,0:T(8,128)(2,1)S(1)}, bf16[8,128,128]{2,1,0:T(8,128)(2,1)S(1)}, u32[]{:S(2)}, u32[]{:S(2)}) collective-permute-start(bf16[8,128,128]{2,1,0:T(8,128)(2,1)S(1)} %bitcast.24), channel_id=1, source_target_pairs={{0,16},{4,20},{8,24},{12,28},{16,0},{20,4},{24,8},{28,12},{1,17},{... | collective-permute-start | bytes 786440 | tf_op jit(solution)/shard_map/ppermute | solution.py:360
  56.8 13.2 %collective-permute-start.22 = (bf16[8,128,128]{2,1,0:T(8,128)(2,1)S(1)}, bf16[8,128,128]{2,1,0:T(8,128)(2,1)S(1)}, u32[]{:S(2)}, u32[]{:S(2)}) collective-permute-start(bf16[8,128,128]{2,1,0:T(8,128)(2,1)S(1)} %bitcast.25), channel_id=1, source_target_pairs={{0,8},{4,12},{8,0},{12,4},{16,24},{20,28},{24,16},{28,20},{1,9},{5... | collective-permute-start | bytes 786440 | tf_op jit(solution)/shard_map/ppermute | solution.py:360
  59.2 10.8 %collective-permute-start.23 = (bf16[8,128,128]{2,1,0:T(8,128)(2,1)S(1)}, bf16[8,128,128]{2,1,0:T(8,128)(2,1)S(1)}, u32[]{:S(2)}, u32[]{:S(2)}) collective-permute-start(bf16[8,128,128]{2,1,0:T(8,128)(2,1)S(1)} %bitcast.26), channel_id=1, source_target_pairs={{0,4},{4,0},{8,12},{12,8},{16,20},{20,16},{24,28},{28,24},{1,5},{5... | collective-permute-start | bytes 786440 | tf_op jit(solution)/shard_map/ppermute | solution.py:360
  70.0 1.7 %collective-permute-start.24 = (bf16[5,256,128]{2,1,0:T(8,128)(2,1)S(1)}, bf16[5,256,128]{2,1,0:T(8,128)(2,1)S(1)}, u32[]{:S(2)}, u32[]{:S(2)}) collective-permute-start(bf16[5,256,128]{2,1,0:T(8,128)(2,1)S(1)} %get-tuple-element.117.refs_0_), channel_id=1, source_target_pairs={{0,1},{1,0},{2,3},{3,2},{4,5},{5,4},{6,7},{7,6},{8,9},{9,8},{10,11... | collective-permute-start | bytes 983048 | tf_op jit(solution)/shard_map/ppermute | solution.py:360
  72.5 22.6 %copy-start = (bf16[1,6,8,128,128]{4,3,2,1,0:T(8,128)(2,1)S(1)}, bf16[1,6,8,128,128]{4,3,2,1,0:T(8,128)(2,1)}, u32[]{:S(2)}) copy-start(bf16[1,6,8,128,128]{4,3,2,1,0:T(8,128)(2,1)} %param.18) | copy-start | bytes 4718596
  72.5 22.6 %copy-start.1 = (bf16[1,16,128,128]{3,2,1,0:T(8,128)(2,1)S(1)}, bf16[1,16,128,128]{3,2,1,0:T(8,128)(2,1)}, u32[]{:S(2)}) copy-start(bf16[1,16,128,128]{3,2,1,0:T(8,128)(2,1)} %param.15) | copy-start | bytes 1572868
  72.5 22.6 %copy-start.6 = (s32[1,6,8]{2,0,1:T(1,128)S(1)}, s32[1,6,8]{2,0,1:T(1,128)}, u32[]{:S(2)}) copy-start(s32[1,6,8]{2,0,1:T(1,128)} %param.19) | copy-start | bytes 580
  72.5 22.5 %copy-start.7 = (s32[1,6,8]{2,0,1:T(1,128)S(1)}, s32[1,6,8]{2,0,1:T(1,128)}, u32[]{:S(2)}) copy-start(s32[1,6,8]{2,0,1:T(1,128)} %param.20) | copy-start | bytes 580
  72.5 22.5 %copy-start.8 = (s32[1,16]{1,0:T(1,128)S(1)}, s32[1,16]{1,0:T(1,128)}, u32[]{:S(2)}) copy-start(s32[1,16]{1,0:T(1,128)} %refs_0_.7) | copy-start | bytes 196
  72.5 22.5 %copy-start.9 = (s32[1,16]{1,0:T(1,128)S(1)}, s32[1,16]{1,0:T(1,128)}, u32[]{:S(2)}) copy-start(s32[1,16]{1,0:T(1,128)} %refs_1_.7) | copy-start | bytes 196
  72.5 5.6 %collective-permute-start.25 = (bf16[4,32,512]{2,1,0:T(8,128)(2,1)S(1)}, bf16[4,32,512]{2,1,0:T(8,128)(2,1)S(1)}, u32[]{:S(2)}, u32[]{:S(2)}) collective-permute-start(bf16[4,32,512]{2,1,0:T(8,128)(2,1)S(1)} %get-tuple-element.121), channel_id=1, source_target_pairs={{0,4},{4,0},{8,12},{12,8},{16,20},{20,16},{24,28},{28,24},{1,5},{5... | collective-permute-start | bytes 393224 | tf_op jit(solution)/shard_map/ppermute | solution.py:360
  78.2 6.5 %collective-permute-start.26 = (bf16[4,32,512]{2,1,0:T(8,128)(2,1)S(1)}, bf16[4,32,512]{2,1,0:T(8,128)(2,1)S(1)}, u32[]{:S(2)}, u32[]{:S(2)}) collective-permute-start(bf16[4,32,512]{2,1,0:T(8,128)(2,1)S(1)} %add_convert_fusion.5), channel_id=1, source_target_pairs={{0,8},{4,12},{8,0},{12,4},{16,24},{20,28},{24,16},{28,20},{1,9},{5... | collective-permute-start | bytes 393224 | tf_op jit(solution)/shard_map/ppermute | solution.py:360
  79.5 11.4 %collective-permute-start.29 = (bf16[8,128,128]{2,1,0:T(8,128)(2,1)S(1)}, bf16[8,128,128]{2,1,0:T(8,128)(2,1)S(1)}, u32[]{:S(2)}, u32[]{:S(2)}) collective-permute-start(bf16[8,128,128]{2,1,0:T(8,128)(2,1)S(1)} %collective-permute-done.19.refs_6_), channel_id=1, source_target_pairs={{0,8},{4,12},{8,0},{12,4},{16,24},{20,28},{24,16},{28,20},{1,9},{5... | collective-permute-start | bytes 786440 | tf_op jit(solution)/shard_map/ppermute | solution.py:360
  80.3 10.6 %collective-permute-start.30 = (bf16[8,128,128]{2,1,0:T(8,128)(2,1)S(1)}, bf16[8,128,128]{2,1,0:T(8,128)(2,1)S(1)}, u32[]{:S(2)}, u32[]{:S(2)}) collective-permute-start(bf16[8,128,128]{2,1,0:T(8,128)(2,1)S(1)} %collective-permute-done.19.refs_6_), channel_id=1, source_target_pairs={{0,4},{4,0},{8,12},{12,8},{16,20},{20,16},{24,28},{28,24},{1,5},{5... | collective-permute-start | bytes 786440 | tf_op jit(solution)/shard_map/ppermute | solution.py:360
  84.7 7.3 %collective-permute-start.27 = (bf16[4,32,512]{2,1,0:T(8,128)(2,1)S(1)}, bf16[4,32,512]{2,1,0:T(8,128)(2,1)S(1)}, u32[]{:S(2)}, u32[]{:S(2)}) collective-permute-start(bf16[4,32,512]{2,1,0:T(8,128)(2,1)S(1)} %add_convert_fusion.4), channel_id=1, source_target_pairs={{0,16},{4,20},{8,24},{12,28},{16,0},{20,4},{24,8},{28,12},{1,17},{... | collective-permute-start | bytes 393224 | tf_op jit(solution)/shard_map/ppermute | solution.py:360
  86.8 6.8 %collective-permute-start.28 = (bf16[8,128,128]{2,1,0:T(8,128)(2,1)S(1)}, bf16[8,128,128]{2,1,0:T(8,128)(2,1)S(1)}, u32[]{:S(2)}, u32[]{:S(2)}) collective-permute-start(bf16[8,128,128]{2,1,0:T(8,128)(2,1)S(1)} %collective-permute-done.22.refs_8_), channel_id=1, source_target_pairs={{0,4},{4,0},{8,12},{12,8},{16,20},{20,16},{24,28},{28,24},{1,5},{5... | collective-permute-start | bytes 786440 | tf_op jit(solution)/shard_map/ppermute | solution.py:360
  90.9 6.4 %collective-permute-start.31 = (bf16[8,128,128]{2,1,0:T(8,128)(2,1)S(1)}, bf16[8,128,128]{2,1,0:T(8,128)(2,1)S(1)}, u32[]{:S(2)}, u32[]{:S(2)}) collective-permute-start(bf16[8,128,128]{2,1,0:T(8,128)(2,1)S(1)} %collective-permute-done.30.refs_7_), channel_id=1, source_target_pairs={{0,8},{4,12},{8,0},{12,4},{16,24},{20,28},{24,16},{28,20},{1,9},{5... | collective-permute-start | bytes 786440 | tf_op jit(solution)/shard_map/ppermute | solution.py:360
  93.6 6.3 %collective-permute-start.32 = (bf16[4,32,512]{2,1,0:T(8,128)(2,1)S(1)}, bf16[4,32,512]{2,1,0:T(8,128)(2,1)S(1)}, u32[]{:S(2)}, u32[]{:S(2)}) collective-permute-start(bf16[4,32,512]{2,1,0:T(8,128)(2,1)S(1)} %add_convert_fusion.3.mine_ref), channel_id=1, source_target_pairs={{0,4},{4,0},{8,12},{12,8},{16,20},{20,16},{24,28},{28,24},{1,5},{5... | collective-permute-start | bytes 393224 | tf_op jit(solution)/shard_map/ppermute | solution.py:360

commit v15 on v14

--- a/solution.py
+++ b/solution.py
@@ -470,10 +470,11 @@
     come = [crossed(sent[0], 1, "feat"), come_2, come_3]
     (out,) = small_call(place_kernel, [like((feats, some, width), BF16)], [own_out, *come])
     dpre = [sent[0], *come]
+    found[5] = crossed(found[4], near)
     found[6] = crossed(found[4], 2)
     found[3] = crossed(found[2], near)
-    found[5] = crossed(found[4], near)
-    found[7] = crossed(tied(found[5], found[6]), 2)
+    found[5], found[6] = lax.optimization_barrier((found[5], found[6]))
+    found[7] = crossed(found[5], 2)
     piece = 2 * width // parts_total
     dx_self, give, keep = small_call(
         functools.partial(grad_kernel, feats),

time: 101 us -> 102 us (level)
  transfers between devices with their start and end apart: 33 -> 33, of which waited for: 18 -> 18; matrix products, arithmetic and copies ran while one was open for 5% -> 4% of each run, Pallas kernels for 10% -> 10%
where the time goes in v15:
time: 102 us
  waiting for transfers between devices  42.2 us (41%)
  starting transfers between devices  36.6 us (36%)
  Pallas kernels  17.2 us (17%)
  other arithmetic  4.15 us (4%)
    ppermute x33, waiting for transfers between devices, crossed(): lax.ppermute(x, axis, [(i, i ^ mask) for i in range(lax.axis_size(axis))])  42.2 us
    ppermute x33, starting transfers between devices, crossed(): lax.ppermute(x, axis, [(i, i ^ mask) for i in range(lax.axis_size(axis))])  36.6 us
    pallas_call x4, Pallas kernels, tiles_call(): pl.pallas_call(functools.partial(tiles_kernel, masks, offsets, parts_tota...  13.3 us
    pallas_call x5, Pallas kernels, small_call(): pl.pallas_call(kernel, out_shape=outs, in_specs=[VMEM] * len(arrays), out...  3.86 us
  transfers between devices with their start and end apart: 33, of which 18 were waited for; matrix products, arithmetic and copies ran while one was open for 4% of the time, Pallas kernels for 10%

profile of v15, /device:TPU:0, one launch (start us, length us, event | category | flops | bytes accessed | tf_op | source)
XLA Modules:
  0.0 101.5 jit_solution(14930192769986199969)
XLA Ops:
  0.6 3.7 %shard_map.139 = (bf16[8,128,128]{2,1,0:T(8,128)(2,1)}, bf16[8,128,128]{2,1,0:T(8,128)(2,1)}, bf16[8,128,128]{2,1,0:T(8,128)(2,1)}, bf16[8,128,128]{2,1,0:T(8,128)(2,1)}) custom-call(s32[1,16]{1,0:T(1,128)} %refs_0_.7, s32[1,16]{1,0:T(1,128)} %refs_1_.7, s32[6,1,8]{2,1,0:T(1,128)} %bitcast.30, s32[6,1,8]{2,1,0:T(1,128)} %bitcast.34, ...), custom_call_target="tpu_custom_call" | custom-call | flops 1 | bytes 1 | tf_op jit(solution)/shard_map/pallas_call | solution.py:224
  4.4 3.0 %collective-permute-start.2 = (bf16[8,128,128]{2,1,0:T(8,128)(2,1)}, bf16[8,128,128]{2,1,0:T(8,128)(2,1)S(1)}, u32[]{:S(2)}, u32[]{:S(2)}) collective-permute-start(bf16[8,128,128]{2,1,0:T(8,128)(2,1)} %get-tuple-element.81), channel_id=1, source_target_pairs={{0,4},{4,0},{8,12},{12,8},{16,20},{20,16},{24,28},{28,24},{1,5},{5... | collective-permute-start | bytes 786440 | tf_op jit(solution)/shard_map/ppermute | solution.py:360
  7.4 4.8 %shard_map.138 = (f32[8,128,128]{2,1,0:T(8,128)}, f32[8,128,128]{2,1,0:T(8,128)}, f32[8,128,128]{2,1,0:T(8,128)}, f32[8,128,128]{2,1,0:T(8,128)}, bf16[2,2,128,1...) custom-call(s32[1,16]{1,0:T(1,128)} %refs_0_.7, ...), custom_call_target="tpu_custom_call" | custom-call | flops 1 | bytes 1 | tf_op jit(solution)/shard_map/pallas_call | solution.py:224
  12.3 1.6 %collective-permute-start.1 = (bf16[2,128,512]{2,1,0:T(8,128)(2,1)}, bf16[2,128,512]{2,1,0:T(8,128)(2,1)S(1)}, u32[]{:S(2)}, u32[]{:S(2)}) collective-permute-start(bf16[2,128,512]{2,1,0:T(8,128)(2,1)} %get-tuple-element.96.refs_0_), channel_id=1, source_target_pairs={{0,2},{1,3},{2,0},{3,1},{4,6},{5,7},{6,4},{7,5},{8,10},{9,11},{10,... | collective-permute-start | bytes 786440 | tf_op jit(solution)/shard_map/ppermute | solution.py:360
  13.8 0.5 collective-permute-start
  14.3 1.1 %add_convert_fusion.2 = bf16[8,128,128]{2,1,0:T(8,128)(2,1)S(1)} fusion(f32[8,128,128]{2,1,0:T(8,128)} %get-tuple-element.80, bf16[8,128,128]{2,1,0:T(8,128)(2,1)S(1)} %collective-permute-done.2), kind=kLoop, calls=%fused_computation.3 | loop fusion | flops 393216 | bytes 1048576 | tf_op jit(solution)/shard_map/convert_element_type | solution.py:429
  15.5 1.6 %collective-permute-start.3 = (bf16[8,128,128]{2,1,0:T(8,128)(2,1)S(1)}, bf16[8,128,128]{2,1,0:T(8,128)(2,1)S(1)}, u32[]{:S(2)}, u32[]{:S(2)}) collective-permute-start(bf16[8,128,128]{2,1,0:T(8,128)(2,1)S(1)} %add_convert_fusion.2), channel_id=1, source_target_pairs={{0,8},{4,12},{8,0},{12,4},{16,24},{20,28},{24,16},{28,20},{1,9},{5... | collective-permute-start | bytes 786440 | tf_op jit(solution)/shard_map/ppermute | solution.py:360
  17.1 1.5 %collective-permute-start.4 = (bf16[8,128,128]{2,1,0:T(8,128)(2,1)S(1)}, bf16[8,128,128]{2,1,0:T(8,128)(2,1)S(1)}, u32[]{:S(2)}, u32[]{:S(2)}) collective-permute-start(bf16[8,128,128]{2,1,0:T(8,128)(2,1)S(1)} %copy-done.13), channel_id=1, source_target_pairs={{0,4},{4,0},{8,12},{12,8},{16,20},{20,16},{24,28},{28,24},{1,5},{5... | collective-permute-start | bytes 786440 | tf_op jit(solution)/shard_map/ppermute | solution.py:360
  18.7 1.7 %collective-permute-done.1.refs_2_ = bf16[2,128,512]{2,1,0:T(8,128)(2,1)S(1)} collective-permute-done((bf16[2,128,512]{2,1,0:T(8,128)(2,1)}, bf16[2,128,512]{2,1,0:T(8,128)(2,1)S(1)}, u32[]{:S(2)}, u32[]{:S(2)}) %collective-permute-start.1) | collective-permute-done | bytes 262176 | tf_op jit(solution)/shard_map/ppermute | solution.py:360
  20.3 2.8 %collective-permute-done = bf16[8,128,128]{2,1,0:T(8,128)(2,1)S(1)} collective-permute-done((bf16[8,128,128]{2,1,0:T(8,128)(2,1)S(1)}, bf16[8,128,128]{2,1,0:T(8,128)(2,1)S(1)}, u32[]{:S(2)}, u32[]{:S(2)}) %collective-permute-start) | collective-permute-done | bytes 262176 | tf_op jit(solution)/shard_map/ppermute | solution.py:360
  23.1 1.1 %add_convert_fusion.1 = bf16[8,128,128]{2,1,0:T(8,128)(2,1)S(1)} fusion(bf16[8,128,128]{2,1,0:T(8,128)(2,1)S(1)} %collective-permute-done.3, f32[8,128,128]{2,1,0:T(8,128)} %get-tuple-element.76, bf16[8,128,128]{2,1,0:T(8,128)(2,1)S(1)} %collective-permute-done), kind=kLoop, calls=%fused_computation.2 | loop fusion | flops 655360 | bytes 1310720 | tf_op jit(solution)/shard_map/convert_element_type | solution.py:431
  24.2 2.6 %collective-permute-start.7 = (bf16[8,128,128]{2,1,0:T(8,128)(2,1)S(1)}, bf16[8,128,128]{2,1,0:T(8,128)(2,1)S(1)}, u32[]{:S(2)}, u32[]{:S(2)}) collective-permute-start(bf16[8,128,128]{2,1,0:T(8,128)(2,1)S(1)} %add_convert_fusion.1), channel_id=1, source_target_pairs={{0,16},{4,20},{8,24},{12,28},{16,0},{20,4},{24,8},{28,12},{1,17},{... | collective-permute-start | bytes 786440 | tf_op jit(solution)/shard_map/ppermute | solution.py:360
  26.9 0.1 collective-permute-done.4
  26.9 0.8 add_convert_fusion
  27.7 1.6 %collective-permute-start.5 = (bf16[8,128,128]{2,1,0:T(8,128)(2,1)}, bf16[8,128,128]{2,1,0:T(8,128)(2,1)S(1)}, u32[]{:S(2)}, u32[]{:S(2)}) collective-permute-start(bf16[8,128,128]{2,1,0:T(8,128)(2,1)} %add_convert_fusion), channel_id=1, source_target_pairs={{0,8},{4,12},{8,0},{12,4},{16,24},{20,28},{24,16},{28,20},{1,9},{5... | collective-permute-start | bytes 786440 | tf_op jit(solution)/shard_map/ppermute | solution.py:360
  29.3 1.1 %collective-permute-start.6 = (bf16[8,128,128]{2,1,0:T(8,128)(2,1)}, bf16[8,128,128]{2,1,0:T(8,128)(2,1)}, u32[]{:S(2)}, u32[]{:S(2)}) collective-permute-start(bf16[8,128,128]{2,1,0:T(8,128)(2,1)} %get-tuple-element.84), channel_id=1, source_target_pairs={{0,4},{4,0},{8,12},{12,8},{16,20},{20,16},{24,28},{28,24},{1,5},{5... | collective-permute-start | bytes 786440 | tf_op jit(solution)/shard_map/ppermute | solution.py:360
  30.4 1.3 %collective-permute-start.8 = (bf16[2,2,128,128]{3,2,1,0:T(8,128)(2,1)}, bf16[2,2,128,128]{3,2,1,0:T(8,128)(2,1)S(1)}, u32[]{:S(2)}, u32[]{:S(2)}) collective-permute-start(bf16[2,2,128,128]{3,2,1,0:T(8,128)(2,1)} %get-tuple-element.86), channel_id=1, source_target_pairs={{0,2},{1,3},{2,0},{3,1},{4,6},{5,7},{6,4},{7,5},{8,10},{9,11},{10,... | collective-permute-start | bytes 393224 | tf_op jit(solution)/shard_map/ppermute | solution.py:360
  31.7 0.2 copy.15.inv_ref
  32.0 4.4 %collective-permute-done.8.refs_6_ = bf16[2,2,128,128]{3,2,1,0:T(8,128)(2,1)S(1)} collective-permute-done((bf16[2,2,128,128]{3,2,1,0:T(8,128)(2,1)}, bf16[2,2,128,128]{3,2,1,0:T(8,128)(2,1)S(1)}, u32[]{:S(2)}, u32[]{:S(2)}) %collective-permute-start.8) | collective-permute-done | bytes 131104 | tf_op jit(solution)/shard_map/ppermute | solution.py:360
  36.3 1.3 %collective-permute-done.9.refs_7_ = bf16[2,2,128,128]{3,2,1,0:T(8,128)(2,1)S(1)} collective-permute-done((bf16[2,2,128,128]{3,2,1,0:T(8,128)(2,1)}, bf16[2,2,128,128]{3,2,1,0:T(8,128)(2,1)S(1)}, u32[]{:S(2)}, u32[]{:S(2)}) %collective-permute-start.9) | collective-permute-done | bytes 131104 | tf_op jit(solution)/shard_map/ppermute | solution.py:360
  37.7 0.9 collective-permute-start.12
  38.5 0.1 collective-permute-start.10
  38.6 0.4 collective-permute-done.5
  39.0 1.0 %convert_add_fusion.keep_ref = f32[8,128,128]{2,1,0:T(8,128)S(1)} fusion(bf16[8,128,128]{2,1,0:T(8,128)(2,1)} %collective-permute-done.6, f32[8,128,128]{2,1,0:T(8,128)S(1)} %copy-done.10, bf16[8,128,128]{2,1,0:T(8,128)(2,1)S(1)} %collective-permute-done.5), kind=kLoop, calls=%fused_computation | loop fusion | flops 524288 | bytes 1572864 | tf_op jit(solution)/shard_map/add | solution.py:442
  40.0 0.2 shard_map.140
  40.3 0.3 collective-permute-start.13
  40.6 1.1 %collective-permute-start.14 = (bf16[2,128,128]{2,1,0:T(8,128)(2,1)S(1)}, bf16[2,128,128]{2,1,0:T(8,128)(2,1)S(1)}, u32[]{:S(2)}, u32[]{:S(2)}) collective-permute-start(bf16[2,128,128]{2,1,0:T(8,128)(2,1)S(1)} %get-tuple-element.106), channel_id=1, source_target_pairs={{0,2},{1,3},{2,0},{3,1},{4,6},{5,7},{6,4},{7,5},{8,10},{9,11},{10,... | collective-permute-start | bytes 196616 | tf_op jit(solution)/shard_map/ppermute | solution.py:360
  41.7 0.5 collective-permute-start.15
  42.2 0.1 dynamic_slice.3
  42.3 0.1 copy.16.inv_ref
  42.4 2.7 %collective-permute-done.14.refs_10_ = bf16[2,128,128]{2,1,0:T(8,128)(2,1)S(1)} collective-permute-done((bf16[2,128,128]{2,1,0:T(8,128)(2,1)S(1)}, bf16[2,128,128]{2,1,0:T(8,128)(2,1)S(1)}, u32[]{:S(2)}, u32[]{:S(2)}) %collective-permute-start.14) | collective-permute-done | bytes 65568 | tf_op jit(solution)/shard_map/ppermute | solution.py:360
  45.1 0.9 collective-permute-done.15.refs_11_
  46.0 1.3 %shard_map.141 = (bf16[5,256,128]{2,1,0:T(8,128)(2,1)S(1)}, bf16[5,256,128]{2,1,0:T(8,128)(2,1)S(1)}, bf16[5,256,128]{2,1,0:T(8,128)(2,1)S(1)}, bf16[256,128]{1,...) custom-call(f32[256,1]{1,0:T(8,128)S(1)} %copy.16.inv_ref, ...), custom_call_target="tpu_custom_call" | custom-call | flops 1 | bytes 1 | tf_op jit(solution)/shard_map/pallas_call | solution.py:244
  47.3 0.2 collective-permute-start.16
  47.5 1.1 %collective-permute-start.17 = (bf16[256,128]{1,0:T(8,128)(2,1)S(1)}, bf16[256,128]{1,0:T(8,128)(2,1)S(1)}, u32[]{:S(2)}, u32[]{:S(2)}) collective-permute-start(bf16[256,128]{1,0:T(8,128)(2,1)S(1)} %get-tuple-element.110), channel_id=1, source_target_pairs={{0,2},{1,3},{2,0},{3,1},{4,6},{5,7},{6,4},{7,5},{8,10},{9,11},{10,... | collective-permute-start | bytes 196616 | tf_op jit(solution)/shard_map/ppermute | solution.py:360
  48.5 0.7 collective-permute-start.18
  49.2 3.1 %collective-permute-done.17 = bf16[256,128]{1,0:T(8,128)(2,1)S(1)} collective-permute-done((bf16[256,128]{1,0:T(8,128)(2,1)S(1)}, bf16[256,128]{1,0:T(8,128)(2,1)S(1)}, u32[]{:S(2)}, u32[]{:S(2)}) %collective-permute-start.17) | collective-permute-done | bytes 65568 | tf_op jit(solution)/shard_map/ppermute | solution.py:360
  52.3 0.6 collective-permute-done.18
  52.9 1.1 %collective-permute-start.20 = (bf16[5,256,128]{2,1,0:T(8,128)(2,1)S(1)}, bf16[5,256,128]{2,1,0:T(8,128)(2,1)S(1)}, u32[]{:S(2)}, u32[]{:S(2)}) collective-permute-start(bf16[5,256,128]{2,1,0:T(8,128)(2,1)S(1)} %get-tuple-element.115), channel_id=1, source_target_pairs={{0,2},{1,3},{2,0},{3,1},{4,6},{5,7},{6,4},{7,5},{8,10},{9,11},{10,... | collective-permute-start | bytes 983048 | tf_op jit(solution)/shard_map/ppermute | solution.py:360
  53.9 0.6 collective-permute-start.21
  54.5 2.3 %collective-permute-start.19 = (bf16[8,128,128]{2,1,0:T(8,128)(2,1)S(1)}, bf16[8,128,128]{2,1,0:T(8,128)(2,1)S(1)}, u32[]{:S(2)}, u32[]{:S(2)}) collective-permute-start(bf16[8,128,128]{2,1,0:T(8,128)(2,1)S(1)} %bitcast.24), channel_id=1, source_target_pairs={{0,16},{4,20},{8,24},{12,28},{16,0},{20,4},{24,8},{28,12},{1,17},{... | collective-permute-start | bytes 786440 | tf_op jit(solution)/shard_map/ppermute | solution.py:360
  56.8 2.4 %collective-permute-start.22 = (bf16[8,128,128]{2,1,0:T(8,128)(2,1)S(1)}, bf16[8,128,128]{2,1,0:T(8,128)(2,1)S(1)}, u32[]{:S(2)}, u32[]{:S(2)}) collective-permute-start(bf16[8,128,128]{2,1,0:T(8,128)(2,1)S(1)} %bitcast.25), channel_id=1, source_target_pairs={{0,8},{4,12},{8,0},{12,4},{16,24},{20,28},{24,16},{28,20},{1,9},{5... | collective-permute-start | bytes 786440 | tf_op jit(solution)/shard_map/ppermute | solution.py:360
  59.2 1.3 %collective-permute-start.23 = (bf16[8,128,128]{2,1,0:T(8,128)(2,1)S(1)}, bf16[8,128,128]{2,1,0:T(8,128)(2,1)S(1)}, u32[]{:S(2)}, u32[]{:S(2)}) collective-permute-start(bf16[8,128,128]{2,1,0:T(8,128)(2,1)S(1)} %bitcast.26), channel_id=1, source_target_pairs={{0,4},{4,0},{8,12},{12,8},{16,20},{20,16},{24,28},{28,24},{1,5},{5... | collective-permute-start | bytes 786440 | tf_op jit(solution)/shard_map/ppermute | solution.py:360
  60.4 9.5 %collective-permute-done.19.refs_6_ = bf16[8,128,128]{2,1,0:T(8,128)(2,1)S(1)} collective-permute-done((bf16[8,128,128]{2,1,0:T(8,128)(2,1)S(1)}, bf16[8,128,128]{2,1,0:T(8,128)(2,1)S(1)}, u32[]{:S(2)}, u32[]{:S(2)}) %collective-permute-start.19) | collective-permute-done | bytes 262176 | tf_op jit(solution)/shard_map/ppermute | solution.py:360
  69.9 0.1 collective-permute-done.22.refs_8_
  70.0 0.1 collective-permute-start.24
  70.1 1.6 %collective-permute-done.24.refs_1_ = bf16[5,256,128]{2,1,0:T(8,128)(2,1)S(1)} collective-permute-done((bf16[5,256,128]{2,1,0:T(8,128)(2,1)S(1)}, bf16[5,256,128]{2,1,0:T(8,128)(2,1)S(1)}, u32[]{:S(2)}, u32[]{:S(2)}) %collective-permute-start.24) | collective-permute-done | bytes 327712 | tf_op jit(solution)/shard_map/ppermute | solution.py:360
  71.7 0.8 shard_map.142
  72.5 1.1 %collective-permute-start.25 = (bf16[4,32,512]{2,1,0:T(8,128)(2,1)S(1)}, bf16[4,32,512]{2,1,0:T(8,128)(2,1)S(1)}, u32[]{:S(2)}, u32[]{:S(2)}) collective-permute-start(bf16[4,32,512]{2,1,0:T(8,128)(2,1)S(1)} %get-tuple-element.122), channel_id=1, source_target_pairs={{0,4},{4,0},{8,12},{12,8},{16,20},{20,16},{24,28},{28,24},{1,5},{5... | collective-permute-start | bytes 393224 | tf_op jit(solution)/shard_map/ppermute | solution.py:360
  73.6 4.5 %collective-permute-done.25 = bf16[4,32,512]{2,1,0:T(8,128)(2,1)S(1)} collective-permute-done((bf16[4,32,512]{2,1,0:T(8,128)(2,1)S(1)}, bf16[4,32,512]{2,1,0:T(8,128)(2,1)S(1)}, u32[]{:S(2)}, u32[]{:S(2)}) %collective-permute-start.25) | collective-permute-done | bytes 131104 | tf_op jit(solution)/shard_map/ppermute | solution.py:360
  78.2 1.3 %collective-permute-start.26 = (bf16[4,32,512]{2,1,0:T(8,128)(2,1)S(1)}, bf16[4,32,512]{2,1,0:T(8,128)(2,1)S(1)}, u32[]{:S(2)}, u32[]{:S(2)}) collective-permute-start(bf16[4,32,512]{2,1,0:T(8,128)(2,1)S(1)} %add_convert_fusion.5), channel_id=1, source_target_pairs={{0,8},{4,12},{8,0},{12,4},{16,24},{20,28},{24,16},{28,20},{1,9},{5... | collective-permute-start | bytes 393224 | tf_op jit(solution)/shard_map/ppermute | solution.py:360
  79.5 1.4 %collective-permute-start.29 = (bf16[8,128,128]{2,1,0:T(8,128)(2,1)S(1)}, bf16[8,128,128]{2,1,0:T(8,128)(2,1)S(1)}, u32[]{:S(2)}, u32[]{:S(2)}) collective-permute-start(bf16[8,128,128]{2,1,0:T(8,128)(2,1)S(1)} %collective-permute-done.19.refs_6_), channel_id=1, source_target_pairs={{0,4},{4,0},{8,12},{12,8},{16,20},{20,16},{24,28},{28,24},{1,5},{5... | collective-permute-start | bytes 786440 | tf_op jit(solution)/shard_map/ppermute | solution.py:360
  80.9 0.4 collective-permute-start.30
  81.3 3.0 %collective-permute-done.26 = bf16[4,32,512]{2,1,0:T(8,128)(2,1)S(1)} collective-permute-done((bf16[4,32,512]{2,1,0:T(8,128)(2,1)S(1)}, bf16[4,32,512]{2,1,0:T(8,128)(2,1)S(1)}, u32[]{:S(2)}, u32[]{:S(2)}) %collective-permute-start.26) | collective-permute-done | bytes 131104 | tf_op jit(solution)/shard_map/ppermute | solution.py:360
  84.3 2.0 %collective-permute-start.27 = (bf16[4,32,512]{2,1,0:T(8,128)(2,1)S(1)}, bf16[4,32,512]{2,1,0:T(8,128)(2,1)S(1)}, u32[]{:S(2)}, u32[]{:S(2)}) collective-permute-start(bf16[4,32,512]{2,1,0:T(8,128)(2,1)S(1)} %add_convert_fusion.4), channel_id=1, source_target_pairs={{0,16},{4,20},{8,24},{12,28},{16,0},{20,4},{24,8},{28,12},{1,17},{... | collective-permute-start | bytes 393224 | tf_op jit(solution)/shard_map/ppermute | solution.py:360
  86.4 1.4 %collective-permute-start.28 = (bf16[8,128,128]{2,1,0:T(8,128)(2,1)S(1)}, bf16[8,128,128]{2,1,0:T(8,128)(2,1)S(1)}, u32[]{:S(2)}, u32[]{:S(2)}) collective-permute-start(bf16[8,128,128]{2,1,0:T(8,128)(2,1)S(1)} %collective-permute-done.22.refs_8_), channel_id=1, source_target_pairs={{0,4},{4,0},{8,12},{12,8},{16,20},{20,16},{24,28},{28,24},{1,5},{5... | collective-permute-start | bytes 786440 | tf_op jit(solution)/shard_map/ppermute | solution.py:360
  87.8 3.9 %collective-permute-done.30.refs_8_ = bf16[8,128,128]{2,1,0:T(8,128)(2,1)S(1)} collective-permute-done((bf16[8,128,128]{2,1,0:T(8,128)(2,1)S(1)}, bf16[8,128,128]{2,1,0:T(8,128)(2,1)S(1)}, u32[]{:S(2)}, u32[]{:S(2)}) %collective-permute-start.30) | collective-permute-done | bytes 262176 | tf_op jit(solution)/shard_map/ppermute | solution.py:360
  91.6 0.7 shard_map.143
  92.4 0.5 collective-permute-done.28.refs_9_
  92.9 1.6 %collective-permute-start.32 = (bf16[4,32,512]{2,1,0:T(8,128)(2,1)S(1)}, bf16[4,32,512]{2,1,0:T(8,128)(2,1)S(1)}, u32[]{:S(2)}, u32[]{:S(2)}) collective-permute-start(bf16[4,32,512]{2,1,0:T(8,128)(2,1)S(1)} %add_convert_fusion.3.mine_ref), channel_id=1, source_target_pairs={{0,4},{4,0},{8,12},{12,8},{16,20},{20,16},{24,28},{28,24},{1,5},{5... | collective-permute-start | bytes 393224 | tf_op jit(solution)/shard_map/ppermute | solution.py:360
  94.6 2.1 %shard_map.144.refs_10_ = f32[8,128,128]{2,1,0:T(8,128)S(1)} custom-call(s32[1,16]{1,0:T(1,128)S(1)} %copy-done.8, s32[1,16]{1,0:T(1,128)S(1)} %copy-done.9, s32[6,1,8]{2,1,0:T(1,128)S(1)} %bitcast.32, s32[6,1,8]{2,1,0:T(1,128)S(1)} %bitcast.36, bf16[16,128,128]{2,1,0:T(8,128)(2,1)S(1)} %bitcast.20, bf16[6,8,128,128]{3,2,1,0:T(8,128)(2,1)S(1)} %bitcast.16, ...), custom_call_target="tpu_custom_call" | custom-call | flops 1 | bytes 1 | tf_op jit(solution)/shard_map/pallas_call | solution.py:224
  96.7 1.3 %collective-permute-done.31.refs_9_ = bf16[8,128,128]{2,1,0:T(8,128)(2,1)S(1)} collective-permute-done((bf16[8,128,128]{2,1,0:T(8,128)(2,1)S(1)}, bf16[8,128,128]{2,1,0:T(8,128)(2,1)S(1)}, u32[]{:S(2)}, u32[]{:S(2)}) %collective-permute-start.31) | collective-permute-done | bytes 262176 | tf_op jit(solution)/shard_map/ppermute | solution.py:360
  98.0 2.6 %shard_map.145 = f32[8,128,128]{2,1,0:T(8,128)} custom-call(s32[1,16]{1,0:T(1,128)S(1)} %copy-done.8, s32[1,16]{1,0:T(1,128)S(1)} %copy-done.9, s32[6,1,8]{2,1,0:T(1,128)S(1)} %bitcast.33, s32[6,1,8]{2,1,0:T(1,128)S(1)} %bitcast.37, bf16[16,128,128]{2,1,0:T(8,128)(2,1)S(1)} %bitcast.21, bf16[6,8,128,128]{3,2,1,0:T(8,128)(2,1)S(1)} %bitcast.17, ...), custom_call_target="tpu_custom_call" | custom-call | flops 1 | bytes 1 | tf_op jit(solution)/shard_map/pallas_call | solution.py:224
  100.7 0.9 shard_map.146
  (55 shorter events, 0.3 us)
Async XLA Ops:
  4.4 9.5 %copy-start.14 = (bf16[8,128,128]{2,1,0:T(8,128)(2,1)S(1)}, bf16[8,128,128]{2,1,0:T(8,128)(2,1)}, u32[]{:S(2)}) copy-start(bf16[8,128,128]{2,1,0:T(8,128)(2,1)} %get-tuple-element.77) | copy-start | bytes 786436
  4.4 10.0 %collective-permute-start.2 = (bf16[8,128,128]{2,1,0:T(8,128)(2,1)}, bf16[8,128,128]{2,1,0:T(8,128)(2,1)S(1)}, u32[]{:S(2)}, u32[]{:S(2)}) collective-permute-start(bf16[8,128,128]{2,1,0:T(8,128)(2,1)} %get-tuple-element.81), channel_id=1, source_target_pairs={{0,4},{4,0},{8,12},{12,8},{16,20},{20,16},{24,28},{28,24},{1,5},{5... | collective-permute-start | bytes 786440 | tf_op jit(solution)/shard_map/ppermute | solution.py:360
  7.4 9.7 %copy-start.13 = (bf16[8,128,128]{2,1,0:T(8,128)(2,1)S(1)}, bf16[8,128,128]{2,1,0:T(8,128)(2,1)}, u32[]{:S(2)}) copy-start(bf16[8,128,128]{2,1,0:T(8,128)(2,1)} %get-tuple-element.83) | copy-start | bytes 786436
  12.3 14.7 %copy-start.11 = (f32[8,128,128]{2,1,0:T(8,128)S(1)}, f32[8,128,128]{2,1,0:T(8,128)}, u32[]{:S(2)}) copy-start(f32[8,128,128]{2,1,0:T(8,128)} %get-tuple-element.82) | copy-start | bytes 1572868
  12.3 8.0 %collective-permute-start.1 = (bf16[2,128,512]{2,1,0:T(8,128)(2,1)}, bf16[2,128,512]{2,1,0:T(8,128)(2,1)S(1)}, u32[]{:S(2)}, u32[]{:S(2)}) collective-permute-start(bf16[2,128,512]{2,1,0:T(8,128)(2,1)} %get-tuple-element.96.refs_0_), channel_id=1, source_target_pairs={{0,2},{1,3},{2,0},{3,1},{4,6},{5,7},{6,4},{7,5},{8,10},{9,11},{10,... | collective-permute-start | bytes 786440 | tf_op jit(solution)/shard_map/ppermute | solution.py:360
  13.8 9.2 %collective-permute-start = (bf16[8,128,128]{2,1,0:T(8,128)(2,1)S(1)}, bf16[8,128,128]{2,1,0:T(8,128)(2,1)S(1)}, u32[]{:S(2)}, u32[]{:S(2)}) collective-permute-start(bf16[8,128,128]{2,1,0:T(8,128)(2,1)S(1)} %copy-done.14), channel_id=1, source_target_pairs={{0,4},{4,0},{8,12},{12,8},{16,20},{20,16},{24,28},{28,24},{1,5},{5... | collective-permute-start | bytes 786440 | tf_op jit(solution)/shard_map/ppermute | solution.py:360
  14.3 17.4 %copy-start.12 = (s32[1024]{0:T(1024)S(1)}, s32[1024]{0:T(1024)}, u32[]{:S(2)}) copy-start(s32[1024]{0:T(1024)} %param.14) | copy-start | bytes 12292
  15.5 20.9 %copy-start.4 = (bf16[2,128,512]{2,1,0:T(8,128)(2,1)S(1)}, bf16[2,128,512]{2,1,0:T(8,128)(2,1)}, u32[]{:S(2)}) copy-start(bf16[2,128,512]{2,1,0:T(8,128)(2,1)} %get-tuple-element.96.refs_0_) | copy-start | bytes 786436
  15.5 23.1 %copy-start.15 = (bf16[2,2,128,128]{3,2,1,0:T(8,128)(2,1)S(1)}, bf16[2,2,128,128]{3,2,1,0:T(8,128)(2,1)}, u32[]{:S(2)}) copy-start(bf16[2,2,128,128]{3,2,1,0:T(8,128)(2,1)} %get-tuple-element.89) | copy-start | bytes 393220
  15.5 23.5 %copy-start.10 = (f32[8,128,128]{2,1,0:T(8,128)S(1)}, f32[8,128,128]{2,1,0:T(8,128)}, u32[]{:S(2)}) copy-start(f32[8,128,128]{2,1,0:T(8,128)} %get-tuple-element.69) | copy-start | bytes 1572868
  15.5 7.6 %collective-permute-start.3 = (bf16[8,128,128]{2,1,0:T(8,128)(2,1)S(1)}, bf16[8,128,128]{2,1,0:T(8,128)(2,1)S(1)}, u32[]{:S(2)}, u32[]{:S(2)}) collective-permute-start(bf16[8,128,128]{2,1,0:T(8,128)(2,1)S(1)} %add_convert_fusion.2), channel_id=1, source_target_pairs={{0,8},{4,12},{8,0},{12,4},{16,24},{20,28},{24,16},{28,20},{1,9},{5... | collective-permute-start | bytes 786440 | tf_op jit(solution)/shard_map/ppermute | solution.py:360
  17.1 9.8 %collective-permute-start.4 = (bf16[8,128,128]{2,1,0:T(8,128)(2,1)S(1)}, bf16[8,128,128]{2,1,0:T(8,128)(2,1)S(1)}, u32[]{:S(2)}, u32[]{:S(2)}) collective-permute-start(bf16[8,128,128]{2,1,0:T(8,128)(2,1)S(1)} %copy-done.13), channel_id=1, source_target_pairs={{0,4},{4,0},{8,12},{12,8},{16,20},{20,16},{24,28},{28,24},{1,5},{5... | collective-permute-start | bytes 786440 | tf_op jit(solution)/shard_map/ppermute | solution.py:360
  24.2 14.3 %collective-permute-start.7 = (bf16[8,128,128]{2,1,0:T(8,128)(2,1)S(1)}, bf16[8,128,128]{2,1,0:T(8,128)(2,1)S(1)}, u32[]{:S(2)}, u32[]{:S(2)}) collective-permute-start(bf16[8,128,128]{2,1,0:T(8,128)(2,1)S(1)} %add_convert_fusion.1), channel_id=1, source_target_pairs={{0,16},{4,20},{8,24},{12,28},{16,0},{20,4},{24,8},{28,12},{1,17},{... | collective-permute-start | bytes 786440 | tf_op jit(solution)/shard_map/ppermute | solution.py:360
  27.7 11.3 %collective-permute-start.5 = (bf16[8,128,128]{2,1,0:T(8,128)(2,1)}, bf16[8,128,128]{2,1,0:T(8,128)(2,1)S(1)}, u32[]{:S(2)}, u32[]{:S(2)}) collective-permute-start(bf16[8,128,128]{2,1,0:T(8,128)(2,1)} %add_convert_fusion), channel_id=1, source_target_pairs={{0,8},{4,12},{8,0},{12,4},{16,24},{20,28},{24,16},{28,20},{1,9},{5... | collective-permute-start | bytes 786440 | tf_op jit(solution)/shard_map/ppermute | solution.py:360
  29.3 9.7 %collective-permute-start.6 = (bf16[8,128,128]{2,1,0:T(8,128)(2,1)}, bf16[8,128,128]{2,1,0:T(8,128)(2,1)}, u32[]{:S(2)}, u32[]{:S(2)}) collective-permute-start(bf16[8,128,128]{2,1,0:T(8,128)(2,1)} %get-tuple-element.84), channel_id=1, source_target_pairs={{0,4},{4,0},{8,12},{12,8},{16,20},{20,16},{24,28},{28,24},{1,5},{5... | collective-permute-start | bytes 786440 | tf_op jit(solution)/shard_map/ppermute | solution.py:360
  30.4 5.9 %collective-permute-start.8 = (bf16[2,2,128,128]{3,2,1,0:T(8,128)(2,1)}, bf16[2,2,128,128]{3,2,1,0:T(8,128)(2,1)S(1)}, u32[]{:S(2)}, u32[]{:S(2)}) collective-permute-start(bf16[2,2,128,128]{3,2,1,0:T(8,128)(2,1)} %get-tuple-element.86), channel_id=1, source_target_pairs={{0,2},{1,3},{2,0},{3,1},{4,6},{5,7},{6,4},{7,5},{8,10},{9,11},{10,... | collective-permute-start | bytes 393224 | tf_op jit(solution)/shard_map/ppermute | solution.py:360
  31.7 6.0 %collective-permute-start.9 = (bf16[2,2,128,128]{3,2,1,0:T(8,128)(2,1)}, bf16[2,2,128,128]{3,2,1,0:T(8,128)(2,1)S(1)}, u32[]{:S(2)}, u32[]{:S(2)}) collective-permute-start(bf16[2,2,128,128]{3,2,1,0:T(8,128)(2,1)} %get-tuple-element.87), channel_id=1, source_target_pairs={{0,3},{1,2},{2,1},{3,0},{4,7},{5,6},{6,5},{7,4},{8,11},{9,10},{10,... | collective-permute-start | bytes 393224 | tf_op jit(solution)/shard_map/ppermute | solution.py:360
  32.0 14.1 %copy-start.5 = (bf16[2,2,128,128]{3,2,1,0:T(8,128)(2,1)S(1)}, bf16[2,2,128,128]{3,2,1,0:T(8,128)(2,1)}, u32[]{:S(2)}) copy-start(bf16[2,2,128,128]{3,2,1,0:T(8,128)(2,1)} %get-tuple-element.100.refs_4_) | copy-start | bytes 393220
  36.3 3.7 %collective-permute-start.11 = (bf16[2,128,512]{2,1,0:T(8,128)(2,1)S(1)}, bf16[2,128,512]{2,1,0:T(8,128)(2,1)S(1)}, u32[]{:S(2)}, u32[]{:S(2)}) collective-permute-start(bf16[2,128,512]{2,1,0:T(8,128)(2,1)S(1)} %copy-done.4), channel_id=1, source_target_pairs={{0,1},{1,0},{2,3},{3,2},{4,5},{5,4},{6,7},{7,6},{8,9},{9,8},{10,11... | collective-permute-start | bytes 786440 | tf_op jit(solution)/shard_map/ppermute | solution.py:360
  37.7 2.3 %collective-permute-start.12 = (bf16[2,128,512]{2,1,0:T(8,128)(2,1)S(1)}, bf16[2,128,512]{2,1,0:T(8,128)(2,1)S(1)}, u32[]{:S(2)}, u32[]{:S(2)}) collective-permute-start(bf16[2,128,512]{2,1,0:T(8,128)(2,1)S(1)} %collective-permute-done.1.refs_2_), channel_id=1, source_target_pairs={{0,1},{1,0},{2,3},{3,2},{4,5},{5,4},{6,7},{7,6},{8,9},{9,8},{10,11... | collective-permute-start | bytes 786440 | tf_op jit(solution)/shard_map/ppermute | solution.py:360
  38.5 1.5 %collective-permute-start.10 = (bf16[2,2,128,128]{3,2,1,0:T(8,128)(2,1)S(1)}, bf16[2,2,128,128]{3,2,1,0:T(8,128)(2,1)S(1)}, u32[]{:S(2)}, u32[]{:S(2)}) collective-permute-start(bf16[2,2,128,128]{3,2,1,0:T(8,128)(2,1)S(1)} %copy-done.15), channel_id=1, source_target_pairs={{0,1},{1,0},{2,3},{3,2},{4,5},{5,4},{6,7},{7,6},{8,9},{9,8},{10,11... | collective-permute-start | bytes 393224 | tf_op jit(solution)/shard_map/ppermute | solution.py:360
  40.3 31.4 %copy-start.2 = (bf16[1024,128]{1,0:T(8,128)(2,1)S(1)}, bf16[1024,128]{1,0:T(8,128)(2,1)}, u32[]{:S(2)}) copy-start(bf16[1024,128]{1,0:T(8,128)(2,1)} %f_ref.1) | copy-start | bytes 786436
  40.3 31.4 %copy-start.3 = (bf16[128,512]{1,0:T(8,128)(2,1)S(1)}, bf16[128,512]{1,0:T(8,128)(2,1)}, u32[]{:S(2)}) copy-start(bf16[128,512]{1,0:T(8,128)(2,1)} %w_ref.1) | copy-start | bytes 393220
  40.3 2.1 %collective-permute-start.13 = (bf16[2,128,128]{2,1,0:T(8,128)(2,1)S(1)}, bf16[2,128,128]{2,1,0:T(8,128)(2,1)S(1)}, u32[]{:S(2)}, u32[]{:S(2)}) collective-permute-start(bf16[2,128,128]{2,1,0:T(8,128)(2,1)S(1)} %get-tuple-element.105), channel_id=1, source_target_pairs={{0,1},{1,0},{2,3},{3,2},{4,5},{5,4},{6,7},{7,6},{8,9},{9,8},{10,11... | collective-permute-start | bytes 196616 | tf_op jit(solution)/shard_map/ppermute | solution.py:360
  40.6 4.5 %collective-permute-start.14 = (bf16[2,128,128]{2,1,0:T(8,128)(2,1)S(1)}, bf16[2,128,128]{2,1,0:T(8,128)(2,1)S(1)}, u32[]{:S(2)}, u32[]{:S(2)}) collective-permute-start(bf16[2,128,128]{2,1,0:T(8,128)(2,1)S(1)} %get-tuple-element.106), channel_id=1, source_target_pairs={{0,2},{1,3},{2,0},{3,1},{4,6},{5,7},{6,4},{7,5},{8,10},{9,11},{10,... | collective-permute-start | bytes 196616 | tf_op jit(solution)/shard_map/ppermute | solution.py:360
  41.7 4.3 %collective-permute-start.15 = (bf16[2,128,128]{2,1,0:T(8,128)(2,1)S(1)}, bf16[2,128,128]{2,1,0:T(8,128)(2,1)S(1)}, u32[]{:S(2)}, u32[]{:S(2)}) collective-permute-start(bf16[2,128,128]{2,1,0:T(8,128)(2,1)S(1)} %get-tuple-element.107), channel_id=1, source_target_pairs={{0,3},{1,2},{2,1},{3,0},{4,7},{5,6},{6,5},{7,4},{8,11},{9,10},{10,... | collective-permute-start | bytes 196616 | tf_op jit(solution)/shard_map/ppermute | solution.py:360
  47.3 1.9 %collective-permute-start.16 = (bf16[256,128]{1,0:T(8,128)(2,1)S(1)}, bf16[256,128]{1,0:T(8,128)(2,1)S(1)}, u32[]{:S(2)}, u32[]{:S(2)}) collective-permute-start(bf16[256,128]{1,0:T(8,128)(2,1)S(1)} %get-tuple-element.109), channel_id=1, source_target_pairs={{0,1},{1,0},{2,3},{3,2},{4,5},{5,4},{6,7},{7,6},{8,9},{9,8},{10,11... | collective-permute-start | bytes 196616 | tf_op jit(solution)/shard_map/ppermute | solution.py:360
  47.5 4.8 %collective-permute-start.17 = (bf16[256,128]{1,0:T(8,128)(2,1)S(1)}, bf16[256,128]{1,0:T(8,128)(2,1)S(1)}, u32[]{:S(2)}, u32[]{:S(2)}) collective-permute-start(bf16[256,128]{1,0:T(8,128)(2,1)S(1)} %get-tuple-element.110), channel_id=1, source_target_pairs={{0,2},{1,3},{2,0},{3,1},{4,6},{5,7},{6,4},{7,5},{8,10},{9,11},{10,... | collective-permute-start | bytes 196616 | tf_op jit(solution)/shard_map/ppermute | solution.py:360
  48.5 4.3 %collective-permute-start.18 = (bf16[256,128]{1,0:T(8,128)(2,1)S(1)}, bf16[256,128]{1,0:T(8,128)(2,1)S(1)}, u32[]{:S(2)}, u32[]{:S(2)}) collective-permute-start(bf16[256,128]{1,0:T(8,128)(2,1)S(1)} %get-tuple-element.111), channel_id=1, source_target_pairs={{0,3},{1,2},{2,1},{3,0},{4,7},{5,6},{6,5},{7,4},{8,11},{9,10},{10,... | collective-permute-start | bytes 196616 | tf_op jit(solution)/shard_map/ppermute | solution.py:360
  52.9 17.1 %collective-permute-start.20 = (bf16[5,256,128]{2,1,0:T(8,128)(2,1)S(1)}, bf16[5,256,128]{2,1,0:T(8,128)(2,1)S(1)}, u32[]{:S(2)}, u32[]{:S(2)}) collective-permute-start(bf16[5,256,128]{2,1,0:T(8,128)(2,1)S(1)} %get-tuple-element.115), channel_id=1, source_target_pairs={{0,2},{1,3},{2,0},{3,1},{4,6},{5,7},{6,4},{7,5},{8,10},{9,11},{10,... | collective-permute-start | bytes 983048 | tf_op jit(solution)/shard_map/ppermute | solution.py:360
  53.9 16.1 %collective-permute-start.21 = (bf16[5,256,128]{2,1,0:T(8,128)(2,1)S(1)}, bf16[5,256,128]{2,1,0:T(8,128)(2,1)S(1)}, u32[]{:S(2)}, u32[]{:S(2)}) collective-permute-start(bf16[5,256,128]{2,1,0:T(8,128)(2,1)S(1)} %get-tuple-element.116), channel_id=1, source_target_pairs={{0,3},{1,2},{2,1},{3,0},{4,7},{5,6},{6,5},{7,4},{8,11},{9,10},{10,... | collective-permute-start | bytes 983048 | tf_op jit(solution)/shard_map/ppermute | solution.py:360
  54.5 15.4 %collective-permute-start.19 = (bf16[8,128,128]{2,1,0:T(8,128)(2,1)S(1)}, bf16[8,128,128]{2,1,0:T(8,128)(2,1)S(1)}, u32[]{:S(2)}, u32[]{:S(2)}) collective-permute-start(bf16[8,128,128]{2,1,0:T(8,128)(2,1)S(1)} %bitcast.24), channel_id=1, source_target_pairs={{0,16},{4,20},{8,24},{12,28},{16,0},{20,4},{24,8},{28,12},{1,17},{... | collective-permute-start | bytes 786440 | tf_op jit(solution)/shard_map/ppermute | solution.py:360
  56.8 13.2 %collective-permute-start.22 = (bf16[8,128,128]{2,1,0:T(8,128)(2,1)S(1)}, bf16[8,128,128]{2,1,0:T(8,128)(2,1)S(1)}, u32[]{:S(2)}, u32[]{:S(2)}) collective-permute-start(bf16[8,128,128]{2,1,0:T(8,128)(2,1)S(1)} %bitcast.25), channel_id=1, source_target_pairs={{0,8},{4,12},{8,0},{12,4},{16,24},{20,28},{24,16},{28,20},{1,9},{5... | collective-permute-start | bytes 786440 | tf_op jit(solution)/shard_map/ppermute | solution.py:360
  59.2 10.8 %collective-permute-start.23 = (bf16[8,128,128]{2,1,0:T(8,128)(2,1)S(1)}, bf16[8,128,128]{2,1,0:T(8,128)(2,1)S(1)}, u32[]{:S(2)}, u32[]{:S(2)}) collective-permute-start(bf16[8,128,128]{2,1,0:T(8,128)(2,1)S(1)} %bitcast.26), channel_id=1, source_target_pairs={{0,4},{4,0},{8,12},{12,8},{16,20},{20,16},{24,28},{28,24},{1,5},{5... | collective-permute-start | bytes 786440 | tf_op jit(solution)/shard_map/ppermute | solution.py:360
  70.0 1.7 %collective-permute-start.24 = (bf16[5,256,128]{2,1,0:T(8,128)(2,1)S(1)}, bf16[5,256,128]{2,1,0:T(8,128)(2,1)S(1)}, u32[]{:S(2)}, u32[]{:S(2)}) collective-permute-start(bf16[5,256,128]{2,1,0:T(8,128)(2,1)S(1)} %get-tuple-element.118.refs_0_), channel_id=1, source_target_pairs={{0,1},{1,0},{2,3},{3,2},{4,5},{5,4},{6,7},{7,6},{8,9},{9,8},{10,11... | collective-permute-start | bytes 983048 | tf_op jit(solution)/shard_map/ppermute | solution.py:360
  72.5 22.1 %copy-start = (bf16[1,6,8,128,128]{4,3,2,1,0:T(8,128)(2,1)S(1)}, bf16[1,6,8,128,128]{4,3,2,1,0:T(8,128)(2,1)}, u32[]{:S(2)}) copy-start(bf16[1,6,8,128,128]{4,3,2,1,0:T(8,128)(2,1)} %param.18) | copy-start | bytes 4718596
  72.5 22.1 %copy-start.1 = (bf16[1,16,128,128]{3,2,1,0:T(8,128)(2,1)S(1)}, bf16[1,16,128,128]{3,2,1,0:T(8,128)(2,1)}, u32[]{:S(2)}) copy-start(bf16[1,16,128,128]{3,2,1,0:T(8,128)(2,1)} %param.15) | copy-start | bytes 1572868
  72.5 22.0 %copy-start.6 = (s32[1,6,8]{2,0,1:T(1,128)S(1)}, s32[1,6,8]{2,0,1:T(1,128)}, u32[]{:S(2)}) copy-start(s32[1,6,8]{2,0,1:T(1,128)} %param.19) | copy-start | bytes 580
  72.5 22.0 %copy-start.7 = (s32[1,6,8]{2,0,1:T(1,128)S(1)}, s32[1,6,8]{2,0,1:T(1,128)}, u32[]{:S(2)}) copy-start(s32[1,6,8]{2,0,1:T(1,128)} %param.20) | copy-start | bytes 580
  72.5 22.0 %copy-start.8 = (s32[1,16]{1,0:T(1,128)S(1)}, s32[1,16]{1,0:T(1,128)}, u32[]{:S(2)}) copy-start(s32[1,16]{1,0:T(1,128)} %refs_0_.7) | copy-start | bytes 196
  72.5 22.0 %copy-start.9 = (s32[1,16]{1,0:T(1,128)S(1)}, s32[1,16]{1,0:T(1,128)}, u32[]{:S(2)}) copy-start(s32[1,16]{1,0:T(1,128)} %refs_1_.7) | copy-start | bytes 196
  72.5 5.6 %collective-permute-start.25 = (bf16[4,32,512]{2,1,0:T(8,128)(2,1)S(1)}, bf16[4,32,512]{2,1,0:T(8,128)(2,1)S(1)}, u32[]{:S(2)}, u32[]{:S(2)}) collective-permute-start(bf16[4,32,512]{2,1,0:T(8,128)(2,1)S(1)} %get-tuple-element.122), channel_id=1, source_target_pairs={{0,4},{4,0},{8,12},{12,8},{16,20},{20,16},{24,28},{28,24},{1,5},{5... | collective-permute-start | bytes 393224 | tf_op jit(solution)/shard_map/ppermute | solution.py:360
  78.2 6.1 %collective-permute-start.26 = (bf16[4,32,512]{2,1,0:T(8,128)(2,1)S(1)}, bf16[4,32,512]{2,1,0:T(8,128)(2,1)S(1)}, u32[]{:S(2)}, u32[]{:S(2)}) collective-permute-start(bf16[4,32,512]{2,1,0:T(8,128)(2,1)S(1)} %add_convert_fusion.5), channel_id=1, source_target_pairs={{0,8},{4,12},{8,0},{12,4},{16,24},{20,28},{24,16},{28,20},{1,9},{5... | collective-permute-start | bytes 393224 | tf_op jit(solution)/shard_map/ppermute | solution.py:360
  79.5 8.3 %collective-permute-start.29 = (bf16[8,128,128]{2,1,0:T(8,128)(2,1)S(1)}, bf16[8,128,128]{2,1,0:T(8,128)(2,1)S(1)}, u32[]{:S(2)}, u32[]{:S(2)}) collective-permute-start(bf16[8,128,128]{2,1,0:T(8,128)(2,1)S(1)} %collective-permute-done.19.refs_6_), channel_id=1, source_target_pairs={{0,4},{4,0},{8,12},{12,8},{16,20},{20,16},{24,28},{28,24},{1,5},{5... | collective-permute-start | bytes 786440 | tf_op jit(solution)/shard_map/ppermute | solution.py:360
  80.9 10.8 %collective-permute-start.30 = (bf16[8,128,128]{2,1,0:T(8,128)(2,1)S(1)}, bf16[8,128,128]{2,1,0:T(8,128)(2,1)S(1)}, u32[]{:S(2)}, u32[]{:S(2)}) collective-permute-start(bf16[8,128,128]{2,1,0:T(8,128)(2,1)S(1)} %collective-permute-done.19.refs_6_), channel_id=1, source_target_pairs={{0,8},{4,12},{8,0},{12,4},{16,24},{20,28},{24,16},{28,20},{1,9},{5... | collective-permute-start | bytes 786440 | tf_op jit(solution)/shard_map/ppermute | solution.py:360
  84.3 8.0 %collective-permute-start.27 = (bf16[4,32,512]{2,1,0:T(8,128)(2,1)S(1)}, bf16[4,32,512]{2,1,0:T(8,128)(2,1)S(1)}, u32[]{:S(2)}, u32[]{:S(2)}) collective-permute-start(bf16[4,32,512]{2,1,0:T(8,128)(2,1)S(1)} %add_convert_fusion.4), channel_id=1, source_target_pairs={{0,16},{4,20},{8,24},{12,28},{16,0},{20,4},{24,8},{28,12},{1,17},{... | collective-permute-start | bytes 393224 | tf_op jit(solution)/shard_map/ppermute | solution.py:360
  86.4 6.5 %collective-permute-start.28 = (bf16[8,128,128]{2,1,0:T(8,128)(2,1)S(1)}, bf16[8,128,128]{2,1,0:T(8,128)(2,1)S(1)}, u32[]{:S(2)}, u32[]{:S(2)}) collective-permute-start(bf16[8,128,128]{2,1,0:T(8,128)(2,1)S(1)} %collective-permute-done.22.refs_8_), channel_id=1, source_target_pairs={{0,4},{4,0},{8,12},{12,8},{16,20},{20,16},{24,28},{28,24},{1,5},{5... | collective-permute-start | bytes 786440 | tf_op jit(solution)/shard_map/ppermute | solution.py:360
  91.6 6.4 %collective-permute-start.31 = (bf16[8,128,128]{2,1,0:T(8,128)(2,1)S(1)}, bf16[8,128,128]{2,1,0:T(8,128)(2,1)S(1)}, u32[]{:S(2)}, u32[]{:S(2)}) collective-permute-start(bf16[8,128,128]{2,1,0:T(8,128)(2,1)S(1)} %collective-permute-done.29.refs_7_), channel_id=1, source_target_pairs={{0,8},{4,12},{8,0},{12,4},{16,24},{20,28},{24,16},{28,20},{1,9},{5... | collective-permute-start | bytes 786440 | tf_op jit(solution)/shard_map/ppermute | solution.py:360
  92.9 7.7 %collective-permute-start.32 = (bf16[4,32,512]{2,1,0:T(8,128)(2,1)S(1)}, bf16[4,32,512]{2,1,0:T(8,128)(2,1)S(1)}, u32[]{:S(2)}, u32[]{:S(2)}) collective-permute-start(bf16[4,32,512]{2,1,0:T(8,128)(2,1)S(1)} %add_convert_fusion.3.mine_ref), channel_id=1, source_target_pairs={{0,4},{4,0},{8,12},{12,8},{16,20},{20,16},{24,28},{28,24},{1,5},{5... | collective-permute-start | bytes 393224 | tf_op jit(solution)/shard_map/ppermute | solution.py:360

commit v16 on v14

--- a/solution.py
+++ b/solution.py
@@ -435,11 +435,12 @@
     sum_2 = (keep_2 + near_2.astype(F32)).astype(BF16)
     mid_0 = crossed(sum_2, 2)
     early_2, early_3 = crossed(early_pieces[2], 2, "feat"), crossed(early_pieces[3], 3, "feat")
-    far_0, early_2, early_3, early_1 = lax.optimization_barrier(
-        (far_0, early_2, early_3, early_pieces[1])
+    part = keep + near_0.astype(F32)
+    far_0, early_2, early_3, early_1, part = lax.optimization_barrier(
+        (far_0, early_2, early_3, early_pieces[1], part)
     )
     early = [early_pieces[0], crossed(early_1, 1, "feat"), early_2, early_3]
-    part = keep + mid_0.astype(F32) + near_0.astype(F32)
+    part = part + mid_0.astype(F32)
     arrived = [far_0]
     early, weights, arrived = lax.optimization_barrier((early, weights, arrived))
     agg, *agg_pieces = small_call(

time: 101 us -> 101 us (level)
  waiting for transfers between devices: 41.3 us -> 43 us
  other arithmetic: 4.15 us -> 2.54 us
    ppermute x33, waiting for transfers between devices: 41.3 us -> 43 us  [crossed(): lax.ppermute(x, axis, [(i, i ^ mask) for i in range(lax.axis_size(axis))])]
  transfers between devices with their start and end apart: 33 -> 33, of which waited for: 18 -> 18; matrix products, arithmetic and copies ran while one was open for 5% -> 3% of each run, Pallas kernels for 10% -> 10%
where the time goes in v16:
time: 101 us
  waiting for transfers between devices  43 us (43%)
  starting transfers between devices  36.8 us (36%)
  Pallas kernels  17.2 us (17%)
  other arithmetic  2.54 us (3%)
    ppermute x33, waiting for transfers between devices, crossed(): lax.ppermute(x, axis, [(i, i ^ mask) for i in range(lax.axis_size(axis))])  43 us
    ppermute x33, starting transfers between devices, crossed(): lax.ppermute(x, axis, [(i, i ^ mask) for i in range(lax.axis_size(axis))])  36.8 us
    pallas_call x4, Pallas kernels, tiles_call(): pl.pallas_call(functools.partial(tiles_kernel, masks, offsets, parts_tota...  13.3 us
    pallas_call x5, Pallas kernels, small_call(): pl.pallas_call(kernel, out_shape=outs, in_specs=[VMEM] * len(arrays), out...  3.85 us
  transfers between devices with their start and end apart: 33, of which 18 were waited for; matrix products, arithmetic and copies ran while one was open for 3% of the time, Pallas kernels for 10%

profile of v16, /device:TPU:0, one launch (start us, length us, event | category | flops | bytes accessed | tf_op | source)
XLA Modules:
  0.0 101.0 jit_solution(4207704740863269680)
XLA Ops:
  0.6 3.7 %shard_map.139 = (bf16[8,128,128]{2,1,0:T(8,128)(2,1)}, bf16[8,128,128]{2,1,0:T(8,128)(2,1)}, bf16[8,128,128]{2,1,0:T(8,128)(2,1)}, bf16[8,128,128]{2,1,0:T(8,128)(2,1)}) custom-call(s32[1,16]{1,0:T(1,128)} %refs_0_.7, s32[1,16]{1,0:T(1,128)} %refs_1_.7, s32[6,1,8]{2,1,0:T(1,128)} %bitcast.30, s32[6,1,8]{2,1,0:T(1,128)} %bitcast.34, ...), custom_call_target="tpu_custom_call" | custom-call | flops 1 | bytes 1 | tf_op jit(solution)/shard_map/pallas_call | solution.py:224
  4.4 3.0 %collective-permute-start.2 = (bf16[8,128,128]{2,1,0:T(8,128)(2,1)}, bf16[8,128,128]{2,1,0:T(8,128)(2,1)S(1)}, u32[]{:S(2)}, u32[]{:S(2)}) collective-permute-start(bf16[8,128,128]{2,1,0:T(8,128)(2,1)} %get-tuple-element.74), channel_id=1, source_target_pairs={{0,4},{4,0},{8,12},{12,8},{16,20},{20,16},{24,28},{28,24},{1,5},{5... | collective-permute-start | bytes 786440 | tf_op jit(solution)/shard_map/ppermute | solution.py:360
  7.4 4.8 %shard_map.138 = (f32[8,128,128]{2,1,0:T(8,128)}, f32[8,128,128]{2,1,0:T(8,128)}, f32[8,128,128]{2,1,0:T(8,128)}, f32[8,128,128]{2,1,0:T(8,128)}, bf16[2,2,128,1...) custom-call(s32[1,16]{1,0:T(1,128)} %refs_0_.7, ...), custom_call_target="tpu_custom_call" | custom-call | flops 1 | bytes 1 | tf_op jit(solution)/shard_map/pallas_call | solution.py:224
  12.3 1.6 %collective-permute-start.1 = (bf16[2,128,512]{2,1,0:T(8,128)(2,1)}, bf16[2,128,512]{2,1,0:T(8,128)(2,1)S(1)}, u32[]{:S(2)}, u32[]{:S(2)}) collective-permute-start(bf16[2,128,512]{2,1,0:T(8,128)(2,1)} %get-tuple-element.97.refs_0_), channel_id=1, source_target_pairs={{0,2},{1,3},{2,0},{3,1},{4,6},{5,7},{6,4},{7,5},{8,10},{9,11},{10,... | collective-permute-start | bytes 786440 | tf_op jit(solution)/shard_map/ppermute | solution.py:360
  13.8 0.5 collective-permute-start
  14.3 1.1 %add_convert_fusion.2 = bf16[8,128,128]{2,1,0:T(8,128)(2,1)S(1)} fusion(f32[8,128,128]{2,1,0:T(8,128)} %get-tuple-element.73, bf16[8,128,128]{2,1,0:T(8,128)(2,1)S(1)} %collective-permute-done.2), kind=kLoop, calls=%fused_computation.4 | loop fusion | flops 393216 | bytes 1048576 | tf_op jit(solution)/shard_map/convert_element_type | solution.py:429
  15.5 1.7 %collective-permute-start.3 = (bf16[8,128,128]{2,1,0:T(8,128)(2,1)S(1)}, bf16[8,128,128]{2,1,0:T(8,128)(2,1)S(1)}, u32[]{:S(2)}, u32[]{:S(2)}) collective-permute-start(bf16[8,128,128]{2,1,0:T(8,128)(2,1)S(1)} %add_convert_fusion.2), channel_id=1, source_target_pairs={{0,8},{4,12},{8,0},{12,4},{16,24},{20,28},{24,16},{28,20},{1,9},{5... | collective-permute-start | bytes 786440 | tf_op jit(solution)/shard_map/ppermute | solution.py:360
  17.1 1.5 %collective-permute-start.8 = (bf16[8,128,128]{2,1,0:T(8,128)(2,1)S(1)}, bf16[8,128,128]{2,1,0:T(8,128)(2,1)S(1)}, u32[]{:S(2)}, u32[]{:S(2)}) collective-permute-start(bf16[8,128,128]{2,1,0:T(8,128)(2,1)S(1)} %copy-done.13), channel_id=1, source_target_pairs={{0,4},{4,0},{8,12},{12,8},{16,20},{20,16},{24,28},{28,24},{1,5},{5... | collective-permute-start | bytes 786440 | tf_op jit(solution)/shard_map/ppermute | solution.py:360
  18.6 1.7 %collective-permute-done.1.refs_2_ = bf16[2,128,512]{2,1,0:T(8,128)(2,1)S(1)} collective-permute-done((bf16[2,128,512]{2,1,0:T(8,128)(2,1)}, bf16[2,128,512]{2,1,0:T(8,128)(2,1)S(1)}, u32[]{:S(2)}, u32[]{:S(2)}) %collective-permute-start.1) | collective-permute-done | bytes 262176 | tf_op jit(solution)/shard_map/ppermute | solution.py:360
  20.3 2.8 %collective-permute-done = bf16[8,128,128]{2,1,0:T(8,128)(2,1)S(1)} collective-permute-done((bf16[8,128,128]{2,1,0:T(8,128)(2,1)S(1)}, bf16[8,128,128]{2,1,0:T(8,128)(2,1)S(1)}, u32[]{:S(2)}, u32[]{:S(2)}) %collective-permute-start) | collective-permute-done | bytes 262176 | tf_op jit(solution)/shard_map/ppermute | solution.py:360
  23.1 1.1 %add_convert_fusion.1 = bf16[8,128,128]{2,1,0:T(8,128)(2,1)S(1)} fusion(bf16[8,128,128]{2,1,0:T(8,128)(2,1)S(1)} %collective-permute-done.3, f32[8,128,128]{2,1,0:T(8,128)} %get-tuple-element.69, bf16[8,128,128]{2,1,0:T(8,128)(2,1)S(1)} %collective-permute-done), kind=kLoop, calls=%fused_computation.3 | loop fusion | flops 655360 | bytes 1310720 | tf_op jit(solution)/shard_map/convert_element_type | solution.py:431
  24.2 2.6 %collective-permute-start.4 = (bf16[8,128,128]{2,1,0:T(8,128)(2,1)S(1)}, bf16[8,128,128]{2,1,0:T(8,128)(2,1)S(1)}, u32[]{:S(2)}, u32[]{:S(2)}) collective-permute-start(bf16[8,128,128]{2,1,0:T(8,128)(2,1)S(1)} %add_convert_fusion.1), channel_id=1, source_target_pairs={{0,16},{4,20},{8,24},{12,28},{16,0},{20,4},{24,8},{28,12},{1,17},{... | collective-permute-start | bytes 786440 | tf_op jit(solution)/shard_map/ppermute | solution.py:360
  26.9 1.2 %collective-permute-start.7 = (bf16[8,128,128]{2,1,0:T(8,128)(2,1)}, bf16[8,128,128]{2,1,0:T(8,128)(2,1)S(1)}, u32[]{:S(2)}, u32[]{:S(2)}) collective-permute-start(bf16[8,128,128]{2,1,0:T(8,128)(2,1)} %get-tuple-element.85), channel_id=1, source_target_pairs={{0,4},{4,0},{8,12},{12,8},{16,20},{20,16},{24,28},{28,24},{1,5},{5... | collective-permute-start | bytes 786440 | tf_op jit(solution)/shard_map/ppermute | solution.py:360
  28.1 1.3 %collective-permute-start.5 = (bf16[2,2,128,128]{3,2,1,0:T(8,128)(2,1)}, bf16[2,2,128,128]{3,2,1,0:T(8,128)(2,1)S(1)}, u32[]{:S(2)}, u32[]{:S(2)}) collective-permute-start(bf16[2,2,128,128]{3,2,1,0:T(8,128)(2,1)} %get-tuple-element.81), channel_id=1, source_target_pairs={{0,2},{1,3},{2,0},{3,1},{4,6},{5,7},{6,4},{7,5},{8,10},{9,11},{10,... | collective-permute-start | bytes 393224 | tf_op jit(solution)/shard_map/ppermute | solution.py:360
  29.3 0.1 add_convert_fusion
  29.4 1.6 %collective-permute-start.9 = (bf16[8,128,128]{2,1,0:T(8,128)(2,1)S(1)}, bf16[8,128,128]{2,1,0:T(8,128)(2,1)S(1)}, u32[]{:S(2)}, u32[]{:S(2)}) collective-permute-start(bf16[8,128,128]{2,1,0:T(8,128)(2,1)S(1)} %add_convert_fusion), channel_id=1, source_target_pairs={{0,8},{4,12},{8,0},{12,4},{16,24},{20,28},{24,16},{28,20},{1,9},{5... | collective-permute-start | bytes 786440 | tf_op jit(solution)/shard_map/ppermute | solution.py:360
  31.1 0.2 copy.15.inv_ref
  31.3 1.9 %collective-permute-done.5.refs_6_ = bf16[2,2,128,128]{3,2,1,0:T(8,128)(2,1)S(1)} collective-permute-done((bf16[2,2,128,128]{3,2,1,0:T(8,128)(2,1)}, bf16[2,2,128,128]{3,2,1,0:T(8,128)(2,1)S(1)}, u32[]{:S(2)}, u32[]{:S(2)}) %collective-permute-start.5) | collective-permute-done | bytes 131104 | tf_op jit(solution)/shard_map/ppermute | solution.py:360
  33.2 0.2 collective-permute-done.7
  33.5 1.2 %collective-permute-start.6 = (bf16[2,2,128,128]{3,2,1,0:T(8,128)(2,1)}, bf16[2,2,128,128]{3,2,1,0:T(8,128)(2,1)S(1)}, u32[]{:S(2)}, u32[]{:S(2)}) collective-permute-start(bf16[2,2,128,128]{3,2,1,0:T(8,128)(2,1)} %get-tuple-element.82), channel_id=1, source_target_pairs={{0,3},{1,2},{2,1},{3,0},{4,7},{5,6},{6,5},{7,4},{8,11},{9,10},{10,... | collective-permute-start | bytes 393224 | tf_op jit(solution)/shard_map/ppermute | solution.py:360
  34.7 4.4 %collective-permute-done.6.refs_7_ = bf16[2,2,128,128]{3,2,1,0:T(8,128)(2,1)S(1)} collective-permute-done((bf16[2,2,128,128]{3,2,1,0:T(8,128)(2,1)}, bf16[2,2,128,128]{3,2,1,0:T(8,128)(2,1)S(1)}, u32[]{:S(2)}, u32[]{:S(2)}) %collective-permute-start.6) | collective-permute-done | bytes 131104 | tf_op jit(solution)/shard_map/ppermute | solution.py:360
  39.1 0.2 collective-permute-start.10
  39.4 1.3 %collective-permute-done.10.refs_5_ = bf16[2,2,128,128]{3,2,1,0:T(8,128)(2,1)S(1)} collective-permute-done((bf16[2,2,128,128]{3,2,1,0:T(8,128)(2,1)}, bf16[2,2,128,128]{3,2,1,0:T(8,128)(2,1)S(1)}, u32[]{:S(2)}, u32[]{:S(2)}) %collective-permute-start.10) | collective-permute-done | bytes 131104 | tf_op jit(solution)/shard_map/ppermute | solution.py:360
  40.6 0.2 shard_map.140
  40.9 0.3 collective-permute-start.13
  41.2 1.1 %collective-permute-start.14 = (bf16[2,128,128]{2,1,0:T(8,128)(2,1)S(1)}, bf16[2,128,128]{2,1,0:T(8,128)(2,1)S(1)}, u32[]{:S(2)}, u32[]{:S(2)}) collective-permute-start(bf16[2,128,128]{2,1,0:T(8,128)(2,1)S(1)} %get-tuple-element.107), channel_id=1, source_target_pairs={{0,2},{1,3},{2,0},{3,1},{4,6},{5,7},{6,4},{7,5},{8,10},{9,11},{10,... | collective-permute-start | bytes 196616 | tf_op jit(solution)/shard_map/ppermute | solution.py:360
  42.2 0.6 collective-permute-start.15
  42.8 0.1 dynamic_slice.3
  42.9 0.1 copy.16.inv_ref
  43.0 2.7 %collective-permute-done.14.refs_10_ = bf16[2,128,128]{2,1,0:T(8,128)(2,1)S(1)} collective-permute-done((bf16[2,128,128]{2,1,0:T(8,128)(2,1)S(1)}, bf16[2,128,128]{2,1,0:T(8,128)(2,1)S(1)}, u32[]{:S(2)}, u32[]{:S(2)}) %collective-permute-start.14) | collective-permute-done | bytes 65568 | tf_op jit(solution)/shard_map/ppermute | solution.py:360
  45.8 0.8 collective-permute-done.15.refs_11_
  46.6 1.3 %shard_map.141 = (bf16[5,256,128]{2,1,0:T(8,128)(2,1)S(1)}, bf16[5,256,128]{2,1,0:T(8,128)(2,1)S(1)}, bf16[5,256,128]{2,1,0:T(8,128)(2,1)S(1)}, bf16[256,128]{1,...) custom-call(f32[256,1]{1,0:T(8,128)S(1)} %copy.16.inv_ref, ...), custom_call_target="tpu_custom_call" | custom-call | flops 1 | bytes 1 | tf_op jit(solution)/shard_map/pallas_call | solution.py:244
  47.8 0.2 collective-permute-start.16
  48.0 1.1 %collective-permute-start.17 = (bf16[256,128]{1,0:T(8,128)(2,1)S(1)}, bf16[256,128]{1,0:T(8,128)(2,1)S(1)}, u32[]{:S(2)}, u32[]{:S(2)}) collective-permute-start(bf16[256,128]{1,0:T(8,128)(2,1)S(1)} %get-tuple-element.111), channel_id=1, source_target_pairs={{0,2},{1,3},{2,0},{3,1},{4,6},{5,7},{6,4},{7,5},{8,10},{9,11},{10,... | collective-permute-start | bytes 196616 | tf_op jit(solution)/shard_map/ppermute | solution.py:360
  49.1 0.7 collective-permute-start.18
  49.8 3.1 %collective-permute-done.17 = bf16[256,128]{1,0:T(8,128)(2,1)S(1)} collective-permute-done((bf16[256,128]{1,0:T(8,128)(2,1)S(1)}, bf16[256,128]{1,0:T(8,128)(2,1)S(1)}, u32[]{:S(2)}, u32[]{:S(2)}) %collective-permute-start.17) | collective-permute-done | bytes 65568 | tf_op jit(solution)/shard_map/ppermute | solution.py:360
  52.8 0.6 collective-permute-done.18
  53.4 1.1 %collective-permute-start.20 = (bf16[5,256,128]{2,1,0:T(8,128)(2,1)S(1)}, bf16[5,256,128]{2,1,0:T(8,128)(2,1)S(1)}, u32[]{:S(2)}, u32[]{:S(2)}) collective-permute-start(bf16[5,256,128]{2,1,0:T(8,128)(2,1)S(1)} %get-tuple-element.116), channel_id=1, source_target_pairs={{0,2},{1,3},{2,0},{3,1},{4,6},{5,7},{6,4},{7,5},{8,10},{9,11},{10,... | collective-permute-start | bytes 983048 | tf_op jit(solution)/shard_map/ppermute | solution.py:360
  54.5 0.6 collective-permute-start.21
  55.1 1.4 %collective-permute-start.19 = (bf16[8,128,128]{2,1,0:T(8,128)(2,1)S(1)}, bf16[8,128,128]{2,1,0:T(8,128)(2,1)S(1)}, u32[]{:S(2)}, u32[]{:S(2)}) collective-permute-start(bf16[8,128,128]{2,1,0:T(8,128)(2,1)S(1)} %bitcast.24), channel_id=1, source_target_pairs={{0,16},{4,20},{8,24},{12,28},{16,0},{20,4},{24,8},{28,12},{1,17},{... | collective-permute-start | bytes 786440 | tf_op jit(solution)/shard_map/ppermute | solution.py:360
  56.5 1.6 %collective-permute-start.22 = (bf16[8,128,128]{2,1,0:T(8,128)(2,1)S(1)}, bf16[8,128,128]{2,1,0:T(8,128)(2,1)S(1)}, u32[]{:S(2)}, u32[]{:S(2)}) collective-permute-start(bf16[8,128,128]{2,1,0:T(8,128)(2,1)S(1)} %bitcast.25), channel_id=1, source_target_pairs={{0,8},{4,12},{8,0},{12,4},{16,24},{20,28},{24,16},{28,20},{1,9},{5... | collective-permute-start | bytes 786440 | tf_op jit(solution)/shard_map/ppermute | solution.py:360
  58.1 0.6 collective-permute-start.23
  58.7 11.7 %collective-permute-done.19.refs_6_ = bf16[8,128,128]{2,1,0:T(8,128)(2,1)S(1)} collective-permute-done((bf16[8,128,128]{2,1,0:T(8,128)(2,1)S(1)}, bf16[8,128,128]{2,1,0:T(8,128)(2,1)S(1)}, u32[]{:S(2)}, u32[]{:S(2)}) %collective-permute-start.19) | collective-permute-done | bytes 262176 | tf_op jit(solution)/shard_map/ppermute | solution.py:360
  70.4 0.1 collective-permute-start.24
  70.5 1.6 %collective-permute-done.24.refs_1_ = bf16[5,256,128]{2,1,0:T(8,128)(2,1)S(1)} collective-permute-done((bf16[5,256,128]{2,1,0:T(8,128)(2,1)S(1)}, bf16[5,256,128]{2,1,0:T(8,128)(2,1)S(1)}, u32[]{:S(2)}, u32[]{:S(2)}) %collective-permute-start.24) | collective-permute-done | bytes 327712 | tf_op jit(solution)/shard_map/ppermute | solution.py:360
  72.1 0.8 shard_map.142
  72.9 1.7 %collective-permute-start.25 = (bf16[4,32,512]{2,1,0:T(8,128)(2,1)S(1)}, bf16[4,32,512]{2,1,0:T(8,128)(2,1)S(1)}, u32[]{:S(2)}, u32[]{:S(2)}) collective-permute-start(bf16[4,32,512]{2,1,0:T(8,128)(2,1)S(1)} %get-tuple-element.123), channel_id=1, source_target_pairs={{0,4},{4,0},{8,12},{12,8},{16,20},{20,16},{24,28},{28,24},{1,5},{5... | collective-permute-start | bytes 393224 | tf_op jit(solution)/shard_map/ppermute | solution.py:360
  74.7 3.9 %collective-permute-done.25 = bf16[4,32,512]{2,1,0:T(8,128)(2,1)S(1)} collective-permute-done((bf16[4,32,512]{2,1,0:T(8,128)(2,1)S(1)}, bf16[4,32,512]{2,1,0:T(8,128)(2,1)S(1)}, u32[]{:S(2)}, u32[]{:S(2)}) %collective-permute-start.25) | collective-permute-done | bytes 131104 | tf_op jit(solution)/shard_map/ppermute | solution.py:360
  78.6 1.3 %collective-permute-start.26 = (bf16[4,32,512]{2,1,0:T(8,128)(2,1)S(1)}, bf16[4,32,512]{2,1,0:T(8,128)(2,1)S(1)}, u32[]{:S(2)}, u32[]{:S(2)}) collective-permute-start(bf16[4,32,512]{2,1,0:T(8,128)(2,1)S(1)} %add_convert_fusion.5), channel_id=1, source_target_pairs={{0,8},{4,12},{8,0},{12,4},{16,24},{20,28},{24,16},{28,20},{1,9},{5... | collective-permute-start | bytes 393224 | tf_op jit(solution)/shard_map/ppermute | solution.py:360
  79.9 0.8 collective-permute-start.29
  80.7 1.7 %collective-permute-start.30 = (bf16[8,128,128]{2,1,0:T(8,128)(2,1)S(1)}, bf16[8,128,128]{2,1,0:T(8,128)(2,1)S(1)}, u32[]{:S(2)}, u32[]{:S(2)}) collective-permute-start(bf16[8,128,128]{2,1,0:T(8,128)(2,1)S(1)} %collective-permute-done.19.refs_6_), channel_id=1, source_target_pairs={{0,4},{4,0},{8,12},{12,8},{16,20},{20,16},{24,28},{28,24},{1,5},{5... | collective-permute-start | bytes 786440 | tf_op jit(solution)/shard_map/ppermute | solution.py:360
  82.3 2.7 %collective-permute-done.26 = bf16[4,32,512]{2,1,0:T(8,128)(2,1)S(1)} collective-permute-done((bf16[4,32,512]{2,1,0:T(8,128)(2,1)S(1)}, bf16[4,32,512]{2,1,0:T(8,128)(2,1)S(1)}, u32[]{:S(2)}, u32[]{:S(2)}) %collective-permute-start.26) | collective-permute-done | bytes 131104 | tf_op jit(solution)/shard_map/ppermute | solution.py:360
  85.1 1.7 %collective-permute-start.27 = (bf16[4,32,512]{2,1,0:T(8,128)(2,1)S(1)}, bf16[4,32,512]{2,1,0:T(8,128)(2,1)S(1)}, u32[]{:S(2)}, u32[]{:S(2)}) collective-permute-start(bf16[4,32,512]{2,1,0:T(8,128)(2,1)S(1)} %add_convert_fusion.4), channel_id=1, source_target_pairs={{0,16},{4,20},{8,24},{12,28},{16,0},{20,4},{24,8},{28,12},{1,17},{... | collective-permute-start | bytes 393224 | tf_op jit(solution)/shard_map/ppermute | solution.py:360
  86.8 1.6 %collective-permute-start.28 = (bf16[8,128,128]{2,1,0:T(8,128)(2,1)S(1)}, bf16[8,128,128]{2,1,0:T(8,128)(2,1)S(1)}, u32[]{:S(2)}, u32[]{:S(2)}) collective-permute-start(bf16[8,128,128]{2,1,0:T(8,128)(2,1)S(1)} %collective-permute-done.22.refs_8_), channel_id=1, source_target_pairs={{0,4},{4,0},{8,12},{12,8},{16,20},{20,16},{24,28},{28,24},{1,5},{5... | collective-permute-start | bytes 786440 | tf_op jit(solution)/shard_map/ppermute | solution.py:360
  88.4 2.7 %collective-permute-done.29.refs_8_ = bf16[8,128,128]{2,1,0:T(8,128)(2,1)S(1)} collective-permute-done((bf16[8,128,128]{2,1,0:T(8,128)(2,1)S(1)}, bf16[8,128,128]{2,1,0:T(8,128)(2,1)S(1)}, u32[]{:S(2)}, u32[]{:S(2)}) %collective-permute-start.29) | collective-permute-done | bytes 262176 | tf_op jit(solution)/shard_map/ppermute | solution.py:360
  91.1 0.8 collective-permute-start.31
  91.9 0.7 shard_map.143
  92.6 0.5 collective-permute-done.27
  93.2 0.1 collective-permute-done.28.refs_9_
  93.3 1.6 %collective-permute-start.32 = (bf16[4,32,512]{2,1,0:T(8,128)(2,1)S(1)}, bf16[4,32,512]{2,1,0:T(8,128)(2,1)S(1)}, u32[]{:S(2)}, u32[]{:S(2)}) collective-permute-start(bf16[4,32,512]{2,1,0:T(8,128)(2,1)S(1)} %add_convert_fusion.3.mine_ref), channel_id=1, source_target_pairs={{0,4},{4,0},{8,12},{12,8},{16,20},{20,16},{24,28},{28,24},{1,5},{5... | collective-permute-start | bytes 393224 | tf_op jit(solution)/shard_map/ppermute | solution.py:360
  94.9 2.1 %shard_map.144.refs_10_ = f32[8,128,128]{2,1,0:T(8,128)S(1)} custom-call(s32[1,16]{1,0:T(1,128)S(1)} %copy-done.8, s32[1,16]{1,0:T(1,128)S(1)} %copy-done.9, s32[6,1,8]{2,1,0:T(1,128)S(1)} %bitcast.32, s32[6,1,8]{2,1,0:T(1,128)S(1)} %bitcast.36, bf16[16,128,128]{2,1,0:T(8,128)(2,1)S(1)} %bitcast.20, bf16[6,8,128,128]{3,2,1,0:T(8,128)(2,1)S(1)} %bitcast.16, ...), custom_call_target="tpu_custom_call" | custom-call | flops 1 | bytes 1 | tf_op jit(solution)/shard_map/pallas_call | solution.py:224
  97.1 0.4 collective-permute-done.31.refs_9_
  97.5 2.6 %shard_map.145 = f32[8,128,128]{2,1,0:T(8,128)} custom-call(s32[1,16]{1,0:T(1,128)S(1)} %copy-done.8, s32[1,16]{1,0:T(1,128)S(1)} %copy-done.9, s32[6,1,8]{2,1,0:T(1,128)S(1)} %bitcast.33, s32[6,1,8]{2,1,0:T(1,128)S(1)} %bitcast.37, bf16[16,128,128]{2,1,0:T(8,128)(2,1)S(1)} %bitcast.21, bf16[6,8,128,128]{3,2,1,0:T(8,128)(2,1)S(1)} %bitcast.17, ...), custom_call_target="tpu_custom_call" | custom-call | flops 1 | bytes 1 | tf_op jit(solution)/shard_map/pallas_call | solution.py:224
  100.1 0.9 shard_map.146
  (54 shorter events, 0.4 us)
Async XLA Ops:
  4.4 9.5 %copy-start.14 = (bf16[8,128,128]{2,1,0:T(8,128)(2,1)S(1)}, bf16[8,128,128]{2,1,0:T(8,128)(2,1)}, u32[]{:S(2)}) copy-start(bf16[8,128,128]{2,1,0:T(8,128)(2,1)} %get-tuple-element.70) | copy-start | bytes 786436
  4.4 9.9 %collective-permute-start.2 = (bf16[8,128,128]{2,1,0:T(8,128)(2,1)}, bf16[8,128,128]{2,1,0:T(8,128)(2,1)S(1)}, u32[]{:S(2)}, u32[]{:S(2)}) collective-permute-start(bf16[8,128,128]{2,1,0:T(8,128)(2,1)} %get-tuple-element.74), channel_id=1, source_target_pairs={{0,4},{4,0},{8,12},{12,8},{16,20},{20,16},{24,28},{28,24},{1,5},{5... | collective-permute-start | bytes 786440 | tf_op jit(solution)/shard_map/ppermute | solution.py:360
  7.4 9.7 %copy-start.13 = (bf16[8,128,128]{2,1,0:T(8,128)(2,1)S(1)}, bf16[8,128,128]{2,1,0:T(8,128)(2,1)}, u32[]{:S(2)}) copy-start(bf16[8,128,128]{2,1,0:T(8,128)(2,1)} %get-tuple-element.88) | copy-start | bytes 786436
  12.3 17.1 %copy-start.11 = (f32[8,128,128]{2,1,0:T(8,128)S(1)}, f32[8,128,128]{2,1,0:T(8,128)}, u32[]{:S(2)}) copy-start(f32[8,128,128]{2,1,0:T(8,128)} %get-tuple-element.87) | copy-start | bytes 1572868
  12.3 8.0 %collective-permute-start.1 = (bf16[2,128,512]{2,1,0:T(8,128)(2,1)}, bf16[2,128,512]{2,1,0:T(8,128)(2,1)S(1)}, u32[]{:S(2)}, u32[]{:S(2)}) collective-permute-start(bf16[2,128,512]{2,1,0:T(8,128)(2,1)} %get-tuple-element.97.refs_0_), channel_id=1, source_target_pairs={{0,2},{1,3},{2,0},{3,1},{4,6},{5,7},{6,4},{7,5},{8,10},{9,11},{10,... | collective-permute-start | bytes 786440 | tf_op jit(solution)/shard_map/ppermute | solution.py:360
  13.8 9.2 %collective-permute-start = (bf16[8,128,128]{2,1,0:T(8,128)(2,1)S(1)}, bf16[8,128,128]{2,1,0:T(8,128)(2,1)S(1)}, u32[]{:S(2)}, u32[]{:S(2)}) collective-permute-start(bf16[8,128,128]{2,1,0:T(8,128)(2,1)S(1)} %copy-done.14), channel_id=1, source_target_pairs={{0,4},{4,0},{8,12},{12,8},{16,20},{20,16},{24,28},{28,24},{1,5},{5... | collective-permute-start | bytes 786440 | tf_op jit(solution)/shard_map/ppermute | solution.py:360
  14.3 16.7 %copy-start.12 = (s32[1024]{0:T(1024)S(1)}, s32[1024]{0:T(1024)}, u32[]{:S(2)}) copy-start(s32[1024]{0:T(1024)} %param.14) | copy-start | bytes 12292
  15.5 19.2 %copy-start.10 = (f32[8,128,128]{2,1,0:T(8,128)S(1)}, f32[8,128,128]{2,1,0:T(8,128)}, u32[]{:S(2)}) copy-start(f32[8,128,128]{2,1,0:T(8,128)} %get-tuple-element.84) | copy-start | bytes 1572868
  15.5 7.6 %collective-permute-start.3 = (bf16[8,128,128]{2,1,0:T(8,128)(2,1)S(1)}, bf16[8,128,128]{2,1,0:T(8,128)(2,1)S(1)}, u32[]{:S(2)}, u32[]{:S(2)}) collective-permute-start(bf16[8,128,128]{2,1,0:T(8,128)(2,1)S(1)} %add_convert_fusion.2), channel_id=1, source_target_pairs={{0,8},{4,12},{8,0},{12,4},{16,24},{20,28},{24,16},{28,20},{1,9},{5... | collective-permute-start | bytes 786440 | tf_op jit(solution)/shard_map/ppermute | solution.py:360
  17.1 12.2 %collective-permute-start.8 = (bf16[8,128,128]{2,1,0:T(8,128)(2,1)S(1)}, bf16[8,128,128]{2,1,0:T(8,128)(2,1)S(1)}, u32[]{:S(2)}, u32[]{:S(2)}) collective-permute-start(bf16[8,128,128]{2,1,0:T(8,128)(2,1)S(1)} %copy-done.13), channel_id=1, source_target_pairs={{0,4},{4,0},{8,12},{12,8},{16,20},{20,16},{24,28},{28,24},{1,5},{5... | collective-permute-start | bytes 786440 | tf_op jit(solution)/shard_map/ppermute | solution.py:360
  18.6 20.7 %collective-permute-start.11 = (bf16[2,128,512]{2,1,0:T(8,128)(2,1)}, bf16[2,128,512]{2,1,0:T(8,128)(2,1)S(1)}, u32[]{:S(2)}, u32[]{:S(2)}) collective-permute-start(bf16[2,128,512]{2,1,0:T(8,128)(2,1)} %get-tuple-element.97.refs_0_), channel_id=1, source_target_pairs={{0,1},{1,0},{2,3},{3,2},{4,5},{5,4},{6,7},{7,6},{8,9},{9,8},{10,11... | collective-permute-start | bytes 786440 | tf_op jit(solution)/shard_map/ppermute | solution.py:360
  24.2 14.8 %collective-permute-start.4 = (bf16[8,128,128]{2,1,0:T(8,128)(2,1)S(1)}, bf16[8,128,128]{2,1,0:T(8,128)(2,1)S(1)}, u32[]{:S(2)}, u32[]{:S(2)}) collective-permute-start(bf16[8,128,128]{2,1,0:T(8,128)(2,1)S(1)} %add_convert_fusion.1), channel_id=1, source_target_pairs={{0,16},{4,20},{8,24},{12,28},{16,0},{20,4},{24,8},{28,12},{1,17},{... | collective-permute-start | bytes 786440 | tf_op jit(solution)/shard_map/ppermute | solution.py:360
  26.9 6.6 %collective-permute-start.7 = (bf16[8,128,128]{2,1,0:T(8,128)(2,1)}, bf16[8,128,128]{2,1,0:T(8,128)(2,1)S(1)}, u32[]{:S(2)}, u32[]{:S(2)}) collective-permute-start(bf16[8,128,128]{2,1,0:T(8,128)(2,1)} %get-tuple-element.85), channel_id=1, source_target_pairs={{0,4},{4,0},{8,12},{12,8},{16,20},{20,16},{24,28},{28,24},{1,5},{5... | collective-permute-start | bytes 786440 | tf_op jit(solution)/shard_map/ppermute | solution.py:360
  28.1 5.2 %collective-permute-start.5 = (bf16[2,2,128,128]{3,2,1,0:T(8,128)(2,1)}, bf16[2,2,128,128]{3,2,1,0:T(8,128)(2,1)S(1)}, u32[]{:S(2)}, u32[]{:S(2)}) collective-permute-start(bf16[2,2,128,128]{3,2,1,0:T(8,128)(2,1)} %get-tuple-element.81), channel_id=1, source_target_pairs={{0,2},{1,3},{2,0},{3,1},{4,6},{5,7},{6,4},{7,5},{8,10},{9,11},{10,... | collective-permute-start | bytes 393224 | tf_op jit(solution)/shard_map/ppermute | solution.py:360
  29.4 9.9 %collective-permute-start.9 = (bf16[8,128,128]{2,1,0:T(8,128)(2,1)S(1)}, bf16[8,128,128]{2,1,0:T(8,128)(2,1)S(1)}, u32[]{:S(2)}, u32[]{:S(2)}) collective-permute-start(bf16[8,128,128]{2,1,0:T(8,128)(2,1)S(1)} %add_convert_fusion), channel_id=1, source_target_pairs={{0,8},{4,12},{8,0},{12,4},{16,24},{20,28},{24,16},{28,20},{1,9},{5... | collective-permute-start | bytes 786440 | tf_op jit(solution)/shard_map/ppermute | solution.py:360
  33.2 6.1 %collective-permute-start.12 = (bf16[2,128,512]{2,1,0:T(8,128)(2,1)S(1)}, bf16[2,128,512]{2,1,0:T(8,128)(2,1)S(1)}, u32[]{:S(2)}, u32[]{:S(2)}) collective-permute-start(bf16[2,128,512]{2,1,0:T(8,128)(2,1)S(1)} %collective-permute-done.1.refs_2_), channel_id=1, source_target_pairs={{0,1},{1,0},{2,3},{3,2},{4,5},{5,4},{6,7},{7,6},{8,9},{9,8},{10,11... | collective-permute-start | bytes 786440 | tf_op jit(solution)/shard_map/ppermute | solution.py:360
  33.5 5.6 %collective-permute-start.6 = (bf16[2,2,128,128]{3,2,1,0:T(8,128)(2,1)}, bf16[2,2,128,128]{3,2,1,0:T(8,128)(2,1)S(1)}, u32[]{:S(2)}, u32[]{:S(2)}) collective-permute-start(bf16[2,2,128,128]{3,2,1,0:T(8,128)(2,1)} %get-tuple-element.82), channel_id=1, source_target_pairs={{0,3},{1,2},{2,1},{3,0},{4,7},{5,6},{6,5},{7,4},{8,11},{9,10},{10,... | collective-permute-start | bytes 393224 | tf_op jit(solution)/shard_map/ppermute | solution.py:360
  34.7 11.9 %copy-start.4 = (bf16[2,128,512]{2,1,0:T(8,128)(2,1)S(1)}, bf16[2,128,512]{2,1,0:T(8,128)(2,1)}, u32[]{:S(2)}) copy-start(bf16[2,128,512]{2,1,0:T(8,128)(2,1)} %get-tuple-element.97.refs_0_) | copy-start | bytes 786436
  34.7 11.9 %copy-start.5 = (bf16[2,2,128,128]{3,2,1,0:T(8,128)(2,1)S(1)}, bf16[2,2,128,128]{3,2,1,0:T(8,128)(2,1)}, u32[]{:S(2)}) copy-start(bf16[2,2,128,128]{3,2,1,0:T(8,128)(2,1)} %get-tuple-element.101.refs_4_) | copy-start | bytes 393220
  39.1 1.6 %collective-permute-start.10 = (bf16[2,2,128,128]{3,2,1,0:T(8,128)(2,1)}, bf16[2,2,128,128]{3,2,1,0:T(8,128)(2,1)S(1)}, u32[]{:S(2)}, u32[]{:S(2)}) collective-permute-start(bf16[2,2,128,128]{3,2,1,0:T(8,128)(2,1)} %get-tuple-element.90), channel_id=1, source_target_pairs={{0,1},{1,0},{2,3},{3,2},{4,5},{5,4},{6,7},{7,6},{8,9},{9,8},{10,11... | collective-permute-start | bytes 393224 | tf_op jit(solution)/shard_map/ppermute | solution.py:360
  40.9 31.2 %copy-start.2 = (bf16[1024,128]{1,0:T(8,128)(2,1)S(1)}, bf16[1024,128]{1,0:T(8,128)(2,1)}, u32[]{:S(2)}) copy-start(bf16[1024,128]{1,0:T(8,128)(2,1)} %f_ref.1) | copy-start | bytes 786436
  40.9 31.2 %copy-start.3 = (bf16[128,512]{1,0:T(8,128)(2,1)S(1)}, bf16[128,512]{1,0:T(8,128)(2,1)}, u32[]{:S(2)}) copy-start(bf16[128,512]{1,0:T(8,128)(2,1)} %w_ref.1) | copy-start | bytes 393220
  40.9 2.1 %collective-permute-start.13 = (bf16[2,128,128]{2,1,0:T(8,128)(2,1)S(1)}, bf16[2,128,128]{2,1,0:T(8,128)(2,1)S(1)}, u32[]{:S(2)}, u32[]{:S(2)}) collective-permute-start(bf16[2,128,128]{2,1,0:T(8,128)(2,1)S(1)} %get-tuple-element.106), channel_id=1, source_target_pairs={{0,1},{1,0},{2,3},{3,2},{4,5},{5,4},{6,7},{7,6},{8,9},{9,8},{10,11... | collective-permute-start | bytes 196616 | tf_op jit(solution)/shard_map/ppermute | solution.py:360
  41.2 4.6 %collective-permute-start.14 = (bf16[2,128,128]{2,1,0:T(8,128)(2,1)S(1)}, bf16[2,128,128]{2,1,0:T(8,128)(2,1)S(1)}, u32[]{:S(2)}, u32[]{:S(2)}) collective-permute-start(bf16[2,128,128]{2,1,0:T(8,128)(2,1)S(1)} %get-tuple-element.107), channel_id=1, source_target_pairs={{0,2},{1,3},{2,0},{3,1},{4,6},{5,7},{6,4},{7,5},{8,10},{9,11},{10,... | collective-permute-start | bytes 196616 | tf_op jit(solution)/shard_map/ppermute | solution.py:360
  42.2 4.3 %collective-permute-start.15 = (bf16[2,128,128]{2,1,0:T(8,128)(2,1)S(1)}, bf16[2,128,128]{2,1,0:T(8,128)(2,1)S(1)}, u32[]{:S(2)}, u32[]{:S(2)}) collective-permute-start(bf16[2,128,128]{2,1,0:T(8,128)(2,1)S(1)} %get-tuple-element.108), channel_id=1, source_target_pairs={{0,3},{1,2},{2,1},{3,0},{4,7},{5,6},{6,5},{7,4},{8,11},{9,10},{10,... | collective-permute-start | bytes 196616 | tf_op jit(solution)/shard_map/ppermute | solution.py:360
  47.8 1.9 %collective-permute-start.16 = (bf16[256,128]{1,0:T(8,128)(2,1)S(1)}, bf16[256,128]{1,0:T(8,128)(2,1)S(1)}, u32[]{:S(2)}, u32[]{:S(2)}) collective-permute-start(bf16[256,128]{1,0:T(8,128)(2,1)S(1)} %get-tuple-element.110), channel_id=1, source_target_pairs={{0,1},{1,0},{2,3},{3,2},{4,5},{5,4},{6,7},{7,6},{8,9},{9,8},{10,11... | collective-permute-start | bytes 196616 | tf_op jit(solution)/shard_map/ppermute | solution.py:360
  48.0 4.8 %collective-permute-start.17 = (bf16[256,128]{1,0:T(8,128)(2,1)S(1)}, bf16[256,128]{1,0:T(8,128)(2,1)S(1)}, u32[]{:S(2)}, u32[]{:S(2)}) collective-permute-start(bf16[256,128]{1,0:T(8,128)(2,1)S(1)} %get-tuple-element.111), channel_id=1, source_target_pairs={{0,2},{1,3},{2,0},{3,1},{4,6},{5,7},{6,4},{7,5},{8,10},{9,11},{10,... | collective-permute-start | bytes 196616 | tf_op jit(solution)/shard_map/ppermute | solution.py:360
  49.1 4.3 %collective-permute-start.18 = (bf16[256,128]{1,0:T(8,128)(2,1)S(1)}, bf16[256,128]{1,0:T(8,128)(2,1)S(1)}, u32[]{:S(2)}, u32[]{:S(2)}) collective-permute-start(bf16[256,128]{1,0:T(8,128)(2,1)S(1)} %get-tuple-element.112), channel_id=1, source_target_pairs={{0,3},{1,2},{2,1},{3,0},{4,7},{5,6},{6,5},{7,4},{8,11},{9,10},{10,... | collective-permute-start | bytes 196616 | tf_op jit(solution)/shard_map/ppermute | solution.py:360
  53.4 16.9 %collective-permute-start.20 = (bf16[5,256,128]{2,1,0:T(8,128)(2,1)S(1)}, bf16[5,256,128]{2,1,0:T(8,128)(2,1)S(1)}, u32[]{:S(2)}, u32[]{:S(2)}) collective-permute-start(bf16[5,256,128]{2,1,0:T(8,128)(2,1)S(1)} %get-tuple-element.116), channel_id=1, source_target_pairs={{0,2},{1,3},{2,0},{3,1},{4,6},{5,7},{6,4},{7,5},{8,10},{9,11},{10,... | collective-permute-start | bytes 983048 | tf_op jit(solution)/shard_map/ppermute | solution.py:360
  54.5 15.9 %collective-permute-start.21 = (bf16[5,256,128]{2,1,0:T(8,128)(2,1)S(1)}, bf16[5,256,128]{2,1,0:T(8,128)(2,1)S(1)}, u32[]{:S(2)}, u32[]{:S(2)}) collective-permute-start(bf16[5,256,128]{2,1,0:T(8,128)(2,1)S(1)} %get-tuple-element.117), channel_id=1, source_target_pairs={{0,3},{1,2},{2,1},{3,0},{4,7},{5,6},{6,5},{7,4},{8,11},{9,10},{10,... | collective-permute-start | bytes 983048 | tf_op jit(solution)/shard_map/ppermute | solution.py:360
  55.1 15.3 %collective-permute-start.19 = (bf16[8,128,128]{2,1,0:T(8,128)(2,1)S(1)}, bf16[8,128,128]{2,1,0:T(8,128)(2,1)S(1)}, u32[]{:S(2)}, u32[]{:S(2)}) collective-permute-start(bf16[8,128,128]{2,1,0:T(8,128)(2,1)S(1)} %bitcast.24), channel_id=1, source_target_pairs={{0,16},{4,20},{8,24},{12,28},{16,0},{20,4},{24,8},{28,12},{1,17},{... | collective-permute-start | bytes 786440 | tf_op jit(solution)/shard_map/ppermute | solution.py:360
  56.5 13.8 %collective-permute-start.22 = (bf16[8,128,128]{2,1,0:T(8,128)(2,1)S(1)}, bf16[8,128,128]{2,1,0:T(8,128)(2,1)S(1)}, u32[]{:S(2)}, u32[]{:S(2)}) collective-permute-start(bf16[8,128,128]{2,1,0:T(8,128)(2,1)S(1)} %bitcast.25), channel_id=1, source_target_pairs={{0,8},{4,12},{8,0},{12,4},{16,24},{20,28},{24,16},{28,20},{1,9},{5... | collective-permute-start | bytes 786440 | tf_op jit(solution)/shard_map/ppermute | solution.py:360
  58.1 12.3 %collective-permute-start.23 = (bf16[8,128,128]{2,1,0:T(8,128)(2,1)S(1)}, bf16[8,128,128]{2,1,0:T(8,128)(2,1)S(1)}, u32[]{:S(2)}, u32[]{:S(2)}) collective-permute-start(bf16[8,128,128]{2,1,0:T(8,128)(2,1)S(1)} %bitcast.26), channel_id=1, source_target_pairs={{0,4},{4,0},{8,12},{12,8},{16,20},{20,16},{24,28},{28,24},{1,5},{5... | collective-permute-start | bytes 786440 | tf_op jit(solution)/shard_map/ppermute | solution.py:360
  70.4 1.7 %collective-permute-start.24 = (bf16[5,256,128]{2,1,0:T(8,128)(2,1)S(1)}, bf16[5,256,128]{2,1,0:T(8,128)(2,1)S(1)}, u32[]{:S(2)}, u32[]{:S(2)}) collective-permute-start(bf16[5,256,128]{2,1,0:T(8,128)(2,1)S(1)} %get-tuple-element.119.refs_0_), channel_id=1, source_target_pairs={{0,1},{1,0},{2,3},{3,2},{4,5},{5,4},{6,7},{7,6},{8,9},{9,8},{10,11... | collective-permute-start | bytes 983048 | tf_op jit(solution)/shard_map/ppermute | solution.py:360
  72.9 22.0 %copy-start = (bf16[1,6,8,128,128]{4,3,2,1,0:T(8,128)(2,1)S(1)}, bf16[1,6,8,128,128]{4,3,2,1,0:T(8,128)(2,1)}, u32[]{:S(2)}) copy-start(bf16[1,6,8,128,128]{4,3,2,1,0:T(8,128)(2,1)} %param.18) | copy-start | bytes 4718596
  72.9 22.0 %copy-start.1 = (bf16[1,16,128,128]{3,2,1,0:T(8,128)(2,1)S(1)}, bf16[1,16,128,128]{3,2,1,0:T(8,128)(2,1)}, u32[]{:S(2)}) copy-start(bf16[1,16,128,128]{3,2,1,0:T(8,128)(2,1)} %param.15) | copy-start | bytes 1572868
  72.9 22.0 %copy-start.6 = (s32[1,6,8]{2,0,1:T(1,128)S(1)}, s32[1,6,8]{2,0,1:T(1,128)}, u32[]{:S(2)}) copy-start(s32[1,6,8]{2,0,1:T(1,128)} %param.19) | copy-start | bytes 580
  72.9 22.0 %copy-start.7 = (s32[1,6,8]{2,0,1:T(1,128)S(1)}, s32[1,6,8]{2,0,1:T(1,128)}, u32[]{:S(2)}) copy-start(s32[1,6,8]{2,0,1:T(1,128)} %param.20) | copy-start | bytes 580
  72.9 22.0 %copy-start.8 = (s32[1,16]{1,0:T(1,128)S(1)}, s32[1,16]{1,0:T(1,128)}, u32[]{:S(2)}) copy-start(s32[1,16]{1,0:T(1,128)} %refs_0_.7) | copy-start | bytes 196
  72.9 22.0 %copy-start.9 = (s32[1,16]{1,0:T(1,128)S(1)}, s32[1,16]{1,0:T(1,128)}, u32[]{:S(2)}) copy-start(s32[1,16]{1,0:T(1,128)} %refs_1_.7) | copy-start | bytes 196
  72.9 5.6 %collective-permute-start.25 = (bf16[4,32,512]{2,1,0:T(8,128)(2,1)S(1)}, bf16[4,32,512]{2,1,0:T(8,128)(2,1)S(1)}, u32[]{:S(2)}, u32[]{:S(2)}) collective-permute-start(bf16[4,32,512]{2,1,0:T(8,128)(2,1)S(1)} %get-tuple-element.123), channel_id=1, source_target_pairs={{0,4},{4,0},{8,12},{12,8},{16,20},{20,16},{24,28},{28,24},{1,5},{5... | collective-permute-start | bytes 393224 | tf_op jit(solution)/shard_map/ppermute | solution.py:360
  78.6 6.5 %collective-permute-start.26 = (bf16[4,32,512]{2,1,0:T(8,128)(2,1)S(1)}, bf16[4,32,512]{2,1,0:T(8,128)(2,1)S(1)}, u32[]{:S(2)}, u32[]{:S(2)}) collective-permute-start(bf16[4,32,512]{2,1,0:T(8,128)(2,1)S(1)} %add_convert_fusion.5), channel_id=1, source_target_pairs={{0,8},{4,12},{8,0},{12,4},{16,24},{20,28},{24,16},{28,20},{1,9},{5... | collective-permute-start | bytes 393224 | tf_op jit(solution)/shard_map/ppermute | solution.py:360
  79.9 11.3 %collective-permute-start.29 = (bf16[8,128,128]{2,1,0:T(8,128)(2,1)S(1)}, bf16[8,128,128]{2,1,0:T(8,128)(2,1)S(1)}, u32[]{:S(2)}, u32[]{:S(2)}) collective-permute-start(bf16[8,128,128]{2,1,0:T(8,128)(2,1)S(1)} %collective-permute-done.19.refs_6_), channel_id=1, source_target_pairs={{0,8},{4,12},{8,0},{12,4},{16,24},{20,28},{24,16},{28,20},{1,9},{5... | collective-permute-start | bytes 786440 | tf_op jit(solution)/shard_map/ppermute | solution.py:360
  80.7 10.4 %collective-permute-start.30 = (bf16[8,128,128]{2,1,0:T(8,128)(2,1)S(1)}, bf16[8,128,128]{2,1,0:T(8,128)(2,1)S(1)}, u32[]{:S(2)}, u32[]{:S(2)}) collective-permute-start(bf16[8,128,128]{2,1,0:T(8,128)(2,1)S(1)} %collective-permute-done.19.refs_6_), channel_id=1, source_target_pairs={{0,4},{4,0},{8,12},{12,8},{16,20},{20,16},{24,28},{28,24},{1,5},{5... | collective-permute-start | bytes 786440 | tf_op jit(solution)/shard_map/ppermute | solution.py:360
  85.1 8.0 %collective-permute-start.27 = (bf16[4,32,512]{2,1,0:T(8,128)(2,1)S(1)}, bf16[4,32,512]{2,1,0:T(8,128)(2,1)S(1)}, u32[]{:S(2)}, u32[]{:S(2)}) collective-permute-start(bf16[4,32,512]{2,1,0:T(8,128)(2,1)S(1)} %add_convert_fusion.4), channel_id=1, source_target_pairs={{0,16},{4,20},{8,24},{12,28},{16,0},{20,4},{24,8},{28,12},{1,17},{... | collective-permute-start | bytes 393224 | tf_op jit(solution)/shard_map/ppermute | solution.py:360
  86.8 6.5 %collective-permute-start.28 = (bf16[8,128,128]{2,1,0:T(8,128)(2,1)S(1)}, bf16[8,128,128]{2,1,0:T(8,128)(2,1)S(1)}, u32[]{:S(2)}, u32[]{:S(2)}) collective-permute-start(bf16[8,128,128]{2,1,0:T(8,128)(2,1)S(1)} %collective-permute-done.22.refs_8_), channel_id=1, source_target_pairs={{0,4},{4,0},{8,12},{12,8},{16,20},{20,16},{24,28},{28,24},{1,5},{5... | collective-permute-start | bytes 786440 | tf_op jit(solution)/shard_map/ppermute | solution.py:360
  91.1 6.4 %collective-permute-start.31 = (bf16[8,128,128]{2,1,0:T(8,128)(2,1)S(1)}, bf16[8,128,128]{2,1,0:T(8,128)(2,1)S(1)}, u32[]{:S(2)}, u32[]{:S(2)}) collective-permute-start(bf16[8,128,128]{2,1,0:T(8,128)(2,1)S(1)} %collective-permute-done.30.refs_7_), channel_id=1, source_target_pairs={{0,8},{4,12},{8,0},{12,4},{16,24},{20,28},{24,16},{28,20},{1,9},{5... | collective-permute-start | bytes 786440 | tf_op jit(solution)/shard_map/ppermute | solution.py:360
  93.3 6.9 %collective-permute-start.32 = (bf16[4,32,512]{2,1,0:T(8,128)(2,1)S(1)}, bf16[4,32,512]{2,1,0:T(8,128)(2,1)S(1)}, u32[]{:S(2)}, u32[]{:S(2)}) collective-permute-start(bf16[4,32,512]{2,1,0:T(8,128)(2,1)S(1)} %add_convert_fusion.3.mine_ref), channel_id=1, source_target_pairs={{0,4},{4,0},{8,12},{12,8},{16,20},{20,16},{24,28},{28,24},{1,5},{5... | collective-permute-start | bytes 393224 | tf_op jit(solution)/shard_map/ppermute | solution.py:360
